TPU v7x, 32 devices: a whole 2x2x4 slice. The times are simulated.
32 devices in a mesh: expert: 32 (over z, y, x, core), dp: 1.
Axes of the slice: x: 2, y: 2, z: 4, core: 2. Of those that a mesh axis runs over, the one named last changes fastest.
Arguments:
- tokens: bfloat16 [2048, 2048], P(('expert', 'dp')), may hold values from -6 to 6
- attn_partials: bfloat16 [1, 2048, 2048], P('dp', 'expert'), may hold values from -5 to 5
- expert_ids: int32 [2048], P(('expert', 'dp')), may hold values from 0 to 1, as said below
- gate: float32 [2048], P(('expert', 'dp')), may hold values from 0.2 to 1
- w_in: float32 [2048, 10240], P('dp', 'expert'), may hold values from -6 to 6
- w_out: float32 [2048, 10240], P('dp', 'expert'), may hold values from -6 to 6
Outputs:
- token_grad: bfloat16 [2048, 2048], P(('expert', 'dp'))
- new_w_in: float32 [2048, 10240], P('dp', 'expert')
- new_w_out: float32 [2048, 10240], P('dp', 'expert')
Inputs may be any that keep to these rules, and one draw needn't show every extreme that they name: `expert_ids`: one expert, the same for all devices, is chosen by half of the 64 rows of every device; the other experts share the remaining rows of a device as evenly as whole numbers allow.
All inputs are finite; a program needn't handle non-finite values.
Results may differ from a plain program's by a relative error of at most 0.025.
Values may be sent and summed in bfloat16 or wider, within the bound.
No kernel may reach another device: no remote copies, remote signals or barrier semaphores. Data moves between devices by JAX's collectives and lax.ppermute only.
A program may use at most 64 MiB of HBM per device.

v0:
```python
import jax
import jax.numpy as jnp
from jax import lax
from jax.sharding import PartitionSpec as P

FF = 5120
SHARDS = 16


gelu_coef = 0.7978845608028654
cubic_coef = 0.044715
step_rate = 0.5


def gelu_value(inputs):
    return (
        0.5
        * inputs
        * (1.0 + jnp.tanh(gelu_coef * (inputs + cubic_coef * inputs * inputs * inputs)))
    )


def gelu_slope(inputs):
    tangent = jnp.tanh(gelu_coef * (inputs + cubic_coef * inputs * inputs * inputs))
    return 0.5 * (1.0 + tangent) + 0.5 * inputs * (1.0 - tangent * tangent) * gelu_coef * (
        1.0 + 3.0 * cubic_coef * inputs * inputs
    )


def contract_rows(left, right):
    return lax.dot_general(
        left, right, (((0,), (0,)), ((), ())), preferred_element_type=jnp.float32
    )


def contract_cols(left, right):
    return lax.dot_general(
        left, right, (((1,), (1,)), ((), ())), preferred_element_type=jnp.float32
    )


def summed_grads(attn_partials, gate):
    terms = attn_partials[0].astype(jnp.float32)
    out_grad = lax.psum_scatter(
        terms.astype(jnp.bfloat16), "dp", scatter_dimension=0, tiled=True
    ).astype(jnp.float32)
    return (gate[:, None] * out_grad).astype(jnp.bfloat16)


def shards(tokens, attn_partials, expert_ids, gate, w_in, w_out):
    tok_rows = tokens.shape[0]
    width = tokens.shape[1]
    n_expert = lax.axis_size("expert")
    experts = n_expert // SHARDS
    capacity = 5 * tok_rows // (8 * experts)
    scale_in = width ** (-0.5)
    scale_out = FF ** (-0.5)
    expert_range = jnp.arange(experts, dtype=jnp.int32)
    member = (expert_ids[:, None] == expert_range[None, :]).astype(jnp.int32)
    slot_rank = jnp.sum(member * (jnp.cumsum(member, axis=0) - 1), axis=1)
    keeping = slot_rank < capacity
    flat_slot = jnp.where(keeping, expert_ids * capacity + slot_rank, -1)
    slot_range = jnp.arange(experts * capacity, dtype=jnp.int32)
    dispatch = (slot_range[:, None] == flat_slot[None, :]).astype(jnp.bfloat16)

    def fan_out(source_rows):
        packed = jnp.dot(dispatch, source_rows, preferred_element_type=jnp.float32).astype(
            jnp.bfloat16
        )
        return jnp.repeat(packed.reshape(experts, capacity, width), SHARDS, axis=0)

    weights_in, weights_out = (
        lax.all_gather(w_in.astype(jnp.bfloat16), "dp", axis=0, tiled=True),
        lax.all_gather(w_out.astype(jnp.bfloat16), "dp", axis=0, tiled=True),
    )
    gated = summed_grads(attn_partials, gate)
    arrived, arrived_grads = (
        lax.all_to_all(fan_out(tokens), "expert", split_axis=0, concat_axis=0, tiled=True),
        lax.all_to_all(fan_out(gated), "expert", split_axis=0, concat_axis=0, tiled=True),
    )
    expert_rows = arrived.reshape(n_expert * capacity, width)
    grad_rows = arrived_grads.reshape(n_expert * capacity, width)
    pre_act = jnp.dot(expert_rows, weights_in, preferred_element_type=jnp.float32) * scale_in
    hidden = gelu_value(pre_act).astype(jnp.bfloat16)
    hidden_grad = jnp.dot(grad_rows, weights_out, preferred_element_type=jnp.float32) * scale_out
    pre_grad = (hidden_grad * gelu_slope(pre_act)).astype(jnp.bfloat16)
    partial_x = (contract_cols(pre_grad, weights_in) * scale_in).astype(jnp.bfloat16)
    returned = lax.all_to_all(
        partial_x.reshape(n_expert, capacity, width),
        "expert",
        split_axis=0,
        concat_axis=0,
        tiled=True,
    )
    slot_sums = jnp.sum(
        returned.reshape(experts, SHARDS, capacity, width).astype(jnp.float32), axis=1
    )
    safe_slot = jnp.maximum(flat_slot, 0)
    picked_sums = jnp.take(slot_sums.reshape(experts * capacity, width), safe_slot, axis=0)
    token_grad = jnp.where(keeping[:, None], picked_sums, 0.0).astype(jnp.bfloat16)
    rows_part = expert_rows
    grad_in = lax.psum_scatter(
        (contract_rows(rows_part, pre_grad) * scale_in).astype(jnp.bfloat16),
        "dp",
        scatter_dimension=0,
        tiled=True,
    ).astype(jnp.float32)
    rows_part = grad_rows
    grad_out = lax.psum_scatter(
        (contract_rows(rows_part, hidden) * scale_out).astype(jnp.bfloat16),
        "dp",
        scatter_dimension=0,
        tiled=True,
    ).astype(jnp.float32)
    new_w_in = w_in - step_rate * grad_in
    new_w_out = w_out - step_rate * grad_out
    return (token_grad, new_w_in, new_w_out)


def solution(mesh):
    in_specs = (
        P(("expert", "dp"), None),
        P("dp", "expert", None),
        P(("expert", "dp")),
        P(("expert", "dp")),
        P("dp", "expert"),
        P("dp", "expert"),
    )
    out_specs = (P(("expert", "dp"), None), P("dp", "expert"), P("dp", "expert"))
    return jax.shard_map(shards, mesh=mesh, in_specs=in_specs, out_specs=out_specs, check_vma=False)
```

profile of v0, /device:TPU:0, one launch (start us, length us, event | category | flops | bytes accessed | tf_op | source)
XLA Modules:
  0.0 258.9 jit_solution(15688102213053490013)
XLA Ops:
  0.6 0.8 fusion.34
  1.5 0.8 select_reduce_fusion
  3.3 2.0 broadcast_in_dim.44
  5.3 7.3 %all-to-all-start.1 = ((bf16[32,20,2048]{2,1,0:T(8,128)(2,1)}), bf16[32,20,2048]{2,1,0:T(8,128)(2,1)S(1)}, u32[]{:S(2)}, u32[]{:S(2)}) async-start(bf16[32,20,2048]{2,1,0:T(8,128)(2,1)} %bitcast.2), calls=%async_computation.1 | async-start | bytes 6291456 | tf_op jit(solution)/shard_map/all_to_all | solution.py:78
  12.6 1.9 convolution_convert_fusion.1
  14.5 1.6 reshape.46
  16.1 67.9 %all-to-all-done.1 = bf16[32,20,2048]{2,1,0:T(8,128)(2,1)S(1)} async-done(((bf16[32,20,2048]{2,1,0:T(8,128)(2,1)}), bf16[32,20,2048]{2,1,0:T(8,128)(2,1)S(1)}, u32[]{:S(2)}, u32[]{:S(2)}) %all-to-all-start.1) | async-done | bytes 2621472 | tf_op jit(solution)/shard_map/all_to_all | solution.py:78
  84.1 3.0 %broadcast_in_dim.43 = bf16[2,16,20,2048]{3,2,1,0:T(8,128)(2,1)} broadcast(bf16[2,20,2048]{2,1,0:T(8,128)(2,1)} %reshape.46), dimensions={0,2,3} | broadcast | bytes 2785280 | tf_op jit(solution)/shard_map/broadcast_in_dim | solution.py:70
  87.1 4.0 %all-to-all-start = ((bf16[32,20,2048]{2,1,0:T(8,128)(2,1)}), bf16[32,20,2048]{2,1,0:T(8,128)(2,1)}, u32[]{:S(2)}, u32[]{:S(2)}) async-start(bf16[32,20,2048]{2,1,0:T(8,128)(2,1)} %bitcast.1), calls=%async_computation | async-start | bytes 6291456 | tf_op jit(solution)/shard_map/all_to_all | solution.py:79
  91.1 2.2 reshape.51
  93.3 4.7 %fusion.23 = f32[640,320]{0,1:T(8,128)} fusion(bf16[640,2048]{1,0:T(8,128)(2,1)} %reshape.51, f32[2048,320]{0,1:T(8,128)} %param.10), kind=kOutput, calls=%fused_computation.26 | convolution fusion | flops 839516160 | bytes 6062080 | tf_op jit(solution)/shard_map/dot_general | solution.py:83
  98.0 64.6 %all-to-all-done = bf16[32,20,2048]{2,1,0:T(8,128)(2,1)} async-done(((bf16[32,20,2048]{2,1,0:T(8,128)(2,1)}), bf16[32,20,2048]{2,1,0:T(8,128)(2,1)}, u32[]{:S(2)}, u32[]{:S(2)}) %all-to-all-start) | async-done | bytes 2621472 | tf_op jit(solution)/shard_map/all_to_all | solution.py:79
  162.6 3.6 %reshape.48 = bf16[640,2048]{1,0:T(8,128)(2,1)S(1)} reshape(bf16[32,20,2048]{2,1,0:T(8,128)(2,1)} %all-to-all-done) | data formatting | bytes 5242880 | tf_op jit(solution)/shard_map/reshape | solution.py:82
  166.2 4.5 %fusion.16 = bf16[640,320]{0,1:T(8,128)(2,1)S(1)} fusion(bf16[640,2048]{1,0:T(8,128)(2,1)S(1)} %reshape.48, f32[2048,320]{0,1:T(8,128)} %param.11, f32[640,320]{0,1:T(8,128)} %fusion.23), kind=kOutput, calls=%fused_computation.19 | convolution fusion | flops 843816960 | bytes 6471680 | tf_op jit(solution)/shard_map/dot_general | solution.py:85
  170.7 0.8 copy-done.6
  171.5 3.0 %multiply_convert_fusion = bf16[640,2048]{1,0:T(8,128)(2,1)} fusion(bf16[640,320]{0,1:T(8,128)(2,1)S(1)} %fusion.16, f32[2048,320]{0,1:T(8,128)S(1)} %copy-done.4), kind=kOutput, calls=%fused_computation.2 | convolution fusion | flops 842137600 | bytes 5652480 | tf_op jit(solution)/shard_map/dot_general | solution.py:37
  174.5 5.2 %reshape.52 = bf16[32,20,2048]{2,1,0:T(8,128)(2,1)} reshape(bf16[640,2048]{1,0:T(8,128)(2,1)} %multiply_convert_fusion) | data formatting | bytes 5242880 | tf_op jit(solution)/shard_map/reshape | solution.py:89
  179.7 3.9 %all-to-all-start.2 = ((bf16[32,20,2048]{2,1,0:T(8,128)(2,1)}), bf16[32,20,2048]{2,1,0:T(8,128)(2,1)S(1)}, u32[]{:S(2)}, u32[]{:S(2)}) async-start(bf16[32,20,2048]{2,1,0:T(8,128)(2,1)} %reshape.52), calls=%async_computation.2 | async-start | bytes 6291456 | tf_op jit(solution)/shard_map/all_to_all | solution.py:88
  183.7 5.5 %fusion.3 = f32[2048,320]{0,1:T(8,128)} fusion(f32[2048,320]{0,1:T(8,128)} %param.10, bf16[640,320]{0,1:T(8,128)(2,1)} %copy-done.6, bf16[640,2048]{1,0:T(8,128)(2,1)} %reshape.51), kind=kOutput, calls=%fused_computation.8 | convolution fusion | flops 842137600 | bytes 8273920 | tf_op jit(solution)/shard_map/dot_general | solution.py:31
  189.2 2.8 %fusion.7 = f32[2048,320]{0,1:T(8,128)} fusion(f32[2048,320]{0,1:T(8,128)S(1)} %copy-done.3, bf16[640,2048]{1,0:T(8,128)(2,1)S(1)} %copy-done.2, f32[640,320]{0,1:T(8,128)S(1)} %copy-done.5), kind=kOutput, calls=%fused_computation.12 | convolution fusion | flops 844185600 | bytes 8683520 | tf_op jit(solution)/shard_map/dot_general | solution.py:31
  192.0 63.1 %all-to-all-done.2 = bf16[32,20,2048]{2,1,0:T(8,128)(2,1)S(1)} async-done(((bf16[32,20,2048]{2,1,0:T(8,128)(2,1)}), bf16[32,20,2048]{2,1,0:T(8,128)(2,1)S(1)}, u32[]{:S(2)}, u32[]{:S(2)}) %all-to-all-start.2) | async-done | bytes 2621472 | tf_op jit(solution)/shard_map/all_to_all | solution.py:88
  255.1 1.2 convert_reduce_fusion
  256.3 1.0 reshape.53
  258.0 0.8 select_convert_fusion
  (22 shorter events, 1.8 us)
Async XLA Ops:
  0.6 2.4 copy-start
  5.3 7.3 %copy-start.7 = (f32[64]{0:T(128)S(1)}, f32[64]{0:T(128)}, u32[]{:S(2)}) copy-start(f32[64]{0:T(128)} %param.9) | copy-start | bytes 772
  5.3 78.8 %all-to-all-start.1 = ((bf16[32,20,2048]{2,1,0:T(8,128)(2,1)}), bf16[32,20,2048]{2,1,0:T(8,128)(2,1)S(1)}, u32[]{:S(2)}, u32[]{:S(2)}) async-start(bf16[32,20,2048]{2,1,0:T(8,128)(2,1)} %bitcast.2), calls=%async_computation.1 | async-start | bytes 6291456 | tf_op jit(solution)/shard_map/all_to_all | solution.py:78
  87.1 75.5 %all-to-all-start = ((bf16[32,20,2048]{2,1,0:T(8,128)(2,1)}), bf16[32,20,2048]{2,1,0:T(8,128)(2,1)}, u32[]{:S(2)}, u32[]{:S(2)}) async-start(bf16[32,20,2048]{2,1,0:T(8,128)(2,1)} %bitcast.1), calls=%async_computation | async-start | bytes 6291456 | tf_op jit(solution)/shard_map/all_to_all | solution.py:79
  166.2 4.5 %copy-start.1 = (bf16[640,2048]{1,0:T(8,128)(2,1)}, bf16[640,2048]{1,0:T(8,128)(2,1)S(1)}, u32[]{:S(2)}) copy-start(bf16[640,2048]{1,0:T(8,128)(2,1)S(1)} %reshape.48) | copy-start | bytes 7864324
  166.2 5.3 %copy-start.4 = (f32[2048,320]{0,1:T(8,128)S(1)}, f32[2048,320]{0,1:T(8,128)}, u32[]{:S(2)}) copy-start(f32[2048,320]{0,1:T(8,128)} %param.10) | copy-start | bytes 7864324
  170.7 0.8 copy-start.6
  179.7 75.4 %all-to-all-start.2 = ((bf16[32,20,2048]{2,1,0:T(8,128)(2,1)}), bf16[32,20,2048]{2,1,0:T(8,128)(2,1)S(1)}, u32[]{:S(2)}, u32[]{:S(2)}) async-start(bf16[32,20,2048]{2,1,0:T(8,128)(2,1)} %reshape.52), calls=%async_computation.2 | async-start | bytes 6291456 | tf_op jit(solution)/shard_map/all_to_all | solution.py:88
  183.7 5.6 %copy-start.2 = (bf16[640,2048]{1,0:T(8,128)(2,1)S(1)}, bf16[640,2048]{1,0:T(8,128)(2,1)}, u32[]{:S(2)}) copy-start(bf16[640,2048]{1,0:T(8,128)(2,1)} %copy-done.1) | copy-start | bytes 7864324
  183.7 5.6 %copy-start.3 = (f32[2048,320]{0,1:T(8,128)S(1)}, f32[2048,320]{0,1:T(8,128)}, u32[]{:S(2)}) copy-start(f32[2048,320]{0,1:T(8,128)} %param.11) | copy-start | bytes 7864324
  183.7 5.5 %copy-start.5 = (f32[640,320]{0,1:T(8,128)S(1)}, f32[640,320]{0,1:T(8,128)}, u32[]{:S(2)}) copy-start(f32[640,320]{0,1:T(8,128)} %fusion.23) | copy-start | bytes 2457604
where the time goes:
time: 259 us
  waiting for transfers between devices  196 us (76%)
  matrix products  22.6 us (9%)
  local copies, waits for them, and re-layouts  20.2 us (8%)
  starting transfers between devices  15.3 us (6%)
  other arithmetic  4.45 us (2%)
    all_to_all x1, waiting for transfers between devices, shards(): lax.all_to_all(fan_out(tokens), 'expert', split_axis=0, concat_axis=0, ti...  67.9 us
    all_to_all x1, waiting for transfers between devices, shards(): lax.all_to_all(fan_out(gated), 'expert', split_axis=0, concat_axis=0, til...  64.6 us
    all_to_all x1, waiting for transfers between devices, shards(): lax.all_to_all(partial_x.reshape(n_expert, capacity, width), 'expert', sp...  63.1 us
    dot_general x2, matrix products, contract_rows(): lax.dot_general(left, right, (((0,), (0,)), ((), ())), preferred_element_...  8.33 us
    all_to_all x1, starting transfers between devices, shards(): lax.all_to_all(fan_out(tokens), 'expert', split_axis=0, concat_axis=0, ti...  7.3 us
    reshape x1, local copies, waits for them, and re-layouts, shards(): partial_x.reshape(n_expert, capacity, width)  5.18 us
  transfers between devices with their start and end apart: 3, of which 3 were waited for; matrix products, arithmetic and copies ran while one was open for 7% of the time, Pallas kernels for 0%

commit v1 on v0

v1 whole, which is shorter than its diff:
```python
import jax
import jax.numpy as jnp
from jax import lax
from jax.sharding import PartitionSpec as P

FF = 5120
SHARDS = 16


gelu_coef = 0.7978845608028654
cubic_coef = 0.044715
step_rate = 0.5


def gelu_value(inputs):
    return (
        0.5
        * inputs
        * (1.0 + jnp.tanh(gelu_coef * (inputs + cubic_coef * inputs * inputs * inputs)))
    )


def gelu_slope(inputs):
    tangent = jnp.tanh(gelu_coef * (inputs + cubic_coef * inputs * inputs * inputs))
    return 0.5 * (1.0 + tangent) + 0.5 * inputs * (1.0 - tangent * tangent) * gelu_coef * (
        1.0 + 3.0 * cubic_coef * inputs * inputs
    )


def contract_rows(left, right):
    return lax.dot_general(
        left, right, (((0,), (0,)), ((), ())), preferred_element_type=jnp.float32
    )


def contract_cols(left, right):
    return lax.dot_general(
        left, right, (((1,), (1,)), ((), ())), preferred_element_type=jnp.float32
    )


def summed_grads(attn_partials, gate):
    if lax.axis_size("dp") == 1:
        out_grad = attn_partials[0].astype(jnp.float32)
    else:
        out_grad = lax.psum_scatter(
            attn_partials[0], "dp", scatter_dimension=0, tiled=True
        ).astype(jnp.float32)
    return (gate[:, None] * out_grad).astype(jnp.bfloat16)


def whole_weights(shard):
    if lax.axis_size("dp") == 1:
        return shard.astype(jnp.bfloat16)
    return lax.all_gather(shard.astype(jnp.bfloat16), "dp", axis=0, tiled=True)


def stepped(weights, grads):
    if lax.axis_size("dp") > 1:
        grads = lax.psum_scatter(
            grads.astype(jnp.bfloat16), "dp", scatter_dimension=0, tiled=True
        ).astype(jnp.float32)
    return weights - step_rate * grads


def shards(tokens, attn_partials, expert_ids, gate, w_in, w_out):
    tok_rows, width = tokens.shape
    n_expert = lax.axis_size("expert")
    experts = n_expert // SHARDS
    capacity = 5 * tok_rows // (8 * experts)
    scale_in = width ** (-0.5)
    scale_out = FF ** (-0.5)
    groups = [[e * SHARDS + k for k in range(SHARDS)] for e in range(experts)]

    def shifted(rows, hops):
        pairs = [(i, (i + SHARDS * hops) % n_expert) for i in range(n_expert)]
        return lax.ppermute(rows, "expert", pairs)

    my_expert = lax.axis_index("expert") // SHARDS
    relative = lax.rem(expert_ids - my_expert + experts, experts)
    expert_range = jnp.arange(experts, dtype=jnp.int32)
    member = (relative[:, None] == expert_range[None, :]).astype(jnp.int32)
    slot_rank = jnp.sum(member * (jnp.cumsum(member, axis=0) - 1), axis=1)
    flat_slot = jnp.where(slot_rank < capacity, relative * capacity + slot_rank, -1)
    slot_range = jnp.arange(experts * capacity, dtype=jnp.int32)
    dispatch = (slot_range[:, None] == flat_slot[None, :]).astype(jnp.bfloat16)

    gated = summed_grads(attn_partials, gate)
    both = jnp.concatenate([tokens, gated], axis=1)
    packed = jnp.dot(dispatch, both, preferred_element_type=jnp.float32).astype(jnp.bfloat16)
    packed = packed.reshape(experts, capacity, 2 * width)
    arrived = [packed[0]] + [shifted(packed[s], s) for s in range(1, experts)]
    own_rows = jnp.concatenate(arrived, axis=0)
    rows = lax.all_gather(own_rows, "expert", axis=0, tiled=True, axis_index_groups=groups)
    expert_rows = rows[:, :width]
    grad_rows = rows[:, width:]

    weights_in = whole_weights(w_in)
    weights_out = whole_weights(w_out)
    pre_act = jnp.dot(expert_rows, weights_in, preferred_element_type=jnp.float32) * scale_in
    hidden = gelu_value(pre_act).astype(jnp.bfloat16)
    hidden_grad = jnp.dot(grad_rows, weights_out, preferred_element_type=jnp.float32) * scale_out
    pre_grad = (hidden_grad * gelu_slope(pre_act)).astype(jnp.bfloat16)
    partial_x = (contract_cols(pre_grad, weights_in) * scale_in).astype(jnp.bfloat16)
    sums = lax.psum_scatter(
        partial_x, "expert", scatter_dimension=0, tiled=True, axis_index_groups=groups
    ).reshape(experts, capacity, width)
    back = [sums[0]] + [shifted(sums[s], -s) for s in range(1, experts)]
    slot_sums = jnp.concatenate(back, axis=0)
    token_grad = contract_rows(dispatch, slot_sums).astype(jnp.bfloat16)
    new_w_in = stepped(w_in, contract_rows(expert_rows, pre_grad) * scale_in)
    new_w_out = stepped(w_out, contract_rows(grad_rows, hidden) * scale_out)
    return (token_grad, new_w_in, new_w_out)


def solution(mesh):
    in_specs = (
        P(("expert", "dp"), None),
        P("dp", "expert", None),
        P(("expert", "dp")),
        P(("expert", "dp")),
        P("dp", "expert"),
        P("dp", "expert"),
    )
    out_specs = (P(("expert", "dp"), None), P("dp", "expert"), P("dp", "expert"))
    return jax.shard_map(shards, mesh=mesh, in_specs=in_specs, out_specs=out_specs, check_vma=False)
```

time: 259 us -> 149 us (0.58)
  waiting for transfers between devices: 196 us -> 102 us
  local copies, waits for them, and re-layouts: 20.2 us -> 1.96 us
  between operations: 0.79 us -> 14.1 us
  starting transfers between devices: 15.3 us -> 6.77 us
    all_to_all x3 -> x0, waiting for transfers between devices: 196 us -> none  [the longest x1 67.9 us: shards(): lax.all_to_all(fan_out(tokens), 'expert', split_axis=0, concat_axis=0, ti...]
    reduce_scatter x0 -> x1, waiting for transfers between devices: none -> 54.1 us  [shards(): lax.psum_scatter(partial_x, 'expert', scatter_dimension=0, tiled=True, ax...]
    all_gather x0 -> x1, waiting for transfers between devices: none -> 38.4 us  [shards(): lax.all_gather(own_rows, 'expert', axis=0, tiled=True, axis_index_groups=...]
    all_to_all x3 -> x0, starting transfers between devices: 15.3 us -> none  [the longest x1 7.3 us: shards(): lax.all_to_all(fan_out(tokens), 'expert', split_axis=0, concat_axis=0, ti...]
    reshape x6 -> x0, local copies, waits for them, and re-layouts: 13.6 us -> none  [the longest x1 5.18 us: shards(): partial_x.reshape(n_expert, capacity, width)]
    ppermute x0 -> x2, waiting for transfers between devices: none -> 9.11 us  [shifted(): return lax.ppermute(rows, 'expert', pairs)]
    ppermute x0 -> x2, starting transfers between devices: none -> 6.69 us  [shifted(): return lax.ppermute(rows, 'expert', pairs)]
    broadcast_in_dim x2 -> x0, local copies, waits for them, and re-layouts: 5.04 us -> none  [fan_out(): return jnp.repeat(packed.reshape(experts, capacity, width), SHARDS, axis=0)]
  transfers between devices with their start and end apart: 3 -> 4, of which waited for: 3 -> 3; matrix products, arithmetic and copies ran while one was open for 7% -> 7% of each run, Pallas kernels for 0% -> 0%
where the time goes in v1:
time: 149 us
  waiting for transfers between devices  102 us (68%)
  matrix products  20.6 us (14%)
  between operations  14.1 us (9%)
  starting transfers between devices  6.77 us (5%)
  other arithmetic  3.54 us (2%)
  local copies, waits for them, and re-layouts  1.96 us (1%)
    reduce_scatter x1, waiting for transfers between devices, shards(): lax.psum_scatter(partial_x, 'expert', scatter_dimension=0, tiled=True, ax...  54.1 us
    all_gather x1, waiting for transfers between devices, shards(): lax.all_gather(own_rows, 'expert', axis=0, tiled=True, axis_index_groups=...  38.4 us
    dot_general x3, matrix products, contract_rows(): lax.dot_general(left, right, (((0,), (0,)), ((), ())), preferred_element_...  10.9 us
    ppermute x2, waiting for transfers between devices, shifted(): return lax.ppermute(rows, 'expert', pairs)  9.11 us
    ppermute x2, starting transfers between devices, shifted(): return lax.ppermute(rows, 'expert', pairs)  6.69 us
    dot_general x1, matrix products, shards(): jnp.dot(expert_rows, weights_in, preferred_element_type=jnp.float32)  3.89 us
    dot_general x1, matrix products, contract_cols(): lax.dot_general(left, right, (((1,), (1,)), ((), ())), preferred_element_...  3.05 us
  transfers between devices with their start and end apart: 4, of which 3 were waited for; matrix products, arithmetic and copies ran while one was open for 7% of the time, Pallas kernels for 0%

profile of v1, /device:TPU:0, one launch (start us, length us, event | category | flops | bytes accessed | tf_op | source)
XLA Modules:
  0.0 148.6 jit_solution(17986698976088674827)
XLA Ops:
  7.2 0.0 all-gather.2.cloned.1.call-start
  7.2 0.7 compare_select_fusion
  7.9 0.1 fusion.41
  8.0 0.1 reduce_window_sum.11
  8.1 0.2 select_reduce_fusion
  8.2 0.7 compare_select_fusion.2
  8.9 1.1 fusion.32
  10.0 1.2 convolution_convert_fusion
  11.2 4.1 %collective-permute-start = (bf16[20,4096]{1,0:T(8,128)(2,1)S(1)}, bf16[20,4096]{1,0:T(8,128)(2,1)S(1)}, u32[]{:S(2)}, u32[]{:S(2)}) collective-permute-start(bf16[20,4096]{1,0:T(8,128)(2,1)S(1)} %get-tuple-element.4), channel_id=1, source_target_pairs={{0,16},{1,17},{2,18},{3,19},{4,20},{5,21},{6,22},{7,23},{8,24},{9,... | collective-permute-start | bytes 491528 | tf_op jit(solution)/shard_map/ppermute | solution.py:77
  15.3 9.1 %collective-permute-done = bf16[20,4096]{1,0:T(8,128)(2,1)S(1)} collective-permute-done((bf16[20,4096]{1,0:T(8,128)(2,1)S(1)}, bf16[20,4096]{1,0:T(8,128)(2,1)S(1)}, u32[]{:S(2)}, u32[]{:S(2)}) %collective-permute-start) | collective-permute-done | bytes 163872 | tf_op jit(solution)/shard_map/ppermute | solution.py:77
  24.4 0.8 pad_maximum_fusion
  25.3 0.0 reduce-scatter.2.cloned.1.call-start
  25.3 38.4 %all-gather.2.cloned.1.call-done = bf16[640,4096]{1,0:T(8,128)(2,1)} async-done(((bf16[40,4096]{1,0:T(8,128)(2,1)}), bf16[640,4096]{1,0:T(8,128)(2,1)}) %all-gather.2.cloned.1.call-update) | async-done | bytes 5242896 | tf_op jit(solution)/shard_map/all_gather | solution.py:94
  63.7 3.9 %fusion.3 = f32[640,320]{0,1:T(8,128)S(1)} fusion(bf16[640,4096]{1,0:T(8,128)(2,1)} %all-gather.2.cloned.1.call-done, f32[2048,320]{0,1:T(8,128)} %param.10), kind=kOutput, calls=%fused_computation.7 | convolution fusion | flops 839516160 | bytes 6062080 | tf_op jit(solution)/shard_map/dot_general | solution.py:100
  67.6 0.1 copy-done.2
  67.7 1.6 %fusion.19 = bf16[640,320]{0,1:T(8,128)(2,1)S(1)} fusion(f32[2048,320]{0,1:T(8,128)S(1)} %copy-done, bf16[640,4096]{1,0:T(8,128)(2,1)S(1)} %copy-done.2, f32[640,320]{0,1:T(8,128)S(1)} %fusion.3), kind=kOutput, calls=%fused_computation.16 | convolution fusion | flops 843816960 | bytes 6471680 | tf_op jit(solution)/shard_map/dot_general | solution.py:102
  69.4 0.8 copy-done.3
  70.2 3.1 %multiply_convert_fusion = bf16[640,2048]{1,0:T(8,128)(2,1)} fusion(bf16[640,320]{0,1:T(8,128)(2,1)S(1)} %fusion.19, f32[2048,320]{0,1:T(8,128)S(1)} %copy-done.1), kind=kOutput, calls=%fused_computation | convolution fusion | flops 842137600 | bytes 5652480 | tf_op jit(solution)/shard_map/dot_general | solution.py:37
  73.2 4.5 %fusion = f32[2048,320]{0,1:T(8,128)} fusion(f32[2048,320]{0,1:T(8,128)S(1)} %copy-done, bf16[640,4096]{1,0:T(8,128)(2,1)} %all-gather.2.cloned.1.call-done, f32[640,320]{0,1:T(8,128)S(1)} %fusion.3), kind=kOutput, calls=%fused_computation.3 | convolution fusion | flops 842219520 | bytes 8683520 | tf_op jit(solution)/shard_map/dot_general | solution.py:31
  77.8 54.1 %reduce-scatter.2.cloned.1.call-done = bf16[40,2048]{1,0:T(8,128)(2,1)} async-done(((bf16[640,2048]{1,0:T(8,128)(2,1)}), bf16[40,2048]{1,0:T(8,128)(2,1)}) %reduce-scatter.2.cloned.1.call-update) | async-done | bytes 163856 | tf_op jit(solution)/shard_map/reduce_scatter | solution.py:105
  131.8 1.0 fusion.53
  132.8 2.6 %collective-permute-start.1 = (bf16[20,2048]{1,0:T(8,128)(2,1)S(1)}, bf16[20,2048]{1,0:T(8,128)(2,1)S(1)}, u32[]{:S(2)}, u32[]{:S(2)}) collective-permute-start(bf16[20,2048]{1,0:T(8,128)(2,1)S(1)} %get-tuple-element.6), channel_id=1, source_target_pairs={{0,16},{1,17},{2,18},{3,19},{4,20},{5,21},{6,22},{7,23},{8,24},{9,... | collective-permute-start | bytes 245768 | tf_op jit(solution)/shard_map/ppermute | solution.py:77
  135.4 5.4 %fusion.1 = f32[2048,320]{0,1:T(8,128)} fusion(f32[2048,320]{0,1:T(8,128)} %param.10, bf16[640,320]{0,1:T(8,128)(2,1)} %copy-done.3, bf16[640,4096]{1,0:T(8,128)(2,1)} %all-gather.2.cloned.1.call-done), kind=kOutput, calls=%fused_computation.5 | convolution fusion | flops 840171520 | bytes 8273920 | tf_op jit(solution)/shard_map/dot_general | solution.py:31
  140.8 1.0 convolution_convert_fusion.1
  (10 shorter events, 0.1 us)
Async XLA Ops:
  7.2 56.5 %all-gather.2.cloned.1.call-start = ((), (), s32[]{:S(2)}) async-start(), calls=%async_computation.1 | async-start | bytes 5570560 | tf_op jit(solution)/shard_map/all_gather | solution.py:94
  11.2 13.2 %collective-permute-start = (bf16[20,4096]{1,0:T(8,128)(2,1)S(1)}, bf16[20,4096]{1,0:T(8,128)(2,1)S(1)}, u32[]{:S(2)}, u32[]{:S(2)}) collective-permute-start(bf16[20,4096]{1,0:T(8,128)(2,1)S(1)} %get-tuple-element.4), channel_id=1, source_target_pairs={{0,16},{1,17},{2,18},{3,19},{4,20},{5,21},{6,22},{7,23},{8,24},{9,... | collective-permute-start | bytes 491528 | tf_op jit(solution)/shard_map/ppermute | solution.py:77
  25.3 42.3 %copy-start = (f32[2048,320]{0,1:T(8,128)S(1)}, f32[2048,320]{0,1:T(8,128)}, u32[]{:S(2)}) copy-start(f32[2048,320]{0,1:T(8,128)} %param.11) | copy-start | bytes 7864324
  25.3 106.6 %reduce-scatter.2.cloned.1.call-start = ((), (), s32[]{:S(2)}) async-start(), calls=%async_computation.2 | async-start | bytes 2785280 | tf_op jit(solution)/shard_map/reduce_scatter | solution.py:105
  63.7 4.1 %copy-start.2 = (bf16[640,4096]{1,0:T(8,128)(2,1)S(1)}, bf16[640,4096]{1,0:T(8,128)(2,1)}, u32[]{:S(2)}) copy-start(bf16[640,4096]{1,0:T(8,128)(2,1)} %all-gather.2.cloned.1.call-done) | copy-start | bytes 15728644
  67.7 2.4 %copy-start.1 = (f32[2048,320]{0,1:T(8,128)S(1)}, f32[2048,320]{0,1:T(8,128)}, u32[]{:S(2)}) copy-start(f32[2048,320]{0,1:T(8,128)} %param.10) | copy-start | bytes 7864324
  69.4 0.8 copy-start.3
  132.8 7.9 %collective-permute-start.1 = (bf16[20,2048]{1,0:T(8,128)(2,1)S(1)}, bf16[20,2048]{1,0:T(8,128)(2,1)S(1)}, u32[]{:S(2)}, u32[]{:S(2)}) collective-permute-start(bf16[20,2048]{1,0:T(8,128)(2,1)S(1)} %get-tuple-element.6), channel_id=1, source_target_pairs={{0,16},{1,17},{2,18},{3,19},{4,20},{5,21},{6,22},{7,23},{8,24},{9,... | collective-permute-start | bytes 245768 | tf_op jit(solution)/shard_map/ppermute | solution.py:77
Sparse Core Ops, SparseCore 0:
  25.4 38.2 all-gather.1
  73.4 58.4 reduce-scatter.1

commit v2 on v1

--- a/solution.py
+++ b/solution.py
@@ -63,14 +63,68 @@
     return weights - step_rate * grads
 
 
+def swap(rows, mask):
+    n_expert = lax.axis_size("expert")
+    return lax.ppermute(rows, "expert", [(i, i ^ mask) for i in range(n_expert)])
+
+
+core_bit, x_bit, y_bit, z_bit = 1, 2, 4, 8
+
+
+def thirds(columns):
+    lanes = columns // 128
+    first = (lanes + 2) // 3 * 128
+    second = first + (lanes + 1) // 3 * 128
+    return (0, first), (first, second), (second, columns)
+
+
+def gather(own):
+    near_x, near_y, near_z = swap(own, x_bit), swap(own, y_bit), swap(own, z_bit)
+    xy, yz, zx = swap(near_x, y_bit), swap(near_y, z_bit), swap(near_z, x_bit)
+    (a0, a1), (b0, b1), (c0, c1) = thirds(own.shape[1])
+    far = jnp.concatenate(
+        [swap(xy[:, a0:a1], z_bit), swap(yz[:, b0:b1], x_bit), swap(zx[:, c0:c1], y_bit)], axis=1
+    )
+    return jnp.concatenate([own, near_x, near_y, near_z, xy, yz, zx, far], axis=0)
+
+
+def added(left, right):
+    return (left.astype(jnp.float32) + right.astype(jnp.float32)).astype(jnp.bfloat16)
+
+
+def scatter_sum(parts):
+    rows = parts.shape[0] // 8
+    own, near_x, near_y, near_z, xy, yz, zx, far = [
+        parts[k * rows : (k + 1) * rows] for k in range(8)
+    ]
+    (a0, a1), (b0, b1), (c0, c1) = thirds(parts.shape[1])
+    far_a, far_b, far_c = (
+        swap(far[:, a0:a1], z_bit),
+        swap(far[:, b0:b1], x_bit),
+        swap(far[:, c0:c1], y_bit),
+    )
+    xy = jnp.concatenate([added(xy[:, a0:a1], far_a), xy[:, a1:]], axis=1)
+    yz = jnp.concatenate([yz[:, :b0], added(yz[:, b0:b1], far_b), yz[:, b1:]], axis=1)
+    zx = jnp.concatenate([zx[:, :c0], added(zx[:, c0:c1], far_c)], axis=1)
+    near_x = added(near_x, swap(xy, y_bit))
+    near_y = added(near_y, swap(yz, z_bit))
+    near_z = added(near_z, swap(zx, x_bit))
+    total = own.astype(jnp.float32) + swap(near_x, x_bit).astype(jnp.float32)
+    total = total + swap(near_y, y_bit).astype(jnp.float32)
+    total = total + swap(near_z, z_bit).astype(jnp.float32)
+    return total.astype(jnp.bfloat16)
+
+
 def shards(tokens, attn_partials, expert_ids, gate, w_in, w_out):
     tok_rows, width = tokens.shape
     n_expert = lax.axis_size("expert")
     experts = n_expert // SHARDS
     capacity = 5 * tok_rows // (8 * experts)
+    first = capacity // 8 * 8
+    rest = experts * capacity - first
+    units = w_in.shape[1]
     scale_in = width ** (-0.5)
     scale_out = FF ** (-0.5)
-    groups = [[e * SHARDS + k for k in range(SHARDS)] for e in range(experts)]
 
     def shifted(rows, hops):
         pairs = [(i, (i + SHARDS * hops) % n_expert) for i in range(n_expert)]
@@ -81,36 +135,59 @@
     expert_range = jnp.arange(experts, dtype=jnp.int32)
     member = (relative[:, None] == expert_range[None, :]).astype(jnp.int32)
     slot_rank = jnp.sum(member * (jnp.cumsum(member, axis=0) - 1), axis=1)
-    flat_slot = jnp.where(slot_rank < capacity, relative * capacity + slot_rank, -1)
-    slot_range = jnp.arange(experts * capacity, dtype=jnp.int32)
-    dispatch = (slot_range[:, None] == flat_slot[None, :]).astype(jnp.bfloat16)
+    across = (relative - 1) * capacity + slot_rank
+    late = (experts - 1) * capacity + slot_rank - first
+
+    def one_hot(rows, index, chosen):
+        index = jnp.where(chosen & (slot_rank < capacity), index, -1)
+        return (jnp.arange(rows, dtype=jnp.int32)[:, None] == index[None, :]).astype(jnp.bfloat16)
+
+    picks = [
+        one_hot(first, slot_rank, (relative == 0) & (slot_rank < first)),
+        one_hot(rest, late, (relative == 0) & (slot_rank >= first)),
+    ] + [one_hot(rest, across, relative == s) for s in range(1, experts)]
 
     gated = summed_grads(attn_partials, gate)
     both = jnp.concatenate([tokens, gated], axis=1)
-    packed = jnp.dot(dispatch, both, preferred_element_type=jnp.float32).astype(jnp.bfloat16)
-    packed = packed.reshape(experts, capacity, 2 * width)
-    arrived = [packed[0]] + [shifted(packed[s], s) for s in range(1, experts)]
-    own_rows = jnp.concatenate(arrived, axis=0)
-    rows = lax.all_gather(own_rows, "expert", axis=0, tiled=True, axis_index_groups=groups)
-    expert_rows = rows[:, :width]
-    grad_rows = rows[:, width:]
-
-    weights_in = whole_weights(w_in)
-    weights_out = whole_weights(w_out)
-    pre_act = jnp.dot(expert_rows, weights_in, preferred_element_type=jnp.float32) * scale_in
-    hidden = gelu_value(pre_act).astype(jnp.bfloat16)
-    hidden_grad = jnp.dot(grad_rows, weights_out, preferred_element_type=jnp.float32) * scale_out
-    pre_grad = (hidden_grad * gelu_slope(pre_act)).astype(jnp.bfloat16)
-    partial_x = (contract_cols(pre_grad, weights_in) * scale_in).astype(jnp.bfloat16)
-    sums = lax.psum_scatter(
-        partial_x, "expert", scatter_dimension=0, tiled=True, axis_index_groups=groups
-    ).reshape(experts, capacity, width)
-    back = [sums[0]] + [shifted(sums[s], -s) for s in range(1, experts)]
-    slot_sums = jnp.concatenate(back, axis=0)
-    token_grad = contract_rows(dispatch, slot_sums).astype(jnp.bfloat16)
-    new_w_in = stepped(w_in, contract_rows(expert_rows, pre_grad) * scale_in)
-    new_w_out = stepped(w_out, contract_rows(grad_rows, hidden) * scale_out)
-    return (token_grad, new_w_in, new_w_out)
+    packed = [
+        jnp.dot(pick, both, preferred_element_type=jnp.float32).astype(jnp.bfloat16)
+        for pick in picks
+    ]
+    early_rows = gather(packed[0])
+    late_own = packed[1]
+    for s in range(1, experts):
+        late_own = late_own + shifted(packed[s + 1], s)
+    late_rows = gather(late_own)
+
+    def paired(weights):
+        own = whole_weights(weights).T
+        return jnp.concatenate([own, swap(own, core_bit)], axis=0)
+
+    weights_in, weights_out = paired(w_in), paired(w_out)
+
+    def worked(rows):
+        expert_rows, grad_rows = rows[:, :width], rows[:, width:]
+        pre_act = contract_cols(expert_rows, weights_in) * scale_in
+        hidden = gelu_value(pre_act).astype(jnp.bfloat16)
+        hidden_grad = contract_cols(grad_rows, weights_out) * scale_out
+        pre_grad = (hidden_grad * gelu_slope(pre_act)).astype(jnp.bfloat16)
+        partial_x = jnp.dot(pre_grad, weights_in, preferred_element_type=jnp.float32) * scale_in
+        return expert_rows, grad_rows, hidden, pre_grad, partial_x.astype(jnp.bfloat16)
+
+    early, later = worked(early_rows), worked(late_rows)
+    early_sum, late_sum = scatter_sum(early[4]), scatter_sum(later[4])
+    returned = [early_sum, late_sum] + [shifted(late_sum, -s) for s in range(1, experts)]
+    token_grad = sum(contract_rows(pick, rows) for pick, rows in zip(picks, returned))
+
+    def step(weights, left, right, scale):
+        theirs = sum(contract_rows(e[left][:, units:], e[right]) for e in (early, later)) * scale
+        theirs = swap(theirs.astype(jnp.bfloat16), core_bit)
+        mine = sum(contract_rows(e[left][:, :units], e[right]) for e in (early, later)) * scale
+        return stepped(weights, (mine + theirs.astype(jnp.float32)).T)
+
+    new_w_in = step(w_in, 3, 0, scale_in)
+    new_w_out = step(w_out, 2, 1, scale_out)
+    return (token_grad.astype(jnp.bfloat16), new_w_in, new_w_out)
 
 
 def solution(mesh):

time: 149 us -> 100 us (0.67)
  waiting for transfers between devices: 102 us -> 41.5 us
  starting transfers between devices: 6.77 us -> 34 us
  between operations: 14.1 us -> 1.12 us
  matrix products: 20.6 us -> 18.1 us
  local copies, waits for them, and re-layouts: 1.96 us -> 0.26 us
  other arithmetic: 3.54 us -> 5.17 us
    reduce_scatter x1 -> x0, waiting for transfers between devices: 54.1 us -> none  [shards(): lax.psum_scatter(partial_x, 'expert', scatter_dimension=0, tiled=True, ax...]
    all_gather x1 -> x0, waiting for transfers between devices: 38.4 us -> none  [shards(): lax.all_gather(own_rows, 'expert', axis=0, tiled=True, axis_index_groups=...]
    ppermute x0 -> x40, waiting for transfers between devices: none -> 31.8 us  [swap(): lax.ppermute(rows, 'expert', [(i, i ^ mask) for i in range(n_expert)])]
    ppermute x0 -> x40, starting transfers between devices: none -> 31.3 us  [swap(): lax.ppermute(rows, 'expert', [(i, i ^ mask) for i in range(n_expert)])]
    ppermute x2, starting transfers between devices: 6.69 us -> 2.72 us  [shifted(): return lax.ppermute(rows, 'expert', pairs)]
    dot_general x3 -> x5, matrix products: 6.72 us -> 4.04 us  [the longest x3 2.63 us: shards(): jnp.dot(pick, both, preferred_element_type=jnp.float32).astype(jnp.bfloat16)]
    transpose x0 -> x2, other arithmetic: none -> 2.11 us  [paired(): own = whole_weights(weights).T]
    dot_general x1 -> x4, matrix products: 3.05 us -> 4.37 us  [contract_cols(): lax.dot_general(left, right, (((1,), (1,)), ((), ())), preferred_element_...]
  transfers between devices with their start and end apart: 4 -> 42, of which waited for: 3 -> 23; matrix products, arithmetic and copies ran while one was open for 7% -> 10% of each run, Pallas kernels for 0% -> 0%
where the time goes in v2:
time: 100 us
  waiting for transfers between devices  41.5 us (42%)
  starting transfers between devices  34 us (34%)
  matrix products  18.1 us (18%)
  other arithmetic  5.17 us (5%)
  between operations  1.12 us (1%)
    ppermute x40, waiting for transfers between devices, swap(): lax.ppermute(rows, 'expert', [(i, i ^ mask) for i in range(n_expert)])  31.8 us
    ppermute x40, starting transfers between devices, swap(): lax.ppermute(rows, 'expert', [(i, i ^ mask) for i in range(n_expert)])  31.3 us
    ppermute x2, waiting for transfers between devices, shifted(): return lax.ppermute(rows, 'expert', pairs)  9.71 us
    dot_general x11, matrix products, contract_rows(): lax.dot_general(left, right, (((0,), (0,)), ((), ())), preferred_element_...  9.66 us
    dot_general x4, matrix products, contract_cols(): lax.dot_general(left, right, (((1,), (1,)), ((), ())), preferred_element_...  4.37 us
    ppermute x2, starting transfers between devices, shifted(): return lax.ppermute(rows, 'expert', pairs)  2.72 us
    dot_general x3, matrix products, shards(): jnp.dot(pick, both, preferred_element_type=jnp.float32).astype(jnp.bfloat16)  2.63 us
    transpose x2, other arithmetic, paired(): own = whole_weights(weights).T  2.11 us
  transfers between devices with their start and end apart: 42, of which 23 were waited for; matrix products, arithmetic and copies ran while one was open for 10% of the time, Pallas kernels for 0%

profile of v2, /device:TPU:0, one launch (start us, length us, event | category | flops | bytes accessed | tf_op | source)
XLA Modules:
  0.0 100.1 jit_solution(5405130891544565734)
XLA Ops:
  4.7 3.1 %collective-permute-start.2 = (bf16[16,4096]{1,0:T(8,128)(2,1)S(1)}, bf16[16,4096]{1,0:T(8,128)(2,1)S(1)}, u32[]{:S(2)}, u32[]{:S(2)}) collective-permute-start(bf16[16,4096]{1,0:T(8,128)(2,1)S(1)} %get-tuple-element.29), channel_id=1, source_target_pairs={{0,8},{1,9},{2,10},{3,11},{4,12},{5,13},{6,14},{7,15},{8,0},{9,1},... | collective-permute-start | bytes 393224 | tf_op jit(solution)/shard_map/ppermute | solution.py:68
  7.8 1.5 %collective-permute-start.1 = (bf16[16,4096]{1,0:T(8,128)(2,1)S(1)}, bf16[16,4096]{1,0:T(8,128)(2,1)S(1)}, u32[]{:S(2)}, u32[]{:S(2)}) collective-permute-start(bf16[16,4096]{1,0:T(8,128)(2,1)S(1)} %get-tuple-element.29), channel_id=1, source_target_pairs={{0,4},{1,5},{2,6},{3,7},{4,0},{5,1},{6,2},{7,3},{8,12},{9,13},{10,... | collective-permute-start | bytes 393224 | tf_op jit(solution)/shard_map/ppermute | solution.py:68
  12.0 2.7 %collective-permute-start.20 = (bf16[24,4096]{1,0:T(8,128)(2,1)S(1)}, bf16[24,4096]{1,0:T(8,128)(2,1)S(1)}, u32[]{:S(2)}, u32[]{:S(2)}) collective-permute-start(bf16[24,4096]{1,0:T(8,128)(2,1)S(1)} %convolution_convert_fusion), channel_id=1, source_target_pairs={{0,16},{1,17},{2,18},{3,19},{4,20},{5,21},{6,22},{7,23},{8,24},{9,... | collective-permute-start | bytes 589832 | tf_op jit(solution)/shard_map/ppermute | solution.py:131
  14.6 1.9 %convert_bitcast_fusion.1 = bf16[320,2048]{1,0:T(8,128)(2,1)S(1)} fusion(f32[2048,320]{0,1:T(8,128)} %param.11), kind=kLoop, calls=%fused_computation.34 | loop fusion | flops 655360 | bytes 3932160 | tf_op jit(solution)/shard_map/transpose | solution.py:163
  18.4 4.5 %collective-permute-done.20 = bf16[24,4096]{1,0:T(8,128)(2,1)S(1)} collective-permute-done((bf16[24,4096]{1,0:T(8,128)(2,1)S(1)}, bf16[24,4096]{1,0:T(8,128)(2,1)S(1)}, u32[]{:S(2)}, u32[]{:S(2)}) %collective-permute-start.20) | collective-permute-done | bytes 196640 | tf_op jit(solution)/shard_map/ppermute | solution.py:131
  26.2 2.5 %collective-permute-done.3 = bf16[16,4096]{1,0:T(8,128)(2,1)S(1)} collective-permute-done((bf16[16,4096]{1,0:T(8,128)(2,1)S(1)}, bf16[16,4096]{1,0:T(8,128)(2,1)S(1)}, u32[]{:S(2)}, u32[]{:S(2)}) %collective-permute-start.3) | collective-permute-done | bytes 131104 | tf_op jit(solution)/shard_map/ppermute | solution.py:68
  29.2 1.7 %collective-permute-start.23 = (bf16[24,4096]{1,0:T(8,128)(2,1)S(1)}, bf16[24,4096]{1,0:T(8,128)(2,1)S(1)}, u32[]{:S(2)}, u32[]{:S(2)}) collective-permute-start(bf16[24,4096]{1,0:T(8,128)(2,1)S(1)} %get-tuple-element.27), channel_id=1, source_target_pairs={{0,8},{1,9},{2,10},{3,11},{4,12},{5,13},{6,14},{7,15},{8,0},{9,1},... | collective-permute-start | bytes 589832 | tf_op jit(solution)/shard_map/ppermute | solution.py:68
  31.5 1.8 %collective-permute-done.6 = bf16[16,1408]{1,0:T(8,128)(2,1)S(1)} collective-permute-done((bf16[16,1408]{1,0:T(8,128)(2,1)S(1)}, bf16[16,1408]{1,0:T(8,128)(2,1)S(1)}, u32[]{:S(2)}, u32[]{:S(2)}) %collective-permute-start.6) | collective-permute-done | bytes 45088 | tf_op jit(solution)/shard_map/ppermute | solution.py:68
  33.9 1.7 %collective-permute-done.23 = bf16[24,4096]{1,0:T(8,128)(2,1)S(1)} collective-permute-done((bf16[24,4096]{1,0:T(8,128)(2,1)S(1)}, bf16[24,4096]{1,0:T(8,128)(2,1)S(1)}, u32[]{:S(2)}, u32[]{:S(2)}) %collective-permute-start.23) | collective-permute-done | bytes 196640 | tf_op jit(solution)/shard_map/ppermute | solution.py:68
  37.1 3.4 %collective-permute-done.21 = bf16[24,4096]{1,0:T(8,128)(2,1)S(1)} collective-permute-done((bf16[24,4096]{1,0:T(8,128)(2,1)S(1)}, bf16[24,4096]{1,0:T(8,128)(2,1)S(1)}, u32[]{:S(2)}, u32[]{:S(2)}) %collective-permute-start.21) | collective-permute-done | bytes 196640 | tf_op jit(solution)/shard_map/ppermute | solution.py:68
  43.5 2.6 %collective-permute-done.24 = bf16[24,4096]{1,0:T(8,128)(2,1)S(1)} collective-permute-done((bf16[24,4096]{1,0:T(8,128)(2,1)S(1)}, bf16[24,4096]{1,0:T(8,128)(2,1)S(1)}, u32[]{:S(2)}, u32[]{:S(2)}) %collective-permute-start.24) | collective-permute-done | bytes 196640 | tf_op jit(solution)/shard_map/ppermute | solution.py:68
  47.5 2.9 %collective-permute-done.27 = bf16[24,1408]{1,0:T(8,128)(2,1)S(1)} collective-permute-done((bf16[24,1408]{1,0:T(8,128)(2,1)S(1)}, bf16[24,1408]{1,0:T(8,128)(2,1)S(1)}, u32[]{:S(2)}, u32[]{:S(2)}) %collective-permute-start.27) | collective-permute-done | bytes 67616 | tf_op jit(solution)/shard_map/ppermute | solution.py:68
  61.3 1.6 %collective-permute-start.30 = (bf16[24,768]{1,0:T(8,128)(2,1)S(1)}, bf16[24,768]{1,0:T(8,128)(2,1)S(1)}, u32[]{:S(2)}, u32[]{:S(2)}) collective-permute-start(bf16[24,768]{1,0:T(8,128)(2,1)S(1)} %get-tuple-element.6), channel_id=1, source_target_pairs={{0,8},{1,9},{2,10},{3,11},{4,12},{5,13},{6,14},{7,15},{8,0},{9,1},... | collective-permute-start | bytes 110600 | tf_op jit(solution)/shard_map/ppermute | solution.py:68
  63.0 1.7 %collective-permute-start.33 = (bf16[24,640]{1,0:T(8,128)(2,1)S(1)}, bf16[24,640]{1,0:T(8,128)(2,1)S(1)}, u32[]{:S(2)}, u32[]{:S(2)}) collective-permute-start(bf16[24,640]{1,0:T(8,128)(2,1)S(1)} %get-tuple-element.10), channel_id=1, source_target_pairs={{0,2},{1,3},{2,0},{3,1},{4,6},{5,7},{6,4},{7,5},{8,10},{9,11},{10,... | collective-permute-start | bytes 92168 | tf_op jit(solution)/shard_map/ppermute | solution.py:68
  66.9 1.7 %collective-permute-done.36 = bf16[24,640]{1,0:T(8,128)(2,1)S(1)} collective-permute-done((bf16[24,640]{1,0:T(8,128)(2,1)S(1)}, bf16[24,640]{1,0:T(8,128)(2,1)S(1)}, u32[]{:S(2)}, u32[]{:S(2)}) %collective-permute-start.36) | collective-permute-done | bytes 30752 | tf_op jit(solution)/shard_map/ppermute | solution.py:68
  69.5 1.8 %collective-permute-start.31 = (bf16[24,2048]{1,0:T(8,128)(2,1)S(1)}, bf16[24,2048]{1,0:T(8,128)(2,1)S(1)}, u32[]{:S(2)}, u32[]{:S(2)}) collective-permute-start(bf16[24,2048]{1,0:T(8,128)(2,1)S(1)} %pad_maximum_fusion.20), channel_id=1, source_target_pairs={{0,4},{1,5},{2,6},{3,7},{4,0},{5,1},{6,2},{7,3},{8,12},{9,13},{10,... | collective-permute-start | bytes 294920 | tf_op jit(solution)/shard_map/ppermute | solution.py:68
  71.3 2.3 %collective-permute-done.37 = bf16[24,2048]{1,0:T(8,128)(2,1)S(1)} collective-permute-done((bf16[24,2048]{1,0:T(8,128)(2,1)S(1)}, bf16[24,2048]{1,0:T(8,128)(2,1)S(1)}, u32[]{:S(2)}, u32[]{:S(2)}) %collective-permute-start.37) | collective-permute-done | bytes 98336 | tf_op jit(solution)/shard_map/ppermute | solution.py:68
  74.8 1.7 %collective-permute-start.12 = (bf16[16,2048]{1,0:T(8,128)(2,1)S(1)}, bf16[16,2048]{1,0:T(8,128)(2,1)S(1)}, u32[]{:S(2)}, u32[]{:S(2)}) collective-permute-start(bf16[16,2048]{1,0:T(8,128)(2,1)S(1)} %pad_maximum_fusion.23), channel_id=1, source_target_pairs={{0,4},{1,5},{2,6},{3,7},{4,0},{5,1},{6,2},{7,3},{8,12},{9,13},{10,... | collective-permute-start | bytes 196616 | tf_op jit(solution)/shard_map/ppermute | solution.py:68
  76.6 1.9 %collective-permute-done.18 = bf16[16,2048]{1,0:T(8,128)(2,1)S(1)} collective-permute-done((bf16[16,2048]{1,0:T(8,128)(2,1)S(1)}, bf16[16,2048]{1,0:T(8,128)(2,1)S(1)}, u32[]{:S(2)}, u32[]{:S(2)}) %collective-permute-start.18) | collective-permute-done | bytes 65568 | tf_op jit(solution)/shard_map/ppermute | solution.py:68
  80.9 2.2 %collective-permute-done.32 = bf16[24,2048]{1,0:T(8,128)(2,1)S(1)} collective-permute-done((bf16[24,2048]{1,0:T(8,128)(2,1)S(1)}, bf16[24,2048]{1,0:T(8,128)(2,1)S(1)}, u32[]{:S(2)}, u32[]{:S(2)}) %collective-permute-start.32) | collective-permute-done | bytes 98336 | tf_op jit(solution)/shard_map/ppermute | solution.py:68
  85.0 5.2 %collective-permute-done.39 = bf16[24,2048]{1,0:T(8,128)(2,1)S(1)} collective-permute-done((bf16[24,2048]{1,0:T(8,128)(2,1)S(1)}, bf16[24,2048]{1,0:T(8,128)(2,1)S(1)}, u32[]{:S(2)}, u32[]{:S(2)}) %collective-permute-start.39) | collective-permute-done | bytes 98336 | tf_op jit(solution)/shard_map/ppermute | solution.py:131
  91.6 2.9 %collective-permute-done.16 = bf16[16,2048]{1,0:T(8,128)(2,1)S(1)} collective-permute-done((bf16[16,2048]{1,0:T(8,128)(2,1)S(1)}, bf16[16,2048]{1,0:T(8,128)(2,1)S(1)}, u32[]{:S(2)}, u32[]{:S(2)}) %collective-permute-start.16) | collective-permute-done | bytes 65568 | tf_op jit(solution)/shard_map/ppermute | solution.py:68
  95.5 2.3 %fusion.12 = f32[2048,320]{0,1:T(8,128)} fusion(f32[2048,320]{0,1:T(8,128)S(1)} %copy-done, f32[320,2048]{1,0:T(8,128)S(1)} %fusion.29, bf16[320,2048]{1,0:T(8,128)(2,1)S(1)} %collective-permute-done.40, bf16[128,4096]{1,0:T(8,128)(2,1)S(1)} %maximum_dynamic-update-slice_fusion.1, bf16[128,640]{1,0:T(8,128)(2,1)S(1)} %fusion.26), kind=kOutput, calls=%fused_computation.19 | convolution fusion | flops 171704320 | bytes 9797632 | tf_op jit(solution)/shard_map/dot_general | solution.py:31
  97.8 2.3 %fusion.6 = f32[2048,320]{0,1:T(8,128)} fusion(f32[2048,320]{0,1:T(8,128)S(1)} %copy-done.1, f32[320,2048]{1,0:T(8,128)S(1)} %fusion.35, bf16[320,2048]{1,0:T(8,128)(2,1)S(1)} %collective-permute-done.41, bf16[128,4096]{1,0:T(8,128)(2,1)S(1)} %maximum_dynamic-update-slice_fusion.1, bf16[128,640]{1,0:T(8,128)(2,1)S(1)} %get-tuple-element.32), kind=kOutput, calls=%fused_computation.11 | convolution fusion | flops 171704320 | bytes 9797632 | tf_op jit(solution)/shard_map/dot_general | solution.py:31
  (135 shorter events, 40.7 us)
Async XLA Ops:
  4.7 12.1 %collective-permute-start.2 = (bf16[16,4096]{1,0:T(8,128)(2,1)S(1)}, bf16[16,4096]{1,0:T(8,128)(2,1)S(1)}, u32[]{:S(2)}, u32[]{:S(2)}) collective-permute-start(bf16[16,4096]{1,0:T(8,128)(2,1)S(1)} %get-tuple-element.29), channel_id=1, source_target_pairs={{0,8},{1,9},{2,10},{3,11},{4,12},{5,13},{6,14},{7,15},{8,0},{9,1},... | collective-permute-start | bytes 393224 | tf_op jit(solution)/shard_map/ppermute | solution.py:68
  7.8 9.6 %collective-permute-start.1 = (bf16[16,4096]{1,0:T(8,128)(2,1)S(1)}, bf16[16,4096]{1,0:T(8,128)(2,1)S(1)}, u32[]{:S(2)}, u32[]{:S(2)}) collective-permute-start(bf16[16,4096]{1,0:T(8,128)(2,1)S(1)} %get-tuple-element.29), channel_id=1, source_target_pairs={{0,4},{1,5},{2,6},{3,7},{4,0},{5,1},{6,2},{7,3},{8,12},{9,13},{10,... | collective-permute-start | bytes 393224 | tf_op jit(solution)/shard_map/ppermute | solution.py:68
  9.3 8.6 %collective-permute-start = (bf16[16,4096]{1,0:T(8,128)(2,1)S(1)}, bf16[16,4096]{1,0:T(8,128)(2,1)S(1)}, u32[]{:S(2)}, u32[]{:S(2)}) collective-permute-start(bf16[16,4096]{1,0:T(8,128)(2,1)S(1)} %get-tuple-element.29), channel_id=1, source_target_pairs={{0,2},{1,3},{2,0},{3,1},{4,6},{5,7},{6,4},{7,5},{8,10},{9,11},{10,... | collective-permute-start | bytes 393224 | tf_op jit(solution)/shard_map/ppermute | solution.py:68
  12.0 11.0 %collective-permute-start.20 = (bf16[24,4096]{1,0:T(8,128)(2,1)S(1)}, bf16[24,4096]{1,0:T(8,128)(2,1)S(1)}, u32[]{:S(2)}, u32[]{:S(2)}) collective-permute-start(bf16[24,4096]{1,0:T(8,128)(2,1)S(1)} %convolution_convert_fusion), channel_id=1, source_target_pairs={{0,16},{1,17},{2,18},{3,19},{4,20},{5,21},{6,22},{7,23},{8,24},{9,... | collective-permute-start | bytes 589832 | tf_op jit(solution)/shard_map/ppermute | solution.py:131
  16.6 35.1 %collective-permute-start.9 = (bf16[320,2048]{1,0:T(8,128)(2,1)S(1)}, bf16[320,2048]{1,0:T(8,128)(2,1)S(1)}, u32[]{:S(2)}, u32[]{:S(2)}) collective-permute-start(bf16[320,2048]{1,0:T(8,128)(2,1)S(1)} %convert_bitcast_fusion.1), channel_id=1, source_target_pairs={{0,1},{1,0},{2,3},{3,2},{4,5},{5,4},{6,7},{7,6},{8,9},{9,8},{10,11... | collective-permute-start | bytes 3932168 | tf_op jit(solution)/shard_map/ppermute | solution.py:68
  16.9 33.6 %collective-permute-start.10 = (bf16[320,2048]{1,0:T(8,128)(2,1)S(1)}, bf16[320,2048]{1,0:T(8,128)(2,1)S(1)}, u32[]{:S(2)}, u32[]{:S(2)}) collective-permute-start(bf16[320,2048]{1,0:T(8,128)(2,1)S(1)} %convert_bitcast_fusion), channel_id=1, source_target_pairs={{0,1},{1,0},{2,3},{3,2},{4,5},{5,4},{6,7},{7,6},{8,9},{9,8},{10,11... | collective-permute-start | bytes 3932168 | tf_op jit(solution)/shard_map/ppermute | solution.py:68
  17.4 6.3 %collective-permute-start.5 = (bf16[16,4096]{1,0:T(8,128)(2,1)S(1)}, bf16[16,4096]{1,0:T(8,128)(2,1)S(1)}, u32[]{:S(2)}, u32[]{:S(2)}) collective-permute-start(bf16[16,4096]{1,0:T(8,128)(2,1)S(1)} %collective-permute-done.2), channel_id=1, source_target_pairs={{0,2},{1,3},{2,0},{3,1},{4,6},{5,7},{6,4},{7,5},{8,10},{9,11},{10,... | collective-permute-start | bytes 393224 | tf_op jit(solution)/shard_map/ppermute | solution.py:68
  17.9 7.7 %collective-permute-start.4 = (bf16[16,4096]{1,0:T(8,128)(2,1)S(1)}, bf16[16,4096]{1,0:T(8,128)(2,1)S(1)}, u32[]{:S(2)}, u32[]{:S(2)}) collective-permute-start(bf16[16,4096]{1,0:T(8,128)(2,1)S(1)} %collective-permute-done.1), channel_id=1, source_target_pairs={{0,8},{1,9},{2,10},{3,11},{4,12},{5,13},{6,14},{7,15},{8,0},{9,1},... | collective-permute-start | bytes 393224 | tf_op jit(solution)/shard_map/ppermute | solution.py:68
  22.9 5.8 %collective-permute-start.3 = (bf16[16,4096]{1,0:T(8,128)(2,1)S(1)}, bf16[16,4096]{1,0:T(8,128)(2,1)S(1)}, u32[]{:S(2)}, u32[]{:S(2)}) collective-permute-start(bf16[16,4096]{1,0:T(8,128)(2,1)S(1)} %collective-permute-done), channel_id=1, source_target_pairs={{0,4},{1,5},{2,6},{3,7},{4,0},{5,1},{6,2},{7,3},{8,12},{9,13},{10,... | collective-permute-start | bytes 393224 | tf_op jit(solution)/shard_map/ppermute | solution.py:68
  29.2 6.4 %collective-permute-start.23 = (bf16[24,4096]{1,0:T(8,128)(2,1)S(1)}, bf16[24,4096]{1,0:T(8,128)(2,1)S(1)}, u32[]{:S(2)}, u32[]{:S(2)}) collective-permute-start(bf16[24,4096]{1,0:T(8,128)(2,1)S(1)} %get-tuple-element.27), channel_id=1, source_target_pairs={{0,8},{1,9},{2,10},{3,11},{4,12},{5,13},{6,14},{7,15},{8,0},{9,1},... | collective-permute-start | bytes 589832 | tf_op jit(solution)/shard_map/ppermute | solution.py:68
  30.9 5.7 %collective-permute-start.22 = (bf16[24,4096]{1,0:T(8,128)(2,1)S(1)}, bf16[24,4096]{1,0:T(8,128)(2,1)S(1)}, u32[]{:S(2)}, u32[]{:S(2)}) collective-permute-start(bf16[24,4096]{1,0:T(8,128)(2,1)S(1)} %get-tuple-element.27), channel_id=1, source_target_pairs={{0,4},{1,5},{2,6},{3,7},{4,0},{5,1},{6,2},{7,3},{8,12},{9,13},{10,... | collective-permute-start | bytes 589832 | tf_op jit(solution)/shard_map/ppermute | solution.py:68
  33.3 7.2 %collective-permute-start.21 = (bf16[24,4096]{1,0:T(8,128)(2,1)S(1)}, bf16[24,4096]{1,0:T(8,128)(2,1)S(1)}, u32[]{:S(2)}, u32[]{:S(2)}) collective-permute-start(bf16[24,4096]{1,0:T(8,128)(2,1)S(1)} %get-tuple-element.27), channel_id=1, source_target_pairs={{0,2},{1,3},{2,0},{3,1},{4,6},{5,7},{6,4},{7,5},{8,10},{9,11},{10,... | collective-permute-start | bytes 589832 | tf_op jit(solution)/shard_map/ppermute | solution.py:68
  35.6 7.0 %collective-permute-start.26 = (bf16[24,4096]{1,0:T(8,128)(2,1)S(1)}, bf16[24,4096]{1,0:T(8,128)(2,1)S(1)}, u32[]{:S(2)}, u32[]{:S(2)}) collective-permute-start(bf16[24,4096]{1,0:T(8,128)(2,1)S(1)} %collective-permute-done.23), channel_id=1, source_target_pairs={{0,2},{1,3},{2,0},{3,1},{4,6},{5,7},{6,4},{7,5},{8,10},{9,11},{10,... | collective-permute-start | bytes 589832 | tf_op jit(solution)/shard_map/ppermute | solution.py:68
  36.6 6.6 %collective-permute-start.25 = (bf16[24,4096]{1,0:T(8,128)(2,1)S(1)}, bf16[24,4096]{1,0:T(8,128)(2,1)S(1)}, u32[]{:S(2)}, u32[]{:S(2)}) collective-permute-start(bf16[24,4096]{1,0:T(8,128)(2,1)S(1)} %collective-permute-done.22), channel_id=1, source_target_pairs={{0,8},{1,9},{2,10},{3,11},{4,12},{5,13},{6,14},{7,15},{8,0},{9,1},... | collective-permute-start | bytes 589832 | tf_op jit(solution)/shard_map/ppermute | solution.py:68
  40.5 5.7 %collective-permute-start.24 = (bf16[24,4096]{1,0:T(8,128)(2,1)S(1)}, bf16[24,4096]{1,0:T(8,128)(2,1)S(1)}, u32[]{:S(2)}, u32[]{:S(2)}) collective-permute-start(bf16[24,4096]{1,0:T(8,128)(2,1)S(1)} %collective-permute-done.21), channel_id=1, source_target_pairs={{0,4},{1,5},{2,6},{3,7},{4,0},{5,1},{6,2},{7,3},{8,12},{9,13},{10,... | collective-permute-start | bytes 589832 | tf_op jit(solution)/shard_map/ppermute | solution.py:68
  58.7 6.0 %collective-permute-start.14 = (bf16[16,640]{1,0:T(8,128)(2,1)S(1)}, bf16[16,640]{1,0:T(8,128)(2,1)S(1)}, u32[]{:S(2)}, u32[]{:S(2)}) collective-permute-start(bf16[16,640]{1,0:T(8,128)(2,1)S(1)} %get-tuple-element.20), channel_id=1, source_target_pairs={{0,2},{1,3},{2,0},{3,1},{4,6},{5,7},{6,4},{7,5},{8,10},{9,11},{10,... | collective-permute-start | bytes 61448 | tf_op jit(solution)/shard_map/ppermute | solution.py:68
  59.2 7.0 %collective-permute-start.17 = (bf16[16,640]{1,0:T(8,128)(2,1)S(1)}, bf16[16,640]{1,0:T(8,128)(2,1)S(1)}, u32[]{:S(2)}, u32[]{:S(2)}) collective-permute-start(bf16[16,640]{1,0:T(8,128)(2,1)S(1)} %get-tuple-element.21), channel_id=1, source_target_pairs={{0,4},{1,5},{2,6},{3,7},{4,0},{5,1},{6,2},{7,3},{8,12},{9,13},{10,... | collective-permute-start | bytes 61448 | tf_op jit(solution)/shard_map/ppermute | solution.py:68
  61.3 8.1 %collective-permute-start.30 = (bf16[24,768]{1,0:T(8,128)(2,1)S(1)}, bf16[24,768]{1,0:T(8,128)(2,1)S(1)}, u32[]{:S(2)}, u32[]{:S(2)}) collective-permute-start(bf16[24,768]{1,0:T(8,128)(2,1)S(1)} %get-tuple-element.6), channel_id=1, source_target_pairs={{0,8},{1,9},{2,10},{3,11},{4,12},{5,13},{6,14},{7,15},{8,0},{9,1},... | collective-permute-start | bytes 110600 | tf_op jit(solution)/shard_map/ppermute | solution.py:68
  66.2 29.3 %collective-permute-start.40 = (bf16[320,2048]{1,0:T(8,128)(2,1)S(1)}, bf16[320,2048]{1,0:T(8,128)(2,1)S(1)}, u32[]{:S(2)}, u32[]{:S(2)}) collective-permute-start(bf16[320,2048]{1,0:T(8,128)(2,1)S(1)} %fusion.13), channel_id=1, source_target_pairs={{0,1},{1,0},{2,3},{3,2},{4,5},{5,4},{6,7},{7,6},{8,9},{9,8},{10,11... | collective-permute-start | bytes 3932168 | tf_op jit(solution)/shard_map/ppermute | solution.py:68
  66.3 31.5 %collective-permute-start.41 = (bf16[320,2048]{1,0:T(8,128)(2,1)S(1)}, bf16[320,2048]{1,0:T(8,128)(2,1)S(1)}, u32[]{:S(2)}, u32[]{:S(2)}) collective-permute-start(bf16[320,2048]{1,0:T(8,128)(2,1)S(1)} %fusion.14), channel_id=1, source_target_pairs={{0,1},{1,0},{2,3},{3,2},{4,5},{5,4},{6,7},{7,6},{8,9},{9,8},{10,11... | collective-permute-start | bytes 3932168 | tf_op jit(solution)/shard_map/ppermute | solution.py:68
  78.9 5.7 %collective-permute-start.38 = (bf16[24,2048]{1,0:T(8,128)(2,1)S(1)}, bf16[24,2048]{1,0:T(8,128)(2,1)S(1)}, u32[]{:S(2)}, u32[]{:S(2)}) collective-permute-start(bf16[24,2048]{1,0:T(8,128)(2,1)S(1)} %get-tuple-element.4), channel_id=1, source_target_pairs={{0,8},{1,9},{2,10},{3,11},{4,12},{5,13},{6,14},{7,15},{8,0},{9,1},... | collective-permute-start | bytes 294920 | tf_op jit(solution)/shard_map/ppermute | solution.py:68
  83.1 8.4 %collective-permute-start.13 = (bf16[16,2048]{1,0:T(8,128)(2,1)S(1)}, bf16[16,2048]{1,0:T(8,128)(2,1)S(1)}, u32[]{:S(2)}, u32[]{:S(2)}) collective-permute-start(bf16[16,2048]{1,0:T(8,128)(2,1)S(1)} %get-tuple-element.13), channel_id=1, source_target_pairs={{0,2},{1,3},{2,0},{3,1},{4,6},{5,7},{6,4},{7,5},{8,10},{9,11},{10,... | collective-permute-start | bytes 196616 | tf_op jit(solution)/shard_map/ppermute | solution.py:68
  84.5 7.0 %collective-permute-start.19 = (bf16[16,2048]{1,0:T(8,128)(2,1)S(1)}, bf16[16,2048]{1,0:T(8,128)(2,1)S(1)}, u32[]{:S(2)}, u32[]{:S(2)}) collective-permute-start(bf16[16,2048]{1,0:T(8,128)(2,1)S(1)} %get-tuple-element.14), channel_id=1, source_target_pairs={{0,8},{1,9},{2,10},{3,11},{4,12},{5,13},{6,14},{7,15},{8,0},{9,1},... | collective-permute-start | bytes 196616 | tf_op jit(solution)/shard_map/ppermute | solution.py:68
  84.6 5.6 %collective-permute-start.39 = (bf16[24,2048]{1,0:T(8,128)(2,1)S(1)}, bf16[24,2048]{1,0:T(8,128)(2,1)S(1)}, u32[]{:S(2)}, u32[]{:S(2)}) collective-permute-start(bf16[24,2048]{1,0:T(8,128)(2,1)S(1)} %add_convert_fusion), channel_id=1, source_target_pairs={{0,16},{1,17},{2,18},{3,19},{4,20},{5,21},{6,22},{7,23},{8,24},{9,... | collective-permute-start | bytes 294920 | tf_op jit(solution)/shard_map/ppermute | solution.py:131
  (21 other events, 107.4 us)

commit v3 on v2

--- a/solution.py
+++ b/solution.py
@@ -68,51 +68,33 @@
     return lax.ppermute(rows, "expert", [(i, i ^ mask) for i in range(n_expert)])
 
 
-core_bit, x_bit, y_bit, z_bit = 1, 2, 4, 8
+core_bit = 1
 
 
-def thirds(columns):
-    lanes = columns // 128
-    first = (lanes + 2) // 3 * 128
-    second = first + (lanes + 1) // 3 * 128
-    return (0, first), (first, second), (second, columns)
+def same_core():
+    n_expert = lax.axis_size("expert")
+    return [
+        [e * SHARDS + k for k in range(c, SHARDS, 2)]
+        for e in range(n_expert // SHARDS)
+        for c in range(2)
+    ]
+
+
+def exchange(blocks):
+    return lax.all_to_all(
+        blocks, "expert", split_axis=0, concat_axis=0, tiled=True, axis_index_groups=same_core()
+    )
 
 
 def gather(own):
-    near_x, near_y, near_z = swap(own, x_bit), swap(own, y_bit), swap(own, z_bit)
-    xy, yz, zx = swap(near_x, y_bit), swap(near_y, z_bit), swap(near_z, x_bit)
-    (a0, a1), (b0, b1), (c0, c1) = thirds(own.shape[1])
-    far = jnp.concatenate(
-        [swap(xy[:, a0:a1], z_bit), swap(yz[:, b0:b1], x_bit), swap(zx[:, c0:c1], y_bit)], axis=1
-    )
-    return jnp.concatenate([own, near_x, near_y, near_z, xy, yz, zx, far], axis=0)
-
-
-def added(left, right):
-    return (left.astype(jnp.float32) + right.astype(jnp.float32)).astype(jnp.bfloat16)
+    rows, columns = own.shape
+    blocks = exchange(jnp.broadcast_to(own[None], (SHARDS // 2, rows, columns)))
+    return blocks.reshape(SHARDS // 2 * rows, columns)
 
 
 def scatter_sum(parts):
-    rows = parts.shape[0] // 8
-    own, near_x, near_y, near_z, xy, yz, zx, far = [
-        parts[k * rows : (k + 1) * rows] for k in range(8)
-    ]
-    (a0, a1), (b0, b1), (c0, c1) = thirds(parts.shape[1])
-    far_a, far_b, far_c = (
-        swap(far[:, a0:a1], z_bit),
-        swap(far[:, b0:b1], x_bit),
-        swap(far[:, c0:c1], y_bit),
-    )
-    xy = jnp.concatenate([added(xy[:, a0:a1], far_a), xy[:, a1:]], axis=1)
-    yz = jnp.concatenate([yz[:, :b0], added(yz[:, b0:b1], far_b), yz[:, b1:]], axis=1)
-    zx = jnp.concatenate([zx[:, :c0], added(zx[:, c0:c1], far_c)], axis=1)
-    near_x = added(near_x, swap(xy, y_bit))
-    near_y = added(near_y, swap(yz, z_bit))
-    near_z = added(near_z, swap(zx, x_bit))
-    total = own.astype(jnp.float32) + swap(near_x, x_bit).astype(jnp.float32)
-    total = total + swap(near_y, y_bit).astype(jnp.float32)
-    total = total + swap(near_z, z_bit).astype(jnp.float32)
-    return total.astype(jnp.bfloat16)
+    blocks = exchange(parts.reshape(SHARDS // 2, -1, parts.shape[1]))
+    return jnp.sum(blocks.astype(jnp.float32), axis=0).astype(jnp.bfloat16)
 
 
 def shards(tokens, attn_partials, expert_ids, gate, w_in, w_out):

time: 100 us -> 103 us (1.030); the launches traced: 100 us -> 102 us
  matrix products: 18.1 us -> 44.2 us
  waiting for transfers between devices: 41.5 us -> 23.5 us
  starting transfers between devices: 34 us -> 23.7 us
  local copies, waits for them, and re-layouts: 0.26 us -> 3.33 us
  other arithmetic: 5.17 us -> 6.32 us
    ppermute x40 -> x4, waiting for transfers between devices: 31.8 us -> 0.01 us  [swap(): lax.ppermute(rows, 'expert', [(i, i ^ mask) for i in range(n_expert)])]
    ppermute x40 -> x4, starting transfers between devices: 31.3 us -> 0.24 us  [swap(): lax.ppermute(rows, 'expert', [(i, i ^ mask) for i in range(n_expert)])]
    all_to_all x0 -> x4, starting transfers between devices: none -> 20.4 us  [exchange(): lax.all_to_all(blocks, 'expert', split_axis=0, concat_axis=0, tiled=True,...]
    dot_general x11, matrix products: 9.66 us -> 26.3 us  [contract_rows(): lax.dot_general(left, right, (((0,), (0,)), ((), ())), preferred_element_...]
    ppermute x2, waiting for transfers between devices: 9.71 us -> 18.6 us  [shifted(): return lax.ppermute(rows, 'expert', pairs)]
    dot_general x4, matrix products: 4.37 us -> 9.87 us  [contract_cols(): lax.dot_general(left, right, (((1,), (1,)), ((), ())), preferred_element_...]
    dot_general x2, matrix products: 1.41 us -> 6.51 us  [worked(): jnp.dot(pre_grad, weights_in, preferred_element_type=jnp.float32) * scale_in]
    all_to_all x0 -> x4, waiting for transfers between devices: none -> 4.84 us  [exchange(): lax.all_to_all(blocks, 'expert', split_axis=0, concat_axis=0, tiled=True,...]
  transfers between devices with their start and end apart: 42 -> 10, of which waited for: 23 -> 4; matrix products, arithmetic and copies ran while one was open for 10% -> 46% of each run, Pallas kernels for 0% -> 0%
where the time goes in v3:
time: 103 us; the launch traced here: 102 us
  matrix products  44.2 us (43%)
  starting transfers between devices  23.7 us (23%)
  waiting for transfers between devices  23.5 us (23%)
  other arithmetic  6.32 us (6%)
  local copies, waits for them, and re-layouts  3.33 us (3%)
    dot_general x11, matrix products, contract_rows(): lax.dot_general(left, right, (((0,), (0,)), ((), ())), preferred_element_...  26.3 us
    all_to_all x4, starting transfers between devices, exchange(): lax.all_to_all(blocks, 'expert', split_axis=0, concat_axis=0, tiled=True,...  20.4 us
    ppermute x2, waiting for transfers between devices, shifted(): return lax.ppermute(rows, 'expert', pairs)  18.6 us
    dot_general x4, matrix products, contract_cols(): lax.dot_general(left, right, (((1,), (1,)), ((), ())), preferred_element_...  9.87 us
    dot_general x2, matrix products, worked(): jnp.dot(pre_grad, weights_in, preferred_element_type=jnp.float32) * scale_in  6.51 us
    all_to_all x4, waiting for transfers between devices, exchange(): lax.all_to_all(blocks, 'expert', split_axis=0, concat_axis=0, tiled=True,...  4.84 us
    transpose x2, other arithmetic, paired(): own = whole_weights(weights).T  3.19 us
    ppermute x2, starting transfers between devices, shifted(): return lax.ppermute(rows, 'expert', pairs)  3.08 us
  transfers between devices with their start and end apart: 10, of which 4 were waited for; matrix products, arithmetic and copies ran while one was open for 46% of the time, Pallas kernels for 0%

profile of v3, /device:TPU:0, one launch (start us, length us, event | category | flops | bytes accessed | tf_op | source)
XLA Modules:
  0.0 101.9 jit_solution(5389355112220483359)
XLA Ops:
  5.8 6.2 %all-to-all-start = ((bf16[8,16,4096]{2,1,0:T(8,128)(2,1)}), bf16[8,16,4096]{2,1,0:T(8,128)(2,1)}, u32[]{:S(2)}, u32[]{:S(2)}) async-start(bf16[8,16,4096]{2,1,0:T(8,128)(2,1)} %broadcast_in_dim.11), calls=%async_computation | async-start | bytes 2097152 | tf_op jit(solution)/shard_map/all_to_all | solution.py:84
  12.2 2.7 %collective-permute-start.2 = (bf16[24,4096]{1,0:T(8,128)(2,1)S(1)}, bf16[24,4096]{1,0:T(8,128)(2,1)S(1)}, u32[]{:S(2)}, u32[]{:S(2)}) collective-permute-start(bf16[24,4096]{1,0:T(8,128)(2,1)S(1)} %convolution_convert_fusion), channel_id=1, source_target_pairs={{0,16},{1,17},{2,18},{3,19},{4,20},{5,21},{6,22},{7,23},{8,24},{9,... | collective-permute-start | bytes 589832 | tf_op jit(solution)/shard_map/ppermute | solution.py:113
  16.2 11.5 %collective-permute-done.2 = bf16[24,4096]{1,0:T(8,128)(2,1)S(1)} collective-permute-done((bf16[24,4096]{1,0:T(8,128)(2,1)S(1)}, bf16[24,4096]{1,0:T(8,128)(2,1)S(1)}, u32[]{:S(2)}, u32[]{:S(2)}) %collective-permute-start.2) | collective-permute-done | bytes 196640 | tf_op jit(solution)/shard_map/ppermute | solution.py:113
  27.8 2.5 %all-to-all-done = bf16[8,16,4096]{2,1,0:T(8,128)(2,1)} async-done(((bf16[8,16,4096]{2,1,0:T(8,128)(2,1)}), bf16[8,16,4096]{2,1,0:T(8,128)(2,1)}, u32[]{:S(2)}, u32[]{:S(2)}) %all-to-all-start) | async-done | bytes 1048608 | tf_op jit(solution)/shard_map/all_to_all | solution.py:84
  30.3 1.3 %broadcast_in_dim.12 = bf16[8,24,4096]{2,1,0:T(8,128)(2,1)} broadcast(bf16[24,4096]{1,0:T(8,128)(2,1)S(1)} %fusion), dimensions={1,2} | broadcast | bytes 1769472 | tf_op jit(solution)/shard_map/broadcast_in_dim | solution.py:91
  31.6 5.4 %all-to-all-start.2 = ((bf16[8,24,4096]{2,1,0:T(8,128)(2,1)}), bf16[8,24,4096]{2,1,0:T(8,128)(2,1)S(1)}, u32[]{:S(2)}, u32[]{:S(2)}) async-start(bf16[8,24,4096]{2,1,0:T(8,128)(2,1)} %broadcast_in_dim.12), calls=%async_computation.2 | async-start | bytes 3145728 | tf_op jit(solution)/shard_map/all_to_all | solution.py:84
  37.1 1.9 %convert_bitcast_fusion.1 = bf16[320,2048]{1,0:T(8,128)(2,1)S(1)} fusion(f32[2048,320]{0,1:T(8,128)} %param.11), kind=kLoop, calls=%fused_computation.28 | loop fusion | flops 655360 | bytes 3932160 | tf_op jit(solution)/shard_map/transpose | solution.py:145
  39.1 3.2 %multiply_convert_fusion.1 = (bf16[128,640]{1,0:T(8,128)(2,1)S(1)}, f32[128,640]{1,0:T(8,128)S(1)}) fusion(bf16[320,2048]{1,0:T(8,128)(2,1)} %collective-permute-done.1, bf16[320,2048]{1,0:T(8,128)(2,1)} %convert_bitcast_fusion, bf16[128,4096]{1,0:T(8,128)(2,1)} %bitcast.1), kind=kOutput, calls=%fused_computation.64 | convolution fusion | flops 341606400 | bytes 3637248 | tf_op jit(solution)/shard_map/dot_general | solution.py:37
  42.4 2.5 %fusion.17 = bf16[128,640]{1,0:T(8,128)(2,1)S(1)} fusion(bf16[320,2048]{1,0:T(8,128)(2,1)S(1)} %collective-permute-done, bf16[320,2048]{1,0:T(8,128)(2,1)S(1)} %convert_bitcast_fusion.1, bf16[128,4096]{1,0:T(8,128)(2,1)} %bitcast.1, f32[128,640]{1,0:T(8,128)S(1)} %get-tuple-element.7), kind=kOutput, calls=%fused_computation.34 | convolution fusion | flops 342507520 | bytes 3637248 | tf_op jit(solution)/shard_map/dot_general | solution.py:37
  44.9 3.1 %fusion.8 = bf16[128,2048]{1,0:T(8,128)(2,1)} fusion(bf16[128,640]{1,0:T(8,128)(2,1)S(1)} %fusion.17, bf16[320,2048]{1,0:T(8,128)(2,1)} %collective-permute-done.1, bf16[320,2048]{1,0:T(8,128)(2,1)} %convert_bitcast_fusion), kind=kOutput, calls=%fused_computation.21 | convolution fusion | flops 341311488 | bytes 3309568 | tf_op jit(solution)/shard_map/dot_general | solution.py:156
  48.0 3.1 %fusion.29 = f32[320,2048]{1,0:T(8,128)} fusion(bf16[128,4096]{1,0:T(8,128)(2,1)} %bitcast.1, bf16[128,640]{1,0:T(8,128)(2,1)S(1)} %fusion.17), kind=kOutput, calls=%fused_computation.51 | convolution fusion | flops 167772160 | bytes 3244032 | tf_op jit(solution)/shard_map/dot_general | solution.py:31
  51.1 3.1 %fusion.35 = f32[320,2048]{1,0:T(8,128)} fusion(bf16[128,4096]{1,0:T(8,128)(2,1)} %bitcast.1, bf16[128,640]{1,0:T(8,128)(2,1)S(1)} %get-tuple-element.6), kind=kOutput, calls=%fused_computation.57 | convolution fusion | flops 167772160 | bytes 3244032 | tf_op jit(solution)/shard_map/dot_general | solution.py:31
  54.2 2.4 %all-to-all-done.2 = bf16[8,24,4096]{2,1,0:T(8,128)(2,1)S(1)} async-done(((bf16[8,24,4096]{2,1,0:T(8,128)(2,1)}), bf16[8,24,4096]{2,1,0:T(8,128)(2,1)S(1)}, u32[]{:S(2)}, u32[]{:S(2)}) %all-to-all-start.2) | async-done | bytes 1572896 | tf_op jit(solution)/shard_map/all_to_all | solution.py:84
  56.6 3.7 %all-to-all-start.1 = ((bf16[8,16,2048]{2,1,0:T(8,128)(2,1)}), bf16[8,16,2048]{2,1,0:T(8,128)(2,1)S(1)}, u32[]{:S(2)}, u32[]{:S(2)}) async-start(bf16[8,16,2048]{2,1,0:T(8,128)(2,1)} %bitcast.4), calls=%async_computation.1 | async-start | bytes 1048576 | tf_op jit(solution)/shard_map/all_to_all | solution.py:84
  60.3 3.0 %multiply_convert_fusion = (bf16[192,640]{1,0:T(8,128)(2,1)S(1)}, f32[192,640]{1,0:T(8,128)S(1)}) fusion(bf16[320,2048]{1,0:T(8,128)(2,1)} %collective-permute-done.1, bf16[320,2048]{1,0:T(8,128)(2,1)} %convert_bitcast_fusion, bf16[192,4096]{1,0:T(8,128)(2,1)S(1)} %bitcast.20), kind=kOutput, calls=%fused_computation.48 | convolution fusion | flops 509788160 | bytes 4145152 | tf_op jit(solution)/shard_map/dot_general | solution.py:37
  65.0 1.7 %fusion.5 = bf16[320,2048]{1,0:T(8,128)(2,1)} fusion(f32[320,2048]{1,0:T(8,128)S(1)} %copy-done.1, bf16[192,4096]{1,0:T(8,128)(2,1)S(1)} %bitcast.22, bf16[192,640]{1,0:T(8,128)(2,1)S(1)} %fusion.14), kind=kOutput, calls=%fused_computation.12 | convolution fusion | flops 253624320 | bytes 4866048 | tf_op jit(solution)/shard_map/dot_general | solution.py:31
  67.1 1.7 %fusion.6 = bf16[320,2048]{1,0:T(8,128)(2,1)} fusion(f32[320,2048]{1,0:T(8,128)S(1)} %copy-done, bf16[192,4096]{1,0:T(8,128)(2,1)S(1)} %bitcast.23, bf16[192,640]{1,0:T(8,128)(2,1)S(1)} %get-tuple-element.8), kind=kOutput, calls=%fused_computation.13 | convolution fusion | flops 253624320 | bytes 4866048 | tf_op jit(solution)/shard_map/dot_general | solution.py:31
  69.0 3.1 %fusion.31 = f32[320,2048]{1,0:T(8,128)} fusion(bf16[128,4096]{1,0:T(8,128)(2,1)} %bitcast.1, bf16[128,640]{1,0:T(8,128)(2,1)S(1)} %fusion.17), kind=kOutput, calls=%fused_computation.53 | convolution fusion | flops 167772160 | bytes 3244032 | tf_op jit(solution)/shard_map/dot_general | solution.py:31
  72.0 3.4 %fusion.7 = bf16[192,2048]{1,0:T(8,128)(2,1)} fusion(bf16[192,640]{1,0:T(8,128)(2,1)S(1)} %fusion.14, bf16[320,2048]{1,0:T(8,128)(2,1)} %collective-permute-done.1, bf16[320,2048]{1,0:T(8,128)(2,1)} %convert_bitcast_fusion), kind=kOutput, calls=%fused_computation.19 | convolution fusion | flops 509345792 | bytes 3653632 | tf_op jit(solution)/shard_map/dot_general | solution.py:156
  75.4 5.1 %all-to-all-start.3 = ((bf16[8,24,2048]{2,1,0:T(8,128)(2,1)}), bf16[8,24,2048]{2,1,0:T(8,128)(2,1)S(1)}, u32[]{:S(2)}, u32[]{:S(2)}) async-start(bf16[8,24,2048]{2,1,0:T(8,128)(2,1)} %bitcast.26), calls=%async_computation.3 | async-start | bytes 1572864 | tf_op jit(solution)/shard_map/all_to_all | solution.py:84
  80.5 3.0 %fusion.37 = f32[320,2048]{1,0:T(8,128)} fusion(bf16[128,4096]{1,0:T(8,128)(2,1)} %bitcast.1, bf16[128,640]{1,0:T(8,128)(2,1)S(1)} %get-tuple-element.6), kind=kOutput, calls=%fused_computation.59 | convolution fusion | flops 167772160 | bytes 3244032 | tf_op jit(solution)/shard_map/dot_general | solution.py:31
  83.9 5.3 %bitcast_subtract_fusion.1 = f32[2048,320]{0,1:T(8,128)} fusion(f32[2048,320]{0,1:T(8,128)} %param.10, bf16[320,2048]{1,0:T(8,128)(2,1)} %collective-permute-done.4, f32[320,2048]{1,0:T(8,128)} %fusion.31, bf16[192,4096]{1,0:T(8,128)(2,1)S(1)} %bitcast.24, bf16[192,640]{1,0:T(8,128)(2,1)S(1)} %fusion.14), kind=kOutput, calls=%fused_computation.17 | convolution fusion | flops 255590400 | bytes 10108928 | tf_op jit(solution)/shard_map/dot_general | solution.py:31
  89.3 3.7 %bitcast_subtract_fusion = f32[2048,320]{0,1:T(8,128)} fusion(f32[2048,320]{0,1:T(8,128)S(1)} %copy-done.4, bf16[320,2048]{1,0:T(8,128)(2,1)} %collective-permute-done.5, f32[320,2048]{1,0:T(8,128)S(1)} %copy-done.2, bf16[192,4096]{1,0:T(8,128)(2,1)S(1)} %bitcast.25, bf16[192,640]{1,0:T(8,128)(2,1)S(1)} %get-tuple-element.8), kind=kOutput, calls=%fused_computation.16 | convolution fusion | flops 255590400 | bytes 10108928 | tf_op jit(solution)/shard_map/dot_general | solution.py:31
  93.8 7.1 %collective-permute-done.3 = bf16[24,2048]{1,0:T(8,128)(2,1)S(1)} collective-permute-done((bf16[24,2048]{1,0:T(8,128)(2,1)S(1)}, bf16[24,2048]{1,0:T(8,128)(2,1)S(1)}, u32[]{:S(2)}, u32[]{:S(2)}) %collective-permute-start.3) | collective-permute-done | bytes 98336 | tf_op jit(solution)/shard_map/ppermute | solution.py:113
  (48 shorter events, 11.3 us)
Async XLA Ops:
  0.6 11.4 %copy-start.9 = (bf16[64,2048]{1,0:T(8,128)(2,1)S(1)}, bf16[64,2048]{1,0:T(8,128)(2,1)}, u32[]{:S(2)}) copy-start(bf16[64,2048]{1,0:T(8,128)(2,1)} %param.6) | copy-start | bytes 786436
  2.4 12.5 %copy-start.3 = (f32[2048,320]{0,1:T(8,128)S(1)}, f32[2048,320]{0,1:T(8,128)}, u32[]{:S(2)}) copy-start(f32[2048,320]{0,1:T(8,128)} %param.10) | copy-start | bytes 7864324
  5.8 24.5 %all-to-all-start = ((bf16[8,16,4096]{2,1,0:T(8,128)(2,1)}), bf16[8,16,4096]{2,1,0:T(8,128)(2,1)}, u32[]{:S(2)}, u32[]{:S(2)}) async-start(bf16[8,16,4096]{2,1,0:T(8,128)(2,1)} %broadcast_in_dim.11), calls=%async_computation | async-start | bytes 2097152 | tf_op jit(solution)/shard_map/all_to_all | solution.py:84
  12.2 15.4 %collective-permute-start.2 = (bf16[24,4096]{1,0:T(8,128)(2,1)S(1)}, bf16[24,4096]{1,0:T(8,128)(2,1)S(1)}, u32[]{:S(2)}, u32[]{:S(2)}) collective-permute-start(bf16[24,4096]{1,0:T(8,128)(2,1)S(1)} %convolution_convert_fusion), channel_id=1, source_target_pairs={{0,16},{1,17},{2,18},{3,19},{4,20},{5,21},{6,22},{7,23},{8,24},{9,... | collective-permute-start | bytes 589832 | tf_op jit(solution)/shard_map/ppermute | solution.py:113
  16.2 22.9 %collective-permute-start.1 = (bf16[320,2048]{1,0:T(8,128)(2,1)}, bf16[320,2048]{1,0:T(8,128)(2,1)}, u32[]{:S(2)}, u32[]{:S(2)}) collective-permute-start(bf16[320,2048]{1,0:T(8,128)(2,1)} %convert_bitcast_fusion), channel_id=1, source_target_pairs={{0,1},{1,0},{2,3},{3,2},{4,5},{5,4},{6,7},{7,6},{8,9},{9,8},{10,11... | collective-permute-start | bytes 3932168 | tf_op jit(solution)/shard_map/ppermute | solution.py:68
  31.6 24.9 %all-to-all-start.2 = ((bf16[8,24,4096]{2,1,0:T(8,128)(2,1)}), bf16[8,24,4096]{2,1,0:T(8,128)(2,1)S(1)}, u32[]{:S(2)}, u32[]{:S(2)}) async-start(bf16[8,24,4096]{2,1,0:T(8,128)(2,1)} %broadcast_in_dim.12), calls=%async_computation.2 | async-start | bytes 3145728 | tf_op jit(solution)/shard_map/all_to_all | solution.py:84
  39.0 3.4 %copy-start.5 = (bf16[320,2048]{1,0:T(8,128)(2,1)}, bf16[320,2048]{1,0:T(8,128)(2,1)S(1)}, u32[]{:S(2)}) copy-start(bf16[320,2048]{1,0:T(8,128)(2,1)S(1)} %convert_bitcast_fusion.1) | copy-start | bytes 3932164
  39.0 3.3 %collective-permute-start = (bf16[320,2048]{1,0:T(8,128)(2,1)S(1)}, bf16[320,2048]{1,0:T(8,128)(2,1)S(1)}, u32[]{:S(2)}, u32[]{:S(2)}) collective-permute-start(bf16[320,2048]{1,0:T(8,128)(2,1)S(1)} %convert_bitcast_fusion.1), channel_id=1, source_target_pairs={{0,1},{1,0},{2,3},{3,2},{4,5},{5,4},{6,7},{7,6},{8,9},{9,8},{10,11... | collective-permute-start | bytes 3932168 | tf_op jit(solution)/shard_map/ppermute | solution.py:68
  42.4 2.5 %copy-start.7 = (bf16[320,2048]{1,0:T(8,128)(2,1)}, bf16[320,2048]{1,0:T(8,128)(2,1)S(1)}, u32[]{:S(2)}) copy-start(bf16[320,2048]{1,0:T(8,128)(2,1)S(1)} %collective-permute-done) | copy-start | bytes 3932164
  56.6 18.9 %all-to-all-start.1 = ((bf16[8,16,2048]{2,1,0:T(8,128)(2,1)}), bf16[8,16,2048]{2,1,0:T(8,128)(2,1)S(1)}, u32[]{:S(2)}, u32[]{:S(2)}) async-start(bf16[8,16,2048]{2,1,0:T(8,128)(2,1)} %bitcast.4), calls=%async_computation.1 | async-start | bytes 1048576 | tf_op jit(solution)/shard_map/all_to_all | solution.py:84
  60.3 3.0 %copy-start.6 = (bf16[320,2048]{1,0:T(8,128)(2,1)S(1)}, bf16[320,2048]{1,0:T(8,128)(2,1)}, u32[]{:S(2)}) copy-start(bf16[320,2048]{1,0:T(8,128)(2,1)} %copy-done.5) | copy-start | bytes 3932164
  60.3 3.0 %copy-start.8 = (bf16[320,2048]{1,0:T(8,128)(2,1)S(1)}, bf16[320,2048]{1,0:T(8,128)(2,1)}, u32[]{:S(2)}) copy-start(bf16[320,2048]{1,0:T(8,128)(2,1)} %copy-done.7) | copy-start | bytes 3932164
  63.3 1.7 %copy-start.1 = (f32[320,2048]{1,0:T(8,128)S(1)}, f32[320,2048]{1,0:T(8,128)}, u32[]{:S(2)}) copy-start(f32[320,2048]{1,0:T(8,128)} %fusion.29) | copy-start | bytes 7864324
  65.0 2.0 %copy-start = (f32[320,2048]{1,0:T(8,128)S(1)}, f32[320,2048]{1,0:T(8,128)}, u32[]{:S(2)}) copy-start(f32[320,2048]{1,0:T(8,128)} %fusion.35) | copy-start | bytes 7864324
  66.7 17.2 %collective-permute-start.4 = (bf16[320,2048]{1,0:T(8,128)(2,1)}, bf16[320,2048]{1,0:T(8,128)(2,1)}, u32[]{:S(2)}, u32[]{:S(2)}) collective-permute-start(bf16[320,2048]{1,0:T(8,128)(2,1)} %fusion.5), channel_id=1, source_target_pairs={{0,1},{1,0},{2,3},{3,2},{4,5},{5,4},{6,7},{7,6},{8,9},{9,8},{10,11... | collective-permute-start | bytes 3932168 | tf_op jit(solution)/shard_map/ppermute | solution.py:68
  68.8 20.5 %collective-permute-start.5 = (bf16[320,2048]{1,0:T(8,128)(2,1)}, bf16[320,2048]{1,0:T(8,128)(2,1)}, u32[]{:S(2)}, u32[]{:S(2)}) collective-permute-start(bf16[320,2048]{1,0:T(8,128)(2,1)} %fusion.6), channel_id=1, source_target_pairs={{0,1},{1,0},{2,3},{3,2},{4,5},{5,4},{6,7},{7,6},{8,9},{9,8},{10,11... | collective-permute-start | bytes 3932168 | tf_op jit(solution)/shard_map/ppermute | solution.py:68
  75.4 17.5 %all-to-all-start.3 = ((bf16[8,24,2048]{2,1,0:T(8,128)(2,1)}), bf16[8,24,2048]{2,1,0:T(8,128)(2,1)S(1)}, u32[]{:S(2)}, u32[]{:S(2)}) async-start(bf16[8,24,2048]{2,1,0:T(8,128)(2,1)} %bitcast.26), calls=%async_computation.3 | async-start | bytes 1572864 | tf_op jit(solution)/shard_map/all_to_all | solution.py:84
  83.9 5.4 %copy-start.2 = (f32[320,2048]{1,0:T(8,128)S(1)}, f32[320,2048]{1,0:T(8,128)}, u32[]{:S(2)}) copy-start(f32[320,2048]{1,0:T(8,128)} %fusion.37) | copy-start | bytes 7864324
  83.9 5.4 %copy-start.4 = (f32[2048,320]{0,1:T(8,128)S(1)}, f32[2048,320]{0,1:T(8,128)}, u32[]{:S(2)}) copy-start(f32[2048,320]{0,1:T(8,128)} %param.11) | copy-start | bytes 7864324
  93.1 7.9 %collective-permute-start.3 = (bf16[24,2048]{1,0:T(8,128)(2,1)S(1)}, bf16[24,2048]{1,0:T(8,128)(2,1)S(1)}, u32[]{:S(2)}, u32[]{:S(2)}) collective-permute-start(bf16[24,2048]{1,0:T(8,128)(2,1)S(1)} %reduce_sum.35), channel_id=1, source_target_pairs={{0,16},{1,17},{2,18},{3,19},{4,20},{5,21},{6,22},{7,23},{8,24},{9,... | collective-permute-start | bytes 294920 | tf_op jit(solution)/shard_map/ppermute | solution.py:113

commit v4 on v3

--- a/solution.py
+++ b/solution.py
@@ -68,33 +68,47 @@
     return lax.ppermute(rows, "expert", [(i, i ^ mask) for i in range(n_expert)])
 
 
-core_bit = 1
-
-
-def same_core():
-    n_expert = lax.axis_size("expert")
-    return [
-        [e * SHARDS + k for k in range(c, SHARDS, 2)]
-        for e in range(n_expert // SHARDS)
-        for c in range(2)
-    ]
-
-
-def exchange(blocks):
-    return lax.all_to_all(
-        blocks, "expert", split_axis=0, concat_axis=0, tiled=True, axis_index_groups=same_core()
-    )
-
-
-def gather(own):
-    rows, columns = own.shape
-    blocks = exchange(jnp.broadcast_to(own[None], (SHARDS // 2, rows, columns)))
-    return blocks.reshape(SHARDS // 2 * rows, columns)
-
-
-def scatter_sum(parts):
-    blocks = exchange(parts.reshape(SHARDS // 2, -1, parts.shape[1]))
-    return jnp.sum(blocks.astype(jnp.float32), axis=0).astype(jnp.bfloat16)
+core_bit, x_bit, y_bit, z_bit = 1, 2, 4, 8
+
+
+def after(values, *others):
+    return lax.optimization_barrier((values, others))[0]
+
+
+def first_hop(own):
+    return swap(own, x_bit), swap(own, y_bit), swap(own, z_bit)
+
+
+def second_hop(near_x, near_y, near_z):
+    return (
+        swap(near_x, y_bit),
+        swap(near_y, z_bit),
+        swap(near_z, x_bit),
+        swap(near_z, x_bit | y_bit),
+    )
+
+
+def second_hop_back(parts):
+    rows = parts.shape[0] // 8
+    blocks = [parts[k * rows : (k + 1) * rows] for k in range(8)]
+    far = (
+        swap(blocks[4], y_bit),
+        swap(blocks[5], z_bit),
+        swap(blocks[6], x_bit),
+        swap(blocks[7], x_bit | y_bit),
+    )
+    return blocks[:4], far
+
+
+def total(*terms):
+    return sum(term.astype(jnp.float32) for term in terms).astype(jnp.bfloat16)
+
+
+def first_hop_back(near, far):
+    near_x = swap(total(near[1], far[0]), x_bit)
+    near_y = swap(total(near[2], far[1]), y_bit)
+    near_z = swap(total(near[3], far[2], far[3]), z_bit)
+    return total(near[0], near_x, near_y, near_z)
 
 
 def shards(tokens, attn_partials, expert_ids, gate, w_in, w_out):
@@ -135,31 +149,45 @@
         jnp.dot(pick, both, preferred_element_type=jnp.float32).astype(jnp.bfloat16)
         for pick in picks
     ]
-    early_rows = gather(packed[0])
-    late_own = packed[1]
-    for s in range(1, experts):
-        late_own = late_own + shifted(packed[s + 1], s)
-    late_rows = gather(late_own)
 
     def paired(weights):
         own = whole_weights(weights).T
         return jnp.concatenate([own, swap(own, core_bit)], axis=0)
 
-    weights_in, weights_out = paired(w_in), paired(w_out)
-
-    def worked(rows):
+    def activated(rows):
         expert_rows, grad_rows = rows[:, :width], rows[:, width:]
         pre_act = contract_cols(expert_rows, weights_in) * scale_in
         hidden = gelu_value(pre_act).astype(jnp.bfloat16)
         hidden_grad = contract_cols(grad_rows, weights_out) * scale_out
         pre_grad = (hidden_grad * gelu_slope(pre_act)).astype(jnp.bfloat16)
-        partial_x = jnp.dot(pre_grad, weights_in, preferred_element_type=jnp.float32) * scale_in
-        return expert_rows, grad_rows, hidden, pre_grad, partial_x.astype(jnp.bfloat16)
-
-    early, later = worked(early_rows), worked(late_rows)
-    early_sum, late_sum = scatter_sum(early[4]), scatter_sum(later[4])
+        return expert_rows, grad_rows, hidden, pre_grad
+
+    def input_parts(pre_grad):
+        parts = jnp.dot(pre_grad, weights_in, preferred_element_type=jnp.float32) * scale_in
+        return parts.astype(jnp.bfloat16)
+
+    early_near = first_hop(packed[0])
+    weights_in, weights_out = paired(w_in), paired(w_out)
+    late_own = packed[1]
+    for s in range(1, experts):
+        late_own = late_own + shifted(packed[s + 1], s)
+    early_far = second_hop(*early_near)
+    late_own = after(late_own, early_near)
+    late_near = first_hop(late_own)
+    early_rows = jnp.concatenate([packed[0], *early_near, *early_far], axis=0)
+    early = activated(early_rows)
+    late_near = after(late_near, early[3])
+    late_far = second_hop(*late_near)
+    early_parts = input_parts(early[3])
+    late_far = after(late_far, early_parts)
+    late_rows = jnp.concatenate([late_own, *late_near, *late_far], axis=0)
+    later = activated(late_rows)
+    late_parts = input_parts(later[3])
+    early_back = second_hop_back(early_parts)
+    late_back = second_hop_back(late_parts)
+    early_sum = first_hop_back(*early_back)
+    late_sum = first_hop_back(*late_back)
     returned = [early_sum, late_sum] + [shifted(late_sum, -s) for s in range(1, experts)]
-    token_grad = sum(contract_rows(pick, rows) for pick, rows in zip(picks, returned))
 
     def step(weights, left, right, scale):
         theirs = sum(contract_rows(e[left][:, units:], e[right]) for e in (early, later)) * scale
@@ -169,6 +197,7 @@
 
     new_w_in = step(w_in, 3, 0, scale_in)
     new_w_out = step(w_out, 2, 1, scale_out)
+    token_grad = sum(contract_rows(pick, rows) for pick, rows in zip(picks, returned))
     return (token_grad.astype(jnp.bfloat16), new_w_in, new_w_out)
 
 

time: 103 us -> 93.4 us (0.907)
  matrix products: 44.2 us -> 17 us
  waiting for transfers between devices: 23.5 us -> 38.8 us
  starting transfers between devices: 23.7 us -> 31 us
  local copies, waits for them, and re-layouts: 3.33 us -> 0.25 us
  other arithmetic: 6.32 us -> 5.09 us
    ppermute x4 -> x32, waiting for transfers between devices: 0.01 us -> 25.7 us  [swap(): lax.ppermute(rows, 'expert', [(i, i ^ mask) for i in range(n_expert)])]
    ppermute x4 -> x32, starting transfers between devices: 0.24 us -> 25.7 us  [swap(): lax.ppermute(rows, 'expert', [(i, i ^ mask) for i in range(n_expert)])]
    all_to_all x4 -> x0, starting transfers between devices: 20.4 us -> none  [exchange(): lax.all_to_all(blocks, 'expert', split_axis=0, concat_axis=0, tiled=True,...]
    dot_general x11, matrix products: 26.3 us -> 9.66 us  [contract_rows(): lax.dot_general(left, right, (((0,), (0,)), ((), ())), preferred_element_...]
    dot_general x4, matrix products: 9.87 us -> 4.33 us  [contract_cols(): lax.dot_general(left, right, (((1,), (1,)), ((), ())), preferred_element_...]
    ppermute x2, waiting for transfers between devices: 18.6 us -> 13.1 us  [shifted(): return lax.ppermute(rows, 'expert', pairs)]
    dot_general x2, matrix products: 6.51 us -> 1.37 us  [input_parts(): jnp.dot(pre_grad, weights_in, preferred_element_type=jnp.float32) * scale_in]
    all_to_all x4 -> x0, waiting for transfers between devices: 4.84 us -> none  [exchange(): lax.all_to_all(blocks, 'expert', split_axis=0, concat_axis=0, tiled=True,...]
  transfers between devices with their start and end apart: 10 -> 34, of which waited for: 4 -> 18; matrix products, arithmetic and copies ran while one was open for 46% -> 17% of each run, Pallas kernels for 0% -> 0%
where the time goes in v4:
time: 93.4 us; the launch traced here: 93.2 us
  waiting for transfers between devices  38.8 us (42%)
  starting transfers between devices  31 us (33%)
  matrix products  17 us (18%)
  other arithmetic  5.09 us (5%)
  between operations  1.01 us (1%)
    ppermute x32, waiting for transfers between devices, swap(): lax.ppermute(rows, 'expert', [(i, i ^ mask) for i in range(n_expert)])  25.7 us
    ppermute x32, starting transfers between devices, swap(): lax.ppermute(rows, 'expert', [(i, i ^ mask) for i in range(n_expert)])  25.7 us
    ppermute x2, waiting for transfers between devices, shifted(): return lax.ppermute(rows, 'expert', pairs)  13.1 us
    dot_general x11, matrix products, contract_rows(): lax.dot_general(left, right, (((0,), (0,)), ((), ())), preferred_element_...  9.66 us
    ppermute x2, starting transfers between devices, shifted(): return lax.ppermute(rows, 'expert', pairs)  5.38 us
    dot_general x4, matrix products, contract_cols(): lax.dot_general(left, right, (((1,), (1,)), ((), ())), preferred_element_...  4.33 us
    transpose x2, other arithmetic, paired(): own = whole_weights(weights).T  2.1 us
  transfers between devices with their start and end apart: 34, of which 18 were waited for; matrix products, arithmetic and copies ran while one was open for 17% of the time, Pallas kernels for 0%

profile of v4, /device:TPU:0, one launch (start us, length us, event | category | flops | bytes accessed | tf_op | source)
XLA Modules:
  0.0 93.2 jit_solution(11102694810522810482)
XLA Ops:
  4.8 3.0 %collective-permute-start = (bf16[16,4096]{1,0:T(8,128)(2,1)S(1)}, bf16[16,4096]{1,0:T(8,128)(2,1)S(1)}, u32[]{:S(2)}, u32[]{:S(2)}) collective-permute-start(bf16[16,4096]{1,0:T(8,128)(2,1)S(1)} %get-tuple-element.37), channel_id=1, source_target_pairs={{0,2},{1,3},{2,0},{3,1},{4,6},{5,7},{6,4},{7,5},{8,10},{9,11},{10,... | collective-permute-start | bytes 393224 | tf_op jit(solution)/shard_map/ppermute | solution.py:68
  7.8 1.5 %collective-permute-start.1 = (bf16[16,4096]{1,0:T(8,128)(2,1)S(1)}, bf16[16,4096]{1,0:T(8,128)(2,1)S(1)}, u32[]{:S(2)}, u32[]{:S(2)}) collective-permute-start(bf16[16,4096]{1,0:T(8,128)(2,1)S(1)} %get-tuple-element.37), channel_id=1, source_target_pairs={{0,4},{1,5},{2,6},{3,7},{4,0},{5,1},{6,2},{7,3},{8,12},{9,13},{10,... | collective-permute-start | bytes 393224 | tf_op jit(solution)/shard_map/ppermute | solution.py:68
  9.3 1.6 %collective-permute-start.2 = (bf16[16,4096]{1,0:T(8,128)(2,1)S(1)}, bf16[16,4096]{1,0:T(8,128)(2,1)S(1)}, u32[]{:S(2)}, u32[]{:S(2)}) collective-permute-start(bf16[16,4096]{1,0:T(8,128)(2,1)S(1)} %get-tuple-element.37), channel_id=1, source_target_pairs={{0,8},{1,9},{2,10},{3,11},{4,12},{5,13},{6,14},{7,15},{8,0},{9,1},... | collective-permute-start | bytes 393224 | tf_op jit(solution)/shard_map/ppermute | solution.py:68
  10.9 1.9 %convert_bitcast_fusion.1 = bf16[320,2048]{1,0:T(8,128)(2,1)S(1)} fusion(f32[2048,320]{0,1:T(8,128)} %param.11), kind=kLoop, calls=%fused_computation.34 | loop fusion | flops 655360 | bytes 3932160 | tf_op jit(solution)/shard_map/transpose | solution.py:154
  13.1 2.7 %collective-permute-start.16 = (bf16[24,4096]{1,0:T(8,128)(2,1)S(1)}, bf16[24,4096]{1,0:T(8,128)(2,1)S(1)}, u32[]{:S(2)}, u32[]{:S(2)}) collective-permute-start(bf16[24,4096]{1,0:T(8,128)(2,1)S(1)} %convolution_convert_fusion), channel_id=1, source_target_pairs={{0,16},{1,17},{2,18},{3,19},{4,20},{5,21},{6,22},{7,23},{8,24},{9,... | collective-permute-start | bytes 589832 | tf_op jit(solution)/shard_map/ppermute | solution.py:127
  17.4 8.2 %collective-permute-done.16 = bf16[24,4096]{1,0:T(8,128)(2,1)S(1)} collective-permute-done((bf16[24,4096]{1,0:T(8,128)(2,1)S(1)}, bf16[24,4096]{1,0:T(8,128)(2,1)S(1)}, u32[]{:S(2)}, u32[]{:S(2)}) %collective-permute-start.16) | collective-permute-done | bytes 196640 | tf_op jit(solution)/shard_map/ppermute | solution.py:127
  26.3 1.5 %collective-permute-start.6 = (bf16[16,4096]{1,0:T(8,128)(2,1)S(1)}, bf16[16,4096]{1,0:T(8,128)(2,1)S(1)}, u32[]{:S(2)}, u32[]{:S(2)}) collective-permute-start(bf16[16,4096]{1,0:T(8,128)(2,1)S(1)} %collective-permute-done.2), channel_id=1, source_target_pairs={{0,6},{1,7},{2,4},{3,5},{4,2},{5,3},{6,0},{7,1},{8,14},{9,15},{10,... | collective-permute-start | bytes 393224 | tf_op jit(solution)/shard_map/ppermute | solution.py:68
  28.4 3.5 %collective-permute-done.5 = bf16[16,4096]{1,0:T(8,128)(2,1)S(1)} collective-permute-done((bf16[16,4096]{1,0:T(8,128)(2,1)S(1)}, bf16[16,4096]{1,0:T(8,128)(2,1)S(1)}, u32[]{:S(2)}, u32[]{:S(2)}) %collective-permute-start.5) | collective-permute-done | bytes 131104 | tf_op jit(solution)/shard_map/ppermute | solution.py:68
  32.4 2.2 %collective-permute-done.6 = bf16[16,4096]{1,0:T(8,128)(2,1)S(1)} collective-permute-done((bf16[16,4096]{1,0:T(8,128)(2,1)S(1)}, bf16[16,4096]{1,0:T(8,128)(2,1)S(1)}, u32[]{:S(2)}, u32[]{:S(2)}) %collective-permute-start.6) | collective-permute-done | bytes 131104 | tf_op jit(solution)/shard_map/ppermute | solution.py:68
  38.0 2.3 %collective-permute-done.19 = bf16[24,4096]{1,0:T(8,128)(2,1)S(1)} collective-permute-done((bf16[24,4096]{1,0:T(8,128)(2,1)S(1)}, bf16[24,4096]{1,0:T(8,128)(2,1)S(1)}, u32[]{:S(2)}, u32[]{:S(2)}) %collective-permute-start.19) | collective-permute-done | bytes 196640 | tf_op jit(solution)/shard_map/ppermute | solution.py:68
  40.3 1.5 %collective-permute-start.20 = (bf16[24,4096]{1,0:T(8,128)(2,1)S(1)}, bf16[24,4096]{1,0:T(8,128)(2,1)S(1)}, u32[]{:S(2)}, u32[]{:S(2)}) collective-permute-start(bf16[24,4096]{1,0:T(8,128)(2,1)S(1)} %collective-permute-done.17), channel_id=1, source_target_pairs={{0,4},{1,5},{2,6},{3,7},{4,0},{5,1},{6,2},{7,3},{8,12},{9,13},{10,... | collective-permute-start | bytes 589832 | tf_op jit(solution)/shard_map/ppermute | solution.py:68
  43.1 1.5 %collective-permute-start.14 = (bf16[16,2048]{1,0:T(8,128)(2,1)S(1)}, bf16[16,2048]{1,0:T(8,128)(2,1)S(1)}, u32[]{:S(2)}, u32[]{:S(2)}) collective-permute-start(bf16[16,2048]{1,0:T(8,128)(2,1)S(1)} %get-tuple-element.30), channel_id=1, source_target_pairs={{0,6},{1,7},{2,4},{3,5},{4,2},{5,3},{6,0},{7,1},{8,14},{9,15},{10,... | collective-permute-start | bytes 196616 | tf_op jit(solution)/shard_map/ppermute | solution.py:68
  44.6 1.5 %collective-permute-start.13 = (bf16[16,2048]{1,0:T(8,128)(2,1)S(1)}, bf16[16,2048]{1,0:T(8,128)(2,1)S(1)}, u32[]{:S(2)}, u32[]{:S(2)}) collective-permute-start(bf16[16,2048]{1,0:T(8,128)(2,1)S(1)} %get-tuple-element.31), channel_id=1, source_target_pairs={{0,2},{1,3},{2,0},{3,1},{4,6},{5,7},{6,4},{7,5},{8,10},{9,11},{10,... | collective-permute-start | bytes 196616 | tf_op jit(solution)/shard_map/ppermute | solution.py:68
  50.4 1.5 %collective-permute-start.23 = (bf16[24,4096]{1,0:T(8,128)(2,1)S(1)}, bf16[24,4096]{1,0:T(8,128)(2,1)S(1)}, u32[]{:S(2)}, u32[]{:S(2)}) collective-permute-start(bf16[24,4096]{1,0:T(8,128)(2,1)S(1)} %collective-permute-done.19), channel_id=1, source_target_pairs={{0,6},{1,7},{2,4},{3,5},{4,2},{5,3},{6,0},{7,1},{8,14},{9,15},{10,... | collective-permute-start | bytes 589832 | tf_op jit(solution)/shard_map/ppermute | solution.py:68
  52.6 2.0 %collective-permute-done.22 = bf16[24,4096]{1,0:T(8,128)(2,1)S(1)} collective-permute-done((bf16[24,4096]{1,0:T(8,128)(2,1)S(1)}, bf16[24,4096]{1,0:T(8,128)(2,1)S(1)}, u32[]{:S(2)}, u32[]{:S(2)}) %collective-permute-start.22) | collective-permute-done | bytes 196640 | tf_op jit(solution)/shard_map/ppermute | solution.py:68
  54.6 3.1 %collective-permute-done.23 = bf16[24,4096]{1,0:T(8,128)(2,1)S(1)} collective-permute-done((bf16[24,4096]{1,0:T(8,128)(2,1)S(1)}, bf16[24,4096]{1,0:T(8,128)(2,1)S(1)}, u32[]{:S(2)}, u32[]{:S(2)}) %collective-permute-start.23) | collective-permute-done | bytes 196640 | tf_op jit(solution)/shard_map/ppermute | solution.py:68
  62.1 1.5 %collective-permute-start.29 = (bf16[24,2048]{1,0:T(8,128)(2,1)S(1)}, bf16[24,2048]{1,0:T(8,128)(2,1)S(1)}, u32[]{:S(2)}, u32[]{:S(2)}) collective-permute-start(bf16[24,2048]{1,0:T(8,128)(2,1)S(1)} %get-tuple-element.23), channel_id=1, source_target_pairs={{0,6},{1,7},{2,4},{3,5},{4,2},{5,3},{6,0},{7,1},{8,14},{9,15},{10,... | collective-permute-start | bytes 294920 | tf_op jit(solution)/shard_map/ppermute | solution.py:68
  63.6 1.5 %collective-permute-start.28 = (bf16[24,2048]{1,0:T(8,128)(2,1)S(1)}, bf16[24,2048]{1,0:T(8,128)(2,1)S(1)}, u32[]{:S(2)}, u32[]{:S(2)}) collective-permute-start(bf16[24,2048]{1,0:T(8,128)(2,1)S(1)} %get-tuple-element.24), channel_id=1, source_target_pairs={{0,2},{1,3},{2,0},{3,1},{4,6},{5,7},{6,4},{7,5},{8,10},{9,11},{10,... | collective-permute-start | bytes 294920 | tf_op jit(solution)/shard_map/ppermute | solution.py:68
  71.8 2.6 %collective-permute-done.30 = bf16[24,2048]{1,0:T(8,128)(2,1)S(1)} collective-permute-done((bf16[24,2048]{1,0:T(8,128)(2,1)S(1)}, bf16[24,2048]{1,0:T(8,128)(2,1)S(1)}, u32[]{:S(2)}, u32[]{:S(2)}) %collective-permute-start.30) | collective-permute-done | bytes 98336 | tf_op jit(solution)/shard_map/ppermute | solution.py:68
  75.4 2.7 %collective-permute-start.31 = (bf16[24,2048]{1,0:T(8,128)(2,1)S(1)}, bf16[24,2048]{1,0:T(8,128)(2,1)S(1)}, u32[]{:S(2)}, u32[]{:S(2)}) collective-permute-start(bf16[24,2048]{1,0:T(8,128)(2,1)S(1)} %add_convert_fusion), channel_id=1, source_target_pairs={{0,16},{1,17},{2,18},{3,19},{4,20},{5,21},{6,22},{7,23},{8,24},{9,... | collective-permute-start | bytes 294920 | tf_op jit(solution)/shard_map/ppermute | solution.py:127
  78.4 4.9 %collective-permute-done.31 = bf16[24,2048]{1,0:T(8,128)(2,1)S(1)} collective-permute-done((bf16[24,2048]{1,0:T(8,128)(2,1)S(1)}, bf16[24,2048]{1,0:T(8,128)(2,1)S(1)}, u32[]{:S(2)}, u32[]{:S(2)}) %collective-permute-start.31) | collective-permute-done | bytes 98336 | tf_op jit(solution)/shard_map/ppermute | solution.py:127
  84.5 3.1 %collective-permute-done.10 = bf16[16,2048]{1,0:T(8,128)(2,1)S(1)} collective-permute-done((bf16[16,2048]{1,0:T(8,128)(2,1)S(1)}, bf16[16,2048]{1,0:T(8,128)(2,1)S(1)}, u32[]{:S(2)}, u32[]{:S(2)}) %collective-permute-start.10) | collective-permute-done | bytes 65568 | tf_op jit(solution)/shard_map/ppermute | solution.py:68
  88.6 2.3 %fusion.12 = f32[2048,320]{0,1:T(8,128)} fusion(f32[2048,320]{0,1:T(8,128)S(1)} %copy-done, f32[320,2048]{1,0:T(8,128)S(1)} %fusion.29, bf16[320,2048]{1,0:T(8,128)(2,1)S(1)} %collective-permute-done.32, bf16[128,4096]{1,0:T(8,128)(2,1)S(1)} %constant_dynamic-update-slice_fusion, bf16[128,640]{1,0:T(8,128)(2,1)S(1)} %fusion.26), kind=kOutput, calls=%fused_computation.19 | convolution fusion | flops 171704320 | bytes 9797632 | tf_op jit(solution)/shard_map/dot_general | solution.py:31
  90.9 2.3 %fusion.6 = f32[2048,320]{0,1:T(8,128)} fusion(f32[2048,320]{0,1:T(8,128)S(1)} %copy-done.1, f32[320,2048]{1,0:T(8,128)S(1)} %fusion.35, bf16[320,2048]{1,0:T(8,128)(2,1)S(1)} %collective-permute-done.33, bf16[128,4096]{1,0:T(8,128)(2,1)S(1)} %constant_dynamic-update-slice_fusion, bf16[128,640]{1,0:T(8,128)(2,1)S(1)} %get-tuple-element.40), kind=kOutput, calls=%fused_computation.11 | convolution fusion | flops 171704320 | bytes 9797632 | tf_op jit(solution)/shard_map/dot_general | solution.py:31
  (98 shorter events, 31.7 us)
Async XLA Ops:
  4.8 11.2 %collective-permute-start = (bf16[16,4096]{1,0:T(8,128)(2,1)S(1)}, bf16[16,4096]{1,0:T(8,128)(2,1)S(1)}, u32[]{:S(2)}, u32[]{:S(2)}) collective-permute-start(bf16[16,4096]{1,0:T(8,128)(2,1)S(1)} %get-tuple-element.37), channel_id=1, source_target_pairs={{0,2},{1,3},{2,0},{3,1},{4,6},{5,7},{6,4},{7,5},{8,10},{9,11},{10,... | collective-permute-start | bytes 393224 | tf_op jit(solution)/shard_map/ppermute | solution.py:68
  7.8 8.5 %collective-permute-start.1 = (bf16[16,4096]{1,0:T(8,128)(2,1)S(1)}, bf16[16,4096]{1,0:T(8,128)(2,1)S(1)}, u32[]{:S(2)}, u32[]{:S(2)}) collective-permute-start(bf16[16,4096]{1,0:T(8,128)(2,1)S(1)} %get-tuple-element.37), channel_id=1, source_target_pairs={{0,4},{1,5},{2,6},{3,7},{4,0},{5,1},{6,2},{7,3},{8,12},{9,13},{10,... | collective-permute-start | bytes 393224 | tf_op jit(solution)/shard_map/ppermute | solution.py:68
  9.3 7.5 %collective-permute-start.2 = (bf16[16,4096]{1,0:T(8,128)(2,1)S(1)}, bf16[16,4096]{1,0:T(8,128)(2,1)S(1)}, u32[]{:S(2)}, u32[]{:S(2)}) collective-permute-start(bf16[16,4096]{1,0:T(8,128)(2,1)S(1)} %get-tuple-element.37), channel_id=1, source_target_pairs={{0,8},{1,9},{2,10},{3,11},{4,12},{5,13},{6,14},{7,15},{8,0},{9,1},... | collective-permute-start | bytes 393224 | tf_op jit(solution)/shard_map/ppermute | solution.py:68
  12.8 22.9 %collective-permute-start.7 = (bf16[320,2048]{1,0:T(8,128)(2,1)S(1)}, bf16[320,2048]{1,0:T(8,128)(2,1)S(1)}, u32[]{:S(2)}, u32[]{:S(2)}) collective-permute-start(bf16[320,2048]{1,0:T(8,128)(2,1)S(1)} %convert_bitcast_fusion.1), channel_id=1, source_target_pairs={{0,1},{1,0},{2,3},{3,2},{4,5},{5,4},{6,7},{7,6},{8,9},{9,8},{10,11... | collective-permute-start | bytes 3932168 | tf_op jit(solution)/shard_map/ppermute | solution.py:68
  13.1 12.5 %collective-permute-start.16 = (bf16[24,4096]{1,0:T(8,128)(2,1)S(1)}, bf16[24,4096]{1,0:T(8,128)(2,1)S(1)}, u32[]{:S(2)}, u32[]{:S(2)}) collective-permute-start(bf16[24,4096]{1,0:T(8,128)(2,1)S(1)} %convolution_convert_fusion), channel_id=1, source_target_pairs={{0,16},{1,17},{2,18},{3,19},{4,20},{5,21},{6,22},{7,23},{8,24},{9,... | collective-permute-start | bytes 589832 | tf_op jit(solution)/shard_map/ppermute | solution.py:127
  15.9 18.7 %collective-permute-start.8 = (bf16[320,2048]{1,0:T(8,128)(2,1)S(1)}, bf16[320,2048]{1,0:T(8,128)(2,1)S(1)}, u32[]{:S(2)}, u32[]{:S(2)}) collective-permute-start(bf16[320,2048]{1,0:T(8,128)(2,1)S(1)} %convert_bitcast_fusion), channel_id=1, source_target_pairs={{0,1},{1,0},{2,3},{3,2},{4,5},{5,4},{6,7},{7,6},{8,9},{9,8},{10,11... | collective-permute-start | bytes 3932168 | tf_op jit(solution)/shard_map/ppermute | solution.py:68
  16.2 10.1 %collective-permute-start.3 = (bf16[16,4096]{1,0:T(8,128)(2,1)S(1)}, bf16[16,4096]{1,0:T(8,128)(2,1)S(1)}, u32[]{:S(2)}, u32[]{:S(2)}) collective-permute-start(bf16[16,4096]{1,0:T(8,128)(2,1)S(1)} %collective-permute-done), channel_id=1, source_target_pairs={{0,4},{1,5},{2,6},{3,7},{4,0},{5,1},{6,2},{7,3},{8,12},{9,13},{10,... | collective-permute-start | bytes 393224 | tf_op jit(solution)/shard_map/ppermute | solution.py:68
  16.8 11.0 %collective-permute-start.4 = (bf16[16,4096]{1,0:T(8,128)(2,1)S(1)}, bf16[16,4096]{1,0:T(8,128)(2,1)S(1)}, u32[]{:S(2)}, u32[]{:S(2)}) collective-permute-start(bf16[16,4096]{1,0:T(8,128)(2,1)S(1)} %collective-permute-done.1), channel_id=1, source_target_pairs={{0,8},{1,9},{2,10},{3,11},{4,12},{5,13},{6,14},{7,15},{8,0},{9,1},... | collective-permute-start | bytes 393224 | tf_op jit(solution)/shard_map/ppermute | solution.py:68
  25.5 6.4 %collective-permute-start.5 = (bf16[16,4096]{1,0:T(8,128)(2,1)S(1)}, bf16[16,4096]{1,0:T(8,128)(2,1)S(1)}, u32[]{:S(2)}, u32[]{:S(2)}) collective-permute-start(bf16[16,4096]{1,0:T(8,128)(2,1)S(1)} %collective-permute-done.2), channel_id=1, source_target_pairs={{0,2},{1,3},{2,0},{3,1},{4,6},{5,7},{6,4},{7,5},{8,10},{9,11},{10,... | collective-permute-start | bytes 393224 | tf_op jit(solution)/shard_map/ppermute | solution.py:68
  26.3 8.3 %collective-permute-start.6 = (bf16[16,4096]{1,0:T(8,128)(2,1)S(1)}, bf16[16,4096]{1,0:T(8,128)(2,1)S(1)}, u32[]{:S(2)}, u32[]{:S(2)}) collective-permute-start(bf16[16,4096]{1,0:T(8,128)(2,1)S(1)} %collective-permute-done.2), channel_id=1, source_target_pairs={{0,6},{1,7},{2,4},{3,5},{4,2},{5,3},{6,0},{7,1},{8,14},{9,15},{10,... | collective-permute-start | bytes 393224 | tf_op jit(solution)/shard_map/ppermute | solution.py:68
  27.8 10.1 %collective-permute-start.17 = (bf16[24,4096]{1,0:T(8,128)(2,1)S(1)}, bf16[24,4096]{1,0:T(8,128)(2,1)S(1)}, u32[]{:S(2)}, u32[]{:S(2)}) collective-permute-start(bf16[24,4096]{1,0:T(8,128)(2,1)S(1)} %fusion), channel_id=1, source_target_pairs={{0,2},{1,3},{2,0},{3,1},{4,6},{5,7},{6,4},{7,5},{8,10},{9,11},{10,... | collective-permute-start | bytes 589832 | tf_op jit(solution)/shard_map/ppermute | solution.py:68
  31.9 6.1 %collective-permute-start.18 = (bf16[24,4096]{1,0:T(8,128)(2,1)S(1)}, bf16[24,4096]{1,0:T(8,128)(2,1)S(1)}, u32[]{:S(2)}, u32[]{:S(2)}) collective-permute-start(bf16[24,4096]{1,0:T(8,128)(2,1)S(1)} %fusion), channel_id=1, source_target_pairs={{0,4},{1,5},{2,6},{3,7},{4,0},{5,1},{6,2},{7,3},{8,12},{9,13},{10,... | collective-permute-start | bytes 589832 | tf_op jit(solution)/shard_map/ppermute | solution.py:68
  40.3 11.7 %collective-permute-start.20 = (bf16[24,4096]{1,0:T(8,128)(2,1)S(1)}, bf16[24,4096]{1,0:T(8,128)(2,1)S(1)}, u32[]{:S(2)}, u32[]{:S(2)}) collective-permute-start(bf16[24,4096]{1,0:T(8,128)(2,1)S(1)} %collective-permute-done.17), channel_id=1, source_target_pairs={{0,4},{1,5},{2,6},{3,7},{4,0},{5,1},{6,2},{7,3},{8,12},{9,13},{10,... | collective-permute-start | bytes 589832 | tf_op jit(solution)/shard_map/ppermute | solution.py:68
  43.1 5.9 %collective-permute-start.14 = (bf16[16,2048]{1,0:T(8,128)(2,1)S(1)}, bf16[16,2048]{1,0:T(8,128)(2,1)S(1)}, u32[]{:S(2)}, u32[]{:S(2)}) collective-permute-start(bf16[16,2048]{1,0:T(8,128)(2,1)S(1)} %get-tuple-element.30), channel_id=1, source_target_pairs={{0,6},{1,7},{2,4},{3,5},{4,2},{5,3},{6,0},{7,1},{8,14},{9,15},{10,... | collective-permute-start | bytes 196616 | tf_op jit(solution)/shard_map/ppermute | solution.py:68
  44.6 5.8 %collective-permute-start.13 = (bf16[16,2048]{1,0:T(8,128)(2,1)S(1)}, bf16[16,2048]{1,0:T(8,128)(2,1)S(1)}, u32[]{:S(2)}, u32[]{:S(2)}) collective-permute-start(bf16[16,2048]{1,0:T(8,128)(2,1)S(1)} %get-tuple-element.31), channel_id=1, source_target_pairs={{0,2},{1,3},{2,0},{3,1},{4,6},{5,7},{6,4},{7,5},{8,10},{9,11},{10,... | collective-permute-start | bytes 196616 | tf_op jit(solution)/shard_map/ppermute | solution.py:68
  46.0 5.9 %collective-permute-start.11 = (bf16[16,2048]{1,0:T(8,128)(2,1)S(1)}, bf16[16,2048]{1,0:T(8,128)(2,1)S(1)}, u32[]{:S(2)}, u32[]{:S(2)}) collective-permute-start(bf16[16,2048]{1,0:T(8,128)(2,1)S(1)} %get-tuple-element.32), channel_id=1, source_target_pairs={{0,8},{1,9},{2,10},{3,11},{4,12},{5,13},{6,14},{7,15},{8,0},{9,1},... | collective-permute-start | bytes 196616 | tf_op jit(solution)/shard_map/ppermute | solution.py:68
  46.9 5.7 %collective-permute-start.21 = (bf16[24,4096]{1,0:T(8,128)(2,1)S(1)}, bf16[24,4096]{1,0:T(8,128)(2,1)S(1)}, u32[]{:S(2)}, u32[]{:S(2)}) collective-permute-start(bf16[24,4096]{1,0:T(8,128)(2,1)S(1)} %collective-permute-done.18), channel_id=1, source_target_pairs={{0,8},{1,9},{2,10},{3,11},{4,12},{5,13},{6,14},{7,15},{8,0},{9,1},... | collective-permute-start | bytes 589832 | tf_op jit(solution)/shard_map/ppermute | solution.py:68
  50.4 7.3 %collective-permute-start.23 = (bf16[24,4096]{1,0:T(8,128)(2,1)S(1)}, bf16[24,4096]{1,0:T(8,128)(2,1)S(1)}, u32[]{:S(2)}, u32[]{:S(2)}) collective-permute-start(bf16[24,4096]{1,0:T(8,128)(2,1)S(1)} %collective-permute-done.19), channel_id=1, source_target_pairs={{0,6},{1,7},{2,4},{3,5},{4,2},{5,3},{6,0},{7,1},{8,14},{9,15},{10,... | collective-permute-start | bytes 589832 | tf_op jit(solution)/shard_map/ppermute | solution.py:68
  52.0 32.5 %collective-permute-start.15 = (bf16[16,2048]{1,0:T(8,128)(2,1)S(1)}, bf16[16,2048]{1,0:T(8,128)(2,1)S(1)}, u32[]{:S(2)}, u32[]{:S(2)}) collective-permute-start(bf16[16,2048]{1,0:T(8,128)(2,1)S(1)} %get-tuple-element.27), channel_id=1, source_target_pairs={{0,8},{1,9},{2,10},{3,11},{4,12},{5,13},{6,14},{7,15},{8,0},{9,1},... | collective-permute-start | bytes 196616 | tf_op jit(solution)/shard_map/ppermute | solution.py:68
  61.5 5.9 %collective-permute-start.24 = (bf16[24,2048]{1,0:T(8,128)(2,1)S(1)}, bf16[24,2048]{1,0:T(8,128)(2,1)S(1)}, u32[]{:S(2)}, u32[]{:S(2)}) collective-permute-start(bf16[24,2048]{1,0:T(8,128)(2,1)S(1)} %get-tuple-element.22), channel_id=1, source_target_pairs={{0,4},{1,5},{2,6},{3,7},{4,0},{5,1},{6,2},{7,3},{8,12},{9,13},{10,... | collective-permute-start | bytes 294920 | tf_op jit(solution)/shard_map/ppermute | solution.py:68
  67.5 21.1 %collective-permute-start.32 = (bf16[320,2048]{1,0:T(8,128)(2,1)S(1)}, bf16[320,2048]{1,0:T(8,128)(2,1)S(1)}, u32[]{:S(2)}, u32[]{:S(2)}) collective-permute-start(bf16[320,2048]{1,0:T(8,128)(2,1)S(1)} %fusion.13), channel_id=1, source_target_pairs={{0,1},{1,0},{2,3},{3,2},{4,5},{5,4},{6,7},{7,6},{8,9},{9,8},{10,11... | collective-permute-start | bytes 3932168 | tf_op jit(solution)/shard_map/ppermute | solution.py:68
  74.5 10.0 %collective-permute-start.12 = (bf16[16,2048]{1,0:T(8,128)(2,1)S(1)}, bf16[16,2048]{1,0:T(8,128)(2,1)S(1)}, u32[]{:S(2)}, u32[]{:S(2)}) collective-permute-start(bf16[16,2048]{1,0:T(8,128)(2,1)S(1)} %get-tuple-element.28), channel_id=1, source_target_pairs={{0,4},{1,5},{2,6},{3,7},{4,0},{5,1},{6,2},{7,3},{8,12},{9,13},{10,... | collective-permute-start | bytes 196616 | tf_op jit(solution)/shard_map/ppermute | solution.py:68
  75.0 15.9 %collective-permute-start.33 = (bf16[320,2048]{1,0:T(8,128)(2,1)S(1)}, bf16[320,2048]{1,0:T(8,128)(2,1)S(1)}, u32[]{:S(2)}, u32[]{:S(2)}) collective-permute-start(bf16[320,2048]{1,0:T(8,128)(2,1)S(1)} %fusion.14), channel_id=1, source_target_pairs={{0,1},{1,0},{2,3},{3,2},{4,5},{5,4},{6,7},{7,6},{8,9},{9,8},{10,11... | collective-permute-start | bytes 3932168 | tf_op jit(solution)/shard_map/ppermute | solution.py:68
  75.4 7.9 %collective-permute-start.31 = (bf16[24,2048]{1,0:T(8,128)(2,1)S(1)}, bf16[24,2048]{1,0:T(8,128)(2,1)S(1)}, u32[]{:S(2)}, u32[]{:S(2)}) collective-permute-start(bf16[24,2048]{1,0:T(8,128)(2,1)S(1)} %add_convert_fusion), channel_id=1, source_target_pairs={{0,16},{1,17},{2,18},{3,19},{4,20},{5,21},{6,22},{7,23},{8,24},{9,... | collective-permute-start | bytes 294920 | tf_op jit(solution)/shard_map/ppermute | solution.py:127
  (13 other events, 74.8 us)

commit v5 on v4

--- a/solution.py
+++ b/solution.py
@@ -1,6 +1,8 @@
 import jax
 import jax.numpy as jnp
 from jax import lax
+from jax.experimental import pallas as pl
+from jax.experimental.pallas import tpu as pltpu
 from jax.sharding import PartitionSpec as P
 
 FF = 5120
@@ -39,14 +41,54 @@
     )
 
 
-def summed_grads(attn_partials, gate):
+def summed_grads(attn_partials):
     if lax.axis_size("dp") == 1:
-        out_grad = attn_partials[0].astype(jnp.float32)
-    else:
-        out_grad = lax.psum_scatter(
-            attn_partials[0], "dp", scatter_dimension=0, tiled=True
-        ).astype(jnp.float32)
-    return (gate[:, None] * out_grad).astype(jnp.bfloat16)
+        return attn_partials[0]
+    return lax.psum_scatter(attn_partials[0], "dp", scatter_dimension=0, tiled=True)
+
+
+def pack_kernel(blocks, capacity, experts, n_in, *refs):
+    ids_ref, gate_ref, tokens_ref, grads_ref = refs[:4]
+    outs = refs[n_in:]
+    n, width = tokens_ref.shape
+    mine = (lax.axis_index("expert") // SHARDS).astype(jnp.float32)
+    ids = ids_ref[...].astype(jnp.float32)
+    relative = ids - mine
+    relative = jnp.where(relative < 0.0, relative + experts, relative)
+    down = lax.broadcasted_iota(jnp.int32, (n, n), 0)
+    across = lax.broadcasted_iota(jnp.int32, (n, n), 1)
+    ids_down = jnp.sum(jnp.where(down == across, ids, 0.0), axis=1, keepdims=True)
+    gate_down = jnp.sum(jnp.where(down == across, gate_ref[...], 0.0), axis=1, keepdims=True)
+    rivals = jnp.where((ids_down == ids) & (down < across), 1.0, 0.0)
+    rank = jnp.sum(rivals, axis=0, keepdims=True)
+    gated = (gate_down * grads_ref[...].astype(jnp.float32)).astype(jnp.bfloat16)
+    for k, (expert, begin, end, row) in enumerate(blocks):
+        rows_ref, pick_ref = outs[2 * k], outs[2 * k + 1]
+        chosen = (relative == expert) & (rank >= begin) & (rank < end)
+        slot = jnp.where(chosen, rank - begin + row, -1.0).astype(jnp.int32)
+        slots = lax.broadcasted_iota(jnp.int32, pick_ref.shape, 0)
+        pick = jnp.where(slots == slot, 1.0, 0.0).astype(jnp.bfloat16)
+        pick_ref[...] = pick
+        for half, source in enumerate((tokens_ref[...], gated)):
+            rows_ref[:, half * width : (half + 1) * width] = jnp.dot(
+                pick, source, preferred_element_type=jnp.float32
+            ).astype(jnp.bfloat16)
+
+
+def pack(blocks, rows, capacity, experts, ids, gate, tokens, grads, *awaited):
+    n, width = tokens.shape
+    shapes = []
+    for count in rows:
+        shapes.append(jax.ShapeDtypeStruct((count, 2 * width), jnp.bfloat16))
+        shapes.append(jax.ShapeDtypeStruct((count, n), jnp.bfloat16))
+    whole = pl.BlockSpec(memory_space=pltpu.VMEM)
+    outs = pl.pallas_call(
+        lambda *refs: pack_kernel(blocks, capacity, experts, 4 + len(awaited), *refs),
+        out_shape=shapes,
+        in_specs=[whole] * 4 + [pl.BlockSpec(memory_space=pl.ANY)] * len(awaited),
+        out_specs=[whole] * len(shapes),
+    )(ids.reshape(1, n), gate.reshape(1, n), tokens, grads, *awaited)
+    return outs[::2], outs[1::2]
 
 
 def whole_weights(shard):
@@ -69,6 +111,7 @@
 
 
 core_bit, x_bit, y_bit, z_bit = 1, 2, 4, 8
+direct_masks = (2, 4, 8, 6, 12, 10, 14)
 
 
 def after(values, *others):
@@ -126,29 +169,16 @@
         pairs = [(i, (i + SHARDS * hops) % n_expert) for i in range(n_expert)]
         return lax.ppermute(rows, "expert", pairs)
 
-    my_expert = lax.axis_index("expert") // SHARDS
-    relative = lax.rem(expert_ids - my_expert + experts, experts)
-    expert_range = jnp.arange(experts, dtype=jnp.int32)
-    member = (relative[:, None] == expert_range[None, :]).astype(jnp.int32)
-    slot_rank = jnp.sum(member * (jnp.cumsum(member, axis=0) - 1), axis=1)
-    across = (relative - 1) * capacity + slot_rank
-    late = (experts - 1) * capacity + slot_rank - first
-
-    def one_hot(rows, index, chosen):
-        index = jnp.where(chosen & (slot_rank < capacity), index, -1)
-        return (jnp.arange(rows, dtype=jnp.int32)[:, None] == index[None, :]).astype(jnp.bfloat16)
-
-    picks = [
-        one_hot(first, slot_rank, (relative == 0) & (slot_rank < first)),
-        one_hot(rest, late, (relative == 0) & (slot_rank >= first)),
-    ] + [one_hot(rest, across, relative == s) for s in range(1, experts)]
-
-    gated = summed_grads(attn_partials, gate)
-    both = jnp.concatenate([tokens, gated], axis=1)
-    packed = [
-        jnp.dot(pick, both, preferred_element_type=jnp.float32).astype(jnp.bfloat16)
-        for pick in picks
-    ]
+    offset = (experts - 1) * capacity - first
+    own_blocks = [(0, 0, first, 0), (0, first, capacity, offset + first)]
+    cross_blocks = [(s, 0, capacity, (s - 1) * capacity) for s in range(1, experts)]
+    grads = summed_grads(attn_partials)
+    sent, sent_picks = pack(
+        cross_blocks, [rest] * len(cross_blocks), capacity, experts, expert_ids, gate, tokens, grads
+    )
+    (early_own, late_own), own_picks = pack(
+        own_blocks, [first, rest], capacity, experts, expert_ids, gate, tokens, grads, *sent
+    )
 
     def paired(weights):
         own = whole_weights(weights).T
@@ -166,15 +196,12 @@
         parts = jnp.dot(pre_grad, weights_in, preferred_element_type=jnp.float32) * scale_in
         return parts.astype(jnp.bfloat16)
 
-    early_near = first_hop(packed[0])
+    for s in range(1, experts):
+        late_own = late_own + shifted(sent[s - 1], s)
+    early_blocks = [early_own] + [swap(early_own, mask) for mask in direct_masks]
     weights_in, weights_out = paired(w_in), paired(w_out)
-    late_own = packed[1]
-    for s in range(1, experts):
-        late_own = late_own + shifted(packed[s + 1], s)
-    early_far = second_hop(*early_near)
-    late_own = after(late_own, early_near)
     late_near = first_hop(late_own)
-    early_rows = jnp.concatenate([packed[0], *early_near, *early_far], axis=0)
+    early_rows = after(jnp.concatenate(early_blocks, axis=0), late_own)
     early = activated(early_rows)
     late_near = after(late_near, early[3])
     late_far = second_hop(*late_near)
@@ -183,10 +210,13 @@
     late_rows = jnp.concatenate([late_own, *late_near, *late_far], axis=0)
     later = activated(late_rows)
     late_parts = input_parts(later[3])
-    early_back = second_hop_back(early_parts)
+    early_back = [early_parts[:first]] + [
+        swap(early_parts[k * first : (k + 1) * first], mask)
+        for k, mask in enumerate(direct_masks, 1)
+    ]
     late_back = second_hop_back(late_parts)
-    early_sum = first_hop_back(*early_back)
-    late_sum = first_hop_back(*late_back)
+    early_sum = total(*early_back)
+    late_sum = after(first_hop_back(*late_back), early_sum)
     returned = [early_sum, late_sum] + [shifted(late_sum, -s) for s in range(1, experts)]
 
     def step(weights, left, right, scale):
@@ -197,6 +227,8 @@
 
     new_w_in = step(w_in, 3, 0, scale_in)
     new_w_out = step(w_out, 2, 1, scale_out)
+    returned = after(returned, new_w_in, new_w_out)
+    picks = [*own_picks, *sent_picks]
     token_grad = sum(contract_rows(pick, rows) for pick, rows in zip(picks, returned))
     return (token_grad.astype(jnp.bfloat16), new_w_in, new_w_out)
 

time: 93.4 us -> 84.3 us (0.903)
  waiting for transfers between devices: 38.8 us -> 17.4 us
  starting transfers between devices: 31 us -> 42.7 us
  Pallas kernels: 0 us -> 4.31 us
  other arithmetic: 5.09 us -> 2.36 us
  matrix products: 17 us -> 15.3 us
    ppermute x32, waiting for transfers between devices: 25.7 us -> 12.4 us  [swap(): lax.ppermute(rows, 'expert', [(i, i ^ mask) for i in range(n_expert)])]
    ppermute x32, starting transfers between devices: 25.7 us -> 38.1 us  [swap(): lax.ppermute(rows, 'expert', [(i, i ^ mask) for i in range(n_expert)])]
    ppermute x2, waiting for transfers between devices: 13.1 us -> 5.01 us  [shifted(): return lax.ppermute(rows, 'expert', pairs)]
    pallas_call x0 -> x2, Pallas kernels: none -> 4.31 us  [pack(): pl.pallas_call(lambda *refs: pack_kernel(blocks, capacity, experts, 4 + l...]
    dot_general x3 -> x0, matrix products: 1.68 us -> none  [shards(): jnp.dot(pick, both, preferred_element_type=jnp.float32).astype(jnp.bfloat16)]
    convert_element_type x2 -> x0, other arithmetic: 1.18 us -> none  [the longest x1 1.11 us: summed_grads(): return (gate[:, None] * out_grad).astype(jnp.bfloat16)]
  transfers between devices with their start and end apart: 34 -> 34, of which waited for: 18 -> 12; matrix products, arithmetic and copies ran while one was open for 17% -> 20% of each run, Pallas kernels for 0% -> 0%
where the time goes in v5:
time: 84.3 us; the launch traced here: 84.1 us
  starting transfers between devices  42.7 us (51%)
  waiting for transfers between devices  17.4 us (21%)
  matrix products  15.3 us (18%)
  Pallas kernels  4.31 us (5%)
  other arithmetic  2.36 us (3%)
  between operations  1.01 us (1%)
  local copies, waits for them, and re-layouts  0.96 us (1%)
    ppermute x32, starting transfers between devices, swap(): lax.ppermute(rows, 'expert', [(i, i ^ mask) for i in range(n_expert)])  38.1 us
    ppermute x32, waiting for transfers between devices, swap(): lax.ppermute(rows, 'expert', [(i, i ^ mask) for i in range(n_expert)])  12.4 us
    dot_general x11, matrix products, contract_rows(): lax.dot_general(left, right, (((0,), (0,)), ((), ())), preferred_element_...  9.65 us
    ppermute x2, waiting for transfers between devices, shifted(): return lax.ppermute(rows, 'expert', pairs)  5.01 us
    ppermute x2, starting transfers between devices, shifted(): return lax.ppermute(rows, 'expert', pairs)  4.61 us
    dot_general x4, matrix products, contract_cols(): lax.dot_general(left, right, (((1,), (1,)), ((), ())), preferred_element_...  4.33 us
    pallas_call x2, Pallas kernels, pack(): pl.pallas_call(lambda *refs: pack_kernel(blocks, capacity, experts, 4 + l...  4.31 us
    transpose x2, other arithmetic, paired(): own = whole_weights(weights).T  2.09 us
  transfers between devices with their start and end apart: 34, of which 12 were waited for; matrix products, arithmetic and copies ran while one was open for 20% of the time, Pallas kernels for 0%

profile of v5, /device:TPU:0, one launch (start us, length us, event | category | flops | bytes accessed | tf_op | source)
XLA Modules:
  0.0 84.1 jit_solution(2046286869260000567)
XLA Ops:
  0.6 2.2 %shard_map.85 = (bf16[24,4096]{1,0:T(8,128)(2,1)}, bf16[24,64]{1,0:T(8,128)(2,1)}) custom-call(s32[1,64]{1,0:T(1,128)} %bitcast.21, f32[1,64]{1,0:T(1,128)} %bitcast.23, bf16[64,2048]{1,0:T(8,128)(2,1)} %refs_2_.3, bf16[64,2048]{1,0:T(8,128)(2,1)} %bitcast.19), custom_call_target="tpu_custom_call" | custom-call | tf_op jit(solution)/shard_map/pallas_call | solution.py:85
  2.8 2.1 %shard_map.86 = (bf16[16,4096]{1,0:T(8,128)(2,1)}, bf16[16,64]{1,0:T(8,128)(2,1)}, bf16[24,4096]{1,0:T(8,128)(2,1)}, bf16[24,64]{1,0:T(8,128)(2,1)}) custom-call(s32[1,64]{1,0:T(1,128)} %bitcast.22, f32[1,64]{1,0:T(1,128)} %bitcast.24, bf16[64,2048]{1,0:T(8,128)(2,1)} %refs_2_.3, bf16[64,2048]{1,0:T(8,128)(2,1)} %bitcast.20, ...), custom_call_target="tpu_custom_call" | custom-call | tf_op jit(solution)/shard_map/pallas_call | solution.py:85
  5.0 2.9 %collective-permute-start = (bf16[16,4096]{1,0:T(8,128)(2,1)}, bf16[16,4096]{1,0:T(8,128)(2,1)S(1)}, u32[]{:S(2)}, u32[]{:S(2)}) collective-permute-start(bf16[16,4096]{1,0:T(8,128)(2,1)} %get-tuple-element.23), channel_id=1, source_target_pairs={{0,2},{1,3},{2,0},{3,1},{4,6},{5,7},{6,4},{7,5},{8,10},{9,11},{10,... | collective-permute-start | bytes 393224 | tf_op jit(solution)/shard_map/ppermute | solution.py:110
  7.9 1.5 %collective-permute-start.1 = (bf16[16,4096]{1,0:T(8,128)(2,1)}, bf16[16,4096]{1,0:T(8,128)(2,1)S(1)}, u32[]{:S(2)}, u32[]{:S(2)}) collective-permute-start(bf16[16,4096]{1,0:T(8,128)(2,1)} %get-tuple-element.23), channel_id=1, source_target_pairs={{0,4},{1,5},{2,6},{3,7},{4,0},{5,1},{6,2},{7,3},{8,12},{9,13},{10,... | collective-permute-start | bytes 393224 | tf_op jit(solution)/shard_map/ppermute | solution.py:110
  9.4 1.6 %collective-permute-start.2 = (bf16[16,4096]{1,0:T(8,128)(2,1)}, bf16[16,4096]{1,0:T(8,128)(2,1)S(1)}, u32[]{:S(2)}, u32[]{:S(2)}) collective-permute-start(bf16[16,4096]{1,0:T(8,128)(2,1)} %get-tuple-element.23), channel_id=1, source_target_pairs={{0,8},{1,9},{2,10},{3,11},{4,12},{5,13},{6,14},{7,15},{8,0},{9,1},... | collective-permute-start | bytes 393224 | tf_op jit(solution)/shard_map/ppermute | solution.py:110
  12.9 1.9 %convert_bitcast_fusion.1 = bf16[320,2048]{1,0:T(8,128)(2,1)S(1)} fusion(f32[2048,320]{0,1:T(8,128)} %param.11), kind=kLoop, calls=%fused_computation.24 | loop fusion | flops 655360 | bytes 3932160 | tf_op jit(solution)/shard_map/transpose | solution.py:184
  15.7 2.6 %collective-permute-start.5 = (bf16[16,4096]{1,0:T(8,128)(2,1)S(1)}, bf16[16,4096]{1,0:T(8,128)(2,1)S(1)}, u32[]{:S(2)}, u32[]{:S(2)}) collective-permute-start(bf16[16,4096]{1,0:T(8,128)(2,1)S(1)} %copy-done.4), channel_id=1, source_target_pairs={{0,10},{1,11},{2,8},{3,9},{4,14},{5,15},{6,12},{7,13},{8,2},{9,3},... | collective-permute-start | bytes 393224 | tf_op jit(solution)/shard_map/ppermute | solution.py:110
  18.3 2.8 %collective-permute-start.6 = (bf16[16,4096]{1,0:T(8,128)(2,1)S(1)}, bf16[16,4096]{1,0:T(8,128)(2,1)S(1)}, u32[]{:S(2)}, u32[]{:S(2)}) collective-permute-start(bf16[16,4096]{1,0:T(8,128)(2,1)S(1)} %copy-done.4), channel_id=1, source_target_pairs={{0,14},{1,15},{2,12},{3,13},{4,10},{5,11},{6,8},{7,9},{8,6},{9,7},... | collective-permute-start | bytes 393224 | tf_op jit(solution)/shard_map/ppermute | solution.py:110
  21.1 2.6 %collective-permute-start.7 = (bf16[24,4096]{1,0:T(8,128)(2,1)S(1)}, bf16[24,4096]{1,0:T(8,128)(2,1)S(1)}, u32[]{:S(2)}, u32[]{:S(2)}) collective-permute-start(bf16[24,4096]{1,0:T(8,128)(2,1)S(1)} %copy-done.3), channel_id=1, source_target_pairs={{0,16},{1,17},{2,18},{3,19},{4,20},{5,21},{6,22},{7,23},{8,24},{9,... | collective-permute-start | bytes 589832 | tf_op jit(solution)/shard_map/ppermute | solution.py:170
  26.2 5.0 %collective-permute-done.7 = bf16[24,4096]{1,0:T(8,128)(2,1)S(1)} collective-permute-done((bf16[24,4096]{1,0:T(8,128)(2,1)S(1)}, bf16[24,4096]{1,0:T(8,128)(2,1)S(1)}, u32[]{:S(2)}, u32[]{:S(2)}) %collective-permute-start.7) | collective-permute-done | bytes 196640 | tf_op jit(solution)/shard_map/ppermute | solution.py:170
  35.1 2.6 %collective-permute-done.17 = bf16[24,4096]{1,0:T(8,128)(2,1)S(1)} collective-permute-done((bf16[24,4096]{1,0:T(8,128)(2,1)S(1)}, bf16[24,4096]{1,0:T(8,128)(2,1)S(1)}, u32[]{:S(2)}, u32[]{:S(2)}) %collective-permute-start.17) | collective-permute-done | bytes 196640 | tf_op jit(solution)/shard_map/ppermute | solution.py:110
  39.3 2.0 %collective-permute-start.23 = (bf16[24,4096]{1,0:T(8,128)(2,1)S(1)}, bf16[24,4096]{1,0:T(8,128)(2,1)S(1)}, u32[]{:S(2)}, u32[]{:S(2)}) collective-permute-start(bf16[24,4096]{1,0:T(8,128)(2,1)S(1)} %collective-permute-done.19), channel_id=1, source_target_pairs={{0,6},{1,7},{2,4},{3,5},{4,2},{5,3},{6,0},{7,1},{8,14},{9,15},{10,... | collective-permute-start | bytes 589832 | tf_op jit(solution)/shard_map/ppermute | solution.py:110
  43.7 1.6 %collective-permute-start.20 = (bf16[24,4096]{1,0:T(8,128)(2,1)S(1)}, bf16[24,4096]{1,0:T(8,128)(2,1)S(1)}, u32[]{:S(2)}, u32[]{:S(2)}) collective-permute-start(bf16[24,4096]{1,0:T(8,128)(2,1)S(1)} %collective-permute-done.17), channel_id=1, source_target_pairs={{0,4},{1,5},{2,6},{3,7},{4,0},{5,1},{6,2},{7,3},{8,12},{9,13},{10,... | collective-permute-start | bytes 589832 | tf_op jit(solution)/shard_map/ppermute | solution.py:110
  45.3 2.1 %collective-permute-start.21 = (bf16[24,4096]{1,0:T(8,128)(2,1)S(1)}, bf16[24,4096]{1,0:T(8,128)(2,1)S(1)}, u32[]{:S(2)}, u32[]{:S(2)}) collective-permute-start(bf16[24,4096]{1,0:T(8,128)(2,1)S(1)} %collective-permute-done.18), channel_id=1, source_target_pairs={{0,8},{1,9},{2,10},{3,11},{4,12},{5,13},{6,14},{7,15},{8,0},{9,1},... | collective-permute-start | bytes 589832 | tf_op jit(solution)/shard_map/ppermute | solution.py:110
  48.5 2.3 %collective-permute-done.20 = bf16[24,4096]{1,0:T(8,128)(2,1)S(1)} collective-permute-done((bf16[24,4096]{1,0:T(8,128)(2,1)S(1)}, bf16[24,4096]{1,0:T(8,128)(2,1)S(1)}, u32[]{:S(2)}, u32[]{:S(2)}) %collective-permute-start.20) | collective-permute-done | bytes 196640 | tf_op jit(solution)/shard_map/ppermute | solution.py:110
  50.8 1.9 %collective-permute-start.15 = (bf16[16,2048]{1,0:T(8,128)(2,1)S(1)}, bf16[16,2048]{1,0:T(8,128)(2,1)S(1)}, u32[]{:S(2)}, u32[]{:S(2)}) collective-permute-start(bf16[16,2048]{1,0:T(8,128)(2,1)S(1)} %get-tuple-element.50), channel_id=1, source_target_pairs={{0,10},{1,11},{2,8},{3,9},{4,14},{5,15},{6,12},{7,13},{8,2},{9,3},... | collective-permute-start | bytes 196616 | tf_op jit(solution)/shard_map/ppermute | solution.py:110
  58.2 1.8 %collective-permute-start.29 = (bf16[24,2048]{1,0:T(8,128)(2,1)S(1)}, bf16[24,2048]{1,0:T(8,128)(2,1)S(1)}, u32[]{:S(2)}, u32[]{:S(2)}) collective-permute-start(bf16[24,2048]{1,0:T(8,128)(2,1)S(1)} %get-tuple-element.45), channel_id=1, source_target_pairs={{0,6},{1,7},{2,4},{3,5},{4,2},{5,3},{6,0},{7,1},{8,14},{9,15},{10,... | collective-permute-start | bytes 294920 | tf_op jit(solution)/shard_map/ppermute | solution.py:110
  65.4 1.6 %collective-permute-start.11 = (bf16[16,2048]{1,0:T(8,128)(2,1)S(1)}, bf16[16,2048]{1,0:T(8,128)(2,1)S(1)}, u32[]{:S(2)}, u32[]{:S(2)}) collective-permute-start(bf16[16,2048]{1,0:T(8,128)(2,1)S(1)} %get-tuple-element.54), channel_id=1, source_target_pairs={{0,4},{1,5},{2,6},{3,7},{4,0},{5,1},{6,2},{7,3},{8,12},{9,13},{10,... | collective-permute-start | bytes 196616 | tf_op jit(solution)/shard_map/ppermute | solution.py:110
  69.8 1.5 %collective-permute-start.27 = (bf16[24,2048]{1,0:T(8,128)(2,1)S(1)}, bf16[24,2048]{1,0:T(8,128)(2,1)S(1)}, u32[]{:S(2)}, u32[]{:S(2)}) collective-permute-start(bf16[24,2048]{1,0:T(8,128)(2,1)S(1)} %get-tuple-element.43), channel_id=1, source_target_pairs={{0,4},{1,5},{2,6},{3,7},{4,0},{5,1},{6,2},{7,3},{8,12},{9,13},{10,... | collective-permute-start | bytes 294920 | tf_op jit(solution)/shard_map/ppermute | solution.py:110
  72.1 1.8 %collective-permute-done.30 = bf16[24,2048]{1,0:T(8,128)(2,1)S(1)} collective-permute-done((bf16[24,2048]{1,0:T(8,128)(2,1)S(1)}, bf16[24,2048]{1,0:T(8,128)(2,1)S(1)}, u32[]{:S(2)}, u32[]{:S(2)}) %collective-permute-start.30) | collective-permute-done | bytes 98336 | tf_op jit(solution)/shard_map/ppermute | solution.py:110
  74.4 1.5 %collective-permute-done.25 = bf16[24,2048]{1,0:T(8,128)(2,1)S(1)} collective-permute-done((bf16[24,2048]{1,0:T(8,128)(2,1)S(1)}, bf16[24,2048]{1,0:T(8,128)(2,1)S(1)}, u32[]{:S(2)}, u32[]{:S(2)}) %collective-permute-start.25) | collective-permute-done | bytes 98336 | tf_op jit(solution)/shard_map/ppermute | solution.py:110
  76.0 2.0 %collective-permute-start.31 = (bf16[24,2048]{1,0:T(8,128)(2,1)S(1)}, bf16[24,2048]{1,0:T(8,128)(2,1)S(1)}, u32[]{:S(2)}, u32[]{:S(2)}) collective-permute-start(bf16[24,2048]{1,0:T(8,128)(2,1)S(1)} %add_convert_fusion), channel_id=1, source_target_pairs={{0,16},{1,17},{2,18},{3,19},{4,20},{5,21},{6,22},{7,23},{8,24},{9,... | collective-permute-start | bytes 294920 | tf_op jit(solution)/shard_map/ppermute | solution.py:170
  77.9 2.4 %bitcast_subtract_fusion.1 = f32[2048,320]{0,1:T(8,128)} fusion(f32[2048,320]{0,1:T(8,128)S(1)} %copy-done, bf16[320,2048]{1,0:T(8,128)(2,1)S(1)} %collective-permute-done.32, f32[320,2048]{1,0:T(8,128)S(1)} %fusion.30, bf16[192,4096]{1,0:T(8,128)(2,1)S(1)} %constant_dynamic-update-slice_fusion.8, bf16[192,640]{1,0:T(8,128)(2,1)S(1)} %fusion.14), kind=kOutput, calls=%fused_computation.13 | convolution fusion | flops 255590400 | bytes 10108928 | tf_op jit(solution)/shard_map/dot_general | solution.py:33
  80.3 2.3 %bitcast_subtract_fusion = f32[2048,320]{0,1:T(8,128)} fusion(f32[2048,320]{0,1:T(8,128)S(1)} %copy-done.1, bf16[320,2048]{1,0:T(8,128)(2,1)S(1)} %collective-permute-done.33, f32[320,2048]{1,0:T(8,128)S(1)} %fusion.36, bf16[192,4096]{1,0:T(8,128)(2,1)S(1)} %constant_dynamic-update-slice_fusion.8, bf16[192,640]{1,0:T(8,128)(2,1)S(1)} %get-tuple-element.57), kind=kOutput, calls=%fused_computation.12 | convolution fusion | flops 255590400 | bytes 10108928 | tf_op jit(solution)/shard_map/dot_general | solution.py:33
  (102 shorter events, 30.6 us)
Async XLA Ops:
  5.0 10.8 %collective-permute-start = (bf16[16,4096]{1,0:T(8,128)(2,1)}, bf16[16,4096]{1,0:T(8,128)(2,1)S(1)}, u32[]{:S(2)}, u32[]{:S(2)}) collective-permute-start(bf16[16,4096]{1,0:T(8,128)(2,1)} %get-tuple-element.23), channel_id=1, source_target_pairs={{0,2},{1,3},{2,0},{3,1},{4,6},{5,7},{6,4},{7,5},{8,10},{9,11},{10,... | collective-permute-start | bytes 393224 | tf_op jit(solution)/shard_map/ppermute | solution.py:110
  7.9 10.4 %collective-permute-start.1 = (bf16[16,4096]{1,0:T(8,128)(2,1)}, bf16[16,4096]{1,0:T(8,128)(2,1)S(1)}, u32[]{:S(2)}, u32[]{:S(2)}) collective-permute-start(bf16[16,4096]{1,0:T(8,128)(2,1)} %get-tuple-element.23), channel_id=1, source_target_pairs={{0,4},{1,5},{2,6},{3,7},{4,0},{5,1},{6,2},{7,3},{8,12},{9,13},{10,... | collective-permute-start | bytes 393224 | tf_op jit(solution)/shard_map/ppermute | solution.py:110
  9.4 11.7 %collective-permute-start.2 = (bf16[16,4096]{1,0:T(8,128)(2,1)}, bf16[16,4096]{1,0:T(8,128)(2,1)S(1)}, u32[]{:S(2)}, u32[]{:S(2)}) collective-permute-start(bf16[16,4096]{1,0:T(8,128)(2,1)} %get-tuple-element.23), channel_id=1, source_target_pairs={{0,8},{1,9},{2,10},{3,11},{4,12},{5,13},{6,14},{7,15},{8,0},{9,1},... | collective-permute-start | bytes 393224 | tf_op jit(solution)/shard_map/ppermute | solution.py:110
  11.0 12.8 %collective-permute-start.3 = (bf16[16,4096]{1,0:T(8,128)(2,1)}, bf16[16,4096]{1,0:T(8,128)(2,1)S(1)}, u32[]{:S(2)}, u32[]{:S(2)}) collective-permute-start(bf16[16,4096]{1,0:T(8,128)(2,1)} %get-tuple-element.23), channel_id=1, source_target_pairs={{0,6},{1,7},{2,4},{3,5},{4,2},{5,3},{6,0},{7,1},{8,14},{9,15},{10,... | collective-permute-start | bytes 393224 | tf_op jit(solution)/shard_map/ppermute | solution.py:110
  11.5 12.4 %collective-permute-start.4 = (bf16[16,4096]{1,0:T(8,128)(2,1)}, bf16[16,4096]{1,0:T(8,128)(2,1)S(1)}, u32[]{:S(2)}, u32[]{:S(2)}) collective-permute-start(bf16[16,4096]{1,0:T(8,128)(2,1)} %get-tuple-element.23), channel_id=1, source_target_pairs={{0,12},{1,13},{2,14},{3,15},{4,8},{5,9},{6,10},{7,11},{8,4},{9,5},... | collective-permute-start | bytes 393224 | tf_op jit(solution)/shard_map/ppermute | solution.py:110
  15.7 9.2 %collective-permute-start.5 = (bf16[16,4096]{1,0:T(8,128)(2,1)S(1)}, bf16[16,4096]{1,0:T(8,128)(2,1)S(1)}, u32[]{:S(2)}, u32[]{:S(2)}) collective-permute-start(bf16[16,4096]{1,0:T(8,128)(2,1)S(1)} %copy-done.4), channel_id=1, source_target_pairs={{0,10},{1,11},{2,8},{3,9},{4,14},{5,15},{6,12},{7,13},{8,2},{9,3},... | collective-permute-start | bytes 393224 | tf_op jit(solution)/shard_map/ppermute | solution.py:110
  18.3 7.9 %collective-permute-start.6 = (bf16[16,4096]{1,0:T(8,128)(2,1)S(1)}, bf16[16,4096]{1,0:T(8,128)(2,1)S(1)}, u32[]{:S(2)}, u32[]{:S(2)}) collective-permute-start(bf16[16,4096]{1,0:T(8,128)(2,1)S(1)} %copy-done.4), channel_id=1, source_target_pairs={{0,14},{1,15},{2,12},{3,13},{4,10},{5,11},{6,8},{7,9},{8,6},{9,7},... | collective-permute-start | bytes 393224 | tf_op jit(solution)/shard_map/ppermute | solution.py:110
  21.1 10.1 %collective-permute-start.7 = (bf16[24,4096]{1,0:T(8,128)(2,1)S(1)}, bf16[24,4096]{1,0:T(8,128)(2,1)S(1)}, u32[]{:S(2)}, u32[]{:S(2)}) collective-permute-start(bf16[24,4096]{1,0:T(8,128)(2,1)S(1)} %copy-done.3), channel_id=1, source_target_pairs={{0,16},{1,17},{2,18},{3,19},{4,20},{5,21},{6,22},{7,23},{8,24},{9,... | collective-permute-start | bytes 589832 | tf_op jit(solution)/shard_map/ppermute | solution.py:170
  23.8 10.2 %collective-permute-start.8 = (bf16[320,2048]{1,0:T(8,128)(2,1)S(1)}, bf16[320,2048]{1,0:T(8,128)(2,1)S(1)}, u32[]{:S(2)}, u32[]{:S(2)}) collective-permute-start(bf16[320,2048]{1,0:T(8,128)(2,1)S(1)} %convert_bitcast_fusion.1), channel_id=1, source_target_pairs={{0,1},{1,0},{2,3},{3,2},{4,5},{5,4},{6,7},{7,6},{8,9},{9,8},{10,11... | collective-permute-start | bytes 3932168 | tf_op jit(solution)/shard_map/ppermute | solution.py:110
  23.9 9.1 %collective-permute-start.9 = (bf16[320,2048]{1,0:T(8,128)(2,1)S(1)}, bf16[320,2048]{1,0:T(8,128)(2,1)S(1)}, u32[]{:S(2)}, u32[]{:S(2)}) collective-permute-start(bf16[320,2048]{1,0:T(8,128)(2,1)S(1)} %convert_bitcast_fusion), channel_id=1, source_target_pairs={{0,1},{1,0},{2,3},{3,2},{4,5},{5,4},{6,7},{7,6},{8,9},{9,8},{10,11... | collective-permute-start | bytes 3932168 | tf_op jit(solution)/shard_map/ppermute | solution.py:110
  31.3 6.4 %collective-permute-start.17 = (bf16[24,4096]{1,0:T(8,128)(2,1)S(1)}, bf16[24,4096]{1,0:T(8,128)(2,1)S(1)}, u32[]{:S(2)}, u32[]{:S(2)}) collective-permute-start(bf16[24,4096]{1,0:T(8,128)(2,1)S(1)} %get-tuple-element.40), channel_id=1, source_target_pairs={{0,2},{1,3},{2,0},{3,1},{4,6},{5,7},{6,4},{7,5},{8,10},{9,11},{10,... | collective-permute-start | bytes 589832 | tf_op jit(solution)/shard_map/ppermute | solution.py:110
  38.7 15.4 %collective-permute-start.22 = (bf16[24,4096]{1,0:T(8,128)(2,1)S(1)}, bf16[24,4096]{1,0:T(8,128)(2,1)S(1)}, u32[]{:S(2)}, u32[]{:S(2)}) collective-permute-start(bf16[24,4096]{1,0:T(8,128)(2,1)S(1)} %collective-permute-done.19), channel_id=1, source_target_pairs={{0,2},{1,3},{2,0},{3,1},{4,6},{5,7},{6,4},{7,5},{8,10},{9,11},{10,... | collective-permute-start | bytes 589832 | tf_op jit(solution)/shard_map/ppermute | solution.py:110
  39.3 14.7 %collective-permute-start.23 = (bf16[24,4096]{1,0:T(8,128)(2,1)S(1)}, bf16[24,4096]{1,0:T(8,128)(2,1)S(1)}, u32[]{:S(2)}, u32[]{:S(2)}) collective-permute-start(bf16[24,4096]{1,0:T(8,128)(2,1)S(1)} %collective-permute-done.19), channel_id=1, source_target_pairs={{0,6},{1,7},{2,4},{3,5},{4,2},{5,3},{6,0},{7,1},{8,14},{9,15},{10,... | collective-permute-start | bytes 589832 | tf_op jit(solution)/shard_map/ppermute | solution.py:110
  43.0 17.6 %collective-permute-start.16 = (bf16[16,2048]{1,0:T(8,128)(2,1)S(1)}, bf16[16,2048]{1,0:T(8,128)(2,1)S(1)}, u32[]{:S(2)}, u32[]{:S(2)}) collective-permute-start(bf16[16,2048]{1,0:T(8,128)(2,1)S(1)} %get-tuple-element.49), channel_id=1, source_target_pairs={{0,14},{1,15},{2,12},{3,13},{4,10},{5,11},{6,8},{7,9},{8,6},{9,7},... | collective-permute-start | bytes 196616 | tf_op jit(solution)/shard_map/ppermute | solution.py:110
  43.7 7.1 %collective-permute-start.20 = (bf16[24,4096]{1,0:T(8,128)(2,1)S(1)}, bf16[24,4096]{1,0:T(8,128)(2,1)S(1)}, u32[]{:S(2)}, u32[]{:S(2)}) collective-permute-start(bf16[24,4096]{1,0:T(8,128)(2,1)S(1)} %collective-permute-done.17), channel_id=1, source_target_pairs={{0,4},{1,5},{2,6},{3,7},{4,0},{5,1},{6,2},{7,3},{8,12},{9,13},{10,... | collective-permute-start | bytes 589832 | tf_op jit(solution)/shard_map/ppermute | solution.py:110
  45.3 7.5 %collective-permute-start.21 = (bf16[24,4096]{1,0:T(8,128)(2,1)S(1)}, bf16[24,4096]{1,0:T(8,128)(2,1)S(1)}, u32[]{:S(2)}, u32[]{:S(2)}) collective-permute-start(bf16[24,4096]{1,0:T(8,128)(2,1)S(1)} %collective-permute-done.18), channel_id=1, source_target_pairs={{0,8},{1,9},{2,10},{3,11},{4,12},{5,13},{6,14},{7,15},{8,0},{9,1},... | collective-permute-start | bytes 589832 | tf_op jit(solution)/shard_map/ppermute | solution.py:110
  50.8 10.8 %collective-permute-start.15 = (bf16[16,2048]{1,0:T(8,128)(2,1)S(1)}, bf16[16,2048]{1,0:T(8,128)(2,1)S(1)}, u32[]{:S(2)}, u32[]{:S(2)}) collective-permute-start(bf16[16,2048]{1,0:T(8,128)(2,1)S(1)} %get-tuple-element.50), channel_id=1, source_target_pairs={{0,10},{1,11},{2,8},{3,9},{4,14},{5,15},{6,12},{7,13},{8,2},{9,3},... | collective-permute-start | bytes 196616 | tf_op jit(solution)/shard_map/ppermute | solution.py:110
  52.7 10.8 %collective-permute-start.14 = (bf16[16,2048]{1,0:T(8,128)(2,1)S(1)}, bf16[16,2048]{1,0:T(8,128)(2,1)S(1)}, u32[]{:S(2)}, u32[]{:S(2)}) collective-permute-start(bf16[16,2048]{1,0:T(8,128)(2,1)S(1)} %get-tuple-element.51), channel_id=1, source_target_pairs={{0,12},{1,13},{2,14},{3,15},{4,8},{5,9},{6,10},{7,11},{8,4},{9,5},... | collective-permute-start | bytes 196616 | tf_op jit(solution)/shard_map/ppermute | solution.py:110
  57.2 7.4 %collective-permute-start.24 = (bf16[24,2048]{1,0:T(8,128)(2,1)S(1)}, bf16[24,2048]{1,0:T(8,128)(2,1)S(1)}, u32[]{:S(2)}, u32[]{:S(2)}) collective-permute-start(bf16[24,2048]{1,0:T(8,128)(2,1)S(1)} %get-tuple-element.44), channel_id=1, source_target_pairs={{0,4},{1,5},{2,6},{3,7},{4,0},{5,1},{6,2},{7,3},{8,12},{9,13},{10,... | collective-permute-start | bytes 294920 | tf_op jit(solution)/shard_map/ppermute | solution.py:110
  58.2 7.3 %collective-permute-start.29 = (bf16[24,2048]{1,0:T(8,128)(2,1)S(1)}, bf16[24,2048]{1,0:T(8,128)(2,1)S(1)}, u32[]{:S(2)}, u32[]{:S(2)}) collective-permute-start(bf16[24,2048]{1,0:T(8,128)(2,1)S(1)} %get-tuple-element.45), channel_id=1, source_target_pairs={{0,6},{1,7},{2,4},{3,5},{4,2},{5,3},{6,0},{7,1},{8,14},{9,15},{10,... | collective-permute-start | bytes 294920 | tf_op jit(solution)/shard_map/ppermute | solution.py:110
  60.7 6.3 %collective-permute-start.28 = (bf16[24,2048]{1,0:T(8,128)(2,1)S(1)}, bf16[24,2048]{1,0:T(8,128)(2,1)S(1)}, u32[]{:S(2)}, u32[]{:S(2)}) collective-permute-start(bf16[24,2048]{1,0:T(8,128)(2,1)S(1)} %get-tuple-element.46), channel_id=1, source_target_pairs={{0,2},{1,3},{2,0},{3,1},{4,6},{5,7},{6,4},{7,5},{8,10},{9,11},{10,... | collective-permute-start | bytes 294920 | tf_op jit(solution)/shard_map/ppermute | solution.py:110
  67.8 10.1 %collective-permute-start.32 = (bf16[320,2048]{1,0:T(8,128)(2,1)S(1)}, bf16[320,2048]{1,0:T(8,128)(2,1)S(1)}, u32[]{:S(2)}, u32[]{:S(2)}) collective-permute-start(bf16[320,2048]{1,0:T(8,128)(2,1)S(1)} %fusion.4), channel_id=1, source_target_pairs={{0,1},{1,0},{2,3},{3,2},{4,5},{5,4},{6,7},{7,6},{8,9},{9,8},{10,11... | collective-permute-start | bytes 3932168 | tf_op jit(solution)/shard_map/ppermute | solution.py:110
  68.8 11.5 %collective-permute-start.33 = (bf16[320,2048]{1,0:T(8,128)(2,1)S(1)}, bf16[320,2048]{1,0:T(8,128)(2,1)S(1)}, u32[]{:S(2)}, u32[]{:S(2)}) collective-permute-start(bf16[320,2048]{1,0:T(8,128)(2,1)S(1)} %fusion.5), channel_id=1, source_target_pairs={{0,1},{1,0},{2,3},{3,2},{4,5},{5,4},{6,7},{7,6},{8,9},{9,8},{10,11... | collective-permute-start | bytes 3932168 | tf_op jit(solution)/shard_map/ppermute | solution.py:110
  76.0 6.7 %collective-permute-start.31 = (bf16[24,2048]{1,0:T(8,128)(2,1)S(1)}, bf16[24,2048]{1,0:T(8,128)(2,1)S(1)}, u32[]{:S(2)}, u32[]{:S(2)}) collective-permute-start(bf16[24,2048]{1,0:T(8,128)(2,1)S(1)} %add_convert_fusion), channel_id=1, source_target_pairs={{0,16},{1,17},{2,18},{3,19},{4,20},{5,21},{6,22},{7,23},{8,24},{9,... | collective-permute-start | bytes 294920 | tf_op jit(solution)/shard_map/ppermute | solution.py:170
  (18 other events, 100.0 us)

commit v6 on v5

--- a/solution.py
+++ b/solution.py
@@ -47,9 +47,8 @@
     return lax.psum_scatter(attn_partials[0], "dp", scatter_dimension=0, tiled=True)
 
 
-def pack_kernel(blocks, capacity, experts, n_in, *refs):
-    ids_ref, gate_ref, tokens_ref, grads_ref = refs[:4]
-    outs = refs[n_in:]
+def pack_kernel(blocks, experts, *refs):
+    ids_ref, gate_ref, tokens_ref, grads_ref, *outs = refs
     n, width = tokens_ref.shape
     mine = (lax.axis_index("expert") // SHARDS).astype(jnp.float32)
     ids = ids_ref[...].astype(jnp.float32)
@@ -75,7 +74,7 @@
             ).astype(jnp.bfloat16)
 
 
-def pack(blocks, rows, capacity, experts, ids, gate, tokens, grads, *awaited):
+def pack(blocks, rows, experts, ids, gate, tokens, grads):
     n, width = tokens.shape
     shapes = []
     for count in rows:
@@ -83,11 +82,11 @@
         shapes.append(jax.ShapeDtypeStruct((count, n), jnp.bfloat16))
     whole = pl.BlockSpec(memory_space=pltpu.VMEM)
     outs = pl.pallas_call(
-        lambda *refs: pack_kernel(blocks, capacity, experts, 4 + len(awaited), *refs),
+        lambda *refs: pack_kernel(blocks, experts, *refs),
         out_shape=shapes,
-        in_specs=[whole] * 4 + [pl.BlockSpec(memory_space=pl.ANY)] * len(awaited),
+        in_specs=[whole] * 4,
         out_specs=[whole] * len(shapes),
-    )(ids.reshape(1, n), gate.reshape(1, n), tokens, grads, *awaited)
+    )(ids.reshape(1, n), gate.reshape(1, n), tokens, grads)
     return outs[::2], outs[1::2]
 
 
@@ -111,7 +110,7 @@
 
 
 core_bit, x_bit, y_bit, z_bit = 1, 2, 4, 8
-direct_masks = (2, 4, 8, 6, 12, 10, 14)
+far_mask = x_bit | y_bit | z_bit
 
 
 def after(values, *others):
@@ -122,36 +121,23 @@
     return swap(own, x_bit), swap(own, y_bit), swap(own, z_bit)
 
 
-def second_hop(near_x, near_y, near_z):
-    return (
-        swap(near_x, y_bit),
-        swap(near_y, z_bit),
-        swap(near_z, x_bit),
-        swap(near_z, x_bit | y_bit),
-    )
-
-
-def second_hop_back(parts):
-    rows = parts.shape[0] // 8
-    blocks = [parts[k * rows : (k + 1) * rows] for k in range(8)]
-    far = (
-        swap(blocks[4], y_bit),
-        swap(blocks[5], z_bit),
-        swap(blocks[6], x_bit),
-        swap(blocks[7], x_bit | y_bit),
-    )
-    return blocks[:4], far
+second_masks = (y_bit, z_bit, x_bit, x_bit | y_bit)
 
 
 def total(*terms):
     return sum(term.astype(jnp.float32) for term in terms).astype(jnp.bfloat16)
 
 
-def first_hop_back(near, far):
-    near_x = swap(total(near[1], far[0]), x_bit)
-    near_y = swap(total(near[2], far[1]), y_bit)
-    near_z = swap(total(near[3], far[2], far[3]), z_bit)
-    return total(near[0], near_x, near_y, near_z)
+def split_rows(array, rows):
+    return [array[k : k + rows] for k in range(0, array.shape[0], rows)]
+
+
+def near_sums(near, far):
+    return (
+        total(near[1], far[0]),
+        total(near[2], far[1]),
+        total(near[3], far[2], far[3]),
+    )
 
 
 def shards(tokens, attn_partials, expert_ids, gate, w_in, w_out):
@@ -173,16 +159,15 @@
     own_blocks = [(0, 0, first, 0), (0, first, capacity, offset + first)]
     cross_blocks = [(s, 0, capacity, (s - 1) * capacity) for s in range(1, experts)]
     grads = summed_grads(attn_partials)
-    sent, sent_picks = pack(
-        cross_blocks, [rest] * len(cross_blocks), capacity, experts, expert_ids, gate, tokens, grads
-    )
-    (early_own, late_own), own_picks = pack(
-        own_blocks, [first, rest], capacity, experts, expert_ids, gate, tokens, grads, *sent
-    )
-
-    def paired(weights):
-        own = whole_weights(weights).T
-        return jnp.concatenate([own, swap(own, core_bit)], axis=0)
+    (early_own, late_own, *sent), picks = pack(
+        own_blocks + cross_blocks,
+        [first] + [rest] * experts,
+        experts,
+        expert_ids,
+        gate,
+        tokens,
+        grads,
+    )
 
     def activated(rows):
         expert_rows, grad_rows = rows[:, :width], rows[:, width:]
@@ -198,37 +183,63 @@
 
     for s in range(1, experts):
         late_own = late_own + shifted(sent[s - 1], s)
-    early_blocks = [early_own] + [swap(early_own, mask) for mask in direct_masks]
-    weights_in, weights_out = paired(w_in), paired(w_out)
-    late_near = first_hop(late_own)
-    early_rows = after(jnp.concatenate(early_blocks, axis=0), late_own)
-    early = activated(early_rows)
-    late_near = after(late_near, early[3])
-    late_far = second_hop(*late_near)
+    early_near = first_hop(early_own)
+    early_far = swap(early_own, far_mask)
+    early_near, early_far = after((early_near, early_far), late_own)
+    arrived = [
+        swap(jnp.concatenate([rows, late_own], axis=0), mask)
+        for rows, mask in zip(
+            (early_near[2], early_near[0], early_near[1]), (x_bit, y_bit, z_bit)
+        )
+    ]
+    early_zx, early_xy, early_yz = [rows[:first] for rows in arrived]
+    late_near = [rows[first:] for rows in arrived]
+    early_rows = [early_own, *early_near, early_xy, early_yz, early_zx, early_far]
+
+    own_weights = jnp.concatenate([whole_weights(w_in).T, whole_weights(w_out).T], axis=0)
+    their_weights = swap(after(own_weights, late_own), core_bit)
+    weights_in, weights_out = [
+        jnp.concatenate([own_weights[part], their_weights[part]], axis=0)
+        for part in (slice(0, units), slice(units, 2 * units))
+    ]
+    near_x, near_y, near_z = late_near
+    late_far = [
+        swap(rows, mask) for rows, mask in zip((near_x, near_y, near_z, near_z), second_masks)
+    ]
+    early = activated(jnp.concatenate(early_rows, axis=0))
     early_parts = input_parts(early[3])
     late_far = after(late_far, early_parts)
-    late_rows = jnp.concatenate([late_own, *late_near, *late_far], axis=0)
-    later = activated(late_rows)
+    later = activated(jnp.concatenate([late_own, *late_near, *late_far], axis=0))
     late_parts = input_parts(later[3])
-    early_back = [early_parts[:first]] + [
-        swap(early_parts[k * first : (k + 1) * first], mask)
-        for k, mask in enumerate(direct_masks, 1)
-    ]
-    late_back = second_hop_back(late_parts)
-    early_sum = total(*early_back)
-    late_sum = after(first_hop_back(*late_back), early_sum)
-    returned = [early_sum, late_sum] + [shifted(late_sum, -s) for s in range(1, experts)]
-
-    def step(weights, left, right, scale):
-        theirs = sum(contract_rows(e[left][:, units:], e[right]) for e in (early, later)) * scale
-        theirs = swap(theirs.astype(jnp.bfloat16), core_bit)
-        mine = sum(contract_rows(e[left][:, :units], e[right]) for e in (early, later)) * scale
-        return stepped(weights, (mine + theirs.astype(jnp.float32)).T)
-
-    new_w_in = step(w_in, 3, 0, scale_in)
-    new_w_out = step(w_out, 2, 1, scale_out)
-    returned = after(returned, new_w_in, new_w_out)
-    picks = [*own_picks, *sent_picks]
+    parts = [
+        jnp.concatenate(pair, axis=0)
+        for pair in zip(split_rows(early_parts, first), split_rows(late_parts, rest))
+    ]
+    back_far = [swap(rows, mask) for rows, mask in zip(parts[4:], second_masks)]
+    back_near = [
+        swap(rows, mask)
+        for rows, mask in zip(near_sums(parts, back_far), (x_bit, y_bit, z_bit))
+    ]
+    sums = total(parts[0], *back_near)
+    early_sum, late_sum = sums[:first], sums[first:]
+    crossed = [shifted(late_sum, -s) for s in range(1, experts)]
+
+    def gradient(left, right, part, scale):
+        return sum(contract_rows(e[left][:, part], e[right]) for e in (early, later)) * scale
+
+    mine, theirs = slice(0, units), slice(units, 2 * units)
+    shared = jnp.concatenate(
+        [
+            gradient(3, 0, theirs, scale_in).astype(jnp.bfloat16),
+            gradient(2, 1, theirs, scale_out).astype(jnp.bfloat16),
+        ],
+        axis=0,
+    )
+    shared = swap(shared, core_bit).astype(jnp.float32)
+    new_w_in = stepped(w_in, (gradient(3, 0, mine, scale_in) + shared[mine]).T)
+    new_w_out = stepped(w_out, (gradient(2, 1, mine, scale_out) + shared[theirs]).T)
+    crossed = after(crossed, new_w_in, new_w_out)
+    returned = [early_sum, late_sum, *crossed]
     token_grad = sum(contract_rows(pick, rows) for pick, rows in zip(picks, returned))
     return (token_grad.astype(jnp.bfloat16), new_w_in, new_w_out)
 

time: 84.3 us -> 76.2 us (0.904)
  starting transfers between devices: 42.7 us -> 30.5 us
  waiting for transfers between devices: 17.4 us -> 20.2 us
  Pallas kernels: 4.31 us -> 2.33 us
  local copies, waits for them, and re-layouts: 0.96 us -> 2.64 us
  other arithmetic: 2.36 us -> 3.84 us
    ppermute x32 -> x20, starting transfers between devices: 38.1 us -> 24.3 us  [swap(): lax.ppermute(rows, 'expert', [(i, i ^ mask) for i in range(n_expert)])]
    ppermute x32 -> x20, waiting for transfers between devices: 12.4 us -> 17 us  [swap(): lax.ppermute(rows, 'expert', [(i, i ^ mask) for i in range(n_expert)])]
    pallas_call x2 -> x1, Pallas kernels: 4.31 us -> 2.33 us  [pack(): pl.pallas_call(lambda *refs: pack_kernel(blocks, experts, *refs), out_sha...]
    ppermute x2, waiting for transfers between devices: 5.01 us -> 3.24 us  [shifted(): return lax.ppermute(rows, 'expert', pairs)]
    ppermute x2, starting transfers between devices: 4.61 us -> 6.19 us  [shifted(): return lax.ppermute(rows, 'expert', pairs)]
    unnamed x29 -> x22, local copies, waits for them, and re-layouts: 0.88 us -> 2.09 us
  transfers between devices with their start and end apart: 34 -> 22, of which waited for: 12 -> 7; matrix products, arithmetic and copies ran while one was open for 20% -> 21% of each run, Pallas kernels for 0% -> 0%
where the time goes in v6:
time: 76.2 us; the launch traced here: 76 us
  starting transfers between devices  30.5 us (40%)
  waiting for transfers between devices  20.2 us (27%)
  matrix products  15.3 us (20%)
  other arithmetic  3.84 us (5%)
  local copies, waits for them, and re-layouts  2.64 us (3%)
  Pallas kernels  2.33 us (3%)
  between operations  1.08 us (1%)
    ppermute x20, starting transfers between devices, swap(): lax.ppermute(rows, 'expert', [(i, i ^ mask) for i in range(n_expert)])  24.3 us
    ppermute x20, waiting for transfers between devices, swap(): lax.ppermute(rows, 'expert', [(i, i ^ mask) for i in range(n_expert)])  17 us
    dot_general x11, matrix products, contract_rows(): lax.dot_general(left, right, (((0,), (0,)), ((), ())), preferred_element_...  9.6 us
    ppermute x2, starting transfers between devices, shifted(): return lax.ppermute(rows, 'expert', pairs)  6.19 us
    dot_general x4, matrix products, contract_cols(): lax.dot_general(left, right, (((1,), (1,)), ((), ())), preferred_element_...  4.34 us
    ppermute x2, waiting for transfers between devices, shifted(): return lax.ppermute(rows, 'expert', pairs)  3.24 us
    pallas_call x1, Pallas kernels, pack(): pl.pallas_call(lambda *refs: pack_kernel(blocks, experts, *refs), out_sha...  2.33 us
    unnamed x22, local copies, waits for them, and re-layouts  2.09 us
  transfers between devices with their start and end apart: 22, of which 7 were waited for; matrix products, arithmetic and copies ran while one was open for 21% of the time, Pallas kernels for 0%

profile of v6, /device:TPU:0, one launch (start us, length us, event | category | flops | bytes accessed | tf_op | source)
XLA Modules:
  0.0 76.0 jit_solution(11783301212820763516)
XLA Ops:
  0.6 2.3 %shard_map.85 = (bf16[16,4096]{1,0:T(8,128)(2,1)}, bf16[16,64]{1,0:T(8,128)(2,1)}, bf16[24,4096]{1,0:T(8,128)(2,1)}, bf16[24,64]{1,0:T(8,128)(2,1)}, bf16[24,4096]{1,0:T(8,128)(2,1)}, /*index=5*/bf16[24,64]{1,0:T(8,128)(2,1)}) custom-call(s32[1,64]{1,0:T(1,128)} %bitcast.22, f32[1,64]{1,0:T(1,128)} %bitcast.23, bf16[64,2048]{1,0:T(8,128)(2,1)} %refs_2_.1, ...), custom_call_target="tpu_custom_call" | custom-call | tf_op jit(solution)/shard_map/pallas_call | solution.py:84
  3.0 2.9 %collective-permute-start = (bf16[16,4096]{1,0:T(8,128)(2,1)}, bf16[16,4096]{1,0:T(8,128)(2,1)S(1)}, u32[]{:S(2)}, u32[]{:S(2)}) collective-permute-start(bf16[16,4096]{1,0:T(8,128)(2,1)} %get-tuple-element.20), channel_id=1, source_target_pairs={{0,2},{1,3},{2,0},{3,1},{4,6},{5,7},{6,4},{7,5},{8,10},{9,11},{10,... | collective-permute-start | bytes 393224 | tf_op jit(solution)/shard_map/ppermute | solution.py:109
  5.9 1.5 %collective-permute-start.1 = (bf16[16,4096]{1,0:T(8,128)(2,1)}, bf16[16,4096]{1,0:T(8,128)(2,1)S(1)}, u32[]{:S(2)}, u32[]{:S(2)}) collective-permute-start(bf16[16,4096]{1,0:T(8,128)(2,1)} %get-tuple-element.20), channel_id=1, source_target_pairs={{0,4},{1,5},{2,6},{3,7},{4,0},{5,1},{6,2},{7,3},{8,12},{9,13},{10,... | collective-permute-start | bytes 393224 | tf_op jit(solution)/shard_map/ppermute | solution.py:109
  7.4 1.6 %collective-permute-start.2 = (bf16[16,4096]{1,0:T(8,128)(2,1)}, bf16[16,4096]{1,0:T(8,128)(2,1)S(1)}, u32[]{:S(2)}, u32[]{:S(2)}) collective-permute-start(bf16[16,4096]{1,0:T(8,128)(2,1)} %get-tuple-element.20), channel_id=1, source_target_pairs={{0,8},{1,9},{2,10},{3,11},{4,12},{5,13},{6,14},{7,15},{8,0},{9,1},... | collective-permute-start | bytes 393224 | tf_op jit(solution)/shard_map/ppermute | solution.py:109
  9.0 3.0 %collective-permute-start.4 = (bf16[24,4096]{1,0:T(8,128)(2,1)}, bf16[24,4096]{1,0:T(8,128)(2,1)S(1)}, u32[]{:S(2)}, u32[]{:S(2)}) collective-permute-start(bf16[24,4096]{1,0:T(8,128)(2,1)} %get-tuple-element.22), channel_id=1, source_target_pairs={{0,16},{1,17},{2,18},{3,19},{4,20},{5,21},{6,22},{7,23},{8,24},{9,... | collective-permute-start | bytes 589832 | tf_op jit(solution)/shard_map/ppermute | solution.py:156
  12.9 1.9 %convert_bitcast_fusion = bf16[320,2048]{1,0:T(8,128)(2,1)S(1)} fusion(f32[2048,320]{0,1:T(8,128)} %param.10), kind=kLoop, calls=%fused_computation.31 | loop fusion | flops 655360 | bytes 3932160 | tf_op jit(solution)/shard_map/transpose | solution.py:199
  15.4 3.2 %collective-permute-done.4 = bf16[24,4096]{1,0:T(8,128)(2,1)S(1)} collective-permute-done((bf16[24,4096]{1,0:T(8,128)(2,1)}, bf16[24,4096]{1,0:T(8,128)(2,1)S(1)}, u32[]{:S(2)}, u32[]{:S(2)}) %collective-permute-start.4) | collective-permute-done | bytes 196640 | tf_op jit(solution)/shard_map/ppermute | solution.py:156
  18.9 3.4 %collective-permute-start.6 = (bf16[40,4096]{1,0:T(8,128)(2,1)S(1)}, bf16[40,4096]{1,0:T(8,128)(2,1)S(1)}, u32[]{:S(2)}, u32[]{:S(2)}) collective-permute-start(bf16[40,4096]{1,0:T(8,128)(2,1)S(1)} %get-tuple-element.61), channel_id=1, source_target_pairs={{0,8},{1,9},{2,10},{3,11},{4,12},{5,13},{6,14},{7,15},{8,0},{9,1},... | collective-permute-start | bytes 983048 | tf_op jit(solution)/shard_map/ppermute | solution.py:109
  23.1 1.4 %collective-permute-start.7 = (bf16[40,4096]{1,0:T(8,128)(2,1)S(1)}, bf16[40,4096]{1,0:T(8,128)(2,1)S(1)}, u32[]{:S(2)}, u32[]{:S(2)}) collective-permute-start(bf16[40,4096]{1,0:T(8,128)(2,1)S(1)} %get-tuple-element.62), channel_id=1, source_target_pairs={{0,2},{1,3},{2,0},{3,1},{4,6},{5,7},{6,4},{7,5},{8,10},{9,11},{10,... | collective-permute-start | bytes 983048 | tf_op jit(solution)/shard_map/ppermute | solution.py:109
  24.5 8.1 %collective-permute-done.7 = bf16[40,4096]{1,0:T(8,128)(2,1)S(1)} collective-permute-done((bf16[40,4096]{1,0:T(8,128)(2,1)S(1)}, bf16[40,4096]{1,0:T(8,128)(2,1)S(1)}, u32[]{:S(2)}, u32[]{:S(2)}) %collective-permute-start.7) | collective-permute-done | bytes 327712 | tf_op jit(solution)/shard_map/ppermute | solution.py:109
  32.7 1.5 %collective-permute-start.11 = (bf16[24,4096]{1,0:T(8,128)(2,1)S(1)}, bf16[24,4096]{1,0:T(8,128)(2,1)S(1)}, u32[]{:S(2)}, u32[]{:S(2)}) collective-permute-start(bf16[24,4096]{1,0:T(8,128)(2,1)S(1)} %get-tuple-element.55), channel_id=1, source_target_pairs={{0,2},{1,3},{2,0},{3,1},{4,6},{5,7},{6,4},{7,5},{8,10},{9,11},{10,... | collective-permute-start | bytes 589832 | tf_op jit(solution)/shard_map/ppermute | solution.py:109
  34.2 1.3 %collective-permute-start.12 = (bf16[24,4096]{1,0:T(8,128)(2,1)S(1)}, bf16[24,4096]{1,0:T(8,128)(2,1)S(1)}, u32[]{:S(2)}, u32[]{:S(2)}) collective-permute-start(bf16[24,4096]{1,0:T(8,128)(2,1)S(1)} %get-tuple-element.55), channel_id=1, source_target_pairs={{0,6},{1,7},{2,4},{3,5},{4,2},{5,3},{6,0},{7,1},{8,14},{9,15},{10,... | collective-permute-start | bytes 589832 | tf_op jit(solution)/shard_map/ppermute | solution.py:109
  40.4 4.6 %collective-permute-done.9 = bf16[24,4096]{1,0:T(8,128)(2,1)S(1)} collective-permute-done((bf16[24,4096]{1,0:T(8,128)(2,1)S(1)}, bf16[24,4096]{1,0:T(8,128)(2,1)S(1)}, u32[]{:S(2)}, u32[]{:S(2)}) %collective-permute-start.9) | collective-permute-done | bytes 196640 | tf_op jit(solution)/shard_map/ppermute | solution.py:109
  45.1 1.1 %multiply_convert_fusion = (bf16[192,640]{1,0:T(8,128)(2,1)S(1)}, f32[192,640]{1,0:T(8,128)S(1)}) fusion(bf16[320,2048]{1,0:T(8,128)(2,1)S(1)} %convert_bitcast_fusion, bf16[320,2048]{1,0:T(8,128)(2,1)S(1)} %get-tuple-element.37, bf16[192,4096]{1,0:T(8,128)(2,1)S(1)} %constant_dynamic-update-slice_fusion.5), kind=kOutput, calls=%fused_computation.53 | convolution fusion | flops 509788160 | bytes 4145152 | tf_op jit(solution)/shard_map/dot_general | solution.py:39
  46.2 1.2 %fusion.21 = bf16[192,640]{1,0:T(8,128)(2,1)S(1)} fusion(bf16[320,2048]{1,0:T(8,128)(2,1)S(1)} %get-tuple-element.38, bf16[320,2048]{1,0:T(8,128)(2,1)S(1)} %convert_bitcast_fusion.1, bf16[192,4096]{1,0:T(8,128)(2,1)S(1)} %constant_dynamic-update-slice_fusion.5, f32[192,640]{1,0:T(8,128)S(1)} %get-tuple-element.65), kind=kOutput, calls=%fused_computation.35 | convolution fusion | flops 511139840 | bytes 4145152 | tf_op jit(solution)/shard_map/dot_general | solution.py:39
  48.9 1.7 %collective-permute-start.18 = (bf16[40,2048]{1,0:T(8,128)(2,1)S(1)}, bf16[40,2048]{1,0:T(8,128)(2,1)S(1)}, u32[]{:S(2)}, u32[]{:S(2)}) collective-permute-start(bf16[40,2048]{1,0:T(8,128)(2,1)S(1)} %pad_maximum_fusion.24), channel_id=1, source_target_pairs={{0,6},{1,7},{2,4},{3,5},{4,2},{5,3},{6,0},{7,1},{8,14},{9,15},{10,... | collective-permute-start | bytes 491528 | tf_op jit(solution)/shard_map/ppermute | solution.py:109
  51.3 1.3 %collective-permute-start.15 = (bf16[40,2048]{1,0:T(8,128)(2,1)S(1)}, bf16[40,2048]{1,0:T(8,128)(2,1)S(1)}, u32[]{:S(2)}, u32[]{:S(2)}) collective-permute-start(bf16[40,2048]{1,0:T(8,128)(2,1)S(1)} %pad_maximum_fusion.22), channel_id=1, source_target_pairs={{0,8},{1,9},{2,10},{3,11},{4,12},{5,13},{6,14},{7,15},{8,0},{9,1},... | collective-permute-start | bytes 491528 | tf_op jit(solution)/shard_map/ppermute | solution.py:109
  56.4 1.3 %collective-permute-start.19 = (bf16[40,2048]{1,0:T(8,128)(2,1)S(1)}, bf16[40,2048]{1,0:T(8,128)(2,1)S(1)}, u32[]{:S(2)}, u32[]{:S(2)}) collective-permute-start(bf16[40,2048]{1,0:T(8,128)(2,1)S(1)} %add_convert_fusion.1), channel_id=1, source_target_pairs={{0,8},{1,9},{2,10},{3,11},{4,12},{5,13},{6,14},{7,15},{8,0},{9,1},... | collective-permute-start | bytes 491528 | tf_op jit(solution)/shard_map/ppermute | solution.py:109
  58.7 1.5 %collective-permute-start.14 = (bf16[40,2048]{1,0:T(8,128)(2,1)S(1)}, bf16[40,2048]{1,0:T(8,128)(2,1)S(1)}, u32[]{:S(2)}, u32[]{:S(2)}) collective-permute-start(bf16[40,2048]{1,0:T(8,128)(2,1)S(1)} %add_convert_fusion.3), channel_id=1, source_target_pairs={{0,2},{1,3},{2,0},{3,1},{4,6},{5,7},{6,4},{7,5},{8,10},{9,11},{10,... | collective-permute-start | bytes 491528 | tf_op jit(solution)/shard_map/ppermute | solution.py:109
  60.6 2.3 %collective-permute-done.19 = bf16[40,2048]{1,0:T(8,128)(2,1)S(1)} collective-permute-done((bf16[40,2048]{1,0:T(8,128)(2,1)S(1)}, bf16[40,2048]{1,0:T(8,128)(2,1)S(1)}, u32[]{:S(2)}, u32[]{:S(2)}) %collective-permute-start.19) | collective-permute-done | bytes 163872 | tf_op jit(solution)/shard_map/ppermute | solution.py:109
  63.0 1.2 %collective-permute-done.16 = bf16[40,2048]{1,0:T(8,128)(2,1)S(1)} collective-permute-done((bf16[40,2048]{1,0:T(8,128)(2,1)S(1)}, bf16[40,2048]{1,0:T(8,128)(2,1)S(1)}, u32[]{:S(2)}, u32[]{:S(2)}) %collective-permute-start.16) | collective-permute-done | bytes 163872 | tf_op jit(solution)/shard_map/ppermute | solution.py:109
  64.9 3.2 %collective-permute-start.20 = (bf16[24,2048]{1,0:T(8,128)(2,1)S(1)}, bf16[24,2048]{1,0:T(8,128)(2,1)S(1)}, u32[]{:S(2)}, u32[]{:S(2)}) collective-permute-start(bf16[24,2048]{1,0:T(8,128)(2,1)S(1)} %slice.189), channel_id=1, source_target_pairs={{0,16},{1,17},{2,18},{3,19},{4,20},{5,21},{6,22},{7,23},{8,24},{9,... | collective-permute-start | bytes 294920 | tf_op jit(solution)/shard_map/ppermute | solution.py:156
  70.4 2.3 %fusion.11 = f32[2048,320]{0,1:T(8,128)} fusion(f32[2048,320]{0,1:T(8,128)S(1)} %copy-done, f32[320,2048]{1,0:T(8,128)S(1)} %fusion.27, f32[640,2048]{1,0:T(8,128)S(1)} %convert_element_type.106, bf16[128,4096]{1,0:T(8,128)(2,1)S(1)} %constant_dynamic-update-slice_fusion, bf16[128,640]{1,0:T(8,128)(2,1)S(1)} %fusion.24), kind=kOutput, calls=%fused_computation.17 | convolution fusion | flops 171048960 | bytes 11108352 | tf_op jit(solution)/shard_map/dot_general | solution.py:33
  72.6 2.4 %fusion.4 = f32[2048,320]{0,1:T(8,128)} fusion(f32[2048,320]{0,1:T(8,128)S(1)} %copy-done.1, f32[320,2048]{1,0:T(8,128)S(1)} %fusion.31, f32[640,2048]{1,0:T(8,128)S(1)} %convert_element_type.106, bf16[128,4096]{1,0:T(8,128)(2,1)S(1)} %constant_dynamic-update-slice_fusion, bf16[128,640]{1,0:T(8,128)(2,1)S(1)} %get-tuple-element.66), kind=kOutput, calls=%fused_computation.7 | convolution fusion | flops 171048960 | bytes 11108352 | tf_op jit(solution)/shard_map/dot_general | solution.py:33
  (84 shorter events, 18.7 us)
Async XLA Ops:
  0.6 14.2 %copy-start.1 = (f32[2048,320]{0,1:T(8,128)S(1)}, f32[2048,320]{0,1:T(8,128)}, u32[]{:S(2)}) copy-start(f32[2048,320]{0,1:T(8,128)} %param.11) | copy-start | bytes 7864324
  3.0 15.8 %collective-permute-start = (bf16[16,4096]{1,0:T(8,128)(2,1)}, bf16[16,4096]{1,0:T(8,128)(2,1)S(1)}, u32[]{:S(2)}, u32[]{:S(2)}) collective-permute-start(bf16[16,4096]{1,0:T(8,128)(2,1)} %get-tuple-element.20), channel_id=1, source_target_pairs={{0,2},{1,3},{2,0},{3,1},{4,6},{5,7},{6,4},{7,5},{8,10},{9,11},{10,... | collective-permute-start | bytes 393224 | tf_op jit(solution)/shard_map/ppermute | solution.py:109
  5.9 12.8 %collective-permute-start.1 = (bf16[16,4096]{1,0:T(8,128)(2,1)}, bf16[16,4096]{1,0:T(8,128)(2,1)S(1)}, u32[]{:S(2)}, u32[]{:S(2)}) collective-permute-start(bf16[16,4096]{1,0:T(8,128)(2,1)} %get-tuple-element.20), channel_id=1, source_target_pairs={{0,4},{1,5},{2,6},{3,7},{4,0},{5,1},{6,2},{7,3},{8,12},{9,13},{10,... | collective-permute-start | bytes 393224 | tf_op jit(solution)/shard_map/ppermute | solution.py:109
  7.4 11.3 %collective-permute-start.2 = (bf16[16,4096]{1,0:T(8,128)(2,1)}, bf16[16,4096]{1,0:T(8,128)(2,1)S(1)}, u32[]{:S(2)}, u32[]{:S(2)}) collective-permute-start(bf16[16,4096]{1,0:T(8,128)(2,1)} %get-tuple-element.20), channel_id=1, source_target_pairs={{0,8},{1,9},{2,10},{3,11},{4,12},{5,13},{6,14},{7,15},{8,0},{9,1},... | collective-permute-start | bytes 393224 | tf_op jit(solution)/shard_map/ppermute | solution.py:109
  9.0 9.7 %collective-permute-start.3 = (bf16[16,4096]{1,0:T(8,128)(2,1)}, bf16[16,4096]{1,0:T(8,128)(2,1)S(1)}, u32[]{:S(2)}, u32[]{:S(2)}) collective-permute-start(bf16[16,4096]{1,0:T(8,128)(2,1)} %get-tuple-element.20), channel_id=1, source_target_pairs={{0,14},{1,15},{2,12},{3,13},{4,10},{5,11},{6,8},{7,9},{8,6},{9,7},... | collective-permute-start | bytes 393224 | tf_op jit(solution)/shard_map/ppermute | solution.py:109
  9.0 9.6 %collective-permute-start.4 = (bf16[24,4096]{1,0:T(8,128)(2,1)}, bf16[24,4096]{1,0:T(8,128)(2,1)S(1)}, u32[]{:S(2)}, u32[]{:S(2)}) collective-permute-start(bf16[24,4096]{1,0:T(8,128)(2,1)} %get-tuple-element.22), channel_id=1, source_target_pairs={{0,16},{1,17},{2,18},{3,19},{4,20},{5,21},{6,22},{7,23},{8,24},{9,... | collective-permute-start | bytes 589832 | tf_op jit(solution)/shard_map/ppermute | solution.py:156
  18.6 18.6 %collective-permute-start.8 = (bf16[640,2048]{1,0:T(8,128)(2,1)S(1)}, bf16[640,2048]{1,0:T(8,128)(2,1)S(1)}, u32[]{:S(2)}, u32[]{:S(2)}) collective-permute-start(bf16[640,2048]{1,0:T(8,128)(2,1)S(1)} %pad_maximum_fusion.1), channel_id=1, source_target_pairs={{0,1},{1,0},{2,3},{3,2},{4,5},{5,4},{6,7},{7,6},{8,9},{9,8},{10,11... | collective-permute-start | bytes 7864328 | tf_op jit(solution)/shard_map/ppermute | solution.py:109
  18.9 13.8 %collective-permute-start.6 = (bf16[40,4096]{1,0:T(8,128)(2,1)S(1)}, bf16[40,4096]{1,0:T(8,128)(2,1)S(1)}, u32[]{:S(2)}, u32[]{:S(2)}) collective-permute-start(bf16[40,4096]{1,0:T(8,128)(2,1)S(1)} %get-tuple-element.61), channel_id=1, source_target_pairs={{0,8},{1,9},{2,10},{3,11},{4,12},{5,13},{6,14},{7,15},{8,0},{9,1},... | collective-permute-start | bytes 983048 | tf_op jit(solution)/shard_map/ppermute | solution.py:109
  22.3 10.4 %collective-permute-start.5 = (bf16[40,4096]{1,0:T(8,128)(2,1)S(1)}, bf16[40,4096]{1,0:T(8,128)(2,1)S(1)}, u32[]{:S(2)}, u32[]{:S(2)}) collective-permute-start(bf16[40,4096]{1,0:T(8,128)(2,1)S(1)} %get-tuple-element.63), channel_id=1, source_target_pairs={{0,4},{1,5},{2,6},{3,7},{4,0},{5,1},{6,2},{7,3},{8,12},{9,13},{10,... | collective-permute-start | bytes 983048 | tf_op jit(solution)/shard_map/ppermute | solution.py:109
  23.1 9.5 %collective-permute-start.7 = (bf16[40,4096]{1,0:T(8,128)(2,1)S(1)}, bf16[40,4096]{1,0:T(8,128)(2,1)S(1)}, u32[]{:S(2)}, u32[]{:S(2)}) collective-permute-start(bf16[40,4096]{1,0:T(8,128)(2,1)S(1)} %get-tuple-element.62), channel_id=1, source_target_pairs={{0,2},{1,3},{2,0},{3,1},{4,6},{5,7},{6,4},{7,5},{8,10},{9,11},{10,... | collective-permute-start | bytes 983048 | tf_op jit(solution)/shard_map/ppermute | solution.py:109
  32.7 12.3 %collective-permute-start.11 = (bf16[24,4096]{1,0:T(8,128)(2,1)S(1)}, bf16[24,4096]{1,0:T(8,128)(2,1)S(1)}, u32[]{:S(2)}, u32[]{:S(2)}) collective-permute-start(bf16[24,4096]{1,0:T(8,128)(2,1)S(1)} %get-tuple-element.55), channel_id=1, source_target_pairs={{0,2},{1,3},{2,0},{3,1},{4,6},{5,7},{6,4},{7,5},{8,10},{9,11},{10,... | collective-permute-start | bytes 589832 | tf_op jit(solution)/shard_map/ppermute | solution.py:109
  34.2 10.8 %collective-permute-start.12 = (bf16[24,4096]{1,0:T(8,128)(2,1)S(1)}, bf16[24,4096]{1,0:T(8,128)(2,1)S(1)}, u32[]{:S(2)}, u32[]{:S(2)}) collective-permute-start(bf16[24,4096]{1,0:T(8,128)(2,1)S(1)} %get-tuple-element.55), channel_id=1, source_target_pairs={{0,6},{1,7},{2,4},{3,5},{4,2},{5,3},{6,0},{7,1},{8,14},{9,15},{10,... | collective-permute-start | bytes 589832 | tf_op jit(solution)/shard_map/ppermute | solution.py:109
  35.5 9.5 %collective-permute-start.9 = (bf16[24,4096]{1,0:T(8,128)(2,1)S(1)}, bf16[24,4096]{1,0:T(8,128)(2,1)S(1)}, u32[]{:S(2)}, u32[]{:S(2)}) collective-permute-start(bf16[24,4096]{1,0:T(8,128)(2,1)S(1)} %get-tuple-element.59), channel_id=1, source_target_pairs={{0,4},{1,5},{2,6},{3,7},{4,0},{5,1},{6,2},{7,3},{8,12},{9,13},{10,... | collective-permute-start | bytes 589832 | tf_op jit(solution)/shard_map/ppermute | solution.py:109
  36.3 8.7 %collective-permute-start.10 = (bf16[24,4096]{1,0:T(8,128)(2,1)S(1)}, bf16[24,4096]{1,0:T(8,128)(2,1)S(1)}, u32[]{:S(2)}, u32[]{:S(2)}) collective-permute-start(bf16[24,4096]{1,0:T(8,128)(2,1)S(1)} %get-tuple-element.57), channel_id=1, source_target_pairs={{0,8},{1,9},{2,10},{3,11},{4,12},{5,13},{6,14},{7,15},{8,0},{9,1},... | collective-permute-start | bytes 589832 | tf_op jit(solution)/shard_map/ppermute | solution.py:109
  48.9 7.3 %collective-permute-start.18 = (bf16[40,2048]{1,0:T(8,128)(2,1)S(1)}, bf16[40,2048]{1,0:T(8,128)(2,1)S(1)}, u32[]{:S(2)}, u32[]{:S(2)}) collective-permute-start(bf16[40,2048]{1,0:T(8,128)(2,1)S(1)} %pad_maximum_fusion.24), channel_id=1, source_target_pairs={{0,6},{1,7},{2,4},{3,5},{4,2},{5,3},{6,0},{7,1},{8,14},{9,15},{10,... | collective-permute-start | bytes 491528 | tf_op jit(solution)/shard_map/ppermute | solution.py:109
  50.6 5.7 %collective-permute-start.17 = (bf16[40,2048]{1,0:T(8,128)(2,1)S(1)}, bf16[40,2048]{1,0:T(8,128)(2,1)S(1)}, u32[]{:S(2)}, u32[]{:S(2)}) collective-permute-start(bf16[40,2048]{1,0:T(8,128)(2,1)S(1)} %pad_maximum_fusion.23), channel_id=1, source_target_pairs={{0,2},{1,3},{2,0},{3,1},{4,6},{5,7},{6,4},{7,5},{8,10},{9,11},{10,... | collective-permute-start | bytes 491528 | tf_op jit(solution)/shard_map/ppermute | solution.py:109
  51.3 6.3 %collective-permute-start.15 = (bf16[40,2048]{1,0:T(8,128)(2,1)S(1)}, bf16[40,2048]{1,0:T(8,128)(2,1)S(1)}, u32[]{:S(2)}, u32[]{:S(2)}) collective-permute-start(bf16[40,2048]{1,0:T(8,128)(2,1)S(1)} %pad_maximum_fusion.22), channel_id=1, source_target_pairs={{0,8},{1,9},{2,10},{3,11},{4,12},{5,13},{6,14},{7,15},{8,0},{9,1},... | collective-permute-start | bytes 491528 | tf_op jit(solution)/shard_map/ppermute | solution.py:109
  52.7 5.9 %collective-permute-start.13 = (bf16[40,2048]{1,0:T(8,128)(2,1)S(1)}, bf16[40,2048]{1,0:T(8,128)(2,1)S(1)}, u32[]{:S(2)}, u32[]{:S(2)}) collective-permute-start(bf16[40,2048]{1,0:T(8,128)(2,1)S(1)} %pad_maximum_fusion.21), channel_id=1, source_target_pairs={{0,4},{1,5},{2,6},{3,7},{4,0},{5,1},{6,2},{7,3},{8,12},{9,13},{10,... | collective-permute-start | bytes 491528 | tf_op jit(solution)/shard_map/ppermute | solution.py:109
  55.6 13.1 %collective-permute-start.21 = (bf16[640,2048]{1,0:T(8,128)(2,1)S(1)}, bf16[640,2048]{1,0:T(8,128)(2,1)S(1)}, u32[]{:S(2)}, u32[]{:S(2)}) collective-permute-start(bf16[640,2048]{1,0:T(8,128)(2,1)S(1)} %pad_maximum_fusion.3), channel_id=1, source_target_pairs={{0,1},{1,0},{2,3},{3,2},{4,5},{5,4},{6,7},{7,6},{8,9},{9,8},{10,11... | collective-permute-start | bytes 7864328 | tf_op jit(solution)/shard_map/ppermute | solution.py:109
  56.4 6.6 %collective-permute-start.19 = (bf16[40,2048]{1,0:T(8,128)(2,1)S(1)}, bf16[40,2048]{1,0:T(8,128)(2,1)S(1)}, u32[]{:S(2)}, u32[]{:S(2)}) collective-permute-start(bf16[40,2048]{1,0:T(8,128)(2,1)S(1)} %add_convert_fusion.1), channel_id=1, source_target_pairs={{0,8},{1,9},{2,10},{3,11},{4,12},{5,13},{6,14},{7,15},{8,0},{9,1},... | collective-permute-start | bytes 491528 | tf_op jit(solution)/shard_map/ppermute | solution.py:109
  57.7 10.4 %copy-start.4 = (bf16[24,64]{1,0:T(8,128)(2,1)S(1)}, bf16[24,64]{1,0:T(8,128)(2,1)}, u32[]{:S(2)}) copy-start(bf16[24,64]{1,0:T(8,128)(2,1)} %get-tuple-element.32) | copy-start | bytes 9220
  57.7 6.4 %collective-permute-start.16 = (bf16[40,2048]{1,0:T(8,128)(2,1)S(1)}, bf16[40,2048]{1,0:T(8,128)(2,1)S(1)}, u32[]{:S(2)}, u32[]{:S(2)}) collective-permute-start(bf16[40,2048]{1,0:T(8,128)(2,1)S(1)} %add_convert_fusion.2), channel_id=1, source_target_pairs={{0,4},{1,5},{2,6},{3,7},{4,0},{5,1},{6,2},{7,3},{8,12},{9,13},{10,... | collective-permute-start | bytes 491528 | tf_op jit(solution)/shard_map/ppermute | solution.py:109
  58.7 6.1 %collective-permute-start.14 = (bf16[40,2048]{1,0:T(8,128)(2,1)S(1)}, bf16[40,2048]{1,0:T(8,128)(2,1)S(1)}, u32[]{:S(2)}, u32[]{:S(2)}) collective-permute-start(bf16[40,2048]{1,0:T(8,128)(2,1)S(1)} %add_convert_fusion.3), channel_id=1, source_target_pairs={{0,2},{1,3},{2,0},{3,1},{4,6},{5,7},{6,4},{7,5},{8,10},{9,11},{10,... | collective-permute-start | bytes 491528 | tf_op jit(solution)/shard_map/ppermute | solution.py:109
  64.9 10.1 %collective-permute-start.20 = (bf16[24,2048]{1,0:T(8,128)(2,1)S(1)}, bf16[24,2048]{1,0:T(8,128)(2,1)S(1)}, u32[]{:S(2)}, u32[]{:S(2)}) collective-permute-start(bf16[24,2048]{1,0:T(8,128)(2,1)S(1)} %slice.189), channel_id=1, source_target_pairs={{0,16},{1,17},{2,18},{3,19},{4,20},{5,21},{6,22},{7,23},{8,24},{9,... | collective-permute-start | bytes 294920 | tf_op jit(solution)/shard_map/ppermute | solution.py:156
  (4 other events, 17.4 us)

commit v7 on v6

--- a/solution.py
+++ b/solution.py
@@ -47,7 +47,7 @@
     return lax.psum_scatter(attn_partials[0], "dp", scatter_dimension=0, tiled=True)
 
 
-def pack_kernel(blocks, experts, *refs):
+def pack_kernel(blocks, copies, experts, *refs):
     ids_ref, gate_ref, tokens_ref, grads_ref, *outs = refs
     n, width = tokens_ref.shape
     mine = (lax.axis_index("expert") // SHARDS).astype(jnp.float32)
@@ -62,7 +62,7 @@
     rank = jnp.sum(rivals, axis=0, keepdims=True)
     gated = (gate_down * grads_ref[...].astype(jnp.float32)).astype(jnp.bfloat16)
     for k, (expert, begin, end, row) in enumerate(blocks):
-        rows_ref, pick_ref = outs[2 * k], outs[2 * k + 1]
+        rows_ref, pick_ref = outs[copies + 2 * k], outs[copies + 2 * k + 1]
         chosen = (relative == expert) & (rank >= begin) & (rank < end)
         slot = jnp.where(chosen, rank - begin + row, -1.0).astype(jnp.int32)
         slots = lax.broadcasted_iota(jnp.int32, pick_ref.shape, 0)
@@ -72,22 +72,24 @@
             rows_ref[:, half * width : (half + 1) * width] = jnp.dot(
                 pick, source, preferred_element_type=jnp.float32
             ).astype(jnp.bfloat16)
-
-
-def pack(blocks, rows, experts, ids, gate, tokens, grads):
+    for copy_ref in outs[:copies]:
+        copy_ref[...] = outs[copies][...]
+
+
+def pack(blocks, rows, copies, experts, ids, gate, tokens, grads):
     n, width = tokens.shape
-    shapes = []
+    shapes = [jax.ShapeDtypeStruct((rows[0], 2 * width), jnp.bfloat16)] * copies
     for count in rows:
         shapes.append(jax.ShapeDtypeStruct((count, 2 * width), jnp.bfloat16))
         shapes.append(jax.ShapeDtypeStruct((count, n), jnp.bfloat16))
     whole = pl.BlockSpec(memory_space=pltpu.VMEM)
     outs = pl.pallas_call(
-        lambda *refs: pack_kernel(blocks, experts, *refs),
+        lambda *refs: pack_kernel(blocks, copies, experts, *refs),
         out_shape=shapes,
         in_specs=[whole] * 4,
         out_specs=[whole] * len(shapes),
     )(ids.reshape(1, n), gate.reshape(1, n), tokens, grads)
-    return outs[::2], outs[1::2]
+    return outs[:copies], outs[copies::2], outs[copies + 1 :: 2]
 
 
 def whole_weights(shard):
@@ -110,15 +112,18 @@
 
 
 core_bit, x_bit, y_bit, z_bit = 1, 2, 4, 8
-far_mask = x_bit | y_bit | z_bit
+early_masks = (x_bit, y_bit, z_bit, x_bit | y_bit | z_bit)
 
 
 def after(values, *others):
-    return lax.optimization_barrier((values, others))[0]
-
-
-def first_hop(own):
-    return swap(own, x_bit), swap(own, y_bit), swap(own, z_bit)
+    return lax.optimization_barrier((others, values))[1]
+
+
+def swaps(blocks, masks):
+    chained = []
+    for block in blocks:
+        chained.append(after(block, chained[-1]) if chained else block)
+    return [swap(block, mask) for block, mask in zip(chained, masks)]
 
 
 second_masks = (y_bit, z_bit, x_bit, x_bit | y_bit)
@@ -159,9 +164,10 @@
     own_blocks = [(0, 0, first, 0), (0, first, capacity, offset + first)]
     cross_blocks = [(s, 0, capacity, (s - 1) * capacity) for s in range(1, experts)]
     grads = summed_grads(attn_partials)
-    (early_own, late_own, *sent), picks = pack(
+    early_copies, (early_own, late_own, *sent), picks = pack(
         own_blocks + cross_blocks,
         [first] + [rest] * experts,
+        len(early_masks),
         experts,
         expert_ids,
         gate,
@@ -183,15 +189,16 @@
 
     for s in range(1, experts):
         late_own = late_own + shifted(sent[s - 1], s)
-    early_near = first_hop(early_own)
-    early_far = swap(early_own, far_mask)
-    early_near, early_far = after((early_near, early_far), late_own)
-    arrived = [
-        swap(jnp.concatenate([rows, late_own], axis=0), mask)
-        for rows, mask in zip(
-            (early_near[2], early_near[0], early_near[1]), (x_bit, y_bit, z_bit)
-        )
-    ]
+    *early_near, early_far = after(
+        [swap(rows, mask) for rows, mask in zip(early_copies, early_masks)], late_own
+    )
+    arrived = swaps(
+        [
+            jnp.concatenate([rows, late_own], axis=0)
+            for rows in (early_near[2], early_near[0], early_near[1])
+        ],
+        (x_bit, y_bit, z_bit),
+    )
     early_zx, early_xy, early_yz = [rows[:first] for rows in arrived]
     late_near = [rows[first:] for rows in arrived]
     early_rows = [early_own, *early_near, early_xy, early_yz, early_zx, early_far]
@@ -208,36 +215,41 @@
     ]
     early = activated(jnp.concatenate(early_rows, axis=0))
     early_parts = input_parts(early[3])
-    late_far = after(late_far, early_parts)
+    mine, theirs = slice(0, units), slice(units, 2 * units)
+
+    def gradients(chunk):
+        return [
+            contract_rows(chunk[left][:, part], chunk[right])
+            for left, right in ((3, 0), (2, 1))
+            for part in (mine, theirs)
+        ]
+
+    early_gradients = gradients(early)
+    late_far = after(late_far, early_parts, early_gradients)
     later = activated(jnp.concatenate([late_own, *late_near, *late_far], axis=0))
     late_parts = input_parts(later[3])
     parts = [
         jnp.concatenate(pair, axis=0)
         for pair in zip(split_rows(early_parts, first), split_rows(late_parts, rest))
     ]
-    back_far = [swap(rows, mask) for rows, mask in zip(parts[4:], second_masks)]
-    back_near = [
-        swap(rows, mask)
-        for rows, mask in zip(near_sums(parts, back_far), (x_bit, y_bit, z_bit))
-    ]
+    back_far = swaps(parts[4:], second_masks)
+    in_mine, in_theirs, out_mine, out_theirs = [
+        sum(pair) * scale
+        for pair, scale in zip(
+            zip(early_gradients, gradients(later)),
+            (scale_in, scale_in, scale_out, scale_out),
+        )
+    ]
+    in_shared = swap(in_theirs.astype(jnp.bfloat16), core_bit).astype(jnp.float32)
+    out_shared = swap(out_theirs.astype(jnp.bfloat16), core_bit).astype(jnp.float32)
+    new_w_in = stepped(w_in, (in_mine + in_shared).T)
+    new_w_out = stepped(w_out, (out_mine + out_shared).T)
+    back_near = swaps(near_sums(parts, back_far), (x_bit, y_bit, z_bit))
+    back_near = after(back_near, new_w_in)
     sums = total(parts[0], *back_near)
     early_sum, late_sum = sums[:first], sums[first:]
     crossed = [shifted(late_sum, -s) for s in range(1, experts)]
 
-    def gradient(left, right, part, scale):
-        return sum(contract_rows(e[left][:, part], e[right]) for e in (early, later)) * scale
-
-    mine, theirs = slice(0, units), slice(units, 2 * units)
-    shared = jnp.concatenate(
-        [
-            gradient(3, 0, theirs, scale_in).astype(jnp.bfloat16),
-            gradient(2, 1, theirs, scale_out).astype(jnp.bfloat16),
-        ],
-        axis=0,
-    )
-    shared = swap(shared, core_bit).astype(jnp.float32)
-    new_w_in = stepped(w_in, (gradient(3, 0, mine, scale_in) + shared[mine]).T)
-    new_w_out = stepped(w_out, (gradient(2, 1, mine, scale_out) + shared[theirs]).T)
     crossed = after(crossed, new_w_in, new_w_out)
     returned = [early_sum, late_sum, *crossed]
     token_grad = sum(contract_rows(pick, rows) for pick, rows in zip(picks, returned))

time: 76.2 us -> 73.5 us (0.965)
  starting transfers between devices: 30.5 us -> 24.5 us
  waiting for transfers between devices: 20.2 us -> 25.8 us
  local copies, waits for them, and re-layouts: 2.64 us -> 1.45 us
  other arithmetic: 3.84 us -> 2.7 us
    ppermute x20 -> x21, waiting for transfers between devices: 17 us -> 22.9 us  [swap(): lax.ppermute(rows, 'expert', [(i, i ^ mask) for i in range(n_expert)])]
    ppermute x20 -> x21, starting transfers between devices: 24.3 us -> 19.4 us  [swap(): lax.ppermute(rows, 'expert', [(i, i ^ mask) for i in range(n_expert)])]
    ppermute x2, starting transfers between devices: 6.19 us -> 5.07 us  [shifted(): return lax.ppermute(rows, 'expert', pairs)]
    unnamed x22, local copies, waits for them, and re-layouts: 2.09 us -> 1.05 us
  transfers between devices with their start and end apart: 22 -> 23, of which waited for: 7 -> 13; matrix products, arithmetic and copies ran while one was open for 21% -> 19% of each run, Pallas kernels for 0% -> 0%
where the time goes in v7:
time: 73.5 us; the launch traced here: 73.3 us
  waiting for transfers between devices  25.8 us (35%)
  starting transfers between devices  24.5 us (33%)
  matrix products  15.4 us (21%)
  other arithmetic  2.7 us (4%)
  Pallas kernels  2.49 us (3%)
  local copies, waits for them, and re-layouts  1.45 us (2%)
  between operations  1.02 us (1%)
    ppermute x21, waiting for transfers between devices, swap(): lax.ppermute(rows, 'expert', [(i, i ^ mask) for i in range(n_expert)])  22.9 us
    ppermute x21, starting transfers between devices, swap(): lax.ppermute(rows, 'expert', [(i, i ^ mask) for i in range(n_expert)])  19.4 us
    dot_general x11, matrix products, contract_rows(): lax.dot_general(left, right, (((0,), (0,)), ((), ())), preferred_element_...  9.68 us
    ppermute x2, starting transfers between devices, shifted(): return lax.ppermute(rows, 'expert', pairs)  5.07 us
    dot_general x4, matrix products, contract_cols(): lax.dot_general(left, right, (((1,), (1,)), ((), ())), preferred_element_...  4.32 us
    ppermute x2, waiting for transfers between devices, shifted(): return lax.ppermute(rows, 'expert', pairs)  2.88 us
    pallas_call x1, Pallas kernels, pack(): pl.pallas_call(lambda *refs: pack_kernel(blocks, copies, experts, *refs),...  2.49 us
    transpose x1, other arithmetic, shards(): whole_weights(w_in)  1.92 us
  transfers between devices with their start and end apart: 23, of which 13 were waited for; matrix products, arithmetic and copies ran while one was open for 19% of the time, Pallas kernels for 0%

profile of v7, /device:TPU:0, one launch (start us, length us, event | category | flops | bytes accessed | tf_op | source)
XLA Modules:
  0.0 73.3 jit_solution(14492514600550024067)
XLA Ops:
  0.6 2.5 %shard_map.85 = (bf16[16,4096]{1,0:T(8,128)(2,1)}, bf16[16,4096]{1,0:T(8,128)(2,1)}, bf16[16,4096]{1,0:T(8,128)(2,1)}, bf16[16,4096]{1,0:T(8,128)(2,1)}, bf16[16...) custom-call(s32[1,64]{1,0:T(1,128)} %bitcast.18, ...), custom_call_target="tpu_custom_call" | custom-call | tf_op jit(solution)/shard_map/pallas_call | solution.py:86
  3.1 4.0 %collective-permute-start = (bf16[24,4096]{1,0:T(8,128)(2,1)}, bf16[24,4096]{1,0:T(8,128)(2,1)S(1)}, u32[]{:S(2)}, u32[]{:S(2)}) collective-permute-start(bf16[24,4096]{1,0:T(8,128)(2,1)} %get-tuple-element.36), channel_id=1, source_target_pairs={{0,16},{1,17},{2,18},{3,19},{4,20},{5,21},{6,22},{7,23},{8,24},{9,... | collective-permute-start | bytes 589832 | tf_op jit(solution)/shard_map/ppermute | solution.py:161
  7.2 1.5 %collective-permute-start.1 = (bf16[16,4096]{1,0:T(8,128)(2,1)}, bf16[16,4096]{1,0:T(8,128)(2,1)S(1)}, u32[]{:S(2)}, u32[]{:S(2)}) collective-permute-start(bf16[16,4096]{1,0:T(8,128)(2,1)} %get-tuple-element.37), channel_id=1, source_target_pairs={{0,2},{1,3},{2,0},{3,1},{4,6},{5,7},{6,4},{7,5},{8,10},{9,11},{10,... | collective-permute-start | bytes 393224 | tf_op jit(solution)/shard_map/ppermute | solution.py:111
  8.7 1.5 %collective-permute-start.2 = (bf16[16,4096]{1,0:T(8,128)(2,1)}, bf16[16,4096]{1,0:T(8,128)(2,1)S(1)}, u32[]{:S(2)}, u32[]{:S(2)}) collective-permute-start(bf16[16,4096]{1,0:T(8,128)(2,1)} %get-tuple-element.38), channel_id=1, source_target_pairs={{0,4},{1,5},{2,6},{3,7},{4,0},{5,1},{6,2},{7,3},{8,12},{9,13},{10,... | collective-permute-start | bytes 393224 | tf_op jit(solution)/shard_map/ppermute | solution.py:111
  10.2 1.6 %collective-permute-start.3 = (bf16[16,4096]{1,0:T(8,128)(2,1)}, bf16[16,4096]{1,0:T(8,128)(2,1)S(1)}, u32[]{:S(2)}, u32[]{:S(2)}) collective-permute-start(bf16[16,4096]{1,0:T(8,128)(2,1)} %get-tuple-element.39), channel_id=1, source_target_pairs={{0,8},{1,9},{2,10},{3,11},{4,12},{5,13},{6,14},{7,15},{8,0},{9,1},... | collective-permute-start | bytes 393224 | tf_op jit(solution)/shard_map/ppermute | solution.py:111
  13.0 1.9 %convert_bitcast_fusion = bf16[320,2048]{1,0:T(8,128)(2,1)S(1)} fusion(f32[2048,320]{0,1:T(8,128)} %param.10), kind=kLoop, calls=%fused_computation.24 | loop fusion | flops 655360 | bytes 3932160 | tf_op jit(solution)/shard_map/transpose | solution.py:206
  15.4 1.2 %collective-permute-done = bf16[24,4096]{1,0:T(8,128)(2,1)S(1)} collective-permute-done((bf16[24,4096]{1,0:T(8,128)(2,1)}, bf16[24,4096]{1,0:T(8,128)(2,1)S(1)}, u32[]{:S(2)}, u32[]{:S(2)}) %collective-permute-start) | collective-permute-done | bytes 196640 | tf_op jit(solution)/shard_map/ppermute | solution.py:161
  16.7 2.4 %collective-permute-done.3 = bf16[16,4096]{1,0:T(8,128)(2,1)S(1)} collective-permute-done((bf16[16,4096]{1,0:T(8,128)(2,1)}, bf16[16,4096]{1,0:T(8,128)(2,1)S(1)}, u32[]{:S(2)}, u32[]{:S(2)}) %collective-permute-start.3) | collective-permute-done | bytes 131104 | tf_op jit(solution)/shard_map/ppermute | solution.py:111
  19.1 2.1 %collective-permute-done.4 = bf16[16,4096]{1,0:T(8,128)(2,1)S(1)} collective-permute-done((bf16[16,4096]{1,0:T(8,128)(2,1)}, bf16[16,4096]{1,0:T(8,128)(2,1)S(1)}, u32[]{:S(2)}, u32[]{:S(2)}) %collective-permute-start.4) | collective-permute-done | bytes 131104 | tf_op jit(solution)/shard_map/ppermute | solution.py:111
  21.3 1.3 %collective-permute-start.7 = (bf16[40,4096]{1,0:T(8,128)(2,1)S(1)}, bf16[40,4096]{1,0:T(8,128)(2,1)S(1)}, u32[]{:S(2)}, u32[]{:S(2)}) collective-permute-start(bf16[40,4096]{1,0:T(8,128)(2,1)S(1)} %get-tuple-element.91), channel_id=1, source_target_pairs={{0,2},{1,3},{2,0},{3,1},{4,6},{5,7},{6,4},{7,5},{8,10},{9,11},{10,... | collective-permute-start | bytes 983048 | tf_op jit(solution)/shard_map/ppermute | solution.py:111
  23.9 6.6 %collective-permute-done.7 = bf16[40,4096]{1,0:T(8,128)(2,1)S(1)} collective-permute-done((bf16[40,4096]{1,0:T(8,128)(2,1)S(1)}, bf16[40,4096]{1,0:T(8,128)(2,1)S(1)}, u32[]{:S(2)}, u32[]{:S(2)}) %collective-permute-start.7) | collective-permute-done | bytes 327712 | tf_op jit(solution)/shard_map/ppermute | solution.py:111
  32.6 1.5 %collective-permute-start.12 = (bf16[24,4096]{1,0:T(8,128)(2,1)S(1)}, bf16[24,4096]{1,0:T(8,128)(2,1)S(1)}, u32[]{:S(2)}, u32[]{:S(2)}) collective-permute-start(bf16[24,4096]{1,0:T(8,128)(2,1)S(1)} %get-tuple-element.83), channel_id=1, source_target_pairs={{0,6},{1,7},{2,4},{3,5},{4,2},{5,3},{6,0},{7,1},{8,14},{9,15},{10,... | collective-permute-start | bytes 589832 | tf_op jit(solution)/shard_map/ppermute | solution.py:111
  34.3 1.2 %collective-permute-start.9 = (bf16[24,4096]{1,0:T(8,128)(2,1)S(1)}, bf16[24,4096]{1,0:T(8,128)(2,1)S(1)}, u32[]{:S(2)}, u32[]{:S(2)}) collective-permute-start(bf16[24,4096]{1,0:T(8,128)(2,1)S(1)} %get-tuple-element.87), channel_id=1, source_target_pairs={{0,4},{1,5},{2,6},{3,7},{4,0},{5,1},{6,2},{7,3},{8,12},{9,13},{10,... | collective-permute-start | bytes 589832 | tf_op jit(solution)/shard_map/ppermute | solution.py:111
  41.0 1.4 %collective-permute-done.9 = bf16[24,4096]{1,0:T(8,128)(2,1)S(1)} collective-permute-done((bf16[24,4096]{1,0:T(8,128)(2,1)S(1)}, bf16[24,4096]{1,0:T(8,128)(2,1)S(1)}, u32[]{:S(2)}, u32[]{:S(2)}) %collective-permute-start.9) | collective-permute-done | bytes 196640 | tf_op jit(solution)/shard_map/ppermute | solution.py:111
  43.6 1.2 %fusion.13 = bf16[192,640]{1,0:T(8,128)(2,1)S(1)} fusion(bf16[320,2048]{1,0:T(8,128)(2,1)S(1)} %get-tuple-element.66, bf16[320,2048]{1,0:T(8,128)(2,1)S(1)} %convert_bitcast_fusion.1, bf16[192,4096]{1,0:T(8,128)(2,1)S(1)} %constant_dynamic-update-slice_fusion.5, f32[192,640]{1,0:T(8,128)S(1)} %get-tuple-element.95), kind=kOutput, calls=%fused_computation.28 | convolution fusion | flops 511139840 | bytes 4145152 | tf_op jit(solution)/shard_map/dot_general | solution.py:39
  49.9 1.6 %collective-permute-start.19 = (bf16[40,2048]{1,0:T(8,128)(2,1)S(1)}, bf16[40,2048]{1,0:T(8,128)(2,1)S(1)}, u32[]{:S(2)}, u32[]{:S(2)}) collective-permute-start(bf16[40,2048]{1,0:T(8,128)(2,1)S(1)} %pad_maximum_fusion.23), channel_id=1, source_target_pairs={{0,6},{1,7},{2,4},{3,5},{4,2},{5,3},{6,0},{7,1},{8,14},{9,15},{10,... | collective-permute-start | bytes 491528 | tf_op jit(solution)/shard_map/ppermute | solution.py:111
  51.6 2.2 %collective-permute-done.14 = bf16[40,2048]{1,0:T(8,128)(2,1)S(1)} collective-permute-done((bf16[40,2048]{1,0:T(8,128)(2,1)S(1)}, bf16[40,2048]{1,0:T(8,128)(2,1)S(1)}, u32[]{:S(2)}, u32[]{:S(2)}) %collective-permute-start.14) | collective-permute-done | bytes 163872 | tf_op jit(solution)/shard_map/ppermute | solution.py:111
  54.5 1.3 %collective-permute-start.15 = (bf16[40,2048]{1,0:T(8,128)(2,1)S(1)}, bf16[40,2048]{1,0:T(8,128)(2,1)S(1)}, u32[]{:S(2)}, u32[]{:S(2)}) collective-permute-start(bf16[40,2048]{1,0:T(8,128)(2,1)S(1)} %add_convert_fusion.3), channel_id=1, source_target_pairs={{0,2},{1,3},{2,0},{3,1},{4,6},{5,7},{6,4},{7,5},{8,10},{9,11},{10,... | collective-permute-start | bytes 491528 | tf_op jit(solution)/shard_map/ppermute | solution.py:111
  55.9 4.2 %collective-permute-done.19 = bf16[40,2048]{1,0:T(8,128)(2,1)S(1)} collective-permute-done((bf16[40,2048]{1,0:T(8,128)(2,1)S(1)}, bf16[40,2048]{1,0:T(8,128)(2,1)S(1)}, u32[]{:S(2)}, u32[]{:S(2)}) %collective-permute-start.19) | collective-permute-done | bytes 163872 | tf_op jit(solution)/shard_map/ppermute | solution.py:111
  61.3 1.2 %collective-permute-start.20 = (bf16[40,2048]{1,0:T(8,128)(2,1)S(1)}, bf16[40,2048]{1,0:T(8,128)(2,1)S(1)}, u32[]{:S(2)}, u32[]{:S(2)}) collective-permute-start(bf16[40,2048]{1,0:T(8,128)(2,1)S(1)} %add_convert_fusion.1), channel_id=1, source_target_pairs={{0,8},{1,9},{2,10},{3,11},{4,12},{5,13},{6,14},{7,15},{8,0},{9,1},... | collective-permute-start | bytes 491528 | tf_op jit(solution)/shard_map/ppermute | solution.py:111
  62.4 2.3 %bitcast_subtract_fusion.1 = f32[2048,320]{0,1:T(8,128)} fusion(f32[2048,320]{0,1:T(8,128)S(1)} %copy-done, bf16[320,2048]{1,0:T(8,128)(2,1)S(1)} %collective-permute-done.13, f32[320,2048]{1,0:T(8,128)S(1)} %fusion.29, bf16[192,4096]{1,0:T(8,128)(2,1)S(1)} %constant_dynamic-update-slice_fusion.5, bf16[192,640]{1,0:T(8,128)(2,1)S(1)} %fusion.13), kind=kOutput, calls=%fused_computation.14 | convolution fusion | flops 255590400 | bytes 10108928 | tf_op jit(solution)/shard_map/dot_general | solution.py:33
  64.8 1.9 %collective-permute-done.20 = bf16[40,2048]{1,0:T(8,128)(2,1)S(1)} collective-permute-done((bf16[40,2048]{1,0:T(8,128)(2,1)S(1)}, bf16[40,2048]{1,0:T(8,128)(2,1)S(1)}, u32[]{:S(2)}, u32[]{:S(2)}) %collective-permute-start.20) | collective-permute-done | bytes 163872 | tf_op jit(solution)/shard_map/ppermute | solution.py:111
  68.1 2.4 %bitcast_subtract_fusion = f32[2048,320]{0,1:T(8,128)} fusion(f32[2048,320]{0,1:T(8,128)S(1)} %copy-done.1, bf16[320,2048]{1,0:T(8,128)(2,1)S(1)} %collective-permute-done.21, f32[320,2048]{1,0:T(8,128)S(1)} %fusion.35, bf16[192,4096]{1,0:T(8,128)(2,1)S(1)} %constant_dynamic-update-slice_fusion.5, bf16[192,640]{1,0:T(8,128)(2,1)S(1)} %get-tuple-element.94), kind=kOutput, calls=%fused_computation.13 | convolution fusion | flops 255590400 | bytes 10108928 | tf_op jit(solution)/shard_map/dot_general | solution.py:33
  70.7 1.7 %collective-permute-done.22 = bf16[24,2048]{1,0:T(8,128)(2,1)S(1)} collective-permute-done((bf16[24,2048]{1,0:T(8,128)(2,1)S(1)}, bf16[24,2048]{1,0:T(8,128)(2,1)S(1)}, u32[]{:S(2)}, u32[]{:S(2)}) %collective-permute-start.22) | collective-permute-done | bytes 98336 | tf_op jit(solution)/shard_map/ppermute | solution.py:161
  (83 shorter events, 21.6 us)
Async XLA Ops:
  3.1 13.5 %collective-permute-start = (bf16[24,4096]{1,0:T(8,128)(2,1)}, bf16[24,4096]{1,0:T(8,128)(2,1)S(1)}, u32[]{:S(2)}, u32[]{:S(2)}) collective-permute-start(bf16[24,4096]{1,0:T(8,128)(2,1)} %get-tuple-element.36), channel_id=1, source_target_pairs={{0,16},{1,17},{2,18},{3,19},{4,20},{5,21},{6,22},{7,23},{8,24},{9,... | collective-permute-start | bytes 589832 | tf_op jit(solution)/shard_map/ppermute | solution.py:161
  7.2 9.5 %collective-permute-start.1 = (bf16[16,4096]{1,0:T(8,128)(2,1)}, bf16[16,4096]{1,0:T(8,128)(2,1)S(1)}, u32[]{:S(2)}, u32[]{:S(2)}) collective-permute-start(bf16[16,4096]{1,0:T(8,128)(2,1)} %get-tuple-element.37), channel_id=1, source_target_pairs={{0,2},{1,3},{2,0},{3,1},{4,6},{5,7},{6,4},{7,5},{8,10},{9,11},{10,... | collective-permute-start | bytes 393224 | tf_op jit(solution)/shard_map/ppermute | solution.py:111
  8.7 8.0 %collective-permute-start.2 = (bf16[16,4096]{1,0:T(8,128)(2,1)}, bf16[16,4096]{1,0:T(8,128)(2,1)S(1)}, u32[]{:S(2)}, u32[]{:S(2)}) collective-permute-start(bf16[16,4096]{1,0:T(8,128)(2,1)} %get-tuple-element.38), channel_id=1, source_target_pairs={{0,4},{1,5},{2,6},{3,7},{4,0},{5,1},{6,2},{7,3},{8,12},{9,13},{10,... | collective-permute-start | bytes 393224 | tf_op jit(solution)/shard_map/ppermute | solution.py:111
  10.2 8.9 %collective-permute-start.3 = (bf16[16,4096]{1,0:T(8,128)(2,1)}, bf16[16,4096]{1,0:T(8,128)(2,1)S(1)}, u32[]{:S(2)}, u32[]{:S(2)}) collective-permute-start(bf16[16,4096]{1,0:T(8,128)(2,1)} %get-tuple-element.39), channel_id=1, source_target_pairs={{0,8},{1,9},{2,10},{3,11},{4,12},{5,13},{6,14},{7,15},{8,0},{9,1},... | collective-permute-start | bytes 393224 | tf_op jit(solution)/shard_map/ppermute | solution.py:111
  11.8 9.4 %collective-permute-start.4 = (bf16[16,4096]{1,0:T(8,128)(2,1)}, bf16[16,4096]{1,0:T(8,128)(2,1)S(1)}, u32[]{:S(2)}, u32[]{:S(2)}) collective-permute-start(bf16[16,4096]{1,0:T(8,128)(2,1)} %get-tuple-element.40), channel_id=1, source_target_pairs={{0,14},{1,15},{2,12},{3,13},{4,10},{5,11},{6,8},{7,9},{8,6},{9,7},... | collective-permute-start | bytes 393224 | tf_op jit(solution)/shard_map/ppermute | solution.py:111
  21.3 9.2 %collective-permute-start.7 = (bf16[40,4096]{1,0:T(8,128)(2,1)S(1)}, bf16[40,4096]{1,0:T(8,128)(2,1)S(1)}, u32[]{:S(2)}, u32[]{:S(2)}) collective-permute-start(bf16[40,4096]{1,0:T(8,128)(2,1)S(1)} %get-tuple-element.91), channel_id=1, source_target_pairs={{0,2},{1,3},{2,0},{3,1},{4,6},{5,7},{6,4},{7,5},{8,10},{9,11},{10,... | collective-permute-start | bytes 983048 | tf_op jit(solution)/shard_map/ppermute | solution.py:111
  22.6 8.2 %collective-permute-start.5 = (bf16[40,4096]{1,0:T(8,128)(2,1)S(1)}, bf16[40,4096]{1,0:T(8,128)(2,1)S(1)}, u32[]{:S(2)}, u32[]{:S(2)}) collective-permute-start(bf16[40,4096]{1,0:T(8,128)(2,1)S(1)} %get-tuple-element.44), channel_id=1, source_target_pairs={{0,4},{1,5},{2,6},{3,7},{4,0},{5,1},{6,2},{7,3},{8,12},{9,13},{10,... | collective-permute-start | bytes 983048 | tf_op jit(solution)/shard_map/ppermute | solution.py:111
  23.7 7.9 %collective-permute-start.6 = (bf16[40,4096]{1,0:T(8,128)(2,1)S(1)}, bf16[40,4096]{1,0:T(8,128)(2,1)S(1)}, u32[]{:S(2)}, u32[]{:S(2)}) collective-permute-start(bf16[40,4096]{1,0:T(8,128)(2,1)S(1)} %get-tuple-element.45), channel_id=1, source_target_pairs={{0,8},{1,9},{2,10},{3,11},{4,12},{5,13},{6,14},{7,15},{8,0},{9,1},... | collective-permute-start | bytes 983048 | tf_op jit(solution)/shard_map/ppermute | solution.py:111
  23.8 11.8 %collective-permute-start.8 = (bf16[640,2048]{1,0:T(8,128)(2,1)S(1)}, bf16[640,2048]{1,0:T(8,128)(2,1)S(1)}, u32[]{:S(2)}, u32[]{:S(2)}) collective-permute-start(bf16[640,2048]{1,0:T(8,128)(2,1)S(1)} %pad_maximum_fusion.1), channel_id=1, source_target_pairs={{0,1},{1,0},{2,3},{3,2},{4,5},{5,4},{6,7},{7,6},{8,9},{9,8},{10,11... | collective-permute-start | bytes 7864328 | tf_op jit(solution)/shard_map/ppermute | solution.py:111
  31.7 9.0 %collective-permute-start.11 = (bf16[24,4096]{1,0:T(8,128)(2,1)S(1)}, bf16[24,4096]{1,0:T(8,128)(2,1)S(1)}, u32[]{:S(2)}, u32[]{:S(2)}) collective-permute-start(bf16[24,4096]{1,0:T(8,128)(2,1)S(1)} %get-tuple-element.83), channel_id=1, source_target_pairs={{0,2},{1,3},{2,0},{3,1},{4,6},{5,7},{6,4},{7,5},{8,10},{9,11},{10,... | collective-permute-start | bytes 589832 | tf_op jit(solution)/shard_map/ppermute | solution.py:111
  32.6 8.5 %collective-permute-start.12 = (bf16[24,4096]{1,0:T(8,128)(2,1)S(1)}, bf16[24,4096]{1,0:T(8,128)(2,1)S(1)}, u32[]{:S(2)}, u32[]{:S(2)}) collective-permute-start(bf16[24,4096]{1,0:T(8,128)(2,1)S(1)} %get-tuple-element.83), channel_id=1, source_target_pairs={{0,6},{1,7},{2,4},{3,5},{4,2},{5,3},{6,0},{7,1},{8,14},{9,15},{10,... | collective-permute-start | bytes 589832 | tf_op jit(solution)/shard_map/ppermute | solution.py:111
  34.0 7.0 %collective-permute-start.10 = (bf16[24,4096]{1,0:T(8,128)(2,1)S(1)}, bf16[24,4096]{1,0:T(8,128)(2,1)S(1)}, u32[]{:S(2)}, u32[]{:S(2)}) collective-permute-start(bf16[24,4096]{1,0:T(8,128)(2,1)S(1)} %get-tuple-element.85), channel_id=1, source_target_pairs={{0,8},{1,9},{2,10},{3,11},{4,12},{5,13},{6,14},{7,15},{8,0},{9,1},... | collective-permute-start | bytes 589832 | tf_op jit(solution)/shard_map/ppermute | solution.py:111
  34.3 8.1 %collective-permute-start.9 = (bf16[24,4096]{1,0:T(8,128)(2,1)S(1)}, bf16[24,4096]{1,0:T(8,128)(2,1)S(1)}, u32[]{:S(2)}, u32[]{:S(2)}) collective-permute-start(bf16[24,4096]{1,0:T(8,128)(2,1)S(1)} %get-tuple-element.87), channel_id=1, source_target_pairs={{0,4},{1,5},{2,6},{3,7},{4,0},{5,1},{6,2},{7,3},{8,12},{9,13},{10,... | collective-permute-start | bytes 589832 | tf_op jit(solution)/shard_map/ppermute | solution.py:111
  46.9 15.5 %copy-start = (f32[2048,320]{0,1:T(8,128)S(1)}, f32[2048,320]{0,1:T(8,128)}, u32[]{:S(2)}) copy-start(f32[2048,320]{0,1:T(8,128)} %param.10) | copy-start | bytes 7864324
  47.0 21.1 %collective-permute-start.21 = (bf16[320,2048]{1,0:T(8,128)(2,1)S(1)}, bf16[320,2048]{1,0:T(8,128)(2,1)S(1)}, u32[]{:S(2)}, u32[]{:S(2)}) collective-permute-start(bf16[320,2048]{1,0:T(8,128)(2,1)S(1)} %fusion.5), channel_id=1, source_target_pairs={{0,1},{1,0},{2,3},{3,2},{4,5},{5,4},{6,7},{7,6},{8,9},{9,8},{10,11... | collective-permute-start | bytes 3932168 | tf_op jit(solution)/shard_map/ppermute | solution.py:111
  47.1 6.7 %collective-permute-start.14 = (bf16[40,2048]{1,0:T(8,128)(2,1)S(1)}, bf16[40,2048]{1,0:T(8,128)(2,1)S(1)}, u32[]{:S(2)}, u32[]{:S(2)}) collective-permute-start(bf16[40,2048]{1,0:T(8,128)(2,1)S(1)} %pad_maximum_fusion.20), channel_id=1, source_target_pairs={{0,4},{1,5},{2,6},{3,7},{4,0},{5,1},{6,2},{7,3},{8,12},{9,13},{10,... | collective-permute-start | bytes 491528 | tf_op jit(solution)/shard_map/ppermute | solution.py:111
  48.1 6.4 %collective-permute-start.16 = (bf16[40,2048]{1,0:T(8,128)(2,1)S(1)}, bf16[40,2048]{1,0:T(8,128)(2,1)S(1)}, u32[]{:S(2)}, u32[]{:S(2)}) collective-permute-start(bf16[40,2048]{1,0:T(8,128)(2,1)S(1)} %get-tuple-element.52), channel_id=1, source_target_pairs={{0,8},{1,9},{2,10},{3,11},{4,12},{5,13},{6,14},{7,15},{8,0},{9,1},... | collective-permute-start | bytes 491528 | tf_op jit(solution)/shard_map/ppermute | solution.py:111
  49.1 12.1 %collective-permute-start.18 = (bf16[40,2048]{1,0:T(8,128)(2,1)S(1)}, bf16[40,2048]{1,0:T(8,128)(2,1)S(1)}, u32[]{:S(2)}, u32[]{:S(2)}) collective-permute-start(bf16[40,2048]{1,0:T(8,128)(2,1)S(1)} %get-tuple-element.54), channel_id=1, source_target_pairs={{0,2},{1,3},{2,0},{3,1},{4,6},{5,7},{6,4},{7,5},{8,10},{9,11},{10,... | collective-permute-start | bytes 491528 | tf_op jit(solution)/shard_map/ppermute | solution.py:111
  49.9 10.1 %collective-permute-start.19 = (bf16[40,2048]{1,0:T(8,128)(2,1)S(1)}, bf16[40,2048]{1,0:T(8,128)(2,1)S(1)}, u32[]{:S(2)}, u32[]{:S(2)}) collective-permute-start(bf16[40,2048]{1,0:T(8,128)(2,1)S(1)} %pad_maximum_fusion.23), channel_id=1, source_target_pairs={{0,6},{1,7},{2,4},{3,5},{4,2},{5,3},{6,0},{7,1},{8,14},{9,15},{10,... | collective-permute-start | bytes 491528 | tf_op jit(solution)/shard_map/ppermute | solution.py:111
  53.8 8.6 %collective-permute-start.13 = (bf16[320,2048]{1,0:T(8,128)(2,1)S(1)}, bf16[320,2048]{1,0:T(8,128)(2,1)S(1)}, u32[]{:S(2)}, u32[]{:S(2)}) collective-permute-start(bf16[320,2048]{1,0:T(8,128)(2,1)S(1)} %fusion.4), channel_id=1, source_target_pairs={{0,1},{1,0},{2,3},{3,2},{4,5},{5,4},{6,7},{7,6},{8,9},{9,8},{10,11... | collective-permute-start | bytes 3932168 | tf_op jit(solution)/shard_map/ppermute | solution.py:111
  54.5 12.1 %collective-permute-start.15 = (bf16[40,2048]{1,0:T(8,128)(2,1)S(1)}, bf16[40,2048]{1,0:T(8,128)(2,1)S(1)}, u32[]{:S(2)}, u32[]{:S(2)}) collective-permute-start(bf16[40,2048]{1,0:T(8,128)(2,1)S(1)} %add_convert_fusion.3), channel_id=1, source_target_pairs={{0,2},{1,3},{2,0},{3,1},{4,6},{5,7},{6,4},{7,5},{8,10},{9,11},{10,... | collective-permute-start | bytes 491528 | tf_op jit(solution)/shard_map/ppermute | solution.py:111
  60.1 6.6 %collective-permute-start.17 = (bf16[40,2048]{1,0:T(8,128)(2,1)S(1)}, bf16[40,2048]{1,0:T(8,128)(2,1)S(1)}, u32[]{:S(2)}, u32[]{:S(2)}) collective-permute-start(bf16[40,2048]{1,0:T(8,128)(2,1)S(1)} %add_convert_fusion.2), channel_id=1, source_target_pairs={{0,4},{1,5},{2,6},{3,7},{4,0},{5,1},{6,2},{7,3},{8,12},{9,13},{10,... | collective-permute-start | bytes 491528 | tf_op jit(solution)/shard_map/ppermute | solution.py:111
  61.3 5.4 %collective-permute-start.20 = (bf16[40,2048]{1,0:T(8,128)(2,1)S(1)}, bf16[40,2048]{1,0:T(8,128)(2,1)S(1)}, u32[]{:S(2)}, u32[]{:S(2)}) collective-permute-start(bf16[40,2048]{1,0:T(8,128)(2,1)S(1)} %add_convert_fusion.1), channel_id=1, source_target_pairs={{0,8},{1,9},{2,10},{3,11},{4,12},{5,13},{6,14},{7,15},{8,0},{9,1},... | collective-permute-start | bytes 491528 | tf_op jit(solution)/shard_map/ppermute | solution.py:111
  66.8 5.6 %collective-permute-start.22 = (bf16[24,2048]{1,0:T(8,128)(2,1)S(1)}, bf16[24,2048]{1,0:T(8,128)(2,1)S(1)}, u32[]{:S(2)}, u32[]{:S(2)}) collective-permute-start(bf16[24,2048]{1,0:T(8,128)(2,1)S(1)} %slice.187), channel_id=1, source_target_pairs={{0,16},{1,17},{2,18},{3,19},{4,20},{5,21},{6,22},{7,23},{8,24},{9,... | collective-permute-start | bytes 294920 | tf_op jit(solution)/shard_map/ppermute | solution.py:161
  (5 other events, 29.0 us)

commit v8 on v7

--- a/solution.py
+++ b/solution.py
@@ -47,7 +47,7 @@
     return lax.psum_scatter(attn_partials[0], "dp", scatter_dimension=0, tiled=True)
 
 
-def pack_kernel(blocks, copies, experts, *refs):
+def pack_kernel(blocks, experts, *refs):
     ids_ref, gate_ref, tokens_ref, grads_ref, *outs = refs
     n, width = tokens_ref.shape
     mine = (lax.axis_index("expert") // SHARDS).astype(jnp.float32)
@@ -62,7 +62,7 @@
     rank = jnp.sum(rivals, axis=0, keepdims=True)
     gated = (gate_down * grads_ref[...].astype(jnp.float32)).astype(jnp.bfloat16)
     for k, (expert, begin, end, row) in enumerate(blocks):
-        rows_ref, pick_ref = outs[copies + 2 * k], outs[copies + 2 * k + 1]
+        rows_ref, pick_ref = outs[2 * k], outs[2 * k + 1]
         chosen = (relative == expert) & (rank >= begin) & (rank < end)
         slot = jnp.where(chosen, rank - begin + row, -1.0).astype(jnp.int32)
         slots = lax.broadcasted_iota(jnp.int32, pick_ref.shape, 0)
@@ -72,24 +72,37 @@
             rows_ref[:, half * width : (half + 1) * width] = jnp.dot(
                 pick, source, preferred_element_type=jnp.float32
             ).astype(jnp.bfloat16)
-    for copy_ref in outs[:copies]:
-        copy_ref[...] = outs[copies][...]
-
-
-def pack(blocks, rows, copies, experts, ids, gate, tokens, grads):
+
+
+def pack(blocks, rows, experts, ids, gate, tokens, grads):
     n, width = tokens.shape
-    shapes = [jax.ShapeDtypeStruct((rows[0], 2 * width), jnp.bfloat16)] * copies
+    shapes = []
     for count in rows:
         shapes.append(jax.ShapeDtypeStruct((count, 2 * width), jnp.bfloat16))
         shapes.append(jax.ShapeDtypeStruct((count, n), jnp.bfloat16))
     whole = pl.BlockSpec(memory_space=pltpu.VMEM)
     outs = pl.pallas_call(
-        lambda *refs: pack_kernel(blocks, copies, experts, *refs),
+        lambda *refs: pack_kernel(blocks, experts, *refs),
         out_shape=shapes,
         in_specs=[whole] * 4,
         out_specs=[whole] * len(shapes),
     )(ids.reshape(1, n), gate.reshape(1, n), tokens, grads)
-    return outs[:copies], outs[copies::2], outs[copies + 1 :: 2]
+    return outs[::2], outs[1::2]
+
+
+def copies_kernel(rows_ref, *refs):
+    for copy_ref in refs[-len(early_masks) :]:
+        copy_ref[...] = rows_ref[...]
+
+
+def early_copies(rows, *awaited):
+    whole = pl.BlockSpec(memory_space=pltpu.VMEM)
+    return pl.pallas_call(
+        copies_kernel,
+        out_shape=[jax.ShapeDtypeStruct(rows.shape, rows.dtype)] * len(early_masks),
+        in_specs=[whole] + [pl.BlockSpec(memory_space=pl.ANY)] * len(awaited),
+        out_specs=[whole] * len(early_masks),
+    )(rows, *awaited)
 
 
 def whole_weights(shard):
@@ -112,7 +125,7 @@
 
 
 core_bit, x_bit, y_bit, z_bit = 1, 2, 4, 8
-early_masks = (x_bit, y_bit, z_bit, x_bit | y_bit | z_bit)
+early_masks = (x_bit, y_bit, z_bit, x_bit | y_bit)
 
 
 def after(values, *others):
@@ -126,23 +139,12 @@
     return [swap(block, mask) for block, mask in zip(chained, masks)]
 
 
-second_masks = (y_bit, z_bit, x_bit, x_bit | y_bit)
-
-
 def total(*terms):
     return sum(term.astype(jnp.float32) for term in terms).astype(jnp.bfloat16)
 
 
 def split_rows(array, rows):
     return [array[k : k + rows] for k in range(0, array.shape[0], rows)]
-
-
-def near_sums(near, far):
-    return (
-        total(near[1], far[0]),
-        total(near[2], far[1]),
-        total(near[3], far[2], far[3]),
-    )
 
 
 def shards(tokens, attn_partials, expert_ids, gate, w_in, w_out):
@@ -164,10 +166,9 @@
     own_blocks = [(0, 0, first, 0), (0, first, capacity, offset + first)]
     cross_blocks = [(s, 0, capacity, (s - 1) * capacity) for s in range(1, experts)]
     grads = summed_grads(attn_partials)
-    early_copies, (early_own, late_own, *sent), picks = pack(
+    (early_own, late_own, *sent), picks = pack(
         own_blocks + cross_blocks,
         [first] + [rest] * experts,
-        len(early_masks),
         experts,
         expert_ids,
         gate,
@@ -189,19 +190,20 @@
 
     for s in range(1, experts):
         late_own = late_own + shifted(sent[s - 1], s)
-    *early_near, early_far = after(
-        [swap(rows, mask) for rows, mask in zip(early_copies, early_masks)], late_own
-    )
-    arrived = swaps(
+    early_x, early_y, early_z, early_xy = after(
+        [swap(rows, mask) for rows, mask in zip(early_copies(early_own, *sent), early_masks)], late_own
+    )
+    late_x, late_y, late_z = swaps(
         [
-            jnp.concatenate([rows, late_own], axis=0)
-            for rows in (early_near[2], early_near[0], early_near[1])
+            jnp.concatenate([late_own, early_z], axis=0),
+            jnp.concatenate([late_own, early_z], axis=0),
+            late_own,
         ],
         (x_bit, y_bit, z_bit),
     )
-    early_zx, early_xy, early_yz = [rows[:first] for rows in arrived]
-    late_near = [rows[first:] for rows in arrived]
-    early_rows = [early_own, *early_near, early_xy, early_yz, early_zx, early_far]
+    early_zx, early_yz = late_x[rest:], late_y[rest:]
+    late_x, late_y = late_x[:rest], late_y[:rest]
+    early_rows = [early_own, early_x, early_y, early_z, early_xy, early_yz, early_zx]
 
     own_weights = jnp.concatenate([whole_weights(w_in).T, whole_weights(w_out).T], axis=0)
     their_weights = swap(after(own_weights, late_own), core_bit)
@@ -209,10 +211,10 @@
         jnp.concatenate([own_weights[part], their_weights[part]], axis=0)
         for part in (slice(0, units), slice(units, 2 * units))
     ]
-    near_x, near_y, near_z = late_near
-    late_far = [
-        swap(rows, mask) for rows, mask in zip((near_x, near_y, near_z, near_z), second_masks)
-    ]
+    late_far, late_zx, late_yz, late_xy = swaps(
+        [late_z, late_z, jnp.concatenate([late_y, early_xy], axis=0), late_x],
+        (x_bit | y_bit, x_bit, z_bit, y_bit),
+    )
     early = activated(jnp.concatenate(early_rows, axis=0))
     early_parts = input_parts(early[3])
     mine, theirs = slice(0, units), slice(units, 2 * units)
@@ -225,14 +227,19 @@
         ]
 
     early_gradients = gradients(early)
-    late_far = after(late_far, early_parts, early_gradients)
-    later = activated(jnp.concatenate([late_own, *late_near, *late_far], axis=0))
+    late_rows = [late_own, late_x, late_y, late_z, late_xy, late_yz[:rest], late_zx, late_far]
+    late_rows = after([*late_rows, late_yz[rest:]], early_parts, early_gradients)
+    later = activated(jnp.concatenate(late_rows, axis=0))
     late_parts = input_parts(later[3])
+    late_parts, last_parts = late_parts[: 8 * rest], late_parts[8 * rest :]
     parts = [
         jnp.concatenate(pair, axis=0)
-        for pair in zip(split_rows(early_parts, first), split_rows(late_parts, rest))
+        for pair in zip([*split_rows(early_parts, first), last_parts], split_rows(late_parts, rest))
     ]
-    back_far = swaps(parts[4:], second_masks)
+    own, sum_x, sum_y, sum_z, sum_xy, sum_yz, sum_zx, sum_far = parts
+    far, zx, xy, yz = swaps(
+        [sum_far, sum_zx, sum_xy, sum_yz], (x_bit | y_bit, x_bit, y_bit, z_bit)
+    )
     in_mine, in_theirs, out_mine, out_theirs = [
         sum(pair) * scale
         for pair, scale in zip(
@@ -244,9 +251,10 @@
     out_shared = swap(out_theirs.astype(jnp.bfloat16), core_bit).astype(jnp.float32)
     new_w_in = stepped(w_in, (in_mine + in_shared).T)
     new_w_out = stepped(w_out, (out_mine + out_shared).T)
-    back_near = swaps(near_sums(parts, back_far), (x_bit, y_bit, z_bit))
-    back_near = after(back_near, new_w_in)
-    sums = total(parts[0], *back_near)
+    near = swaps(
+        [total(sum_z, zx, far), total(sum_x, xy), total(sum_y, yz)], (z_bit, x_bit, y_bit)
+    )
+    sums = total(own, *near)
     early_sum, late_sum = sums[:first], sums[first:]
     crossed = [shifted(late_sum, -s) for s in range(1, experts)]
 

time: 73.5 us -> 70.7 us (0.962)
  waiting for transfers between devices: 25.8 us -> 21.7 us
  starting transfers between devices: 24.5 us -> 22.6 us
  Pallas kernels: 2.49 us -> 4.05 us
  local copies, waits for them, and re-layouts: 1.45 us -> 2.97 us
    ppermute x2, waiting for transfers between devices: 2.88 us -> 0.01 us  [shifted(): return lax.ppermute(rows, 'expert', pairs)]
    pallas_call x1 -> x2, Pallas kernels: 2.49 us -> 4.05 us  [the longest x1 2.33 us: pack(): pl.pallas_call(lambda *refs: pack_kernel(blocks, experts, *refs), out_sha...]
    unnamed x22 -> x28, local copies, waits for them, and re-layouts: 1.05 us -> 2.37 us
    ppermute x21, starting transfers between devices: 19.4 us -> 18.1 us  [swap(): lax.ppermute(rows, 'expert', [(i, i ^ mask) for i in range(n_expert)])]
    ppermute x21, waiting for transfers between devices: 22.9 us -> 21.7 us  [swap(): lax.ppermute(rows, 'expert', [(i, i ^ mask) for i in range(n_expert)])]
  transfers between devices with their start and end apart: 23 -> 23, of which waited for: 13 -> 10; matrix products, arithmetic and copies ran while one was open for 19% -> 21% of each run, Pallas kernels for 0% -> 2%
where the time goes in v8:
time: 70.7 us; the launch traced here: 70.5 us
  starting transfers between devices  22.6 us (32%)
  waiting for transfers between devices  21.7 us (31%)
  matrix products  15.4 us (22%)
  Pallas kernels  4.05 us (6%)
  local copies, waits for them, and re-layouts  2.97 us (4%)
  other arithmetic  2.65 us (4%)
  between operations  1.11 us (2%)
    ppermute x21, waiting for transfers between devices, swap(): lax.ppermute(rows, 'expert', [(i, i ^ mask) for i in range(n_expert)])  21.7 us
    ppermute x21, starting transfers between devices, swap(): lax.ppermute(rows, 'expert', [(i, i ^ mask) for i in range(n_expert)])  18.1 us
    dot_general x11, matrix products, contract_rows(): lax.dot_general(left, right, (((0,), (0,)), ((), ())), preferred_element_...  9.64 us
    ppermute x2, starting transfers between devices, shifted(): return lax.ppermute(rows, 'expert', pairs)  4.52 us
    dot_general x4, matrix products, contract_cols(): lax.dot_general(left, right, (((1,), (1,)), ((), ())), preferred_element_...  4.3 us
    unnamed x28, local copies, waits for them, and re-layouts  2.37 us
    pallas_call x1, Pallas kernels, pack(): pl.pallas_call(lambda *refs: pack_kernel(blocks, experts, *refs), out_sha...  2.33 us
    transpose x1, other arithmetic, shards(): whole_weights(w_in)  1.92 us
  transfers between devices with their start and end apart: 23, of which 10 were waited for; matrix products, arithmetic and copies ran while one was open for 21% of the time, Pallas kernels for 2%

profile of v8, /device:TPU:0, one launch (start us, length us, event | category | flops | bytes accessed | tf_op | source)
XLA Modules:
  0.0 70.5 jit_solution(18013196207306436623)
XLA Ops:
  0.6 2.3 %shard_map.85 = (bf16[16,4096]{1,0:T(8,128)(2,1)}, bf16[16,64]{1,0:T(8,128)(2,1)}, bf16[24,4096]{1,0:T(8,128)(2,1)}, bf16[24,64]{1,0:T(8,128)(2,1)}, bf16[24,4096]{1,0:T(8,128)(2,1)}, /*index=5*/bf16[24,64]{1,0:T(8,128)(2,1)}) custom-call(s32[1,64]{1,0:T(1,128)} %bitcast.18, f32[1,64]{1,0:T(1,128)} %bitcast.19, bf16[64,2048]{1,0:T(8,128)(2,1)} %refs_2_.1, ...), custom_call_target="tpu_custom_call" | custom-call | tf_op jit(solution)/shard_map/pallas_call | solution.py:84
  3.0 4.0 %collective-permute-start = (bf16[24,4096]{1,0:T(8,128)(2,1)}, bf16[24,4096]{1,0:T(8,128)(2,1)S(1)}, u32[]{:S(2)}, u32[]{:S(2)}) collective-permute-start(bf16[24,4096]{1,0:T(8,128)(2,1)} %get-tuple-element.41.refs_0_), channel_id=1, source_target_pairs={{0,16},{1,17},{2,18},{3,19},{4,20},{5,21},{6,22},{7,23},{8,24},{9,... | collective-permute-start | bytes 589832 | tf_op jit(solution)/shard_map/ppermute | solution.py:163
  7.0 1.7 %shard_map.86 = (bf16[16,4096]{1,0:T(8,128)(2,1)}, bf16[16,4096]{1,0:T(8,128)(2,1)}, bf16[16,4096]{1,0:T(8,128)(2,1)}, bf16[16,4096]{1,0:T(8,128)(2,1)}) custom-call(bf16[16,4096]{1,0:T(8,128)(2,1)} %get-tuple-element.39.rows_ref, bf16[24,4096]{1,0:T(8,128)(2,1)} %get-tuple-element.41.refs_0_), custom_call_target="tpu_custom_call" | custom-call | tf_op jit(solution)/shard_map/pallas_call | solution.py:100
  8.7 1.5 %collective-permute-start.1 = (bf16[16,4096]{1,0:T(8,128)(2,1)}, bf16[16,4096]{1,0:T(8,128)(2,1)S(1)}, u32[]{:S(2)}, u32[]{:S(2)}) collective-permute-start(bf16[16,4096]{1,0:T(8,128)(2,1)} %get-tuple-element.42), channel_id=1, source_target_pairs={{0,2},{1,3},{2,0},{3,1},{4,6},{5,7},{6,4},{7,5},{8,10},{9,11},{10,... | collective-permute-start | bytes 393224 | tf_op jit(solution)/shard_map/ppermute | solution.py:124
  10.2 1.5 %collective-permute-start.2 = (bf16[16,4096]{1,0:T(8,128)(2,1)}, bf16[16,4096]{1,0:T(8,128)(2,1)S(1)}, u32[]{:S(2)}, u32[]{:S(2)}) collective-permute-start(bf16[16,4096]{1,0:T(8,128)(2,1)} %get-tuple-element.43), channel_id=1, source_target_pairs={{0,4},{1,5},{2,6},{3,7},{4,0},{5,1},{6,2},{7,3},{8,12},{9,13},{10,... | collective-permute-start | bytes 393224 | tf_op jit(solution)/shard_map/ppermute | solution.py:124
  11.7 1.6 %collective-permute-start.3 = (bf16[16,4096]{1,0:T(8,128)(2,1)}, bf16[16,4096]{1,0:T(8,128)(2,1)S(1)}, u32[]{:S(2)}, u32[]{:S(2)}) collective-permute-start(bf16[16,4096]{1,0:T(8,128)(2,1)} %get-tuple-element.44), channel_id=1, source_target_pairs={{0,8},{1,9},{2,10},{3,11},{4,12},{5,13},{6,14},{7,15},{8,0},{9,1},... | collective-permute-start | bytes 393224 | tf_op jit(solution)/shard_map/ppermute | solution.py:124
  14.7 1.9 %convert_bitcast_fusion = bf16[320,2048]{1,0:T(8,128)(2,1)S(1)} fusion(f32[2048,320]{0,1:T(8,128)} %param.10), kind=kLoop, calls=%fused_computation.24 | loop fusion | flops 655360 | bytes 3932160 | tf_op jit(solution)/shard_map/transpose | solution.py:208
  17.8 1.3 %collective-permute-done.3 = bf16[16,4096]{1,0:T(8,128)(2,1)S(1)} collective-permute-done((bf16[16,4096]{1,0:T(8,128)(2,1)}, bf16[16,4096]{1,0:T(8,128)(2,1)S(1)}, u32[]{:S(2)}, u32[]{:S(2)}) %collective-permute-start.3) | collective-permute-done | bytes 131104 | tf_op jit(solution)/shard_map/ppermute | solution.py:124
  21.9 4.8 %collective-permute-done.8 = bf16[24,4096]{1,0:T(8,128)(2,1)S(1)} collective-permute-done((bf16[24,4096]{1,0:T(8,128)(2,1)S(1)}, bf16[24,4096]{1,0:T(8,128)(2,1)S(1)}, u32[]{:S(2)}, u32[]{:S(2)}) %collective-permute-start.8) | collective-permute-done | bytes 196640 | tf_op jit(solution)/shard_map/ppermute | solution.py:124
  26.6 1.2 %collective-permute-start.11 = (bf16[24,4096]{1,0:T(8,128)(2,1)S(1)}, bf16[24,4096]{1,0:T(8,128)(2,1)S(1)}, u32[]{:S(2)}, u32[]{:S(2)}) collective-permute-start(bf16[24,4096]{1,0:T(8,128)(2,1)S(1)} %collective-permute-done.8), channel_id=1, source_target_pairs={{0,2},{1,3},{2,0},{3,1},{4,6},{5,7},{6,4},{7,5},{8,10},{9,11},{10,... | collective-permute-start | bytes 589832 | tf_op jit(solution)/shard_map/ppermute | solution.py:124
  27.9 1.4 %collective-permute-start.12 = (bf16[24,4096]{1,0:T(8,128)(2,1)S(1)}, bf16[24,4096]{1,0:T(8,128)(2,1)S(1)}, u32[]{:S(2)}, u32[]{:S(2)}) collective-permute-start(bf16[24,4096]{1,0:T(8,128)(2,1)S(1)} %collective-permute-done.8), channel_id=1, source_target_pairs={{0,6},{1,7},{2,4},{3,5},{4,2},{5,3},{6,0},{7,1},{8,14},{9,15},{10,... | collective-permute-start | bytes 589832 | tf_op jit(solution)/shard_map/ppermute | solution.py:124
  30.7 1.6 %collective-permute-start.9 = (bf16[24,4096]{1,0:T(8,128)(2,1)S(1)}, bf16[24,4096]{1,0:T(8,128)(2,1)S(1)}, u32[]{:S(2)}, u32[]{:S(2)}) collective-permute-start(bf16[24,4096]{1,0:T(8,128)(2,1)S(1)} %slice.172), channel_id=1, source_target_pairs={{0,4},{1,5},{2,6},{3,7},{4,0},{5,1},{6,2},{7,3},{8,12},{9,13},{10,... | collective-permute-start | bytes 589832 | tf_op jit(solution)/shard_map/ppermute | solution.py:124
  32.3 5.2 %collective-permute-done.10 = bf16[40,4096]{1,0:T(8,128)(2,1)S(1)} collective-permute-done((bf16[40,4096]{1,0:T(8,128)(2,1)S(1)}, bf16[40,4096]{1,0:T(8,128)(2,1)S(1)}, u32[]{:S(2)}, u32[]{:S(2)}) %collective-permute-start.10) | collective-permute-done | bytes 327712 | tf_op jit(solution)/shard_map/ppermute | solution.py:124
  38.2 1.0 %multiply_convert_fusion.1 = (bf16[112,640]{1,0:T(8,128)(2,1)S(1)}, f32[112,640]{1,0:T(8,128)S(1)}) fusion(bf16[320,2048]{1,0:T(8,128)(2,1)S(1)} %convert_bitcast_fusion, bf16[320,2048]{1,0:T(8,128)(2,1)S(1)} %get-tuple-element.73, bf16[112,4096]{1,0:T(8,128)(2,1)S(1)} %slice_dynamic-update-slice_fusion), kind=kOutput, calls=%fused_computation.64 | convolution fusion | flops 299560960 | bytes 3510272 | tf_op jit(solution)/shard_map/dot_general | solution.py:39
  39.2 1.0 %fusion.16 = bf16[112,640]{1,0:T(8,128)(2,1)S(1)} fusion(bf16[320,2048]{1,0:T(8,128)(2,1)S(1)} %get-tuple-element.74, bf16[320,2048]{1,0:T(8,128)(2,1)S(1)} %convert_bitcast_fusion.1, bf16[112,4096]{1,0:T(8,128)(2,1)S(1)} %slice_dynamic-update-slice_fusion, f32[112,640]{1,0:T(8,128)S(1)} %get-tuple-element.91), kind=kOutput, calls=%fused_computation.31 | convolution fusion | flops 300349440 | bytes 3510272 | tf_op jit(solution)/shard_map/dot_general | solution.py:39
  43.6 1.1 %multiply_convert_fusion = (bf16[208,640]{1,0:T(8,128)(2,1)S(1)}, f32[208,640]{1,0:T(8,128)S(1)}) fusion(bf16[320,2048]{1,0:T(8,128)(2,1)S(1)} %convert_bitcast_fusion, bf16[320,2048]{1,0:T(8,128)(2,1)S(1)} %get-tuple-element.73, bf16[208,4096]{1,0:T(8,128)(2,1)S(1)} %constant_dynamic-update-slice_fusion.5), kind=kOutput, calls=%fused_computation.42 | convolution fusion | flops 551833600 | bytes 4272128 | tf_op jit(solution)/shard_map/dot_general | solution.py:39
  44.7 1.2 %fusion.13 = bf16[208,640]{1,0:T(8,128)(2,1)S(1)} fusion(bf16[320,2048]{1,0:T(8,128)(2,1)S(1)} %get-tuple-element.74, bf16[320,2048]{1,0:T(8,128)(2,1)S(1)} %convert_bitcast_fusion.1, bf16[208,4096]{1,0:T(8,128)(2,1)S(1)} %constant_dynamic-update-slice_fusion.5, f32[208,640]{1,0:T(8,128)S(1)} %get-tuple-element.93), kind=kOutput, calls=%fused_computation.28 | convolution fusion | flops 553297920 | bytes 4272128 | tf_op jit(solution)/shard_map/dot_general | solution.py:39
  49.2 2.1 %collective-permute-start.16 = (bf16[40,2048]{1,0:T(8,128)(2,1)S(1)}, bf16[40,2048]{1,0:T(8,128)(2,1)S(1)}, u32[]{:S(2)}, u32[]{:S(2)}) collective-permute-start(bf16[40,2048]{1,0:T(8,128)(2,1)S(1)} %get-tuple-element.66), channel_id=1, source_target_pairs={{0,4},{1,5},{2,6},{3,7},{4,0},{5,1},{6,2},{7,3},{8,12},{9,13},{10,... | collective-permute-start | bytes 491528 | tf_op jit(solution)/shard_map/ppermute | solution.py:124
  51.5 2.6 %collective-permute-done.13 = bf16[40,2048]{1,0:T(8,128)(2,1)S(1)} collective-permute-done((bf16[40,2048]{1,0:T(8,128)(2,1)S(1)}, bf16[40,2048]{1,0:T(8,128)(2,1)S(1)}, u32[]{:S(2)}, u32[]{:S(2)}) %collective-permute-start.13) | collective-permute-done | bytes 163872 | tf_op jit(solution)/shard_map/ppermute | solution.py:124
  55.7 1.0 %collective-permute-start.17 = (bf16[40,2048]{1,0:T(8,128)(2,1)S(1)}, bf16[40,2048]{1,0:T(8,128)(2,1)S(1)}, u32[]{:S(2)}, u32[]{:S(2)}) collective-permute-start(bf16[40,2048]{1,0:T(8,128)(2,1)S(1)} %add_convert_fusion.2), channel_id=1, source_target_pairs={{0,2},{1,3},{2,0},{3,1},{4,6},{5,7},{6,4},{7,5},{8,10},{9,11},{10,... | collective-permute-start | bytes 491528 | tf_op jit(solution)/shard_map/ppermute | solution.py:124
  56.7 1.6 %collective-permute-done.18 = bf16[40,2048]{1,0:T(8,128)(2,1)S(1)} collective-permute-done((bf16[40,2048]{1,0:T(8,128)(2,1)S(1)}, bf16[40,2048]{1,0:T(8,128)(2,1)S(1)}, u32[]{:S(2)}, u32[]{:S(2)}) %collective-permute-start.18) | collective-permute-done | bytes 163872 | tf_op jit(solution)/shard_map/ppermute | solution.py:124
  60.0 3.7 %collective-permute-done.19 = bf16[40,2048]{1,0:T(8,128)(2,1)S(1)} collective-permute-done((bf16[40,2048]{1,0:T(8,128)(2,1)S(1)}, bf16[40,2048]{1,0:T(8,128)(2,1)S(1)}, u32[]{:S(2)}, u32[]{:S(2)}) %collective-permute-start.19) | collective-permute-done | bytes 163872 | tf_op jit(solution)/shard_map/ppermute | solution.py:124
  64.8 2.3 %bitcast_subtract_fusion.1 = f32[2048,320]{0,1:T(8,128)} fusion(f32[2048,320]{0,1:T(8,128)S(1)} %copy-done, bf16[320,2048]{1,0:T(8,128)(2,1)S(1)} %collective-permute-done.20, f32[320,2048]{1,0:T(8,128)S(1)} %fusion.29, bf16[208,4096]{1,0:T(8,128)(2,1)S(1)} %constant_dynamic-update-slice_fusion.5, bf16[208,640]{1,0:T(8,128)(2,1)S(1)} %fusion.13), kind=kOutput, calls=%fused_computation.15 | convolution fusion | flops 276561920 | bytes 10186752 | tf_op jit(solution)/shard_map/dot_general | solution.py:33
  67.2 2.3 %bitcast_subtract_fusion = f32[2048,320]{0,1:T(8,128)} fusion(f32[2048,320]{0,1:T(8,128)S(1)} %copy-done.1, bf16[320,2048]{1,0:T(8,128)(2,1)S(1)} %collective-permute-done.21, f32[320,2048]{1,0:T(8,128)S(1)} %fusion.35, bf16[208,4096]{1,0:T(8,128)(2,1)S(1)} %constant_dynamic-update-slice_fusion.5, bf16[208,640]{1,0:T(8,128)(2,1)S(1)} %get-tuple-element.92), kind=kOutput, calls=%fused_computation.14 | convolution fusion | flops 276561920 | bytes 10186752 | tf_op jit(solution)/shard_map/dot_general | solution.py:33
  (95 shorter events, 19.4 us)
Async XLA Ops:
  0.6 16.0 %copy-start.1 = (f32[2048,320]{0,1:T(8,128)S(1)}, f32[2048,320]{0,1:T(8,128)}, u32[]{:S(2)}) copy-start(f32[2048,320]{0,1:T(8,128)} %param.11) | copy-start | bytes 7864324
  3.0 14.1 %collective-permute-start = (bf16[24,4096]{1,0:T(8,128)(2,1)}, bf16[24,4096]{1,0:T(8,128)(2,1)S(1)}, u32[]{:S(2)}, u32[]{:S(2)}) collective-permute-start(bf16[24,4096]{1,0:T(8,128)(2,1)} %get-tuple-element.41.refs_0_), channel_id=1, source_target_pairs={{0,16},{1,17},{2,18},{3,19},{4,20},{5,21},{6,22},{7,23},{8,24},{9,... | collective-permute-start | bytes 589832 | tf_op jit(solution)/shard_map/ppermute | solution.py:163
  8.7 9.1 %collective-permute-start.1 = (bf16[16,4096]{1,0:T(8,128)(2,1)}, bf16[16,4096]{1,0:T(8,128)(2,1)S(1)}, u32[]{:S(2)}, u32[]{:S(2)}) collective-permute-start(bf16[16,4096]{1,0:T(8,128)(2,1)} %get-tuple-element.42), channel_id=1, source_target_pairs={{0,2},{1,3},{2,0},{3,1},{4,6},{5,7},{6,4},{7,5},{8,10},{9,11},{10,... | collective-permute-start | bytes 393224 | tf_op jit(solution)/shard_map/ppermute | solution.py:124
  10.2 7.6 %collective-permute-start.2 = (bf16[16,4096]{1,0:T(8,128)(2,1)}, bf16[16,4096]{1,0:T(8,128)(2,1)S(1)}, u32[]{:S(2)}, u32[]{:S(2)}) collective-permute-start(bf16[16,4096]{1,0:T(8,128)(2,1)} %get-tuple-element.43), channel_id=1, source_target_pairs={{0,4},{1,5},{2,6},{3,7},{4,0},{5,1},{6,2},{7,3},{8,12},{9,13},{10,... | collective-permute-start | bytes 393224 | tf_op jit(solution)/shard_map/ppermute | solution.py:124
  11.7 7.4 %collective-permute-start.3 = (bf16[16,4096]{1,0:T(8,128)(2,1)}, bf16[16,4096]{1,0:T(8,128)(2,1)S(1)}, u32[]{:S(2)}, u32[]{:S(2)}) collective-permute-start(bf16[16,4096]{1,0:T(8,128)(2,1)} %get-tuple-element.44), channel_id=1, source_target_pairs={{0,8},{1,9},{2,10},{3,11},{4,12},{5,13},{6,14},{7,15},{8,0},{9,1},... | collective-permute-start | bytes 393224 | tf_op jit(solution)/shard_map/ppermute | solution.py:124
  13.3 6.1 %collective-permute-start.4 = (bf16[16,4096]{1,0:T(8,128)(2,1)}, bf16[16,4096]{1,0:T(8,128)(2,1)S(1)}, u32[]{:S(2)}, u32[]{:S(2)}) collective-permute-start(bf16[16,4096]{1,0:T(8,128)(2,1)} %get-tuple-element.45), channel_id=1, source_target_pairs={{0,6},{1,7},{2,4},{3,5},{4,2},{5,3},{6,0},{7,1},{8,14},{9,15},{10,... | collective-permute-start | bytes 393224 | tf_op jit(solution)/shard_map/ppermute | solution.py:124
  19.4 9.9 %collective-permute-start.5 = (bf16[40,4096]{1,0:T(8,128)(2,1)S(1)}, bf16[40,4096]{1,0:T(8,128)(2,1)S(1)}, u32[]{:S(2)}, u32[]{:S(2)}) collective-permute-start(bf16[40,4096]{1,0:T(8,128)(2,1)S(1)} %pad_maximum_fusion.17), channel_id=1, source_target_pairs={{0,4},{1,5},{2,6},{3,7},{4,0},{5,1},{6,2},{7,3},{8,12},{9,13},{10,... | collective-permute-start | bytes 983048 | tf_op jit(solution)/shard_map/ppermute | solution.py:124
  20.0 10.6 %collective-permute-start.6 = (bf16[40,4096]{1,0:T(8,128)(2,1)S(1)}, bf16[40,4096]{1,0:T(8,128)(2,1)S(1)}, u32[]{:S(2)}, u32[]{:S(2)}) collective-permute-start(bf16[40,4096]{1,0:T(8,128)(2,1)S(1)} %pad_maximum_fusion.17), channel_id=1, source_target_pairs={{0,2},{1,3},{2,0},{3,1},{4,6},{5,7},{6,4},{7,5},{8,10},{9,11},{10,... | collective-permute-start | bytes 983048 | tf_op jit(solution)/shard_map/ppermute | solution.py:124
  21.0 5.7 %collective-permute-start.8 = (bf16[24,4096]{1,0:T(8,128)(2,1)S(1)}, bf16[24,4096]{1,0:T(8,128)(2,1)S(1)}, u32[]{:S(2)}, u32[]{:S(2)}) collective-permute-start(bf16[24,4096]{1,0:T(8,128)(2,1)S(1)} %add.76), channel_id=1, source_target_pairs={{0,8},{1,9},{2,10},{3,11},{4,12},{5,13},{6,14},{7,15},{8,0},{9,1},... | collective-permute-start | bytes 589832 | tf_op jit(solution)/shard_map/ppermute | solution.py:124
  21.8 15.7 %collective-permute-start.7 = (bf16[640,2048]{1,0:T(8,128)(2,1)S(1)}, bf16[640,2048]{1,0:T(8,128)(2,1)S(1)}, u32[]{:S(2)}, u32[]{:S(2)}) collective-permute-start(bf16[640,2048]{1,0:T(8,128)(2,1)S(1)} %pad_maximum_fusion.1), channel_id=1, source_target_pairs={{0,1},{1,0},{2,3},{3,2},{4,5},{5,4},{6,7},{7,6},{8,9},{9,8},{10,11... | collective-permute-start | bytes 7864328 | tf_op jit(solution)/shard_map/ppermute | solution.py:124
  26.6 16.5 %collective-permute-start.11 = (bf16[24,4096]{1,0:T(8,128)(2,1)S(1)}, bf16[24,4096]{1,0:T(8,128)(2,1)S(1)}, u32[]{:S(2)}, u32[]{:S(2)}) collective-permute-start(bf16[24,4096]{1,0:T(8,128)(2,1)S(1)} %collective-permute-done.8), channel_id=1, source_target_pairs={{0,2},{1,3},{2,0},{3,1},{4,6},{5,7},{6,4},{7,5},{8,10},{9,11},{10,... | collective-permute-start | bytes 589832 | tf_op jit(solution)/shard_map/ppermute | solution.py:124
  27.9 15.2 %collective-permute-start.12 = (bf16[24,4096]{1,0:T(8,128)(2,1)S(1)}, bf16[24,4096]{1,0:T(8,128)(2,1)S(1)}, u32[]{:S(2)}, u32[]{:S(2)}) collective-permute-start(bf16[24,4096]{1,0:T(8,128)(2,1)S(1)} %collective-permute-done.8), channel_id=1, source_target_pairs={{0,6},{1,7},{2,4},{3,5},{4,2},{5,3},{6,0},{7,1},{8,14},{9,15},{10,... | collective-permute-start | bytes 589832 | tf_op jit(solution)/shard_map/ppermute | solution.py:124
  29.3 8.2 %collective-permute-start.10 = (bf16[40,4096]{1,0:T(8,128)(2,1)S(1)}, bf16[40,4096]{1,0:T(8,128)(2,1)S(1)}, u32[]{:S(2)}, u32[]{:S(2)}) collective-permute-start(bf16[40,4096]{1,0:T(8,128)(2,1)S(1)} %pad_maximum_fusion.18), channel_id=1, source_target_pairs={{0,8},{1,9},{2,10},{3,11},{4,12},{5,13},{6,14},{7,15},{8,0},{9,1},... | collective-permute-start | bytes 983048 | tf_op jit(solution)/shard_map/ppermute | solution.py:124
  30.7 12.4 %collective-permute-start.9 = (bf16[24,4096]{1,0:T(8,128)(2,1)S(1)}, bf16[24,4096]{1,0:T(8,128)(2,1)S(1)}, u32[]{:S(2)}, u32[]{:S(2)}) collective-permute-start(bf16[24,4096]{1,0:T(8,128)(2,1)S(1)} %slice.172), channel_id=1, source_target_pairs={{0,4},{1,5},{2,6},{3,7},{4,0},{5,1},{6,2},{7,3},{8,12},{9,13},{10,... | collective-permute-start | bytes 589832 | tf_op jit(solution)/shard_map/ppermute | solution.py:124
  47.5 6.6 %collective-permute-start.14 = (bf16[40,2048]{1,0:T(8,128)(2,1)S(1)}, bf16[40,2048]{1,0:T(8,128)(2,1)S(1)}, u32[]{:S(2)}, u32[]{:S(2)}) collective-permute-start(bf16[40,2048]{1,0:T(8,128)(2,1)S(1)} %pad_maximum_fusion.19), channel_id=1, source_target_pairs={{0,6},{1,7},{2,4},{3,5},{4,2},{5,3},{6,0},{7,1},{8,14},{9,15},{10,... | collective-permute-start | bytes 491528 | tf_op jit(solution)/shard_map/ppermute | solution.py:124
  48.2 5.9 %collective-permute-start.13 = (bf16[40,2048]{1,0:T(8,128)(2,1)S(1)}, bf16[40,2048]{1,0:T(8,128)(2,1)S(1)}, u32[]{:S(2)}, u32[]{:S(2)}) collective-permute-start(bf16[40,2048]{1,0:T(8,128)(2,1)S(1)} %pad_maximum_fusion.20), channel_id=1, source_target_pairs={{0,2},{1,3},{2,0},{3,1},{4,6},{5,7},{6,4},{7,5},{8,10},{9,11},{10,... | collective-permute-start | bytes 491528 | tf_op jit(solution)/shard_map/ppermute | solution.py:124
  49.2 6.5 %collective-permute-start.16 = (bf16[40,2048]{1,0:T(8,128)(2,1)S(1)}, bf16[40,2048]{1,0:T(8,128)(2,1)S(1)}, u32[]{:S(2)}, u32[]{:S(2)}) collective-permute-start(bf16[40,2048]{1,0:T(8,128)(2,1)S(1)} %get-tuple-element.66), channel_id=1, source_target_pairs={{0,4},{1,5},{2,6},{3,7},{4,0},{5,1},{6,2},{7,3},{8,12},{9,13},{10,... | collective-permute-start | bytes 491528 | tf_op jit(solution)/shard_map/ppermute | solution.py:124
  51.2 7.0 %collective-permute-start.18 = (bf16[40,2048]{1,0:T(8,128)(2,1)S(1)}, bf16[40,2048]{1,0:T(8,128)(2,1)S(1)}, u32[]{:S(2)}, u32[]{:S(2)}) collective-permute-start(bf16[40,2048]{1,0:T(8,128)(2,1)S(1)} %get-tuple-element.68), channel_id=1, source_target_pairs={{0,8},{1,9},{2,10},{3,11},{4,12},{5,13},{6,14},{7,15},{8,0},{9,1},... | collective-permute-start | bytes 491528 | tf_op jit(solution)/shard_map/ppermute | solution.py:124
  51.5 13.3 %collective-permute-start.20 = (bf16[320,2048]{1,0:T(8,128)(2,1)S(1)}, bf16[320,2048]{1,0:T(8,128)(2,1)S(1)}, u32[]{:S(2)}, u32[]{:S(2)}) collective-permute-start(bf16[320,2048]{1,0:T(8,128)(2,1)S(1)} %fusion.4), channel_id=1, source_target_pairs={{0,1},{1,0},{2,3},{3,2},{4,5},{5,4},{6,7},{7,6},{8,9},{9,8},{10,11... | collective-permute-start | bytes 3932168 | tf_op jit(solution)/shard_map/ppermute | solution.py:124
  54.2 5.8 %collective-permute-start.15 = (bf16[40,2048]{1,0:T(8,128)(2,1)S(1)}, bf16[40,2048]{1,0:T(8,128)(2,1)S(1)}, u32[]{:S(2)}, u32[]{:S(2)}) collective-permute-start(bf16[40,2048]{1,0:T(8,128)(2,1)S(1)} %add_convert_fusion.3), channel_id=1, source_target_pairs={{0,8},{1,9},{2,10},{3,11},{4,12},{5,13},{6,14},{7,15},{8,0},{9,1},... | collective-permute-start | bytes 491528 | tf_op jit(solution)/shard_map/ppermute | solution.py:124
  55.7 8.0 %collective-permute-start.17 = (bf16[40,2048]{1,0:T(8,128)(2,1)S(1)}, bf16[40,2048]{1,0:T(8,128)(2,1)S(1)}, u32[]{:S(2)}, u32[]{:S(2)}) collective-permute-start(bf16[40,2048]{1,0:T(8,128)(2,1)S(1)} %add_convert_fusion.2), channel_id=1, source_target_pairs={{0,2},{1,3},{2,0},{3,1},{4,6},{5,7},{6,4},{7,5},{8,10},{9,11},{10,... | collective-permute-start | bytes 491528 | tf_op jit(solution)/shard_map/ppermute | solution.py:124
  58.3 5.4 %collective-permute-start.19 = (bf16[40,2048]{1,0:T(8,128)(2,1)S(1)}, bf16[40,2048]{1,0:T(8,128)(2,1)S(1)}, u32[]{:S(2)}, u32[]{:S(2)}) collective-permute-start(bf16[40,2048]{1,0:T(8,128)(2,1)S(1)} %add_convert_fusion.1), channel_id=1, source_target_pairs={{0,4},{1,5},{2,6},{3,7},{4,0},{5,1},{6,2},{7,3},{8,12},{9,13},{10,... | collective-permute-start | bytes 491528 | tf_op jit(solution)/shard_map/ppermute | solution.py:124
  59.1 8.1 %collective-permute-start.21 = (bf16[320,2048]{1,0:T(8,128)(2,1)S(1)}, bf16[320,2048]{1,0:T(8,128)(2,1)S(1)}, u32[]{:S(2)}, u32[]{:S(2)}) collective-permute-start(bf16[320,2048]{1,0:T(8,128)(2,1)S(1)} %fusion.5), channel_id=1, source_target_pairs={{0,1},{1,0},{2,3},{3,2},{4,5},{5,4},{6,7},{7,6},{8,9},{9,8},{10,11... | collective-permute-start | bytes 3932168 | tf_op jit(solution)/shard_map/ppermute | solution.py:124
  63.8 5.7 %collective-permute-start.22 = (bf16[24,2048]{1,0:T(8,128)(2,1)S(1)}, bf16[24,2048]{1,0:T(8,128)(2,1)S(1)}, u32[]{:S(2)}, u32[]{:S(2)}) collective-permute-start(bf16[24,2048]{1,0:T(8,128)(2,1)S(1)} %slice.194), channel_id=1, source_target_pairs={{0,16},{1,17},{2,18},{3,19},{4,20},{5,21},{6,22},{7,23},{8,24},{9,... | collective-permute-start | bytes 294920 | tf_op jit(solution)/shard_map/ppermute | solution.py:163
  (8 other events, 24.4 us)

commit v9 on v8

--- a/solution.py
+++ b/solution.py
@@ -47,9 +47,17 @@
     return lax.psum_scatter(attn_partials[0], "dp", scatter_dimension=0, tiled=True)
 
 
-def pack_kernel(blocks, experts, *refs):
-    ids_ref, gate_ref, tokens_ref, grads_ref, *outs = refs
-    n, width = tokens_ref.shape
+def pick_rows(rows_ref, pick, tokens, gated):
+    width = tokens.shape[1]
+    for half, source in enumerate((tokens, gated)):
+        rows_ref[:, half * width : (half + 1) * width] = jnp.dot(
+            pick, source, preferred_element_type=jnp.float32
+        ).astype(jnp.bfloat16)
+
+
+def cross_kernel(blocks, experts, ids_ref, gate_ref, tokens_ref, grads_ref, gated_ref, *outs):
+    picks, sent = outs[: len(blocks)], outs[len(blocks) :]
+    n = tokens_ref.shape[0]
     mine = (lax.axis_index("expert") // SHARDS).astype(jnp.float32)
     ids = ids_ref[...].astype(jnp.float32)
     relative = ids - mine
@@ -61,48 +69,53 @@
     rivals = jnp.where((ids_down == ids) & (down < across), 1.0, 0.0)
     rank = jnp.sum(rivals, axis=0, keepdims=True)
     gated = (gate_down * grads_ref[...].astype(jnp.float32)).astype(jnp.bfloat16)
+    gated_ref[...] = gated
     for k, (expert, begin, end, row) in enumerate(blocks):
-        rows_ref, pick_ref = outs[2 * k], outs[2 * k + 1]
         chosen = (relative == expert) & (rank >= begin) & (rank < end)
         slot = jnp.where(chosen, rank - begin + row, -1.0).astype(jnp.int32)
-        slots = lax.broadcasted_iota(jnp.int32, pick_ref.shape, 0)
+        slots = lax.broadcasted_iota(jnp.int32, picks[k].shape, 0)
         pick = jnp.where(slots == slot, 1.0, 0.0).astype(jnp.bfloat16)
-        pick_ref[...] = pick
-        for half, source in enumerate((tokens_ref[...], gated)):
-            rows_ref[:, half * width : (half + 1) * width] = jnp.dot(
-                pick, source, preferred_element_type=jnp.float32
-            ).astype(jnp.bfloat16)
-
-
-def pack(blocks, rows, experts, ids, gate, tokens, grads):
+        picks[k][...] = pick
+        if k >= len(blocks) - len(sent):
+            pick_rows(sent[k - len(blocks) + len(sent)], pick, tokens_ref[...], gated)
+
+
+def pack_cross(blocks, rows, experts, ids, gate, tokens, grads):
     n, width = tokens.shape
-    shapes = []
-    for count in rows:
-        shapes.append(jax.ShapeDtypeStruct((count, 2 * width), jnp.bfloat16))
-        shapes.append(jax.ShapeDtypeStruct((count, n), jnp.bfloat16))
     whole = pl.BlockSpec(memory_space=pltpu.VMEM)
-    outs = pl.pallas_call(
-        lambda *refs: pack_kernel(blocks, experts, *refs),
+    gated, *outs = pl.pallas_call(
+        lambda *refs: cross_kernel(blocks, experts, *refs),
+        out_shape=[jax.ShapeDtypeStruct((n, width), jnp.bfloat16)]
+        + [jax.ShapeDtypeStruct((count, n), jnp.bfloat16) for count in rows]
+        + [jax.ShapeDtypeStruct((count, 2 * width), jnp.bfloat16) for count in rows[2:]],
+        in_specs=[whole] * 4,
+        out_specs=[whole] * (2 * len(rows) - 1),
+    )(ids.reshape(1, n), gate.reshape(1, n), tokens, grads)
+    return gated, outs[: len(rows)], outs[len(rows) :]
+
+
+def own_kernel(early_pick_ref, late_pick_ref, tokens_ref, gated_ref, *refs):
+    late_ref, early_ref, *copies = refs[-len(early_masks) - 2 :]
+    pick_rows(early_ref, early_pick_ref[...], tokens_ref[...], gated_ref[...])
+    for copy_ref in copies:
+        copy_ref[...] = early_ref[...]
+    pick_rows(late_ref, late_pick_ref[...], tokens_ref[...], gated_ref[...])
+
+
+def pack_own(early_pick, late_pick, tokens, gated, *sent):
+    whole = pl.BlockSpec(memory_space=pltpu.VMEM)
+    width = tokens.shape[1]
+    early, late = [
+        jax.ShapeDtypeStruct((pick.shape[0], 2 * width), jnp.bfloat16)
+        for pick in (early_pick, late_pick)
+    ]
+    shapes = [late] + [early] * (len(early_masks) + 1)
+    return pl.pallas_call(
+        own_kernel,
         out_shape=shapes,
-        in_specs=[whole] * 4,
+        in_specs=[whole] * 4 + [pl.BlockSpec(memory_space=pl.ANY)] * len(sent),
         out_specs=[whole] * len(shapes),
-    )(ids.reshape(1, n), gate.reshape(1, n), tokens, grads)
-    return outs[::2], outs[1::2]
-
-
-def copies_kernel(rows_ref, *refs):
-    for copy_ref in refs[-len(early_masks) :]:
-        copy_ref[...] = rows_ref[...]
-
-
-def early_copies(rows, *awaited):
-    whole = pl.BlockSpec(memory_space=pltpu.VMEM)
-    return pl.pallas_call(
-        copies_kernel,
-        out_shape=[jax.ShapeDtypeStruct(rows.shape, rows.dtype)] * len(early_masks),
-        in_specs=[whole] + [pl.BlockSpec(memory_space=pl.ANY)] * len(awaited),
-        out_specs=[whole] * len(early_masks),
-    )(rows, *awaited)
+    )(early_pick, late_pick, tokens, gated, *sent)
 
 
 def whole_weights(shard):
@@ -166,7 +179,7 @@
     own_blocks = [(0, 0, first, 0), (0, first, capacity, offset + first)]
     cross_blocks = [(s, 0, capacity, (s - 1) * capacity) for s in range(1, experts)]
     grads = summed_grads(attn_partials)
-    (early_own, late_own, *sent), picks = pack(
+    gated, picks, sent = pack_cross(
         own_blocks + cross_blocks,
         [first] + [rest] * experts,
         experts,
@@ -175,6 +188,7 @@
         tokens,
         grads,
     )
+    late_own, early_own, *early_copies = pack_own(picks[0], picks[1], tokens, gated, *sent)
 
     def activated(rows):
         expert_rows, grad_rows = rows[:, :width], rows[:, width:]
@@ -182,7 +196,7 @@
         hidden = gelu_value(pre_act).astype(jnp.bfloat16)
         hidden_grad = contract_cols(grad_rows, weights_out) * scale_out
         pre_grad = (hidden_grad * gelu_slope(pre_act)).astype(jnp.bfloat16)
-        return expert_rows, grad_rows, hidden, pre_grad
+        return [expert_rows, grad_rows, hidden, pre_grad]
 
     def input_parts(pre_grad):
         parts = jnp.dot(pre_grad, weights_in, preferred_element_type=jnp.float32) * scale_in
@@ -191,19 +205,19 @@
     for s in range(1, experts):
         late_own = late_own + shifted(sent[s - 1], s)
     early_x, early_y, early_z, early_xy = after(
-        [swap(rows, mask) for rows, mask in zip(early_copies(early_own, *sent), early_masks)], late_own
+        [swap(rows, mask) for rows, mask in zip(early_copies, early_masks)], late_own
     )
     late_x, late_y, late_z = swaps(
         [
             jnp.concatenate([late_own, early_z], axis=0),
             jnp.concatenate([late_own, early_z], axis=0),
-            late_own,
+            jnp.concatenate([late_own, early_xy], axis=0),
         ],
         (x_bit, y_bit, z_bit),
     )
-    early_zx, early_yz = late_x[rest:], late_y[rest:]
-    late_x, late_y = late_x[:rest], late_y[:rest]
-    early_rows = [early_own, early_x, early_y, early_z, early_xy, early_yz, early_zx]
+    early_zx, early_yz, early_far = late_x[rest:], late_y[rest:], late_z[rest:]
+    late_x, late_y, late_z = late_x[:rest], late_y[:rest], late_z[:rest]
+    early_rows = [early_own, early_x, early_y, early_z, early_xy, early_yz, early_zx, early_far]
 
     own_weights = jnp.concatenate([whole_weights(w_in).T, whole_weights(w_out).T], axis=0)
     their_weights = swap(after(own_weights, late_own), core_bit)
@@ -212,7 +226,7 @@
         for part in (slice(0, units), slice(units, 2 * units))
     ]
     late_far, late_zx, late_yz, late_xy = swaps(
-        [late_z, late_z, jnp.concatenate([late_y, early_xy], axis=0), late_x],
+        [late_z, late_z, late_y, late_x],
         (x_bit | y_bit, x_bit, z_bit, y_bit),
     )
     early = activated(jnp.concatenate(early_rows, axis=0))
@@ -227,14 +241,13 @@
         ]
 
     early_gradients = gradients(early)
-    late_rows = [late_own, late_x, late_y, late_z, late_xy, late_yz[:rest], late_zx, late_far]
-    late_rows = after([*late_rows, late_yz[rest:]], early_parts, early_gradients)
+    late_far = after([late_xy, late_yz, late_zx, late_far], early_parts, early_gradients)
+    late_rows = [late_own, late_x, late_y, late_z, *late_far]
     later = activated(jnp.concatenate(late_rows, axis=0))
     late_parts = input_parts(later[3])
-    late_parts, last_parts = late_parts[: 8 * rest], late_parts[8 * rest :]
     parts = [
         jnp.concatenate(pair, axis=0)
-        for pair in zip([*split_rows(early_parts, first), last_parts], split_rows(late_parts, rest))
+        for pair in zip(split_rows(early_parts, first), split_rows(late_parts, rest))
     ]
     own, sum_x, sum_y, sum_z, sum_xy, sum_yz, sum_zx, sum_far = parts
     far, zx, xy, yz = swaps(
@@ -243,7 +256,7 @@
     in_mine, in_theirs, out_mine, out_theirs = [
         sum(pair) * scale
         for pair, scale in zip(
-            zip(early_gradients, gradients(later)),
+            zip(early_gradients, gradients(later[:2] + after(later[2:], zx))),
             (scale_in, scale_in, scale_out, scale_out),
         )
     ]

time: 70.7 us -> 70.3 us (level)
  starting transfers between devices: 22.6 us -> 24.8 us
  waiting for transfers between devices: 21.7 us -> 19.6 us
  local copies, waits for them, and re-layouts: 2.97 us -> 2.18 us
    ppermute x2, starting transfers between devices: 4.52 us -> 6.88 us  [shifted(): return lax.ppermute(rows, 'expert', pairs)]
    ppermute x21, waiting for transfers between devices: 21.7 us -> 19.6 us  [swap(): lax.ppermute(rows, 'expert', [(i, i ^ mask) for i in range(n_expert)])]
    unnamed x28 -> x22, local copies, waits for them, and re-layouts: 2.37 us -> 1.77 us
  transfers between devices with their start and end apart: 23 -> 23, of which waited for: 10 -> 7; matrix products, arithmetic and copies ran while one was open for 21% -> 22% of each run, Pallas kernels for 2% -> 3%
where the time goes in v9:
time: 70.3 us; the launch traced here: 70.1 us
  starting transfers between devices  24.8 us (35%)
  waiting for transfers between devices  19.6 us (28%)
  matrix products  15.4 us (22%)
  Pallas kernels  4.38 us (6%)
  other arithmetic  2.66 us (4%)
  local copies, waits for them, and re-layouts  2.18 us (3%)
  between operations  1.08 us (2%)
    ppermute x21, waiting for transfers between devices, swap(): lax.ppermute(rows, 'expert', [(i, i ^ mask) for i in range(n_expert)])  19.6 us
    ppermute x21, starting transfers between devices, swap(): lax.ppermute(rows, 'expert', [(i, i ^ mask) for i in range(n_expert)])  18 us
    dot_general x11, matrix products, contract_rows(): lax.dot_general(left, right, (((0,), (0,)), ((), ())), preferred_element_...  9.67 us
    ppermute x2, starting transfers between devices, shifted(): return lax.ppermute(rows, 'expert', pairs)  6.88 us
    dot_general x4, matrix products, contract_cols(): lax.dot_general(left, right, (((1,), (1,)), ((), ())), preferred_element_...  4.33 us
    pallas_call x1, Pallas kernels, pack_cross(): pl.pallas_call(lambda *refs: cross_kernel(blocks, experts, *refs), out_sh...  2.22 us
    pallas_call x1, Pallas kernels, pack_own(): pl.pallas_call(own_kernel, out_shape=shapes, in_specs=[whole] * 4 + [pl.B...  2.16 us
    transpose x1, other arithmetic, shards(): whole_weights(w_in)  1.92 us
  transfers between devices with their start and end apart: 23, of which 7 were waited for; matrix products, arithmetic and copies ran while one was open for 22% of the time, Pallas kernels for 3%

profile of v9, /device:TPU:0, one launch (start us, length us, event | category | flops | bytes accessed | tf_op | source)
XLA Modules:
  0.0 70.1 jit_solution(13927974002419807393)
XLA Ops:
  0.6 2.2 %shard_map.85 = (bf16[64,2048]{1,0:T(8,128)(2,1)}, bf16[16,64]{1,0:T(8,128)(2,1)}, bf16[24,64]{1,0:T(8,128)(2,1)}, bf16[24,64]{1,0:T(8,128)(2,1)}, bf16[24,4096]{1,0:T(8,128)(2,1)}) custom-call(s32[1,64]{1,0:T(1,128)} %bitcast.22, f32[1,64]{1,0:T(1,128)} %bitcast.23, bf16[64,2048]{1,0:T(8,128)(2,1)} %tokens_ref.1, bf16[64,2048]{1,0:T(8,128)(2,1)} %bitcast.21), custom_call_target="tpu_custom_call" | custom-call | tf_op jit(solution)/shard_map/pallas_call | solution.py:86
  2.9 4.0 %collective-permute-start = (bf16[24,4096]{1,0:T(8,128)(2,1)}, bf16[24,4096]{1,0:T(8,128)(2,1)S(1)}, u32[]{:S(2)}, u32[]{:S(2)}) collective-permute-start(bf16[24,4096]{1,0:T(8,128)(2,1)} %get-tuple-element.39.refs_0_), channel_id=1, source_target_pairs={{0,16},{1,17},{2,18},{3,19},{4,20},{5,21},{6,22},{7,23},{8,24},{9,... | collective-permute-start | bytes 589832 | tf_op jit(solution)/shard_map/ppermute | solution.py:176
  6.9 2.2 %shard_map.86 = (bf16[24,4096]{1,0:T(8,128)(2,1)}, bf16[16,4096]{1,0:T(8,128)(2,1)}, bf16[16,4096]{1,0:T(8,128)(2,1)}, bf16[16,4096]{1,0:T(8,128)(2,1)}, bf16[16...) custom-call(bf16[16,64]{1,0:T(8,128)(2,1)} %get-tuple-element.36.early_pick_ref, ...), custom_call_target="tpu_custom_call" | custom-call | tf_op jit(solution)/shard_map/pallas_call | solution.py:113
  9.1 1.5 %collective-permute-start.1 = (bf16[16,4096]{1,0:T(8,128)(2,1)}, bf16[16,4096]{1,0:T(8,128)(2,1)S(1)}, u32[]{:S(2)}, u32[]{:S(2)}) collective-permute-start(bf16[16,4096]{1,0:T(8,128)(2,1)} %get-tuple-element.42), channel_id=1, source_target_pairs={{0,2},{1,3},{2,0},{3,1},{4,6},{5,7},{6,4},{7,5},{8,10},{9,11},{10,... | collective-permute-start | bytes 393224 | tf_op jit(solution)/shard_map/ppermute | solution.py:137
  10.5 1.5 %collective-permute-start.2 = (bf16[16,4096]{1,0:T(8,128)(2,1)}, bf16[16,4096]{1,0:T(8,128)(2,1)S(1)}, u32[]{:S(2)}, u32[]{:S(2)}) collective-permute-start(bf16[16,4096]{1,0:T(8,128)(2,1)} %get-tuple-element.43), channel_id=1, source_target_pairs={{0,4},{1,5},{2,6},{3,7},{4,0},{5,1},{6,2},{7,3},{8,12},{9,13},{10,... | collective-permute-start | bytes 393224 | tf_op jit(solution)/shard_map/ppermute | solution.py:137
  12.1 1.6 %collective-permute-start.3 = (bf16[16,4096]{1,0:T(8,128)(2,1)}, bf16[16,4096]{1,0:T(8,128)(2,1)S(1)}, u32[]{:S(2)}, u32[]{:S(2)}) collective-permute-start(bf16[16,4096]{1,0:T(8,128)(2,1)} %get-tuple-element.44), channel_id=1, source_target_pairs={{0,8},{1,9},{2,10},{3,11},{4,12},{5,13},{6,14},{7,15},{8,0},{9,1},... | collective-permute-start | bytes 393224 | tf_op jit(solution)/shard_map/ppermute | solution.py:137
  14.1 0.9 %constant_dynamic-update-slice_fusion.4 = bf16[128,4096]{1,0:T(8,128)(2,1)S(1)} fusion(bf16[16,4096]{1,0:T(8,128)(2,1)} %get-tuple-element.40), kind=kLoop, calls=%fused_computation.92 | loop fusion | bytes 262144
  15.0 1.9 %convert_bitcast_fusion = bf16[320,2048]{1,0:T(8,128)(2,1)S(1)} fusion(f32[2048,320]{0,1:T(8,128)} %param.10), kind=kLoop, calls=%fused_computation.30 | loop fusion | flops 655360 | bytes 3932160 | tf_op jit(solution)/shard_map/transpose | solution.py:222
  22.2 6.5 %collective-permute-done.6 = bf16[40,4096]{1,0:T(8,128)(2,1)S(1)} collective-permute-done((bf16[40,4096]{1,0:T(8,128)(2,1)S(1)}, bf16[40,4096]{1,0:T(8,128)(2,1)S(1)}, u32[]{:S(2)}, u32[]{:S(2)}) %collective-permute-start.6) | collective-permute-done | bytes 327712 | tf_op jit(solution)/shard_map/ppermute | solution.py:137
  29.5 2.3 %collective-permute-start.12 = (bf16[24,4096]{1,0:T(8,128)(2,1)S(1)}, bf16[24,4096]{1,0:T(8,128)(2,1)S(1)}, u32[]{:S(2)}, u32[]{:S(2)}) collective-permute-start(bf16[24,4096]{1,0:T(8,128)(2,1)S(1)} %get-tuple-element.53), channel_id=1, source_target_pairs={{0,6},{1,7},{2,4},{3,5},{4,2},{5,3},{6,0},{7,1},{8,14},{9,15},{10,... | collective-permute-start | bytes 589832 | tf_op jit(solution)/shard_map/ppermute | solution.py:137
  33.5 1.0 %multiply_convert_fusion.1 = (bf16[128,640]{1,0:T(8,128)(2,1)S(1)}, f32[128,640]{1,0:T(8,128)S(1)}) fusion(bf16[320,2048]{1,0:T(8,128)(2,1)S(1)} %convert_bitcast_fusion, bf16[320,2048]{1,0:T(8,128)(2,1)S(1)} %get-tuple-element.71, bf16[128,4096]{1,0:T(8,128)(2,1)S(1)} %slice_dynamic-update-slice_fusion), kind=kOutput, calls=%fused_computation.70 | convolution fusion | flops 341606400 | bytes 3637248 | tf_op jit(solution)/shard_map/dot_general | solution.py:39
  35.7 1.0 %fusion.24 = bf16[128,640]{1,0:T(8,128)(2,1)S(1)} fusion(bf16[320,2048]{1,0:T(8,128)(2,1)S(1)} %get-tuple-element.72, bf16[320,2048]{1,0:T(8,128)(2,1)S(1)} %convert_bitcast_fusion.1, bf16[128,4096]{1,0:T(8,128)(2,1)S(1)} %slice_dynamic-update-slice_fusion, f32[128,640]{1,0:T(8,128)S(1)} %get-tuple-element.98), kind=kOutput, calls=%fused_computation.37 | convolution fusion | flops 342507520 | bytes 3637248 | tf_op jit(solution)/shard_map/dot_general | solution.py:39
  38.4 1.5 %collective-permute-done.9 = bf16[24,4096]{1,0:T(8,128)(2,1)S(1)} collective-permute-done((bf16[24,4096]{1,0:T(8,128)(2,1)S(1)}, bf16[24,4096]{1,0:T(8,128)(2,1)S(1)}, u32[]{:S(2)}, u32[]{:S(2)}) %collective-permute-start.9) | collective-permute-done | bytes 196640 | tf_op jit(solution)/shard_map/ppermute | solution.py:137
  40.0 1.1 %multiply_convert_fusion = (bf16[192,640]{1,0:T(8,128)(2,1)S(1)}, f32[192,640]{1,0:T(8,128)S(1)}) fusion(bf16[320,2048]{1,0:T(8,128)(2,1)S(1)} %convert_bitcast_fusion, bf16[320,2048]{1,0:T(8,128)(2,1)S(1)} %get-tuple-element.71, bf16[192,4096]{1,0:T(8,128)(2,1)S(1)} %constant_dynamic-update-slice_fusion.5), kind=kOutput, calls=%fused_computation.48 | convolution fusion | flops 509788160 | bytes 4145152 | tf_op jit(solution)/shard_map/dot_general | solution.py:39
  41.2 1.2 %fusion.21 = bf16[192,640]{1,0:T(8,128)(2,1)S(1)} fusion(bf16[320,2048]{1,0:T(8,128)(2,1)S(1)} %get-tuple-element.72, bf16[320,2048]{1,0:T(8,128)(2,1)S(1)} %convert_bitcast_fusion.1, bf16[192,4096]{1,0:T(8,128)(2,1)S(1)} %constant_dynamic-update-slice_fusion.5, f32[192,640]{1,0:T(8,128)S(1)} %get-tuple-element.100), kind=kOutput, calls=%fused_computation.34 | convolution fusion | flops 511139840 | bytes 4145152 | tf_op jit(solution)/shard_map/dot_general | solution.py:39
  43.2 1.7 %collective-permute-start.14 = (bf16[40,2048]{1,0:T(8,128)(2,1)S(1)}, bf16[40,2048]{1,0:T(8,128)(2,1)S(1)}, u32[]{:S(2)}, u32[]{:S(2)}) collective-permute-start(bf16[40,2048]{1,0:T(8,128)(2,1)S(1)} %pad_maximum_fusion.19), channel_id=1, source_target_pairs={{0,6},{1,7},{2,4},{3,5},{4,2},{5,3},{6,0},{7,1},{8,14},{9,15},{10,... | collective-permute-start | bytes 491528 | tf_op jit(solution)/shard_map/ppermute | solution.py:137
  44.9 1.3 %collective-permute-start.13 = (bf16[40,2048]{1,0:T(8,128)(2,1)S(1)}, bf16[40,2048]{1,0:T(8,128)(2,1)S(1)}, u32[]{:S(2)}, u32[]{:S(2)}) collective-permute-start(bf16[40,2048]{1,0:T(8,128)(2,1)S(1)} %pad_maximum_fusion.20), channel_id=1, source_target_pairs={{0,2},{1,3},{2,0},{3,1},{4,6},{5,7},{6,4},{7,5},{8,10},{9,11},{10,... | collective-permute-start | bytes 491528 | tf_op jit(solution)/shard_map/ppermute | solution.py:137
  47.9 4.7 %collective-permute-done.13 = bf16[40,2048]{1,0:T(8,128)(2,1)S(1)} collective-permute-done((bf16[40,2048]{1,0:T(8,128)(2,1)S(1)}, bf16[40,2048]{1,0:T(8,128)(2,1)S(1)}, u32[]{:S(2)}, u32[]{:S(2)}) %collective-permute-start.13) | collective-permute-done | bytes 163872 | tf_op jit(solution)/shard_map/ppermute | solution.py:137
  53.5 1.3 %collective-permute-start.17 = (bf16[40,2048]{1,0:T(8,128)(2,1)S(1)}, bf16[40,2048]{1,0:T(8,128)(2,1)S(1)}, u32[]{:S(2)}, u32[]{:S(2)}) collective-permute-start(bf16[40,2048]{1,0:T(8,128)(2,1)S(1)} %add_convert_fusion.2), channel_id=1, source_target_pairs={{0,2},{1,3},{2,0},{3,1},{4,6},{5,7},{6,4},{7,5},{8,10},{9,11},{10,... | collective-permute-start | bytes 491528 | tf_op jit(solution)/shard_map/ppermute | solution.py:137
  56.3 4.7 %collective-permute-done.19 = bf16[40,2048]{1,0:T(8,128)(2,1)S(1)} collective-permute-done((bf16[40,2048]{1,0:T(8,128)(2,1)S(1)}, bf16[40,2048]{1,0:T(8,128)(2,1)S(1)}, u32[]{:S(2)}, u32[]{:S(2)}) %collective-permute-start.19) | collective-permute-done | bytes 163872 | tf_op jit(solution)/shard_map/ppermute | solution.py:137
  61.1 2.8 %collective-permute-start.22 = (bf16[24,2048]{1,0:T(8,128)(2,1)S(1)}, bf16[24,2048]{1,0:T(8,128)(2,1)S(1)}, u32[]{:S(2)}, u32[]{:S(2)}) collective-permute-start(bf16[24,2048]{1,0:T(8,128)(2,1)S(1)} %slice.185), channel_id=1, source_target_pairs={{0,16},{1,17},{2,18},{3,19},{4,20},{5,21},{6,22},{7,23},{8,24},{9,... | collective-permute-start | bytes 294920 | tf_op jit(solution)/shard_map/ppermute | solution.py:176
  64.4 2.4 %fusion.5 = f32[2048,320]{0,1:T(8,128)} fusion(f32[2048,320]{0,1:T(8,128)S(1)} %copy-done, f32[320,2048]{1,0:T(8,128)S(1)} %fusion.43, bf16[320,2048]{1,0:T(8,128)(2,1)S(1)} %collective-permute-done.21, bf16[192,4096]{1,0:T(8,128)(2,1)S(1)} %constant_dynamic-update-slice_fusion.5, bf16[192,640]{1,0:T(8,128)(2,1)S(1)} %get-tuple-element.67), kind=kOutput, calls=%fused_computation.9 | convolution fusion | flops 255590400 | bytes 10108928 | tf_op jit(solution)/shard_map/dot_general | solution.py:33
  66.8 2.3 %fusion.11 = f32[2048,320]{0,1:T(8,128)} fusion(f32[2048,320]{0,1:T(8,128)S(1)} %copy-done.1, f32[320,2048]{1,0:T(8,128)S(1)} %fusion.37, bf16[320,2048]{1,0:T(8,128)(2,1)S(1)} %collective-permute-done.20, bf16[192,4096]{1,0:T(8,128)(2,1)S(1)} %constant_dynamic-update-slice_fusion.5, bf16[192,640]{1,0:T(8,128)(2,1)S(1)} %fusion.21), kind=kOutput, calls=%fused_computation.17 | convolution fusion | flops 255590400 | bytes 10108928 | tf_op jit(solution)/shard_map/dot_general | solution.py:33
  69.1 1.0 %fusion.16 = bf16[64,2048]{1,0:T(8,128)(2,1)} fusion(f32[64,2048]{1,0:T(8,128)S(1)} %convolution_add_fusion.5, bf16[24,64]{1,0:T(8,128)(2,1)S(1)} %copy-done.5, bf16[24,2048]{1,0:T(8,128)(2,1)S(1)} %collective-permute-done.22), kind=kOutput, calls=%fused_computation.27 | convolution fusion | flops 6553600 | bytes 887808 | tf_op jit(solution)/shard_map/dot_general | solution.py:33
  (84 shorter events, 16.4 us)
Async XLA Ops:
  0.6 16.3 %copy-start = (f32[2048,320]{0,1:T(8,128)S(1)}, f32[2048,320]{0,1:T(8,128)}, u32[]{:S(2)}) copy-start(f32[2048,320]{0,1:T(8,128)} %param.11) | copy-start | bytes 7864324
  2.9 14.5 %collective-permute-start = (bf16[24,4096]{1,0:T(8,128)(2,1)}, bf16[24,4096]{1,0:T(8,128)(2,1)S(1)}, u32[]{:S(2)}, u32[]{:S(2)}) collective-permute-start(bf16[24,4096]{1,0:T(8,128)(2,1)} %get-tuple-element.39.refs_0_), channel_id=1, source_target_pairs={{0,16},{1,17},{2,18},{3,19},{4,20},{5,21},{6,22},{7,23},{8,24},{9,... | collective-permute-start | bytes 589832 | tf_op jit(solution)/shard_map/ppermute | solution.py:176
  9.1 9.1 %collective-permute-start.1 = (bf16[16,4096]{1,0:T(8,128)(2,1)}, bf16[16,4096]{1,0:T(8,128)(2,1)S(1)}, u32[]{:S(2)}, u32[]{:S(2)}) collective-permute-start(bf16[16,4096]{1,0:T(8,128)(2,1)} %get-tuple-element.42), channel_id=1, source_target_pairs={{0,2},{1,3},{2,0},{3,1},{4,6},{5,7},{6,4},{7,5},{8,10},{9,11},{10,... | collective-permute-start | bytes 393224 | tf_op jit(solution)/shard_map/ppermute | solution.py:137
  10.5 7.6 %collective-permute-start.2 = (bf16[16,4096]{1,0:T(8,128)(2,1)}, bf16[16,4096]{1,0:T(8,128)(2,1)S(1)}, u32[]{:S(2)}, u32[]{:S(2)}) collective-permute-start(bf16[16,4096]{1,0:T(8,128)(2,1)} %get-tuple-element.43), channel_id=1, source_target_pairs={{0,4},{1,5},{2,6},{3,7},{4,0},{5,1},{6,2},{7,3},{8,12},{9,13},{10,... | collective-permute-start | bytes 393224 | tf_op jit(solution)/shard_map/ppermute | solution.py:137
  12.1 7.0 %collective-permute-start.3 = (bf16[16,4096]{1,0:T(8,128)(2,1)}, bf16[16,4096]{1,0:T(8,128)(2,1)S(1)}, u32[]{:S(2)}, u32[]{:S(2)}) collective-permute-start(bf16[16,4096]{1,0:T(8,128)(2,1)} %get-tuple-element.44), channel_id=1, source_target_pairs={{0,8},{1,9},{2,10},{3,11},{4,12},{5,13},{6,14},{7,15},{8,0},{9,1},... | collective-permute-start | bytes 393224 | tf_op jit(solution)/shard_map/ppermute | solution.py:137
  13.6 6.1 %collective-permute-start.4 = (bf16[16,4096]{1,0:T(8,128)(2,1)}, bf16[16,4096]{1,0:T(8,128)(2,1)S(1)}, u32[]{:S(2)}, u32[]{:S(2)}) collective-permute-start(bf16[16,4096]{1,0:T(8,128)(2,1)} %get-tuple-element.45), channel_id=1, source_target_pairs={{0,6},{1,7},{2,4},{3,5},{4,2},{5,3},{6,0},{7,1},{8,14},{9,15},{10,... | collective-permute-start | bytes 393224 | tf_op jit(solution)/shard_map/ppermute | solution.py:137
  19.8 9.0 %collective-permute-start.6 = (bf16[40,4096]{1,0:T(8,128)(2,1)S(1)}, bf16[40,4096]{1,0:T(8,128)(2,1)S(1)}, u32[]{:S(2)}, u32[]{:S(2)}) collective-permute-start(bf16[40,4096]{1,0:T(8,128)(2,1)S(1)} %get-tuple-element.50), channel_id=1, source_target_pairs={{0,2},{1,3},{2,0},{3,1},{4,6},{5,7},{6,4},{7,5},{8,10},{9,11},{10,... | collective-permute-start | bytes 983048 | tf_op jit(solution)/shard_map/ppermute | solution.py:137
  20.4 9.0 %collective-permute-start.5 = (bf16[40,4096]{1,0:T(8,128)(2,1)S(1)}, bf16[40,4096]{1,0:T(8,128)(2,1)S(1)}, u32[]{:S(2)}, u32[]{:S(2)}) collective-permute-start(bf16[40,4096]{1,0:T(8,128)(2,1)S(1)} %get-tuple-element.50), channel_id=1, source_target_pairs={{0,4},{1,5},{2,6},{3,7},{4,0},{5,1},{6,2},{7,3},{8,12},{9,13},{10,... | collective-permute-start | bytes 983048 | tf_op jit(solution)/shard_map/ppermute | solution.py:137
  21.3 8.1 %collective-permute-start.7 = (bf16[40,4096]{1,0:T(8,128)(2,1)S(1)}, bf16[40,4096]{1,0:T(8,128)(2,1)S(1)}, u32[]{:S(2)}, u32[]{:S(2)}) collective-permute-start(bf16[40,4096]{1,0:T(8,128)(2,1)S(1)} %get-tuple-element.51), channel_id=1, source_target_pairs={{0,8},{1,9},{2,10},{3,11},{4,12},{5,13},{6,14},{7,15},{8,0},{9,1},... | collective-permute-start | bytes 983048 | tf_op jit(solution)/shard_map/ppermute | solution.py:137
  22.2 11.2 %collective-permute-start.8 = (bf16[640,2048]{1,0:T(8,128)(2,1)S(1)}, bf16[640,2048]{1,0:T(8,128)(2,1)S(1)}, u32[]{:S(2)}, u32[]{:S(2)}) collective-permute-start(bf16[640,2048]{1,0:T(8,128)(2,1)S(1)} %pad_maximum_fusion.1), channel_id=1, source_target_pairs={{0,1},{1,0},{2,3},{3,2},{4,5},{5,4},{6,7},{7,6},{8,9},{9,8},{10,11... | collective-permute-start | bytes 7864328 | tf_op jit(solution)/shard_map/ppermute | solution.py:137
  29.5 10.5 %collective-permute-start.12 = (bf16[24,4096]{1,0:T(8,128)(2,1)S(1)}, bf16[24,4096]{1,0:T(8,128)(2,1)S(1)}, u32[]{:S(2)}, u32[]{:S(2)}) collective-permute-start(bf16[24,4096]{1,0:T(8,128)(2,1)S(1)} %get-tuple-element.53), channel_id=1, source_target_pairs={{0,6},{1,7},{2,4},{3,5},{4,2},{5,3},{6,0},{7,1},{8,14},{9,15},{10,... | collective-permute-start | bytes 589832 | tf_op jit(solution)/shard_map/ppermute | solution.py:137
  31.8 8.1 %collective-permute-start.11 = (bf16[24,4096]{1,0:T(8,128)(2,1)S(1)}, bf16[24,4096]{1,0:T(8,128)(2,1)S(1)}, u32[]{:S(2)}, u32[]{:S(2)}) collective-permute-start(bf16[24,4096]{1,0:T(8,128)(2,1)S(1)} %get-tuple-element.53), channel_id=1, source_target_pairs={{0,2},{1,3},{2,0},{3,1},{4,6},{5,7},{6,4},{7,5},{8,10},{9,11},{10,... | collective-permute-start | bytes 589832 | tf_op jit(solution)/shard_map/ppermute | solution.py:137
  32.7 7.2 %collective-permute-start.10 = (bf16[24,4096]{1,0:T(8,128)(2,1)S(1)}, bf16[24,4096]{1,0:T(8,128)(2,1)S(1)}, u32[]{:S(2)}, u32[]{:S(2)}) collective-permute-start(bf16[24,4096]{1,0:T(8,128)(2,1)S(1)} %get-tuple-element.54), channel_id=1, source_target_pairs={{0,8},{1,9},{2,10},{3,11},{4,12},{5,13},{6,14},{7,15},{8,0},{9,1},... | collective-permute-start | bytes 589832 | tf_op jit(solution)/shard_map/ppermute | solution.py:137
  33.0 6.9 %collective-permute-start.9 = (bf16[24,4096]{1,0:T(8,128)(2,1)S(1)}, bf16[24,4096]{1,0:T(8,128)(2,1)S(1)}, u32[]{:S(2)}, u32[]{:S(2)}) collective-permute-start(bf16[24,4096]{1,0:T(8,128)(2,1)S(1)} %get-tuple-element.55), channel_id=1, source_target_pairs={{0,4},{1,5},{2,6},{3,7},{4,0},{5,1},{6,2},{7,3},{8,12},{9,13},{10,... | collective-permute-start | bytes 589832 | tf_op jit(solution)/shard_map/ppermute | solution.py:137
  43.2 10.1 %collective-permute-start.14 = (bf16[40,2048]{1,0:T(8,128)(2,1)S(1)}, bf16[40,2048]{1,0:T(8,128)(2,1)S(1)}, u32[]{:S(2)}, u32[]{:S(2)}) collective-permute-start(bf16[40,2048]{1,0:T(8,128)(2,1)S(1)} %pad_maximum_fusion.19), channel_id=1, source_target_pairs={{0,6},{1,7},{2,4},{3,5},{4,2},{5,3},{6,0},{7,1},{8,14},{9,15},{10,... | collective-permute-start | bytes 491528 | tf_op jit(solution)/shard_map/ppermute | solution.py:137
  44.9 7.6 %collective-permute-start.13 = (bf16[40,2048]{1,0:T(8,128)(2,1)S(1)}, bf16[40,2048]{1,0:T(8,128)(2,1)S(1)}, u32[]{:S(2)}, u32[]{:S(2)}) collective-permute-start(bf16[40,2048]{1,0:T(8,128)(2,1)S(1)} %pad_maximum_fusion.20), channel_id=1, source_target_pairs={{0,2},{1,3},{2,0},{3,1},{4,6},{5,7},{6,4},{7,5},{8,10},{9,11},{10,... | collective-permute-start | bytes 491528 | tf_op jit(solution)/shard_map/ppermute | solution.py:137
  46.3 7.2 %collective-permute-start.16 = (bf16[40,2048]{1,0:T(8,128)(2,1)S(1)}, bf16[40,2048]{1,0:T(8,128)(2,1)S(1)}, u32[]{:S(2)}, u32[]{:S(2)}) collective-permute-start(bf16[40,2048]{1,0:T(8,128)(2,1)S(1)} %get-tuple-element.61), channel_id=1, source_target_pairs={{0,4},{1,5},{2,6},{3,7},{4,0},{5,1},{6,2},{7,3},{8,12},{9,13},{10,... | collective-permute-start | bytes 491528 | tf_op jit(solution)/shard_map/ppermute | solution.py:137
  47.0 7.8 %collective-permute-start.18 = (bf16[40,2048]{1,0:T(8,128)(2,1)S(1)}, bf16[40,2048]{1,0:T(8,128)(2,1)S(1)}, u32[]{:S(2)}, u32[]{:S(2)}) collective-permute-start(bf16[40,2048]{1,0:T(8,128)(2,1)S(1)} %get-tuple-element.63), channel_id=1, source_target_pairs={{0,8},{1,9},{2,10},{3,11},{4,12},{5,13},{6,14},{7,15},{8,0},{9,1},... | collective-permute-start | bytes 491528 | tf_op jit(solution)/shard_map/ppermute | solution.py:137
  53.2 11.2 %collective-permute-start.21 = (bf16[320,2048]{1,0:T(8,128)(2,1)S(1)}, bf16[320,2048]{1,0:T(8,128)(2,1)S(1)}, u32[]{:S(2)}, u32[]{:S(2)}) collective-permute-start(bf16[320,2048]{1,0:T(8,128)(2,1)S(1)} %fusion.13), channel_id=1, source_target_pairs={{0,1},{1,0},{2,3},{3,2},{4,5},{5,4},{6,7},{7,6},{8,9},{9,8},{10,11... | collective-permute-start | bytes 3932168 | tf_op jit(solution)/shard_map/ppermute | solution.py:137
  53.4 7.6 %collective-permute-start.15 = (bf16[40,2048]{1,0:T(8,128)(2,1)S(1)}, bf16[40,2048]{1,0:T(8,128)(2,1)S(1)}, u32[]{:S(2)}, u32[]{:S(2)}) collective-permute-start(bf16[40,2048]{1,0:T(8,128)(2,1)S(1)} %add_convert_fusion.3), channel_id=1, source_target_pairs={{0,8},{1,9},{2,10},{3,11},{4,12},{5,13},{6,14},{7,15},{8,0},{9,1},... | collective-permute-start | bytes 491528 | tf_op jit(solution)/shard_map/ppermute | solution.py:137
  53.5 7.4 %collective-permute-start.17 = (bf16[40,2048]{1,0:T(8,128)(2,1)S(1)}, bf16[40,2048]{1,0:T(8,128)(2,1)S(1)}, u32[]{:S(2)}, u32[]{:S(2)}) collective-permute-start(bf16[40,2048]{1,0:T(8,128)(2,1)S(1)} %add_convert_fusion.2), channel_id=1, source_target_pairs={{0,2},{1,3},{2,0},{3,1},{4,6},{5,7},{6,4},{7,5},{8,10},{9,11},{10,... | collective-permute-start | bytes 491528 | tf_op jit(solution)/shard_map/ppermute | solution.py:137
  54.9 6.1 %collective-permute-start.19 = (bf16[40,2048]{1,0:T(8,128)(2,1)S(1)}, bf16[40,2048]{1,0:T(8,128)(2,1)S(1)}, u32[]{:S(2)}, u32[]{:S(2)}) collective-permute-start(bf16[40,2048]{1,0:T(8,128)(2,1)S(1)} %add_convert_fusion.1), channel_id=1, source_target_pairs={{0,4},{1,5},{2,6},{3,7},{4,0},{5,1},{6,2},{7,3},{8,12},{9,13},{10,... | collective-permute-start | bytes 491528 | tf_op jit(solution)/shard_map/ppermute | solution.py:137
  56.2 10.6 %collective-permute-start.20 = (bf16[320,2048]{1,0:T(8,128)(2,1)S(1)}, bf16[320,2048]{1,0:T(8,128)(2,1)S(1)}, u32[]{:S(2)}, u32[]{:S(2)}) collective-permute-start(bf16[320,2048]{1,0:T(8,128)(2,1)S(1)} %fusion.12), channel_id=1, source_target_pairs={{0,1},{1,0},{2,3},{3,2},{4,5},{5,4},{6,7},{7,6},{8,9},{9,8},{10,11... | collective-permute-start | bytes 3932168 | tf_op jit(solution)/shard_map/ppermute | solution.py:137
  61.1 8.1 %collective-permute-start.22 = (bf16[24,2048]{1,0:T(8,128)(2,1)S(1)}, bf16[24,2048]{1,0:T(8,128)(2,1)S(1)}, u32[]{:S(2)}, u32[]{:S(2)}) collective-permute-start(bf16[24,2048]{1,0:T(8,128)(2,1)S(1)} %slice.185), channel_id=1, source_target_pairs={{0,16},{1,17},{2,18},{3,19},{4,20},{5,21},{6,22},{7,23},{8,24},{9,... | collective-permute-start | bytes 294920 | tf_op jit(solution)/shard_map/ppermute | solution.py:176
  (5 other events, 24.0 us)

commit v10 on v9

--- a/solution.py
+++ b/solution.py
@@ -139,6 +139,7 @@
 
 core_bit, x_bit, y_bit, z_bit = 1, 2, 4, 8
 early_masks = (x_bit, y_bit, z_bit, x_bit | y_bit)
+back_masks = (14, 12, 10, 6, 2, 4, 8)
 
 
 def after(values, *others):
@@ -245,18 +246,26 @@
     late_rows = [late_own, late_x, late_y, late_z, *late_far]
     later = activated(jnp.concatenate(late_rows, axis=0))
     late_parts = input_parts(later[3])
-    parts = [
-        jnp.concatenate(pair, axis=0)
-        for pair in zip(split_rows(early_parts, first), split_rows(late_parts, rest))
-    ]
-    own, sum_x, sum_y, sum_z, sum_xy, sum_yz, sum_zx, sum_far = parts
-    far, zx, xy, yz = swaps(
-        [sum_far, sum_zx, sum_xy, sum_yz], (x_bit | y_bit, x_bit, y_bit, z_bit)
-    )
+    early_parts, late_parts = split_rows(early_parts, first), split_rows(late_parts, rest)
+    back = swaps(
+        [
+            late_parts[7],
+            late_parts[5],
+            late_parts[6],
+            jnp.concatenate([late_parts[4], early_parts[7]], axis=0),
+            jnp.concatenate([late_parts[1], early_parts[6]], axis=0),
+            jnp.concatenate([late_parts[2], early_parts[4]], axis=0),
+            jnp.concatenate([late_parts[3], early_parts[5]], axis=0),
+        ],
+        back_masks,
+    )
+    far, zx, xy, yz = [rows[rest:] for rows in back[3:]]
+    late_sum = total(late_parts[0], *[rows[:rest] for rows in back])
+    crossed = [shifted(late_sum, -s) for s in range(1, experts)]
     in_mine, in_theirs, out_mine, out_theirs = [
         sum(pair) * scale
         for pair, scale in zip(
-            zip(early_gradients, gradients(later[:2] + after(later[2:], zx))),
+            zip(early_gradients, gradients(later[:2] + after(later[2:], back[0]))),
             (scale_in, scale_in, scale_out, scale_out),
         )
     ]
@@ -264,13 +273,13 @@
     out_shared = swap(out_theirs.astype(jnp.bfloat16), core_bit).astype(jnp.float32)
     new_w_in = stepped(w_in, (in_mine + in_shared).T)
     new_w_out = stepped(w_out, (out_mine + out_shared).T)
-    near = swaps(
-        [total(sum_z, zx, far), total(sum_x, xy), total(sum_y, yz)], (z_bit, x_bit, y_bit)
-    )
-    sums = total(own, *near)
-    early_sum, late_sum = sums[:first], sums[first:]
-    crossed = [shifted(late_sum, -s) for s in range(1, experts)]
-
+    near = [
+        total(early_parts[3], zx, far),
+        total(early_parts[1], xy),
+        total(early_parts[2], yz),
+    ]
+    near = swaps(after(near, late_sum), (z_bit, x_bit, y_bit))
+    early_sum = total(early_parts[0], *near)
     crossed = after(crossed, new_w_in, new_w_out)
     returned = [early_sum, late_sum, *crossed]
     token_grad = sum(contract_rows(pick, rows) for pick, rows in zip(picks, returned))

time: 70.3 us -> 71 us (level)
  starting transfers between devices: 24.8 us -> 31.1 us
  waiting for transfers between devices: 19.6 us -> 14.2 us
    ppermute x21 -> x24, starting transfers between devices: 18 us -> 25 us  [swap(): lax.ppermute(rows, 'expert', [(i, i ^ mask) for i in range(n_expert)])]
    ppermute x21 -> x24, waiting for transfers between devices: 19.6 us -> 14.2 us  [swap(): lax.ppermute(rows, 'expert', [(i, i ^ mask) for i in range(n_expert)])]
    ppermute x2, starting transfers between devices: 6.88 us -> 6.12 us  [shifted(): return lax.ppermute(rows, 'expert', pairs)]
  transfers between devices with their start and end apart: 23 -> 26, of which waited for: 7 -> 9; matrix products, arithmetic and copies ran while one was open for 22% -> 21% of each run, Pallas kernels for 3% -> 3%
where the time goes in v10:
time: 71 us; the launch traced here: 70.8 us
  starting transfers between devices  31.1 us (44%)
  matrix products  15.4 us (22%)
  waiting for transfers between devices  14.2 us (20%)
  Pallas kernels  4.38 us (6%)
  other arithmetic  2.59 us (4%)
  local copies, waits for them, and re-layouts  2.13 us (3%)
  between operations  0.99 us (1%)
    ppermute x24, starting transfers between devices, swap(): lax.ppermute(rows, 'expert', [(i, i ^ mask) for i in range(n_expert)])  25 us
    ppermute x24, waiting for transfers between devices, swap(): lax.ppermute(rows, 'expert', [(i, i ^ mask) for i in range(n_expert)])  14.2 us
    dot_general x11, matrix products, contract_rows(): lax.dot_general(left, right, (((0,), (0,)), ((), ())), preferred_element_...  9.66 us
    ppermute x2, starting transfers between devices, shifted(): return lax.ppermute(rows, 'expert', pairs)  6.12 us
    dot_general x4, matrix products, contract_cols(): lax.dot_general(left, right, (((1,), (1,)), ((), ())), preferred_element_...  4.33 us
    pallas_call x1, Pallas kernels, pack_cross(): pl.pallas_call(lambda *refs: cross_kernel(blocks, experts, *refs), out_sh...  2.22 us
    pallas_call x1, Pallas kernels, pack_own(): pl.pallas_call(own_kernel, out_shape=shapes, in_specs=[whole] * 4 + [pl.B...  2.16 us
    transpose x1, other arithmetic, shards(): whole_weights(w_in)  1.92 us
  transfers between devices with their start and end apart: 26, of which 9 were waited for; matrix products, arithmetic and copies ran while one was open for 21% of the time, Pallas kernels for 3%

profile of v10, /device:TPU:0, one launch (start us, length us, event | category | flops | bytes accessed | tf_op | source)
XLA Modules:
  0.0 70.8 jit_solution(8253634634034599390)
XLA Ops:
  0.6 2.2 %shard_map.85 = (bf16[64,2048]{1,0:T(8,128)(2,1)}, bf16[16,64]{1,0:T(8,128)(2,1)}, bf16[24,64]{1,0:T(8,128)(2,1)}, bf16[24,64]{1,0:T(8,128)(2,1)}, bf16[24,4096]{1,0:T(8,128)(2,1)}) custom-call(s32[1,64]{1,0:T(1,128)} %bitcast.23, f32[1,64]{1,0:T(1,128)} %bitcast.24, bf16[64,2048]{1,0:T(8,128)(2,1)} %tokens_ref.1, bf16[64,2048]{1,0:T(8,128)(2,1)} %bitcast.22), custom_call_target="tpu_custom_call" | custom-call | tf_op jit(solution)/shard_map/pallas_call | solution.py:86
  2.9 4.0 %collective-permute-start = (bf16[24,4096]{1,0:T(8,128)(2,1)}, bf16[24,4096]{1,0:T(8,128)(2,1)S(1)}, u32[]{:S(2)}, u32[]{:S(2)}) collective-permute-start(bf16[24,4096]{1,0:T(8,128)(2,1)} %get-tuple-element.45.refs_0_), channel_id=1, source_target_pairs={{0,16},{1,17},{2,18},{3,19},{4,20},{5,21},{6,22},{7,23},{8,24},{9,... | collective-permute-start | bytes 589832 | tf_op jit(solution)/shard_map/ppermute | solution.py:177
  6.9 2.2 %shard_map.86 = (bf16[24,4096]{1,0:T(8,128)(2,1)}, bf16[16,4096]{1,0:T(8,128)(2,1)}, bf16[16,4096]{1,0:T(8,128)(2,1)}, bf16[16,4096]{1,0:T(8,128)(2,1)}, bf16[16...) custom-call(bf16[16,64]{1,0:T(8,128)(2,1)} %get-tuple-element.42.early_pick_ref, ...), custom_call_target="tpu_custom_call" | custom-call | tf_op jit(solution)/shard_map/pallas_call | solution.py:113
  9.1 1.5 %collective-permute-start.1 = (bf16[16,4096]{1,0:T(8,128)(2,1)}, bf16[16,4096]{1,0:T(8,128)(2,1)S(1)}, u32[]{:S(2)}, u32[]{:S(2)}) collective-permute-start(bf16[16,4096]{1,0:T(8,128)(2,1)} %get-tuple-element.48), channel_id=1, source_target_pairs={{0,2},{1,3},{2,0},{3,1},{4,6},{5,7},{6,4},{7,5},{8,10},{9,11},{10,... | collective-permute-start | bytes 393224 | tf_op jit(solution)/shard_map/ppermute | solution.py:137
  10.5 1.5 %collective-permute-start.2 = (bf16[16,4096]{1,0:T(8,128)(2,1)}, bf16[16,4096]{1,0:T(8,128)(2,1)S(1)}, u32[]{:S(2)}, u32[]{:S(2)}) collective-permute-start(bf16[16,4096]{1,0:T(8,128)(2,1)} %get-tuple-element.49), channel_id=1, source_target_pairs={{0,4},{1,5},{2,6},{3,7},{4,0},{5,1},{6,2},{7,3},{8,12},{9,13},{10,... | collective-permute-start | bytes 393224 | tf_op jit(solution)/shard_map/ppermute | solution.py:137
  12.1 1.6 %collective-permute-start.3 = (bf16[16,4096]{1,0:T(8,128)(2,1)}, bf16[16,4096]{1,0:T(8,128)(2,1)S(1)}, u32[]{:S(2)}, u32[]{:S(2)}) collective-permute-start(bf16[16,4096]{1,0:T(8,128)(2,1)} %get-tuple-element.50), channel_id=1, source_target_pairs={{0,8},{1,9},{2,10},{3,11},{4,12},{5,13},{6,14},{7,15},{8,0},{9,1},... | collective-permute-start | bytes 393224 | tf_op jit(solution)/shard_map/ppermute | solution.py:137
  15.0 1.9 %convert_bitcast_fusion = bf16[320,2048]{1,0:T(8,128)(2,1)S(1)} fusion(f32[2048,320]{0,1:T(8,128)} %param.10), kind=kLoop, calls=%fused_computation.30 | loop fusion | flops 655360 | bytes 3932160 | tf_op jit(solution)/shard_map/transpose | solution.py:223
  22.2 6.6 %collective-permute-done.6 = bf16[40,4096]{1,0:T(8,128)(2,1)S(1)} collective-permute-done((bf16[40,4096]{1,0:T(8,128)(2,1)S(1)}, bf16[40,4096]{1,0:T(8,128)(2,1)S(1)}, u32[]{:S(2)}, u32[]{:S(2)}) %collective-permute-start.6) | collective-permute-done | bytes 327712 | tf_op jit(solution)/shard_map/ppermute | solution.py:137
  29.6 2.3 %collective-permute-start.12 = (bf16[24,4096]{1,0:T(8,128)(2,1)S(1)}, bf16[24,4096]{1,0:T(8,128)(2,1)S(1)}, u32[]{:S(2)}, u32[]{:S(2)}) collective-permute-start(bf16[24,4096]{1,0:T(8,128)(2,1)S(1)} %get-tuple-element.59), channel_id=1, source_target_pairs={{0,6},{1,7},{2,4},{3,5},{4,2},{5,3},{6,0},{7,1},{8,14},{9,15},{10,... | collective-permute-start | bytes 589832 | tf_op jit(solution)/shard_map/ppermute | solution.py:137
  38.6 1.4 %collective-permute-done.9 = bf16[24,4096]{1,0:T(8,128)(2,1)S(1)} collective-permute-done((bf16[24,4096]{1,0:T(8,128)(2,1)S(1)}, bf16[24,4096]{1,0:T(8,128)(2,1)S(1)}, u32[]{:S(2)}, u32[]{:S(2)}) %collective-permute-start.9) | collective-permute-done | bytes 196640 | tf_op jit(solution)/shard_map/ppermute | solution.py:137
  40.2 1.1 %multiply_convert_fusion = (bf16[192,640]{1,0:T(8,128)(2,1)S(1)}, f32[192,640]{1,0:T(8,128)S(1)}) fusion(bf16[320,2048]{1,0:T(8,128)(2,1)S(1)} %convert_bitcast_fusion, bf16[320,2048]{1,0:T(8,128)(2,1)S(1)} %get-tuple-element.83, bf16[192,4096]{1,0:T(8,128)(2,1)S(1)} %constant_dynamic-update-slice_fusion.5), kind=kOutput, calls=%fused_computation.48 | convolution fusion | flops 509788160 | bytes 4145152 | tf_op jit(solution)/shard_map/dot_general | solution.py:39
  41.3 1.2 %fusion.22 = bf16[192,640]{1,0:T(8,128)(2,1)S(1)} fusion(bf16[320,2048]{1,0:T(8,128)(2,1)S(1)} %get-tuple-element.84, bf16[320,2048]{1,0:T(8,128)(2,1)S(1)} %convert_bitcast_fusion.1, bf16[192,4096]{1,0:T(8,128)(2,1)S(1)} %constant_dynamic-update-slice_fusion.5, f32[192,640]{1,0:T(8,128)S(1)} %get-tuple-element.110), kind=kOutput, calls=%fused_computation.34 | convolution fusion | flops 511139840 | bytes 4145152 | tf_op jit(solution)/shard_map/dot_general | solution.py:39
  43.3 2.1 %collective-permute-start.13 = (bf16[24,2048]{1,0:T(8,128)(2,1)S(1)}, bf16[24,2048]{1,0:T(8,128)(2,1)S(1)}, u32[]{:S(2)}, u32[]{:S(2)}) collective-permute-start(bf16[24,2048]{1,0:T(8,128)(2,1)S(1)} %get-tuple-element.91), channel_id=1, source_target_pairs={{0,14},{1,15},{2,12},{3,13},{4,10},{5,11},{6,8},{7,9},{8,6},{9,7},... | collective-permute-start | bytes 294920 | tf_op jit(solution)/shard_map/ppermute | solution.py:137
  45.4 1.6 %collective-permute-start.14 = (bf16[24,2048]{1,0:T(8,128)(2,1)S(1)}, bf16[24,2048]{1,0:T(8,128)(2,1)S(1)}, u32[]{:S(2)}, u32[]{:S(2)}) collective-permute-start(bf16[24,2048]{1,0:T(8,128)(2,1)S(1)} %get-tuple-element.66), channel_id=1, source_target_pairs={{0,12},{1,13},{2,14},{3,15},{4,8},{5,9},{6,10},{7,11},{8,4},{9,5},... | collective-permute-start | bytes 294920 | tf_op jit(solution)/shard_map/ppermute | solution.py:137
  47.0 1.1 %collective-permute-start.15 = (bf16[24,2048]{1,0:T(8,128)(2,1)S(1)}, bf16[24,2048]{1,0:T(8,128)(2,1)S(1)}, u32[]{:S(2)}, u32[]{:S(2)}) collective-permute-start(bf16[24,2048]{1,0:T(8,128)(2,1)S(1)} %get-tuple-element.67), channel_id=1, source_target_pairs={{0,10},{1,11},{2,8},{3,9},{4,14},{5,15},{6,12},{7,13},{8,2},{9,3},... | collective-permute-start | bytes 294920 | tf_op jit(solution)/shard_map/ppermute | solution.py:137
  49.2 1.3 %collective-permute-start.18 = (bf16[40,2048]{1,0:T(8,128)(2,1)S(1)}, bf16[40,2048]{1,0:T(8,128)(2,1)S(1)}, u32[]{:S(2)}, u32[]{:S(2)}) collective-permute-start(bf16[40,2048]{1,0:T(8,128)(2,1)S(1)} %get-tuple-element.70), channel_id=1, source_target_pairs={{0,4},{1,5},{2,6},{3,7},{4,0},{5,1},{6,2},{7,3},{8,12},{9,13},{10,... | collective-permute-start | bytes 491528 | tf_op jit(solution)/shard_map/ppermute | solution.py:137
  50.9 1.3 %collective-permute-start.16 = (bf16[40,2048]{1,0:T(8,128)(2,1)S(1)}, bf16[40,2048]{1,0:T(8,128)(2,1)S(1)}, u32[]{:S(2)}, u32[]{:S(2)}) collective-permute-start(bf16[40,2048]{1,0:T(8,128)(2,1)S(1)} %get-tuple-element.68), channel_id=1, source_target_pairs={{0,6},{1,7},{2,4},{3,5},{4,2},{5,3},{6,0},{7,1},{8,14},{9,15},{10,... | collective-permute-start | bytes 491528 | tf_op jit(solution)/shard_map/ppermute | solution.py:137
  52.9 1.6 %collective-permute-start.19 = (bf16[40,2048]{1,0:T(8,128)(2,1)S(1)}, bf16[40,2048]{1,0:T(8,128)(2,1)S(1)}, u32[]{:S(2)}, u32[]{:S(2)}) collective-permute-start(bf16[40,2048]{1,0:T(8,128)(2,1)S(1)} %get-tuple-element.71), channel_id=1, source_target_pairs={{0,8},{1,9},{2,10},{3,11},{4,12},{5,13},{6,14},{7,15},{8,0},{9,1},... | collective-permute-start | bytes 491528 | tf_op jit(solution)/shard_map/ppermute | solution.py:137
  55.2 3.0 %collective-permute-done.19 = bf16[40,2048]{1,0:T(8,128)(2,1)S(1)} collective-permute-done((bf16[40,2048]{1,0:T(8,128)(2,1)S(1)}, bf16[40,2048]{1,0:T(8,128)(2,1)S(1)}, u32[]{:S(2)}, u32[]{:S(2)}) %collective-permute-start.19) | collective-permute-done | bytes 163872 | tf_op jit(solution)/shard_map/ppermute | solution.py:137
  58.8 2.1 %collective-permute-start.25 = (bf16[24,2048]{1,0:T(8,128)(2,1)S(1)}, bf16[24,2048]{1,0:T(8,128)(2,1)S(1)}, u32[]{:S(2)}, u32[]{:S(2)}) collective-permute-start(bf16[24,2048]{1,0:T(8,128)(2,1)S(1)} %add_convert_fusion), channel_id=1, source_target_pairs={{0,16},{1,17},{2,18},{3,19},{4,20},{5,21},{6,22},{7,23},{8,24},{9,... | collective-permute-start | bytes 294920 | tf_op jit(solution)/shard_map/ppermute | solution.py:177
  60.9 1.9 %collective-permute-start.20 = (bf16[16,2048]{1,0:T(8,128)(2,1)S(1)}, bf16[16,2048]{1,0:T(8,128)(2,1)S(1)}, u32[]{:S(2)}, u32[]{:S(2)}) collective-permute-start(bf16[16,2048]{1,0:T(8,128)(2,1)S(1)} %get-tuple-element.72), channel_id=1, source_target_pairs={{0,8},{1,9},{2,10},{3,11},{4,12},{5,13},{6,14},{7,15},{8,0},{9,1},... | collective-permute-start | bytes 196616 | tf_op jit(solution)/shard_map/ppermute | solution.py:137
  63.1 1.7 %collective-permute-start.22 = (bf16[16,2048]{1,0:T(8,128)(2,1)S(1)}, bf16[16,2048]{1,0:T(8,128)(2,1)S(1)}, u32[]{:S(2)}, u32[]{:S(2)}) collective-permute-start(bf16[16,2048]{1,0:T(8,128)(2,1)S(1)} %get-tuple-element.76), channel_id=1, source_target_pairs={{0,4},{1,5},{2,6},{3,7},{4,0},{5,1},{6,2},{7,3},{8,12},{9,13},{10,... | collective-permute-start | bytes 196616 | tf_op jit(solution)/shard_map/ppermute | solution.py:137
  64.8 2.3 %fusion.11 = f32[2048,320]{0,1:T(8,128)} fusion(f32[2048,320]{0,1:T(8,128)S(1)} %copy-done, f32[320,2048]{1,0:T(8,128)S(1)} %fusion.38, bf16[320,2048]{1,0:T(8,128)(2,1)S(1)} %collective-permute-done.23, bf16[192,4096]{1,0:T(8,128)(2,1)S(1)} %constant_dynamic-update-slice_fusion.5, bf16[192,640]{1,0:T(8,128)(2,1)S(1)} %fusion.22), kind=kOutput, calls=%fused_computation.17 | convolution fusion | flops 255590400 | bytes 10108928 | tf_op jit(solution)/shard_map/dot_general | solution.py:33
  67.1 2.4 %fusion.5 = f32[2048,320]{0,1:T(8,128)} fusion(f32[2048,320]{0,1:T(8,128)S(1)} %copy-done.1, f32[320,2048]{1,0:T(8,128)S(1)} %fusion.44, bf16[320,2048]{1,0:T(8,128)(2,1)S(1)} %collective-permute-done.24, bf16[192,4096]{1,0:T(8,128)(2,1)S(1)} %constant_dynamic-update-slice_fusion.5, bf16[192,640]{1,0:T(8,128)(2,1)S(1)} %get-tuple-element.79), kind=kOutput, calls=%fused_computation.9 | convolution fusion | flops 255590400 | bytes 10108928 | tf_op jit(solution)/shard_map/dot_general | solution.py:33
  (86 shorter events, 19.9 us)
Async XLA Ops:
  2.9 14.5 %collective-permute-start = (bf16[24,4096]{1,0:T(8,128)(2,1)}, bf16[24,4096]{1,0:T(8,128)(2,1)S(1)}, u32[]{:S(2)}, u32[]{:S(2)}) collective-permute-start(bf16[24,4096]{1,0:T(8,128)(2,1)} %get-tuple-element.45.refs_0_), channel_id=1, source_target_pairs={{0,16},{1,17},{2,18},{3,19},{4,20},{5,21},{6,22},{7,23},{8,24},{9,... | collective-permute-start | bytes 589832 | tf_op jit(solution)/shard_map/ppermute | solution.py:177
  9.1 9.1 %collective-permute-start.1 = (bf16[16,4096]{1,0:T(8,128)(2,1)}, bf16[16,4096]{1,0:T(8,128)(2,1)S(1)}, u32[]{:S(2)}, u32[]{:S(2)}) collective-permute-start(bf16[16,4096]{1,0:T(8,128)(2,1)} %get-tuple-element.48), channel_id=1, source_target_pairs={{0,2},{1,3},{2,0},{3,1},{4,6},{5,7},{6,4},{7,5},{8,10},{9,11},{10,... | collective-permute-start | bytes 393224 | tf_op jit(solution)/shard_map/ppermute | solution.py:137
  10.5 7.6 %collective-permute-start.2 = (bf16[16,4096]{1,0:T(8,128)(2,1)}, bf16[16,4096]{1,0:T(8,128)(2,1)S(1)}, u32[]{:S(2)}, u32[]{:S(2)}) collective-permute-start(bf16[16,4096]{1,0:T(8,128)(2,1)} %get-tuple-element.49), channel_id=1, source_target_pairs={{0,4},{1,5},{2,6},{3,7},{4,0},{5,1},{6,2},{7,3},{8,12},{9,13},{10,... | collective-permute-start | bytes 393224 | tf_op jit(solution)/shard_map/ppermute | solution.py:137
  12.1 7.0 %collective-permute-start.3 = (bf16[16,4096]{1,0:T(8,128)(2,1)}, bf16[16,4096]{1,0:T(8,128)(2,1)S(1)}, u32[]{:S(2)}, u32[]{:S(2)}) collective-permute-start(bf16[16,4096]{1,0:T(8,128)(2,1)} %get-tuple-element.50), channel_id=1, source_target_pairs={{0,8},{1,9},{2,10},{3,11},{4,12},{5,13},{6,14},{7,15},{8,0},{9,1},... | collective-permute-start | bytes 393224 | tf_op jit(solution)/shard_map/ppermute | solution.py:137
  13.6 6.1 %collective-permute-start.4 = (bf16[16,4096]{1,0:T(8,128)(2,1)}, bf16[16,4096]{1,0:T(8,128)(2,1)S(1)}, u32[]{:S(2)}, u32[]{:S(2)}) collective-permute-start(bf16[16,4096]{1,0:T(8,128)(2,1)} %get-tuple-element.51), channel_id=1, source_target_pairs={{0,6},{1,7},{2,4},{3,5},{4,2},{5,3},{6,0},{7,1},{8,14},{9,15},{10,... | collective-permute-start | bytes 393224 | tf_op jit(solution)/shard_map/ppermute | solution.py:137
  19.8 9.0 %collective-permute-start.6 = (bf16[40,4096]{1,0:T(8,128)(2,1)S(1)}, bf16[40,4096]{1,0:T(8,128)(2,1)S(1)}, u32[]{:S(2)}, u32[]{:S(2)}) collective-permute-start(bf16[40,4096]{1,0:T(8,128)(2,1)S(1)} %get-tuple-element.56), channel_id=1, source_target_pairs={{0,2},{1,3},{2,0},{3,1},{4,6},{5,7},{6,4},{7,5},{8,10},{9,11},{10,... | collective-permute-start | bytes 983048 | tf_op jit(solution)/shard_map/ppermute | solution.py:137
  20.5 9.1 %collective-permute-start.5 = (bf16[40,4096]{1,0:T(8,128)(2,1)S(1)}, bf16[40,4096]{1,0:T(8,128)(2,1)S(1)}, u32[]{:S(2)}, u32[]{:S(2)}) collective-permute-start(bf16[40,4096]{1,0:T(8,128)(2,1)S(1)} %get-tuple-element.56), channel_id=1, source_target_pairs={{0,4},{1,5},{2,6},{3,7},{4,0},{5,1},{6,2},{7,3},{8,12},{9,13},{10,... | collective-permute-start | bytes 983048 | tf_op jit(solution)/shard_map/ppermute | solution.py:137
  21.4 8.2 %collective-permute-start.7 = (bf16[40,4096]{1,0:T(8,128)(2,1)S(1)}, bf16[40,4096]{1,0:T(8,128)(2,1)S(1)}, u32[]{:S(2)}, u32[]{:S(2)}) collective-permute-start(bf16[40,4096]{1,0:T(8,128)(2,1)S(1)} %get-tuple-element.57), channel_id=1, source_target_pairs={{0,8},{1,9},{2,10},{3,11},{4,12},{5,13},{6,14},{7,15},{8,0},{9,1},... | collective-permute-start | bytes 983048 | tf_op jit(solution)/shard_map/ppermute | solution.py:137
  22.2 11.3 %collective-permute-start.8 = (bf16[640,2048]{1,0:T(8,128)(2,1)S(1)}, bf16[640,2048]{1,0:T(8,128)(2,1)S(1)}, u32[]{:S(2)}, u32[]{:S(2)}) collective-permute-start(bf16[640,2048]{1,0:T(8,128)(2,1)S(1)} %pad_maximum_fusion.1), channel_id=1, source_target_pairs={{0,1},{1,0},{2,3},{3,2},{4,5},{5,4},{6,7},{7,6},{8,9},{9,8},{10,11... | collective-permute-start | bytes 7864328 | tf_op jit(solution)/shard_map/ppermute | solution.py:137
  29.6 10.4 %collective-permute-start.12 = (bf16[24,4096]{1,0:T(8,128)(2,1)S(1)}, bf16[24,4096]{1,0:T(8,128)(2,1)S(1)}, u32[]{:S(2)}, u32[]{:S(2)}) collective-permute-start(bf16[24,4096]{1,0:T(8,128)(2,1)S(1)} %get-tuple-element.59), channel_id=1, source_target_pairs={{0,6},{1,7},{2,4},{3,5},{4,2},{5,3},{6,0},{7,1},{8,14},{9,15},{10,... | collective-permute-start | bytes 589832 | tf_op jit(solution)/shard_map/ppermute | solution.py:137
  31.9 8.1 %collective-permute-start.11 = (bf16[24,4096]{1,0:T(8,128)(2,1)S(1)}, bf16[24,4096]{1,0:T(8,128)(2,1)S(1)}, u32[]{:S(2)}, u32[]{:S(2)}) collective-permute-start(bf16[24,4096]{1,0:T(8,128)(2,1)S(1)} %get-tuple-element.59), channel_id=1, source_target_pairs={{0,2},{1,3},{2,0},{3,1},{4,6},{5,7},{6,4},{7,5},{8,10},{9,11},{10,... | collective-permute-start | bytes 589832 | tf_op jit(solution)/shard_map/ppermute | solution.py:137
  32.8 7.2 %collective-permute-start.10 = (bf16[24,4096]{1,0:T(8,128)(2,1)S(1)}, bf16[24,4096]{1,0:T(8,128)(2,1)S(1)}, u32[]{:S(2)}, u32[]{:S(2)}) collective-permute-start(bf16[24,4096]{1,0:T(8,128)(2,1)S(1)} %get-tuple-element.60), channel_id=1, source_target_pairs={{0,8},{1,9},{2,10},{3,11},{4,12},{5,13},{6,14},{7,15},{8,0},{9,1},... | collective-permute-start | bytes 589832 | tf_op jit(solution)/shard_map/ppermute | solution.py:137
  33.1 6.9 %collective-permute-start.9 = (bf16[24,4096]{1,0:T(8,128)(2,1)S(1)}, bf16[24,4096]{1,0:T(8,128)(2,1)S(1)}, u32[]{:S(2)}, u32[]{:S(2)}) collective-permute-start(bf16[24,4096]{1,0:T(8,128)(2,1)S(1)} %get-tuple-element.61), channel_id=1, source_target_pairs={{0,4},{1,5},{2,6},{3,7},{4,0},{5,1},{6,2},{7,3},{8,12},{9,13},{10,... | collective-permute-start | bytes 589832 | tf_op jit(solution)/shard_map/ppermute | solution.py:137
  43.3 7.6 %collective-permute-start.13 = (bf16[24,2048]{1,0:T(8,128)(2,1)S(1)}, bf16[24,2048]{1,0:T(8,128)(2,1)S(1)}, u32[]{:S(2)}, u32[]{:S(2)}) collective-permute-start(bf16[24,2048]{1,0:T(8,128)(2,1)S(1)} %get-tuple-element.91), channel_id=1, source_target_pairs={{0,14},{1,15},{2,12},{3,13},{4,10},{5,11},{6,8},{7,9},{8,6},{9,7},... | collective-permute-start | bytes 294920 | tf_op jit(solution)/shard_map/ppermute | solution.py:137
  45.4 9.2 %collective-permute-start.14 = (bf16[24,2048]{1,0:T(8,128)(2,1)S(1)}, bf16[24,2048]{1,0:T(8,128)(2,1)S(1)}, u32[]{:S(2)}, u32[]{:S(2)}) collective-permute-start(bf16[24,2048]{1,0:T(8,128)(2,1)S(1)} %get-tuple-element.66), channel_id=1, source_target_pairs={{0,12},{1,13},{2,14},{3,15},{4,8},{5,9},{6,10},{7,11},{8,4},{9,5},... | collective-permute-start | bytes 294920 | tf_op jit(solution)/shard_map/ppermute | solution.py:137
  48.2 10.1 %collective-permute-start.17 = (bf16[40,2048]{1,0:T(8,128)(2,1)S(1)}, bf16[40,2048]{1,0:T(8,128)(2,1)S(1)}, u32[]{:S(2)}, u32[]{:S(2)}) collective-permute-start(bf16[40,2048]{1,0:T(8,128)(2,1)S(1)} %get-tuple-element.69), channel_id=1, source_target_pairs={{0,2},{1,3},{2,0},{3,1},{4,6},{5,7},{6,4},{7,5},{8,10},{9,11},{10,... | collective-permute-start | bytes 491528 | tf_op jit(solution)/shard_map/ppermute | solution.py:137
  49.2 9.0 %collective-permute-start.18 = (bf16[40,2048]{1,0:T(8,128)(2,1)S(1)}, bf16[40,2048]{1,0:T(8,128)(2,1)S(1)}, u32[]{:S(2)}, u32[]{:S(2)}) collective-permute-start(bf16[40,2048]{1,0:T(8,128)(2,1)S(1)} %get-tuple-element.70), channel_id=1, source_target_pairs={{0,4},{1,5},{2,6},{3,7},{4,0},{5,1},{6,2},{7,3},{8,12},{9,13},{10,... | collective-permute-start | bytes 491528 | tf_op jit(solution)/shard_map/ppermute | solution.py:137
  50.9 7.8 %collective-permute-start.16 = (bf16[40,2048]{1,0:T(8,128)(2,1)S(1)}, bf16[40,2048]{1,0:T(8,128)(2,1)S(1)}, u32[]{:S(2)}, u32[]{:S(2)}) collective-permute-start(bf16[40,2048]{1,0:T(8,128)(2,1)S(1)} %get-tuple-element.68), channel_id=1, source_target_pairs={{0,6},{1,7},{2,4},{3,5},{4,2},{5,3},{6,0},{7,1},{8,14},{9,15},{10,... | collective-permute-start | bytes 491528 | tf_op jit(solution)/shard_map/ppermute | solution.py:137
  54.6 8.5 %collective-permute-start.23 = (bf16[320,2048]{1,0:T(8,128)(2,1)S(1)}, bf16[320,2048]{1,0:T(8,128)(2,1)S(1)}, u32[]{:S(2)}, u32[]{:S(2)}) collective-permute-start(bf16[320,2048]{1,0:T(8,128)(2,1)S(1)} %fusion.12), channel_id=1, source_target_pairs={{0,1},{1,0},{2,3},{3,2},{4,5},{5,4},{6,7},{7,6},{8,9},{9,8},{10,11... | collective-permute-start | bytes 3932168 | tf_op jit(solution)/shard_map/ppermute | solution.py:137
  58.3 8.9 %collective-permute-start.24 = (bf16[320,2048]{1,0:T(8,128)(2,1)S(1)}, bf16[320,2048]{1,0:T(8,128)(2,1)S(1)}, u32[]{:S(2)}, u32[]{:S(2)}) collective-permute-start(bf16[320,2048]{1,0:T(8,128)(2,1)S(1)} %fusion.13), channel_id=1, source_target_pairs={{0,1},{1,0},{2,3},{3,2},{4,5},{5,4},{6,7},{7,6},{8,9},{9,8},{10,11... | collective-permute-start | bytes 3932168 | tf_op jit(solution)/shard_map/ppermute | solution.py:137
  58.8 10.7 %collective-permute-start.25 = (bf16[24,2048]{1,0:T(8,128)(2,1)S(1)}, bf16[24,2048]{1,0:T(8,128)(2,1)S(1)}, u32[]{:S(2)}, u32[]{:S(2)}) collective-permute-start(bf16[24,2048]{1,0:T(8,128)(2,1)S(1)} %add_convert_fusion), channel_id=1, source_target_pairs={{0,16},{1,17},{2,18},{3,19},{4,20},{5,21},{6,22},{7,23},{8,24},{9,... | collective-permute-start | bytes 294920 | tf_op jit(solution)/shard_map/ppermute | solution.py:177
  60.9 8.9 %collective-permute-start.20 = (bf16[16,2048]{1,0:T(8,128)(2,1)S(1)}, bf16[16,2048]{1,0:T(8,128)(2,1)S(1)}, u32[]{:S(2)}, u32[]{:S(2)}) collective-permute-start(bf16[16,2048]{1,0:T(8,128)(2,1)S(1)} %get-tuple-element.72), channel_id=1, source_target_pairs={{0,8},{1,9},{2,10},{3,11},{4,12},{5,13},{6,14},{7,15},{8,0},{9,1},... | collective-permute-start | bytes 196616 | tf_op jit(solution)/shard_map/ppermute | solution.py:137
  62.8 7.0 %collective-permute-start.21 = (bf16[16,2048]{1,0:T(8,128)(2,1)S(1)}, bf16[16,2048]{1,0:T(8,128)(2,1)S(1)}, u32[]{:S(2)}, u32[]{:S(2)}) collective-permute-start(bf16[16,2048]{1,0:T(8,128)(2,1)S(1)} %get-tuple-element.74), channel_id=1, source_target_pairs={{0,2},{1,3},{2,0},{3,1},{4,6},{5,7},{6,4},{7,5},{8,10},{9,11},{10,... | collective-permute-start | bytes 196616 | tf_op jit(solution)/shard_map/ppermute | solution.py:137
  63.1 6.7 %collective-permute-start.22 = (bf16[16,2048]{1,0:T(8,128)(2,1)S(1)}, bf16[16,2048]{1,0:T(8,128)(2,1)S(1)}, u32[]{:S(2)}, u32[]{:S(2)}) collective-permute-start(bf16[16,2048]{1,0:T(8,128)(2,1)S(1)} %get-tuple-element.76), channel_id=1, source_target_pairs={{0,4},{1,5},{2,6},{3,7},{4,0},{5,1},{6,2},{7,3},{8,12},{9,13},{10,... | collective-permute-start | bytes 196616 | tf_op jit(solution)/shard_map/ppermute | solution.py:137
  (8 other events, 55.2 us)

commit v11 on v9

--- a/solution.py
+++ b/solution.py
@@ -47,17 +47,12 @@
     return lax.psum_scatter(attn_partials[0], "dp", scatter_dimension=0, tiled=True)
 
 
-def pick_rows(rows_ref, pick, tokens, gated):
-    width = tokens.shape[1]
-    for half, source in enumerate((tokens, gated)):
-        rows_ref[:, half * width : (half + 1) * width] = jnp.dot(
-            pick, source, preferred_element_type=jnp.float32
-        ).astype(jnp.bfloat16)
-
-
-def cross_kernel(blocks, experts, ids_ref, gate_ref, tokens_ref, grads_ref, gated_ref, *outs):
-    picks, sent = outs[: len(blocks)], outs[len(blocks) :]
-    n = tokens_ref.shape[0]
+def picked(pick, source):
+    return jnp.dot(pick, source, preferred_element_type=jnp.float32)
+
+
+def pack_kernel(blocks, experts, ids_ref, gate_ref, tokens_ref, grads_ref, *outs):
+    n, width = tokens_ref.shape
     mine = (lax.axis_index("expert") // SHARDS).astype(jnp.float32)
     ids = ids_ref[...].astype(jnp.float32)
     relative = ids - mine
@@ -68,54 +63,84 @@
     gate_down = jnp.sum(jnp.where(down == across, gate_ref[...], 0.0), axis=1, keepdims=True)
     rivals = jnp.where((ids_down == ids) & (down < across), 1.0, 0.0)
     rank = jnp.sum(rivals, axis=0, keepdims=True)
+    tokens = tokens_ref[...]
     gated = (gate_down * grads_ref[...].astype(jnp.float32)).astype(jnp.bfloat16)
-    gated_ref[...] = gated
-    for k, (expert, begin, end, row) in enumerate(blocks):
+    rows, picks = outs[: len(blocks)], outs[len(blocks) : 3 * len(blocks) - 2]
+    copies = outs[3 * len(blocks) - 2 :]
+
+    def one_hot(shape, block, shift):
+        expert, begin, end, row = block
         chosen = (relative == expert) & (rank >= begin) & (rank < end)
-        slot = jnp.where(chosen, rank - begin + row, -1.0).astype(jnp.int32)
-        slots = lax.broadcasted_iota(jnp.int32, picks[k].shape, 0)
-        pick = jnp.where(slots == slot, 1.0, 0.0).astype(jnp.bfloat16)
+        slot = jnp.where(chosen, rank - begin + row + shift, -1.0).astype(jnp.int32)
+        slots = lax.broadcasted_iota(jnp.int32, shape, 0)
+        return jnp.where(slots == slot, 1.0, 0.0).astype(jnp.bfloat16)
+
+    for k, block in enumerate(blocks[2:]):
+        upper_ref, lower_ref = picks[2 * k + 2], picks[2 * k + 3]
+        upper = one_hot(upper_ref.shape, block, 0)
+        lower = one_hot(lower_ref.shape, block, block[2])
+        upper_ref[...], lower_ref[...] = upper, lower
+        both = picked(upper, tokens) + picked(lower, gated)
+        rows[k + 2][...] = both.astype(jnp.bfloat16)
+    for k, block in enumerate(blocks[:2]):
+        pick = one_hot(picks[k].shape, block, 0)
         picks[k][...] = pick
-        if k >= len(blocks) - len(sent):
-            pick_rows(sent[k - len(blocks) + len(sent)], pick, tokens_ref[...], gated)
-
-
-def pack_cross(blocks, rows, experts, ids, gate, tokens, grads):
+        rows[k][:, :width] = picked(pick, tokens).astype(jnp.bfloat16)
+        rows[k][:, width:] = picked(pick, gated).astype(jnp.bfloat16)
+    for copy_ref in copies:
+        copy_ref[...] = rows[0][...]
+
+
+def pack(blocks, first, rest, capacity, experts, ids, gate, tokens, grads):
     n, width = tokens.shape
     whole = pl.BlockSpec(memory_space=pltpu.VMEM)
-    gated, *outs = pl.pallas_call(
-        lambda *refs: cross_kernel(blocks, experts, *refs),
-        out_shape=[jax.ShapeDtypeStruct((n, width), jnp.bfloat16)]
-        + [jax.ShapeDtypeStruct((count, n), jnp.bfloat16) for count in rows]
-        + [jax.ShapeDtypeStruct((count, 2 * width), jnp.bfloat16) for count in rows[2:]],
+    crossing = len(blocks) - 2
+
+    def shape(rows, columns):
+        return jax.ShapeDtypeStruct((rows, columns), jnp.bfloat16)
+
+    shapes = [shape(first, 2 * width), shape(rest, 2 * width)]
+    shapes += [shape(2 * capacity, width)] * crossing
+    shapes += [shape(first, n), shape(rest, n)] + [shape(2 * capacity, n)] * (2 * crossing)
+    shapes += [shape(first, 2 * width)] * len(early_masks)
+    outs = pl.pallas_call(
+        lambda *refs: pack_kernel(blocks, experts, *refs),
+        out_shape=shapes,
         in_specs=[whole] * 4,
-        out_specs=[whole] * (2 * len(rows) - 1),
+        out_specs=[whole] * len(shapes),
     )(ids.reshape(1, n), gate.reshape(1, n), tokens, grads)
-    return gated, outs[: len(rows)], outs[len(rows) :]
-
-
-def own_kernel(early_pick_ref, late_pick_ref, tokens_ref, gated_ref, *refs):
-    late_ref, early_ref, *copies = refs[-len(early_masks) - 2 :]
-    pick_rows(early_ref, early_pick_ref[...], tokens_ref[...], gated_ref[...])
-    for copy_ref in copies:
-        copy_ref[...] = early_ref[...]
-    pick_rows(late_ref, late_pick_ref[...], tokens_ref[...], gated_ref[...])
-
-
-def pack_own(early_pick, late_pick, tokens, gated, *sent):
-    whole = pl.BlockSpec(memory_space=pltpu.VMEM)
-    width = tokens.shape[1]
-    early, late = [
-        jax.ShapeDtypeStruct((pick.shape[0], 2 * width), jnp.bfloat16)
-        for pick in (early_pick, late_pick)
-    ]
-    shapes = [late] + [early] * (len(early_masks) + 1)
+    rows, picks = outs[: len(blocks)], outs[len(blocks) : 3 * len(blocks) - 2]
+    return rows, picks, outs[3 * len(blocks) - 2 :]
+
+
+def handed_on(copies, sent):
+    anywhere = pl.BlockSpec(memory_space=pl.ANY)
     return pl.pallas_call(
-        own_kernel,
-        out_shape=shapes,
-        in_specs=[whole] * 4 + [pl.BlockSpec(memory_space=pl.ANY)] * len(sent),
-        out_specs=[whole] * len(shapes),
-    )(early_pick, late_pick, tokens, gated, *sent)
+        lambda *refs: None,
+        out_shape=[jax.ShapeDtypeStruct(rows.shape, rows.dtype) for rows in copies],
+        in_specs=[anywhere] * (len(copies) + len(sent)),
+        out_specs=[anywhere] * len(copies),
+        input_output_aliases={k: k for k in range(len(copies))},
+    )(*copies, *sent)
+
+
+def unpack_kernel(own_ref, *refs):
+    *refs, out_ref = refs
+    crossings = len(refs) // 3
+    picks, rows = refs[: 2 * crossings], refs[2 * crossings :]
+    half = out_ref.shape[1] // 2
+    for side in range(2):
+        columns = slice(side * half, (side + 1) * half)
+        both = own_ref[:, columns].astype(jnp.float32)
+        for pick_ref, rows_ref in zip(picks[side::2], rows):
+            both = both + contract_rows(pick_ref[...], rows_ref[...])
+        out_ref[:, columns] = both.astype(jnp.bfloat16)
+
+
+def unpacked(own_grad, picks, crossed):
+    return pl.pallas_call(
+        unpack_kernel, out_shape=jax.ShapeDtypeStruct(own_grad.shape, own_grad.dtype)
+    )(own_grad, *picks, *crossed)
 
 
 def whole_weights(shard):
@@ -177,18 +202,12 @@
 
     offset = (experts - 1) * capacity - first
     own_blocks = [(0, 0, first, 0), (0, first, capacity, offset + first)]
-    cross_blocks = [(s, 0, capacity, (s - 1) * capacity) for s in range(1, experts)]
+    cross_blocks = [(s, 0, capacity, 0) for s in range(1, experts)]
     grads = summed_grads(attn_partials)
-    gated, picks, sent = pack_cross(
-        own_blocks + cross_blocks,
-        [first] + [rest] * experts,
-        experts,
-        expert_ids,
-        gate,
-        tokens,
-        grads,
-    )
-    late_own, early_own, *early_copies = pack_own(picks[0], picks[1], tokens, gated, *sent)
+    (early_own, late_own, *sent), picks, copies = pack(
+        own_blocks + cross_blocks, first, rest, capacity, experts, expert_ids, gate, tokens, grads
+    )
+    early_copies = handed_on(copies, sent)
 
     def activated(rows):
         expert_rows, grad_rows = rows[:, :width], rows[:, width:]
@@ -203,7 +222,10 @@
         return parts.astype(jnp.bfloat16)
 
     for s in range(1, experts):
-        late_own = late_own + shifted(sent[s - 1], s)
+        side_by_side = jnp.concatenate(split_rows(shifted(sent[s - 1], s), capacity), axis=1)
+        late_own = late_own + jnp.pad(
+            side_by_side, (((s - 1) * capacity, rest - s * capacity), (0, 0))
+        )
     early_x, early_y, early_z, early_xy = after(
         [swap(rows, mask) for rows, mask in zip(early_copies, early_masks)], late_own
     )
@@ -269,12 +291,17 @@
     )
     sums = total(own, *near)
     early_sum, late_sum = sums[:first], sums[first:]
-    crossed = [shifted(late_sum, -s) for s in range(1, experts)]
-
+    half = width // 2
+    crossed = []
+    for s in range(1, experts):
+        rows = late_sum[(s - 1) * capacity : s * capacity]
+        crossed.append(
+            shifted(jnp.concatenate([rows[:, :half], rows[:, half:]], axis=0), -s)
+        )
     crossed = after(crossed, new_w_in, new_w_out)
-    returned = [early_sum, late_sum, *crossed]
-    token_grad = sum(contract_rows(pick, rows) for pick, rows in zip(picks, returned))
-    return (token_grad.astype(jnp.bfloat16), new_w_in, new_w_out)
+    own_grad = contract_rows(picks[0], early_sum) + contract_rows(picks[1], late_sum)
+    token_grad = unpacked(own_grad.astype(jnp.bfloat16), picks[2:], crossed)
+    return (token_grad, new_w_in, new_w_out)
 
 
 def solution(mesh):

time: 70.3 us -> 69.3 us (0.986)
  waiting for transfers between devices: 19.6 us -> 15.2 us
  starting transfers between devices: 24.8 us -> 27.7 us
    ppermute x21, waiting for transfers between devices: 19.6 us -> 15.2 us  [swap(): lax.ppermute(rows, 'expert', [(i, i ^ mask) for i in range(n_expert)])]
    ppermute x21, starting transfers between devices: 18 us -> 20.3 us  [swap(): lax.ppermute(rows, 'expert', [(i, i ^ mask) for i in range(n_expert)])]
    dot_general x11 -> x10, matrix products: 9.67 us -> 9.42 us  [contract_rows(): lax.dot_general(left, right, (((0,), (0,)), ((), ())), preferred_element_...]
    pallas_call x2 -> x3, Pallas kernels: 4.38 us -> 4.56 us  [the longest x1 2.6 us: pack(): pl.pallas_call(lambda *refs: pack_kernel(blocks, experts, *refs), out_sha...]
  transfers between devices with their start and end apart: 23 -> 23, of which waited for: 7 -> 7; matrix products, arithmetic and copies ran while one was open for 22% -> 23% of each run, Pallas kernels for 3% -> 0%
where the time goes in v11:
time: 69.3 us; the launch traced here: 69.1 us
  starting transfers between devices  27.7 us (40%)
  waiting for transfers between devices  15.2 us (22%)
  matrix products  15.1 us (22%)
  Pallas kernels  4.56 us (7%)
  local copies, waits for them, and re-layouts  2.79 us (4%)
  other arithmetic  2.69 us (4%)
  between operations  1.05 us (2%)
    ppermute x21, starting transfers between devices, swap(): lax.ppermute(rows, 'expert', [(i, i ^ mask) for i in range(n_expert)])  20.3 us
    ppermute x21, waiting for transfers between devices, swap(): lax.ppermute(rows, 'expert', [(i, i ^ mask) for i in range(n_expert)])  15.2 us
    dot_general x10, matrix products, contract_rows(): lax.dot_general(left, right, (((0,), (0,)), ((), ())), preferred_element_...  9.42 us
    ppermute x2, starting transfers between devices, shifted(): return lax.ppermute(rows, 'expert', pairs)  7.4 us
    dot_general x4, matrix products, contract_cols(): lax.dot_general(left, right, (((1,), (1,)), ((), ())), preferred_element_...  4.32 us
    pallas_call x1, Pallas kernels, pack(): pl.pallas_call(lambda *refs: pack_kernel(blocks, experts, *refs), out_sha...  2.6 us
    unnamed x22, local copies, waits for them, and re-layouts  2.36 us
    pallas_call x1, Pallas kernels, unpacked(): pl.pallas_call(unpack_kernel, out_shape=jax.ShapeDtypeStruct(own_grad.sha...  1.96 us
  transfers between devices with their start and end apart: 23, of which 7 were waited for; matrix products, arithmetic and copies ran while one was open for 23% of the time, Pallas kernels for 0%

profile of v11, /device:TPU:0, one launch (start us, length us, event | category | flops | bytes accessed | tf_op | source)
XLA Modules:
  0.0 69.1 jit_solution(6541316528593916740)
XLA Ops:
  0.6 2.6 %shard_map.85 = (bf16[16,4096]{1,0:T(8,128)(2,1)}, bf16[24,4096]{1,0:T(8,128)(2,1)}, bf16[40,2048]{1,0:T(8,128)(2,1)}, bf16[16,64]{1,0:T(8,128)(2,1)}, bf16[24,6...) custom-call(s32[1,64]{1,0:T(1,128)} %bitcast.20, ...), custom_call_target="tpu_custom_call" | custom-call | tf_op jit(solution)/shard_map/pallas_call | solution.py:106
  3.2 4.1 %collective-permute-start = (bf16[40,2048]{1,0:T(8,128)(2,1)}, bf16[40,2048]{1,0:T(8,128)(2,1)S(1)}, u32[]{:S(2)}, u32[]{:S(2)}) collective-permute-start(bf16[40,2048]{1,0:T(8,128)(2,1)} %get-tuple-element.43.refs_4_), channel_id=1, source_target_pairs={{0,16},{1,17},{2,18},{3,19},{4,20},{5,21},{6,22},{7,23},{8,24},{9,... | collective-permute-start | bytes 491528 | tf_op jit(solution)/shard_map/ppermute | solution.py:201
  7.4 1.5 %collective-permute-start.1 = (bf16[16,4096]{1,0:T(8,128)(2,1)}, bf16[16,4096]{1,0:T(8,128)(2,1)S(1)}, u32[]{:S(2)}, u32[]{:S(2)}) collective-permute-start(bf16[16,4096]{1,0:T(8,128)(2,1)} %get-tuple-element.48), channel_id=1, source_target_pairs={{0,2},{1,3},{2,0},{3,1},{4,6},{5,7},{6,4},{7,5},{8,10},{9,11},{10,... | collective-permute-start | bytes 393224 | tf_op jit(solution)/shard_map/ppermute | solution.py:162
  8.8 1.5 %collective-permute-start.2 = (bf16[16,4096]{1,0:T(8,128)(2,1)}, bf16[16,4096]{1,0:T(8,128)(2,1)S(1)}, u32[]{:S(2)}, u32[]{:S(2)}) collective-permute-start(bf16[16,4096]{1,0:T(8,128)(2,1)} %get-tuple-element.49), channel_id=1, source_target_pairs={{0,4},{1,5},{2,6},{3,7},{4,0},{5,1},{6,2},{7,3},{8,12},{9,13},{10,... | collective-permute-start | bytes 393224 | tf_op jit(solution)/shard_map/ppermute | solution.py:162
  10.4 1.6 %collective-permute-start.3 = (bf16[16,4096]{1,0:T(8,128)(2,1)}, bf16[16,4096]{1,0:T(8,128)(2,1)S(1)}, u32[]{:S(2)}, u32[]{:S(2)}) collective-permute-start(bf16[16,4096]{1,0:T(8,128)(2,1)} %get-tuple-element.50), channel_id=1, source_target_pairs={{0,8},{1,9},{2,10},{3,11},{4,12},{5,13},{6,14},{7,15},{8,0},{9,1},... | collective-permute-start | bytes 393224 | tf_op jit(solution)/shard_map/ppermute | solution.py:162
  13.3 1.9 %convert_bitcast_fusion = bf16[320,2048]{1,0:T(8,128)(2,1)S(1)} fusion(f32[2048,320]{0,1:T(8,128)} %param.10), kind=kLoop, calls=%fused_computation.29 | loop fusion | flops 655360 | bytes 3932160 | tf_op jit(solution)/shard_map/transpose | solution.py:244
  20.5 5.7 %collective-permute-done.6 = bf16[40,4096]{1,0:T(8,128)(2,1)S(1)} collective-permute-done((bf16[40,4096]{1,0:T(8,128)(2,1)S(1)}, bf16[40,4096]{1,0:T(8,128)(2,1)S(1)}, u32[]{:S(2)}, u32[]{:S(2)}) %collective-permute-start.6) | collective-permute-done | bytes 327712 | tf_op jit(solution)/shard_map/ppermute | solution.py:162
  27.2 2.1 %collective-permute-start.12 = (bf16[24,4096]{1,0:T(8,128)(2,1)S(1)}, bf16[24,4096]{1,0:T(8,128)(2,1)S(1)}, u32[]{:S(2)}, u32[]{:S(2)}) collective-permute-start(bf16[24,4096]{1,0:T(8,128)(2,1)S(1)} %get-tuple-element.59), channel_id=1, source_target_pairs={{0,6},{1,7},{2,4},{3,5},{4,2},{5,3},{6,0},{7,1},{8,14},{9,15},{10,... | collective-permute-start | bytes 589832 | tf_op jit(solution)/shard_map/ppermute | solution.py:162
  29.6 1.4 %collective-permute-start.10 = (bf16[24,4096]{1,0:T(8,128)(2,1)S(1)}, bf16[24,4096]{1,0:T(8,128)(2,1)S(1)}, u32[]{:S(2)}, u32[]{:S(2)}) collective-permute-start(bf16[24,4096]{1,0:T(8,128)(2,1)S(1)} %get-tuple-element.60), channel_id=1, source_target_pairs={{0,8},{1,9},{2,10},{3,11},{4,12},{5,13},{6,14},{7,15},{8,0},{9,1},... | collective-permute-start | bytes 589832 | tf_op jit(solution)/shard_map/ppermute | solution.py:162
  31.0 1.0 %collective-permute-start.9 = (bf16[24,4096]{1,0:T(8,128)(2,1)S(1)}, bf16[24,4096]{1,0:T(8,128)(2,1)S(1)}, u32[]{:S(2)}, u32[]{:S(2)}) collective-permute-start(bf16[24,4096]{1,0:T(8,128)(2,1)S(1)} %get-tuple-element.61), channel_id=1, source_target_pairs={{0,4},{1,5},{2,6},{3,7},{4,0},{5,1},{6,2},{7,3},{8,12},{9,13},{10,... | collective-permute-start | bytes 589832 | tf_op jit(solution)/shard_map/ppermute | solution.py:162
  32.3 1.0 %multiply_convert_fusion.1 = (bf16[128,640]{1,0:T(8,128)(2,1)S(1)}, f32[128,640]{1,0:T(8,128)S(1)}) fusion(bf16[320,2048]{1,0:T(8,128)(2,1)S(1)} %convert_bitcast_fusion, bf16[320,2048]{1,0:T(8,128)(2,1)S(1)} %get-tuple-element.79, bf16[128,4096]{1,0:T(8,128)(2,1)S(1)} %slice_dynamic-update-slice_fusion), kind=kOutput, calls=%fused_computation.72 | convolution fusion | flops 341606400 | bytes 3637248 | tf_op jit(solution)/shard_map/dot_general | solution.py:39
  34.4 1.0 %fusion.24 = bf16[128,640]{1,0:T(8,128)(2,1)S(1)} fusion(bf16[320,2048]{1,0:T(8,128)(2,1)S(1)} %get-tuple-element.80, bf16[320,2048]{1,0:T(8,128)(2,1)S(1)} %convert_bitcast_fusion.1, bf16[128,4096]{1,0:T(8,128)(2,1)S(1)} %slice_dynamic-update-slice_fusion, f32[128,640]{1,0:T(8,128)S(1)} %get-tuple-element.110), kind=kOutput, calls=%fused_computation.36 | convolution fusion | flops 342507520 | bytes 3637248 | tf_op jit(solution)/shard_map/dot_general | solution.py:39
  37.3 1.1 %multiply_convert_fusion = (bf16[192,640]{1,0:T(8,128)(2,1)S(1)}, f32[192,640]{1,0:T(8,128)S(1)}) fusion(bf16[320,2048]{1,0:T(8,128)(2,1)S(1)} %convert_bitcast_fusion, bf16[320,2048]{1,0:T(8,128)(2,1)S(1)} %get-tuple-element.79, bf16[192,4096]{1,0:T(8,128)(2,1)S(1)} %constant_dynamic-update-slice_fusion.5), kind=kOutput, calls=%fused_computation.47 | convolution fusion | flops 509788160 | bytes 4145152 | tf_op jit(solution)/shard_map/dot_general | solution.py:39
  38.5 1.2 %fusion.21 = bf16[192,640]{1,0:T(8,128)(2,1)S(1)} fusion(bf16[320,2048]{1,0:T(8,128)(2,1)S(1)} %get-tuple-element.80, bf16[320,2048]{1,0:T(8,128)(2,1)S(1)} %convert_bitcast_fusion.1, bf16[192,4096]{1,0:T(8,128)(2,1)S(1)} %constant_dynamic-update-slice_fusion.5, f32[192,640]{1,0:T(8,128)S(1)} %get-tuple-element.112), kind=kOutput, calls=%fused_computation.33 | convolution fusion | flops 511139840 | bytes 4145152 | tf_op jit(solution)/shard_map/dot_general | solution.py:39
  40.5 1.1 %collective-permute-start.14 = (bf16[40,2048]{1,0:T(8,128)(2,1)S(1)}, bf16[40,2048]{1,0:T(8,128)(2,1)S(1)}, u32[]{:S(2)}, u32[]{:S(2)}) collective-permute-start(bf16[40,2048]{1,0:T(8,128)(2,1)S(1)} %pad_maximum_fusion.19), channel_id=1, source_target_pairs={{0,6},{1,7},{2,4},{3,5},{4,2},{5,3},{6,0},{7,1},{8,14},{9,15},{10,... | collective-permute-start | bytes 491528 | tf_op jit(solution)/shard_map/ppermute | solution.py:162
  41.6 1.6 %collective-permute-start.13 = (bf16[40,2048]{1,0:T(8,128)(2,1)S(1)}, bf16[40,2048]{1,0:T(8,128)(2,1)S(1)}, u32[]{:S(2)}, u32[]{:S(2)}) collective-permute-start(bf16[40,2048]{1,0:T(8,128)(2,1)S(1)} %pad_maximum_fusion.20), channel_id=1, source_target_pairs={{0,2},{1,3},{2,0},{3,1},{4,6},{5,7},{6,4},{7,5},{8,10},{9,11},{10,... | collective-permute-start | bytes 491528 | tf_op jit(solution)/shard_map/ppermute | solution.py:162
  43.2 1.1 %collective-permute-start.16 = (bf16[40,2048]{1,0:T(8,128)(2,1)S(1)}, bf16[40,2048]{1,0:T(8,128)(2,1)S(1)}, u32[]{:S(2)}, u32[]{:S(2)}) collective-permute-start(bf16[40,2048]{1,0:T(8,128)(2,1)S(1)} %get-tuple-element.67), channel_id=1, source_target_pairs={{0,4},{1,5},{2,6},{3,7},{4,0},{5,1},{6,2},{7,3},{8,12},{9,13},{10,... | collective-permute-start | bytes 491528 | tf_op jit(solution)/shard_map/ppermute | solution.py:162
  45.0 3.7 %collective-permute-done.13 = bf16[40,2048]{1,0:T(8,128)(2,1)S(1)} collective-permute-done((bf16[40,2048]{1,0:T(8,128)(2,1)S(1)}, bf16[40,2048]{1,0:T(8,128)(2,1)S(1)}, u32[]{:S(2)}, u32[]{:S(2)}) %collective-permute-start.13) | collective-permute-done | bytes 163872 | tf_op jit(solution)/shard_map/ppermute | solution.py:162
  49.3 2.4 %collective-permute-start.17 = (bf16[40,2048]{1,0:T(8,128)(2,1)S(1)}, bf16[40,2048]{1,0:T(8,128)(2,1)S(1)}, u32[]{:S(2)}, u32[]{:S(2)}) collective-permute-start(bf16[40,2048]{1,0:T(8,128)(2,1)S(1)} %add_convert_fusion.2), channel_id=1, source_target_pairs={{0,2},{1,3},{2,0},{3,1},{4,6},{5,7},{6,4},{7,5},{8,10},{9,11},{10,... | collective-permute-start | bytes 491528 | tf_op jit(solution)/shard_map/ppermute | solution.py:162
  53.9 3.3 %collective-permute-done.19 = bf16[40,2048]{1,0:T(8,128)(2,1)S(1)} collective-permute-done((bf16[40,2048]{1,0:T(8,128)(2,1)S(1)}, bf16[40,2048]{1,0:T(8,128)(2,1)S(1)}, u32[]{:S(2)}, u32[]{:S(2)}) %collective-permute-start.19) | collective-permute-done | bytes 163872 | tf_op jit(solution)/shard_map/ppermute | solution.py:162
  57.3 3.3 %collective-permute-start.22 = (bf16[40,1024]{1,0:T(8,128)(2,1)S(1)}, bf16[40,1024]{1,0:T(8,128)(2,1)S(1)}, u32[]{:S(2)}, u32[]{:S(2)}) collective-permute-start(bf16[40,1024]{1,0:T(8,128)(2,1)S(1)} %pad_maximum_fusion.23), channel_id=1, source_target_pairs={{0,16},{1,17},{2,18},{3,19},{4,20},{5,21},{6,22},{7,23},{8,24},{9,... | collective-permute-start | bytes 245768 | tf_op jit(solution)/shard_map/ppermute | solution.py:201
  61.8 2.4 %fusion.5 = f32[2048,320]{0,1:T(8,128)} fusion(f32[2048,320]{0,1:T(8,128)S(1)} %copy-done, f32[320,2048]{1,0:T(8,128)S(1)} %fusion.43, bf16[320,2048]{1,0:T(8,128)(2,1)S(1)} %collective-permute-done.21, bf16[192,4096]{1,0:T(8,128)(2,1)S(1)} %constant_dynamic-update-slice_fusion.5, bf16[192,640]{1,0:T(8,128)(2,1)S(1)} %get-tuple-element.75), kind=kOutput, calls=%fused_computation.9 | convolution fusion | flops 255590400 | bytes 10108928 | tf_op jit(solution)/shard_map/dot_general | solution.py:33
  64.2 2.3 %fusion.11 = f32[2048,320]{0,1:T(8,128)} fusion(f32[2048,320]{0,1:T(8,128)S(1)} %copy-done.1, f32[320,2048]{1,0:T(8,128)S(1)} %fusion.37, bf16[320,2048]{1,0:T(8,128)(2,1)S(1)} %collective-permute-done.20, bf16[192,4096]{1,0:T(8,128)(2,1)S(1)} %constant_dynamic-update-slice_fusion.5, bf16[192,640]{1,0:T(8,128)(2,1)S(1)} %fusion.21), kind=kOutput, calls=%fused_computation.17 | convolution fusion | flops 255590400 | bytes 10108928 | tf_op jit(solution)/shard_map/dot_general | solution.py:33
  67.1 2.0 %shard_map.87 = bf16[64,2048]{1,0:T(8,128)(2,1)} custom-call(bf16[64,2048]{1,0:T(8,128)(2,1)} %fusion.16.own_ref, bf16[40,64]{1,0:T(8,128)(2,1)} %get-tuple-element.72.refs_0_, bf16[40,64]{1,0:T(8,128)(2,1)} %get-tuple-element.73.refs_1_, bf16[40,1024]{1,0:T(8,128)(2,1)} %copy-done.3), custom_call_target="tpu_custom_call" | custom-call | tf_op jit(solution)/shard_map/pallas_call | solution.py:141
  (86 shorter events, 17.3 us)
Async XLA Ops:
  0.6 14.6 %copy-start = (f32[2048,320]{0,1:T(8,128)S(1)}, f32[2048,320]{0,1:T(8,128)}, u32[]{:S(2)}) copy-start(f32[2048,320]{0,1:T(8,128)} %param.11) | copy-start | bytes 7864324
  3.2 12.4 %collective-permute-start = (bf16[40,2048]{1,0:T(8,128)(2,1)}, bf16[40,2048]{1,0:T(8,128)(2,1)S(1)}, u32[]{:S(2)}, u32[]{:S(2)}) collective-permute-start(bf16[40,2048]{1,0:T(8,128)(2,1)} %get-tuple-element.43.refs_4_), channel_id=1, source_target_pairs={{0,16},{1,17},{2,18},{3,19},{4,20},{5,21},{6,22},{7,23},{8,24},{9,... | collective-permute-start | bytes 491528 | tf_op jit(solution)/shard_map/ppermute | solution.py:201
  7.4 9.1 %collective-permute-start.1 = (bf16[16,4096]{1,0:T(8,128)(2,1)}, bf16[16,4096]{1,0:T(8,128)(2,1)S(1)}, u32[]{:S(2)}, u32[]{:S(2)}) collective-permute-start(bf16[16,4096]{1,0:T(8,128)(2,1)} %get-tuple-element.48), channel_id=1, source_target_pairs={{0,2},{1,3},{2,0},{3,1},{4,6},{5,7},{6,4},{7,5},{8,10},{9,11},{10,... | collective-permute-start | bytes 393224 | tf_op jit(solution)/shard_map/ppermute | solution.py:162
  8.8 7.6 %collective-permute-start.2 = (bf16[16,4096]{1,0:T(8,128)(2,1)}, bf16[16,4096]{1,0:T(8,128)(2,1)S(1)}, u32[]{:S(2)}, u32[]{:S(2)}) collective-permute-start(bf16[16,4096]{1,0:T(8,128)(2,1)} %get-tuple-element.49), channel_id=1, source_target_pairs={{0,4},{1,5},{2,6},{3,7},{4,0},{5,1},{6,2},{7,3},{8,12},{9,13},{10,... | collective-permute-start | bytes 393224 | tf_op jit(solution)/shard_map/ppermute | solution.py:162
  10.4 6.9 %collective-permute-start.3 = (bf16[16,4096]{1,0:T(8,128)(2,1)}, bf16[16,4096]{1,0:T(8,128)(2,1)S(1)}, u32[]{:S(2)}, u32[]{:S(2)}) collective-permute-start(bf16[16,4096]{1,0:T(8,128)(2,1)} %get-tuple-element.50), channel_id=1, source_target_pairs={{0,8},{1,9},{2,10},{3,11},{4,12},{5,13},{6,14},{7,15},{8,0},{9,1},... | collective-permute-start | bytes 393224 | tf_op jit(solution)/shard_map/ppermute | solution.py:162
  11.9 6.1 %collective-permute-start.4 = (bf16[16,4096]{1,0:T(8,128)(2,1)}, bf16[16,4096]{1,0:T(8,128)(2,1)S(1)}, u32[]{:S(2)}, u32[]{:S(2)}) collective-permute-start(bf16[16,4096]{1,0:T(8,128)(2,1)} %get-tuple-element.51), channel_id=1, source_target_pairs={{0,6},{1,7},{2,4},{3,5},{4,2},{5,3},{6,0},{7,1},{8,14},{9,15},{10,... | collective-permute-start | bytes 393224 | tf_op jit(solution)/shard_map/ppermute | solution.py:162
  18.1 8.2 %collective-permute-start.6 = (bf16[40,4096]{1,0:T(8,128)(2,1)S(1)}, bf16[40,4096]{1,0:T(8,128)(2,1)S(1)}, u32[]{:S(2)}, u32[]{:S(2)}) collective-permute-start(bf16[40,4096]{1,0:T(8,128)(2,1)S(1)} %get-tuple-element.56), channel_id=1, source_target_pairs={{0,2},{1,3},{2,0},{3,1},{4,6},{5,7},{6,4},{7,5},{8,10},{9,11},{10,... | collective-permute-start | bytes 983048 | tf_op jit(solution)/shard_map/ppermute | solution.py:162
  18.7 7.6 %collective-permute-start.5 = (bf16[40,4096]{1,0:T(8,128)(2,1)S(1)}, bf16[40,4096]{1,0:T(8,128)(2,1)S(1)}, u32[]{:S(2)}, u32[]{:S(2)}) collective-permute-start(bf16[40,4096]{1,0:T(8,128)(2,1)S(1)} %get-tuple-element.56), channel_id=1, source_target_pairs={{0,4},{1,5},{2,6},{3,7},{4,0},{5,1},{6,2},{7,3},{8,12},{9,13},{10,... | collective-permute-start | bytes 983048 | tf_op jit(solution)/shard_map/ppermute | solution.py:162
  19.6 7.5 %collective-permute-start.7 = (bf16[40,4096]{1,0:T(8,128)(2,1)S(1)}, bf16[40,4096]{1,0:T(8,128)(2,1)S(1)}, u32[]{:S(2)}, u32[]{:S(2)}) collective-permute-start(bf16[40,4096]{1,0:T(8,128)(2,1)S(1)} %get-tuple-element.57), channel_id=1, source_target_pairs={{0,8},{1,9},{2,10},{3,11},{4,12},{5,13},{6,14},{7,15},{8,0},{9,1},... | collective-permute-start | bytes 983048 | tf_op jit(solution)/shard_map/ppermute | solution.py:162
  20.4 11.6 %collective-permute-start.8 = (bf16[640,2048]{1,0:T(8,128)(2,1)S(1)}, bf16[640,2048]{1,0:T(8,128)(2,1)S(1)}, u32[]{:S(2)}, u32[]{:S(2)}) collective-permute-start(bf16[640,2048]{1,0:T(8,128)(2,1)S(1)} %pad_maximum_fusion.1), channel_id=1, source_target_pairs={{0,1},{1,0},{2,3},{3,2},{4,5},{5,4},{6,7},{7,6},{8,9},{9,8},{10,11... | collective-permute-start | bytes 7864328 | tf_op jit(solution)/shard_map/ppermute | solution.py:162
  27.2 10.1 %collective-permute-start.12 = (bf16[24,4096]{1,0:T(8,128)(2,1)S(1)}, bf16[24,4096]{1,0:T(8,128)(2,1)S(1)}, u32[]{:S(2)}, u32[]{:S(2)}) collective-permute-start(bf16[24,4096]{1,0:T(8,128)(2,1)S(1)} %get-tuple-element.59), channel_id=1, source_target_pairs={{0,6},{1,7},{2,4},{3,5},{4,2},{5,3},{6,0},{7,1},{8,14},{9,15},{10,... | collective-permute-start | bytes 589832 | tf_op jit(solution)/shard_map/ppermute | solution.py:162
  29.3 8.0 %collective-permute-start.11 = (bf16[24,4096]{1,0:T(8,128)(2,1)S(1)}, bf16[24,4096]{1,0:T(8,128)(2,1)S(1)}, u32[]{:S(2)}, u32[]{:S(2)}) collective-permute-start(bf16[24,4096]{1,0:T(8,128)(2,1)S(1)} %get-tuple-element.59), channel_id=1, source_target_pairs={{0,2},{1,3},{2,0},{3,1},{4,6},{5,7},{6,4},{7,5},{8,10},{9,11},{10,... | collective-permute-start | bytes 589832 | tf_op jit(solution)/shard_map/ppermute | solution.py:162
  29.6 7.6 %collective-permute-start.10 = (bf16[24,4096]{1,0:T(8,128)(2,1)S(1)}, bf16[24,4096]{1,0:T(8,128)(2,1)S(1)}, u32[]{:S(2)}, u32[]{:S(2)}) collective-permute-start(bf16[24,4096]{1,0:T(8,128)(2,1)S(1)} %get-tuple-element.60), channel_id=1, source_target_pairs={{0,8},{1,9},{2,10},{3,11},{4,12},{5,13},{6,14},{7,15},{8,0},{9,1},... | collective-permute-start | bytes 589832 | tf_op jit(solution)/shard_map/ppermute | solution.py:162
  31.0 6.2 %collective-permute-start.9 = (bf16[24,4096]{1,0:T(8,128)(2,1)S(1)}, bf16[24,4096]{1,0:T(8,128)(2,1)S(1)}, u32[]{:S(2)}, u32[]{:S(2)}) collective-permute-start(bf16[24,4096]{1,0:T(8,128)(2,1)S(1)} %get-tuple-element.61), channel_id=1, source_target_pairs={{0,4},{1,5},{2,6},{3,7},{4,0},{5,1},{6,2},{7,3},{8,12},{9,13},{10,... | collective-permute-start | bytes 589832 | tf_op jit(solution)/shard_map/ppermute | solution.py:162
  40.5 8.2 %collective-permute-start.14 = (bf16[40,2048]{1,0:T(8,128)(2,1)S(1)}, bf16[40,2048]{1,0:T(8,128)(2,1)S(1)}, u32[]{:S(2)}, u32[]{:S(2)}) collective-permute-start(bf16[40,2048]{1,0:T(8,128)(2,1)S(1)} %pad_maximum_fusion.19), channel_id=1, source_target_pairs={{0,6},{1,7},{2,4},{3,5},{4,2},{5,3},{6,0},{7,1},{8,14},{9,15},{10,... | collective-permute-start | bytes 491528 | tf_op jit(solution)/shard_map/ppermute | solution.py:162
  41.6 7.1 %collective-permute-start.13 = (bf16[40,2048]{1,0:T(8,128)(2,1)S(1)}, bf16[40,2048]{1,0:T(8,128)(2,1)S(1)}, u32[]{:S(2)}, u32[]{:S(2)}) collective-permute-start(bf16[40,2048]{1,0:T(8,128)(2,1)S(1)} %pad_maximum_fusion.20), channel_id=1, source_target_pairs={{0,2},{1,3},{2,0},{3,1},{4,6},{5,7},{6,4},{7,5},{8,10},{9,11},{10,... | collective-permute-start | bytes 491528 | tf_op jit(solution)/shard_map/ppermute | solution.py:162
  43.2 6.1 %collective-permute-start.16 = (bf16[40,2048]{1,0:T(8,128)(2,1)S(1)}, bf16[40,2048]{1,0:T(8,128)(2,1)S(1)}, u32[]{:S(2)}, u32[]{:S(2)}) collective-permute-start(bf16[40,2048]{1,0:T(8,128)(2,1)S(1)} %get-tuple-element.67), channel_id=1, source_target_pairs={{0,4},{1,5},{2,6},{3,7},{4,0},{5,1},{6,2},{7,3},{8,12},{9,13},{10,... | collective-permute-start | bytes 491528 | tf_op jit(solution)/shard_map/ppermute | solution.py:162
  44.3 7.5 %collective-permute-start.18 = (bf16[40,2048]{1,0:T(8,128)(2,1)S(1)}, bf16[40,2048]{1,0:T(8,128)(2,1)S(1)}, u32[]{:S(2)}, u32[]{:S(2)}) collective-permute-start(bf16[40,2048]{1,0:T(8,128)(2,1)S(1)} %get-tuple-element.69), channel_id=1, source_target_pairs={{0,8},{1,9},{2,10},{3,11},{4,12},{5,13},{6,14},{7,15},{8,0},{9,1},... | collective-permute-start | bytes 491528 | tf_op jit(solution)/shard_map/ppermute | solution.py:162
  48.8 8.3 %collective-permute-start.15 = (bf16[40,2048]{1,0:T(8,128)(2,1)S(1)}, bf16[40,2048]{1,0:T(8,128)(2,1)S(1)}, u32[]{:S(2)}, u32[]{:S(2)}) collective-permute-start(bf16[40,2048]{1,0:T(8,128)(2,1)S(1)} %add_convert_fusion.3), channel_id=1, source_target_pairs={{0,8},{1,9},{2,10},{3,11},{4,12},{5,13},{6,14},{7,15},{8,0},{9,1},... | collective-permute-start | bytes 491528 | tf_op jit(solution)/shard_map/ppermute | solution.py:162
  49.3 7.9 %collective-permute-start.17 = (bf16[40,2048]{1,0:T(8,128)(2,1)S(1)}, bf16[40,2048]{1,0:T(8,128)(2,1)S(1)}, u32[]{:S(2)}, u32[]{:S(2)}) collective-permute-start(bf16[40,2048]{1,0:T(8,128)(2,1)S(1)} %add_convert_fusion.2), channel_id=1, source_target_pairs={{0,2},{1,3},{2,0},{3,1},{4,6},{5,7},{6,4},{7,5},{8,10},{9,11},{10,... | collective-permute-start | bytes 491528 | tf_op jit(solution)/shard_map/ppermute | solution.py:162
  51.8 5.4 %collective-permute-start.19 = (bf16[40,2048]{1,0:T(8,128)(2,1)S(1)}, bf16[40,2048]{1,0:T(8,128)(2,1)S(1)}, u32[]{:S(2)}, u32[]{:S(2)}) collective-permute-start(bf16[40,2048]{1,0:T(8,128)(2,1)S(1)} %add_convert_fusion.1), channel_id=1, source_target_pairs={{0,4},{1,5},{2,6},{3,7},{4,0},{5,1},{6,2},{7,3},{8,12},{9,13},{10,... | collective-permute-start | bytes 491528 | tf_op jit(solution)/shard_map/ppermute | solution.py:162
  52.6 9.2 %collective-permute-start.21 = (bf16[320,2048]{1,0:T(8,128)(2,1)S(1)}, bf16[320,2048]{1,0:T(8,128)(2,1)S(1)}, u32[]{:S(2)}, u32[]{:S(2)}) collective-permute-start(bf16[320,2048]{1,0:T(8,128)(2,1)S(1)} %fusion.13), channel_id=1, source_target_pairs={{0,1},{1,0},{2,3},{3,2},{4,5},{5,4},{6,7},{7,6},{8,9},{9,8},{10,11... | collective-permute-start | bytes 3932168 | tf_op jit(solution)/shard_map/ppermute | solution.py:162
  53.3 10.9 %collective-permute-start.20 = (bf16[320,2048]{1,0:T(8,128)(2,1)S(1)}, bf16[320,2048]{1,0:T(8,128)(2,1)S(1)}, u32[]{:S(2)}, u32[]{:S(2)}) collective-permute-start(bf16[320,2048]{1,0:T(8,128)(2,1)S(1)} %fusion.12), channel_id=1, source_target_pairs={{0,1},{1,0},{2,3},{3,2},{4,5},{5,4},{6,7},{7,6},{8,9},{9,8},{10,11... | collective-permute-start | bytes 3932168 | tf_op jit(solution)/shard_map/ppermute | solution.py:162
  57.3 9.2 %collective-permute-start.22 = (bf16[40,1024]{1,0:T(8,128)(2,1)S(1)}, bf16[40,1024]{1,0:T(8,128)(2,1)S(1)}, u32[]{:S(2)}, u32[]{:S(2)}) collective-permute-start(bf16[40,1024]{1,0:T(8,128)(2,1)S(1)} %pad_maximum_fusion.23), channel_id=1, source_target_pairs={{0,16},{1,17},{2,18},{3,19},{4,20},{5,21},{6,22},{7,23},{8,24},{9,... | collective-permute-start | bytes 245768 | tf_op jit(solution)/shard_map/ppermute | solution.py:201
  (5 other events, 20.2 us)

commit v12 on v11

--- a/solution.py
+++ b/solution.py
@@ -124,25 +124,6 @@
     )(*copies, *sent)
 
 
-def unpack_kernel(own_ref, *refs):
-    *refs, out_ref = refs
-    crossings = len(refs) // 3
-    picks, rows = refs[: 2 * crossings], refs[2 * crossings :]
-    half = out_ref.shape[1] // 2
-    for side in range(2):
-        columns = slice(side * half, (side + 1) * half)
-        both = own_ref[:, columns].astype(jnp.float32)
-        for pick_ref, rows_ref in zip(picks[side::2], rows):
-            both = both + contract_rows(pick_ref[...], rows_ref[...])
-        out_ref[:, columns] = both.astype(jnp.bfloat16)
-
-
-def unpacked(own_grad, picks, crossed):
-    return pl.pallas_call(
-        unpack_kernel, out_shape=jax.ShapeDtypeStruct(own_grad.shape, own_grad.dtype)
-    )(own_grad, *picks, *crossed)
-
-
 def whole_weights(shard):
     if lax.axis_size("dp") == 1:
         return shard.astype(jnp.bfloat16)
@@ -170,11 +151,15 @@
     return lax.optimization_barrier((others, values))[1]
 
 
-def swaps(blocks, masks):
+def chain(blocks):
     chained = []
     for block in blocks:
         chained.append(after(block, chained[-1]) if chained else block)
-    return [swap(block, mask) for block, mask in zip(chained, masks)]
+    return chained
+
+
+def swaps(blocks, masks):
+    return [swap(block, mask) for block, mask in zip(chain(blocks), masks)]
 
 
 def total(*terms):
@@ -253,17 +238,7 @@
     )
     early = activated(jnp.concatenate(early_rows, axis=0))
     early_parts = input_parts(early[3])
-    mine, theirs = slice(0, units), slice(units, 2 * units)
-
-    def gradients(chunk):
-        return [
-            contract_rows(chunk[left][:, part], chunk[right])
-            for left, right in ((3, 0), (2, 1))
-            for part in (mine, theirs)
-        ]
-
-    early_gradients = gradients(early)
-    late_far = after([late_xy, late_yz, late_zx, late_far], early_parts, early_gradients)
+    late_far = after([late_xy, late_yz, late_zx, late_far], early_parts)
     late_rows = [late_own, late_x, late_y, late_z, *late_far]
     later = activated(jnp.concatenate(late_rows, axis=0))
     late_parts = input_parts(later[3])
@@ -272,16 +247,21 @@
         for pair in zip(split_rows(early_parts, first), split_rows(late_parts, rest))
     ]
     own, sum_x, sum_y, sum_z, sum_xy, sum_yz, sum_zx, sum_far = parts
-    far, zx, xy, yz = swaps(
-        [sum_far, sum_zx, sum_xy, sum_yz], (x_bit | y_bit, x_bit, y_bit, z_bit)
-    )
-    in_mine, in_theirs, out_mine, out_theirs = [
-        sum(pair) * scale
-        for pair, scale in zip(
-            zip(early_gradients, gradients(later[:2] + after(later[2:], zx))),
-            (scale_in, scale_in, scale_out, scale_out),
-        )
+    back = chain([sum_far, sum_zx, sum_xy, sum_yz])
+    far, zx, xy, yz = [
+        swap(rows, mask) for rows, mask in zip(back, (x_bit | y_bit, x_bit, y_bit, z_bit))
     ]
+
+    def gradients(part, awaited):
+        chunks = [chunk[:2] + after(chunk[2:], awaited) for chunk in (early, later)]
+        return [
+            sum(contract_rows(chunk[left][:, part], chunk[right]) for chunk in chunks) * scale
+            for left, right, scale in ((3, 0, scale_in), (2, 1, scale_out))
+        ]
+
+    in_mine, out_mine = gradients(slice(0, units), back[-1])
+    zx = after(zx, in_mine, out_mine)
+    in_theirs, out_theirs = gradients(slice(units, 2 * units), zx)
     in_shared = swap(in_theirs.astype(jnp.bfloat16), core_bit).astype(jnp.float32)
     out_shared = swap(out_theirs.astype(jnp.bfloat16), core_bit).astype(jnp.float32)
     new_w_in = stepped(w_in, (in_mine + in_shared).T)
@@ -292,16 +272,15 @@
     sums = total(own, *near)
     early_sum, late_sum = sums[:first], sums[first:]
     half = width // 2
-    crossed = []
+    returned = [early_sum, late_sum]
     for s in range(1, experts):
         rows = late_sum[(s - 1) * capacity : s * capacity]
-        crossed.append(
-            shifted(jnp.concatenate([rows[:, :half], rows[:, half:]], axis=0), -s)
-        )
-    crossed = after(crossed, new_w_in, new_w_out)
-    own_grad = contract_rows(picks[0], early_sum) + contract_rows(picks[1], late_sum)
-    token_grad = unpacked(own_grad.astype(jnp.bfloat16), picks[2:], crossed)
-    return (token_grad, new_w_in, new_w_out)
+        rows = jnp.concatenate([rows[:, :half], rows[:, half:]], axis=0)
+        rows = after(shifted(rows, -s), new_w_in, new_w_out)
+        returned.append(jnp.concatenate(split_rows(rows, capacity), axis=1))
+    picks = [*picks[:2], *[pick[:capacity] for pick in picks[2::2]]]
+    token_grad = sum(contract_rows(pick, rows) for pick, rows in zip(picks, returned))
+    return (token_grad.astype(jnp.bfloat16), new_w_in, new_w_out)
 
 
 def solution(mesh):

time: 69.3 us -> 67 us (0.967)
  other arithmetic: 2.69 us -> 7.43 us
  matrix products: 15.1 us -> 11.8 us
  waiting for transfers between devices: 15.2 us -> 12.7 us
  Pallas kernels: 4.56 us -> 2.6 us
  starting transfers between devices: 27.7 us -> 29.2 us
  local copies, waits for them, and re-layouts: 2.79 us -> 2.04 us
    sub x0 -> x2, other arithmetic: none -> 4.59 us  [stepped(): return weights - step_rate * grads]
    dot_general x10 -> x11, matrix products: 9.42 us -> 6.03 us  [contract_rows(): lax.dot_general(left, right, (((0,), (0,)), ((), ())), preferred_element_...]
    ppermute x21, waiting for transfers between devices: 15.2 us -> 12.7 us  [swap(): lax.ppermute(rows, 'expert', [(i, i ^ mask) for i in range(n_expert)])]
    pallas_call x1 -> x0, Pallas kernels: 1.96 us -> none  [unpacked(): pl.pallas_call(unpack_kernel, out_shape=jax.ShapeDtypeStruct(own_grad.sha...]
    ppermute x2, starting transfers between devices: 7.4 us -> 8.79 us  [shifted(): return lax.ppermute(rows, 'expert', pairs)]
    unnamed x22, local copies, waits for them, and re-layouts: 2.36 us -> 1.6 us
  transfers between devices with their start and end apart: 23 -> 23, of which waited for: 7 -> 8; matrix products, arithmetic and copies ran while one was open for 23% -> 24% of each run, Pallas kernels for 0% -> 0%
where the time goes in v12:
time: 67 us; the launch traced here: 66.8 us
  starting transfers between devices  29.2 us (44%)
  waiting for transfers between devices  12.7 us (19%)
  matrix products  11.8 us (18%)
  other arithmetic  7.43 us (11%)
  Pallas kernels  2.6 us (4%)
  local copies, waits for them, and re-layouts  2.04 us (3%)
  between operations  1.07 us (2%)
    ppermute x21, starting transfers between devices, swap(): lax.ppermute(rows, 'expert', [(i, i ^ mask) for i in range(n_expert)])  20.4 us
    ppermute x21, waiting for transfers between devices, swap(): lax.ppermute(rows, 'expert', [(i, i ^ mask) for i in range(n_expert)])  12.7 us
    ppermute x2, starting transfers between devices, shifted(): return lax.ppermute(rows, 'expert', pairs)  8.79 us
    dot_general x11, matrix products, contract_rows(): lax.dot_general(left, right, (((0,), (0,)), ((), ())), preferred_element_...  6.03 us
    sub x2, other arithmetic, stepped(): return weights - step_rate * grads  4.59 us
    dot_general x4, matrix products, contract_cols(): lax.dot_general(left, right, (((1,), (1,)), ((), ())), preferred_element_...  4.34 us
    pallas_call x1, Pallas kernels, pack(): pl.pallas_call(lambda *refs: pack_kernel(blocks, experts, *refs), out_sha...  2.6 us
    transpose x1, other arithmetic, shards(): whole_weights(w_in)  1.92 us
  transfers between devices with their start and end apart: 23, of which 8 were waited for; matrix products, arithmetic and copies ran while one was open for 24% of the time, Pallas kernels for 0%

profile of v12, /device:TPU:0, one launch (start us, length us, event | category | flops | bytes accessed | tf_op | source)
XLA Modules:
  0.0 66.8 jit_solution(11171295918656726643)
XLA Ops:
  0.6 2.6 %shard_map.85 = (bf16[16,4096]{1,0:T(8,128)(2,1)}, bf16[24,4096]{1,0:T(8,128)(2,1)}, bf16[40,2048]{1,0:T(8,128)(2,1)}, bf16[16,64]{1,0:T(8,128)(2,1)}, bf16[24,6...) custom-call(s32[1,64]{1,0:T(1,128)} %bitcast.16, ...), custom_call_target="tpu_custom_call" | custom-call | tf_op jit(solution)/shard_map/pallas_call | solution.py:106
  3.2 4.1 %collective-permute-start = (bf16[40,2048]{1,0:T(8,128)(2,1)}, bf16[40,2048]{1,0:T(8,128)(2,1)S(1)}, u32[]{:S(2)}, u32[]{:S(2)}) collective-permute-start(bf16[40,2048]{1,0:T(8,128)(2,1)} %get-tuple-element.49.refs_4_), channel_id=1, source_target_pairs={{0,16},{1,17},{2,18},{3,19},{4,20},{5,21},{6,22},{7,23},{8,24},{9,... | collective-permute-start | bytes 491528 | tf_op jit(solution)/shard_map/ppermute | solution.py:186
  7.4 1.5 %collective-permute-start.1 = (bf16[16,4096]{1,0:T(8,128)(2,1)}, bf16[16,4096]{1,0:T(8,128)(2,1)S(1)}, u32[]{:S(2)}, u32[]{:S(2)}) collective-permute-start(bf16[16,4096]{1,0:T(8,128)(2,1)} %get-tuple-element.54), channel_id=1, source_target_pairs={{0,2},{1,3},{2,0},{3,1},{4,6},{5,7},{6,4},{7,5},{8,10},{9,11},{10,... | collective-permute-start | bytes 393224 | tf_op jit(solution)/shard_map/ppermute | solution.py:143
  8.8 1.5 %collective-permute-start.2 = (bf16[16,4096]{1,0:T(8,128)(2,1)}, bf16[16,4096]{1,0:T(8,128)(2,1)S(1)}, u32[]{:S(2)}, u32[]{:S(2)}) collective-permute-start(bf16[16,4096]{1,0:T(8,128)(2,1)} %get-tuple-element.55), channel_id=1, source_target_pairs={{0,4},{1,5},{2,6},{3,7},{4,0},{5,1},{6,2},{7,3},{8,12},{9,13},{10,... | collective-permute-start | bytes 393224 | tf_op jit(solution)/shard_map/ppermute | solution.py:143
  10.4 1.6 %collective-permute-start.3 = (bf16[16,4096]{1,0:T(8,128)(2,1)}, bf16[16,4096]{1,0:T(8,128)(2,1)S(1)}, u32[]{:S(2)}, u32[]{:S(2)}) collective-permute-start(bf16[16,4096]{1,0:T(8,128)(2,1)} %get-tuple-element.56), channel_id=1, source_target_pairs={{0,8},{1,9},{2,10},{3,11},{4,12},{5,13},{6,14},{7,15},{8,0},{9,1},... | collective-permute-start | bytes 393224 | tf_op jit(solution)/shard_map/ppermute | solution.py:143
  13.3 1.9 %convert_bitcast_fusion = bf16[320,2048]{1,0:T(8,128)(2,1)S(1)} fusion(f32[2048,320]{0,1:T(8,128)} %param.10), kind=kLoop, calls=%fused_computation.24 | loop fusion | flops 655360 | bytes 3932160 | tf_op jit(solution)/shard_map/transpose | solution.py:229
  20.5 5.7 %collective-permute-done.6 = bf16[40,4096]{1,0:T(8,128)(2,1)S(1)} collective-permute-done((bf16[40,4096]{1,0:T(8,128)(2,1)S(1)}, bf16[40,4096]{1,0:T(8,128)(2,1)S(1)}, u32[]{:S(2)}, u32[]{:S(2)}) %collective-permute-start.6) | collective-permute-done | bytes 327712 | tf_op jit(solution)/shard_map/ppermute | solution.py:143
  27.2 2.1 %collective-permute-start.12 = (bf16[24,4096]{1,0:T(8,128)(2,1)S(1)}, bf16[24,4096]{1,0:T(8,128)(2,1)S(1)}, u32[]{:S(2)}, u32[]{:S(2)}) collective-permute-start(bf16[24,4096]{1,0:T(8,128)(2,1)S(1)} %get-tuple-element.65), channel_id=1, source_target_pairs={{0,6},{1,7},{2,4},{3,5},{4,2},{5,3},{6,0},{7,1},{8,14},{9,15},{10,... | collective-permute-start | bytes 589832 | tf_op jit(solution)/shard_map/ppermute | solution.py:143
  29.6 1.4 %collective-permute-start.10 = (bf16[24,4096]{1,0:T(8,128)(2,1)S(1)}, bf16[24,4096]{1,0:T(8,128)(2,1)S(1)}, u32[]{:S(2)}, u32[]{:S(2)}) collective-permute-start(bf16[24,4096]{1,0:T(8,128)(2,1)S(1)} %get-tuple-element.66), channel_id=1, source_target_pairs={{0,8},{1,9},{2,10},{3,11},{4,12},{5,13},{6,14},{7,15},{8,0},{9,1},... | collective-permute-start | bytes 589832 | tf_op jit(solution)/shard_map/ppermute | solution.py:143
  31.0 1.0 %collective-permute-start.9 = (bf16[24,4096]{1,0:T(8,128)(2,1)S(1)}, bf16[24,4096]{1,0:T(8,128)(2,1)S(1)}, u32[]{:S(2)}, u32[]{:S(2)}) collective-permute-start(bf16[24,4096]{1,0:T(8,128)(2,1)S(1)} %get-tuple-element.67), channel_id=1, source_target_pairs={{0,4},{1,5},{2,6},{3,7},{4,0},{5,1},{6,2},{7,3},{8,12},{9,13},{10,... | collective-permute-start | bytes 589832 | tf_op jit(solution)/shard_map/ppermute | solution.py:143
  32.3 1.0 %multiply_convert_fusion.1 = (bf16[128,640]{1,0:T(8,128)(2,1)S(1)}, f32[128,640]{1,0:T(8,128)S(1)}) fusion(bf16[320,2048]{1,0:T(8,128)(2,1)S(1)} %convert_bitcast_fusion, bf16[320,2048]{1,0:T(8,128)(2,1)S(1)} %get-tuple-element.91, bf16[128,4096]{1,0:T(8,128)(2,1)S(1)} %slice_dynamic-update-slice_fusion), kind=kOutput, calls=%fused_computation.67 | convolution fusion | flops 341606400 | bytes 3637248 | tf_op jit(solution)/shard_map/dot_general | solution.py:39
  33.3 1.0 %fusion.16 = bf16[128,640]{1,0:T(8,128)(2,1)S(1)} fusion(bf16[320,2048]{1,0:T(8,128)(2,1)S(1)} %get-tuple-element.92, bf16[320,2048]{1,0:T(8,128)(2,1)S(1)} %convert_bitcast_fusion.1, bf16[128,4096]{1,0:T(8,128)(2,1)S(1)} %slice_dynamic-update-slice_fusion, f32[128,640]{1,0:T(8,128)S(1)} %get-tuple-element.126), kind=kOutput, calls=%fused_computation.31 | convolution fusion | flops 342507520 | bytes 3637248 | tf_op jit(solution)/shard_map/dot_general | solution.py:39
  35.0 1.7 %collective-permute-done.9 = bf16[24,4096]{1,0:T(8,128)(2,1)S(1)} collective-permute-done((bf16[24,4096]{1,0:T(8,128)(2,1)S(1)}, bf16[24,4096]{1,0:T(8,128)(2,1)S(1)}, u32[]{:S(2)}, u32[]{:S(2)}) %collective-permute-start.9) | collective-permute-done | bytes 196640 | tf_op jit(solution)/shard_map/ppermute | solution.py:143
  36.8 1.1 %multiply_convert_fusion = (bf16[192,640]{1,0:T(8,128)(2,1)S(1)}, f32[192,640]{1,0:T(8,128)S(1)}) fusion(bf16[320,2048]{1,0:T(8,128)(2,1)S(1)} %convert_bitcast_fusion, bf16[320,2048]{1,0:T(8,128)(2,1)S(1)} %get-tuple-element.91, bf16[192,4096]{1,0:T(8,128)(2,1)S(1)} %constant_dynamic-update-slice_fusion.5), kind=kOutput, calls=%fused_computation.46 | convolution fusion | flops 509788160 | bytes 4145152 | tf_op jit(solution)/shard_map/dot_general | solution.py:39
  37.9 1.2 %fusion.13 = bf16[192,640]{1,0:T(8,128)(2,1)S(1)} fusion(bf16[320,2048]{1,0:T(8,128)(2,1)S(1)} %get-tuple-element.92, bf16[320,2048]{1,0:T(8,128)(2,1)S(1)} %convert_bitcast_fusion.1, bf16[192,4096]{1,0:T(8,128)(2,1)S(1)} %constant_dynamic-update-slice_fusion.5, f32[192,640]{1,0:T(8,128)S(1)} %get-tuple-element.124), kind=kOutput, calls=%fused_computation.28 | convolution fusion | flops 511139840 | bytes 4145152 | tf_op jit(solution)/shard_map/dot_general | solution.py:39
  40.1 1.5 %collective-permute-start.14 = (bf16[40,2048]{1,0:T(8,128)(2,1)S(1)}, bf16[40,2048]{1,0:T(8,128)(2,1)S(1)}, u32[]{:S(2)}, u32[]{:S(2)}) collective-permute-start(bf16[40,2048]{1,0:T(8,128)(2,1)S(1)} %pad_maximum_fusion.19), channel_id=1, source_target_pairs={{0,6},{1,7},{2,4},{3,5},{4,2},{5,3},{6,0},{7,1},{8,14},{9,15},{10,... | collective-permute-start | bytes 491528 | tf_op jit(solution)/shard_map/ppermute | solution.py:143
  41.6 1.1 %collective-permute-start.13 = (bf16[40,2048]{1,0:T(8,128)(2,1)S(1)}, bf16[40,2048]{1,0:T(8,128)(2,1)S(1)}, u32[]{:S(2)}, u32[]{:S(2)}) collective-permute-start(bf16[40,2048]{1,0:T(8,128)(2,1)S(1)} %get-tuple-element.72), channel_id=1, source_target_pairs={{0,2},{1,3},{2,0},{3,1},{4,6},{5,7},{6,4},{7,5},{8,10},{9,11},{10,... | collective-permute-start | bytes 491528 | tf_op jit(solution)/shard_map/ppermute | solution.py:143
  42.7 1.0 %collective-permute-start.16 = (bf16[40,2048]{1,0:T(8,128)(2,1)S(1)}, bf16[40,2048]{1,0:T(8,128)(2,1)S(1)}, u32[]{:S(2)}, u32[]{:S(2)}) collective-permute-start(bf16[40,2048]{1,0:T(8,128)(2,1)S(1)} %get-tuple-element.73), channel_id=1, source_target_pairs={{0,4},{1,5},{2,6},{3,7},{4,0},{5,1},{6,2},{7,3},{8,12},{9,13},{10,... | collective-permute-start | bytes 491528 | tf_op jit(solution)/shard_map/ppermute | solution.py:143
  43.7 1.4 %collective-permute-start.18 = (bf16[40,2048]{1,0:T(8,128)(2,1)S(1)}, bf16[40,2048]{1,0:T(8,128)(2,1)S(1)}, u32[]{:S(2)}, u32[]{:S(2)}) collective-permute-start(bf16[40,2048]{1,0:T(8,128)(2,1)S(1)} %pad_maximum_fusion.22), channel_id=1, source_target_pairs={{0,8},{1,9},{2,10},{3,11},{4,12},{5,13},{6,14},{7,15},{8,0},{9,1},... | collective-permute-start | bytes 491528 | tf_op jit(solution)/shard_map/ppermute | solution.py:143
  50.4 1.2 %collective-permute-start.19 = (bf16[40,2048]{1,0:T(8,128)(2,1)S(1)}, bf16[40,2048]{1,0:T(8,128)(2,1)S(1)}, u32[]{:S(2)}, u32[]{:S(2)}) collective-permute-start(bf16[40,2048]{1,0:T(8,128)(2,1)S(1)} %add_convert_fusion.1), channel_id=1, source_target_pairs={{0,4},{1,5},{2,6},{3,7},{4,0},{5,1},{6,2},{7,3},{8,12},{9,13},{10,... | collective-permute-start | bytes 491528 | tf_op jit(solution)/shard_map/ppermute | solution.py:143
  54.8 1.0 %collective-permute-done.19 = bf16[40,2048]{1,0:T(8,128)(2,1)S(1)} collective-permute-done((bf16[40,2048]{1,0:T(8,128)(2,1)S(1)}, bf16[40,2048]{1,0:T(8,128)(2,1)S(1)}, u32[]{:S(2)}, u32[]{:S(2)}) %collective-permute-start.19) | collective-permute-done | bytes 163872 | tf_op jit(solution)/shard_map/ppermute | solution.py:143
  56.0 4.7 %collective-permute-start.22 = (bf16[40,1024]{1,0:T(8,128)(2,1)S(1)}, bf16[40,1024]{1,0:T(8,128)(2,1)S(1)}, u32[]{:S(2)}, u32[]{:S(2)}) collective-permute-start(bf16[40,1024]{1,0:T(8,128)(2,1)S(1)} %pad_maximum_fusion.23), channel_id=1, source_target_pairs={{0,16},{1,17},{2,18},{3,19},{4,20},{5,21},{6,22},{7,23},{8,24},{9,... | collective-permute-start | bytes 245768 | tf_op jit(solution)/shard_map/ppermute | solution.py:186
  61.2 2.3 %bitcast_subtract_fusion = f32[2048,320]{0,1:T(8,128)} fusion(f32[2048,320]{0,1:T(8,128)S(1)} %copy-done, f32[320,2048]{1,0:T(8,128)S(1)} %fusion.2, bf16[320,2048]{1,0:T(8,128)(2,1)S(1)} %collective-permute-done.21), kind=kLoop, calls=%fused_computation.13 | loop fusion | flops 2621440 | bytes 9175040 | tf_op jit(solution)/shard_map/sub | solution.py:138
  63.5 2.3 %bitcast_subtract_fusion.1 = f32[2048,320]{0,1:T(8,128)} fusion(f32[2048,320]{0,1:T(8,128)S(1)} %copy-done.1, f32[320,2048]{1,0:T(8,128)S(1)} %fusion.3, bf16[320,2048]{1,0:T(8,128)(2,1)S(1)} %collective-permute-done.20), kind=kLoop, calls=%fused_computation.14 | loop fusion | flops 2621440 | bytes 9175040 | tf_op jit(solution)/shard_map/sub | solution.py:138
  (89 shorter events, 19.7 us)
Async XLA Ops:
  0.6 14.6 %copy-start = (f32[2048,320]{0,1:T(8,128)S(1)}, f32[2048,320]{0,1:T(8,128)}, u32[]{:S(2)}) copy-start(f32[2048,320]{0,1:T(8,128)} %param.11) | copy-start | bytes 7864324
  3.2 12.6 %collective-permute-start = (bf16[40,2048]{1,0:T(8,128)(2,1)}, bf16[40,2048]{1,0:T(8,128)(2,1)S(1)}, u32[]{:S(2)}, u32[]{:S(2)}) collective-permute-start(bf16[40,2048]{1,0:T(8,128)(2,1)} %get-tuple-element.49.refs_4_), channel_id=1, source_target_pairs={{0,16},{1,17},{2,18},{3,19},{4,20},{5,21},{6,22},{7,23},{8,24},{9,... | collective-permute-start | bytes 491528 | tf_op jit(solution)/shard_map/ppermute | solution.py:186
  7.4 9.1 %collective-permute-start.1 = (bf16[16,4096]{1,0:T(8,128)(2,1)}, bf16[16,4096]{1,0:T(8,128)(2,1)S(1)}, u32[]{:S(2)}, u32[]{:S(2)}) collective-permute-start(bf16[16,4096]{1,0:T(8,128)(2,1)} %get-tuple-element.54), channel_id=1, source_target_pairs={{0,2},{1,3},{2,0},{3,1},{4,6},{5,7},{6,4},{7,5},{8,10},{9,11},{10,... | collective-permute-start | bytes 393224 | tf_op jit(solution)/shard_map/ppermute | solution.py:143
  8.8 7.6 %collective-permute-start.2 = (bf16[16,4096]{1,0:T(8,128)(2,1)}, bf16[16,4096]{1,0:T(8,128)(2,1)S(1)}, u32[]{:S(2)}, u32[]{:S(2)}) collective-permute-start(bf16[16,4096]{1,0:T(8,128)(2,1)} %get-tuple-element.55), channel_id=1, source_target_pairs={{0,4},{1,5},{2,6},{3,7},{4,0},{5,1},{6,2},{7,3},{8,12},{9,13},{10,... | collective-permute-start | bytes 393224 | tf_op jit(solution)/shard_map/ppermute | solution.py:143
  10.4 6.9 %collective-permute-start.3 = (bf16[16,4096]{1,0:T(8,128)(2,1)}, bf16[16,4096]{1,0:T(8,128)(2,1)S(1)}, u32[]{:S(2)}, u32[]{:S(2)}) collective-permute-start(bf16[16,4096]{1,0:T(8,128)(2,1)} %get-tuple-element.56), channel_id=1, source_target_pairs={{0,8},{1,9},{2,10},{3,11},{4,12},{5,13},{6,14},{7,15},{8,0},{9,1},... | collective-permute-start | bytes 393224 | tf_op jit(solution)/shard_map/ppermute | solution.py:143
  11.9 6.1 %collective-permute-start.4 = (bf16[16,4096]{1,0:T(8,128)(2,1)}, bf16[16,4096]{1,0:T(8,128)(2,1)S(1)}, u32[]{:S(2)}, u32[]{:S(2)}) collective-permute-start(bf16[16,4096]{1,0:T(8,128)(2,1)} %get-tuple-element.57), channel_id=1, source_target_pairs={{0,6},{1,7},{2,4},{3,5},{4,2},{5,3},{6,0},{7,1},{8,14},{9,15},{10,... | collective-permute-start | bytes 393224 | tf_op jit(solution)/shard_map/ppermute | solution.py:143
  18.1 8.2 %collective-permute-start.6 = (bf16[40,4096]{1,0:T(8,128)(2,1)S(1)}, bf16[40,4096]{1,0:T(8,128)(2,1)S(1)}, u32[]{:S(2)}, u32[]{:S(2)}) collective-permute-start(bf16[40,4096]{1,0:T(8,128)(2,1)S(1)} %get-tuple-element.62), channel_id=1, source_target_pairs={{0,2},{1,3},{2,0},{3,1},{4,6},{5,7},{6,4},{7,5},{8,10},{9,11},{10,... | collective-permute-start | bytes 983048 | tf_op jit(solution)/shard_map/ppermute | solution.py:143
  18.7 7.6 %collective-permute-start.5 = (bf16[40,4096]{1,0:T(8,128)(2,1)S(1)}, bf16[40,4096]{1,0:T(8,128)(2,1)S(1)}, u32[]{:S(2)}, u32[]{:S(2)}) collective-permute-start(bf16[40,4096]{1,0:T(8,128)(2,1)S(1)} %get-tuple-element.62), channel_id=1, source_target_pairs={{0,4},{1,5},{2,6},{3,7},{4,0},{5,1},{6,2},{7,3},{8,12},{9,13},{10,... | collective-permute-start | bytes 983048 | tf_op jit(solution)/shard_map/ppermute | solution.py:143
  19.6 7.5 %collective-permute-start.7 = (bf16[40,4096]{1,0:T(8,128)(2,1)S(1)}, bf16[40,4096]{1,0:T(8,128)(2,1)S(1)}, u32[]{:S(2)}, u32[]{:S(2)}) collective-permute-start(bf16[40,4096]{1,0:T(8,128)(2,1)S(1)} %get-tuple-element.63), channel_id=1, source_target_pairs={{0,8},{1,9},{2,10},{3,11},{4,12},{5,13},{6,14},{7,15},{8,0},{9,1},... | collective-permute-start | bytes 983048 | tf_op jit(solution)/shard_map/ppermute | solution.py:143
  20.4 11.6 %collective-permute-start.8 = (bf16[640,2048]{1,0:T(8,128)(2,1)S(1)}, bf16[640,2048]{1,0:T(8,128)(2,1)S(1)}, u32[]{:S(2)}, u32[]{:S(2)}) collective-permute-start(bf16[640,2048]{1,0:T(8,128)(2,1)S(1)} %pad_maximum_fusion.1), channel_id=1, source_target_pairs={{0,1},{1,0},{2,3},{3,2},{4,5},{5,4},{6,7},{7,6},{8,9},{9,8},{10,11... | collective-permute-start | bytes 7864328 | tf_op jit(solution)/shard_map/ppermute | solution.py:143
  27.2 9.5 %collective-permute-start.12 = (bf16[24,4096]{1,0:T(8,128)(2,1)S(1)}, bf16[24,4096]{1,0:T(8,128)(2,1)S(1)}, u32[]{:S(2)}, u32[]{:S(2)}) collective-permute-start(bf16[24,4096]{1,0:T(8,128)(2,1)S(1)} %get-tuple-element.65), channel_id=1, source_target_pairs={{0,6},{1,7},{2,4},{3,5},{4,2},{5,3},{6,0},{7,1},{8,14},{9,15},{10,... | collective-permute-start | bytes 589832 | tf_op jit(solution)/shard_map/ppermute | solution.py:143
  29.3 7.5 %collective-permute-start.11 = (bf16[24,4096]{1,0:T(8,128)(2,1)S(1)}, bf16[24,4096]{1,0:T(8,128)(2,1)S(1)}, u32[]{:S(2)}, u32[]{:S(2)}) collective-permute-start(bf16[24,4096]{1,0:T(8,128)(2,1)S(1)} %get-tuple-element.65), channel_id=1, source_target_pairs={{0,2},{1,3},{2,0},{3,1},{4,6},{5,7},{6,4},{7,5},{8,10},{9,11},{10,... | collective-permute-start | bytes 589832 | tf_op jit(solution)/shard_map/ppermute | solution.py:143
  29.6 7.1 %collective-permute-start.10 = (bf16[24,4096]{1,0:T(8,128)(2,1)S(1)}, bf16[24,4096]{1,0:T(8,128)(2,1)S(1)}, u32[]{:S(2)}, u32[]{:S(2)}) collective-permute-start(bf16[24,4096]{1,0:T(8,128)(2,1)S(1)} %get-tuple-element.66), channel_id=1, source_target_pairs={{0,8},{1,9},{2,10},{3,11},{4,12},{5,13},{6,14},{7,15},{8,0},{9,1},... | collective-permute-start | bytes 589832 | tf_op jit(solution)/shard_map/ppermute | solution.py:143
  31.0 5.7 %collective-permute-start.9 = (bf16[24,4096]{1,0:T(8,128)(2,1)S(1)}, bf16[24,4096]{1,0:T(8,128)(2,1)S(1)}, u32[]{:S(2)}, u32[]{:S(2)}) collective-permute-start(bf16[24,4096]{1,0:T(8,128)(2,1)S(1)} %get-tuple-element.67), channel_id=1, source_target_pairs={{0,4},{1,5},{2,6},{3,7},{4,0},{5,1},{6,2},{7,3},{8,12},{9,13},{10,... | collective-permute-start | bytes 589832 | tf_op jit(solution)/shard_map/ppermute | solution.py:143
  40.1 8.1 %collective-permute-start.14 = (bf16[40,2048]{1,0:T(8,128)(2,1)S(1)}, bf16[40,2048]{1,0:T(8,128)(2,1)S(1)}, u32[]{:S(2)}, u32[]{:S(2)}) collective-permute-start(bf16[40,2048]{1,0:T(8,128)(2,1)S(1)} %pad_maximum_fusion.19), channel_id=1, source_target_pairs={{0,6},{1,7},{2,4},{3,5},{4,2},{5,3},{6,0},{7,1},{8,14},{9,15},{10,... | collective-permute-start | bytes 491528 | tf_op jit(solution)/shard_map/ppermute | solution.py:143
  41.6 6.5 %collective-permute-start.13 = (bf16[40,2048]{1,0:T(8,128)(2,1)S(1)}, bf16[40,2048]{1,0:T(8,128)(2,1)S(1)}, u32[]{:S(2)}, u32[]{:S(2)}) collective-permute-start(bf16[40,2048]{1,0:T(8,128)(2,1)S(1)} %get-tuple-element.72), channel_id=1, source_target_pairs={{0,2},{1,3},{2,0},{3,1},{4,6},{5,7},{6,4},{7,5},{8,10},{9,11},{10,... | collective-permute-start | bytes 491528 | tf_op jit(solution)/shard_map/ppermute | solution.py:143
  42.7 6.3 %collective-permute-start.16 = (bf16[40,2048]{1,0:T(8,128)(2,1)S(1)}, bf16[40,2048]{1,0:T(8,128)(2,1)S(1)}, u32[]{:S(2)}, u32[]{:S(2)}) collective-permute-start(bf16[40,2048]{1,0:T(8,128)(2,1)S(1)} %get-tuple-element.73), channel_id=1, source_target_pairs={{0,4},{1,5},{2,6},{3,7},{4,0},{5,1},{6,2},{7,3},{8,12},{9,13},{10,... | collective-permute-start | bytes 491528 | tf_op jit(solution)/shard_map/ppermute | solution.py:143
  43.7 6.7 %collective-permute-start.18 = (bf16[40,2048]{1,0:T(8,128)(2,1)S(1)}, bf16[40,2048]{1,0:T(8,128)(2,1)S(1)}, u32[]{:S(2)}, u32[]{:S(2)}) collective-permute-start(bf16[40,2048]{1,0:T(8,128)(2,1)S(1)} %pad_maximum_fusion.22), channel_id=1, source_target_pairs={{0,8},{1,9},{2,10},{3,11},{4,12},{5,13},{6,14},{7,15},{8,0},{9,1},... | collective-permute-start | bytes 491528 | tf_op jit(solution)/shard_map/ppermute | solution.py:143
  48.2 7.6 %collective-permute-start.15 = (bf16[40,2048]{1,0:T(8,128)(2,1)S(1)}, bf16[40,2048]{1,0:T(8,128)(2,1)S(1)}, u32[]{:S(2)}, u32[]{:S(2)}) collective-permute-start(bf16[40,2048]{1,0:T(8,128)(2,1)S(1)} %add_convert_fusion.3), channel_id=1, source_target_pairs={{0,8},{1,9},{2,10},{3,11},{4,12},{5,13},{6,14},{7,15},{8,0},{9,1},... | collective-permute-start | bytes 491528 | tf_op jit(solution)/shard_map/ppermute | solution.py:143
  49.0 6.8 %collective-permute-start.17 = (bf16[40,2048]{1,0:T(8,128)(2,1)S(1)}, bf16[40,2048]{1,0:T(8,128)(2,1)S(1)}, u32[]{:S(2)}, u32[]{:S(2)}) collective-permute-start(bf16[40,2048]{1,0:T(8,128)(2,1)S(1)} %add_convert_fusion.2), channel_id=1, source_target_pairs={{0,2},{1,3},{2,0},{3,1},{4,6},{5,7},{6,4},{7,5},{8,10},{9,11},{10,... | collective-permute-start | bytes 491528 | tf_op jit(solution)/shard_map/ppermute | solution.py:143
  50.4 5.4 %collective-permute-start.19 = (bf16[40,2048]{1,0:T(8,128)(2,1)S(1)}, bf16[40,2048]{1,0:T(8,128)(2,1)S(1)}, u32[]{:S(2)}, u32[]{:S(2)}) collective-permute-start(bf16[40,2048]{1,0:T(8,128)(2,1)S(1)} %add_convert_fusion.1), channel_id=1, source_target_pairs={{0,4},{1,5},{2,6},{3,7},{4,0},{5,1},{6,2},{7,3},{8,12},{9,13},{10,... | collective-permute-start | bytes 491528 | tf_op jit(solution)/shard_map/ppermute | solution.py:143
  52.9 8.3 %collective-permute-start.21 = (bf16[320,2048]{1,0:T(8,128)(2,1)S(1)}, bf16[320,2048]{1,0:T(8,128)(2,1)S(1)}, u32[]{:S(2)}, u32[]{:S(2)}) collective-permute-start(bf16[320,2048]{1,0:T(8,128)(2,1)S(1)} %fusion.5), channel_id=1, source_target_pairs={{0,1},{1,0},{2,3},{3,2},{4,5},{5,4},{6,7},{7,6},{8,9},{9,8},{10,11... | collective-permute-start | bytes 3932168 | tf_op jit(solution)/shard_map/ppermute | solution.py:143
  54.2 9.2 %collective-permute-start.20 = (bf16[320,2048]{1,0:T(8,128)(2,1)S(1)}, bf16[320,2048]{1,0:T(8,128)(2,1)S(1)}, u32[]{:S(2)}, u32[]{:S(2)}) collective-permute-start(bf16[320,2048]{1,0:T(8,128)(2,1)S(1)} %fusion.4), channel_id=1, source_target_pairs={{0,1},{1,0},{2,3},{3,2},{4,5},{5,4},{6,7},{7,6},{8,9},{9,8},{10,11... | collective-permute-start | bytes 3932168 | tf_op jit(solution)/shard_map/ppermute | solution.py:143
  56.0 9.8 %collective-permute-start.22 = (bf16[40,1024]{1,0:T(8,128)(2,1)S(1)}, bf16[40,1024]{1,0:T(8,128)(2,1)S(1)}, u32[]{:S(2)}, u32[]{:S(2)}) collective-permute-start(bf16[40,1024]{1,0:T(8,128)(2,1)S(1)} %pad_maximum_fusion.23), channel_id=1, source_target_pairs={{0,16},{1,17},{2,18},{3,19},{4,20},{5,21},{6,22},{7,23},{8,24},{9,... | collective-permute-start | bytes 245768 | tf_op jit(solution)/shard_map/ppermute | solution.py:186
  (5 other events, 19.9 us)

commit v13 on v12

--- a/solution.py
+++ b/solution.py
@@ -65,28 +65,33 @@
     rank = jnp.sum(rivals, axis=0, keepdims=True)
     tokens = tokens_ref[...]
     gated = (gate_down * grads_ref[...].astype(jnp.float32)).astype(jnp.bfloat16)
-    rows, picks = outs[: len(blocks)], outs[len(blocks) : 3 * len(blocks) - 2]
-    copies = outs[3 * len(blocks) - 2 :]
+    rows, picks = outs[: len(blocks)], outs[len(blocks) : 2 * len(blocks)]
+    copies = outs[2 * len(blocks) :]
 
     def one_hot(shape, block, shift):
         expert, begin, end, row = block
         chosen = (relative == expert) & (rank >= begin) & (rank < end)
         slot = jnp.where(chosen, rank - begin + row + shift, -1.0).astype(jnp.int32)
         slots = lax.broadcasted_iota(jnp.int32, shape, 0)
-        return jnp.where(slots == slot, 1.0, 0.0).astype(jnp.bfloat16)
-
-    for k, block in enumerate(blocks[2:]):
-        upper_ref, lower_ref = picks[2 * k + 2], picks[2 * k + 3]
-        upper = one_hot(upper_ref.shape, block, 0)
-        lower = one_hot(lower_ref.shape, block, block[2])
-        upper_ref[...], lower_ref[...] = upper, lower
-        both = picked(upper, tokens) + picked(lower, gated)
-        rows[k + 2][...] = both.astype(jnp.bfloat16)
-    for k, block in enumerate(blocks[:2]):
-        pick = one_hot(picks[k].shape, block, 0)
-        picks[k][...] = pick
-        rows[k][:, :width] = picked(pick, tokens).astype(jnp.bfloat16)
-        rows[k][:, width:] = picked(pick, gated).astype(jnp.bfloat16)
+        return jnp.where(slots == slot, 1.0, 0.0)
+
+    uppers, lowers = [], []
+    for k, block in enumerate(blocks):
+        shape = picks[k].shape
+        uppers.append(one_hot(shape, block, 0))
+        lowers.append(uppers[k] if k < 2 else one_hot(shape, block, block[2]))
+        picks[k][...] = uppers[k].astype(jnp.bfloat16)
+    upper, lower = [jnp.concatenate(p, axis=0).astype(jnp.bfloat16) for p in (uppers, lowers)]
+    from_tokens, from_gated = picked(upper, tokens), picked(lower, gated)
+    start = 0
+    for k, rows_ref in enumerate(rows):
+        part = slice(start, start + rows_ref.shape[0])
+        start = part.stop
+        if k < 2:
+            rows_ref[:, :width] = from_tokens[part].astype(jnp.bfloat16)
+            rows_ref[:, width:] = from_gated[part].astype(jnp.bfloat16)
+        else:
+            rows_ref[...] = (from_tokens[part] + from_gated[part]).astype(jnp.bfloat16)
     for copy_ref in copies:
         copy_ref[...] = rows[0][...]
 
@@ -101,7 +106,7 @@
 
     shapes = [shape(first, 2 * width), shape(rest, 2 * width)]
     shapes += [shape(2 * capacity, width)] * crossing
-    shapes += [shape(first, n), shape(rest, n)] + [shape(2 * capacity, n)] * (2 * crossing)
+    shapes += [shape(first, n), shape(rest, n)] + [shape(2 * capacity, n)] * crossing
     shapes += [shape(first, 2 * width)] * len(early_masks)
     outs = pl.pallas_call(
         lambda *refs: pack_kernel(blocks, experts, *refs),
@@ -109,8 +114,7 @@
         in_specs=[whole] * 4,
         out_specs=[whole] * len(shapes),
     )(ids.reshape(1, n), gate.reshape(1, n), tokens, grads)
-    rows, picks = outs[: len(blocks)], outs[len(blocks) : 3 * len(blocks) - 2]
-    return rows, picks, outs[3 * len(blocks) - 2 :]
+    return outs[: len(blocks)], outs[len(blocks) : 2 * len(blocks)], outs[2 * len(blocks) :]
 
 
 def handed_on(copies, sent):
@@ -130,11 +134,36 @@
     return lax.all_gather(shard.astype(jnp.bfloat16), "dp", axis=0, tiled=True)
 
 
-def stepped(weights, grads):
-    if lax.axis_size("dp") > 1:
-        grads = lax.psum_scatter(
-            grads.astype(jnp.bfloat16), "dp", scatter_dimension=0, tiled=True
-        ).astype(jnp.float32)
+def step_kernel(*refs):
+    count = len(refs) // 3
+    bases, shares, outs = refs[:count], refs[count : 2 * count], refs[2 * count :]
+    rows = outs[0].shape[0]
+    part = pl.ds(pl.multiple_of(pl.program_id(0) * rows, rows), rows)
+    for base_ref, share_ref, out_ref in zip(bases, shares, outs):
+        out_ref[...] = base_ref[part, :] - step_rate * share_ref[part, :].astype(jnp.float32)
+
+
+def stepped(bases, shares):
+    units, width = bases[0].shape
+    rows = 64 if units % 64 == 0 else units
+    whole = pl.BlockSpec(memory_space=pltpu.VMEM)
+    return pl.pallas_call(
+        step_kernel,
+        grid=(units // rows,),
+        out_shape=[jax.ShapeDtypeStruct(base.shape, base.dtype) for base in bases],
+        in_specs=[whole] * (2 * len(bases)),
+        out_specs=[pl.BlockSpec((rows, width), lambda i: (i, 0))] * len(bases),
+        compiler_params=pltpu.CompilerParams(vmem_limit_bytes=32 * 1024 * 1024),
+        cost_estimate=pl.CostEstimate(
+            flops=4 * units * width, bytes_accessed=8 * units * width, transcendentals=0
+        ),
+    )(*bases, *shares)
+
+
+def stepped_over_dp(weights, grads):
+    grads = lax.psum_scatter(
+        grads.astype(jnp.bfloat16), "dp", scatter_dimension=0, tiled=True
+    ).astype(jnp.float32)
     return weights - step_rate * grads
 
 
@@ -144,7 +173,7 @@
 
 
 core_bit, x_bit, y_bit, z_bit = 1, 2, 4, 8
-early_masks = (x_bit, y_bit, z_bit, x_bit | y_bit)
+early_masks = (x_bit | y_bit, z_bit, x_bit, y_bit)
 
 
 def after(values, *others):
@@ -211,7 +240,7 @@
         late_own = late_own + jnp.pad(
             side_by_side, (((s - 1) * capacity, rest - s * capacity), (0, 0))
         )
-    early_x, early_y, early_z, early_xy = after(
+    early_xy, early_z, early_x, early_y = after(
         [swap(rows, mask) for rows, mask in zip(early_copies, early_masks)], late_own
     )
     late_x, late_y, late_z = swaps(
@@ -259,13 +288,20 @@
             for left, right, scale in ((3, 0, scale_in), (2, 1, scale_out))
         ]
 
-    in_mine, out_mine = gradients(slice(0, units), back[-1])
-    zx = after(zx, in_mine, out_mine)
-    in_theirs, out_theirs = gradients(slice(units, 2 * units), zx)
-    in_shared = swap(in_theirs.astype(jnp.bfloat16), core_bit).astype(jnp.float32)
-    out_shared = swap(out_theirs.astype(jnp.bfloat16), core_bit).astype(jnp.float32)
-    new_w_in = stepped(w_in, (in_mine + in_shared).T)
-    new_w_out = stepped(w_out, (out_mine + out_shared).T)
+    mine = gradients(slice(0, units), back[-1])
+    split_width = lax.axis_size("dp") > 1
+    if not split_width:
+        mine = [weights.T - step_rate * grads for weights, grads in zip((w_in, w_out), mine)]
+    zx = after(zx, mine)
+    theirs = gradients(slice(units, 2 * units), zx)
+    shares = [swap(grads.astype(jnp.bfloat16), core_bit) for grads in theirs]
+    if split_width:
+        new_weights = [
+            stepped_over_dp(weights, (grads + share.astype(jnp.float32)).T)
+            for weights, grads, share in zip((w_in, w_out), mine, shares)
+        ]
+    else:
+        new_weights = [weights.T for weights in stepped(mine, shares)]
     near = swaps(
         [total(sum_z, zx, far), total(sum_x, xy), total(sum_y, yz)], (z_bit, x_bit, y_bit)
     )
@@ -276,11 +312,11 @@
     for s in range(1, experts):
         rows = late_sum[(s - 1) * capacity : s * capacity]
         rows = jnp.concatenate([rows[:, :half], rows[:, half:]], axis=0)
-        rows = after(shifted(rows, -s), new_w_in, new_w_out)
+        rows = after(shifted(rows, -s), new_weights)
         returned.append(jnp.concatenate(split_rows(rows, capacity), axis=1))
-    picks = [*picks[:2], *[pick[:capacity] for pick in picks[2::2]]]
+    picks = [*picks[:2], *[pick[:capacity] for pick in picks[2:]]]
     token_grad = sum(contract_rows(pick, rows) for pick, rows in zip(picks, returned))
-    return (token_grad.astype(jnp.bfloat16), new_w_in, new_w_out)
+    return (token_grad.astype(jnp.bfloat16), *new_weights)
 
 
 def solution(mesh):

time: 67 us -> 65.5 us (0.978)
  other arithmetic: 7.43 us -> 2.84 us
  waiting for transfers between devices: 12.7 us -> 9.34 us
  Pallas kernels: 2.6 us -> 5.67 us
  starting transfers between devices: 29.2 us -> 31.3 us
  local copies, waits for them, and re-layouts: 2.04 us -> 3.19 us
    sub x2 -> x0, other arithmetic: 4.59 us -> none  [stepped(): return weights - step_rate * grads]
    ppermute x21, waiting for transfers between devices: 12.7 us -> 9.34 us  [swap(): lax.ppermute(rows, 'expert', [(i, i ^ mask) for i in range(n_expert)])]
    pallas_call x0 -> x1, Pallas kernels: none -> 3.12 us  [stepped(): pl.pallas_call(step_kernel, grid=(units // rows,), out_shape=[jax.ShapeDt...]
    ppermute x21, starting transfers between devices: 20.4 us -> 22.8 us  [swap(): lax.ppermute(rows, 'expert', [(i, i ^ mask) for i in range(n_expert)])]
    unnamed x22, local copies, waits for them, and re-layouts: 1.6 us -> 2.74 us
  transfers between devices with their start and end apart: 23 -> 23, of which waited for: 8 -> 7; matrix products, arithmetic and copies ran while one was open for 24% -> 18% of each run, Pallas kernels for 0% -> 5%
where the time goes in v13:
time: 65.5 us; the launch traced here: 65.2 us
  starting transfers between devices  31.3 us (48%)
  matrix products  11.8 us (18%)
  waiting for transfers between devices  9.34 us (14%)
  Pallas kernels  5.67 us (9%)
  local copies, waits for them, and re-layouts  3.19 us (5%)
  other arithmetic  2.84 us (4%)
  between operations  1.1 us (2%)
    ppermute x21, starting transfers between devices, swap(): lax.ppermute(rows, 'expert', [(i, i ^ mask) for i in range(n_expert)])  22.8 us
    ppermute x21, waiting for transfers between devices, swap(): lax.ppermute(rows, 'expert', [(i, i ^ mask) for i in range(n_expert)])  9.34 us
    ppermute x2, starting transfers between devices, shifted(): return lax.ppermute(rows, 'expert', pairs)  8.49 us
    dot_general x11, matrix products, contract_rows(): lax.dot_general(left, right, (((0,), (0,)), ((), ())), preferred_element_...  6.09 us
    dot_general x4, matrix products, contract_cols(): lax.dot_general(left, right, (((1,), (1,)), ((), ())), preferred_element_...  4.3 us
    pallas_call x1, Pallas kernels, stepped(): pl.pallas_call(step_kernel, grid=(units // rows,), out_shape=[jax.ShapeDt...  3.12 us
    unnamed x22, local copies, waits for them, and re-layouts  2.74 us
    pallas_call x1, Pallas kernels, pack(): pl.pallas_call(lambda *refs: pack_kernel(blocks, experts, *refs), out_sha...  2.55 us
  transfers between devices with their start and end apart: 23, of which 7 were waited for; matrix products, arithmetic and copies ran while one was open for 18% of the time, Pallas kernels for 5%

profile of v13, /device:TPU:0, one launch (start us, length us, event | category | flops | bytes accessed | tf_op | source)
XLA Modules:
  0.0 65.2 jit_solution(7043153463183194612)
XLA Ops:
  0.6 2.5 %shard_map.85 = (bf16[16,4096]{1,0:T(8,128)(2,1)}, bf16[24,4096]{1,0:T(8,128)(2,1)}, bf16[40,2048]{1,0:T(8,128)(2,1)}, bf16[16,64]{1,0:T(8,128)(2,1)}, bf16[24,6...) custom-call(s32[1,64]{1,0:T(1,128)} %bitcast.18, ...), custom_call_target="tpu_custom_call" | custom-call | tf_op jit(solution)/shard_map/pallas_call | solution.py:111
  3.2 4.1 %collective-permute-start = (bf16[40,2048]{1,0:T(8,128)(2,1)}, bf16[40,2048]{1,0:T(8,128)(2,1)S(1)}, u32[]{:S(2)}, u32[]{:S(2)}) collective-permute-start(bf16[40,2048]{1,0:T(8,128)(2,1)} %get-tuple-element.51.refs_4_), channel_id=1, source_target_pairs={{0,16},{1,17},{2,18},{3,19},{4,20},{5,21},{6,22},{7,23},{8,24},{9,... | collective-permute-start | bytes 491528 | tf_op jit(solution)/shard_map/ppermute | solution.py:215
  7.3 2.4 %collective-permute-start.1 = (bf16[16,4096]{1,0:T(8,128)(2,1)}, bf16[16,4096]{1,0:T(8,128)(2,1)S(1)}, u32[]{:S(2)}, u32[]{:S(2)}) collective-permute-start(bf16[16,4096]{1,0:T(8,128)(2,1)} %get-tuple-element.56), channel_id=1, source_target_pairs={{0,6},{1,7},{2,4},{3,5},{4,2},{5,3},{6,0},{7,1},{8,14},{9,15},{10,... | collective-permute-start | bytes 393224 | tf_op jit(solution)/shard_map/ppermute | solution.py:172
  9.7 1.6 %collective-permute-start.2 = (bf16[16,4096]{1,0:T(8,128)(2,1)}, bf16[16,4096]{1,0:T(8,128)(2,1)S(1)}, u32[]{:S(2)}, u32[]{:S(2)}) collective-permute-start(bf16[16,4096]{1,0:T(8,128)(2,1)} %get-tuple-element.57), channel_id=1, source_target_pairs={{0,8},{1,9},{2,10},{3,11},{4,12},{5,13},{6,14},{7,15},{8,0},{9,1},... | collective-permute-start | bytes 393224 | tf_op jit(solution)/shard_map/ppermute | solution.py:172
  13.3 1.9 %convert_bitcast_fusion = bf16[320,2048]{1,0:T(8,128)(2,1)S(1)} fusion(f32[2048,320]{0,1:T(8,128)} %param.10), kind=kLoop, calls=%fused_computation.24 | loop fusion | flops 655360 | bytes 3932160 | tf_op jit(solution)/shard_map/transpose | solution.py:258
  17.1 1.6 %collective-permute-start.6 = (bf16[40,4096]{1,0:T(8,128)(2,1)S(1)}, bf16[40,4096]{1,0:T(8,128)(2,1)S(1)}, u32[]{:S(2)}, u32[]{:S(2)}) collective-permute-start(bf16[40,4096]{1,0:T(8,128)(2,1)S(1)} %get-tuple-element.64), channel_id=1, source_target_pairs={{0,2},{1,3},{2,0},{3,1},{4,6},{5,7},{6,4},{7,5},{8,10},{9,11},{10,... | collective-permute-start | bytes 983048 | tf_op jit(solution)/shard_map/ppermute | solution.py:172
  19.6 1.3 %collective-permute-start.7 = (bf16[40,4096]{1,0:T(8,128)(2,1)S(1)}, bf16[40,4096]{1,0:T(8,128)(2,1)S(1)}, u32[]{:S(2)}, u32[]{:S(2)}) collective-permute-start(bf16[40,4096]{1,0:T(8,128)(2,1)S(1)} %get-tuple-element.65), channel_id=1, source_target_pairs={{0,8},{1,9},{2,10},{3,11},{4,12},{5,13},{6,14},{7,15},{8,0},{9,1},... | collective-permute-start | bytes 983048 | tf_op jit(solution)/shard_map/ppermute | solution.py:172
  21.0 4.9 %collective-permute-done.6 = bf16[40,4096]{1,0:T(8,128)(2,1)S(1)} collective-permute-done((bf16[40,4096]{1,0:T(8,128)(2,1)S(1)}, bf16[40,4096]{1,0:T(8,128)(2,1)S(1)}, u32[]{:S(2)}, u32[]{:S(2)}) %collective-permute-start.6) | collective-permute-done | bytes 327712 | tf_op jit(solution)/shard_map/ppermute | solution.py:172
  27.5 1.5 %collective-permute-start.12 = (bf16[24,4096]{1,0:T(8,128)(2,1)S(1)}, bf16[24,4096]{1,0:T(8,128)(2,1)S(1)}, u32[]{:S(2)}, u32[]{:S(2)}) collective-permute-start(bf16[24,4096]{1,0:T(8,128)(2,1)S(1)} %get-tuple-element.67), channel_id=1, source_target_pairs={{0,6},{1,7},{2,4},{3,5},{4,2},{5,3},{6,0},{7,1},{8,14},{9,15},{10,... | collective-permute-start | bytes 589832 | tf_op jit(solution)/shard_map/ppermute | solution.py:172
  29.8 1.3 %collective-permute-start.10 = (bf16[24,4096]{1,0:T(8,128)(2,1)S(1)}, bf16[24,4096]{1,0:T(8,128)(2,1)S(1)}, u32[]{:S(2)}, u32[]{:S(2)}) collective-permute-start(bf16[24,4096]{1,0:T(8,128)(2,1)S(1)} %get-tuple-element.68), channel_id=1, source_target_pairs={{0,8},{1,9},{2,10},{3,11},{4,12},{5,13},{6,14},{7,15},{8,0},{9,1},... | collective-permute-start | bytes 589832 | tf_op jit(solution)/shard_map/ppermute | solution.py:172
  31.1 1.7 %collective-permute-start.9 = (bf16[24,4096]{1,0:T(8,128)(2,1)S(1)}, bf16[24,4096]{1,0:T(8,128)(2,1)S(1)}, u32[]{:S(2)}, u32[]{:S(2)}) collective-permute-start(bf16[24,4096]{1,0:T(8,128)(2,1)S(1)} %get-tuple-element.69), channel_id=1, source_target_pairs={{0,4},{1,5},{2,6},{3,7},{4,0},{5,1},{6,2},{7,3},{8,12},{9,13},{10,... | collective-permute-start | bytes 589832 | tf_op jit(solution)/shard_map/ppermute | solution.py:172
  33.0 1.0 %multiply_convert_fusion.1 = (bf16[128,640]{1,0:T(8,128)(2,1)S(1)}, f32[128,640]{1,0:T(8,128)S(1)}) fusion(bf16[320,2048]{1,0:T(8,128)(2,1)S(1)} %convert_bitcast_fusion, bf16[320,2048]{1,0:T(8,128)(2,1)S(1)} %get-tuple-element.95, bf16[128,4096]{1,0:T(8,128)(2,1)S(1)} %slice_dynamic-update-slice_fusion), kind=kOutput, calls=%fused_computation.67 | convolution fusion | flops 341606400 | bytes 3637248 | tf_op jit(solution)/shard_map/dot_general | solution.py:39
  34.0 1.0 %fusion.18 = bf16[128,640]{1,0:T(8,128)(2,1)S(1)} fusion(bf16[320,2048]{1,0:T(8,128)(2,1)S(1)} %get-tuple-element.96, bf16[320,2048]{1,0:T(8,128)(2,1)S(1)} %convert_bitcast_fusion.1, bf16[128,4096]{1,0:T(8,128)(2,1)S(1)} %slice_dynamic-update-slice_fusion, f32[128,640]{1,0:T(8,128)S(1)} %get-tuple-element.130), kind=kOutput, calls=%fused_computation.31 | convolution fusion | flops 342507520 | bytes 3637248 | tf_op jit(solution)/shard_map/dot_general | solution.py:39
  35.7 1.5 %collective-permute-done.9 = bf16[24,4096]{1,0:T(8,128)(2,1)S(1)} collective-permute-done((bf16[24,4096]{1,0:T(8,128)(2,1)S(1)}, bf16[24,4096]{1,0:T(8,128)(2,1)S(1)}, u32[]{:S(2)}, u32[]{:S(2)}) %collective-permute-start.9) | collective-permute-done | bytes 196640 | tf_op jit(solution)/shard_map/ppermute | solution.py:172
  37.3 1.1 %multiply_convert_fusion = (bf16[192,640]{1,0:T(8,128)(2,1)S(1)}, f32[192,640]{1,0:T(8,128)S(1)}) fusion(bf16[320,2048]{1,0:T(8,128)(2,1)S(1)} %convert_bitcast_fusion, bf16[320,2048]{1,0:T(8,128)(2,1)S(1)} %get-tuple-element.95, bf16[192,4096]{1,0:T(8,128)(2,1)S(1)} %constant_dynamic-update-slice_fusion.5), kind=kOutput, calls=%fused_computation.46 | convolution fusion | flops 509788160 | bytes 4145152 | tf_op jit(solution)/shard_map/dot_general | solution.py:39
  38.4 1.2 %fusion.15 = bf16[192,640]{1,0:T(8,128)(2,1)S(1)} fusion(bf16[320,2048]{1,0:T(8,128)(2,1)S(1)} %get-tuple-element.96, bf16[320,2048]{1,0:T(8,128)(2,1)S(1)} %convert_bitcast_fusion.1, bf16[192,4096]{1,0:T(8,128)(2,1)S(1)} %constant_dynamic-update-slice_fusion.5, f32[192,640]{1,0:T(8,128)S(1)} %get-tuple-element.128), kind=kOutput, calls=%fused_computation.28 | convolution fusion | flops 511139840 | bytes 4145152 | tf_op jit(solution)/shard_map/dot_general | solution.py:39
  40.5 1.4 %collective-permute-start.14 = (bf16[40,2048]{1,0:T(8,128)(2,1)S(1)}, bf16[40,2048]{1,0:T(8,128)(2,1)S(1)}, u32[]{:S(2)}, u32[]{:S(2)}) collective-permute-start(bf16[40,2048]{1,0:T(8,128)(2,1)S(1)} %pad_maximum_fusion.19), channel_id=1, source_target_pairs={{0,6},{1,7},{2,4},{3,5},{4,2},{5,3},{6,0},{7,1},{8,14},{9,15},{10,... | collective-permute-start | bytes 491528 | tf_op jit(solution)/shard_map/ppermute | solution.py:172
  42.0 1.6 %collective-permute-start.13 = (bf16[40,2048]{1,0:T(8,128)(2,1)S(1)}, bf16[40,2048]{1,0:T(8,128)(2,1)S(1)}, u32[]{:S(2)}, u32[]{:S(2)}) collective-permute-start(bf16[40,2048]{1,0:T(8,128)(2,1)S(1)} %get-tuple-element.74), channel_id=1, source_target_pairs={{0,2},{1,3},{2,0},{3,1},{4,6},{5,7},{6,4},{7,5},{8,10},{9,11},{10,... | collective-permute-start | bytes 491528 | tf_op jit(solution)/shard_map/ppermute | solution.py:172
  44.2 1.8 %collective-permute-start.18 = (bf16[40,2048]{1,0:T(8,128)(2,1)S(1)}, bf16[40,2048]{1,0:T(8,128)(2,1)S(1)}, u32[]{:S(2)}, u32[]{:S(2)}) collective-permute-start(bf16[40,2048]{1,0:T(8,128)(2,1)S(1)} %pad_maximum_fusion.22), channel_id=1, source_target_pairs={{0,8},{1,9},{2,10},{3,11},{4,12},{5,13},{6,14},{7,15},{8,0},{9,1},... | collective-permute-start | bytes 491528 | tf_op jit(solution)/shard_map/ppermute | solution.py:172
  47.7 1.2 %copy-done.1 = f32[2048,320]{0,1:T(8,128)S(1)} copy-done((f32[2048,320]{0,1:T(8,128)S(1)}, f32[2048,320]{0,1:T(8,128)}, u32[]{:S(2)}) %copy-start.1) | copy-done | bytes 2621464
  50.7 1.4 %collective-permute-start.19 = (bf16[40,2048]{1,0:T(8,128)(2,1)S(1)}, bf16[40,2048]{1,0:T(8,128)(2,1)S(1)}, u32[]{:S(2)}, u32[]{:S(2)}) collective-permute-start(bf16[40,2048]{1,0:T(8,128)(2,1)S(1)} %add_convert_fusion.1), channel_id=1, source_target_pairs={{0,4},{1,5},{2,6},{3,7},{4,0},{5,1},{6,2},{7,3},{8,12},{9,13},{10,... | collective-permute-start | bytes 491528 | tf_op jit(solution)/shard_map/ppermute | solution.py:172
  56.2 4.4 %collective-permute-start.22 = (bf16[40,1024]{1,0:T(8,128)(2,1)S(1)}, bf16[40,1024]{1,0:T(8,128)(2,1)S(1)}, u32[]{:S(2)}, u32[]{:S(2)}) collective-permute-start(bf16[40,1024]{1,0:T(8,128)(2,1)S(1)} %pad_maximum_fusion.23), channel_id=1, source_target_pairs={{0,16},{1,17},{2,18},{3,19},{4,20},{5,21},{6,22},{7,23},{8,24},{9,... | collective-permute-start | bytes 245768 | tf_op jit(solution)/shard_map/ppermute | solution.py:215
  61.1 3.1 %shard_map.87 = (f32[320,2048]{1,0:T(8,128)}, f32[320,2048]{1,0:T(8,128)}) custom-call(f32[320,2048]{1,0:T(8,128)S(1)} %fusion.5.refs_0_, f32[320,2048]{1,0:T(8,128)S(1)} %fusion.3.refs_1_, bf16[320,2048]{1,0:T(8,128)(2,1)S(1)} %collective-permute-done.20.refs_2_, bf16[320,2048]{1,0:T(8,128)(2,1)S(1)} %collective-permute-done.21.refs_3_), custom_call_target="tpu_custom_call" | custom-call | flops 2621440 | bytes 5242880 | tf_op jit(solution)/shard_map/pallas_call | solution.py:150
  64.3 1.0 %fusion.10 = bf16[64,2048]{1,0:T(8,128)(2,1)} fusion(f32[64,2048]{1,0:T(8,128)S(1)} %convolution_add_fusion.5, bf16[20,1024]{1,0:T(8,128)(2,1)S(1)} %get-tuple-element.126, bf16[20,1024]{1,0:T(8,128)(2,1)S(1)} %get-tuple-element.125, bf16[40,64]{1,0:T(8,128)(2,1)S(1)} %copy-done.5), kind=kOutput, calls=%fused_computation.21 | convolution fusion | flops 5668864 | bytes 890880 | tf_op jit(solution)/shard_map/dot_general | solution.py:33
  (88 shorter events, 17.6 us)
Async XLA Ops:
  0.6 14.6 %copy-start = (f32[2048,320]{0,1:T(8,128)S(1)}, f32[2048,320]{0,1:T(8,128)}, u32[]{:S(2)}) copy-start(f32[2048,320]{0,1:T(8,128)} %param.11) | copy-start | bytes 7864324
  3.2 12.6 %collective-permute-start = (bf16[40,2048]{1,0:T(8,128)(2,1)}, bf16[40,2048]{1,0:T(8,128)(2,1)S(1)}, u32[]{:S(2)}, u32[]{:S(2)}) collective-permute-start(bf16[40,2048]{1,0:T(8,128)(2,1)} %get-tuple-element.51.refs_4_), channel_id=1, source_target_pairs={{0,16},{1,17},{2,18},{3,19},{4,20},{5,21},{6,22},{7,23},{8,24},{9,... | collective-permute-start | bytes 491528 | tf_op jit(solution)/shard_map/ppermute | solution.py:215
  7.3 9.1 %collective-permute-start.1 = (bf16[16,4096]{1,0:T(8,128)(2,1)}, bf16[16,4096]{1,0:T(8,128)(2,1)S(1)}, u32[]{:S(2)}, u32[]{:S(2)}) collective-permute-start(bf16[16,4096]{1,0:T(8,128)(2,1)} %get-tuple-element.56), channel_id=1, source_target_pairs={{0,6},{1,7},{2,4},{3,5},{4,2},{5,3},{6,0},{7,1},{8,14},{9,15},{10,... | collective-permute-start | bytes 393224 | tf_op jit(solution)/shard_map/ppermute | solution.py:172
  9.7 7.2 %collective-permute-start.2 = (bf16[16,4096]{1,0:T(8,128)(2,1)}, bf16[16,4096]{1,0:T(8,128)(2,1)S(1)}, u32[]{:S(2)}, u32[]{:S(2)}) collective-permute-start(bf16[16,4096]{1,0:T(8,128)(2,1)} %get-tuple-element.57), channel_id=1, source_target_pairs={{0,8},{1,9},{2,10},{3,11},{4,12},{5,13},{6,14},{7,15},{8,0},{9,1},... | collective-permute-start | bytes 393224 | tf_op jit(solution)/shard_map/ppermute | solution.py:172
  11.3 5.6 %collective-permute-start.3 = (bf16[16,4096]{1,0:T(8,128)(2,1)}, bf16[16,4096]{1,0:T(8,128)(2,1)S(1)}, u32[]{:S(2)}, u32[]{:S(2)}) collective-permute-start(bf16[16,4096]{1,0:T(8,128)(2,1)} %get-tuple-element.58), channel_id=1, source_target_pairs={{0,2},{1,3},{2,0},{3,1},{4,6},{5,7},{6,4},{7,5},{8,10},{9,11},{10,... | collective-permute-start | bytes 393224 | tf_op jit(solution)/shard_map/ppermute | solution.py:172
  11.9 5.2 %collective-permute-start.4 = (bf16[16,4096]{1,0:T(8,128)(2,1)}, bf16[16,4096]{1,0:T(8,128)(2,1)S(1)}, u32[]{:S(2)}, u32[]{:S(2)}) collective-permute-start(bf16[16,4096]{1,0:T(8,128)(2,1)} %get-tuple-element.59), channel_id=1, source_target_pairs={{0,4},{1,5},{2,6},{3,7},{4,0},{5,1},{6,2},{7,3},{8,12},{9,13},{10,... | collective-permute-start | bytes 393224 | tf_op jit(solution)/shard_map/ppermute | solution.py:172
  17.1 8.8 %collective-permute-start.6 = (bf16[40,4096]{1,0:T(8,128)(2,1)S(1)}, bf16[40,4096]{1,0:T(8,128)(2,1)S(1)}, u32[]{:S(2)}, u32[]{:S(2)}) collective-permute-start(bf16[40,4096]{1,0:T(8,128)(2,1)S(1)} %get-tuple-element.64), channel_id=1, source_target_pairs={{0,2},{1,3},{2,0},{3,1},{4,6},{5,7},{6,4},{7,5},{8,10},{9,11},{10,... | collective-permute-start | bytes 983048 | tf_op jit(solution)/shard_map/ppermute | solution.py:172
  18.7 7.8 %collective-permute-start.5 = (bf16[40,4096]{1,0:T(8,128)(2,1)S(1)}, bf16[40,4096]{1,0:T(8,128)(2,1)S(1)}, u32[]{:S(2)}, u32[]{:S(2)}) collective-permute-start(bf16[40,4096]{1,0:T(8,128)(2,1)S(1)} %get-tuple-element.64), channel_id=1, source_target_pairs={{0,4},{1,5},{2,6},{3,7},{4,0},{5,1},{6,2},{7,3},{8,12},{9,13},{10,... | collective-permute-start | bytes 983048 | tf_op jit(solution)/shard_map/ppermute | solution.py:172
  19.6 7.9 %collective-permute-start.7 = (bf16[40,4096]{1,0:T(8,128)(2,1)S(1)}, bf16[40,4096]{1,0:T(8,128)(2,1)S(1)}, u32[]{:S(2)}, u32[]{:S(2)}) collective-permute-start(bf16[40,4096]{1,0:T(8,128)(2,1)S(1)} %get-tuple-element.65), channel_id=1, source_target_pairs={{0,8},{1,9},{2,10},{3,11},{4,12},{5,13},{6,14},{7,15},{8,0},{9,1},... | collective-permute-start | bytes 983048 | tf_op jit(solution)/shard_map/ppermute | solution.py:172
  20.9 11.9 %collective-permute-start.8 = (bf16[640,2048]{1,0:T(8,128)(2,1)S(1)}, bf16[640,2048]{1,0:T(8,128)(2,1)S(1)}, u32[]{:S(2)}, u32[]{:S(2)}) collective-permute-start(bf16[640,2048]{1,0:T(8,128)(2,1)S(1)} %pad_maximum_fusion.1), channel_id=1, source_target_pairs={{0,1},{1,0},{2,3},{3,2},{4,5},{5,4},{6,7},{7,6},{8,9},{9,8},{10,11... | collective-permute-start | bytes 7864328 | tf_op jit(solution)/shard_map/ppermute | solution.py:172
  27.5 9.7 %collective-permute-start.12 = (bf16[24,4096]{1,0:T(8,128)(2,1)S(1)}, bf16[24,4096]{1,0:T(8,128)(2,1)S(1)}, u32[]{:S(2)}, u32[]{:S(2)}) collective-permute-start(bf16[24,4096]{1,0:T(8,128)(2,1)S(1)} %get-tuple-element.67), channel_id=1, source_target_pairs={{0,6},{1,7},{2,4},{3,5},{4,2},{5,3},{6,0},{7,1},{8,14},{9,15},{10,... | collective-permute-start | bytes 589832 | tf_op jit(solution)/shard_map/ppermute | solution.py:172
  28.9 8.3 %collective-permute-start.11 = (bf16[24,4096]{1,0:T(8,128)(2,1)S(1)}, bf16[24,4096]{1,0:T(8,128)(2,1)S(1)}, u32[]{:S(2)}, u32[]{:S(2)}) collective-permute-start(bf16[24,4096]{1,0:T(8,128)(2,1)S(1)} %get-tuple-element.67), channel_id=1, source_target_pairs={{0,2},{1,3},{2,0},{3,1},{4,6},{5,7},{6,4},{7,5},{8,10},{9,11},{10,... | collective-permute-start | bytes 589832 | tf_op jit(solution)/shard_map/ppermute | solution.py:172
  29.8 7.4 %collective-permute-start.10 = (bf16[24,4096]{1,0:T(8,128)(2,1)S(1)}, bf16[24,4096]{1,0:T(8,128)(2,1)S(1)}, u32[]{:S(2)}, u32[]{:S(2)}) collective-permute-start(bf16[24,4096]{1,0:T(8,128)(2,1)S(1)} %get-tuple-element.68), channel_id=1, source_target_pairs={{0,8},{1,9},{2,10},{3,11},{4,12},{5,13},{6,14},{7,15},{8,0},{9,1},... | collective-permute-start | bytes 589832 | tf_op jit(solution)/shard_map/ppermute | solution.py:172
  31.1 6.1 %collective-permute-start.9 = (bf16[24,4096]{1,0:T(8,128)(2,1)S(1)}, bf16[24,4096]{1,0:T(8,128)(2,1)S(1)}, u32[]{:S(2)}, u32[]{:S(2)}) collective-permute-start(bf16[24,4096]{1,0:T(8,128)(2,1)S(1)} %get-tuple-element.69), channel_id=1, source_target_pairs={{0,4},{1,5},{2,6},{3,7},{4,0},{5,1},{6,2},{7,3},{8,12},{9,13},{10,... | collective-permute-start | bytes 589832 | tf_op jit(solution)/shard_map/ppermute | solution.py:172
  40.5 8.9 %collective-permute-start.14 = (bf16[40,2048]{1,0:T(8,128)(2,1)S(1)}, bf16[40,2048]{1,0:T(8,128)(2,1)S(1)}, u32[]{:S(2)}, u32[]{:S(2)}) collective-permute-start(bf16[40,2048]{1,0:T(8,128)(2,1)S(1)} %pad_maximum_fusion.19), channel_id=1, source_target_pairs={{0,6},{1,7},{2,4},{3,5},{4,2},{5,3},{6,0},{7,1},{8,14},{9,15},{10,... | collective-permute-start | bytes 491528 | tf_op jit(solution)/shard_map/ppermute | solution.py:172
  42.0 7.4 %collective-permute-start.13 = (bf16[40,2048]{1,0:T(8,128)(2,1)S(1)}, bf16[40,2048]{1,0:T(8,128)(2,1)S(1)}, u32[]{:S(2)}, u32[]{:S(2)}) collective-permute-start(bf16[40,2048]{1,0:T(8,128)(2,1)S(1)} %get-tuple-element.74), channel_id=1, source_target_pairs={{0,2},{1,3},{2,0},{3,1},{4,6},{5,7},{6,4},{7,5},{8,10},{9,11},{10,... | collective-permute-start | bytes 491528 | tf_op jit(solution)/shard_map/ppermute | solution.py:172
  43.6 6.2 %collective-permute-start.16 = (bf16[40,2048]{1,0:T(8,128)(2,1)S(1)}, bf16[40,2048]{1,0:T(8,128)(2,1)S(1)}, u32[]{:S(2)}, u32[]{:S(2)}) collective-permute-start(bf16[40,2048]{1,0:T(8,128)(2,1)S(1)} %get-tuple-element.75), channel_id=1, source_target_pairs={{0,4},{1,5},{2,6},{3,7},{4,0},{5,1},{6,2},{7,3},{8,12},{9,13},{10,... | collective-permute-start | bytes 491528 | tf_op jit(solution)/shard_map/ppermute | solution.py:172
  44.2 6.4 %collective-permute-start.18 = (bf16[40,2048]{1,0:T(8,128)(2,1)S(1)}, bf16[40,2048]{1,0:T(8,128)(2,1)S(1)}, u32[]{:S(2)}, u32[]{:S(2)}) collective-permute-start(bf16[40,2048]{1,0:T(8,128)(2,1)S(1)} %pad_maximum_fusion.22), channel_id=1, source_target_pairs={{0,8},{1,9},{2,10},{3,11},{4,12},{5,13},{6,14},{7,15},{8,0},{9,1},... | collective-permute-start | bytes 491528 | tf_op jit(solution)/shard_map/ppermute | solution.py:172
  49.5 6.6 %collective-permute-start.15 = (bf16[40,2048]{1,0:T(8,128)(2,1)S(1)}, bf16[40,2048]{1,0:T(8,128)(2,1)S(1)}, u32[]{:S(2)}, u32[]{:S(2)}) collective-permute-start(bf16[40,2048]{1,0:T(8,128)(2,1)S(1)} %add_convert_fusion.3), channel_id=1, source_target_pairs={{0,8},{1,9},{2,10},{3,11},{4,12},{5,13},{6,14},{7,15},{8,0},{9,1},... | collective-permute-start | bytes 491528 | tf_op jit(solution)/shard_map/ppermute | solution.py:172
  49.8 6.2 %collective-permute-start.17 = (bf16[40,2048]{1,0:T(8,128)(2,1)S(1)}, bf16[40,2048]{1,0:T(8,128)(2,1)S(1)}, u32[]{:S(2)}, u32[]{:S(2)}) collective-permute-start(bf16[40,2048]{1,0:T(8,128)(2,1)S(1)} %add_convert_fusion.2), channel_id=1, source_target_pairs={{0,2},{1,3},{2,0},{3,1},{4,6},{5,7},{6,4},{7,5},{8,10},{9,11},{10,... | collective-permute-start | bytes 491528 | tf_op jit(solution)/shard_map/ppermute | solution.py:172
  50.7 5.4 %collective-permute-start.19 = (bf16[40,2048]{1,0:T(8,128)(2,1)S(1)}, bf16[40,2048]{1,0:T(8,128)(2,1)S(1)}, u32[]{:S(2)}, u32[]{:S(2)}) collective-permute-start(bf16[40,2048]{1,0:T(8,128)(2,1)S(1)} %add_convert_fusion.1), channel_id=1, source_target_pairs={{0,4},{1,5},{2,6},{3,7},{4,0},{5,1},{6,2},{7,3},{8,12},{9,13},{10,... | collective-permute-start | bytes 491528 | tf_op jit(solution)/shard_map/ppermute | solution.py:172
  53.4 7.8 %collective-permute-start.21 = (bf16[320,2048]{1,0:T(8,128)(2,1)S(1)}, bf16[320,2048]{1,0:T(8,128)(2,1)S(1)}, u32[]{:S(2)}, u32[]{:S(2)}) collective-permute-start(bf16[320,2048]{1,0:T(8,128)(2,1)S(1)} %fusion.7), channel_id=1, source_target_pairs={{0,1},{1,0},{2,3},{3,2},{4,5},{5,4},{6,7},{7,6},{8,9},{9,8},{10,11... | collective-permute-start | bytes 3932168 | tf_op jit(solution)/shard_map/ppermute | solution.py:172
  54.7 6.4 %collective-permute-start.20 = (bf16[320,2048]{1,0:T(8,128)(2,1)S(1)}, bf16[320,2048]{1,0:T(8,128)(2,1)S(1)}, u32[]{:S(2)}, u32[]{:S(2)}) collective-permute-start(bf16[320,2048]{1,0:T(8,128)(2,1)S(1)} %fusion.6), channel_id=1, source_target_pairs={{0,1},{1,0},{2,3},{3,2},{4,5},{5,4},{6,7},{7,6},{8,9},{9,8},{10,11... | collective-permute-start | bytes 3932168 | tf_op jit(solution)/shard_map/ppermute | solution.py:172
  56.2 8.1 %collective-permute-start.22 = (bf16[40,1024]{1,0:T(8,128)(2,1)S(1)}, bf16[40,1024]{1,0:T(8,128)(2,1)S(1)}, u32[]{:S(2)}, u32[]{:S(2)}) collective-permute-start(bf16[40,1024]{1,0:T(8,128)(2,1)S(1)} %pad_maximum_fusion.23), channel_id=1, source_target_pairs={{0,16},{1,17},{2,18},{3,19},{4,20},{5,21},{6,22},{7,23},{8,24},{9,... | collective-permute-start | bytes 245768 | tf_op jit(solution)/shard_map/ppermute | solution.py:215
  (5 other events, 19.1 us)

commit v14 on v13

--- a/solution.py
+++ b/solution.py
@@ -134,30 +134,27 @@
     return lax.all_gather(shard.astype(jnp.bfloat16), "dp", axis=0, tiled=True)
 
 
-def step_kernel(*refs):
-    count = len(refs) // 3
-    bases, shares, outs = refs[:count], refs[count : 2 * count], refs[2 * count :]
-    rows = outs[0].shape[0]
+def step_kernel(base_ref, share_ref, out_ref):
+    rows = out_ref.shape[0]
     part = pl.ds(pl.multiple_of(pl.program_id(0) * rows, rows), rows)
-    for base_ref, share_ref, out_ref in zip(bases, shares, outs):
-        out_ref[...] = base_ref[part, :] - step_rate * share_ref[part, :].astype(jnp.float32)
-
-
-def stepped(bases, shares):
-    units, width = bases[0].shape
+    out_ref[...] = base_ref[part, :] - step_rate * share_ref[part, :].astype(jnp.float32)
+
+
+def stepped(base, share):
+    units, width = base.shape
     rows = 64 if units % 64 == 0 else units
     whole = pl.BlockSpec(memory_space=pltpu.VMEM)
     return pl.pallas_call(
         step_kernel,
         grid=(units // rows,),
-        out_shape=[jax.ShapeDtypeStruct(base.shape, base.dtype) for base in bases],
-        in_specs=[whole] * (2 * len(bases)),
-        out_specs=[pl.BlockSpec((rows, width), lambda i: (i, 0))] * len(bases),
+        out_shape=jax.ShapeDtypeStruct(base.shape, base.dtype),
+        in_specs=[whole] * 2,
+        out_specs=pl.BlockSpec((rows, width), lambda i: (i, 0)),
         compiler_params=pltpu.CompilerParams(vmem_limit_bytes=32 * 1024 * 1024),
         cost_estimate=pl.CostEstimate(
-            flops=4 * units * width, bytes_accessed=8 * units * width, transcendentals=0
+            flops=2 * units * width, bytes_accessed=4 * units * width, transcendentals=0
         ),
-    )(*bases, *shares)
+    )(base, share)
 
 
 def stepped_over_dp(weights, grads):
@@ -247,13 +244,13 @@
         [
             jnp.concatenate([late_own, early_z], axis=0),
             jnp.concatenate([late_own, early_z], axis=0),
-            jnp.concatenate([late_own, early_xy], axis=0),
+            late_own,
         ],
         (x_bit, y_bit, z_bit),
     )
-    early_zx, early_yz, early_far = late_x[rest:], late_y[rest:], late_z[rest:]
-    late_x, late_y, late_z = late_x[:rest], late_y[:rest], late_z[:rest]
-    early_rows = [early_own, early_x, early_y, early_z, early_xy, early_yz, early_zx, early_far]
+    early_zx, early_yz = late_x[rest:], late_y[rest:]
+    late_x, late_y = late_x[:rest], late_y[:rest]
+    early_rows = [early_own, early_x, early_y, early_z, early_xy, early_yz, early_zx]
 
     own_weights = jnp.concatenate([whole_weights(w_in).T, whole_weights(w_out).T], axis=0)
     their_weights = swap(after(own_weights, late_own), core_bit)
@@ -261,24 +258,30 @@
         jnp.concatenate([own_weights[part], their_weights[part]], axis=0)
         for part in (slice(0, units), slice(units, 2 * units))
     ]
-    late_far, late_zx, late_yz, late_xy = swaps(
-        [late_z, late_z, late_y, late_x],
-        (x_bit | y_bit, x_bit, z_bit, y_bit),
+    late_xy, late_yz, late_far, late_zx = swaps(
+        [late_x, jnp.concatenate([late_y, early_xy], axis=0), late_z, late_z],
+        (y_bit, z_bit, x_bit | y_bit, x_bit),
     )
     early = activated(jnp.concatenate(early_rows, axis=0))
     early_parts = input_parts(early[3])
-    late_far = after([late_xy, late_yz, late_zx, late_far], early_parts)
-    late_rows = [late_own, late_x, late_y, late_z, *late_far]
+    late_xy, late_yz, late_zx, late_far = after(
+        [late_xy, late_yz, late_zx, late_far], early_parts
+    )
+    late_yz, early_far = late_yz[:rest], late_yz[rest:]
+    late_rows = [late_own, late_x, late_y, late_z, late_xy, late_yz, late_zx, late_far, early_far]
     later = activated(jnp.concatenate(late_rows, axis=0))
     late_parts = input_parts(later[3])
     parts = [
         jnp.concatenate(pair, axis=0)
-        for pair in zip(split_rows(early_parts, first), split_rows(late_parts, rest))
+        for pair in zip(
+            [*split_rows(early_parts, first), late_parts[8 * rest :]],
+            split_rows(late_parts[: 8 * rest], rest),
+        )
     ]
     own, sum_x, sum_y, sum_z, sum_xy, sum_yz, sum_zx, sum_far = parts
-    back = chain([sum_far, sum_zx, sum_xy, sum_yz])
-    far, zx, xy, yz = [
-        swap(rows, mask) for rows, mask in zip(back, (x_bit | y_bit, x_bit, y_bit, z_bit))
+    back = chain([sum_far, sum_yz, sum_zx, sum_xy])
+    far, yz, zx, xy = [
+        swap(rows, mask) for rows, mask in zip(back, (x_bit | y_bit, z_bit, x_bit, y_bit))
     ]
 
     def gradients(part, awaited):
@@ -301,9 +304,9 @@
             for weights, grads, share in zip((w_in, w_out), mine, shares)
         ]
     else:
-        new_weights = [weights.T for weights in stepped(mine, shares)]
+        new_weights = [stepped(base, share).T for base, share in zip(mine, shares)]
     near = swaps(
-        [total(sum_z, zx, far), total(sum_x, xy), total(sum_y, yz)], (z_bit, x_bit, y_bit)
+        [total(sum_y, yz), total(sum_z, zx, far), total(sum_x, xy)], (y_bit, z_bit, x_bit)
     )
     sums = total(own, *near)
     early_sum, late_sum = sums[:first], sums[first:]

time: 65.5 us -> 68.2 us (1.041)
  waiting for transfers between devices: 9.34 us -> 12 us
  Pallas kernels: 5.67 us -> 7.65 us
  starting transfers between devices: 31.3 us -> 29.4 us
    ppermute x21, waiting for transfers between devices: 9.34 us -> 12 us  [swap(): lax.ppermute(rows, 'expert', [(i, i ^ mask) for i in range(n_expert)])]
    pallas_call x1 -> x2, Pallas kernels: 3.12 us -> 5.1 us  [stepped(): pl.pallas_call(step_kernel, grid=(units // rows,), out_shape=jax.ShapeDty...]
    ppermute x2, starting transfers between devices: 8.49 us -> 7.43 us  [shifted(): return lax.ppermute(rows, 'expert', pairs)]
    ppermute x21, starting transfers between devices: 22.8 us -> 21.9 us  [swap(): lax.ppermute(rows, 'expert', [(i, i ^ mask) for i in range(n_expert)])]
    unnamed x22 -> x23, local copies, waits for them, and re-layouts: 2.74 us -> 2.76 us
  transfers between devices with their start and end apart: 23 -> 23, of which waited for: 7 -> 7; matrix products, arithmetic and copies ran while one was open for 18% -> 17% of each run, Pallas kernels for 5% -> 8%
where the time goes in v14:
time: 68.2 us; the launch traced here: 67.9 us
  starting transfers between devices  29.4 us (43%)
  waiting for transfers between devices  12 us (18%)
  matrix products  11.8 us (17%)
  Pallas kernels  7.65 us (11%)
  local copies, waits for them, and re-layouts  3.18 us (5%)
  other arithmetic  2.84 us (4%)
  between operations  1.1 us (2%)
    ppermute x21, starting transfers between devices, swap(): lax.ppermute(rows, 'expert', [(i, i ^ mask) for i in range(n_expert)])  21.9 us
    ppermute x21, waiting for transfers between devices, swap(): lax.ppermute(rows, 'expert', [(i, i ^ mask) for i in range(n_expert)])  12 us
    ppermute x2, starting transfers between devices, shifted(): return lax.ppermute(rows, 'expert', pairs)  7.43 us
    dot_general x11, matrix products, contract_rows(): lax.dot_general(left, right, (((0,), (0,)), ((), ())), preferred_element_...  6.04 us
    pallas_call x2, Pallas kernels, stepped(): pl.pallas_call(step_kernel, grid=(units // rows,), out_shape=jax.ShapeDty...  5.1 us
    dot_general x4, matrix products, contract_cols(): lax.dot_general(left, right, (((1,), (1,)), ((), ())), preferred_element_...  4.31 us
    unnamed x23, local copies, waits for them, and re-layouts  2.76 us
    pallas_call x1, Pallas kernels, pack(): pl.pallas_call(lambda *refs: pack_kernel(blocks, experts, *refs), out_sha...  2.55 us
  transfers between devices with their start and end apart: 23, of which 7 were waited for; matrix products, arithmetic and copies ran while one was open for 17% of the time, Pallas kernels for 8%

profile of v14, /device:TPU:0, one launch (start us, length us, event | category | flops | bytes accessed | tf_op | source)
XLA Modules:
  0.0 67.9 jit_solution(7649583577797715952)
XLA Ops:
  0.6 2.5 %shard_map.85 = (bf16[16,4096]{1,0:T(8,128)(2,1)}, bf16[24,4096]{1,0:T(8,128)(2,1)}, bf16[40,2048]{1,0:T(8,128)(2,1)}, bf16[16,64]{1,0:T(8,128)(2,1)}, bf16[24,6...) custom-call(s32[1,64]{1,0:T(1,128)} %bitcast.20, ...), custom_call_target="tpu_custom_call" | custom-call | tf_op jit(solution)/shard_map/pallas_call | solution.py:111
  3.2 4.1 %collective-permute-start = (bf16[40,2048]{1,0:T(8,128)(2,1)}, bf16[40,2048]{1,0:T(8,128)(2,1)S(1)}, u32[]{:S(2)}, u32[]{:S(2)}) collective-permute-start(bf16[40,2048]{1,0:T(8,128)(2,1)} %get-tuple-element.49.refs_4_), channel_id=1, source_target_pairs={{0,16},{1,17},{2,18},{3,19},{4,20},{5,21},{6,22},{7,23},{8,24},{9,... | collective-permute-start | bytes 491528 | tf_op jit(solution)/shard_map/ppermute | solution.py:212
  7.3 2.4 %collective-permute-start.1 = (bf16[16,4096]{1,0:T(8,128)(2,1)}, bf16[16,4096]{1,0:T(8,128)(2,1)S(1)}, u32[]{:S(2)}, u32[]{:S(2)}) collective-permute-start(bf16[16,4096]{1,0:T(8,128)(2,1)} %get-tuple-element.54), channel_id=1, source_target_pairs={{0,6},{1,7},{2,4},{3,5},{4,2},{5,3},{6,0},{7,1},{8,14},{9,15},{10,... | collective-permute-start | bytes 393224 | tf_op jit(solution)/shard_map/ppermute | solution.py:169
  9.7 1.6 %collective-permute-start.2 = (bf16[16,4096]{1,0:T(8,128)(2,1)}, bf16[16,4096]{1,0:T(8,128)(2,1)S(1)}, u32[]{:S(2)}, u32[]{:S(2)}) collective-permute-start(bf16[16,4096]{1,0:T(8,128)(2,1)} %get-tuple-element.55), channel_id=1, source_target_pairs={{0,8},{1,9},{2,10},{3,11},{4,12},{5,13},{6,14},{7,15},{8,0},{9,1},... | collective-permute-start | bytes 393224 | tf_op jit(solution)/shard_map/ppermute | solution.py:169
  13.3 1.9 %convert_bitcast_fusion = bf16[320,2048]{1,0:T(8,128)(2,1)S(1)} fusion(f32[2048,320]{0,1:T(8,128)} %param.10), kind=kLoop, calls=%fused_computation.24 | loop fusion | flops 655360 | bytes 3932160 | tf_op jit(solution)/shard_map/transpose | solution.py:255
  17.1 1.6 %collective-permute-start.6 = (bf16[40,4096]{1,0:T(8,128)(2,1)S(1)}, bf16[40,4096]{1,0:T(8,128)(2,1)S(1)}, u32[]{:S(2)}, u32[]{:S(2)}) collective-permute-start(bf16[40,4096]{1,0:T(8,128)(2,1)S(1)} %pad_maximum_fusion.17), channel_id=1, source_target_pairs={{0,2},{1,3},{2,0},{3,1},{4,6},{5,7},{6,4},{7,5},{8,10},{9,11},{10,... | collective-permute-start | bytes 983048 | tf_op jit(solution)/shard_map/ppermute | solution.py:169
  19.6 1.3 %collective-permute-start.8 = (bf16[24,4096]{1,0:T(8,128)(2,1)S(1)}, bf16[24,4096]{1,0:T(8,128)(2,1)S(1)}, u32[]{:S(2)}, u32[]{:S(2)}) collective-permute-start(bf16[24,4096]{1,0:T(8,128)(2,1)S(1)} %get-tuple-element.64), channel_id=1, source_target_pairs={{0,8},{1,9},{2,10},{3,11},{4,12},{5,13},{6,14},{7,15},{8,0},{9,1},... | collective-permute-start | bytes 589832 | tf_op jit(solution)/shard_map/ppermute | solution.py:169
  21.0 4.9 %collective-permute-done.6 = bf16[40,4096]{1,0:T(8,128)(2,1)S(1)} collective-permute-done((bf16[40,4096]{1,0:T(8,128)(2,1)S(1)}, bf16[40,4096]{1,0:T(8,128)(2,1)S(1)}, u32[]{:S(2)}, u32[]{:S(2)}) %collective-permute-start.6) | collective-permute-done | bytes 327712 | tf_op jit(solution)/shard_map/ppermute | solution.py:169
  26.5 1.3 %collective-permute-start.9 = (bf16[24,4096]{1,0:T(8,128)(2,1)S(1)}, bf16[24,4096]{1,0:T(8,128)(2,1)S(1)}, u32[]{:S(2)}, u32[]{:S(2)}) collective-permute-start(bf16[24,4096]{1,0:T(8,128)(2,1)S(1)} %get-tuple-element.110), channel_id=1, source_target_pairs={{0,4},{1,5},{2,6},{3,7},{4,0},{5,1},{6,2},{7,3},{8,12},{9,13},{10,... | collective-permute-start | bytes 589832 | tf_op jit(solution)/shard_map/ppermute | solution.py:169
  27.8 1.8 %collective-permute-start.10 = (bf16[40,4096]{1,0:T(8,128)(2,1)S(1)}, bf16[40,4096]{1,0:T(8,128)(2,1)S(1)}, u32[]{:S(2)}, u32[]{:S(2)}) collective-permute-start(bf16[40,4096]{1,0:T(8,128)(2,1)S(1)} %pad_maximum_fusion.18), channel_id=1, source_target_pairs={{0,8},{1,9},{2,10},{3,11},{4,12},{5,13},{6,14},{7,15},{8,0},{9,1},... | collective-permute-start | bytes 983048 | tf_op jit(solution)/shard_map/ppermute | solution.py:169
  29.9 1.5 %collective-permute-start.11 = (bf16[24,4096]{1,0:T(8,128)(2,1)S(1)}, bf16[24,4096]{1,0:T(8,128)(2,1)S(1)}, u32[]{:S(2)}, u32[]{:S(2)}) collective-permute-start(bf16[24,4096]{1,0:T(8,128)(2,1)S(1)} %collective-permute-done.8), channel_id=1, source_target_pairs={{0,2},{1,3},{2,0},{3,1},{4,6},{5,7},{6,4},{7,5},{8,10},{9,11},{10,... | collective-permute-start | bytes 589832 | tf_op jit(solution)/shard_map/ppermute | solution.py:169
  31.7 1.0 %multiply_convert_fusion.1 = (bf16[112,640]{1,0:T(8,128)(2,1)S(1)}, f32[112,640]{1,0:T(8,128)S(1)}) fusion(bf16[320,2048]{1,0:T(8,128)(2,1)S(1)} %convert_bitcast_fusion, bf16[320,2048]{1,0:T(8,128)(2,1)S(1)} %get-tuple-element.91, bf16[112,4096]{1,0:T(8,128)(2,1)S(1)} %slice_dynamic-update-slice_fusion.1), kind=kOutput, calls=%fused_computation.67 | convolution fusion | flops 299560960 | bytes 3510272 | tf_op jit(solution)/shard_map/dot_general | solution.py:39
  32.6 1.0 %fusion.18 = bf16[112,640]{1,0:T(8,128)(2,1)S(1)} fusion(bf16[320,2048]{1,0:T(8,128)(2,1)S(1)} %get-tuple-element.92, bf16[320,2048]{1,0:T(8,128)(2,1)S(1)} %convert_bitcast_fusion.1, bf16[112,4096]{1,0:T(8,128)(2,1)S(1)} %slice_dynamic-update-slice_fusion.1, f32[112,640]{1,0:T(8,128)S(1)} %get-tuple-element.121), kind=kOutput, calls=%fused_computation.31 | convolution fusion | flops 300349440 | bytes 3510272 | tf_op jit(solution)/shard_map/dot_general | solution.py:39
  34.3 3.6 %collective-permute-done.11 = bf16[24,4096]{1,0:T(8,128)(2,1)S(1)} collective-permute-done((bf16[24,4096]{1,0:T(8,128)(2,1)S(1)}, bf16[24,4096]{1,0:T(8,128)(2,1)S(1)}, u32[]{:S(2)}, u32[]{:S(2)}) %collective-permute-start.11) | collective-permute-done | bytes 196640 | tf_op jit(solution)/shard_map/ppermute | solution.py:169
  38.0 1.1 %multiply_convert_fusion = (bf16[208,640]{1,0:T(8,128)(2,1)S(1)}, f32[208,640]{1,0:T(8,128)S(1)}) fusion(bf16[320,2048]{1,0:T(8,128)(2,1)S(1)} %convert_bitcast_fusion, bf16[320,2048]{1,0:T(8,128)(2,1)S(1)} %get-tuple-element.91, bf16[208,4096]{1,0:T(8,128)(2,1)S(1)} %slice_dynamic-update-slice_fusion.3), kind=kOutput, calls=%fused_computation.46 | convolution fusion | flops 551833600 | bytes 4272128 | tf_op jit(solution)/shard_map/dot_general | solution.py:39
  39.2 1.2 %fusion.15 = bf16[208,640]{1,0:T(8,128)(2,1)S(1)} fusion(bf16[320,2048]{1,0:T(8,128)(2,1)S(1)} %get-tuple-element.92, bf16[320,2048]{1,0:T(8,128)(2,1)S(1)} %convert_bitcast_fusion.1, bf16[208,4096]{1,0:T(8,128)(2,1)S(1)} %slice_dynamic-update-slice_fusion.3, f32[208,640]{1,0:T(8,128)S(1)} %get-tuple-element.119), kind=kOutput, calls=%fused_computation.28 | convolution fusion | flops 553297920 | bytes 4272128 | tf_op jit(solution)/shard_map/dot_general | solution.py:39
  41.4 1.8 %collective-permute-start.16 = (bf16[40,2048]{1,0:T(8,128)(2,1)S(1)}, bf16[40,2048]{1,0:T(8,128)(2,1)S(1)}, u32[]{:S(2)}, u32[]{:S(2)}) collective-permute-start(bf16[40,2048]{1,0:T(8,128)(2,1)S(1)} %pad_maximum_fusion.19), channel_id=1, source_target_pairs={{0,6},{1,7},{2,4},{3,5},{4,2},{5,3},{6,0},{7,1},{8,14},{9,15},{10,... | collective-permute-start | bytes 491528 | tf_op jit(solution)/shard_map/ppermute | solution.py:169
  43.5 1.5 %collective-permute-start.15 = (bf16[40,2048]{1,0:T(8,128)(2,1)S(1)}, bf16[40,2048]{1,0:T(8,128)(2,1)S(1)}, u32[]{:S(2)}, u32[]{:S(2)}) collective-permute-start(bf16[40,2048]{1,0:T(8,128)(2,1)S(1)} %get-tuple-element.73), channel_id=1, source_target_pairs={{0,2},{1,3},{2,0},{3,1},{4,6},{5,7},{6,4},{7,5},{8,10},{9,11},{10,... | collective-permute-start | bytes 491528 | tf_op jit(solution)/shard_map/ppermute | solution.py:169
  47.2 1.2 %copy-done.1 = f32[2048,320]{0,1:T(8,128)S(1)} copy-done((f32[2048,320]{0,1:T(8,128)S(1)}, f32[2048,320]{0,1:T(8,128)}, u32[]{:S(2)}) %copy-start.1) | copy-done | bytes 2621464
  50.6 1.8 %collective-permute-start.17 = (bf16[40,2048]{1,0:T(8,128)(2,1)S(1)}, bf16[40,2048]{1,0:T(8,128)(2,1)S(1)}, u32[]{:S(2)}, u32[]{:S(2)}) collective-permute-start(bf16[40,2048]{1,0:T(8,128)(2,1)S(1)} %add_convert_fusion.2), channel_id=1, source_target_pairs={{0,8},{1,9},{2,10},{3,11},{4,12},{5,13},{6,14},{7,15},{8,0},{9,1},... | collective-permute-start | bytes 491528 | tf_op jit(solution)/shard_map/ppermute | solution.py:169
  56.3 1.6 %collective-permute-done.19 = bf16[40,2048]{1,0:T(8,128)(2,1)S(1)} collective-permute-done((bf16[40,2048]{1,0:T(8,128)(2,1)S(1)}, bf16[40,2048]{1,0:T(8,128)(2,1)S(1)}, u32[]{:S(2)}, u32[]{:S(2)}) %collective-permute-start.19) | collective-permute-done | bytes 163872 | tf_op jit(solution)/shard_map/ppermute | solution.py:169
  58.0 3.3 %collective-permute-start.22 = (bf16[40,1024]{1,0:T(8,128)(2,1)S(1)}, bf16[40,1024]{1,0:T(8,128)(2,1)S(1)}, u32[]{:S(2)}, u32[]{:S(2)}) collective-permute-start(bf16[40,1024]{1,0:T(8,128)(2,1)S(1)} %pad_maximum_fusion.23), channel_id=1, source_target_pairs={{0,16},{1,17},{2,18},{3,19},{4,20},{5,21},{6,22},{7,23},{8,24},{9,... | collective-permute-start | bytes 245768 | tf_op jit(solution)/shard_map/ppermute | solution.py:212
  61.8 2.6 %shard_map.88 = f32[320,2048]{1,0:T(8,128)} custom-call(f32[320,2048]{1,0:T(8,128)S(1)} %fusion.5.base_ref, bf16[320,2048]{1,0:T(8,128)(2,1)S(1)} %collective-permute-done.21.share_ref), custom_call_target="tpu_custom_call" | custom-call | flops 1310720 | bytes 2621440 | tf_op jit(solution)/shard_map/pallas_call | solution.py:147
  64.4 2.5 %shard_map.87 = f32[320,2048]{1,0:T(8,128)} custom-call(f32[320,2048]{1,0:T(8,128)S(1)} %fusion.4.base_ref, bf16[320,2048]{1,0:T(8,128)(2,1)S(1)} %collective-permute-done.20.share_ref), custom_call_target="tpu_custom_call" | custom-call | flops 1310720 | bytes 2621440 | tf_op jit(solution)/shard_map/pallas_call | solution.py:147
  (91 shorter events, 17.8 us)
Async XLA Ops:
  0.6 14.6 %copy-start = (f32[2048,320]{0,1:T(8,128)S(1)}, f32[2048,320]{0,1:T(8,128)}, u32[]{:S(2)}) copy-start(f32[2048,320]{0,1:T(8,128)} %param.11) | copy-start | bytes 7864324
  3.2 12.6 %collective-permute-start = (bf16[40,2048]{1,0:T(8,128)(2,1)}, bf16[40,2048]{1,0:T(8,128)(2,1)S(1)}, u32[]{:S(2)}, u32[]{:S(2)}) collective-permute-start(bf16[40,2048]{1,0:T(8,128)(2,1)} %get-tuple-element.49.refs_4_), channel_id=1, source_target_pairs={{0,16},{1,17},{2,18},{3,19},{4,20},{5,21},{6,22},{7,23},{8,24},{9,... | collective-permute-start | bytes 491528 | tf_op jit(solution)/shard_map/ppermute | solution.py:212
  7.3 9.1 %collective-permute-start.1 = (bf16[16,4096]{1,0:T(8,128)(2,1)}, bf16[16,4096]{1,0:T(8,128)(2,1)S(1)}, u32[]{:S(2)}, u32[]{:S(2)}) collective-permute-start(bf16[16,4096]{1,0:T(8,128)(2,1)} %get-tuple-element.54), channel_id=1, source_target_pairs={{0,6},{1,7},{2,4},{3,5},{4,2},{5,3},{6,0},{7,1},{8,14},{9,15},{10,... | collective-permute-start | bytes 393224 | tf_op jit(solution)/shard_map/ppermute | solution.py:169
  9.7 7.2 %collective-permute-start.2 = (bf16[16,4096]{1,0:T(8,128)(2,1)}, bf16[16,4096]{1,0:T(8,128)(2,1)S(1)}, u32[]{:S(2)}, u32[]{:S(2)}) collective-permute-start(bf16[16,4096]{1,0:T(8,128)(2,1)} %get-tuple-element.55), channel_id=1, source_target_pairs={{0,8},{1,9},{2,10},{3,11},{4,12},{5,13},{6,14},{7,15},{8,0},{9,1},... | collective-permute-start | bytes 393224 | tf_op jit(solution)/shard_map/ppermute | solution.py:169
  11.3 5.6 %collective-permute-start.3 = (bf16[16,4096]{1,0:T(8,128)(2,1)}, bf16[16,4096]{1,0:T(8,128)(2,1)S(1)}, u32[]{:S(2)}, u32[]{:S(2)}) collective-permute-start(bf16[16,4096]{1,0:T(8,128)(2,1)} %get-tuple-element.56), channel_id=1, source_target_pairs={{0,2},{1,3},{2,0},{3,1},{4,6},{5,7},{6,4},{7,5},{8,10},{9,11},{10,... | collective-permute-start | bytes 393224 | tf_op jit(solution)/shard_map/ppermute | solution.py:169
  11.9 5.2 %collective-permute-start.4 = (bf16[16,4096]{1,0:T(8,128)(2,1)}, bf16[16,4096]{1,0:T(8,128)(2,1)S(1)}, u32[]{:S(2)}, u32[]{:S(2)}) collective-permute-start(bf16[16,4096]{1,0:T(8,128)(2,1)} %get-tuple-element.57), channel_id=1, source_target_pairs={{0,4},{1,5},{2,6},{3,7},{4,0},{5,1},{6,2},{7,3},{8,12},{9,13},{10,... | collective-permute-start | bytes 393224 | tf_op jit(solution)/shard_map/ppermute | solution.py:169
  17.1 8.8 %collective-permute-start.6 = (bf16[40,4096]{1,0:T(8,128)(2,1)S(1)}, bf16[40,4096]{1,0:T(8,128)(2,1)S(1)}, u32[]{:S(2)}, u32[]{:S(2)}) collective-permute-start(bf16[40,4096]{1,0:T(8,128)(2,1)S(1)} %pad_maximum_fusion.17), channel_id=1, source_target_pairs={{0,2},{1,3},{2,0},{3,1},{4,6},{5,7},{6,4},{7,5},{8,10},{9,11},{10,... | collective-permute-start | bytes 983048 | tf_op jit(solution)/shard_map/ppermute | solution.py:169
  18.6 7.8 %collective-permute-start.5 = (bf16[40,4096]{1,0:T(8,128)(2,1)S(1)}, bf16[40,4096]{1,0:T(8,128)(2,1)S(1)}, u32[]{:S(2)}, u32[]{:S(2)}) collective-permute-start(bf16[40,4096]{1,0:T(8,128)(2,1)S(1)} %pad_maximum_fusion.17), channel_id=1, source_target_pairs={{0,4},{1,5},{2,6},{3,7},{4,0},{5,1},{6,2},{7,3},{8,12},{9,13},{10,... | collective-permute-start | bytes 983048 | tf_op jit(solution)/shard_map/ppermute | solution.py:169
  19.6 10.0 %collective-permute-start.8 = (bf16[24,4096]{1,0:T(8,128)(2,1)S(1)}, bf16[24,4096]{1,0:T(8,128)(2,1)S(1)}, u32[]{:S(2)}, u32[]{:S(2)}) collective-permute-start(bf16[24,4096]{1,0:T(8,128)(2,1)S(1)} %get-tuple-element.64), channel_id=1, source_target_pairs={{0,8},{1,9},{2,10},{3,11},{4,12},{5,13},{6,14},{7,15},{8,0},{9,1},... | collective-permute-start | bytes 589832 | tf_op jit(solution)/shard_map/ppermute | solution.py:169
  20.9 10.5 %collective-permute-start.7 = (bf16[640,2048]{1,0:T(8,128)(2,1)S(1)}, bf16[640,2048]{1,0:T(8,128)(2,1)S(1)}, u32[]{:S(2)}, u32[]{:S(2)}) collective-permute-start(bf16[640,2048]{1,0:T(8,128)(2,1)S(1)} %pad_maximum_fusion.1), channel_id=1, source_target_pairs={{0,1},{1,0},{2,3},{3,2},{4,5},{5,4},{6,7},{7,6},{8,9},{9,8},{10,11... | collective-permute-start | bytes 7864328 | tf_op jit(solution)/shard_map/ppermute | solution.py:169
  26.5 11.4 %collective-permute-start.9 = (bf16[24,4096]{1,0:T(8,128)(2,1)S(1)}, bf16[24,4096]{1,0:T(8,128)(2,1)S(1)}, u32[]{:S(2)}, u32[]{:S(2)}) collective-permute-start(bf16[24,4096]{1,0:T(8,128)(2,1)S(1)} %get-tuple-element.110), channel_id=1, source_target_pairs={{0,4},{1,5},{2,6},{3,7},{4,0},{5,1},{6,2},{7,3},{8,12},{9,13},{10,... | collective-permute-start | bytes 589832 | tf_op jit(solution)/shard_map/ppermute | solution.py:169
  27.8 10.1 %collective-permute-start.10 = (bf16[40,4096]{1,0:T(8,128)(2,1)S(1)}, bf16[40,4096]{1,0:T(8,128)(2,1)S(1)}, u32[]{:S(2)}, u32[]{:S(2)}) collective-permute-start(bf16[40,4096]{1,0:T(8,128)(2,1)S(1)} %pad_maximum_fusion.18), channel_id=1, source_target_pairs={{0,8},{1,9},{2,10},{3,11},{4,12},{5,13},{6,14},{7,15},{8,0},{9,1},... | collective-permute-start | bytes 983048 | tf_op jit(solution)/shard_map/ppermute | solution.py:169
  29.6 8.3 %collective-permute-start.12 = (bf16[24,4096]{1,0:T(8,128)(2,1)S(1)}, bf16[24,4096]{1,0:T(8,128)(2,1)S(1)}, u32[]{:S(2)}, u32[]{:S(2)}) collective-permute-start(bf16[24,4096]{1,0:T(8,128)(2,1)S(1)} %collective-permute-done.8), channel_id=1, source_target_pairs={{0,6},{1,7},{2,4},{3,5},{4,2},{5,3},{6,0},{7,1},{8,14},{9,15},{10,... | collective-permute-start | bytes 589832 | tf_op jit(solution)/shard_map/ppermute | solution.py:169
  29.9 8.0 %collective-permute-start.11 = (bf16[24,4096]{1,0:T(8,128)(2,1)S(1)}, bf16[24,4096]{1,0:T(8,128)(2,1)S(1)}, u32[]{:S(2)}, u32[]{:S(2)}) collective-permute-start(bf16[24,4096]{1,0:T(8,128)(2,1)S(1)} %collective-permute-done.8), channel_id=1, source_target_pairs={{0,2},{1,3},{2,0},{3,1},{4,6},{5,7},{6,4},{7,5},{8,10},{9,11},{10,... | collective-permute-start | bytes 589832 | tf_op jit(solution)/shard_map/ppermute | solution.py:169
  41.4 9.1 %collective-permute-start.16 = (bf16[40,2048]{1,0:T(8,128)(2,1)S(1)}, bf16[40,2048]{1,0:T(8,128)(2,1)S(1)}, u32[]{:S(2)}, u32[]{:S(2)}) collective-permute-start(bf16[40,2048]{1,0:T(8,128)(2,1)S(1)} %pad_maximum_fusion.19), channel_id=1, source_target_pairs={{0,6},{1,7},{2,4},{3,5},{4,2},{5,3},{6,0},{7,1},{8,14},{9,15},{10,... | collective-permute-start | bytes 491528 | tf_op jit(solution)/shard_map/ppermute | solution.py:169
  43.2 5.7 %collective-permute-start.13 = (bf16[40,2048]{1,0:T(8,128)(2,1)S(1)}, bf16[40,2048]{1,0:T(8,128)(2,1)S(1)}, u32[]{:S(2)}, u32[]{:S(2)}) collective-permute-start(bf16[40,2048]{1,0:T(8,128)(2,1)S(1)} %pad_maximum_fusion.20), channel_id=1, source_target_pairs={{0,8},{1,9},{2,10},{3,11},{4,12},{5,13},{6,14},{7,15},{8,0},{9,1},... | collective-permute-start | bytes 491528 | tf_op jit(solution)/shard_map/ppermute | solution.py:169
  43.5 6.1 %collective-permute-start.15 = (bf16[40,2048]{1,0:T(8,128)(2,1)S(1)}, bf16[40,2048]{1,0:T(8,128)(2,1)S(1)}, u32[]{:S(2)}, u32[]{:S(2)}) collective-permute-start(bf16[40,2048]{1,0:T(8,128)(2,1)S(1)} %get-tuple-element.73), channel_id=1, source_target_pairs={{0,2},{1,3},{2,0},{3,1},{4,6},{5,7},{6,4},{7,5},{8,10},{9,11},{10,... | collective-permute-start | bytes 491528 | tf_op jit(solution)/shard_map/ppermute | solution.py:169
  45.0 7.4 %collective-permute-start.18 = (bf16[40,2048]{1,0:T(8,128)(2,1)S(1)}, bf16[40,2048]{1,0:T(8,128)(2,1)S(1)}, u32[]{:S(2)}, u32[]{:S(2)}) collective-permute-start(bf16[40,2048]{1,0:T(8,128)(2,1)S(1)} %get-tuple-element.74), channel_id=1, source_target_pairs={{0,4},{1,5},{2,6},{3,7},{4,0},{5,1},{6,2},{7,3},{8,12},{9,13},{10,... | collective-permute-start | bytes 491528 | tf_op jit(solution)/shard_map/ppermute | solution.py:169
  49.6 8.2 %collective-permute-start.14 = (bf16[40,2048]{1,0:T(8,128)(2,1)S(1)}, bf16[40,2048]{1,0:T(8,128)(2,1)S(1)}, u32[]{:S(2)}, u32[]{:S(2)}) collective-permute-start(bf16[40,2048]{1,0:T(8,128)(2,1)S(1)} %add_convert_fusion.3), channel_id=1, source_target_pairs={{0,4},{1,5},{2,6},{3,7},{4,0},{5,1},{6,2},{7,3},{8,12},{9,13},{10,... | collective-permute-start | bytes 491528 | tf_op jit(solution)/shard_map/ppermute | solution.py:169
  50.6 7.3 %collective-permute-start.17 = (bf16[40,2048]{1,0:T(8,128)(2,1)S(1)}, bf16[40,2048]{1,0:T(8,128)(2,1)S(1)}, u32[]{:S(2)}, u32[]{:S(2)}) collective-permute-start(bf16[40,2048]{1,0:T(8,128)(2,1)S(1)} %add_convert_fusion.2), channel_id=1, source_target_pairs={{0,8},{1,9},{2,10},{3,11},{4,12},{5,13},{6,14},{7,15},{8,0},{9,1},... | collective-permute-start | bytes 491528 | tf_op jit(solution)/shard_map/ppermute | solution.py:169
  52.5 5.4 %collective-permute-start.19 = (bf16[40,2048]{1,0:T(8,128)(2,1)S(1)}, bf16[40,2048]{1,0:T(8,128)(2,1)S(1)}, u32[]{:S(2)}, u32[]{:S(2)}) collective-permute-start(bf16[40,2048]{1,0:T(8,128)(2,1)S(1)} %add_convert_fusion.1), channel_id=1, source_target_pairs={{0,2},{1,3},{2,0},{3,1},{4,6},{5,7},{6,4},{7,5},{8,10},{9,11},{10,... | collective-permute-start | bytes 491528 | tf_op jit(solution)/shard_map/ppermute | solution.py:169
  54.4 7.5 %collective-permute-start.21 = (bf16[320,2048]{1,0:T(8,128)(2,1)S(1)}, bf16[320,2048]{1,0:T(8,128)(2,1)S(1)}, u32[]{:S(2)}, u32[]{:S(2)}) collective-permute-start(bf16[320,2048]{1,0:T(8,128)(2,1)S(1)} %fusion.7), channel_id=1, source_target_pairs={{0,1},{1,0},{2,3},{3,2},{4,5},{5,4},{6,7},{7,6},{8,9},{9,8},{10,11... | collective-permute-start | bytes 3932168 | tf_op jit(solution)/shard_map/ppermute | solution.py:169
  55.7 8.7 %collective-permute-start.20 = (bf16[320,2048]{1,0:T(8,128)(2,1)S(1)}, bf16[320,2048]{1,0:T(8,128)(2,1)S(1)}, u32[]{:S(2)}, u32[]{:S(2)}) collective-permute-start(bf16[320,2048]{1,0:T(8,128)(2,1)S(1)} %fusion.6), channel_id=1, source_target_pairs={{0,1},{1,0},{2,3},{3,2},{4,5},{5,4},{6,7},{7,6},{8,9},{9,8},{10,11... | collective-permute-start | bytes 3932168 | tf_op jit(solution)/shard_map/ppermute | solution.py:169
  58.0 8.9 %collective-permute-start.22 = (bf16[40,1024]{1,0:T(8,128)(2,1)S(1)}, bf16[40,1024]{1,0:T(8,128)(2,1)S(1)}, u32[]{:S(2)}, u32[]{:S(2)}) collective-permute-start(bf16[40,1024]{1,0:T(8,128)(2,1)S(1)} %pad_maximum_fusion.23), channel_id=1, source_target_pairs={{0,16},{1,17},{2,18},{3,19},{4,20},{5,21},{6,22},{7,23},{8,24},{9,... | collective-permute-start | bytes 245768 | tf_op jit(solution)/shard_map/ppermute | solution.py:212
  (5 other events, 18.0 us)

commit v15 on v13

--- a/solution.py
+++ b/solution.py
@@ -113,6 +113,7 @@
         out_shape=shapes,
         in_specs=[whole] * 4,
         out_specs=[whole] * len(shapes),
+        compiler_params=pltpu.CompilerParams(vmem_limit_bytes=8 * 1024 * 1024),
     )(ids.reshape(1, n), gate.reshape(1, n), tokens, grads)
     return outs[: len(blocks)], outs[len(blocks) : 2 * len(blocks)], outs[2 * len(blocks) :]
 
@@ -125,6 +126,7 @@
         in_specs=[anywhere] * (len(copies) + len(sent)),
         out_specs=[anywhere] * len(copies),
         input_output_aliases={k: k for k in range(len(copies))},
+        compiler_params=pltpu.CompilerParams(vmem_limit_bytes=1024 * 1024),
     )(*copies, *sent)
 
 
@@ -153,7 +155,7 @@
         out_shape=[jax.ShapeDtypeStruct(base.shape, base.dtype) for base in bases],
         in_specs=[whole] * (2 * len(bases)),
         out_specs=[pl.BlockSpec((rows, width), lambda i: (i, 0))] * len(bases),
-        compiler_params=pltpu.CompilerParams(vmem_limit_bytes=32 * 1024 * 1024),
+        compiler_params=pltpu.CompilerParams(vmem_limit_bytes=14 * 1024 * 1024),
         cost_estimate=pl.CostEstimate(
             flops=4 * units * width, bytes_accessed=8 * units * width, transcendentals=0
         ),

time: 65.5 us -> 66.3 us (1.012)
  Pallas kernels: 5.67 us -> 3.52 us
  local copies, waits for them, and re-layouts: 3.19 us -> 5.08 us
    pallas_call x1, Pallas kernels: 2.55 us -> 0.39 us  [pack(): pl.pallas_call(lambda *refs: pack_kernel(blocks, experts, *refs), out_sha...]
    unnamed x22, local copies, waits for them, and re-layouts: 2.74 us -> 4.51 us
  transfers between devices with their start and end apart: 23 -> 23, of which waited for: 7 -> 8; matrix products, arithmetic and copies ran while one was open for 18% -> 17% of each run, Pallas kernels for 5% -> 5%
where the time goes in v15:
time: 66.3 us; the launch traced here: 66 us
  starting transfers between devices  31.7 us (48%)
  matrix products  11.9 us (18%)
  waiting for transfers between devices  9.93 us (15%)
  local copies, waits for them, and re-layouts  5.08 us (8%)
  Pallas kernels  3.52 us (5%)
  other arithmetic  2.85 us (4%)
  between operations  1.05 us (2%)
    ppermute x21, starting transfers between devices, swap(): lax.ppermute(rows, 'expert', [(i, i ^ mask) for i in range(n_expert)])  23.2 us
    ppermute x21, waiting for transfers between devices, swap(): lax.ppermute(rows, 'expert', [(i, i ^ mask) for i in range(n_expert)])  9.66 us
    ppermute x2, starting transfers between devices, shifted(): return lax.ppermute(rows, 'expert', pairs)  8.58 us
    dot_general x11, matrix products, contract_rows(): lax.dot_general(left, right, (((0,), (0,)), ((), ())), preferred_element_...  6.08 us
    unnamed x22, local copies, waits for them, and re-layouts  4.51 us
    dot_general x4, matrix products, contract_cols(): lax.dot_general(left, right, (((1,), (1,)), ((), ())), preferred_element_...  4.37 us
    pallas_call x1, Pallas kernels, stepped(): pl.pallas_call(step_kernel, grid=(units // rows,), out_shape=[jax.ShapeDt...  3.12 us
    transpose x1, other arithmetic, shards(): whole_weights(w_in)  1.93 us
  transfers between devices with their start and end apart: 23, of which 8 were waited for; matrix products, arithmetic and copies ran while one was open for 17% of the time, Pallas kernels for 5%

profile of v15, /device:TPU:0, one launch (start us, length us, event | category | flops | bytes accessed | tf_op | source)
XLA Modules:
  0.0 66.0 jit_solution(1585269903531097382)
XLA Ops:
  4.2 4.1 %collective-permute-start = (bf16[40,2048]{1,0:T(8,128)(2,1)S(1)}, bf16[40,2048]{1,0:T(8,128)(2,1)S(1)}, u32[]{:S(2)}, u32[]{:S(2)}) collective-permute-start(bf16[40,2048]{1,0:T(8,128)(2,1)S(1)} %get-tuple-element.51.refs_4_), channel_id=1, source_target_pairs={{0,16},{1,17},{2,18},{3,19},{4,20},{5,21},{6,22},{7,23},{8,24},{9,... | collective-permute-start | bytes 491528 | tf_op jit(solution)/shard_map/ppermute | solution.py:217
  8.4 2.4 %collective-permute-start.1 = (bf16[16,4096]{1,0:T(8,128)(2,1)S(1)}, bf16[16,4096]{1,0:T(8,128)(2,1)S(1)}, u32[]{:S(2)}, u32[]{:S(2)}) collective-permute-start(bf16[16,4096]{1,0:T(8,128)(2,1)S(1)} %get-tuple-element.56), channel_id=1, source_target_pairs={{0,6},{1,7},{2,4},{3,5},{4,2},{5,3},{6,0},{7,1},{8,14},{9,15},{10,... | collective-permute-start | bytes 393224 | tf_op jit(solution)/shard_map/ppermute | solution.py:174
  10.8 1.6 %collective-permute-start.2 = (bf16[16,4096]{1,0:T(8,128)(2,1)S(1)}, bf16[16,4096]{1,0:T(8,128)(2,1)S(1)}, u32[]{:S(2)}, u32[]{:S(2)}) collective-permute-start(bf16[16,4096]{1,0:T(8,128)(2,1)S(1)} %get-tuple-element.57), channel_id=1, source_target_pairs={{0,8},{1,9},{2,10},{3,11},{4,12},{5,13},{6,14},{7,15},{8,0},{9,1},... | collective-permute-start | bytes 393224 | tf_op jit(solution)/shard_map/ppermute | solution.py:174
  13.4 1.9 %convert_bitcast_fusion = bf16[320,2048]{1,0:T(8,128)(2,1)S(1)} fusion(f32[2048,320]{0,1:T(8,128)} %param.10), kind=kLoop, calls=%fused_computation.24 | loop fusion | flops 655360 | bytes 3932160 | tf_op jit(solution)/shard_map/transpose | solution.py:260
  16.3 1.5 %collective-permute-done.2 = bf16[16,4096]{1,0:T(8,128)(2,1)S(1)} collective-permute-done((bf16[16,4096]{1,0:T(8,128)(2,1)S(1)}, bf16[16,4096]{1,0:T(8,128)(2,1)S(1)}, u32[]{:S(2)}, u32[]{:S(2)}) %collective-permute-start.2) | collective-permute-done | bytes 131104 | tf_op jit(solution)/shard_map/ppermute | solution.py:174
  17.9 1.5 %collective-permute-start.6 = (bf16[40,4096]{1,0:T(8,128)(2,1)S(1)}, bf16[40,4096]{1,0:T(8,128)(2,1)S(1)}, u32[]{:S(2)}, u32[]{:S(2)}) collective-permute-start(bf16[40,4096]{1,0:T(8,128)(2,1)S(1)} %get-tuple-element.64), channel_id=1, source_target_pairs={{0,2},{1,3},{2,0},{3,1},{4,6},{5,7},{6,4},{7,5},{8,10},{9,11},{10,... | collective-permute-start | bytes 983048 | tf_op jit(solution)/shard_map/ppermute | solution.py:174
  20.3 1.4 %collective-permute-start.7 = (bf16[40,4096]{1,0:T(8,128)(2,1)S(1)}, bf16[40,4096]{1,0:T(8,128)(2,1)S(1)}, u32[]{:S(2)}, u32[]{:S(2)}) collective-permute-start(bf16[40,4096]{1,0:T(8,128)(2,1)S(1)} %get-tuple-element.65), channel_id=1, source_target_pairs={{0,8},{1,9},{2,10},{3,11},{4,12},{5,13},{6,14},{7,15},{8,0},{9,1},... | collective-permute-start | bytes 983048 | tf_op jit(solution)/shard_map/ppermute | solution.py:174
  21.9 4.9 %collective-permute-done.6 = bf16[40,4096]{1,0:T(8,128)(2,1)S(1)} collective-permute-done((bf16[40,4096]{1,0:T(8,128)(2,1)S(1)}, bf16[40,4096]{1,0:T(8,128)(2,1)S(1)}, u32[]{:S(2)}, u32[]{:S(2)}) %collective-permute-start.6) | collective-permute-done | bytes 327712 | tf_op jit(solution)/shard_map/ppermute | solution.py:174
  28.3 1.5 %collective-permute-start.12 = (bf16[24,4096]{1,0:T(8,128)(2,1)S(1)}, bf16[24,4096]{1,0:T(8,128)(2,1)S(1)}, u32[]{:S(2)}, u32[]{:S(2)}) collective-permute-start(bf16[24,4096]{1,0:T(8,128)(2,1)S(1)} %get-tuple-element.67), channel_id=1, source_target_pairs={{0,6},{1,7},{2,4},{3,5},{4,2},{5,3},{6,0},{7,1},{8,14},{9,15},{10,... | collective-permute-start | bytes 589832 | tf_op jit(solution)/shard_map/ppermute | solution.py:174
  30.6 1.3 %collective-permute-start.10 = (bf16[24,4096]{1,0:T(8,128)(2,1)S(1)}, bf16[24,4096]{1,0:T(8,128)(2,1)S(1)}, u32[]{:S(2)}, u32[]{:S(2)}) collective-permute-start(bf16[24,4096]{1,0:T(8,128)(2,1)S(1)} %get-tuple-element.68), channel_id=1, source_target_pairs={{0,8},{1,9},{2,10},{3,11},{4,12},{5,13},{6,14},{7,15},{8,0},{9,1},... | collective-permute-start | bytes 589832 | tf_op jit(solution)/shard_map/ppermute | solution.py:174
  31.9 1.7 %collective-permute-start.9 = (bf16[24,4096]{1,0:T(8,128)(2,1)S(1)}, bf16[24,4096]{1,0:T(8,128)(2,1)S(1)}, u32[]{:S(2)}, u32[]{:S(2)}) collective-permute-start(bf16[24,4096]{1,0:T(8,128)(2,1)S(1)} %get-tuple-element.69), channel_id=1, source_target_pairs={{0,4},{1,5},{2,6},{3,7},{4,0},{5,1},{6,2},{7,3},{8,12},{9,13},{10,... | collective-permute-start | bytes 589832 | tf_op jit(solution)/shard_map/ppermute | solution.py:174
  34.0 1.0 %multiply_convert_fusion.1 = (bf16[128,640]{1,0:T(8,128)(2,1)S(1)}, f32[128,640]{1,0:T(8,128)S(1)}) fusion(bf16[320,2048]{1,0:T(8,128)(2,1)S(1)} %convert_bitcast_fusion, bf16[320,2048]{1,0:T(8,128)(2,1)S(1)} %get-tuple-element.95, bf16[128,4096]{1,0:T(8,128)(2,1)S(1)} %slice_dynamic-update-slice_fusion), kind=kOutput, calls=%fused_computation.67 | convolution fusion | flops 341606400 | bytes 3637248 | tf_op jit(solution)/shard_map/dot_general | solution.py:39
  35.0 1.0 %fusion.18 = bf16[128,640]{1,0:T(8,128)(2,1)S(1)} fusion(bf16[320,2048]{1,0:T(8,128)(2,1)S(1)} %get-tuple-element.96, bf16[320,2048]{1,0:T(8,128)(2,1)S(1)} %convert_bitcast_fusion.1, bf16[128,4096]{1,0:T(8,128)(2,1)S(1)} %slice_dynamic-update-slice_fusion, f32[128,640]{1,0:T(8,128)S(1)} %get-tuple-element.130), kind=kOutput, calls=%fused_computation.31 | convolution fusion | flops 342507520 | bytes 3637248 | tf_op jit(solution)/shard_map/dot_general | solution.py:39
  36.7 1.3 %collective-permute-done.9 = bf16[24,4096]{1,0:T(8,128)(2,1)S(1)} collective-permute-done((bf16[24,4096]{1,0:T(8,128)(2,1)S(1)}, bf16[24,4096]{1,0:T(8,128)(2,1)S(1)}, u32[]{:S(2)}, u32[]{:S(2)}) %collective-permute-start.9) | collective-permute-done | bytes 196640 | tf_op jit(solution)/shard_map/ppermute | solution.py:174
  38.1 1.1 %multiply_convert_fusion = (bf16[192,640]{1,0:T(8,128)(2,1)S(1)}, f32[192,640]{1,0:T(8,128)S(1)}) fusion(bf16[320,2048]{1,0:T(8,128)(2,1)S(1)} %convert_bitcast_fusion, bf16[320,2048]{1,0:T(8,128)(2,1)S(1)} %get-tuple-element.95, bf16[192,4096]{1,0:T(8,128)(2,1)S(1)} %constant_dynamic-update-slice_fusion.5), kind=kOutput, calls=%fused_computation.46 | convolution fusion | flops 509788160 | bytes 4145152 | tf_op jit(solution)/shard_map/dot_general | solution.py:39
  39.3 1.2 %fusion.15 = bf16[192,640]{1,0:T(8,128)(2,1)S(1)} fusion(bf16[320,2048]{1,0:T(8,128)(2,1)S(1)} %get-tuple-element.96, bf16[320,2048]{1,0:T(8,128)(2,1)S(1)} %convert_bitcast_fusion.1, bf16[192,4096]{1,0:T(8,128)(2,1)S(1)} %constant_dynamic-update-slice_fusion.5, f32[192,640]{1,0:T(8,128)S(1)} %get-tuple-element.128), kind=kOutput, calls=%fused_computation.28 | convolution fusion | flops 511139840 | bytes 4145152 | tf_op jit(solution)/shard_map/dot_general | solution.py:39
  41.3 1.5 %collective-permute-start.14 = (bf16[40,2048]{1,0:T(8,128)(2,1)S(1)}, bf16[40,2048]{1,0:T(8,128)(2,1)S(1)}, u32[]{:S(2)}, u32[]{:S(2)}) collective-permute-start(bf16[40,2048]{1,0:T(8,128)(2,1)S(1)} %pad_maximum_fusion.19), channel_id=1, source_target_pairs={{0,6},{1,7},{2,4},{3,5},{4,2},{5,3},{6,0},{7,1},{8,14},{9,15},{10,... | collective-permute-start | bytes 491528 | tf_op jit(solution)/shard_map/ppermute | solution.py:174
  42.9 1.5 %collective-permute-start.13 = (bf16[40,2048]{1,0:T(8,128)(2,1)S(1)}, bf16[40,2048]{1,0:T(8,128)(2,1)S(1)}, u32[]{:S(2)}, u32[]{:S(2)}) collective-permute-start(bf16[40,2048]{1,0:T(8,128)(2,1)S(1)} %get-tuple-element.74), channel_id=1, source_target_pairs={{0,2},{1,3},{2,0},{3,1},{4,6},{5,7},{6,4},{7,5},{8,10},{9,11},{10,... | collective-permute-start | bytes 491528 | tf_op jit(solution)/shard_map/ppermute | solution.py:174
  45.0 1.8 %collective-permute-start.18 = (bf16[40,2048]{1,0:T(8,128)(2,1)S(1)}, bf16[40,2048]{1,0:T(8,128)(2,1)S(1)}, u32[]{:S(2)}, u32[]{:S(2)}) collective-permute-start(bf16[40,2048]{1,0:T(8,128)(2,1)S(1)} %pad_maximum_fusion.22), channel_id=1, source_target_pairs={{0,8},{1,9},{2,10},{3,11},{4,12},{5,13},{6,14},{7,15},{8,0},{9,1},... | collective-permute-start | bytes 491528 | tf_op jit(solution)/shard_map/ppermute | solution.py:174
  48.5 1.2 %copy-done.5 = f32[2048,320]{0,1:T(8,128)S(1)} copy-done((f32[2048,320]{0,1:T(8,128)S(1)}, f32[2048,320]{0,1:T(8,128)}, u32[]{:S(2)}) %copy-start.5) | copy-done | bytes 2621464
  51.4 1.9 %collective-permute-start.19 = (bf16[40,2048]{1,0:T(8,128)(2,1)S(1)}, bf16[40,2048]{1,0:T(8,128)(2,1)S(1)}, u32[]{:S(2)}, u32[]{:S(2)}) collective-permute-start(bf16[40,2048]{1,0:T(8,128)(2,1)S(1)} %add_convert_fusion.1), channel_id=1, source_target_pairs={{0,4},{1,5},{2,6},{3,7},{4,0},{5,1},{6,2},{7,3},{8,12},{9,13},{10,... | collective-permute-start | bytes 491528 | tf_op jit(solution)/shard_map/ppermute | solution.py:174
  56.9 4.5 %collective-permute-start.22 = (bf16[40,1024]{1,0:T(8,128)(2,1)S(1)}, bf16[40,1024]{1,0:T(8,128)(2,1)S(1)}, u32[]{:S(2)}, u32[]{:S(2)}) collective-permute-start(bf16[40,1024]{1,0:T(8,128)(2,1)S(1)} %pad_maximum_fusion.23), channel_id=1, source_target_pairs={{0,16},{1,17},{2,18},{3,19},{4,20},{5,21},{6,22},{7,23},{8,24},{9,... | collective-permute-start | bytes 245768 | tf_op jit(solution)/shard_map/ppermute | solution.py:217
  61.9 3.1 %shard_map.87 = (f32[320,2048]{1,0:T(8,128)}, f32[320,2048]{1,0:T(8,128)}) custom-call(f32[320,2048]{1,0:T(8,128)S(1)} %fusion.5.refs_0_, f32[320,2048]{1,0:T(8,128)S(1)} %fusion.3.refs_1_, bf16[320,2048]{1,0:T(8,128)(2,1)S(1)} %collective-permute-done.20.refs_2_, bf16[320,2048]{1,0:T(8,128)(2,1)S(1)} %collective-permute-done.21.refs_3_), custom_call_target="tpu_custom_call" | custom-call | flops 2621440 | bytes 5242880 | tf_op jit(solution)/shard_map/pallas_call | solution.py:152
  65.1 1.0 %fusion.10 = bf16[64,2048]{1,0:T(8,128)(2,1)} fusion(f32[64,2048]{1,0:T(8,128)S(1)} %convolution_add_fusion.5, bf16[20,1024]{1,0:T(8,128)(2,1)S(1)} %get-tuple-element.126, bf16[20,1024]{1,0:T(8,128)(2,1)S(1)} %get-tuple-element.125, bf16[40,64]{1,0:T(8,128)(2,1)S(1)} %get-tuple-element.85), kind=kOutput, calls=%fused_computation.21 | convolution fusion | flops 5668864 | bytes 890880 | tf_op jit(solution)/shard_map/dot_general | solution.py:33
  (88 shorter events, 18.9 us)
Async XLA Ops:
  3.8 11.5 %copy-start.4 = (f32[2048,320]{0,1:T(8,128)S(1)}, f32[2048,320]{0,1:T(8,128)}, u32[]{:S(2)}) copy-start(f32[2048,320]{0,1:T(8,128)} %param.11) | copy-start | bytes 7864324
  4.2 11.9 %collective-permute-start = (bf16[40,2048]{1,0:T(8,128)(2,1)S(1)}, bf16[40,2048]{1,0:T(8,128)(2,1)S(1)}, u32[]{:S(2)}, u32[]{:S(2)}) collective-permute-start(bf16[40,2048]{1,0:T(8,128)(2,1)S(1)} %get-tuple-element.51.refs_4_), channel_id=1, source_target_pairs={{0,16},{1,17},{2,18},{3,19},{4,20},{5,21},{6,22},{7,23},{8,24},{9,... | collective-permute-start | bytes 491528 | tf_op jit(solution)/shard_map/ppermute | solution.py:217
  8.4 7.9 %collective-permute-start.1 = (bf16[16,4096]{1,0:T(8,128)(2,1)S(1)}, bf16[16,4096]{1,0:T(8,128)(2,1)S(1)}, u32[]{:S(2)}, u32[]{:S(2)}) collective-permute-start(bf16[16,4096]{1,0:T(8,128)(2,1)S(1)} %get-tuple-element.56), channel_id=1, source_target_pairs={{0,6},{1,7},{2,4},{3,5},{4,2},{5,3},{6,0},{7,1},{8,14},{9,15},{10,... | collective-permute-start | bytes 393224 | tf_op jit(solution)/shard_map/ppermute | solution.py:174
  10.8 7.0 %collective-permute-start.2 = (bf16[16,4096]{1,0:T(8,128)(2,1)S(1)}, bf16[16,4096]{1,0:T(8,128)(2,1)S(1)}, u32[]{:S(2)}, u32[]{:S(2)}) collective-permute-start(bf16[16,4096]{1,0:T(8,128)(2,1)S(1)} %get-tuple-element.57), channel_id=1, source_target_pairs={{0,8},{1,9},{2,10},{3,11},{4,12},{5,13},{6,14},{7,15},{8,0},{9,1},... | collective-permute-start | bytes 393224 | tf_op jit(solution)/shard_map/ppermute | solution.py:174
  12.4 5.5 %collective-permute-start.3 = (bf16[16,4096]{1,0:T(8,128)(2,1)S(1)}, bf16[16,4096]{1,0:T(8,128)(2,1)S(1)}, u32[]{:S(2)}, u32[]{:S(2)}) collective-permute-start(bf16[16,4096]{1,0:T(8,128)(2,1)S(1)} %get-tuple-element.58), channel_id=1, source_target_pairs={{0,2},{1,3},{2,0},{3,1},{4,6},{5,7},{6,4},{7,5},{8,10},{9,11},{10,... | collective-permute-start | bytes 393224 | tf_op jit(solution)/shard_map/ppermute | solution.py:174
  12.9 5.0 %collective-permute-start.4 = (bf16[16,4096]{1,0:T(8,128)(2,1)S(1)}, bf16[16,4096]{1,0:T(8,128)(2,1)S(1)}, u32[]{:S(2)}, u32[]{:S(2)}) collective-permute-start(bf16[16,4096]{1,0:T(8,128)(2,1)S(1)} %get-tuple-element.59), channel_id=1, source_target_pairs={{0,4},{1,5},{2,6},{3,7},{4,0},{5,1},{6,2},{7,3},{8,12},{9,13},{10,... | collective-permute-start | bytes 393224 | tf_op jit(solution)/shard_map/ppermute | solution.py:174
  17.9 8.8 %collective-permute-start.6 = (bf16[40,4096]{1,0:T(8,128)(2,1)S(1)}, bf16[40,4096]{1,0:T(8,128)(2,1)S(1)}, u32[]{:S(2)}, u32[]{:S(2)}) collective-permute-start(bf16[40,4096]{1,0:T(8,128)(2,1)S(1)} %get-tuple-element.64), channel_id=1, source_target_pairs={{0,2},{1,3},{2,0},{3,1},{4,6},{5,7},{6,4},{7,5},{8,10},{9,11},{10,... | collective-permute-start | bytes 983048 | tf_op jit(solution)/shard_map/ppermute | solution.py:174
  19.5 7.8 %collective-permute-start.5 = (bf16[40,4096]{1,0:T(8,128)(2,1)S(1)}, bf16[40,4096]{1,0:T(8,128)(2,1)S(1)}, u32[]{:S(2)}, u32[]{:S(2)}) collective-permute-start(bf16[40,4096]{1,0:T(8,128)(2,1)S(1)} %get-tuple-element.64), channel_id=1, source_target_pairs={{0,4},{1,5},{2,6},{3,7},{4,0},{5,1},{6,2},{7,3},{8,12},{9,13},{10,... | collective-permute-start | bytes 983048 | tf_op jit(solution)/shard_map/ppermute | solution.py:174
  20.3 8.0 %collective-permute-start.7 = (bf16[40,4096]{1,0:T(8,128)(2,1)S(1)}, bf16[40,4096]{1,0:T(8,128)(2,1)S(1)}, u32[]{:S(2)}, u32[]{:S(2)}) collective-permute-start(bf16[40,4096]{1,0:T(8,128)(2,1)S(1)} %get-tuple-element.65), channel_id=1, source_target_pairs={{0,8},{1,9},{2,10},{3,11},{4,12},{5,13},{6,14},{7,15},{8,0},{9,1},... | collective-permute-start | bytes 983048 | tf_op jit(solution)/shard_map/ppermute | solution.py:174
  21.8 11.9 %collective-permute-start.8 = (bf16[640,2048]{1,0:T(8,128)(2,1)S(1)}, bf16[640,2048]{1,0:T(8,128)(2,1)S(1)}, u32[]{:S(2)}, u32[]{:S(2)}) collective-permute-start(bf16[640,2048]{1,0:T(8,128)(2,1)S(1)} %pad_maximum_fusion.1), channel_id=1, source_target_pairs={{0,1},{1,0},{2,3},{3,2},{4,5},{5,4},{6,7},{7,6},{8,9},{9,8},{10,11... | collective-permute-start | bytes 7864328 | tf_op jit(solution)/shard_map/ppermute | solution.py:174
  28.3 9.7 %collective-permute-start.12 = (bf16[24,4096]{1,0:T(8,128)(2,1)S(1)}, bf16[24,4096]{1,0:T(8,128)(2,1)S(1)}, u32[]{:S(2)}, u32[]{:S(2)}) collective-permute-start(bf16[24,4096]{1,0:T(8,128)(2,1)S(1)} %get-tuple-element.67), channel_id=1, source_target_pairs={{0,6},{1,7},{2,4},{3,5},{4,2},{5,3},{6,0},{7,1},{8,14},{9,15},{10,... | collective-permute-start | bytes 589832 | tf_op jit(solution)/shard_map/ppermute | solution.py:174
  29.8 8.3 %collective-permute-start.11 = (bf16[24,4096]{1,0:T(8,128)(2,1)S(1)}, bf16[24,4096]{1,0:T(8,128)(2,1)S(1)}, u32[]{:S(2)}, u32[]{:S(2)}) collective-permute-start(bf16[24,4096]{1,0:T(8,128)(2,1)S(1)} %get-tuple-element.67), channel_id=1, source_target_pairs={{0,2},{1,3},{2,0},{3,1},{4,6},{5,7},{6,4},{7,5},{8,10},{9,11},{10,... | collective-permute-start | bytes 589832 | tf_op jit(solution)/shard_map/ppermute | solution.py:174
  30.6 7.4 %collective-permute-start.10 = (bf16[24,4096]{1,0:T(8,128)(2,1)S(1)}, bf16[24,4096]{1,0:T(8,128)(2,1)S(1)}, u32[]{:S(2)}, u32[]{:S(2)}) collective-permute-start(bf16[24,4096]{1,0:T(8,128)(2,1)S(1)} %get-tuple-element.68), channel_id=1, source_target_pairs={{0,8},{1,9},{2,10},{3,11},{4,12},{5,13},{6,14},{7,15},{8,0},{9,1},... | collective-permute-start | bytes 589832 | tf_op jit(solution)/shard_map/ppermute | solution.py:174
  31.9 6.1 %collective-permute-start.9 = (bf16[24,4096]{1,0:T(8,128)(2,1)S(1)}, bf16[24,4096]{1,0:T(8,128)(2,1)S(1)}, u32[]{:S(2)}, u32[]{:S(2)}) collective-permute-start(bf16[24,4096]{1,0:T(8,128)(2,1)S(1)} %get-tuple-element.69), channel_id=1, source_target_pairs={{0,4},{1,5},{2,6},{3,7},{4,0},{5,1},{6,2},{7,3},{8,12},{9,13},{10,... | collective-permute-start | bytes 589832 | tf_op jit(solution)/shard_map/ppermute | solution.py:174
  41.3 8.9 %collective-permute-start.14 = (bf16[40,2048]{1,0:T(8,128)(2,1)S(1)}, bf16[40,2048]{1,0:T(8,128)(2,1)S(1)}, u32[]{:S(2)}, u32[]{:S(2)}) collective-permute-start(bf16[40,2048]{1,0:T(8,128)(2,1)S(1)} %pad_maximum_fusion.19), channel_id=1, source_target_pairs={{0,6},{1,7},{2,4},{3,5},{4,2},{5,3},{6,0},{7,1},{8,14},{9,15},{10,... | collective-permute-start | bytes 491528 | tf_op jit(solution)/shard_map/ppermute | solution.py:174
  42.9 7.4 %collective-permute-start.13 = (bf16[40,2048]{1,0:T(8,128)(2,1)S(1)}, bf16[40,2048]{1,0:T(8,128)(2,1)S(1)}, u32[]{:S(2)}, u32[]{:S(2)}) collective-permute-start(bf16[40,2048]{1,0:T(8,128)(2,1)S(1)} %get-tuple-element.74), channel_id=1, source_target_pairs={{0,2},{1,3},{2,0},{3,1},{4,6},{5,7},{6,4},{7,5},{8,10},{9,11},{10,... | collective-permute-start | bytes 491528 | tf_op jit(solution)/shard_map/ppermute | solution.py:174
  44.4 6.2 %collective-permute-start.16 = (bf16[40,2048]{1,0:T(8,128)(2,1)S(1)}, bf16[40,2048]{1,0:T(8,128)(2,1)S(1)}, u32[]{:S(2)}, u32[]{:S(2)}) collective-permute-start(bf16[40,2048]{1,0:T(8,128)(2,1)S(1)} %get-tuple-element.75), channel_id=1, source_target_pairs={{0,4},{1,5},{2,6},{3,7},{4,0},{5,1},{6,2},{7,3},{8,12},{9,13},{10,... | collective-permute-start | bytes 491528 | tf_op jit(solution)/shard_map/ppermute | solution.py:174
  45.0 6.3 %collective-permute-start.18 = (bf16[40,2048]{1,0:T(8,128)(2,1)S(1)}, bf16[40,2048]{1,0:T(8,128)(2,1)S(1)}, u32[]{:S(2)}, u32[]{:S(2)}) collective-permute-start(bf16[40,2048]{1,0:T(8,128)(2,1)S(1)} %pad_maximum_fusion.22), channel_id=1, source_target_pairs={{0,8},{1,9},{2,10},{3,11},{4,12},{5,13},{6,14},{7,15},{8,0},{9,1},... | collective-permute-start | bytes 491528 | tf_op jit(solution)/shard_map/ppermute | solution.py:174
  50.3 6.5 %collective-permute-start.15 = (bf16[40,2048]{1,0:T(8,128)(2,1)S(1)}, bf16[40,2048]{1,0:T(8,128)(2,1)S(1)}, u32[]{:S(2)}, u32[]{:S(2)}) collective-permute-start(bf16[40,2048]{1,0:T(8,128)(2,1)S(1)} %add_convert_fusion.3), channel_id=1, source_target_pairs={{0,8},{1,9},{2,10},{3,11},{4,12},{5,13},{6,14},{7,15},{8,0},{9,1},... | collective-permute-start | bytes 491528 | tf_op jit(solution)/shard_map/ppermute | solution.py:174
  50.7 6.1 %collective-permute-start.17 = (bf16[40,2048]{1,0:T(8,128)(2,1)S(1)}, bf16[40,2048]{1,0:T(8,128)(2,1)S(1)}, u32[]{:S(2)}, u32[]{:S(2)}) collective-permute-start(bf16[40,2048]{1,0:T(8,128)(2,1)S(1)} %add_convert_fusion.2), channel_id=1, source_target_pairs={{0,2},{1,3},{2,0},{3,1},{4,6},{5,7},{6,4},{7,5},{8,10},{9,11},{10,... | collective-permute-start | bytes 491528 | tf_op jit(solution)/shard_map/ppermute | solution.py:174
  51.4 5.4 %collective-permute-start.19 = (bf16[40,2048]{1,0:T(8,128)(2,1)S(1)}, bf16[40,2048]{1,0:T(8,128)(2,1)S(1)}, u32[]{:S(2)}, u32[]{:S(2)}) collective-permute-start(bf16[40,2048]{1,0:T(8,128)(2,1)S(1)} %add_convert_fusion.1), channel_id=1, source_target_pairs={{0,4},{1,5},{2,6},{3,7},{4,0},{5,1},{6,2},{7,3},{8,12},{9,13},{10,... | collective-permute-start | bytes 491528 | tf_op jit(solution)/shard_map/ppermute | solution.py:174
  54.5 7.4 %collective-permute-start.21 = (bf16[320,2048]{1,0:T(8,128)(2,1)S(1)}, bf16[320,2048]{1,0:T(8,128)(2,1)S(1)}, u32[]{:S(2)}, u32[]{:S(2)}) collective-permute-start(bf16[320,2048]{1,0:T(8,128)(2,1)S(1)} %fusion.7), channel_id=1, source_target_pairs={{0,1},{1,0},{2,3},{3,2},{4,5},{5,4},{6,7},{7,6},{8,9},{9,8},{10,11... | collective-permute-start | bytes 3932168 | tf_op jit(solution)/shard_map/ppermute | solution.py:174
  55.8 6.1 %collective-permute-start.20 = (bf16[320,2048]{1,0:T(8,128)(2,1)S(1)}, bf16[320,2048]{1,0:T(8,128)(2,1)S(1)}, u32[]{:S(2)}, u32[]{:S(2)}) collective-permute-start(bf16[320,2048]{1,0:T(8,128)(2,1)S(1)} %fusion.6), channel_id=1, source_target_pairs={{0,1},{1,0},{2,3},{3,2},{4,5},{5,4},{6,7},{7,6},{8,9},{9,8},{10,11... | collective-permute-start | bytes 3932168 | tf_op jit(solution)/shard_map/ppermute | solution.py:174
  56.9 8.1 %collective-permute-start.22 = (bf16[40,1024]{1,0:T(8,128)(2,1)S(1)}, bf16[40,1024]{1,0:T(8,128)(2,1)S(1)}, u32[]{:S(2)}, u32[]{:S(2)}) collective-permute-start(bf16[40,1024]{1,0:T(8,128)(2,1)S(1)} %pad_maximum_fusion.23), channel_id=1, source_target_pairs={{0,16},{1,17},{2,18},{3,19},{4,20},{5,21},{6,22},{7,23},{8,24},{9,... | collective-permute-start | bytes 245768 | tf_op jit(solution)/shard_map/ppermute | solution.py:217
  (5 other events, 5.0 us)

commit v16 on v15

--- a/solution.py
+++ b/solution.py
@@ -51,7 +51,18 @@
     return jnp.dot(pick, source, preferred_element_type=jnp.float32)
 
 
-def pack_kernel(blocks, experts, ids_ref, gate_ref, tokens_ref, grads_ref, *outs):
+def pack_kernel(blocks, experts, *refs):
+    sources, (*outs, ids_ref, gate_ref, tokens_ref, grads_ref, sems) = refs[:4], refs[4:]
+    fetches = [
+        pltpu.make_async_copy(source, target, sems.at[k])
+        for k, (source, target) in enumerate(
+            zip(sources, (ids_ref, gate_ref, tokens_ref, grads_ref))
+        )
+    ]
+    for fetch in fetches:
+        fetch.start()
+    for fetch in fetches:
+        fetch.wait()
     n, width = tokens_ref.shape
     mine = (lax.axis_index("expert") // SHARDS).astype(jnp.float32)
     ids = ids_ref[...].astype(jnp.float32)
@@ -111,8 +122,15 @@
     outs = pl.pallas_call(
         lambda *refs: pack_kernel(blocks, experts, *refs),
         out_shape=shapes,
-        in_specs=[whole] * 4,
+        in_specs=[pl.BlockSpec(memory_space=pltpu.HBM)] * 4,
         out_specs=[whole] * len(shapes),
+        scratch_shapes=[
+            pltpu.VMEM((1, n), jnp.int32),
+            pltpu.VMEM((1, n), jnp.float32),
+            pltpu.VMEM((n, width), jnp.bfloat16),
+            pltpu.VMEM((n, width), jnp.bfloat16),
+            pltpu.SemaphoreType.DMA((4,)),
+        ],
         compiler_params=pltpu.CompilerParams(vmem_limit_bytes=8 * 1024 * 1024),
     )(ids.reshape(1, n), gate.reshape(1, n), tokens, grads)
     return outs[: len(blocks)], outs[len(blocks) : 2 * len(blocks)], outs[2 * len(blocks) :]
@@ -136,13 +154,21 @@
     return lax.all_gather(shard.astype(jnp.bfloat16), "dp", axis=0, tiled=True)
 
 
-def step_kernel(*refs):
+def step_kernel(rows, *refs):
+    *refs, done_ref, sems = refs
     count = len(refs) // 3
     bases, shares, outs = refs[:count], refs[count : 2 * count], refs[2 * count :]
-    rows = outs[0].shape[0]
-    part = pl.ds(pl.multiple_of(pl.program_id(0) * rows, rows), rows)
-    for base_ref, share_ref, out_ref in zip(bases, shares, outs):
-        out_ref[...] = base_ref[part, :] - step_rate * share_ref[part, :].astype(jnp.float32)
+    writes = []
+    for start in range(0, outs[0].shape[0], rows):
+        part = slice(start, start + rows)
+        for k in range(count):
+            done_ref[k, part] = bases[k][part] - step_rate * shares[k][part].astype(jnp.float32)
+            writes.append(
+                pltpu.make_async_copy(done_ref.at[k, part], outs[k].at[part], sems.at[len(writes)])
+            )
+            writes[-1].start()
+    for write in writes:
+        write.wait()
 
 
 def stepped(bases, shares):
@@ -150,12 +176,15 @@
     rows = 64 if units % 64 == 0 else units
     whole = pl.BlockSpec(memory_space=pltpu.VMEM)
     return pl.pallas_call(
-        step_kernel,
-        grid=(units // rows,),
+        lambda *refs: step_kernel(rows, *refs),
         out_shape=[jax.ShapeDtypeStruct(base.shape, base.dtype) for base in bases],
         in_specs=[whole] * (2 * len(bases)),
-        out_specs=[pl.BlockSpec((rows, width), lambda i: (i, 0))] * len(bases),
-        compiler_params=pltpu.CompilerParams(vmem_limit_bytes=14 * 1024 * 1024),
+        out_specs=[pl.BlockSpec(memory_space=pltpu.HBM)] * len(bases),
+        scratch_shapes=[
+            pltpu.VMEM((len(bases), units, width), jnp.float32),
+            pltpu.SemaphoreType.DMA((len(bases) * (units // rows),)),
+        ],
+        compiler_params=pltpu.CompilerParams(vmem_limit_bytes=16 * 1024 * 1024),
         cost_estimate=pl.CostEstimate(
             flops=4 * units * width, bytes_accessed=8 * units * width, transcendentals=0
         ),

time: 66.3 us -> 66.1 us (level)
  transfers between devices with their start and end apart: 23 -> 23, of which waited for: 8 -> 9; matrix products, arithmetic and copies ran while one was open for 17% -> 17% of each run, Pallas kernels for 5% -> 4%
where the time goes in v16:
time: 66.1 us; the launch traced here: 65.8 us
  starting transfers between devices  31.8 us (48%)
  matrix products  11.8 us (18%)
  waiting for transfers between devices  10.3 us (16%)
  local copies, waits for them, and re-layouts  5.08 us (8%)
  Pallas kernels  2.96 us (4%)
  other arithmetic  2.85 us (4%)
  between operations  1.06 us (2%)
    ppermute x21, starting transfers between devices, swap(): lax.ppermute(rows, 'expert', [(i, i ^ mask) for i in range(n_expert)])  23.2 us
    ppermute x21, waiting for transfers between devices, swap(): lax.ppermute(rows, 'expert', [(i, i ^ mask) for i in range(n_expert)])  9.67 us
    ppermute x2, starting transfers between devices, shifted(): return lax.ppermute(rows, 'expert', pairs)  8.61 us
    dot_general x11, matrix products, contract_rows(): lax.dot_general(left, right, (((0,), (0,)), ((), ())), preferred_element_...  6.06 us
    unnamed x22, local copies, waits for them, and re-layouts  4.51 us
    dot_general x4, matrix products, contract_cols(): lax.dot_general(left, right, (((1,), (1,)), ((), ())), preferred_element_...  4.38 us
    pallas_call x1, Pallas kernels, stepped(): pl.pallas_call(lambda *refs: step_kernel(rows, *refs), out_shape=[jax.Sha...  2.47 us
    transpose x1, other arithmetic, shards(): whole_weights(w_in)  1.93 us
  transfers between devices with their start and end apart: 23, of which 9 were waited for; matrix products, arithmetic and copies ran while one was open for 17% of the time, Pallas kernels for 4%

profile of v16, /device:TPU:0, one launch (start us, length us, event | category | flops | bytes accessed | tf_op | source)
XLA Modules:
  0.0 65.8 jit_solution(10962854127427533498)
XLA Ops:
  4.3 4.1 %collective-permute-start = (bf16[40,2048]{1,0:T(8,128)(2,1)S(1)}, bf16[40,2048]{1,0:T(8,128)(2,1)S(1)}, u32[]{:S(2)}, u32[]{:S(2)}) collective-permute-start(bf16[40,2048]{1,0:T(8,128)(2,1)S(1)} %get-tuple-element.51.refs_4_), channel_id=1, source_target_pairs={{0,16},{1,17},{2,18},{3,19},{4,20},{5,21},{6,22},{7,23},{8,24},{9,... | collective-permute-start | bytes 491528 | tf_op jit(solution)/shard_map/ppermute | solution.py:246
  8.4 2.5 %collective-permute-start.1 = (bf16[16,4096]{1,0:T(8,128)(2,1)S(1)}, bf16[16,4096]{1,0:T(8,128)(2,1)S(1)}, u32[]{:S(2)}, u32[]{:S(2)}) collective-permute-start(bf16[16,4096]{1,0:T(8,128)(2,1)S(1)} %get-tuple-element.56), channel_id=1, source_target_pairs={{0,6},{1,7},{2,4},{3,5},{4,2},{5,3},{6,0},{7,1},{8,14},{9,15},{10,... | collective-permute-start | bytes 393224 | tf_op jit(solution)/shard_map/ppermute | solution.py:203
  10.9 1.6 %collective-permute-start.2 = (bf16[16,4096]{1,0:T(8,128)(2,1)S(1)}, bf16[16,4096]{1,0:T(8,128)(2,1)S(1)}, u32[]{:S(2)}, u32[]{:S(2)}) collective-permute-start(bf16[16,4096]{1,0:T(8,128)(2,1)S(1)} %get-tuple-element.57), channel_id=1, source_target_pairs={{0,8},{1,9},{2,10},{3,11},{4,12},{5,13},{6,14},{7,15},{8,0},{9,1},... | collective-permute-start | bytes 393224 | tf_op jit(solution)/shard_map/ppermute | solution.py:203
  13.5 1.9 %convert_bitcast_fusion = bf16[320,2048]{1,0:T(8,128)(2,1)S(1)} fusion(f32[2048,320]{0,1:T(8,128)} %param.10), kind=kLoop, calls=%fused_computation.24 | loop fusion | flops 655360 | bytes 3932160 | tf_op jit(solution)/shard_map/transpose | solution.py:289
  16.4 1.5 %collective-permute-done.2 = bf16[16,4096]{1,0:T(8,128)(2,1)S(1)} collective-permute-done((bf16[16,4096]{1,0:T(8,128)(2,1)S(1)}, bf16[16,4096]{1,0:T(8,128)(2,1)S(1)}, u32[]{:S(2)}, u32[]{:S(2)}) %collective-permute-start.2) | collective-permute-done | bytes 131104 | tf_op jit(solution)/shard_map/ppermute | solution.py:203
  18.0 1.6 %collective-permute-start.6 = (bf16[40,4096]{1,0:T(8,128)(2,1)S(1)}, bf16[40,4096]{1,0:T(8,128)(2,1)S(1)}, u32[]{:S(2)}, u32[]{:S(2)}) collective-permute-start(bf16[40,4096]{1,0:T(8,128)(2,1)S(1)} %get-tuple-element.64), channel_id=1, source_target_pairs={{0,2},{1,3},{2,0},{3,1},{4,6},{5,7},{6,4},{7,5},{8,10},{9,11},{10,... | collective-permute-start | bytes 983048 | tf_op jit(solution)/shard_map/ppermute | solution.py:203
  20.4 1.4 %collective-permute-start.7 = (bf16[40,4096]{1,0:T(8,128)(2,1)S(1)}, bf16[40,4096]{1,0:T(8,128)(2,1)S(1)}, u32[]{:S(2)}, u32[]{:S(2)}) collective-permute-start(bf16[40,4096]{1,0:T(8,128)(2,1)S(1)} %get-tuple-element.65), channel_id=1, source_target_pairs={{0,8},{1,9},{2,10},{3,11},{4,12},{5,13},{6,14},{7,15},{8,0},{9,1},... | collective-permute-start | bytes 983048 | tf_op jit(solution)/shard_map/ppermute | solution.py:203
  22.0 4.9 %collective-permute-done.6 = bf16[40,4096]{1,0:T(8,128)(2,1)S(1)} collective-permute-done((bf16[40,4096]{1,0:T(8,128)(2,1)S(1)}, bf16[40,4096]{1,0:T(8,128)(2,1)S(1)}, u32[]{:S(2)}, u32[]{:S(2)}) %collective-permute-start.6) | collective-permute-done | bytes 327712 | tf_op jit(solution)/shard_map/ppermute | solution.py:203
  28.4 1.5 %collective-permute-start.12 = (bf16[24,4096]{1,0:T(8,128)(2,1)S(1)}, bf16[24,4096]{1,0:T(8,128)(2,1)S(1)}, u32[]{:S(2)}, u32[]{:S(2)}) collective-permute-start(bf16[24,4096]{1,0:T(8,128)(2,1)S(1)} %get-tuple-element.67), channel_id=1, source_target_pairs={{0,6},{1,7},{2,4},{3,5},{4,2},{5,3},{6,0},{7,1},{8,14},{9,15},{10,... | collective-permute-start | bytes 589832 | tf_op jit(solution)/shard_map/ppermute | solution.py:203
  30.7 1.3 %collective-permute-start.10 = (bf16[24,4096]{1,0:T(8,128)(2,1)S(1)}, bf16[24,4096]{1,0:T(8,128)(2,1)S(1)}, u32[]{:S(2)}, u32[]{:S(2)}) collective-permute-start(bf16[24,4096]{1,0:T(8,128)(2,1)S(1)} %get-tuple-element.68), channel_id=1, source_target_pairs={{0,8},{1,9},{2,10},{3,11},{4,12},{5,13},{6,14},{7,15},{8,0},{9,1},... | collective-permute-start | bytes 589832 | tf_op jit(solution)/shard_map/ppermute | solution.py:203
  32.0 1.7 %collective-permute-start.9 = (bf16[24,4096]{1,0:T(8,128)(2,1)S(1)}, bf16[24,4096]{1,0:T(8,128)(2,1)S(1)}, u32[]{:S(2)}, u32[]{:S(2)}) collective-permute-start(bf16[24,4096]{1,0:T(8,128)(2,1)S(1)} %get-tuple-element.69), channel_id=1, source_target_pairs={{0,4},{1,5},{2,6},{3,7},{4,0},{5,1},{6,2},{7,3},{8,12},{9,13},{10,... | collective-permute-start | bytes 589832 | tf_op jit(solution)/shard_map/ppermute | solution.py:203
  34.1 1.0 %multiply_convert_fusion.1 = (bf16[128,640]{1,0:T(8,128)(2,1)S(1)}, f32[128,640]{1,0:T(8,128)S(1)}) fusion(bf16[320,2048]{1,0:T(8,128)(2,1)S(1)} %convert_bitcast_fusion, bf16[320,2048]{1,0:T(8,128)(2,1)S(1)} %get-tuple-element.95, bf16[128,4096]{1,0:T(8,128)(2,1)S(1)} %slice_dynamic-update-slice_fusion), kind=kOutput, calls=%fused_computation.67 | convolution fusion | flops 341606400 | bytes 3637248 | tf_op jit(solution)/shard_map/dot_general | solution.py:39
  35.1 1.1 %fusion.18 = bf16[128,640]{1,0:T(8,128)(2,1)S(1)} fusion(bf16[320,2048]{1,0:T(8,128)(2,1)S(1)} %get-tuple-element.96, bf16[320,2048]{1,0:T(8,128)(2,1)S(1)} %convert_bitcast_fusion.1, bf16[128,4096]{1,0:T(8,128)(2,1)S(1)} %slice_dynamic-update-slice_fusion, f32[128,640]{1,0:T(8,128)S(1)} %get-tuple-element.130), kind=kOutput, calls=%fused_computation.31 | convolution fusion | flops 342507520 | bytes 3637248 | tf_op jit(solution)/shard_map/dot_general | solution.py:39
  36.8 1.3 %collective-permute-done.9 = bf16[24,4096]{1,0:T(8,128)(2,1)S(1)} collective-permute-done((bf16[24,4096]{1,0:T(8,128)(2,1)S(1)}, bf16[24,4096]{1,0:T(8,128)(2,1)S(1)}, u32[]{:S(2)}, u32[]{:S(2)}) %collective-permute-start.9) | collective-permute-done | bytes 196640 | tf_op jit(solution)/shard_map/ppermute | solution.py:203
  38.2 1.1 %multiply_convert_fusion = (bf16[192,640]{1,0:T(8,128)(2,1)S(1)}, f32[192,640]{1,0:T(8,128)S(1)}) fusion(bf16[320,2048]{1,0:T(8,128)(2,1)S(1)} %convert_bitcast_fusion, bf16[320,2048]{1,0:T(8,128)(2,1)S(1)} %get-tuple-element.95, bf16[192,4096]{1,0:T(8,128)(2,1)S(1)} %constant_dynamic-update-slice_fusion.5), kind=kOutput, calls=%fused_computation.46 | convolution fusion | flops 509788160 | bytes 4145152 | tf_op jit(solution)/shard_map/dot_general | solution.py:39
  39.3 1.2 %fusion.15 = bf16[192,640]{1,0:T(8,128)(2,1)S(1)} fusion(bf16[320,2048]{1,0:T(8,128)(2,1)S(1)} %get-tuple-element.96, bf16[320,2048]{1,0:T(8,128)(2,1)S(1)} %convert_bitcast_fusion.1, bf16[192,4096]{1,0:T(8,128)(2,1)S(1)} %constant_dynamic-update-slice_fusion.5, f32[192,640]{1,0:T(8,128)S(1)} %get-tuple-element.128), kind=kOutput, calls=%fused_computation.28 | convolution fusion | flops 511139840 | bytes 4145152 | tf_op jit(solution)/shard_map/dot_general | solution.py:39
  41.4 1.5 %collective-permute-start.14 = (bf16[40,2048]{1,0:T(8,128)(2,1)S(1)}, bf16[40,2048]{1,0:T(8,128)(2,1)S(1)}, u32[]{:S(2)}, u32[]{:S(2)}) collective-permute-start(bf16[40,2048]{1,0:T(8,128)(2,1)S(1)} %pad_maximum_fusion.19), channel_id=1, source_target_pairs={{0,6},{1,7},{2,4},{3,5},{4,2},{5,3},{6,0},{7,1},{8,14},{9,15},{10,... | collective-permute-start | bytes 491528 | tf_op jit(solution)/shard_map/ppermute | solution.py:203
  42.9 1.5 %collective-permute-start.13 = (bf16[40,2048]{1,0:T(8,128)(2,1)S(1)}, bf16[40,2048]{1,0:T(8,128)(2,1)S(1)}, u32[]{:S(2)}, u32[]{:S(2)}) collective-permute-start(bf16[40,2048]{1,0:T(8,128)(2,1)S(1)} %get-tuple-element.74), channel_id=1, source_target_pairs={{0,2},{1,3},{2,0},{3,1},{4,6},{5,7},{6,4},{7,5},{8,10},{9,11},{10,... | collective-permute-start | bytes 491528 | tf_op jit(solution)/shard_map/ppermute | solution.py:203
  45.1 1.8 %collective-permute-start.18 = (bf16[40,2048]{1,0:T(8,128)(2,1)S(1)}, bf16[40,2048]{1,0:T(8,128)(2,1)S(1)}, u32[]{:S(2)}, u32[]{:S(2)}) collective-permute-start(bf16[40,2048]{1,0:T(8,128)(2,1)S(1)} %pad_maximum_fusion.22), channel_id=1, source_target_pairs={{0,8},{1,9},{2,10},{3,11},{4,12},{5,13},{6,14},{7,15},{8,0},{9,1},... | collective-permute-start | bytes 491528 | tf_op jit(solution)/shard_map/ppermute | solution.py:203
  48.5 1.2 %copy-done.5 = f32[2048,320]{0,1:T(8,128)S(1)} copy-done((f32[2048,320]{0,1:T(8,128)S(1)}, f32[2048,320]{0,1:T(8,128)}, u32[]{:S(2)}) %copy-start.5) | copy-done | bytes 2621464
  51.5 1.9 %collective-permute-start.19 = (bf16[40,2048]{1,0:T(8,128)(2,1)S(1)}, bf16[40,2048]{1,0:T(8,128)(2,1)S(1)}, u32[]{:S(2)}, u32[]{:S(2)}) collective-permute-start(bf16[40,2048]{1,0:T(8,128)(2,1)S(1)} %add_convert_fusion.1), channel_id=1, source_target_pairs={{0,4},{1,5},{2,6},{3,7},{4,0},{5,1},{6,2},{7,3},{8,12},{9,13},{10,... | collective-permute-start | bytes 491528 | tf_op jit(solution)/shard_map/ppermute | solution.py:203
  57.0 4.5 %collective-permute-start.22 = (bf16[40,1024]{1,0:T(8,128)(2,1)S(1)}, bf16[40,1024]{1,0:T(8,128)(2,1)S(1)}, u32[]{:S(2)}, u32[]{:S(2)}) collective-permute-start(bf16[40,1024]{1,0:T(8,128)(2,1)S(1)} %pad_maximum_fusion.23), channel_id=1, source_target_pairs={{0,16},{1,17},{2,18},{3,19},{4,20},{5,21},{6,22},{7,23},{8,24},{9,... | collective-permute-start | bytes 245768 | tf_op jit(solution)/shard_map/ppermute | solution.py:246
  62.0 2.5 %shard_map.87 = (f32[320,2048]{1,0:T(8,128)}, f32[320,2048]{1,0:T(8,128)}) custom-call(f32[320,2048]{1,0:T(8,128)S(1)} %fusion.5.refs_0_, f32[320,2048]{1,0:T(8,128)S(1)} %fusion.3.refs_1_, bf16[320,2048]{1,0:T(8,128)(2,1)S(1)} %collective-permute-done.20.refs_2_, bf16[320,2048]{1,0:T(8,128)(2,1)S(1)} %collective-permute-done.21.refs_3_), custom_call_target="tpu_custom_call" | custom-call | flops 2621440 | bytes 5242880 | tf_op jit(solution)/shard_map/pallas_call | solution.py:178
  64.9 1.0 %fusion.10 = bf16[64,2048]{1,0:T(8,128)(2,1)} fusion(f32[64,2048]{1,0:T(8,128)S(1)} %convolution_add_fusion.5, bf16[20,1024]{1,0:T(8,128)(2,1)S(1)} %get-tuple-element.126, bf16[20,1024]{1,0:T(8,128)(2,1)S(1)} %get-tuple-element.125, bf16[40,64]{1,0:T(8,128)(2,1)S(1)} %get-tuple-element.85), kind=kOutput, calls=%fused_computation.21 | convolution fusion | flops 5668864 | bytes 890880 | tf_op jit(solution)/shard_map/dot_general | solution.py:33
  (88 shorter events, 19.3 us)
Async XLA Ops:
  3.8 11.6 %copy-start.4 = (f32[2048,320]{0,1:T(8,128)S(1)}, f32[2048,320]{0,1:T(8,128)}, u32[]{:S(2)}) copy-start(f32[2048,320]{0,1:T(8,128)} %param.11) | copy-start | bytes 7864324
  4.3 11.9 %collective-permute-start = (bf16[40,2048]{1,0:T(8,128)(2,1)S(1)}, bf16[40,2048]{1,0:T(8,128)(2,1)S(1)}, u32[]{:S(2)}, u32[]{:S(2)}) collective-permute-start(bf16[40,2048]{1,0:T(8,128)(2,1)S(1)} %get-tuple-element.51.refs_4_), channel_id=1, source_target_pairs={{0,16},{1,17},{2,18},{3,19},{4,20},{5,21},{6,22},{7,23},{8,24},{9,... | collective-permute-start | bytes 491528 | tf_op jit(solution)/shard_map/ppermute | solution.py:246
  8.4 7.9 %collective-permute-start.1 = (bf16[16,4096]{1,0:T(8,128)(2,1)S(1)}, bf16[16,4096]{1,0:T(8,128)(2,1)S(1)}, u32[]{:S(2)}, u32[]{:S(2)}) collective-permute-start(bf16[16,4096]{1,0:T(8,128)(2,1)S(1)} %get-tuple-element.56), channel_id=1, source_target_pairs={{0,6},{1,7},{2,4},{3,5},{4,2},{5,3},{6,0},{7,1},{8,14},{9,15},{10,... | collective-permute-start | bytes 393224 | tf_op jit(solution)/shard_map/ppermute | solution.py:203
  10.9 7.0 %collective-permute-start.2 = (bf16[16,4096]{1,0:T(8,128)(2,1)S(1)}, bf16[16,4096]{1,0:T(8,128)(2,1)S(1)}, u32[]{:S(2)}, u32[]{:S(2)}) collective-permute-start(bf16[16,4096]{1,0:T(8,128)(2,1)S(1)} %get-tuple-element.57), channel_id=1, source_target_pairs={{0,8},{1,9},{2,10},{3,11},{4,12},{5,13},{6,14},{7,15},{8,0},{9,1},... | collective-permute-start | bytes 393224 | tf_op jit(solution)/shard_map/ppermute | solution.py:203
  12.5 5.4 %collective-permute-start.3 = (bf16[16,4096]{1,0:T(8,128)(2,1)S(1)}, bf16[16,4096]{1,0:T(8,128)(2,1)S(1)}, u32[]{:S(2)}, u32[]{:S(2)}) collective-permute-start(bf16[16,4096]{1,0:T(8,128)(2,1)S(1)} %get-tuple-element.58), channel_id=1, source_target_pairs={{0,2},{1,3},{2,0},{3,1},{4,6},{5,7},{6,4},{7,5},{8,10},{9,11},{10,... | collective-permute-start | bytes 393224 | tf_op jit(solution)/shard_map/ppermute | solution.py:203
  13.0 5.0 %collective-permute-start.4 = (bf16[16,4096]{1,0:T(8,128)(2,1)S(1)}, bf16[16,4096]{1,0:T(8,128)(2,1)S(1)}, u32[]{:S(2)}, u32[]{:S(2)}) collective-permute-start(bf16[16,4096]{1,0:T(8,128)(2,1)S(1)} %get-tuple-element.59), channel_id=1, source_target_pairs={{0,4},{1,5},{2,6},{3,7},{4,0},{5,1},{6,2},{7,3},{8,12},{9,13},{10,... | collective-permute-start | bytes 393224 | tf_op jit(solution)/shard_map/ppermute | solution.py:203
  18.0 8.8 %collective-permute-start.6 = (bf16[40,4096]{1,0:T(8,128)(2,1)S(1)}, bf16[40,4096]{1,0:T(8,128)(2,1)S(1)}, u32[]{:S(2)}, u32[]{:S(2)}) collective-permute-start(bf16[40,4096]{1,0:T(8,128)(2,1)S(1)} %get-tuple-element.64), channel_id=1, source_target_pairs={{0,2},{1,3},{2,0},{3,1},{4,6},{5,7},{6,4},{7,5},{8,10},{9,11},{10,... | collective-permute-start | bytes 983048 | tf_op jit(solution)/shard_map/ppermute | solution.py:203
  19.6 7.8 %collective-permute-start.5 = (bf16[40,4096]{1,0:T(8,128)(2,1)S(1)}, bf16[40,4096]{1,0:T(8,128)(2,1)S(1)}, u32[]{:S(2)}, u32[]{:S(2)}) collective-permute-start(bf16[40,4096]{1,0:T(8,128)(2,1)S(1)} %get-tuple-element.64), channel_id=1, source_target_pairs={{0,4},{1,5},{2,6},{3,7},{4,0},{5,1},{6,2},{7,3},{8,12},{9,13},{10,... | collective-permute-start | bytes 983048 | tf_op jit(solution)/shard_map/ppermute | solution.py:203
  20.4 8.0 %collective-permute-start.7 = (bf16[40,4096]{1,0:T(8,128)(2,1)S(1)}, bf16[40,4096]{1,0:T(8,128)(2,1)S(1)}, u32[]{:S(2)}, u32[]{:S(2)}) collective-permute-start(bf16[40,4096]{1,0:T(8,128)(2,1)S(1)} %get-tuple-element.65), channel_id=1, source_target_pairs={{0,8},{1,9},{2,10},{3,11},{4,12},{5,13},{6,14},{7,15},{8,0},{9,1},... | collective-permute-start | bytes 983048 | tf_op jit(solution)/shard_map/ppermute | solution.py:203
  21.9 11.9 %collective-permute-start.8 = (bf16[640,2048]{1,0:T(8,128)(2,1)S(1)}, bf16[640,2048]{1,0:T(8,128)(2,1)S(1)}, u32[]{:S(2)}, u32[]{:S(2)}) collective-permute-start(bf16[640,2048]{1,0:T(8,128)(2,1)S(1)} %pad_maximum_fusion.1), channel_id=1, source_target_pairs={{0,1},{1,0},{2,3},{3,2},{4,5},{5,4},{6,7},{7,6},{8,9},{9,8},{10,11... | collective-permute-start | bytes 7864328 | tf_op jit(solution)/shard_map/ppermute | solution.py:203
  28.4 9.7 %collective-permute-start.12 = (bf16[24,4096]{1,0:T(8,128)(2,1)S(1)}, bf16[24,4096]{1,0:T(8,128)(2,1)S(1)}, u32[]{:S(2)}, u32[]{:S(2)}) collective-permute-start(bf16[24,4096]{1,0:T(8,128)(2,1)S(1)} %get-tuple-element.67), channel_id=1, source_target_pairs={{0,6},{1,7},{2,4},{3,5},{4,2},{5,3},{6,0},{7,1},{8,14},{9,15},{10,... | collective-permute-start | bytes 589832 | tf_op jit(solution)/shard_map/ppermute | solution.py:203
  29.9 8.2 %collective-permute-start.11 = (bf16[24,4096]{1,0:T(8,128)(2,1)S(1)}, bf16[24,4096]{1,0:T(8,128)(2,1)S(1)}, u32[]{:S(2)}, u32[]{:S(2)}) collective-permute-start(bf16[24,4096]{1,0:T(8,128)(2,1)S(1)} %get-tuple-element.67), channel_id=1, source_target_pairs={{0,2},{1,3},{2,0},{3,1},{4,6},{5,7},{6,4},{7,5},{8,10},{9,11},{10,... | collective-permute-start | bytes 589832 | tf_op jit(solution)/shard_map/ppermute | solution.py:203
  30.7 7.4 %collective-permute-start.10 = (bf16[24,4096]{1,0:T(8,128)(2,1)S(1)}, bf16[24,4096]{1,0:T(8,128)(2,1)S(1)}, u32[]{:S(2)}, u32[]{:S(2)}) collective-permute-start(bf16[24,4096]{1,0:T(8,128)(2,1)S(1)} %get-tuple-element.68), channel_id=1, source_target_pairs={{0,8},{1,9},{2,10},{3,11},{4,12},{5,13},{6,14},{7,15},{8,0},{9,1},... | collective-permute-start | bytes 589832 | tf_op jit(solution)/shard_map/ppermute | solution.py:203
  32.0 6.1 %collective-permute-start.9 = (bf16[24,4096]{1,0:T(8,128)(2,1)S(1)}, bf16[24,4096]{1,0:T(8,128)(2,1)S(1)}, u32[]{:S(2)}, u32[]{:S(2)}) collective-permute-start(bf16[24,4096]{1,0:T(8,128)(2,1)S(1)} %get-tuple-element.69), channel_id=1, source_target_pairs={{0,4},{1,5},{2,6},{3,7},{4,0},{5,1},{6,2},{7,3},{8,12},{9,13},{10,... | collective-permute-start | bytes 589832 | tf_op jit(solution)/shard_map/ppermute | solution.py:203
  41.4 8.9 %collective-permute-start.14 = (bf16[40,2048]{1,0:T(8,128)(2,1)S(1)}, bf16[40,2048]{1,0:T(8,128)(2,1)S(1)}, u32[]{:S(2)}, u32[]{:S(2)}) collective-permute-start(bf16[40,2048]{1,0:T(8,128)(2,1)S(1)} %pad_maximum_fusion.19), channel_id=1, source_target_pairs={{0,6},{1,7},{2,4},{3,5},{4,2},{5,3},{6,0},{7,1},{8,14},{9,15},{10,... | collective-permute-start | bytes 491528 | tf_op jit(solution)/shard_map/ppermute | solution.py:203
  42.9 7.4 %collective-permute-start.13 = (bf16[40,2048]{1,0:T(8,128)(2,1)S(1)}, bf16[40,2048]{1,0:T(8,128)(2,1)S(1)}, u32[]{:S(2)}, u32[]{:S(2)}) collective-permute-start(bf16[40,2048]{1,0:T(8,128)(2,1)S(1)} %get-tuple-element.74), channel_id=1, source_target_pairs={{0,2},{1,3},{2,0},{3,1},{4,6},{5,7},{6,4},{7,5},{8,10},{9,11},{10,... | collective-permute-start | bytes 491528 | tf_op jit(solution)/shard_map/ppermute | solution.py:203
  44.5 6.2 %collective-permute-start.16 = (bf16[40,2048]{1,0:T(8,128)(2,1)S(1)}, bf16[40,2048]{1,0:T(8,128)(2,1)S(1)}, u32[]{:S(2)}, u32[]{:S(2)}) collective-permute-start(bf16[40,2048]{1,0:T(8,128)(2,1)S(1)} %get-tuple-element.75), channel_id=1, source_target_pairs={{0,4},{1,5},{2,6},{3,7},{4,0},{5,1},{6,2},{7,3},{8,12},{9,13},{10,... | collective-permute-start | bytes 491528 | tf_op jit(solution)/shard_map/ppermute | solution.py:203
  45.1 6.3 %collective-permute-start.18 = (bf16[40,2048]{1,0:T(8,128)(2,1)S(1)}, bf16[40,2048]{1,0:T(8,128)(2,1)S(1)}, u32[]{:S(2)}, u32[]{:S(2)}) collective-permute-start(bf16[40,2048]{1,0:T(8,128)(2,1)S(1)} %pad_maximum_fusion.22), channel_id=1, source_target_pairs={{0,8},{1,9},{2,10},{3,11},{4,12},{5,13},{6,14},{7,15},{8,0},{9,1},... | collective-permute-start | bytes 491528 | tf_op jit(solution)/shard_map/ppermute | solution.py:203
  50.4 6.5 %collective-permute-start.15 = (bf16[40,2048]{1,0:T(8,128)(2,1)S(1)}, bf16[40,2048]{1,0:T(8,128)(2,1)S(1)}, u32[]{:S(2)}, u32[]{:S(2)}) collective-permute-start(bf16[40,2048]{1,0:T(8,128)(2,1)S(1)} %add_convert_fusion.3), channel_id=1, source_target_pairs={{0,8},{1,9},{2,10},{3,11},{4,12},{5,13},{6,14},{7,15},{8,0},{9,1},... | collective-permute-start | bytes 491528 | tf_op jit(solution)/shard_map/ppermute | solution.py:203
  50.7 6.1 %collective-permute-start.17 = (bf16[40,2048]{1,0:T(8,128)(2,1)S(1)}, bf16[40,2048]{1,0:T(8,128)(2,1)S(1)}, u32[]{:S(2)}, u32[]{:S(2)}) collective-permute-start(bf16[40,2048]{1,0:T(8,128)(2,1)S(1)} %add_convert_fusion.2), channel_id=1, source_target_pairs={{0,2},{1,3},{2,0},{3,1},{4,6},{5,7},{6,4},{7,5},{8,10},{9,11},{10,... | collective-permute-start | bytes 491528 | tf_op jit(solution)/shard_map/ppermute | solution.py:203
  51.5 5.4 %collective-permute-start.19 = (bf16[40,2048]{1,0:T(8,128)(2,1)S(1)}, bf16[40,2048]{1,0:T(8,128)(2,1)S(1)}, u32[]{:S(2)}, u32[]{:S(2)}) collective-permute-start(bf16[40,2048]{1,0:T(8,128)(2,1)S(1)} %add_convert_fusion.1), channel_id=1, source_target_pairs={{0,4},{1,5},{2,6},{3,7},{4,0},{5,1},{6,2},{7,3},{8,12},{9,13},{10,... | collective-permute-start | bytes 491528 | tf_op jit(solution)/shard_map/ppermute | solution.py:203
  54.6 7.4 %collective-permute-start.21 = (bf16[320,2048]{1,0:T(8,128)(2,1)S(1)}, bf16[320,2048]{1,0:T(8,128)(2,1)S(1)}, u32[]{:S(2)}, u32[]{:S(2)}) collective-permute-start(bf16[320,2048]{1,0:T(8,128)(2,1)S(1)} %fusion.7), channel_id=1, source_target_pairs={{0,1},{1,0},{2,3},{3,2},{4,5},{5,4},{6,7},{7,6},{8,9},{9,8},{10,11... | collective-permute-start | bytes 3932168 | tf_op jit(solution)/shard_map/ppermute | solution.py:203
  55.9 6.1 %collective-permute-start.20 = (bf16[320,2048]{1,0:T(8,128)(2,1)S(1)}, bf16[320,2048]{1,0:T(8,128)(2,1)S(1)}, u32[]{:S(2)}, u32[]{:S(2)}) collective-permute-start(bf16[320,2048]{1,0:T(8,128)(2,1)S(1)} %fusion.6), channel_id=1, source_target_pairs={{0,1},{1,0},{2,3},{3,2},{4,5},{5,4},{6,7},{7,6},{8,9},{9,8},{10,11... | collective-permute-start | bytes 3932168 | tf_op jit(solution)/shard_map/ppermute | solution.py:203
  57.0 7.9 %collective-permute-start.22 = (bf16[40,1024]{1,0:T(8,128)(2,1)S(1)}, bf16[40,1024]{1,0:T(8,128)(2,1)S(1)}, u32[]{:S(2)}, u32[]{:S(2)}) collective-permute-start(bf16[40,1024]{1,0:T(8,128)(2,1)S(1)} %pad_maximum_fusion.23), channel_id=1, source_target_pairs={{0,16},{1,17},{2,18},{3,19},{4,20},{5,21},{6,22},{7,23},{8,24},{9,... | collective-permute-start | bytes 245768 | tf_op jit(solution)/shard_map/ppermute | solution.py:246
  (5 other events, 5.0 us)

commit v17 on v16

--- a/solution.py
+++ b/solution.py
@@ -119,6 +119,7 @@
     shapes += [shape(2 * capacity, width)] * crossing
     shapes += [shape(first, n), shape(rest, n)] + [shape(2 * capacity, n)] * crossing
     shapes += [shape(first, 2 * width)] * len(early_masks)
+    sources = (ids.reshape(1, n), gate.reshape(1, n), tokens, grads)
     outs = pl.pallas_call(
         lambda *refs: pack_kernel(blocks, experts, *refs),
         out_shape=shapes,
@@ -132,7 +133,7 @@
             pltpu.SemaphoreType.DMA((4,)),
         ],
         compiler_params=pltpu.CompilerParams(vmem_limit_bytes=8 * 1024 * 1024),
-    )(ids.reshape(1, n), gate.reshape(1, n), tokens, grads)
+    )(*[pltpu.with_memory_space_constraint(source, pltpu.HBM) for source in sources])
     return outs[: len(blocks)], outs[len(blocks) : 2 * len(blocks)], outs[2 * len(blocks) :]
 
 

time: 66.1 us -> 64 us (0.968)
  local copies, waits for them, and re-layouts: 5.08 us -> 1.88 us
  Pallas kernels: 2.96 us -> 4.13 us
    unnamed x22 -> x14, local copies, waits for them, and re-layouts: 4.51 us -> 1.31 us
    pallas_call x1, Pallas kernels: 0.49 us -> 1.66 us  [pack(): pl.pallas_call(lambda *refs: pack_kernel(blocks, experts, *refs), out_sha...]
where the time goes in v17:
time: 64 us; the launch traced here: 63.8 us
  starting transfers between devices  31.8 us (50%)
  matrix products  11.8 us (18%)
  waiting for transfers between devices  10.3 us (16%)
  Pallas kernels  4.13 us (6%)
  other arithmetic  2.85 us (4%)
  local copies, waits for them, and re-layouts  1.88 us (3%)
  between operations  1.06 us (2%)
    ppermute x21, starting transfers between devices, swap(): lax.ppermute(rows, 'expert', [(i, i ^ mask) for i in range(n_expert)])  23.2 us
    ppermute x21, waiting for transfers between devices, swap(): lax.ppermute(rows, 'expert', [(i, i ^ mask) for i in range(n_expert)])  9.67 us
    ppermute x2, starting transfers between devices, shifted(): return lax.ppermute(rows, 'expert', pairs)  8.61 us
    dot_general x11, matrix products, contract_rows(): lax.dot_general(left, right, (((0,), (0,)), ((), ())), preferred_element_...  6.06 us
    dot_general x4, matrix products, contract_cols(): lax.dot_general(left, right, (((1,), (1,)), ((), ())), preferred_element_...  4.38 us
    pallas_call x1, Pallas kernels, stepped(): pl.pallas_call(lambda *refs: step_kernel(rows, *refs), out_shape=[jax.Sha...  2.47 us
    transpose x1, other arithmetic, shards(): whole_weights(w_in)  1.93 us
    pallas_call x1, Pallas kernels, pack(): pl.pallas_call(lambda *refs: pack_kernel(blocks, experts, *refs), out_sha...  1.66 us
  transfers between devices with their start and end apart: 23, of which 9 were waited for; matrix products, arithmetic and copies ran while one was open for 17% of the time, Pallas kernels for 4%

profile of v17, /device:TPU:0, one launch (start us, length us, event | category | flops | bytes accessed | tf_op | source)
XLA Modules:
  0.0 63.8 jit_solution(9449573072007914565)
XLA Ops:
  0.6 1.7 %shard_map.85 = (bf16[16,4096]{1,0:T(8,128)(2,1)S(1)}, bf16[24,4096]{1,0:T(8,128)(2,1)S(1)}, bf16[40,2048]{1,0:T(8,128)(2,1)S(1)}, bf16[16,64]{1,0:T(8,128)(2,1)...) custom-call(s32[1,64]{1,0:T(1,128)} %bitcast.18, ...), custom_call_target="tpu_custom_call" | custom-call | tf_op jit(solution)/shard_map/pallas_call | solution.py:123
  2.3 4.1 %collective-permute-start = (bf16[40,2048]{1,0:T(8,128)(2,1)S(1)}, bf16[40,2048]{1,0:T(8,128)(2,1)S(1)}, u32[]{:S(2)}, u32[]{:S(2)}) collective-permute-start(bf16[40,2048]{1,0:T(8,128)(2,1)S(1)} %get-tuple-element.51.refs_4_), channel_id=1, source_target_pairs={{0,16},{1,17},{2,18},{3,19},{4,20},{5,21},{6,22},{7,23},{8,24},{9,... | collective-permute-start | bytes 491528 | tf_op jit(solution)/shard_map/ppermute | solution.py:247
  6.4 2.5 %collective-permute-start.1 = (bf16[16,4096]{1,0:T(8,128)(2,1)S(1)}, bf16[16,4096]{1,0:T(8,128)(2,1)S(1)}, u32[]{:S(2)}, u32[]{:S(2)}) collective-permute-start(bf16[16,4096]{1,0:T(8,128)(2,1)S(1)} %get-tuple-element.56), channel_id=1, source_target_pairs={{0,6},{1,7},{2,4},{3,5},{4,2},{5,3},{6,0},{7,1},{8,14},{9,15},{10,... | collective-permute-start | bytes 393224 | tf_op jit(solution)/shard_map/ppermute | solution.py:204
  8.9 1.6 %collective-permute-start.2 = (bf16[16,4096]{1,0:T(8,128)(2,1)S(1)}, bf16[16,4096]{1,0:T(8,128)(2,1)S(1)}, u32[]{:S(2)}, u32[]{:S(2)}) collective-permute-start(bf16[16,4096]{1,0:T(8,128)(2,1)S(1)} %get-tuple-element.57), channel_id=1, source_target_pairs={{0,8},{1,9},{2,10},{3,11},{4,12},{5,13},{6,14},{7,15},{8,0},{9,1},... | collective-permute-start | bytes 393224 | tf_op jit(solution)/shard_map/ppermute | solution.py:204
  11.5 1.9 %convert_bitcast_fusion = bf16[320,2048]{1,0:T(8,128)(2,1)S(1)} fusion(f32[2048,320]{0,1:T(8,128)} %param.10), kind=kLoop, calls=%fused_computation.24 | loop fusion | flops 655360 | bytes 3932160 | tf_op jit(solution)/shard_map/transpose | solution.py:290
  14.3 1.5 %collective-permute-done.2 = bf16[16,4096]{1,0:T(8,128)(2,1)S(1)} collective-permute-done((bf16[16,4096]{1,0:T(8,128)(2,1)S(1)}, bf16[16,4096]{1,0:T(8,128)(2,1)S(1)}, u32[]{:S(2)}, u32[]{:S(2)}) %collective-permute-start.2) | collective-permute-done | bytes 131104 | tf_op jit(solution)/shard_map/ppermute | solution.py:204
  16.0 1.6 %collective-permute-start.6 = (bf16[40,4096]{1,0:T(8,128)(2,1)S(1)}, bf16[40,4096]{1,0:T(8,128)(2,1)S(1)}, u32[]{:S(2)}, u32[]{:S(2)}) collective-permute-start(bf16[40,4096]{1,0:T(8,128)(2,1)S(1)} %get-tuple-element.64), channel_id=1, source_target_pairs={{0,2},{1,3},{2,0},{3,1},{4,6},{5,7},{6,4},{7,5},{8,10},{9,11},{10,... | collective-permute-start | bytes 983048 | tf_op jit(solution)/shard_map/ppermute | solution.py:204
  18.3 1.4 %collective-permute-start.7 = (bf16[40,4096]{1,0:T(8,128)(2,1)S(1)}, bf16[40,4096]{1,0:T(8,128)(2,1)S(1)}, u32[]{:S(2)}, u32[]{:S(2)}) collective-permute-start(bf16[40,4096]{1,0:T(8,128)(2,1)S(1)} %get-tuple-element.65), channel_id=1, source_target_pairs={{0,8},{1,9},{2,10},{3,11},{4,12},{5,13},{6,14},{7,15},{8,0},{9,1},... | collective-permute-start | bytes 983048 | tf_op jit(solution)/shard_map/ppermute | solution.py:204
  19.9 4.9 %collective-permute-done.6 = bf16[40,4096]{1,0:T(8,128)(2,1)S(1)} collective-permute-done((bf16[40,4096]{1,0:T(8,128)(2,1)S(1)}, bf16[40,4096]{1,0:T(8,128)(2,1)S(1)}, u32[]{:S(2)}, u32[]{:S(2)}) %collective-permute-start.6) | collective-permute-done | bytes 327712 | tf_op jit(solution)/shard_map/ppermute | solution.py:204
  26.4 1.5 %collective-permute-start.12 = (bf16[24,4096]{1,0:T(8,128)(2,1)S(1)}, bf16[24,4096]{1,0:T(8,128)(2,1)S(1)}, u32[]{:S(2)}, u32[]{:S(2)}) collective-permute-start(bf16[24,4096]{1,0:T(8,128)(2,1)S(1)} %get-tuple-element.67), channel_id=1, source_target_pairs={{0,6},{1,7},{2,4},{3,5},{4,2},{5,3},{6,0},{7,1},{8,14},{9,15},{10,... | collective-permute-start | bytes 589832 | tf_op jit(solution)/shard_map/ppermute | solution.py:204
  28.7 1.3 %collective-permute-start.10 = (bf16[24,4096]{1,0:T(8,128)(2,1)S(1)}, bf16[24,4096]{1,0:T(8,128)(2,1)S(1)}, u32[]{:S(2)}, u32[]{:S(2)}) collective-permute-start(bf16[24,4096]{1,0:T(8,128)(2,1)S(1)} %get-tuple-element.68), channel_id=1, source_target_pairs={{0,8},{1,9},{2,10},{3,11},{4,12},{5,13},{6,14},{7,15},{8,0},{9,1},... | collective-permute-start | bytes 589832 | tf_op jit(solution)/shard_map/ppermute | solution.py:204
  30.0 1.7 %collective-permute-start.9 = (bf16[24,4096]{1,0:T(8,128)(2,1)S(1)}, bf16[24,4096]{1,0:T(8,128)(2,1)S(1)}, u32[]{:S(2)}, u32[]{:S(2)}) collective-permute-start(bf16[24,4096]{1,0:T(8,128)(2,1)S(1)} %get-tuple-element.69), channel_id=1, source_target_pairs={{0,4},{1,5},{2,6},{3,7},{4,0},{5,1},{6,2},{7,3},{8,12},{9,13},{10,... | collective-permute-start | bytes 589832 | tf_op jit(solution)/shard_map/ppermute | solution.py:204
  32.0 1.0 %multiply_convert_fusion.1 = (bf16[128,640]{1,0:T(8,128)(2,1)S(1)}, f32[128,640]{1,0:T(8,128)S(1)}) fusion(bf16[320,2048]{1,0:T(8,128)(2,1)S(1)} %convert_bitcast_fusion, bf16[320,2048]{1,0:T(8,128)(2,1)S(1)} %get-tuple-element.95, bf16[128,4096]{1,0:T(8,128)(2,1)S(1)} %slice_dynamic-update-slice_fusion), kind=kOutput, calls=%fused_computation.67 | convolution fusion | flops 341606400 | bytes 3637248 | tf_op jit(solution)/shard_map/dot_general | solution.py:39
  33.1 1.1 %fusion.18 = bf16[128,640]{1,0:T(8,128)(2,1)S(1)} fusion(bf16[320,2048]{1,0:T(8,128)(2,1)S(1)} %get-tuple-element.96, bf16[320,2048]{1,0:T(8,128)(2,1)S(1)} %convert_bitcast_fusion.1, bf16[128,4096]{1,0:T(8,128)(2,1)S(1)} %slice_dynamic-update-slice_fusion, f32[128,640]{1,0:T(8,128)S(1)} %get-tuple-element.130), kind=kOutput, calls=%fused_computation.31 | convolution fusion | flops 342507520 | bytes 3637248 | tf_op jit(solution)/shard_map/dot_general | solution.py:39
  34.8 1.3 %collective-permute-done.9 = bf16[24,4096]{1,0:T(8,128)(2,1)S(1)} collective-permute-done((bf16[24,4096]{1,0:T(8,128)(2,1)S(1)}, bf16[24,4096]{1,0:T(8,128)(2,1)S(1)}, u32[]{:S(2)}, u32[]{:S(2)}) %collective-permute-start.9) | collective-permute-done | bytes 196640 | tf_op jit(solution)/shard_map/ppermute | solution.py:204
  36.2 1.1 %multiply_convert_fusion = (bf16[192,640]{1,0:T(8,128)(2,1)S(1)}, f32[192,640]{1,0:T(8,128)S(1)}) fusion(bf16[320,2048]{1,0:T(8,128)(2,1)S(1)} %convert_bitcast_fusion, bf16[320,2048]{1,0:T(8,128)(2,1)S(1)} %get-tuple-element.95, bf16[192,4096]{1,0:T(8,128)(2,1)S(1)} %constant_dynamic-update-slice_fusion.5), kind=kOutput, calls=%fused_computation.46 | convolution fusion | flops 509788160 | bytes 4145152 | tf_op jit(solution)/shard_map/dot_general | solution.py:39
  37.3 1.2 %fusion.15 = bf16[192,640]{1,0:T(8,128)(2,1)S(1)} fusion(bf16[320,2048]{1,0:T(8,128)(2,1)S(1)} %get-tuple-element.96, bf16[320,2048]{1,0:T(8,128)(2,1)S(1)} %convert_bitcast_fusion.1, bf16[192,4096]{1,0:T(8,128)(2,1)S(1)} %constant_dynamic-update-slice_fusion.5, f32[192,640]{1,0:T(8,128)S(1)} %get-tuple-element.128), kind=kOutput, calls=%fused_computation.28 | convolution fusion | flops 511139840 | bytes 4145152 | tf_op jit(solution)/shard_map/dot_general | solution.py:39
  39.4 1.5 %collective-permute-start.14 = (bf16[40,2048]{1,0:T(8,128)(2,1)S(1)}, bf16[40,2048]{1,0:T(8,128)(2,1)S(1)}, u32[]{:S(2)}, u32[]{:S(2)}) collective-permute-start(bf16[40,2048]{1,0:T(8,128)(2,1)S(1)} %pad_maximum_fusion.19), channel_id=1, source_target_pairs={{0,6},{1,7},{2,4},{3,5},{4,2},{5,3},{6,0},{7,1},{8,14},{9,15},{10,... | collective-permute-start | bytes 491528 | tf_op jit(solution)/shard_map/ppermute | solution.py:204
  40.9 1.5 %collective-permute-start.13 = (bf16[40,2048]{1,0:T(8,128)(2,1)S(1)}, bf16[40,2048]{1,0:T(8,128)(2,1)S(1)}, u32[]{:S(2)}, u32[]{:S(2)}) collective-permute-start(bf16[40,2048]{1,0:T(8,128)(2,1)S(1)} %get-tuple-element.74), channel_id=1, source_target_pairs={{0,2},{1,3},{2,0},{3,1},{4,6},{5,7},{6,4},{7,5},{8,10},{9,11},{10,... | collective-permute-start | bytes 491528 | tf_op jit(solution)/shard_map/ppermute | solution.py:204
  43.0 1.8 %collective-permute-start.18 = (bf16[40,2048]{1,0:T(8,128)(2,1)S(1)}, bf16[40,2048]{1,0:T(8,128)(2,1)S(1)}, u32[]{:S(2)}, u32[]{:S(2)}) collective-permute-start(bf16[40,2048]{1,0:T(8,128)(2,1)S(1)} %pad_maximum_fusion.22), channel_id=1, source_target_pairs={{0,8},{1,9},{2,10},{3,11},{4,12},{5,13},{6,14},{7,15},{8,0},{9,1},... | collective-permute-start | bytes 491528 | tf_op jit(solution)/shard_map/ppermute | solution.py:204
  46.5 1.2 %copy-done.1 = f32[2048,320]{0,1:T(8,128)S(1)} copy-done((f32[2048,320]{0,1:T(8,128)S(1)}, f32[2048,320]{0,1:T(8,128)}, u32[]{:S(2)}) %copy-start.1) | copy-done | bytes 2621464
  49.4 1.9 %collective-permute-start.19 = (bf16[40,2048]{1,0:T(8,128)(2,1)S(1)}, bf16[40,2048]{1,0:T(8,128)(2,1)S(1)}, u32[]{:S(2)}, u32[]{:S(2)}) collective-permute-start(bf16[40,2048]{1,0:T(8,128)(2,1)S(1)} %add_convert_fusion.1), channel_id=1, source_target_pairs={{0,4},{1,5},{2,6},{3,7},{4,0},{5,1},{6,2},{7,3},{8,12},{9,13},{10,... | collective-permute-start | bytes 491528 | tf_op jit(solution)/shard_map/ppermute | solution.py:204
  54.9 4.5 %collective-permute-start.22 = (bf16[40,1024]{1,0:T(8,128)(2,1)S(1)}, bf16[40,1024]{1,0:T(8,128)(2,1)S(1)}, u32[]{:S(2)}, u32[]{:S(2)}) collective-permute-start(bf16[40,1024]{1,0:T(8,128)(2,1)S(1)} %pad_maximum_fusion.23), channel_id=1, source_target_pairs={{0,16},{1,17},{2,18},{3,19},{4,20},{5,21},{6,22},{7,23},{8,24},{9,... | collective-permute-start | bytes 245768 | tf_op jit(solution)/shard_map/ppermute | solution.py:247
  60.0 2.5 %shard_map.87 = (f32[320,2048]{1,0:T(8,128)}, f32[320,2048]{1,0:T(8,128)}) custom-call(f32[320,2048]{1,0:T(8,128)S(1)} %fusion.5.refs_0_, f32[320,2048]{1,0:T(8,128)S(1)} %fusion.3.refs_1_, bf16[320,2048]{1,0:T(8,128)(2,1)S(1)} %collective-permute-done.20.refs_2_, bf16[320,2048]{1,0:T(8,128)(2,1)S(1)} %collective-permute-done.21.refs_3_), custom_call_target="tpu_custom_call" | custom-call | flops 2621440 | bytes 5242880 | tf_op jit(solution)/shard_map/pallas_call | solution.py:179
  (80 shorter events, 16.6 us)
Async XLA Ops:
  0.6 12.8 %copy-start = (f32[2048,320]{0,1:T(8,128)S(1)}, f32[2048,320]{0,1:T(8,128)}, u32[]{:S(2)}) copy-start(f32[2048,320]{0,1:T(8,128)} %param.11) | copy-start | bytes 7864324
  2.3 11.9 %collective-permute-start = (bf16[40,2048]{1,0:T(8,128)(2,1)S(1)}, bf16[40,2048]{1,0:T(8,128)(2,1)S(1)}, u32[]{:S(2)}, u32[]{:S(2)}) collective-permute-start(bf16[40,2048]{1,0:T(8,128)(2,1)S(1)} %get-tuple-element.51.refs_4_), channel_id=1, source_target_pairs={{0,16},{1,17},{2,18},{3,19},{4,20},{5,21},{6,22},{7,23},{8,24},{9,... | collective-permute-start | bytes 491528 | tf_op jit(solution)/shard_map/ppermute | solution.py:247
  6.4 7.9 %collective-permute-start.1 = (bf16[16,4096]{1,0:T(8,128)(2,1)S(1)}, bf16[16,4096]{1,0:T(8,128)(2,1)S(1)}, u32[]{:S(2)}, u32[]{:S(2)}) collective-permute-start(bf16[16,4096]{1,0:T(8,128)(2,1)S(1)} %get-tuple-element.56), channel_id=1, source_target_pairs={{0,6},{1,7},{2,4},{3,5},{4,2},{5,3},{6,0},{7,1},{8,14},{9,15},{10,... | collective-permute-start | bytes 393224 | tf_op jit(solution)/shard_map/ppermute | solution.py:204
  8.9 7.0 %collective-permute-start.2 = (bf16[16,4096]{1,0:T(8,128)(2,1)S(1)}, bf16[16,4096]{1,0:T(8,128)(2,1)S(1)}, u32[]{:S(2)}, u32[]{:S(2)}) collective-permute-start(bf16[16,4096]{1,0:T(8,128)(2,1)S(1)} %get-tuple-element.57), channel_id=1, source_target_pairs={{0,8},{1,9},{2,10},{3,11},{4,12},{5,13},{6,14},{7,15},{8,0},{9,1},... | collective-permute-start | bytes 393224 | tf_op jit(solution)/shard_map/ppermute | solution.py:204
  10.4 5.4 %collective-permute-start.3 = (bf16[16,4096]{1,0:T(8,128)(2,1)S(1)}, bf16[16,4096]{1,0:T(8,128)(2,1)S(1)}, u32[]{:S(2)}, u32[]{:S(2)}) collective-permute-start(bf16[16,4096]{1,0:T(8,128)(2,1)S(1)} %get-tuple-element.58), channel_id=1, source_target_pairs={{0,2},{1,3},{2,0},{3,1},{4,6},{5,7},{6,4},{7,5},{8,10},{9,11},{10,... | collective-permute-start | bytes 393224 | tf_op jit(solution)/shard_map/ppermute | solution.py:204
  11.0 5.0 %collective-permute-start.4 = (bf16[16,4096]{1,0:T(8,128)(2,1)S(1)}, bf16[16,4096]{1,0:T(8,128)(2,1)S(1)}, u32[]{:S(2)}, u32[]{:S(2)}) collective-permute-start(bf16[16,4096]{1,0:T(8,128)(2,1)S(1)} %get-tuple-element.59), channel_id=1, source_target_pairs={{0,4},{1,5},{2,6},{3,7},{4,0},{5,1},{6,2},{7,3},{8,12},{9,13},{10,... | collective-permute-start | bytes 393224 | tf_op jit(solution)/shard_map/ppermute | solution.py:204
  16.0 8.8 %collective-permute-start.6 = (bf16[40,4096]{1,0:T(8,128)(2,1)S(1)}, bf16[40,4096]{1,0:T(8,128)(2,1)S(1)}, u32[]{:S(2)}, u32[]{:S(2)}) collective-permute-start(bf16[40,4096]{1,0:T(8,128)(2,1)S(1)} %get-tuple-element.64), channel_id=1, source_target_pairs={{0,2},{1,3},{2,0},{3,1},{4,6},{5,7},{6,4},{7,5},{8,10},{9,11},{10,... | collective-permute-start | bytes 983048 | tf_op jit(solution)/shard_map/ppermute | solution.py:204
  17.5 7.8 %collective-permute-start.5 = (bf16[40,4096]{1,0:T(8,128)(2,1)S(1)}, bf16[40,4096]{1,0:T(8,128)(2,1)S(1)}, u32[]{:S(2)}, u32[]{:S(2)}) collective-permute-start(bf16[40,4096]{1,0:T(8,128)(2,1)S(1)} %get-tuple-element.64), channel_id=1, source_target_pairs={{0,4},{1,5},{2,6},{3,7},{4,0},{5,1},{6,2},{7,3},{8,12},{9,13},{10,... | collective-permute-start | bytes 983048 | tf_op jit(solution)/shard_map/ppermute | solution.py:204
  18.3 8.0 %collective-permute-start.7 = (bf16[40,4096]{1,0:T(8,128)(2,1)S(1)}, bf16[40,4096]{1,0:T(8,128)(2,1)S(1)}, u32[]{:S(2)}, u32[]{:S(2)}) collective-permute-start(bf16[40,4096]{1,0:T(8,128)(2,1)S(1)} %get-tuple-element.65), channel_id=1, source_target_pairs={{0,8},{1,9},{2,10},{3,11},{4,12},{5,13},{6,14},{7,15},{8,0},{9,1},... | collective-permute-start | bytes 983048 | tf_op jit(solution)/shard_map/ppermute | solution.py:204
  19.8 11.9 %collective-permute-start.8 = (bf16[640,2048]{1,0:T(8,128)(2,1)S(1)}, bf16[640,2048]{1,0:T(8,128)(2,1)S(1)}, u32[]{:S(2)}, u32[]{:S(2)}) collective-permute-start(bf16[640,2048]{1,0:T(8,128)(2,1)S(1)} %pad_maximum_fusion.1), channel_id=1, source_target_pairs={{0,1},{1,0},{2,3},{3,2},{4,5},{5,4},{6,7},{7,6},{8,9},{9,8},{10,11... | collective-permute-start | bytes 7864328 | tf_op jit(solution)/shard_map/ppermute | solution.py:204
  26.4 9.7 %collective-permute-start.12 = (bf16[24,4096]{1,0:T(8,128)(2,1)S(1)}, bf16[24,4096]{1,0:T(8,128)(2,1)S(1)}, u32[]{:S(2)}, u32[]{:S(2)}) collective-permute-start(bf16[24,4096]{1,0:T(8,128)(2,1)S(1)} %get-tuple-element.67), channel_id=1, source_target_pairs={{0,6},{1,7},{2,4},{3,5},{4,2},{5,3},{6,0},{7,1},{8,14},{9,15},{10,... | collective-permute-start | bytes 589832 | tf_op jit(solution)/shard_map/ppermute | solution.py:204
  27.8 8.2 %collective-permute-start.11 = (bf16[24,4096]{1,0:T(8,128)(2,1)S(1)}, bf16[24,4096]{1,0:T(8,128)(2,1)S(1)}, u32[]{:S(2)}, u32[]{:S(2)}) collective-permute-start(bf16[24,4096]{1,0:T(8,128)(2,1)S(1)} %get-tuple-element.67), channel_id=1, source_target_pairs={{0,2},{1,3},{2,0},{3,1},{4,6},{5,7},{6,4},{7,5},{8,10},{9,11},{10,... | collective-permute-start | bytes 589832 | tf_op jit(solution)/shard_map/ppermute | solution.py:204
  28.7 7.4 %collective-permute-start.10 = (bf16[24,4096]{1,0:T(8,128)(2,1)S(1)}, bf16[24,4096]{1,0:T(8,128)(2,1)S(1)}, u32[]{:S(2)}, u32[]{:S(2)}) collective-permute-start(bf16[24,4096]{1,0:T(8,128)(2,1)S(1)} %get-tuple-element.68), channel_id=1, source_target_pairs={{0,8},{1,9},{2,10},{3,11},{4,12},{5,13},{6,14},{7,15},{8,0},{9,1},... | collective-permute-start | bytes 589832 | tf_op jit(solution)/shard_map/ppermute | solution.py:204
  30.0 6.1 %collective-permute-start.9 = (bf16[24,4096]{1,0:T(8,128)(2,1)S(1)}, bf16[24,4096]{1,0:T(8,128)(2,1)S(1)}, u32[]{:S(2)}, u32[]{:S(2)}) collective-permute-start(bf16[24,4096]{1,0:T(8,128)(2,1)S(1)} %get-tuple-element.69), channel_id=1, source_target_pairs={{0,4},{1,5},{2,6},{3,7},{4,0},{5,1},{6,2},{7,3},{8,12},{9,13},{10,... | collective-permute-start | bytes 589832 | tf_op jit(solution)/shard_map/ppermute | solution.py:204
  39.4 8.9 %collective-permute-start.14 = (bf16[40,2048]{1,0:T(8,128)(2,1)S(1)}, bf16[40,2048]{1,0:T(8,128)(2,1)S(1)}, u32[]{:S(2)}, u32[]{:S(2)}) collective-permute-start(bf16[40,2048]{1,0:T(8,128)(2,1)S(1)} %pad_maximum_fusion.19), channel_id=1, source_target_pairs={{0,6},{1,7},{2,4},{3,5},{4,2},{5,3},{6,0},{7,1},{8,14},{9,15},{10,... | collective-permute-start | bytes 491528 | tf_op jit(solution)/shard_map/ppermute | solution.py:204
  40.9 7.4 %collective-permute-start.13 = (bf16[40,2048]{1,0:T(8,128)(2,1)S(1)}, bf16[40,2048]{1,0:T(8,128)(2,1)S(1)}, u32[]{:S(2)}, u32[]{:S(2)}) collective-permute-start(bf16[40,2048]{1,0:T(8,128)(2,1)S(1)} %get-tuple-element.74), channel_id=1, source_target_pairs={{0,2},{1,3},{2,0},{3,1},{4,6},{5,7},{6,4},{7,5},{8,10},{9,11},{10,... | collective-permute-start | bytes 491528 | tf_op jit(solution)/shard_map/ppermute | solution.py:204
  42.4 6.2 %collective-permute-start.16 = (bf16[40,2048]{1,0:T(8,128)(2,1)S(1)}, bf16[40,2048]{1,0:T(8,128)(2,1)S(1)}, u32[]{:S(2)}, u32[]{:S(2)}) collective-permute-start(bf16[40,2048]{1,0:T(8,128)(2,1)S(1)} %get-tuple-element.75), channel_id=1, source_target_pairs={{0,4},{1,5},{2,6},{3,7},{4,0},{5,1},{6,2},{7,3},{8,12},{9,13},{10,... | collective-permute-start | bytes 491528 | tf_op jit(solution)/shard_map/ppermute | solution.py:204
  43.0 6.3 %collective-permute-start.18 = (bf16[40,2048]{1,0:T(8,128)(2,1)S(1)}, bf16[40,2048]{1,0:T(8,128)(2,1)S(1)}, u32[]{:S(2)}, u32[]{:S(2)}) collective-permute-start(bf16[40,2048]{1,0:T(8,128)(2,1)S(1)} %pad_maximum_fusion.22), channel_id=1, source_target_pairs={{0,8},{1,9},{2,10},{3,11},{4,12},{5,13},{6,14},{7,15},{8,0},{9,1},... | collective-permute-start | bytes 491528 | tf_op jit(solution)/shard_map/ppermute | solution.py:204
  48.3 6.5 %collective-permute-start.15 = (bf16[40,2048]{1,0:T(8,128)(2,1)S(1)}, bf16[40,2048]{1,0:T(8,128)(2,1)S(1)}, u32[]{:S(2)}, u32[]{:S(2)}) collective-permute-start(bf16[40,2048]{1,0:T(8,128)(2,1)S(1)} %add_convert_fusion.3), channel_id=1, source_target_pairs={{0,8},{1,9},{2,10},{3,11},{4,12},{5,13},{6,14},{7,15},{8,0},{9,1},... | collective-permute-start | bytes 491528 | tf_op jit(solution)/shard_map/ppermute | solution.py:204
  48.7 6.1 %collective-permute-start.17 = (bf16[40,2048]{1,0:T(8,128)(2,1)S(1)}, bf16[40,2048]{1,0:T(8,128)(2,1)S(1)}, u32[]{:S(2)}, u32[]{:S(2)}) collective-permute-start(bf16[40,2048]{1,0:T(8,128)(2,1)S(1)} %add_convert_fusion.2), channel_id=1, source_target_pairs={{0,2},{1,3},{2,0},{3,1},{4,6},{5,7},{6,4},{7,5},{8,10},{9,11},{10,... | collective-permute-start | bytes 491528 | tf_op jit(solution)/shard_map/ppermute | solution.py:204
  49.4 5.4 %collective-permute-start.19 = (bf16[40,2048]{1,0:T(8,128)(2,1)S(1)}, bf16[40,2048]{1,0:T(8,128)(2,1)S(1)}, u32[]{:S(2)}, u32[]{:S(2)}) collective-permute-start(bf16[40,2048]{1,0:T(8,128)(2,1)S(1)} %add_convert_fusion.1), channel_id=1, source_target_pairs={{0,4},{1,5},{2,6},{3,7},{4,0},{5,1},{6,2},{7,3},{8,12},{9,13},{10,... | collective-permute-start | bytes 491528 | tf_op jit(solution)/shard_map/ppermute | solution.py:204
  52.5 7.4 %collective-permute-start.21 = (bf16[320,2048]{1,0:T(8,128)(2,1)S(1)}, bf16[320,2048]{1,0:T(8,128)(2,1)S(1)}, u32[]{:S(2)}, u32[]{:S(2)}) collective-permute-start(bf16[320,2048]{1,0:T(8,128)(2,1)S(1)} %fusion.7), channel_id=1, source_target_pairs={{0,1},{1,0},{2,3},{3,2},{4,5},{5,4},{6,7},{7,6},{8,9},{9,8},{10,11... | collective-permute-start | bytes 3932168 | tf_op jit(solution)/shard_map/ppermute | solution.py:204
  53.8 6.1 %collective-permute-start.20 = (bf16[320,2048]{1,0:T(8,128)(2,1)S(1)}, bf16[320,2048]{1,0:T(8,128)(2,1)S(1)}, u32[]{:S(2)}, u32[]{:S(2)}) collective-permute-start(bf16[320,2048]{1,0:T(8,128)(2,1)S(1)} %fusion.6), channel_id=1, source_target_pairs={{0,1},{1,0},{2,3},{3,2},{4,5},{5,4},{6,7},{7,6},{8,9},{9,8},{10,11... | collective-permute-start | bytes 3932168 | tf_op jit(solution)/shard_map/ppermute | solution.py:204
  54.9 7.9 %collective-permute-start.22 = (bf16[40,1024]{1,0:T(8,128)(2,1)S(1)}, bf16[40,1024]{1,0:T(8,128)(2,1)S(1)}, u32[]{:S(2)}, u32[]{:S(2)}) collective-permute-start(bf16[40,1024]{1,0:T(8,128)(2,1)S(1)} %pad_maximum_fusion.23), channel_id=1, source_target_pairs={{0,16},{1,17},{2,18},{3,19},{4,20},{5,21},{6,22},{7,23},{8,24},{9,... | collective-permute-start | bytes 245768 | tf_op jit(solution)/shard_map/ppermute | solution.py:247
  (1 other events, 1.7 us)

commit v18 on v17

--- a/solution.py
+++ b/solution.py
@@ -61,7 +61,7 @@
     ]
     for fetch in fetches:
         fetch.start()
-    for fetch in fetches:
+    for fetch in fetches[:2]:
         fetch.wait()
     n, width = tokens_ref.shape
     mine = (lax.axis_index("expert") // SHARDS).astype(jnp.float32)
@@ -74,8 +74,6 @@
     gate_down = jnp.sum(jnp.where(down == across, gate_ref[...], 0.0), axis=1, keepdims=True)
     rivals = jnp.where((ids_down == ids) & (down < across), 1.0, 0.0)
     rank = jnp.sum(rivals, axis=0, keepdims=True)
-    tokens = tokens_ref[...]
-    gated = (gate_down * grads_ref[...].astype(jnp.float32)).astype(jnp.bfloat16)
     rows, picks = outs[: len(blocks)], outs[len(blocks) : 2 * len(blocks)]
     copies = outs[2 * len(blocks) :]
 
@@ -93,7 +91,10 @@
         lowers.append(uppers[k] if k < 2 else one_hot(shape, block, block[2]))
         picks[k][...] = uppers[k].astype(jnp.bfloat16)
     upper, lower = [jnp.concatenate(p, axis=0).astype(jnp.bfloat16) for p in (uppers, lowers)]
-    from_tokens, from_gated = picked(upper, tokens), picked(lower, gated)
+    for fetch in fetches[2:]:
+        fetch.wait()
+    gated = (gate_down * grads_ref[...].astype(jnp.float32)).astype(jnp.bfloat16)
+    from_tokens, from_gated = picked(upper, tokens_ref[...]), picked(lower, gated)
     start = 0
     for k, rows_ref in enumerate(rows):
         part = slice(start, start + rows_ref.shape[0])
@@ -320,13 +321,14 @@
             for left, right, scale in ((3, 0, scale_in), (2, 1, scale_out))
         ]
 
-    mine = gradients(slice(0, units), back[-1])
+    theirs = gradients(slice(units, 2 * units), back[-1])
+    theirs = [grads.astype(jnp.bfloat16) for grads in theirs]
+    zx, theirs = lax.optimization_barrier((zx, theirs))
+    shares = [swap(grads, core_bit) for grads in theirs]
+    mine = gradients(slice(0, units), zx)
     split_width = lax.axis_size("dp") > 1
     if not split_width:
         mine = [weights.T - step_rate * grads for weights, grads in zip((w_in, w_out), mine)]
-    zx = after(zx, mine)
-    theirs = gradients(slice(units, 2 * units), zx)
-    shares = [swap(grads.astype(jnp.bfloat16), core_bit) for grads in theirs]
     if split_width:
         new_weights = [
             stepped_over_dp(weights, (grads + share.astype(jnp.float32)).T)

time: 64 us -> 63.8 us (level)
  local copies, waits for them, and re-layouts: 1.88 us -> 1.22 us
where the time goes in v18:
time: 63.8 us; the launch traced here: 63.7 us
  starting transfers between devices  32 us (50%)
  matrix products  11.8 us (18%)
  waiting for transfers between devices  10.7 us (17%)
  Pallas kernels  4.03 us (6%)
  other arithmetic  2.85 us (4%)
  local copies, waits for them, and re-layouts  1.22 us (2%)
  between operations  1.03 us (2%)
    ppermute x21, starting transfers between devices, swap(): lax.ppermute(rows, 'expert', [(i, i ^ mask) for i in range(n_expert)])  23.3 us
    ppermute x21, waiting for transfers between devices, swap(): lax.ppermute(rows, 'expert', [(i, i ^ mask) for i in range(n_expert)])  10.2 us
    ppermute x2, starting transfers between devices, shifted(): return lax.ppermute(rows, 'expert', pairs)  8.68 us
    dot_general x11, matrix products, contract_rows(): lax.dot_general(left, right, (((0,), (0,)), ((), ())), preferred_element_...  6.06 us
    dot_general x4, matrix products, contract_cols(): lax.dot_general(left, right, (((1,), (1,)), ((), ())), preferred_element_...  4.36 us
    pallas_call x1, Pallas kernels, stepped(): pl.pallas_call(lambda *refs: step_kernel(rows, *refs), out_shape=[jax.Sha...  2.47 us
    transpose x1, other arithmetic, shards(): whole_weights(w_in)  1.93 us
    pallas_call x1, Pallas kernels, pack(): pl.pallas_call(lambda *refs: pack_kernel(blocks, experts, *refs), out_sha...  1.56 us
  transfers between devices with their start and end apart: 23, of which 9 were waited for; matrix products, arithmetic and copies ran while one was open for 17% of the time, Pallas kernels for 4%

profile of v18, /device:TPU:0, one launch (start us, length us, event | category | flops | bytes accessed | tf_op | source)
XLA Modules:
  0.0 63.7 jit_solution(336429367768266416)
XLA Ops:
  0.6 1.6 %shard_map.85 = (bf16[16,4096]{1,0:T(8,128)(2,1)S(1)}, bf16[24,4096]{1,0:T(8,128)(2,1)S(1)}, bf16[40,2048]{1,0:T(8,128)(2,1)S(1)}, bf16[16,64]{1,0:T(8,128)(2,1)...) custom-call(s32[1,64]{1,0:T(1,128)} %bitcast.18, ...), custom_call_target="tpu_custom_call" | custom-call | tf_op jit(solution)/shard_map/pallas_call | solution.py:124
  2.2 4.1 %collective-permute-start = (bf16[40,2048]{1,0:T(8,128)(2,1)S(1)}, bf16[40,2048]{1,0:T(8,128)(2,1)S(1)}, u32[]{:S(2)}, u32[]{:S(2)}) collective-permute-start(bf16[40,2048]{1,0:T(8,128)(2,1)S(1)} %get-tuple-element.53.refs_4_), channel_id=1, source_target_pairs={{0,16},{1,17},{2,18},{3,19},{4,20},{5,21},{6,22},{7,23},{8,24},{9,... | collective-permute-start | bytes 491528 | tf_op jit(solution)/shard_map/ppermute | solution.py:248
  6.3 2.5 %collective-permute-start.1 = (bf16[16,4096]{1,0:T(8,128)(2,1)S(1)}, bf16[16,4096]{1,0:T(8,128)(2,1)S(1)}, u32[]{:S(2)}, u32[]{:S(2)}) collective-permute-start(bf16[16,4096]{1,0:T(8,128)(2,1)S(1)} %get-tuple-element.58), channel_id=1, source_target_pairs={{0,6},{1,7},{2,4},{3,5},{4,2},{5,3},{6,0},{7,1},{8,14},{9,15},{10,... | collective-permute-start | bytes 393224 | tf_op jit(solution)/shard_map/ppermute | solution.py:205
  8.8 1.6 %collective-permute-start.2 = (bf16[16,4096]{1,0:T(8,128)(2,1)S(1)}, bf16[16,4096]{1,0:T(8,128)(2,1)S(1)}, u32[]{:S(2)}, u32[]{:S(2)}) collective-permute-start(bf16[16,4096]{1,0:T(8,128)(2,1)S(1)} %get-tuple-element.59), channel_id=1, source_target_pairs={{0,8},{1,9},{2,10},{3,11},{4,12},{5,13},{6,14},{7,15},{8,0},{9,1},... | collective-permute-start | bytes 393224 | tf_op jit(solution)/shard_map/ppermute | solution.py:205
  11.4 1.9 %convert_bitcast_fusion = bf16[320,2048]{1,0:T(8,128)(2,1)S(1)} fusion(f32[2048,320]{0,1:T(8,128)} %param.10), kind=kLoop, calls=%fused_computation.24 | loop fusion | flops 655360 | bytes 3932160 | tf_op jit(solution)/shard_map/transpose | solution.py:291
  14.2 1.5 %collective-permute-done.2 = bf16[16,4096]{1,0:T(8,128)(2,1)S(1)} collective-permute-done((bf16[16,4096]{1,0:T(8,128)(2,1)S(1)}, bf16[16,4096]{1,0:T(8,128)(2,1)S(1)}, u32[]{:S(2)}, u32[]{:S(2)}) %collective-permute-start.2) | collective-permute-done | bytes 131104 | tf_op jit(solution)/shard_map/ppermute | solution.py:205
  15.9 1.6 %collective-permute-start.6 = (bf16[40,4096]{1,0:T(8,128)(2,1)S(1)}, bf16[40,4096]{1,0:T(8,128)(2,1)S(1)}, u32[]{:S(2)}, u32[]{:S(2)}) collective-permute-start(bf16[40,4096]{1,0:T(8,128)(2,1)S(1)} %get-tuple-element.66), channel_id=1, source_target_pairs={{0,2},{1,3},{2,0},{3,1},{4,6},{5,7},{6,4},{7,5},{8,10},{9,11},{10,... | collective-permute-start | bytes 983048 | tf_op jit(solution)/shard_map/ppermute | solution.py:205
  18.2 1.4 %collective-permute-start.7 = (bf16[40,4096]{1,0:T(8,128)(2,1)S(1)}, bf16[40,4096]{1,0:T(8,128)(2,1)S(1)}, u32[]{:S(2)}, u32[]{:S(2)}) collective-permute-start(bf16[40,4096]{1,0:T(8,128)(2,1)S(1)} %get-tuple-element.67), channel_id=1, source_target_pairs={{0,8},{1,9},{2,10},{3,11},{4,12},{5,13},{6,14},{7,15},{8,0},{9,1},... | collective-permute-start | bytes 983048 | tf_op jit(solution)/shard_map/ppermute | solution.py:205
  19.8 4.9 %collective-permute-done.6 = bf16[40,4096]{1,0:T(8,128)(2,1)S(1)} collective-permute-done((bf16[40,4096]{1,0:T(8,128)(2,1)S(1)}, bf16[40,4096]{1,0:T(8,128)(2,1)S(1)}, u32[]{:S(2)}, u32[]{:S(2)}) %collective-permute-start.6) | collective-permute-done | bytes 327712 | tf_op jit(solution)/shard_map/ppermute | solution.py:205
  26.3 1.5 %collective-permute-start.12 = (bf16[24,4096]{1,0:T(8,128)(2,1)S(1)}, bf16[24,4096]{1,0:T(8,128)(2,1)S(1)}, u32[]{:S(2)}, u32[]{:S(2)}) collective-permute-start(bf16[24,4096]{1,0:T(8,128)(2,1)S(1)} %get-tuple-element.69), channel_id=1, source_target_pairs={{0,6},{1,7},{2,4},{3,5},{4,2},{5,3},{6,0},{7,1},{8,14},{9,15},{10,... | collective-permute-start | bytes 589832 | tf_op jit(solution)/shard_map/ppermute | solution.py:205
  28.6 1.3 %collective-permute-start.10 = (bf16[24,4096]{1,0:T(8,128)(2,1)S(1)}, bf16[24,4096]{1,0:T(8,128)(2,1)S(1)}, u32[]{:S(2)}, u32[]{:S(2)}) collective-permute-start(bf16[24,4096]{1,0:T(8,128)(2,1)S(1)} %get-tuple-element.70), channel_id=1, source_target_pairs={{0,8},{1,9},{2,10},{3,11},{4,12},{5,13},{6,14},{7,15},{8,0},{9,1},... | collective-permute-start | bytes 589832 | tf_op jit(solution)/shard_map/ppermute | solution.py:205
  29.9 1.7 %collective-permute-start.9 = (bf16[24,4096]{1,0:T(8,128)(2,1)S(1)}, bf16[24,4096]{1,0:T(8,128)(2,1)S(1)}, u32[]{:S(2)}, u32[]{:S(2)}) collective-permute-start(bf16[24,4096]{1,0:T(8,128)(2,1)S(1)} %get-tuple-element.71), channel_id=1, source_target_pairs={{0,4},{1,5},{2,6},{3,7},{4,0},{5,1},{6,2},{7,3},{8,12},{9,13},{10,... | collective-permute-start | bytes 589832 | tf_op jit(solution)/shard_map/ppermute | solution.py:205
  31.9 1.0 %multiply_convert_fusion.1 = (bf16[128,640]{1,0:T(8,128)(2,1)S(1)}, f32[128,640]{1,0:T(8,128)S(1)}) fusion(bf16[320,2048]{1,0:T(8,128)(2,1)S(1)} %convert_bitcast_fusion, bf16[320,2048]{1,0:T(8,128)(2,1)S(1)} %get-tuple-element.99, bf16[128,4096]{1,0:T(8,128)(2,1)S(1)} %slice_dynamic-update-slice_fusion), kind=kOutput, calls=%fused_computation.67 | convolution fusion | flops 341606400 | bytes 3637248 | tf_op jit(solution)/shard_map/dot_general | solution.py:39
  32.9 1.0 %fusion.18 = bf16[128,640]{1,0:T(8,128)(2,1)S(1)} fusion(bf16[320,2048]{1,0:T(8,128)(2,1)S(1)} %get-tuple-element.100, bf16[320,2048]{1,0:T(8,128)(2,1)S(1)} %convert_bitcast_fusion.1, bf16[128,4096]{1,0:T(8,128)(2,1)S(1)} %slice_dynamic-update-slice_fusion, f32[128,640]{1,0:T(8,128)S(1)} %get-tuple-element.134), kind=kOutput, calls=%fused_computation.31 | convolution fusion | flops 342507520 | bytes 3637248 | tf_op jit(solution)/shard_map/dot_general | solution.py:39
  34.6 1.4 %collective-permute-done.9 = bf16[24,4096]{1,0:T(8,128)(2,1)S(1)} collective-permute-done((bf16[24,4096]{1,0:T(8,128)(2,1)S(1)}, bf16[24,4096]{1,0:T(8,128)(2,1)S(1)}, u32[]{:S(2)}, u32[]{:S(2)}) %collective-permute-start.9) | collective-permute-done | bytes 196640 | tf_op jit(solution)/shard_map/ppermute | solution.py:205
  36.1 1.1 %multiply_convert_fusion = (bf16[192,640]{1,0:T(8,128)(2,1)S(1)}, f32[192,640]{1,0:T(8,128)S(1)}) fusion(bf16[320,2048]{1,0:T(8,128)(2,1)S(1)} %convert_bitcast_fusion, bf16[320,2048]{1,0:T(8,128)(2,1)S(1)} %get-tuple-element.99, bf16[192,4096]{1,0:T(8,128)(2,1)S(1)} %constant_dynamic-update-slice_fusion.5), kind=kOutput, calls=%fused_computation.46 | convolution fusion | flops 509788160 | bytes 4145152 | tf_op jit(solution)/shard_map/dot_general | solution.py:39
  37.2 1.2 %fusion.15 = bf16[192,640]{1,0:T(8,128)(2,1)S(1)} fusion(bf16[320,2048]{1,0:T(8,128)(2,1)S(1)} %get-tuple-element.100, bf16[320,2048]{1,0:T(8,128)(2,1)S(1)} %convert_bitcast_fusion.1, bf16[192,4096]{1,0:T(8,128)(2,1)S(1)} %constant_dynamic-update-slice_fusion.5, f32[192,640]{1,0:T(8,128)S(1)} %get-tuple-element.132), kind=kOutput, calls=%fused_computation.28 | convolution fusion | flops 511139840 | bytes 4145152 | tf_op jit(solution)/shard_map/dot_general | solution.py:39
  39.3 1.5 %collective-permute-start.14 = (bf16[40,2048]{1,0:T(8,128)(2,1)S(1)}, bf16[40,2048]{1,0:T(8,128)(2,1)S(1)}, u32[]{:S(2)}, u32[]{:S(2)}) collective-permute-start(bf16[40,2048]{1,0:T(8,128)(2,1)S(1)} %pad_maximum_fusion.19), channel_id=1, source_target_pairs={{0,6},{1,7},{2,4},{3,5},{4,2},{5,3},{6,0},{7,1},{8,14},{9,15},{10,... | collective-permute-start | bytes 491528 | tf_op jit(solution)/shard_map/ppermute | solution.py:205
  40.8 1.5 %collective-permute-start.13 = (bf16[40,2048]{1,0:T(8,128)(2,1)S(1)}, bf16[40,2048]{1,0:T(8,128)(2,1)S(1)}, u32[]{:S(2)}, u32[]{:S(2)}) collective-permute-start(bf16[40,2048]{1,0:T(8,128)(2,1)S(1)} %get-tuple-element.76), channel_id=1, source_target_pairs={{0,2},{1,3},{2,0},{3,1},{4,6},{5,7},{6,4},{7,5},{8,10},{9,11},{10,... | collective-permute-start | bytes 491528 | tf_op jit(solution)/shard_map/ppermute | solution.py:205
  43.0 1.8 %collective-permute-start.18 = (bf16[40,2048]{1,0:T(8,128)(2,1)S(1)}, bf16[40,2048]{1,0:T(8,128)(2,1)S(1)}, u32[]{:S(2)}, u32[]{:S(2)}) collective-permute-start(bf16[40,2048]{1,0:T(8,128)(2,1)S(1)} %pad_maximum_fusion.22), channel_id=1, source_target_pairs={{0,8},{1,9},{2,10},{3,11},{4,12},{5,13},{6,14},{7,15},{8,0},{9,1},... | collective-permute-start | bytes 491528 | tf_op jit(solution)/shard_map/ppermute | solution.py:205
  49.3 2.0 %collective-permute-start.19 = (bf16[40,2048]{1,0:T(8,128)(2,1)S(1)}, bf16[40,2048]{1,0:T(8,128)(2,1)S(1)}, u32[]{:S(2)}, u32[]{:S(2)}) collective-permute-start(bf16[40,2048]{1,0:T(8,128)(2,1)S(1)} %add_convert_fusion.1), channel_id=1, source_target_pairs={{0,4},{1,5},{2,6},{3,7},{4,0},{5,1},{6,2},{7,3},{8,12},{9,13},{10,... | collective-permute-start | bytes 491528 | tf_op jit(solution)/shard_map/ppermute | solution.py:205
  54.8 4.6 %collective-permute-start.22 = (bf16[40,1024]{1,0:T(8,128)(2,1)S(1)}, bf16[40,1024]{1,0:T(8,128)(2,1)S(1)}, u32[]{:S(2)}, u32[]{:S(2)}) collective-permute-start(bf16[40,1024]{1,0:T(8,128)(2,1)S(1)} %pad_maximum_fusion.23), channel_id=1, source_target_pairs={{0,16},{1,17},{2,18},{3,19},{4,20},{5,21},{6,22},{7,23},{8,24},{9,... | collective-permute-start | bytes 245768 | tf_op jit(solution)/shard_map/ppermute | solution.py:248
  59.9 2.5 %shard_map.87 = (f32[320,2048]{1,0:T(8,128)}, f32[320,2048]{1,0:T(8,128)}) custom-call(f32[320,2048]{1,0:T(8,128)S(1)} %fusion.3.refs_0_, f32[320,2048]{1,0:T(8,128)S(1)} %fusion.1.refs_1_, bf16[320,2048]{1,0:T(8,128)(2,1)S(1)} %collective-permute-done.20.refs_2_, bf16[320,2048]{1,0:T(8,128)(2,1)S(1)} %collective-permute-done.21.refs_3_), custom_call_target="tpu_custom_call" | custom-call | flops 2621440 | bytes 5242880 | tf_op jit(solution)/shard_map/pallas_call | solution.py:180
  62.7 1.0 %fusion.10 = bf16[64,2048]{1,0:T(8,128)(2,1)} fusion(f32[64,2048]{1,0:T(8,128)S(1)} %convolution_add_fusion.5, bf16[20,1024]{1,0:T(8,128)(2,1)S(1)} %get-tuple-element.130, bf16[20,1024]{1,0:T(8,128)(2,1)S(1)} %get-tuple-element.129, bf16[40,64]{1,0:T(8,128)(2,1)S(1)} %get-tuple-element.87), kind=kOutput, calls=%fused_computation.21 | convolution fusion | flops 5668864 | bytes 890880 | tf_op jit(solution)/shard_map/dot_general | solution.py:33
  (80 shorter events, 16.5 us)
Async XLA Ops:
  0.6 12.7 %copy-start = (f32[2048,320]{0,1:T(8,128)S(1)}, f32[2048,320]{0,1:T(8,128)}, u32[]{:S(2)}) copy-start(f32[2048,320]{0,1:T(8,128)} %param.11) | copy-start | bytes 7864324
  2.2 11.9 %collective-permute-start = (bf16[40,2048]{1,0:T(8,128)(2,1)S(1)}, bf16[40,2048]{1,0:T(8,128)(2,1)S(1)}, u32[]{:S(2)}, u32[]{:S(2)}) collective-permute-start(bf16[40,2048]{1,0:T(8,128)(2,1)S(1)} %get-tuple-element.53.refs_4_), channel_id=1, source_target_pairs={{0,16},{1,17},{2,18},{3,19},{4,20},{5,21},{6,22},{7,23},{8,24},{9,... | collective-permute-start | bytes 491528 | tf_op jit(solution)/shard_map/ppermute | solution.py:248
  6.3 7.9 %collective-permute-start.1 = (bf16[16,4096]{1,0:T(8,128)(2,1)S(1)}, bf16[16,4096]{1,0:T(8,128)(2,1)S(1)}, u32[]{:S(2)}, u32[]{:S(2)}) collective-permute-start(bf16[16,4096]{1,0:T(8,128)(2,1)S(1)} %get-tuple-element.58), channel_id=1, source_target_pairs={{0,6},{1,7},{2,4},{3,5},{4,2},{5,3},{6,0},{7,1},{8,14},{9,15},{10,... | collective-permute-start | bytes 393224 | tf_op jit(solution)/shard_map/ppermute | solution.py:205
  8.8 7.0 %collective-permute-start.2 = (bf16[16,4096]{1,0:T(8,128)(2,1)S(1)}, bf16[16,4096]{1,0:T(8,128)(2,1)S(1)}, u32[]{:S(2)}, u32[]{:S(2)}) collective-permute-start(bf16[16,4096]{1,0:T(8,128)(2,1)S(1)} %get-tuple-element.59), channel_id=1, source_target_pairs={{0,8},{1,9},{2,10},{3,11},{4,12},{5,13},{6,14},{7,15},{8,0},{9,1},... | collective-permute-start | bytes 393224 | tf_op jit(solution)/shard_map/ppermute | solution.py:205
  10.3 5.5 %collective-permute-start.3 = (bf16[16,4096]{1,0:T(8,128)(2,1)S(1)}, bf16[16,4096]{1,0:T(8,128)(2,1)S(1)}, u32[]{:S(2)}, u32[]{:S(2)}) collective-permute-start(bf16[16,4096]{1,0:T(8,128)(2,1)S(1)} %get-tuple-element.60), channel_id=1, source_target_pairs={{0,2},{1,3},{2,0},{3,1},{4,6},{5,7},{6,4},{7,5},{8,10},{9,11},{10,... | collective-permute-start | bytes 393224 | tf_op jit(solution)/shard_map/ppermute | solution.py:205
  10.9 5.0 %collective-permute-start.4 = (bf16[16,4096]{1,0:T(8,128)(2,1)S(1)}, bf16[16,4096]{1,0:T(8,128)(2,1)S(1)}, u32[]{:S(2)}, u32[]{:S(2)}) collective-permute-start(bf16[16,4096]{1,0:T(8,128)(2,1)S(1)} %get-tuple-element.61), channel_id=1, source_target_pairs={{0,4},{1,5},{2,6},{3,7},{4,0},{5,1},{6,2},{7,3},{8,12},{9,13},{10,... | collective-permute-start | bytes 393224 | tf_op jit(solution)/shard_map/ppermute | solution.py:205
  15.9 8.8 %collective-permute-start.6 = (bf16[40,4096]{1,0:T(8,128)(2,1)S(1)}, bf16[40,4096]{1,0:T(8,128)(2,1)S(1)}, u32[]{:S(2)}, u32[]{:S(2)}) collective-permute-start(bf16[40,4096]{1,0:T(8,128)(2,1)S(1)} %get-tuple-element.66), channel_id=1, source_target_pairs={{0,2},{1,3},{2,0},{3,1},{4,6},{5,7},{6,4},{7,5},{8,10},{9,11},{10,... | collective-permute-start | bytes 983048 | tf_op jit(solution)/shard_map/ppermute | solution.py:205
  17.4 7.8 %collective-permute-start.5 = (bf16[40,4096]{1,0:T(8,128)(2,1)S(1)}, bf16[40,4096]{1,0:T(8,128)(2,1)S(1)}, u32[]{:S(2)}, u32[]{:S(2)}) collective-permute-start(bf16[40,4096]{1,0:T(8,128)(2,1)S(1)} %get-tuple-element.66), channel_id=1, source_target_pairs={{0,4},{1,5},{2,6},{3,7},{4,0},{5,1},{6,2},{7,3},{8,12},{9,13},{10,... | collective-permute-start | bytes 983048 | tf_op jit(solution)/shard_map/ppermute | solution.py:205
  18.2 8.0 %collective-permute-start.7 = (bf16[40,4096]{1,0:T(8,128)(2,1)S(1)}, bf16[40,4096]{1,0:T(8,128)(2,1)S(1)}, u32[]{:S(2)}, u32[]{:S(2)}) collective-permute-start(bf16[40,4096]{1,0:T(8,128)(2,1)S(1)} %get-tuple-element.67), channel_id=1, source_target_pairs={{0,8},{1,9},{2,10},{3,11},{4,12},{5,13},{6,14},{7,15},{8,0},{9,1},... | collective-permute-start | bytes 983048 | tf_op jit(solution)/shard_map/ppermute | solution.py:205
  19.7 11.9 %collective-permute-start.8 = (bf16[640,2048]{1,0:T(8,128)(2,1)S(1)}, bf16[640,2048]{1,0:T(8,128)(2,1)S(1)}, u32[]{:S(2)}, u32[]{:S(2)}) collective-permute-start(bf16[640,2048]{1,0:T(8,128)(2,1)S(1)} %pad_maximum_fusion.1), channel_id=1, source_target_pairs={{0,1},{1,0},{2,3},{3,2},{4,5},{5,4},{6,7},{7,6},{8,9},{9,8},{10,11... | collective-permute-start | bytes 7864328 | tf_op jit(solution)/shard_map/ppermute | solution.py:205
  26.3 9.7 %collective-permute-start.12 = (bf16[24,4096]{1,0:T(8,128)(2,1)S(1)}, bf16[24,4096]{1,0:T(8,128)(2,1)S(1)}, u32[]{:S(2)}, u32[]{:S(2)}) collective-permute-start(bf16[24,4096]{1,0:T(8,128)(2,1)S(1)} %get-tuple-element.69), channel_id=1, source_target_pairs={{0,6},{1,7},{2,4},{3,5},{4,2},{5,3},{6,0},{7,1},{8,14},{9,15},{10,... | collective-permute-start | bytes 589832 | tf_op jit(solution)/shard_map/ppermute | solution.py:205
  27.7 8.2 %collective-permute-start.11 = (bf16[24,4096]{1,0:T(8,128)(2,1)S(1)}, bf16[24,4096]{1,0:T(8,128)(2,1)S(1)}, u32[]{:S(2)}, u32[]{:S(2)}) collective-permute-start(bf16[24,4096]{1,0:T(8,128)(2,1)S(1)} %get-tuple-element.69), channel_id=1, source_target_pairs={{0,2},{1,3},{2,0},{3,1},{4,6},{5,7},{6,4},{7,5},{8,10},{9,11},{10,... | collective-permute-start | bytes 589832 | tf_op jit(solution)/shard_map/ppermute | solution.py:205
  28.6 7.4 %collective-permute-start.10 = (bf16[24,4096]{1,0:T(8,128)(2,1)S(1)}, bf16[24,4096]{1,0:T(8,128)(2,1)S(1)}, u32[]{:S(2)}, u32[]{:S(2)}) collective-permute-start(bf16[24,4096]{1,0:T(8,128)(2,1)S(1)} %get-tuple-element.70), channel_id=1, source_target_pairs={{0,8},{1,9},{2,10},{3,11},{4,12},{5,13},{6,14},{7,15},{8,0},{9,1},... | collective-permute-start | bytes 589832 | tf_op jit(solution)/shard_map/ppermute | solution.py:205
  29.9 6.1 %collective-permute-start.9 = (bf16[24,4096]{1,0:T(8,128)(2,1)S(1)}, bf16[24,4096]{1,0:T(8,128)(2,1)S(1)}, u32[]{:S(2)}, u32[]{:S(2)}) collective-permute-start(bf16[24,4096]{1,0:T(8,128)(2,1)S(1)} %get-tuple-element.71), channel_id=1, source_target_pairs={{0,4},{1,5},{2,6},{3,7},{4,0},{5,1},{6,2},{7,3},{8,12},{9,13},{10,... | collective-permute-start | bytes 589832 | tf_op jit(solution)/shard_map/ppermute | solution.py:205
  39.3 8.7 %collective-permute-start.14 = (bf16[40,2048]{1,0:T(8,128)(2,1)S(1)}, bf16[40,2048]{1,0:T(8,128)(2,1)S(1)}, u32[]{:S(2)}, u32[]{:S(2)}) collective-permute-start(bf16[40,2048]{1,0:T(8,128)(2,1)S(1)} %pad_maximum_fusion.19), channel_id=1, source_target_pairs={{0,6},{1,7},{2,4},{3,5},{4,2},{5,3},{6,0},{7,1},{8,14},{9,15},{10,... | collective-permute-start | bytes 491528 | tf_op jit(solution)/shard_map/ppermute | solution.py:205
  40.8 7.1 %collective-permute-start.13 = (bf16[40,2048]{1,0:T(8,128)(2,1)S(1)}, bf16[40,2048]{1,0:T(8,128)(2,1)S(1)}, u32[]{:S(2)}, u32[]{:S(2)}) collective-permute-start(bf16[40,2048]{1,0:T(8,128)(2,1)S(1)} %get-tuple-element.76), channel_id=1, source_target_pairs={{0,2},{1,3},{2,0},{3,1},{4,6},{5,7},{6,4},{7,5},{8,10},{9,11},{10,... | collective-permute-start | bytes 491528 | tf_op jit(solution)/shard_map/ppermute | solution.py:205
  42.4 6.1 %collective-permute-start.16 = (bf16[40,2048]{1,0:T(8,128)(2,1)S(1)}, bf16[40,2048]{1,0:T(8,128)(2,1)S(1)}, u32[]{:S(2)}, u32[]{:S(2)}) collective-permute-start(bf16[40,2048]{1,0:T(8,128)(2,1)S(1)} %get-tuple-element.77), channel_id=1, source_target_pairs={{0,4},{1,5},{2,6},{3,7},{4,0},{5,1},{6,2},{7,3},{8,12},{9,13},{10,... | collective-permute-start | bytes 491528 | tf_op jit(solution)/shard_map/ppermute | solution.py:205
  43.0 6.2 %collective-permute-start.18 = (bf16[40,2048]{1,0:T(8,128)(2,1)S(1)}, bf16[40,2048]{1,0:T(8,128)(2,1)S(1)}, u32[]{:S(2)}, u32[]{:S(2)}) collective-permute-start(bf16[40,2048]{1,0:T(8,128)(2,1)S(1)} %pad_maximum_fusion.22), channel_id=1, source_target_pairs={{0,8},{1,9},{2,10},{3,11},{4,12},{5,13},{6,14},{7,15},{8,0},{9,1},... | collective-permute-start | bytes 491528 | tf_op jit(solution)/shard_map/ppermute | solution.py:205
  48.0 6.6 %collective-permute-start.15 = (bf16[40,2048]{1,0:T(8,128)(2,1)S(1)}, bf16[40,2048]{1,0:T(8,128)(2,1)S(1)}, u32[]{:S(2)}, u32[]{:S(2)}) collective-permute-start(bf16[40,2048]{1,0:T(8,128)(2,1)S(1)} %add_convert_fusion.3), channel_id=1, source_target_pairs={{0,8},{1,9},{2,10},{3,11},{4,12},{5,13},{6,14},{7,15},{8,0},{9,1},... | collective-permute-start | bytes 491528 | tf_op jit(solution)/shard_map/ppermute | solution.py:205
  48.5 6.2 %collective-permute-start.17 = (bf16[40,2048]{1,0:T(8,128)(2,1)S(1)}, bf16[40,2048]{1,0:T(8,128)(2,1)S(1)}, u32[]{:S(2)}, u32[]{:S(2)}) collective-permute-start(bf16[40,2048]{1,0:T(8,128)(2,1)S(1)} %add_convert_fusion.2), channel_id=1, source_target_pairs={{0,2},{1,3},{2,0},{3,1},{4,6},{5,7},{6,4},{7,5},{8,10},{9,11},{10,... | collective-permute-start | bytes 491528 | tf_op jit(solution)/shard_map/ppermute | solution.py:205
  49.3 5.4 %collective-permute-start.19 = (bf16[40,2048]{1,0:T(8,128)(2,1)S(1)}, bf16[40,2048]{1,0:T(8,128)(2,1)S(1)}, u32[]{:S(2)}, u32[]{:S(2)}) collective-permute-start(bf16[40,2048]{1,0:T(8,128)(2,1)S(1)} %add_convert_fusion.1), channel_id=1, source_target_pairs={{0,4},{1,5},{2,6},{3,7},{4,0},{5,1},{6,2},{7,3},{8,12},{9,13},{10,... | collective-permute-start | bytes 491528 | tf_op jit(solution)/shard_map/ppermute | solution.py:205
  52.3 7.6 %collective-permute-start.20 = (bf16[320,2048]{1,0:T(8,128)(2,1)S(1)}, bf16[320,2048]{1,0:T(8,128)(2,1)S(1)}, u32[]{:S(2)}, u32[]{:S(2)}) collective-permute-start(bf16[320,2048]{1,0:T(8,128)(2,1)S(1)} %fusion.6), channel_id=1, source_target_pairs={{0,1},{1,0},{2,3},{3,2},{4,5},{5,4},{6,7},{7,6},{8,9},{9,8},{10,11... | collective-permute-start | bytes 3932168 | tf_op jit(solution)/shard_map/ppermute | solution.py:205
  52.4 7.5 %collective-permute-start.21 = (bf16[320,2048]{1,0:T(8,128)(2,1)S(1)}, bf16[320,2048]{1,0:T(8,128)(2,1)S(1)}, u32[]{:S(2)}, u32[]{:S(2)}) collective-permute-start(bf16[320,2048]{1,0:T(8,128)(2,1)S(1)} %fusion.7), channel_id=1, source_target_pairs={{0,1},{1,0},{2,3},{3,2},{4,5},{5,4},{6,7},{7,6},{8,9},{9,8},{10,11... | collective-permute-start | bytes 3932168 | tf_op jit(solution)/shard_map/ppermute | solution.py:205
  54.8 7.9 %collective-permute-start.22 = (bf16[40,1024]{1,0:T(8,128)(2,1)S(1)}, bf16[40,1024]{1,0:T(8,128)(2,1)S(1)}, u32[]{:S(2)}, u32[]{:S(2)}) collective-permute-start(bf16[40,1024]{1,0:T(8,128)(2,1)S(1)} %pad_maximum_fusion.23), channel_id=1, source_target_pairs={{0,16},{1,17},{2,18},{3,19},{4,20},{5,21},{6,22},{7,23},{8,24},{9,... | collective-permute-start | bytes 245768 | tf_op jit(solution)/shard_map/ppermute | solution.py:248
  (1 other events, 1.7 us)

commit v19 on v18

--- a/solution.py
+++ b/solution.py
@@ -294,9 +294,9 @@
         jnp.concatenate([own_weights[part], their_weights[part]], axis=0)
         for part in (slice(0, units), slice(units, 2 * units))
     ]
-    late_far, late_zx, late_yz, late_xy = swaps(
-        [late_z, late_z, late_y, late_x],
-        (x_bit | y_bit, x_bit, z_bit, y_bit),
+    late_xy, late_far, late_yz, late_zx = swaps(
+        [late_x, late_x, late_y, late_z],
+        (y_bit, y_bit | z_bit, z_bit, x_bit),
     )
     early = activated(jnp.concatenate(early_rows, axis=0))
     early_parts = input_parts(early[3])

time: 63.8 us -> 63.1 us (0.989)
  starting transfers between devices: 32 us -> 30.2 us
  waiting for transfers between devices: 10.7 us -> 11.7 us
    ppermute x2, starting transfers between devices: 8.68 us -> 6.99 us  [shifted(): return lax.ppermute(rows, 'expert', pairs)]
    ppermute x21, waiting for transfers between devices: 10.2 us -> 11.4 us  [swap(): lax.ppermute(rows, 'expert', [(i, i ^ mask) for i in range(n_expert)])]
  transfers between devices with their start and end apart: 23 -> 23, of which waited for: 9 -> 6; matrix products, arithmetic and copies ran while one was open for 17% -> 17% of each run, Pallas kernels for 4% -> 4%
where the time goes in v19:
time: 63.1 us; the launch traced here: 62.9 us
  starting transfers between devices  30.2 us (48%)
  matrix products  11.8 us (19%)
  waiting for transfers between devices  11.7 us (19%)
  Pallas kernels  4.03 us (6%)
  other arithmetic  2.85 us (5%)
  local copies, waits for them, and re-layouts  1.21 us (2%)
  between operations  1.07 us (2%)
    ppermute x21, starting transfers between devices, swap(): lax.ppermute(rows, 'expert', [(i, i ^ mask) for i in range(n_expert)])  23.2 us
    ppermute x21, waiting for transfers between devices, swap(): lax.ppermute(rows, 'expert', [(i, i ^ mask) for i in range(n_expert)])  11.4 us
    ppermute x2, starting transfers between devices, shifted(): return lax.ppermute(rows, 'expert', pairs)  6.99 us
    dot_general x11, matrix products, contract_rows(): lax.dot_general(left, right, (((0,), (0,)), ((), ())), preferred_element_...  6.06 us
    dot_general x4, matrix products, contract_cols(): lax.dot_general(left, right, (((1,), (1,)), ((), ())), preferred_element_...  4.37 us
    pallas_call x1, Pallas kernels, stepped(): pl.pallas_call(lambda *refs: step_kernel(rows, *refs), out_shape=[jax.Sha...  2.47 us
    transpose x1, other arithmetic, shards(): whole_weights(w_in)  1.93 us
    pallas_call x1, Pallas kernels, pack(): pl.pallas_call(lambda *refs: pack_kernel(blocks, experts, *refs), out_sha...  1.56 us
  transfers between devices with their start and end apart: 23, of which 6 were waited for; matrix products, arithmetic and copies ran while one was open for 17% of the time, Pallas kernels for 4%

profile of v19, /device:TPU:0, one launch (start us, length us, event | category | flops | bytes accessed | tf_op | source)
XLA Modules:
  0.0 62.9 jit_solution(6047474095136844778)
XLA Ops:
  0.6 1.6 %shard_map.85 = (bf16[16,4096]{1,0:T(8,128)(2,1)S(1)}, bf16[24,4096]{1,0:T(8,128)(2,1)S(1)}, bf16[40,2048]{1,0:T(8,128)(2,1)S(1)}, bf16[16,64]{1,0:T(8,128)(2,1)...) custom-call(s32[1,64]{1,0:T(1,128)} %bitcast.18, ...), custom_call_target="tpu_custom_call" | custom-call | tf_op jit(solution)/shard_map/pallas_call | solution.py:124
  2.2 4.1 %collective-permute-start = (bf16[40,2048]{1,0:T(8,128)(2,1)S(1)}, bf16[40,2048]{1,0:T(8,128)(2,1)S(1)}, u32[]{:S(2)}, u32[]{:S(2)}) collective-permute-start(bf16[40,2048]{1,0:T(8,128)(2,1)S(1)} %get-tuple-element.53.refs_4_), channel_id=1, source_target_pairs={{0,16},{1,17},{2,18},{3,19},{4,20},{5,21},{6,22},{7,23},{8,24},{9,... | collective-permute-start | bytes 491528 | tf_op jit(solution)/shard_map/ppermute | solution.py:248
  6.3 2.5 %collective-permute-start.1 = (bf16[16,4096]{1,0:T(8,128)(2,1)S(1)}, bf16[16,4096]{1,0:T(8,128)(2,1)S(1)}, u32[]{:S(2)}, u32[]{:S(2)}) collective-permute-start(bf16[16,4096]{1,0:T(8,128)(2,1)S(1)} %get-tuple-element.58), channel_id=1, source_target_pairs={{0,6},{1,7},{2,4},{3,5},{4,2},{5,3},{6,0},{7,1},{8,14},{9,15},{10,... | collective-permute-start | bytes 393224 | tf_op jit(solution)/shard_map/ppermute | solution.py:205
  8.8 1.6 %collective-permute-start.2 = (bf16[16,4096]{1,0:T(8,128)(2,1)S(1)}, bf16[16,4096]{1,0:T(8,128)(2,1)S(1)}, u32[]{:S(2)}, u32[]{:S(2)}) collective-permute-start(bf16[16,4096]{1,0:T(8,128)(2,1)S(1)} %get-tuple-element.59), channel_id=1, source_target_pairs={{0,8},{1,9},{2,10},{3,11},{4,12},{5,13},{6,14},{7,15},{8,0},{9,1},... | collective-permute-start | bytes 393224 | tf_op jit(solution)/shard_map/ppermute | solution.py:205
  11.4 1.9 %convert_bitcast_fusion = bf16[320,2048]{1,0:T(8,128)(2,1)S(1)} fusion(f32[2048,320]{0,1:T(8,128)} %param.10), kind=kLoop, calls=%fused_computation.24 | loop fusion | flops 655360 | bytes 3932160 | tf_op jit(solution)/shard_map/transpose | solution.py:291
  14.2 1.5 %collective-permute-done.2 = bf16[16,4096]{1,0:T(8,128)(2,1)S(1)} collective-permute-done((bf16[16,4096]{1,0:T(8,128)(2,1)S(1)}, bf16[16,4096]{1,0:T(8,128)(2,1)S(1)}, u32[]{:S(2)}, u32[]{:S(2)}) %collective-permute-start.2) | collective-permute-done | bytes 131104 | tf_op jit(solution)/shard_map/ppermute | solution.py:205
  15.9 1.6 %collective-permute-start.6 = (bf16[40,4096]{1,0:T(8,128)(2,1)S(1)}, bf16[40,4096]{1,0:T(8,128)(2,1)S(1)}, u32[]{:S(2)}, u32[]{:S(2)}) collective-permute-start(bf16[40,4096]{1,0:T(8,128)(2,1)S(1)} %get-tuple-element.66), channel_id=1, source_target_pairs={{0,2},{1,3},{2,0},{3,1},{4,6},{5,7},{6,4},{7,5},{8,10},{9,11},{10,... | collective-permute-start | bytes 983048 | tf_op jit(solution)/shard_map/ppermute | solution.py:205
  18.2 1.4 %collective-permute-start.7 = (bf16[40,4096]{1,0:T(8,128)(2,1)S(1)}, bf16[40,4096]{1,0:T(8,128)(2,1)S(1)}, u32[]{:S(2)}, u32[]{:S(2)}) collective-permute-start(bf16[40,4096]{1,0:T(8,128)(2,1)S(1)} %get-tuple-element.67), channel_id=1, source_target_pairs={{0,8},{1,9},{2,10},{3,11},{4,12},{5,13},{6,14},{7,15},{8,0},{9,1},... | collective-permute-start | bytes 983048 | tf_op jit(solution)/shard_map/ppermute | solution.py:205
  19.8 4.9 %collective-permute-done.6 = bf16[40,4096]{1,0:T(8,128)(2,1)S(1)} collective-permute-done((bf16[40,4096]{1,0:T(8,128)(2,1)S(1)}, bf16[40,4096]{1,0:T(8,128)(2,1)S(1)}, u32[]{:S(2)}, u32[]{:S(2)}) %collective-permute-start.6) | collective-permute-done | bytes 327712 | tf_op jit(solution)/shard_map/ppermute | solution.py:205
  25.1 1.8 %collective-permute-start.12 = (bf16[24,4096]{1,0:T(8,128)(2,1)S(1)}, bf16[24,4096]{1,0:T(8,128)(2,1)S(1)}, u32[]{:S(2)}, u32[]{:S(2)}) collective-permute-start(bf16[24,4096]{1,0:T(8,128)(2,1)S(1)} %get-tuple-element.69), channel_id=1, source_target_pairs={{0,12},{1,13},{2,14},{3,15},{4,8},{5,9},{6,10},{7,11},{8,4},{9,5},... | collective-permute-start | bytes 589832 | tf_op jit(solution)/shard_map/ppermute | solution.py:205
  27.0 1.4 %collective-permute-start.10 = (bf16[24,4096]{1,0:T(8,128)(2,1)S(1)}, bf16[24,4096]{1,0:T(8,128)(2,1)S(1)}, u32[]{:S(2)}, u32[]{:S(2)}) collective-permute-start(bf16[24,4096]{1,0:T(8,128)(2,1)S(1)} %get-tuple-element.70), channel_id=1, source_target_pairs={{0,8},{1,9},{2,10},{3,11},{4,12},{5,13},{6,14},{7,15},{8,0},{9,1},... | collective-permute-start | bytes 589832 | tf_op jit(solution)/shard_map/ppermute | solution.py:205
  30.6 1.0 %fusion.18 = bf16[128,640]{1,0:T(8,128)(2,1)S(1)} fusion(bf16[320,2048]{1,0:T(8,128)(2,1)S(1)} %get-tuple-element.100, bf16[320,2048]{1,0:T(8,128)(2,1)S(1)} %convert_bitcast_fusion.1, bf16[128,4096]{1,0:T(8,128)(2,1)S(1)} %slice_dynamic-update-slice_fusion, f32[128,640]{1,0:T(8,128)S(1)} %get-tuple-element.134), kind=kOutput, calls=%fused_computation.31 | convolution fusion | flops 342507520 | bytes 3637248 | tf_op jit(solution)/shard_map/dot_general | solution.py:39
  32.3 1.8 %collective-permute-done.11 = bf16[24,4096]{1,0:T(8,128)(2,1)S(1)} collective-permute-done((bf16[24,4096]{1,0:T(8,128)(2,1)S(1)}, bf16[24,4096]{1,0:T(8,128)(2,1)S(1)}, u32[]{:S(2)}, u32[]{:S(2)}) %collective-permute-start.11) | collective-permute-done | bytes 196640 | tf_op jit(solution)/shard_map/ppermute | solution.py:205
  34.2 1.1 %collective-permute-done.10 = bf16[24,4096]{1,0:T(8,128)(2,1)S(1)} collective-permute-done((bf16[24,4096]{1,0:T(8,128)(2,1)S(1)}, bf16[24,4096]{1,0:T(8,128)(2,1)S(1)}, u32[]{:S(2)}, u32[]{:S(2)}) %collective-permute-start.10) | collective-permute-done | bytes 196640 | tf_op jit(solution)/shard_map/ppermute | solution.py:205
  35.4 1.1 %multiply_convert_fusion = (bf16[192,640]{1,0:T(8,128)(2,1)S(1)}, f32[192,640]{1,0:T(8,128)S(1)}) fusion(bf16[320,2048]{1,0:T(8,128)(2,1)S(1)} %convert_bitcast_fusion, bf16[320,2048]{1,0:T(8,128)(2,1)S(1)} %get-tuple-element.99, bf16[192,4096]{1,0:T(8,128)(2,1)S(1)} %constant_dynamic-update-slice_fusion.5), kind=kOutput, calls=%fused_computation.46 | convolution fusion | flops 509788160 | bytes 4145152 | tf_op jit(solution)/shard_map/dot_general | solution.py:39
  36.5 1.2 %fusion.15 = bf16[192,640]{1,0:T(8,128)(2,1)S(1)} fusion(bf16[320,2048]{1,0:T(8,128)(2,1)S(1)} %get-tuple-element.100, bf16[320,2048]{1,0:T(8,128)(2,1)S(1)} %convert_bitcast_fusion.1, bf16[192,4096]{1,0:T(8,128)(2,1)S(1)} %constant_dynamic-update-slice_fusion.5, f32[192,640]{1,0:T(8,128)S(1)} %get-tuple-element.132), kind=kOutput, calls=%fused_computation.28 | convolution fusion | flops 511139840 | bytes 4145152 | tf_op jit(solution)/shard_map/dot_general | solution.py:39
  38.6 1.4 %collective-permute-start.14 = (bf16[40,2048]{1,0:T(8,128)(2,1)S(1)}, bf16[40,2048]{1,0:T(8,128)(2,1)S(1)}, u32[]{:S(2)}, u32[]{:S(2)}) collective-permute-start(bf16[40,2048]{1,0:T(8,128)(2,1)S(1)} %pad_maximum_fusion.19), channel_id=1, source_target_pairs={{0,6},{1,7},{2,4},{3,5},{4,2},{5,3},{6,0},{7,1},{8,14},{9,15},{10,... | collective-permute-start | bytes 491528 | tf_op jit(solution)/shard_map/ppermute | solution.py:205
  40.6 1.7 %collective-permute-start.16 = (bf16[40,2048]{1,0:T(8,128)(2,1)S(1)}, bf16[40,2048]{1,0:T(8,128)(2,1)S(1)}, u32[]{:S(2)}, u32[]{:S(2)}) collective-permute-start(bf16[40,2048]{1,0:T(8,128)(2,1)S(1)} %get-tuple-element.77), channel_id=1, source_target_pairs={{0,4},{1,5},{2,6},{3,7},{4,0},{5,1},{6,2},{7,3},{8,12},{9,13},{10,... | collective-permute-start | bytes 491528 | tf_op jit(solution)/shard_map/ppermute | solution.py:205
  42.3 1.2 %collective-permute-start.18 = (bf16[40,2048]{1,0:T(8,128)(2,1)S(1)}, bf16[40,2048]{1,0:T(8,128)(2,1)S(1)}, u32[]{:S(2)}, u32[]{:S(2)}) collective-permute-start(bf16[40,2048]{1,0:T(8,128)(2,1)S(1)} %pad_maximum_fusion.22), channel_id=1, source_target_pairs={{0,8},{1,9},{2,10},{3,11},{4,12},{5,13},{6,14},{7,15},{8,0},{9,1},... | collective-permute-start | bytes 491528 | tf_op jit(solution)/shard_map/ppermute | solution.py:205
  46.1 2.0 %collective-permute-start.15 = (bf16[40,2048]{1,0:T(8,128)(2,1)S(1)}, bf16[40,2048]{1,0:T(8,128)(2,1)S(1)}, u32[]{:S(2)}, u32[]{:S(2)}) collective-permute-start(bf16[40,2048]{1,0:T(8,128)(2,1)S(1)} %add_convert_fusion.3), channel_id=1, source_target_pairs={{0,8},{1,9},{2,10},{3,11},{4,12},{5,13},{6,14},{7,15},{8,0},{9,1},... | collective-permute-start | bytes 491528 | tf_op jit(solution)/shard_map/ppermute | solution.py:205
  48.1 2.3 %collective-permute-start.17 = (bf16[40,2048]{1,0:T(8,128)(2,1)S(1)}, bf16[40,2048]{1,0:T(8,128)(2,1)S(1)}, u32[]{:S(2)}, u32[]{:S(2)}) collective-permute-start(bf16[40,2048]{1,0:T(8,128)(2,1)S(1)} %add_convert_fusion.2), channel_id=1, source_target_pairs={{0,2},{1,3},{2,0},{3,1},{4,6},{5,7},{6,4},{7,5},{8,10},{9,11},{10,... | collective-permute-start | bytes 491528 | tf_op jit(solution)/shard_map/ppermute | solution.py:205
  53.9 2.0 %collective-permute-done.19 = bf16[40,2048]{1,0:T(8,128)(2,1)S(1)} collective-permute-done((bf16[40,2048]{1,0:T(8,128)(2,1)S(1)}, bf16[40,2048]{1,0:T(8,128)(2,1)S(1)}, u32[]{:S(2)}, u32[]{:S(2)}) %collective-permute-start.19) | collective-permute-done | bytes 163872 | tf_op jit(solution)/shard_map/ppermute | solution.py:205
  56.0 2.9 %collective-permute-start.22 = (bf16[40,1024]{1,0:T(8,128)(2,1)S(1)}, bf16[40,1024]{1,0:T(8,128)(2,1)S(1)}, u32[]{:S(2)}, u32[]{:S(2)}) collective-permute-start(bf16[40,1024]{1,0:T(8,128)(2,1)S(1)} %pad_maximum_fusion.23), channel_id=1, source_target_pairs={{0,16},{1,17},{2,18},{3,19},{4,20},{5,21},{6,22},{7,23},{8,24},{9,... | collective-permute-start | bytes 245768 | tf_op jit(solution)/shard_map/ppermute | solution.py:248
  59.4 2.5 %shard_map.87 = (f32[320,2048]{1,0:T(8,128)}, f32[320,2048]{1,0:T(8,128)}) custom-call(f32[320,2048]{1,0:T(8,128)S(1)} %fusion.3.refs_0_, f32[320,2048]{1,0:T(8,128)S(1)} %fusion.1.refs_1_, bf16[320,2048]{1,0:T(8,128)(2,1)S(1)} %collective-permute-done.20.refs_2_, bf16[320,2048]{1,0:T(8,128)(2,1)S(1)} %collective-permute-done.21.refs_3_), custom_call_target="tpu_custom_call" | custom-call | flops 2621440 | bytes 5242880 | tf_op jit(solution)/shard_map/pallas_call | solution.py:180
  (80 shorter events, 15.4 us)
Async XLA Ops:
  0.6 12.7 %copy-start = (f32[2048,320]{0,1:T(8,128)S(1)}, f32[2048,320]{0,1:T(8,128)}, u32[]{:S(2)}) copy-start(f32[2048,320]{0,1:T(8,128)} %param.11) | copy-start | bytes 7864324
  2.2 11.9 %collective-permute-start = (bf16[40,2048]{1,0:T(8,128)(2,1)S(1)}, bf16[40,2048]{1,0:T(8,128)(2,1)S(1)}, u32[]{:S(2)}, u32[]{:S(2)}) collective-permute-start(bf16[40,2048]{1,0:T(8,128)(2,1)S(1)} %get-tuple-element.53.refs_4_), channel_id=1, source_target_pairs={{0,16},{1,17},{2,18},{3,19},{4,20},{5,21},{6,22},{7,23},{8,24},{9,... | collective-permute-start | bytes 491528 | tf_op jit(solution)/shard_map/ppermute | solution.py:248
  6.3 7.9 %collective-permute-start.1 = (bf16[16,4096]{1,0:T(8,128)(2,1)S(1)}, bf16[16,4096]{1,0:T(8,128)(2,1)S(1)}, u32[]{:S(2)}, u32[]{:S(2)}) collective-permute-start(bf16[16,4096]{1,0:T(8,128)(2,1)S(1)} %get-tuple-element.58), channel_id=1, source_target_pairs={{0,6},{1,7},{2,4},{3,5},{4,2},{5,3},{6,0},{7,1},{8,14},{9,15},{10,... | collective-permute-start | bytes 393224 | tf_op jit(solution)/shard_map/ppermute | solution.py:205
  8.8 7.0 %collective-permute-start.2 = (bf16[16,4096]{1,0:T(8,128)(2,1)S(1)}, bf16[16,4096]{1,0:T(8,128)(2,1)S(1)}, u32[]{:S(2)}, u32[]{:S(2)}) collective-permute-start(bf16[16,4096]{1,0:T(8,128)(2,1)S(1)} %get-tuple-element.59), channel_id=1, source_target_pairs={{0,8},{1,9},{2,10},{3,11},{4,12},{5,13},{6,14},{7,15},{8,0},{9,1},... | collective-permute-start | bytes 393224 | tf_op jit(solution)/shard_map/ppermute | solution.py:205
  10.3 5.5 %collective-permute-start.3 = (bf16[16,4096]{1,0:T(8,128)(2,1)S(1)}, bf16[16,4096]{1,0:T(8,128)(2,1)S(1)}, u32[]{:S(2)}, u32[]{:S(2)}) collective-permute-start(bf16[16,4096]{1,0:T(8,128)(2,1)S(1)} %get-tuple-element.60), channel_id=1, source_target_pairs={{0,2},{1,3},{2,0},{3,1},{4,6},{5,7},{6,4},{7,5},{8,10},{9,11},{10,... | collective-permute-start | bytes 393224 | tf_op jit(solution)/shard_map/ppermute | solution.py:205
  10.9 5.0 %collective-permute-start.4 = (bf16[16,4096]{1,0:T(8,128)(2,1)S(1)}, bf16[16,4096]{1,0:T(8,128)(2,1)S(1)}, u32[]{:S(2)}, u32[]{:S(2)}) collective-permute-start(bf16[16,4096]{1,0:T(8,128)(2,1)S(1)} %get-tuple-element.61), channel_id=1, source_target_pairs={{0,4},{1,5},{2,6},{3,7},{4,0},{5,1},{6,2},{7,3},{8,12},{9,13},{10,... | collective-permute-start | bytes 393224 | tf_op jit(solution)/shard_map/ppermute | solution.py:205
  15.9 8.8 %collective-permute-start.6 = (bf16[40,4096]{1,0:T(8,128)(2,1)S(1)}, bf16[40,4096]{1,0:T(8,128)(2,1)S(1)}, u32[]{:S(2)}, u32[]{:S(2)}) collective-permute-start(bf16[40,4096]{1,0:T(8,128)(2,1)S(1)} %get-tuple-element.66), channel_id=1, source_target_pairs={{0,2},{1,3},{2,0},{3,1},{4,6},{5,7},{6,4},{7,5},{8,10},{9,11},{10,... | collective-permute-start | bytes 983048 | tf_op jit(solution)/shard_map/ppermute | solution.py:205
  17.4 9.5 %collective-permute-start.5 = (bf16[40,4096]{1,0:T(8,128)(2,1)S(1)}, bf16[40,4096]{1,0:T(8,128)(2,1)S(1)}, u32[]{:S(2)}, u32[]{:S(2)}) collective-permute-start(bf16[40,4096]{1,0:T(8,128)(2,1)S(1)} %get-tuple-element.66), channel_id=1, source_target_pairs={{0,4},{1,5},{2,6},{3,7},{4,0},{5,1},{6,2},{7,3},{8,12},{9,13},{10,... | collective-permute-start | bytes 983048 | tf_op jit(solution)/shard_map/ppermute | solution.py:205
  18.2 10.2 %collective-permute-start.7 = (bf16[40,4096]{1,0:T(8,128)(2,1)S(1)}, bf16[40,4096]{1,0:T(8,128)(2,1)S(1)}, u32[]{:S(2)}, u32[]{:S(2)}) collective-permute-start(bf16[40,4096]{1,0:T(8,128)(2,1)S(1)} %get-tuple-element.67), channel_id=1, source_target_pairs={{0,8},{1,9},{2,10},{3,11},{4,12},{5,13},{6,14},{7,15},{8,0},{9,1},... | collective-permute-start | bytes 983048 | tf_op jit(solution)/shard_map/ppermute | solution.py:205
  19.7 9.7 %collective-permute-start.8 = (bf16[640,2048]{1,0:T(8,128)(2,1)S(1)}, bf16[640,2048]{1,0:T(8,128)(2,1)S(1)}, u32[]{:S(2)}, u32[]{:S(2)}) collective-permute-start(bf16[640,2048]{1,0:T(8,128)(2,1)S(1)} %pad_maximum_fusion.1), channel_id=1, source_target_pairs={{0,1},{1,0},{2,3},{3,2},{4,5},{5,4},{6,7},{7,6},{8,9},{9,8},{10,11... | collective-permute-start | bytes 7864328 | tf_op jit(solution)/shard_map/ppermute | solution.py:205
  24.8 10.5 %collective-permute-start.9 = (bf16[24,4096]{1,0:T(8,128)(2,1)S(1)}, bf16[24,4096]{1,0:T(8,128)(2,1)S(1)}, u32[]{:S(2)}, u32[]{:S(2)}) collective-permute-start(bf16[24,4096]{1,0:T(8,128)(2,1)S(1)} %get-tuple-element.69), channel_id=1, source_target_pairs={{0,4},{1,5},{2,6},{3,7},{4,0},{5,1},{6,2},{7,3},{8,12},{9,13},{10,... | collective-permute-start | bytes 589832 | tf_op jit(solution)/shard_map/ppermute | solution.py:205
  25.1 10.2 %collective-permute-start.12 = (bf16[24,4096]{1,0:T(8,128)(2,1)S(1)}, bf16[24,4096]{1,0:T(8,128)(2,1)S(1)}, u32[]{:S(2)}, u32[]{:S(2)}) collective-permute-start(bf16[24,4096]{1,0:T(8,128)(2,1)S(1)} %get-tuple-element.69), channel_id=1, source_target_pairs={{0,12},{1,13},{2,14},{3,15},{4,8},{5,9},{6,10},{7,11},{8,4},{9,5},... | collective-permute-start | bytes 589832 | tf_op jit(solution)/shard_map/ppermute | solution.py:205
  27.0 8.3 %collective-permute-start.10 = (bf16[24,4096]{1,0:T(8,128)(2,1)S(1)}, bf16[24,4096]{1,0:T(8,128)(2,1)S(1)}, u32[]{:S(2)}, u32[]{:S(2)}) collective-permute-start(bf16[24,4096]{1,0:T(8,128)(2,1)S(1)} %get-tuple-element.70), channel_id=1, source_target_pairs={{0,8},{1,9},{2,10},{3,11},{4,12},{5,13},{6,14},{7,15},{8,0},{9,1},... | collective-permute-start | bytes 589832 | tf_op jit(solution)/shard_map/ppermute | solution.py:205
  28.4 5.7 %collective-permute-start.11 = (bf16[24,4096]{1,0:T(8,128)(2,1)S(1)}, bf16[24,4096]{1,0:T(8,128)(2,1)S(1)}, u32[]{:S(2)}, u32[]{:S(2)}) collective-permute-start(bf16[24,4096]{1,0:T(8,128)(2,1)S(1)} %get-tuple-element.71), channel_id=1, source_target_pairs={{0,2},{1,3},{2,0},{3,1},{4,6},{5,7},{6,4},{7,5},{8,10},{9,11},{10,... | collective-permute-start | bytes 589832 | tf_op jit(solution)/shard_map/ppermute | solution.py:205
  38.6 7.4 %collective-permute-start.14 = (bf16[40,2048]{1,0:T(8,128)(2,1)S(1)}, bf16[40,2048]{1,0:T(8,128)(2,1)S(1)}, u32[]{:S(2)}, u32[]{:S(2)}) collective-permute-start(bf16[40,2048]{1,0:T(8,128)(2,1)S(1)} %pad_maximum_fusion.19), channel_id=1, source_target_pairs={{0,6},{1,7},{2,4},{3,5},{4,2},{5,3},{6,0},{7,1},{8,14},{9,15},{10,... | collective-permute-start | bytes 491528 | tf_op jit(solution)/shard_map/ppermute | solution.py:205
  40.0 6.0 %collective-permute-start.13 = (bf16[40,2048]{1,0:T(8,128)(2,1)S(1)}, bf16[40,2048]{1,0:T(8,128)(2,1)S(1)}, u32[]{:S(2)}, u32[]{:S(2)}) collective-permute-start(bf16[40,2048]{1,0:T(8,128)(2,1)S(1)} %get-tuple-element.76), channel_id=1, source_target_pairs={{0,2},{1,3},{2,0},{3,1},{4,6},{5,7},{6,4},{7,5},{8,10},{9,11},{10,... | collective-permute-start | bytes 491528 | tf_op jit(solution)/shard_map/ppermute | solution.py:205
  40.6 7.5 %collective-permute-start.16 = (bf16[40,2048]{1,0:T(8,128)(2,1)S(1)}, bf16[40,2048]{1,0:T(8,128)(2,1)S(1)}, u32[]{:S(2)}, u32[]{:S(2)}) collective-permute-start(bf16[40,2048]{1,0:T(8,128)(2,1)S(1)} %get-tuple-element.77), channel_id=1, source_target_pairs={{0,4},{1,5},{2,6},{3,7},{4,0},{5,1},{6,2},{7,3},{8,12},{9,13},{10,... | collective-permute-start | bytes 491528 | tf_op jit(solution)/shard_map/ppermute | solution.py:205
  42.3 8.1 %collective-permute-start.18 = (bf16[40,2048]{1,0:T(8,128)(2,1)S(1)}, bf16[40,2048]{1,0:T(8,128)(2,1)S(1)}, u32[]{:S(2)}, u32[]{:S(2)}) collective-permute-start(bf16[40,2048]{1,0:T(8,128)(2,1)S(1)} %pad_maximum_fusion.22), channel_id=1, source_target_pairs={{0,8},{1,9},{2,10},{3,11},{4,12},{5,13},{6,14},{7,15},{8,0},{9,1},... | collective-permute-start | bytes 491528 | tf_op jit(solution)/shard_map/ppermute | solution.py:205
  46.1 9.8 %collective-permute-start.15 = (bf16[40,2048]{1,0:T(8,128)(2,1)S(1)}, bf16[40,2048]{1,0:T(8,128)(2,1)S(1)}, u32[]{:S(2)}, u32[]{:S(2)}) collective-permute-start(bf16[40,2048]{1,0:T(8,128)(2,1)S(1)} %add_convert_fusion.3), channel_id=1, source_target_pairs={{0,8},{1,9},{2,10},{3,11},{4,12},{5,13},{6,14},{7,15},{8,0},{9,1},... | collective-permute-start | bytes 491528 | tf_op jit(solution)/shard_map/ppermute | solution.py:205
  48.1 7.7 %collective-permute-start.17 = (bf16[40,2048]{1,0:T(8,128)(2,1)S(1)}, bf16[40,2048]{1,0:T(8,128)(2,1)S(1)}, u32[]{:S(2)}, u32[]{:S(2)}) collective-permute-start(bf16[40,2048]{1,0:T(8,128)(2,1)S(1)} %add_convert_fusion.2), channel_id=1, source_target_pairs={{0,2},{1,3},{2,0},{3,1},{4,6},{5,7},{6,4},{7,5},{8,10},{9,11},{10,... | collective-permute-start | bytes 491528 | tf_op jit(solution)/shard_map/ppermute | solution.py:205
  50.5 5.4 %collective-permute-start.19 = (bf16[40,2048]{1,0:T(8,128)(2,1)S(1)}, bf16[40,2048]{1,0:T(8,128)(2,1)S(1)}, u32[]{:S(2)}, u32[]{:S(2)}) collective-permute-start(bf16[40,2048]{1,0:T(8,128)(2,1)S(1)} %add_convert_fusion.1), channel_id=1, source_target_pairs={{0,4},{1,5},{2,6},{3,7},{4,0},{5,1},{6,2},{7,3},{8,12},{9,13},{10,... | collective-permute-start | bytes 491528 | tf_op jit(solution)/shard_map/ppermute | solution.py:205
  51.6 7.8 %collective-permute-start.20 = (bf16[320,2048]{1,0:T(8,128)(2,1)S(1)}, bf16[320,2048]{1,0:T(8,128)(2,1)S(1)}, u32[]{:S(2)}, u32[]{:S(2)}) collective-permute-start(bf16[320,2048]{1,0:T(8,128)(2,1)S(1)} %fusion.6), channel_id=1, source_target_pairs={{0,1},{1,0},{2,3},{3,2},{4,5},{5,4},{6,7},{7,6},{8,9},{9,8},{10,11... | collective-permute-start | bytes 3932168 | tf_op jit(solution)/shard_map/ppermute | solution.py:205
  51.7 7.7 %collective-permute-start.21 = (bf16[320,2048]{1,0:T(8,128)(2,1)S(1)}, bf16[320,2048]{1,0:T(8,128)(2,1)S(1)}, u32[]{:S(2)}, u32[]{:S(2)}) collective-permute-start(bf16[320,2048]{1,0:T(8,128)(2,1)S(1)} %fusion.7), channel_id=1, source_target_pairs={{0,1},{1,0},{2,3},{3,2},{4,5},{5,4},{6,7},{7,6},{8,9},{9,8},{10,11... | collective-permute-start | bytes 3932168 | tf_op jit(solution)/shard_map/ppermute | solution.py:205
  56.0 5.9 %collective-permute-start.22 = (bf16[40,1024]{1,0:T(8,128)(2,1)S(1)}, bf16[40,1024]{1,0:T(8,128)(2,1)S(1)}, u32[]{:S(2)}, u32[]{:S(2)}) collective-permute-start(bf16[40,1024]{1,0:T(8,128)(2,1)S(1)} %pad_maximum_fusion.23), channel_id=1, source_target_pairs={{0,16},{1,17},{2,18},{3,19},{4,20},{5,21},{6,22},{7,23},{8,24},{9,... | collective-permute-start | bytes 245768 | tf_op jit(solution)/shard_map/ppermute | solution.py:248
  (1 other events, 1.7 us)

commit v20 on v19

--- a/solution.py
+++ b/solution.py
@@ -206,7 +206,7 @@
 
 
 core_bit, x_bit, y_bit, z_bit = 1, 2, 4, 8
-early_masks = (x_bit | y_bit, z_bit, x_bit, y_bit)
+early_masks = (z_bit, x_bit | y_bit, x_bit, y_bit)
 
 
 def after(values, *others):
@@ -273,7 +273,7 @@
         late_own = late_own + jnp.pad(
             side_by_side, (((s - 1) * capacity, rest - s * capacity), (0, 0))
         )
-    early_xy, early_z, early_x, early_y = after(
+    early_z, early_xy, early_x, early_y = after(
         [swap(rows, mask) for rows, mask in zip(early_copies, early_masks)], late_own
     )
     late_x, late_y, late_z = swaps(

time: 63.1 us -> 63.1 us (level)
  starting transfers between devices: 30.2 us -> 29.4 us
  waiting for transfers between devices: 11.7 us -> 12.5 us
    ppermute x21, starting transfers between devices: 23.2 us -> 22 us  [swap(): lax.ppermute(rows, 'expert', [(i, i ^ mask) for i in range(n_expert)])]
    ppermute x21, waiting for transfers between devices: 11.4 us -> 12.4 us  [swap(): lax.ppermute(rows, 'expert', [(i, i ^ mask) for i in range(n_expert)])]
  transfers between devices with their start and end apart: 23 -> 23, of which waited for: 6 -> 9; matrix products, arithmetic and copies ran while one was open for 17% -> 17% of each run, Pallas kernels for 4% -> 4%
where the time goes in v20:
time: 63.1 us; the launch traced here: 62.9 us
  starting transfers between devices  29.4 us (47%)
  waiting for transfers between devices  12.5 us (20%)
  matrix products  11.8 us (19%)
  Pallas kernels  4.03 us (6%)
  other arithmetic  2.85 us (5%)
  local copies, waits for them, and re-layouts  1.21 us (2%)
  between operations  1.05 us (2%)
    ppermute x21, starting transfers between devices, swap(): lax.ppermute(rows, 'expert', [(i, i ^ mask) for i in range(n_expert)])  22 us
    ppermute x21, waiting for transfers between devices, swap(): lax.ppermute(rows, 'expert', [(i, i ^ mask) for i in range(n_expert)])  12.4 us
    ppermute x2, starting transfers between devices, shifted(): return lax.ppermute(rows, 'expert', pairs)  7.43 us
    dot_general x11, matrix products, contract_rows(): lax.dot_general(left, right, (((0,), (0,)), ((), ())), preferred_element_...  6.05 us
    dot_general x4, matrix products, contract_cols(): lax.dot_general(left, right, (((1,), (1,)), ((), ())), preferred_element_...  4.36 us
    pallas_call x1, Pallas kernels, stepped(): pl.pallas_call(lambda *refs: step_kernel(rows, *refs), out_shape=[jax.Sha...  2.47 us
    transpose x1, other arithmetic, shards(): whole_weights(w_in)  1.93 us
    pallas_call x1, Pallas kernels, pack(): pl.pallas_call(lambda *refs: pack_kernel(blocks, experts, *refs), out_sha...  1.56 us
  transfers between devices with their start and end apart: 23, of which 9 were waited for; matrix products, arithmetic and copies ran while one was open for 17% of the time, Pallas kernels for 4%

profile of v20, /device:TPU:0, one launch (start us, length us, event | category | flops | bytes accessed | tf_op | source)
XLA Modules:
  0.0 62.9 jit_solution(15947685458523288136)
XLA Ops:
  0.6 1.6 %shard_map.85 = (bf16[16,4096]{1,0:T(8,128)(2,1)S(1)}, bf16[24,4096]{1,0:T(8,128)(2,1)S(1)}, bf16[40,2048]{1,0:T(8,128)(2,1)S(1)}, bf16[16,64]{1,0:T(8,128)(2,1)...) custom-call(s32[1,64]{1,0:T(1,128)} %bitcast.18, ...), custom_call_target="tpu_custom_call" | custom-call | tf_op jit(solution)/shard_map/pallas_call | solution.py:124
  2.2 4.1 %collective-permute-start = (bf16[40,2048]{1,0:T(8,128)(2,1)S(1)}, bf16[40,2048]{1,0:T(8,128)(2,1)S(1)}, u32[]{:S(2)}, u32[]{:S(2)}) collective-permute-start(bf16[40,2048]{1,0:T(8,128)(2,1)S(1)} %get-tuple-element.53.refs_4_), channel_id=1, source_target_pairs={{0,16},{1,17},{2,18},{3,19},{4,20},{5,21},{6,22},{7,23},{8,24},{9,... | collective-permute-start | bytes 491528 | tf_op jit(solution)/shard_map/ppermute | solution.py:248
  6.3 1.6 %collective-permute-start.1 = (bf16[16,4096]{1,0:T(8,128)(2,1)S(1)}, bf16[16,4096]{1,0:T(8,128)(2,1)S(1)}, u32[]{:S(2)}, u32[]{:S(2)}) collective-permute-start(bf16[16,4096]{1,0:T(8,128)(2,1)S(1)} %get-tuple-element.58), channel_id=1, source_target_pairs={{0,8},{1,9},{2,10},{3,11},{4,12},{5,13},{6,14},{7,15},{8,0},{9,1},... | collective-permute-start | bytes 393224 | tf_op jit(solution)/shard_map/ppermute | solution.py:205
  7.9 2.4 %collective-permute-start.2 = (bf16[16,4096]{1,0:T(8,128)(2,1)S(1)}, bf16[16,4096]{1,0:T(8,128)(2,1)S(1)}, u32[]{:S(2)}, u32[]{:S(2)}) collective-permute-start(bf16[16,4096]{1,0:T(8,128)(2,1)S(1)} %get-tuple-element.59), channel_id=1, source_target_pairs={{0,6},{1,7},{2,4},{3,5},{4,2},{5,3},{6,0},{7,1},{8,14},{9,15},{10,... | collective-permute-start | bytes 393224 | tf_op jit(solution)/shard_map/ppermute | solution.py:205
  11.4 1.9 %convert_bitcast_fusion = bf16[320,2048]{1,0:T(8,128)(2,1)S(1)} fusion(f32[2048,320]{0,1:T(8,128)} %param.10), kind=kLoop, calls=%fused_computation.24 | loop fusion | flops 655360 | bytes 3932160 | tf_op jit(solution)/shard_map/transpose | solution.py:291
  15.0 1.4 %collective-permute-done.3 = bf16[16,4096]{1,0:T(8,128)(2,1)S(1)} collective-permute-done((bf16[16,4096]{1,0:T(8,128)(2,1)S(1)}, bf16[16,4096]{1,0:T(8,128)(2,1)S(1)}, u32[]{:S(2)}, u32[]{:S(2)}) %collective-permute-start.3) | collective-permute-done | bytes 131104 | tf_op jit(solution)/shard_map/ppermute | solution.py:205
  16.5 1.5 %collective-permute-start.6 = (bf16[40,4096]{1,0:T(8,128)(2,1)S(1)}, bf16[40,4096]{1,0:T(8,128)(2,1)S(1)}, u32[]{:S(2)}, u32[]{:S(2)}) collective-permute-start(bf16[40,4096]{1,0:T(8,128)(2,1)S(1)} %get-tuple-element.66), channel_id=1, source_target_pairs={{0,2},{1,3},{2,0},{3,1},{4,6},{5,7},{6,4},{7,5},{8,10},{9,11},{10,... | collective-permute-start | bytes 983048 | tf_op jit(solution)/shard_map/ppermute | solution.py:205
  18.0 1.4 %collective-permute-start.5 = (bf16[40,4096]{1,0:T(8,128)(2,1)S(1)}, bf16[40,4096]{1,0:T(8,128)(2,1)S(1)}, u32[]{:S(2)}, u32[]{:S(2)}) collective-permute-start(bf16[40,4096]{1,0:T(8,128)(2,1)S(1)} %get-tuple-element.66), channel_id=1, source_target_pairs={{0,4},{1,5},{2,6},{3,7},{4,0},{5,1},{6,2},{7,3},{8,12},{9,13},{10,... | collective-permute-start | bytes 983048 | tf_op jit(solution)/shard_map/ppermute | solution.py:205
  20.0 4.9 %collective-permute-done.6 = bf16[40,4096]{1,0:T(8,128)(2,1)S(1)} collective-permute-done((bf16[40,4096]{1,0:T(8,128)(2,1)S(1)}, bf16[40,4096]{1,0:T(8,128)(2,1)S(1)}, u32[]{:S(2)}, u32[]{:S(2)}) %collective-permute-start.6) | collective-permute-done | bytes 327712 | tf_op jit(solution)/shard_map/ppermute | solution.py:205
  25.0 1.9 %collective-permute-start.9 = (bf16[24,4096]{1,0:T(8,128)(2,1)S(1)}, bf16[24,4096]{1,0:T(8,128)(2,1)S(1)}, u32[]{:S(2)}, u32[]{:S(2)}) collective-permute-start(bf16[24,4096]{1,0:T(8,128)(2,1)S(1)} %get-tuple-element.69), channel_id=1, source_target_pairs={{0,4},{1,5},{2,6},{3,7},{4,0},{5,1},{6,2},{7,3},{8,12},{9,13},{10,... | collective-permute-start | bytes 589832 | tf_op jit(solution)/shard_map/ppermute | solution.py:205
  27.0 1.7 %collective-permute-start.10 = (bf16[24,4096]{1,0:T(8,128)(2,1)S(1)}, bf16[24,4096]{1,0:T(8,128)(2,1)S(1)}, u32[]{:S(2)}, u32[]{:S(2)}) collective-permute-start(bf16[24,4096]{1,0:T(8,128)(2,1)S(1)} %get-tuple-element.70), channel_id=1, source_target_pairs={{0,8},{1,9},{2,10},{3,11},{4,12},{5,13},{6,14},{7,15},{8,0},{9,1},... | collective-permute-start | bytes 589832 | tf_op jit(solution)/shard_map/ppermute | solution.py:205
  28.7 1.5 %collective-permute-start.11 = (bf16[24,4096]{1,0:T(8,128)(2,1)S(1)}, bf16[24,4096]{1,0:T(8,128)(2,1)S(1)}, u32[]{:S(2)}, u32[]{:S(2)}) collective-permute-start(bf16[24,4096]{1,0:T(8,128)(2,1)S(1)} %get-tuple-element.71), channel_id=1, source_target_pairs={{0,2},{1,3},{2,0},{3,1},{4,6},{5,7},{6,4},{7,5},{8,10},{9,11},{10,... | collective-permute-start | bytes 589832 | tf_op jit(solution)/shard_map/ppermute | solution.py:205
  31.5 1.0 %fusion.18 = bf16[128,640]{1,0:T(8,128)(2,1)S(1)} fusion(bf16[320,2048]{1,0:T(8,128)(2,1)S(1)} %get-tuple-element.100, bf16[320,2048]{1,0:T(8,128)(2,1)S(1)} %convert_bitcast_fusion.1, bf16[128,4096]{1,0:T(8,128)(2,1)S(1)} %slice_dynamic-update-slice_fusion, f32[128,640]{1,0:T(8,128)S(1)} %get-tuple-element.134), kind=kOutput, calls=%fused_computation.31 | convolution fusion | flops 342507520 | bytes 3637248 | tf_op jit(solution)/shard_map/dot_general | solution.py:39
  33.2 1.2 %collective-permute-done.11 = bf16[24,4096]{1,0:T(8,128)(2,1)S(1)} collective-permute-done((bf16[24,4096]{1,0:T(8,128)(2,1)S(1)}, bf16[24,4096]{1,0:T(8,128)(2,1)S(1)}, u32[]{:S(2)}, u32[]{:S(2)}) %collective-permute-start.11) | collective-permute-done | bytes 196640 | tf_op jit(solution)/shard_map/ppermute | solution.py:205
  34.4 1.7 %collective-permute-done.10 = bf16[24,4096]{1,0:T(8,128)(2,1)S(1)} collective-permute-done((bf16[24,4096]{1,0:T(8,128)(2,1)S(1)}, bf16[24,4096]{1,0:T(8,128)(2,1)S(1)}, u32[]{:S(2)}, u32[]{:S(2)}) %collective-permute-start.10) | collective-permute-done | bytes 196640 | tf_op jit(solution)/shard_map/ppermute | solution.py:205
  36.2 1.1 %multiply_convert_fusion = (bf16[192,640]{1,0:T(8,128)(2,1)S(1)}, f32[192,640]{1,0:T(8,128)S(1)}) fusion(bf16[320,2048]{1,0:T(8,128)(2,1)S(1)} %convert_bitcast_fusion, bf16[320,2048]{1,0:T(8,128)(2,1)S(1)} %get-tuple-element.99, bf16[192,4096]{1,0:T(8,128)(2,1)S(1)} %constant_dynamic-update-slice_fusion.5), kind=kOutput, calls=%fused_computation.46 | convolution fusion | flops 509788160 | bytes 4145152 | tf_op jit(solution)/shard_map/dot_general | solution.py:39
  37.3 1.2 %fusion.15 = bf16[192,640]{1,0:T(8,128)(2,1)S(1)} fusion(bf16[320,2048]{1,0:T(8,128)(2,1)S(1)} %get-tuple-element.100, bf16[320,2048]{1,0:T(8,128)(2,1)S(1)} %convert_bitcast_fusion.1, bf16[192,4096]{1,0:T(8,128)(2,1)S(1)} %constant_dynamic-update-slice_fusion.5, f32[192,640]{1,0:T(8,128)S(1)} %get-tuple-element.132), kind=kOutput, calls=%fused_computation.28 | convolution fusion | flops 511139840 | bytes 4145152 | tf_op jit(solution)/shard_map/dot_general | solution.py:39
  39.4 2.2 %collective-permute-start.14 = (bf16[40,2048]{1,0:T(8,128)(2,1)S(1)}, bf16[40,2048]{1,0:T(8,128)(2,1)S(1)}, u32[]{:S(2)}, u32[]{:S(2)}) collective-permute-start(bf16[40,2048]{1,0:T(8,128)(2,1)S(1)} %pad_maximum_fusion.19), channel_id=1, source_target_pairs={{0,6},{1,7},{2,4},{3,5},{4,2},{5,3},{6,0},{7,1},{8,14},{9,15},{10,... | collective-permute-start | bytes 491528 | tf_op jit(solution)/shard_map/ppermute | solution.py:205
  46.1 1.2 %collective-permute-done.13 = bf16[40,2048]{1,0:T(8,128)(2,1)S(1)} collective-permute-done((bf16[40,2048]{1,0:T(8,128)(2,1)S(1)}, bf16[40,2048]{1,0:T(8,128)(2,1)S(1)}, u32[]{:S(2)}, u32[]{:S(2)}) %collective-permute-start.13) | collective-permute-done | bytes 163872 | tf_op jit(solution)/shard_map/ppermute | solution.py:205
  47.9 2.1 %collective-permute-start.17 = (bf16[40,2048]{1,0:T(8,128)(2,1)S(1)}, bf16[40,2048]{1,0:T(8,128)(2,1)S(1)}, u32[]{:S(2)}, u32[]{:S(2)}) collective-permute-start(bf16[40,2048]{1,0:T(8,128)(2,1)S(1)} %add_convert_fusion.2), channel_id=1, source_target_pairs={{0,2},{1,3},{2,0},{3,1},{4,6},{5,7},{6,4},{7,5},{8,10},{9,11},{10,... | collective-permute-start | bytes 491528 | tf_op jit(solution)/shard_map/ppermute | solution.py:205
  50.0 1.0 %collective-permute-start.19 = (bf16[40,2048]{1,0:T(8,128)(2,1)S(1)}, bf16[40,2048]{1,0:T(8,128)(2,1)S(1)}, u32[]{:S(2)}, u32[]{:S(2)}) collective-permute-start(bf16[40,2048]{1,0:T(8,128)(2,1)S(1)} %add_convert_fusion.1), channel_id=1, source_target_pairs={{0,4},{1,5},{2,6},{3,7},{4,0},{5,1},{6,2},{7,3},{8,12},{9,13},{10,... | collective-permute-start | bytes 491528 | tf_op jit(solution)/shard_map/ppermute | solution.py:205
  54.4 1.0 %collective-permute-done.19 = bf16[40,2048]{1,0:T(8,128)(2,1)S(1)} collective-permute-done((bf16[40,2048]{1,0:T(8,128)(2,1)S(1)}, bf16[40,2048]{1,0:T(8,128)(2,1)S(1)}, u32[]{:S(2)}, u32[]{:S(2)}) %collective-permute-start.19) | collective-permute-done | bytes 163872 | tf_op jit(solution)/shard_map/ppermute | solution.py:205
  55.6 3.3 %collective-permute-start.22 = (bf16[40,1024]{1,0:T(8,128)(2,1)S(1)}, bf16[40,1024]{1,0:T(8,128)(2,1)S(1)}, u32[]{:S(2)}, u32[]{:S(2)}) collective-permute-start(bf16[40,1024]{1,0:T(8,128)(2,1)S(1)} %pad_maximum_fusion.23), channel_id=1, source_target_pairs={{0,16},{1,17},{2,18},{3,19},{4,20},{5,21},{6,22},{7,23},{8,24},{9,... | collective-permute-start | bytes 245768 | tf_op jit(solution)/shard_map/ppermute | solution.py:248
  59.4 2.5 %shard_map.87 = (f32[320,2048]{1,0:T(8,128)}, f32[320,2048]{1,0:T(8,128)}) custom-call(f32[320,2048]{1,0:T(8,128)S(1)} %fusion.3.refs_0_, f32[320,2048]{1,0:T(8,128)S(1)} %fusion.1.refs_1_, bf16[320,2048]{1,0:T(8,128)(2,1)S(1)} %collective-permute-done.20.refs_2_, bf16[320,2048]{1,0:T(8,128)(2,1)S(1)} %collective-permute-done.21.refs_3_), custom_call_target="tpu_custom_call" | custom-call | flops 2621440 | bytes 5242880 | tf_op jit(solution)/shard_map/pallas_call | solution.py:180
  (80 shorter events, 16.3 us)
Async XLA Ops:
  0.6 12.7 %copy-start = (f32[2048,320]{0,1:T(8,128)S(1)}, f32[2048,320]{0,1:T(8,128)}, u32[]{:S(2)}) copy-start(f32[2048,320]{0,1:T(8,128)} %param.11) | copy-start | bytes 7864324
  2.2 11.8 %collective-permute-start = (bf16[40,2048]{1,0:T(8,128)(2,1)S(1)}, bf16[40,2048]{1,0:T(8,128)(2,1)S(1)}, u32[]{:S(2)}, u32[]{:S(2)}) collective-permute-start(bf16[40,2048]{1,0:T(8,128)(2,1)S(1)} %get-tuple-element.53.refs_4_), channel_id=1, source_target_pairs={{0,16},{1,17},{2,18},{3,19},{4,20},{5,21},{6,22},{7,23},{8,24},{9,... | collective-permute-start | bytes 491528 | tf_op jit(solution)/shard_map/ppermute | solution.py:248
  6.3 7.8 %collective-permute-start.1 = (bf16[16,4096]{1,0:T(8,128)(2,1)S(1)}, bf16[16,4096]{1,0:T(8,128)(2,1)S(1)}, u32[]{:S(2)}, u32[]{:S(2)}) collective-permute-start(bf16[16,4096]{1,0:T(8,128)(2,1)S(1)} %get-tuple-element.58), channel_id=1, source_target_pairs={{0,8},{1,9},{2,10},{3,11},{4,12},{5,13},{6,14},{7,15},{8,0},{9,1},... | collective-permute-start | bytes 393224 | tf_op jit(solution)/shard_map/ppermute | solution.py:205
  7.9 7.1 %collective-permute-start.2 = (bf16[16,4096]{1,0:T(8,128)(2,1)S(1)}, bf16[16,4096]{1,0:T(8,128)(2,1)S(1)}, u32[]{:S(2)}, u32[]{:S(2)}) collective-permute-start(bf16[16,4096]{1,0:T(8,128)(2,1)S(1)} %get-tuple-element.59), channel_id=1, source_target_pairs={{0,6},{1,7},{2,4},{3,5},{4,2},{5,3},{6,0},{7,1},{8,14},{9,15},{10,... | collective-permute-start | bytes 393224 | tf_op jit(solution)/shard_map/ppermute | solution.py:205
  10.3 6.0 %collective-permute-start.3 = (bf16[16,4096]{1,0:T(8,128)(2,1)S(1)}, bf16[16,4096]{1,0:T(8,128)(2,1)S(1)}, u32[]{:S(2)}, u32[]{:S(2)}) collective-permute-start(bf16[16,4096]{1,0:T(8,128)(2,1)S(1)} %get-tuple-element.60), channel_id=1, source_target_pairs={{0,2},{1,3},{2,0},{3,1},{4,6},{5,7},{6,4},{7,5},{8,10},{9,11},{10,... | collective-permute-start | bytes 393224 | tf_op jit(solution)/shard_map/ppermute | solution.py:205
  10.9 5.5 %collective-permute-start.4 = (bf16[16,4096]{1,0:T(8,128)(2,1)S(1)}, bf16[16,4096]{1,0:T(8,128)(2,1)S(1)}, u32[]{:S(2)}, u32[]{:S(2)}) collective-permute-start(bf16[16,4096]{1,0:T(8,128)(2,1)S(1)} %get-tuple-element.61), channel_id=1, source_target_pairs={{0,4},{1,5},{2,6},{3,7},{4,0},{5,1},{6,2},{7,3},{8,12},{9,13},{10,... | collective-permute-start | bytes 393224 | tf_op jit(solution)/shard_map/ppermute | solution.py:205
  16.5 8.5 %collective-permute-start.6 = (bf16[40,4096]{1,0:T(8,128)(2,1)S(1)}, bf16[40,4096]{1,0:T(8,128)(2,1)S(1)}, u32[]{:S(2)}, u32[]{:S(2)}) collective-permute-start(bf16[40,4096]{1,0:T(8,128)(2,1)S(1)} %get-tuple-element.66), channel_id=1, source_target_pairs={{0,2},{1,3},{2,0},{3,1},{4,6},{5,7},{6,4},{7,5},{8,10},{9,11},{10,... | collective-permute-start | bytes 983048 | tf_op jit(solution)/shard_map/ppermute | solution.py:205
  18.0 8.9 %collective-permute-start.5 = (bf16[40,4096]{1,0:T(8,128)(2,1)S(1)}, bf16[40,4096]{1,0:T(8,128)(2,1)S(1)}, u32[]{:S(2)}, u32[]{:S(2)}) collective-permute-start(bf16[40,4096]{1,0:T(8,128)(2,1)S(1)} %get-tuple-element.66), channel_id=1, source_target_pairs={{0,4},{1,5},{2,6},{3,7},{4,0},{5,1},{6,2},{7,3},{8,12},{9,13},{10,... | collective-permute-start | bytes 983048 | tf_op jit(solution)/shard_map/ppermute | solution.py:205
  19.4 9.2 %collective-permute-start.7 = (bf16[40,4096]{1,0:T(8,128)(2,1)S(1)}, bf16[40,4096]{1,0:T(8,128)(2,1)S(1)}, u32[]{:S(2)}, u32[]{:S(2)}) collective-permute-start(bf16[40,4096]{1,0:T(8,128)(2,1)S(1)} %get-tuple-element.67), channel_id=1, source_target_pairs={{0,8},{1,9},{2,10},{3,11},{4,12},{5,13},{6,14},{7,15},{8,0},{9,1},... | collective-permute-start | bytes 983048 | tf_op jit(solution)/shard_map/ppermute | solution.py:205
  19.9 10.3 %collective-permute-start.8 = (bf16[640,2048]{1,0:T(8,128)(2,1)S(1)}, bf16[640,2048]{1,0:T(8,128)(2,1)S(1)}, u32[]{:S(2)}, u32[]{:S(2)}) collective-permute-start(bf16[640,2048]{1,0:T(8,128)(2,1)S(1)} %pad_maximum_fusion.1), channel_id=1, source_target_pairs={{0,1},{1,0},{2,3},{3,2},{4,5},{5,4},{6,7},{7,6},{8,9},{9,8},{10,11... | collective-permute-start | bytes 7864328 | tf_op jit(solution)/shard_map/ppermute | solution.py:205
  25.0 11.1 %collective-permute-start.9 = (bf16[24,4096]{1,0:T(8,128)(2,1)S(1)}, bf16[24,4096]{1,0:T(8,128)(2,1)S(1)}, u32[]{:S(2)}, u32[]{:S(2)}) collective-permute-start(bf16[24,4096]{1,0:T(8,128)(2,1)S(1)} %get-tuple-element.69), channel_id=1, source_target_pairs={{0,4},{1,5},{2,6},{3,7},{4,0},{5,1},{6,2},{7,3},{8,12},{9,13},{10,... | collective-permute-start | bytes 589832 | tf_op jit(solution)/shard_map/ppermute | solution.py:205
  26.8 9.3 %collective-permute-start.12 = (bf16[24,4096]{1,0:T(8,128)(2,1)S(1)}, bf16[24,4096]{1,0:T(8,128)(2,1)S(1)}, u32[]{:S(2)}, u32[]{:S(2)}) collective-permute-start(bf16[24,4096]{1,0:T(8,128)(2,1)S(1)} %get-tuple-element.69), channel_id=1, source_target_pairs={{0,12},{1,13},{2,14},{3,15},{4,8},{5,9},{6,10},{7,11},{8,4},{9,5},... | collective-permute-start | bytes 589832 | tf_op jit(solution)/shard_map/ppermute | solution.py:205
  27.0 9.2 %collective-permute-start.10 = (bf16[24,4096]{1,0:T(8,128)(2,1)S(1)}, bf16[24,4096]{1,0:T(8,128)(2,1)S(1)}, u32[]{:S(2)}, u32[]{:S(2)}) collective-permute-start(bf16[24,4096]{1,0:T(8,128)(2,1)S(1)} %get-tuple-element.70), channel_id=1, source_target_pairs={{0,8},{1,9},{2,10},{3,11},{4,12},{5,13},{6,14},{7,15},{8,0},{9,1},... | collective-permute-start | bytes 589832 | tf_op jit(solution)/shard_map/ppermute | solution.py:205
  28.7 5.7 %collective-permute-start.11 = (bf16[24,4096]{1,0:T(8,128)(2,1)S(1)}, bf16[24,4096]{1,0:T(8,128)(2,1)S(1)}, u32[]{:S(2)}, u32[]{:S(2)}) collective-permute-start(bf16[24,4096]{1,0:T(8,128)(2,1)S(1)} %get-tuple-element.71), channel_id=1, source_target_pairs={{0,2},{1,3},{2,0},{3,1},{4,6},{5,7},{6,4},{7,5},{8,10},{9,11},{10,... | collective-permute-start | bytes 589832 | tf_op jit(solution)/shard_map/ppermute | solution.py:205
  39.4 7.8 %collective-permute-start.14 = (bf16[40,2048]{1,0:T(8,128)(2,1)S(1)}, bf16[40,2048]{1,0:T(8,128)(2,1)S(1)}, u32[]{:S(2)}, u32[]{:S(2)}) collective-permute-start(bf16[40,2048]{1,0:T(8,128)(2,1)S(1)} %pad_maximum_fusion.19), channel_id=1, source_target_pairs={{0,6},{1,7},{2,4},{3,5},{4,2},{5,3},{6,0},{7,1},{8,14},{9,15},{10,... | collective-permute-start | bytes 491528 | tf_op jit(solution)/shard_map/ppermute | solution.py:205
  41.7 5.6 %collective-permute-start.13 = (bf16[40,2048]{1,0:T(8,128)(2,1)S(1)}, bf16[40,2048]{1,0:T(8,128)(2,1)S(1)}, u32[]{:S(2)}, u32[]{:S(2)}) collective-permute-start(bf16[40,2048]{1,0:T(8,128)(2,1)S(1)} %get-tuple-element.76), channel_id=1, source_target_pairs={{0,2},{1,3},{2,0},{3,1},{4,6},{5,7},{6,4},{7,5},{8,10},{9,11},{10,... | collective-permute-start | bytes 491528 | tf_op jit(solution)/shard_map/ppermute | solution.py:205
  42.3 5.5 %collective-permute-start.16 = (bf16[40,2048]{1,0:T(8,128)(2,1)S(1)}, bf16[40,2048]{1,0:T(8,128)(2,1)S(1)}, u32[]{:S(2)}, u32[]{:S(2)}) collective-permute-start(bf16[40,2048]{1,0:T(8,128)(2,1)S(1)} %get-tuple-element.77), channel_id=1, source_target_pairs={{0,4},{1,5},{2,6},{3,7},{4,0},{5,1},{6,2},{7,3},{8,12},{9,13},{10,... | collective-permute-start | bytes 491528 | tf_op jit(solution)/shard_map/ppermute | solution.py:205
  43.1 6.9 %collective-permute-start.18 = (bf16[40,2048]{1,0:T(8,128)(2,1)S(1)}, bf16[40,2048]{1,0:T(8,128)(2,1)S(1)}, u32[]{:S(2)}, u32[]{:S(2)}) collective-permute-start(bf16[40,2048]{1,0:T(8,128)(2,1)S(1)} %pad_maximum_fusion.22), channel_id=1, source_target_pairs={{0,8},{1,9},{2,10},{3,11},{4,12},{5,13},{6,14},{7,15},{8,0},{9,1},... | collective-permute-start | bytes 491528 | tf_op jit(solution)/shard_map/ppermute | solution.py:205
  47.4 8.1 %collective-permute-start.15 = (bf16[40,2048]{1,0:T(8,128)(2,1)S(1)}, bf16[40,2048]{1,0:T(8,128)(2,1)S(1)}, u32[]{:S(2)}, u32[]{:S(2)}) collective-permute-start(bf16[40,2048]{1,0:T(8,128)(2,1)S(1)} %add_convert_fusion.3), channel_id=1, source_target_pairs={{0,8},{1,9},{2,10},{3,11},{4,12},{5,13},{6,14},{7,15},{8,0},{9,1},... | collective-permute-start | bytes 491528 | tf_op jit(solution)/shard_map/ppermute | solution.py:205
  47.9 7.5 %collective-permute-start.17 = (bf16[40,2048]{1,0:T(8,128)(2,1)S(1)}, bf16[40,2048]{1,0:T(8,128)(2,1)S(1)}, u32[]{:S(2)}, u32[]{:S(2)}) collective-permute-start(bf16[40,2048]{1,0:T(8,128)(2,1)S(1)} %add_convert_fusion.2), channel_id=1, source_target_pairs={{0,2},{1,3},{2,0},{3,1},{4,6},{5,7},{6,4},{7,5},{8,10},{9,11},{10,... | collective-permute-start | bytes 491528 | tf_op jit(solution)/shard_map/ppermute | solution.py:205
  50.0 5.4 %collective-permute-start.19 = (bf16[40,2048]{1,0:T(8,128)(2,1)S(1)}, bf16[40,2048]{1,0:T(8,128)(2,1)S(1)}, u32[]{:S(2)}, u32[]{:S(2)}) collective-permute-start(bf16[40,2048]{1,0:T(8,128)(2,1)S(1)} %add_convert_fusion.1), channel_id=1, source_target_pairs={{0,4},{1,5},{2,6},{3,7},{4,0},{5,1},{6,2},{7,3},{8,12},{9,13},{10,... | collective-permute-start | bytes 491528 | tf_op jit(solution)/shard_map/ppermute | solution.py:205
  52.1 7.3 %collective-permute-start.20 = (bf16[320,2048]{1,0:T(8,128)(2,1)S(1)}, bf16[320,2048]{1,0:T(8,128)(2,1)S(1)}, u32[]{:S(2)}, u32[]{:S(2)}) collective-permute-start(bf16[320,2048]{1,0:T(8,128)(2,1)S(1)} %fusion.6), channel_id=1, source_target_pairs={{0,1},{1,0},{2,3},{3,2},{4,5},{5,4},{6,7},{7,6},{8,9},{9,8},{10,11... | collective-permute-start | bytes 3932168 | tf_op jit(solution)/shard_map/ppermute | solution.py:205
  52.2 7.2 %collective-permute-start.21 = (bf16[320,2048]{1,0:T(8,128)(2,1)S(1)}, bf16[320,2048]{1,0:T(8,128)(2,1)S(1)}, u32[]{:S(2)}, u32[]{:S(2)}) collective-permute-start(bf16[320,2048]{1,0:T(8,128)(2,1)S(1)} %fusion.7), channel_id=1, source_target_pairs={{0,1},{1,0},{2,3},{3,2},{4,5},{5,4},{6,7},{7,6},{8,9},{9,8},{10,11... | collective-permute-start | bytes 3932168 | tf_op jit(solution)/shard_map/ppermute | solution.py:205
  55.6 6.3 %collective-permute-start.22 = (bf16[40,1024]{1,0:T(8,128)(2,1)S(1)}, bf16[40,1024]{1,0:T(8,128)(2,1)S(1)}, u32[]{:S(2)}, u32[]{:S(2)}) collective-permute-start(bf16[40,1024]{1,0:T(8,128)(2,1)S(1)} %pad_maximum_fusion.23), channel_id=1, source_target_pairs={{0,16},{1,17},{2,18},{3,19},{4,20},{5,21},{6,22},{7,23},{8,24},{9,... | collective-permute-start | bytes 245768 | tf_op jit(solution)/shard_map/ppermute | solution.py:248
  (1 other events, 1.7 us)

commit v21 on v19

--- a/solution.py
+++ b/solution.py
@@ -156,6 +156,39 @@
     return lax.all_gather(shard.astype(jnp.bfloat16), "dp", axis=0, tiled=True)
 
 
+def expert_kernel(scale_in, scale_out, rows_ref, in_ref, out_ref, hidden_ref, pre_ref, parts_ref):
+    width = in_ref.shape[1]
+    pre_act = contract_cols(rows_ref[:, :width], in_ref[...]) * scale_in
+    hidden_ref[...] = gelu_value(pre_act).astype(jnp.bfloat16)
+    hidden_grad = contract_cols(rows_ref[:, width:], out_ref[...]) * scale_out
+    pre_grad = (hidden_grad * gelu_slope(pre_act)).astype(jnp.bfloat16)
+    pre_ref[...] = pre_grad
+    for start in range(0, width, 512):
+        columns = slice(start, start + 512)
+        parts = jnp.dot(pre_grad, in_ref[:, columns], preferred_element_type=jnp.float32)
+        parts_ref[:, columns] = (parts * scale_in).astype(jnp.bfloat16)
+
+
+def worked(rows, weights_in, weights_out, scale_in, scale_out):
+    count, (units, width) = rows.shape[0], weights_in.shape
+    whole = pl.BlockSpec(memory_space=pltpu.VMEM)
+    return pl.pallas_call(
+        lambda *refs: expert_kernel(scale_in, scale_out, *refs),
+        out_shape=[
+            jax.ShapeDtypeStruct((count, columns), jnp.bfloat16)
+            for columns in (units, units, width)
+        ],
+        in_specs=[whole] * 3,
+        out_specs=[whole] * 3,
+        compiler_params=pltpu.CompilerParams(vmem_limit_bytes=20 * 1024 * 1024),
+        cost_estimate=pl.CostEstimate(
+            flops=6 * count * units * width,
+            bytes_accessed=4 * units * width,
+            transcendentals=count * units,
+        ),
+    )(rows, weights_in, weights_out)
+
+
 def step_kernel(rows, *refs):
     *refs, done_ref, sems = refs
     count = len(refs) // 3
@@ -302,8 +335,9 @@
     early_parts = input_parts(early[3])
     late_far = after([late_xy, late_yz, late_zx, late_far], early_parts)
     late_rows = [late_own, late_x, late_y, late_z, *late_far]
-    later = activated(jnp.concatenate(late_rows, axis=0))
-    late_parts = input_parts(later[3])
+    late_rows = jnp.concatenate(late_rows, axis=0)
+    hidden, pre_grad, late_parts = worked(late_rows, weights_in, weights_out, scale_in, scale_out)
+    later = [late_rows[:, :width], late_rows[:, width:], hidden, pre_grad]
     parts = [
         jnp.concatenate(pair, axis=0)
         for pair in zip(split_rows(early_parts, first), split_rows(late_parts, rest))

time: 63.1 us -> 62.6 us (level)
  matrix products: 11.8 us -> 8.74 us
  Pallas kernels: 4.03 us -> 6.64 us
  other arithmetic: 2.85 us -> 3.59 us
  waiting for transfers between devices: 11.7 us -> 11 us
    pallas_call x0 -> x1, Pallas kernels: none -> 2.6 us  [worked(): pl.pallas_call(lambda *refs: expert_kernel(scale_in, scale_out, *refs), o...]
    dot_general x4 -> x2, matrix products: 4.37 us -> 2.07 us  [contract_cols(): lax.dot_general(left, right, (((1,), (1,)), ((), ())), preferred_element_...]
    concatenate x0 -> x1, other arithmetic: none -> 0.87 us  [shards(): jnp.concatenate([own_weights[part], their_weights[part]], axis=0)]
    ppermute x21, waiting for transfers between devices: 11.4 us -> 10.6 us  [swap(): lax.ppermute(rows, 'expert', [(i, i ^ mask) for i in range(n_expert)])]
    dot_general x2 -> x1, matrix products: 1.4 us -> 0.6 us  [input_parts(): jnp.dot(pre_grad, weights_in, preferred_element_type=jnp.float32) * scale_in]
  transfers between devices with their start and end apart: 23 -> 23, of which waited for: 6 -> 7; matrix products, arithmetic and copies ran while one was open for 17% -> 19% of each run, Pallas kernels for 4% -> 4%
where the time goes in v21:
time: 62.6 us; the launch traced here: 62.4 us
  starting transfers between devices  30.2 us (48%)
  waiting for transfers between devices  11 us (18%)
  matrix products  8.74 us (14%)
  Pallas kernels  6.64 us (11%)
  other arithmetic  3.59 us (6%)
  local copies, waits for them, and re-layouts  1.17 us (2%)
  between operations  1.04 us (2%)
    ppermute x21, starting transfers between devices, swap(): lax.ppermute(rows, 'expert', [(i, i ^ mask) for i in range(n_expert)])  23.2 us
    ppermute x21, waiting for transfers between devices, swap(): lax.ppermute(rows, 'expert', [(i, i ^ mask) for i in range(n_expert)])  10.6 us
    ppermute x2, starting transfers between devices, shifted(): return lax.ppermute(rows, 'expert', pairs)  7.03 us
    dot_general x11, matrix products, contract_rows(): lax.dot_general(left, right, (((0,), (0,)), ((), ())), preferred_element_...  6.07 us
    pallas_call x1, Pallas kernels, worked(): pl.pallas_call(lambda *refs: expert_kernel(scale_in, scale_out, *refs), o...  2.6 us
    pallas_call x1, Pallas kernels, stepped(): pl.pallas_call(lambda *refs: step_kernel(rows, *refs), out_shape=[jax.Sha...  2.47 us
    dot_general x2, matrix products, contract_cols(): lax.dot_general(left, right, (((1,), (1,)), ((), ())), preferred_element_...  2.07 us
    transpose x1, other arithmetic, shards(): whole_weights(w_in)  1.93 us
  transfers between devices with their start and end apart: 23, of which 7 were waited for; matrix products, arithmetic and copies ran while one was open for 19% of the time, Pallas kernels for 4%

profile of v21, /device:TPU:0, one launch (start us, length us, event | category | flops | bytes accessed | tf_op | source)
XLA Modules:
  0.0 62.4 jit_solution(5884613219318270590)
XLA Ops:
  0.6 1.6 %shard_map.85 = (bf16[16,4096]{1,0:T(8,128)(2,1)S(1)}, bf16[24,4096]{1,0:T(8,128)(2,1)S(1)}, bf16[40,2048]{1,0:T(8,128)(2,1)S(1)}, bf16[16,64]{1,0:T(8,128)(2,1)...) custom-call(s32[1,64]{1,0:T(1,128)} %bitcast.17, ...), custom_call_target="tpu_custom_call" | custom-call | tf_op jit(solution)/shard_map/pallas_call | solution.py:124
  2.2 4.1 %collective-permute-start = (bf16[40,2048]{1,0:T(8,128)(2,1)S(1)}, bf16[40,2048]{1,0:T(8,128)(2,1)S(1)}, u32[]{:S(2)}, u32[]{:S(2)}) collective-permute-start(bf16[40,2048]{1,0:T(8,128)(2,1)S(1)} %get-tuple-element.56.refs_4_), channel_id=1, source_target_pairs={{0,16},{1,17},{2,18},{3,19},{4,20},{5,21},{6,22},{7,23},{8,24},{9,... | collective-permute-start | bytes 491528 | tf_op jit(solution)/shard_map/ppermute | solution.py:281
  6.3 2.5 %collective-permute-start.1 = (bf16[16,4096]{1,0:T(8,128)(2,1)S(1)}, bf16[16,4096]{1,0:T(8,128)(2,1)S(1)}, u32[]{:S(2)}, u32[]{:S(2)}) collective-permute-start(bf16[16,4096]{1,0:T(8,128)(2,1)S(1)} %get-tuple-element.61), channel_id=1, source_target_pairs={{0,6},{1,7},{2,4},{3,5},{4,2},{5,3},{6,0},{7,1},{8,14},{9,15},{10,... | collective-permute-start | bytes 393224 | tf_op jit(solution)/shard_map/ppermute | solution.py:238
  8.8 1.6 %collective-permute-start.2 = (bf16[16,4096]{1,0:T(8,128)(2,1)S(1)}, bf16[16,4096]{1,0:T(8,128)(2,1)S(1)}, u32[]{:S(2)}, u32[]{:S(2)}) collective-permute-start(bf16[16,4096]{1,0:T(8,128)(2,1)S(1)} %get-tuple-element.62), channel_id=1, source_target_pairs={{0,8},{1,9},{2,10},{3,11},{4,12},{5,13},{6,14},{7,15},{8,0},{9,1},... | collective-permute-start | bytes 393224 | tf_op jit(solution)/shard_map/ppermute | solution.py:238
  11.4 1.9 %convert_bitcast_fusion = bf16[320,2048]{1,0:T(8,128)(2,1)S(1)} fusion(f32[2048,320]{0,1:T(8,128)} %param.10), kind=kLoop, calls=%fused_computation.20 | loop fusion | flops 655360 | bytes 3932160 | tf_op jit(solution)/shard_map/transpose | solution.py:324
  14.2 1.6 %collective-permute-done.2 = bf16[16,4096]{1,0:T(8,128)(2,1)S(1)} collective-permute-done((bf16[16,4096]{1,0:T(8,128)(2,1)S(1)}, bf16[16,4096]{1,0:T(8,128)(2,1)S(1)}, u32[]{:S(2)}, u32[]{:S(2)}) %collective-permute-start.2) | collective-permute-done | bytes 131104 | tf_op jit(solution)/shard_map/ppermute | solution.py:238
  15.9 1.6 %collective-permute-start.6 = (bf16[40,4096]{1,0:T(8,128)(2,1)S(1)}, bf16[40,4096]{1,0:T(8,128)(2,1)S(1)}, u32[]{:S(2)}, u32[]{:S(2)}) collective-permute-start(bf16[40,4096]{1,0:T(8,128)(2,1)S(1)} %get-tuple-element.69), channel_id=1, source_target_pairs={{0,2},{1,3},{2,0},{3,1},{4,6},{5,7},{6,4},{7,5},{8,10},{9,11},{10,... | collective-permute-start | bytes 983048 | tf_op jit(solution)/shard_map/ppermute | solution.py:238
  18.4 1.4 %collective-permute-start.7 = (bf16[40,4096]{1,0:T(8,128)(2,1)S(1)}, bf16[40,4096]{1,0:T(8,128)(2,1)S(1)}, u32[]{:S(2)}, u32[]{:S(2)}) collective-permute-start(bf16[40,4096]{1,0:T(8,128)(2,1)S(1)} %get-tuple-element.70), channel_id=1, source_target_pairs={{0,8},{1,9},{2,10},{3,11},{4,12},{5,13},{6,14},{7,15},{8,0},{9,1},... | collective-permute-start | bytes 983048 | tf_op jit(solution)/shard_map/ppermute | solution.py:238
  19.8 4.9 %collective-permute-done.6 = bf16[40,4096]{1,0:T(8,128)(2,1)S(1)} collective-permute-done((bf16[40,4096]{1,0:T(8,128)(2,1)S(1)}, bf16[40,4096]{1,0:T(8,128)(2,1)S(1)}, u32[]{:S(2)}, u32[]{:S(2)}) %collective-permute-start.6) | collective-permute-done | bytes 327712 | tf_op jit(solution)/shard_map/ppermute | solution.py:238
  25.2 1.8 %collective-permute-start.12 = (bf16[24,4096]{1,0:T(8,128)(2,1)S(1)}, bf16[24,4096]{1,0:T(8,128)(2,1)S(1)}, u32[]{:S(2)}, u32[]{:S(2)}) collective-permute-start(bf16[24,4096]{1,0:T(8,128)(2,1)S(1)} %get-tuple-element.72), channel_id=1, source_target_pairs={{0,12},{1,13},{2,14},{3,15},{4,8},{5,9},{6,10},{7,11},{8,4},{9,5},... | collective-permute-start | bytes 589832 | tf_op jit(solution)/shard_map/ppermute | solution.py:238
  27.0 1.4 %collective-permute-start.10 = (bf16[24,4096]{1,0:T(8,128)(2,1)S(1)}, bf16[24,4096]{1,0:T(8,128)(2,1)S(1)}, u32[]{:S(2)}, u32[]{:S(2)}) collective-permute-start(bf16[24,4096]{1,0:T(8,128)(2,1)S(1)} %get-tuple-element.73), channel_id=1, source_target_pairs={{0,8},{1,9},{2,10},{3,11},{4,12},{5,13},{6,14},{7,15},{8,0},{9,1},... | collective-permute-start | bytes 589832 | tf_op jit(solution)/shard_map/ppermute | solution.py:238
  29.6 1.0 %multiply_convert_fusion = (bf16[128,640]{1,0:T(8,128)(2,1)S(1)}, f32[128,640]{1,0:T(8,128)S(1)}) fusion(bf16[320,2048]{1,0:T(8,128)(2,1)S(1)} %convert_bitcast_fusion, bf16[320,2048]{1,0:T(8,128)(2,1)S(1)} %get-tuple-element.106, bf16[128,4096]{1,0:T(8,128)(2,1)S(1)} %slice_dynamic-update-slice_fusion), kind=kOutput, calls=%fused_computation.52 | convolution fusion | flops 341606400 | bytes 3637248 | tf_op jit(solution)/shard_map/dot_general | solution.py:39
  30.6 1.1 %fusion.11 = bf16[128,640]{1,0:T(8,128)(2,1)S(1)} fusion(bf16[128,4096]{1,0:T(8,128)(2,1)S(1)} %slice_dynamic-update-slice_fusion, f32[128,640]{1,0:T(8,128)S(1)} %get-tuple-element.138, bf16[320,2048]{1,0:T(8,128)(2,1)S(1)} %get-tuple-element.105, bf16[320,2048]{1,0:T(8,128)(2,1)S(1)} %convert_bitcast_fusion.1), kind=kOutput, calls=%fused_computation.24 | convolution fusion | flops 342507520 | bytes 3637248 | tf_op jit(solution)/shard_map/dot_general | solution.py:39
  33.2 1.0 %collective-permute-done.11 = bf16[24,4096]{1,0:T(8,128)(2,1)S(1)} collective-permute-done((bf16[24,4096]{1,0:T(8,128)(2,1)S(1)}, bf16[24,4096]{1,0:T(8,128)(2,1)S(1)}, u32[]{:S(2)}, u32[]{:S(2)}) %collective-permute-start.11) | collective-permute-done | bytes 196640 | tf_op jit(solution)/shard_map/ppermute | solution.py:238
  34.2 1.1 %collective-permute-done.10 = bf16[24,4096]{1,0:T(8,128)(2,1)S(1)} collective-permute-done((bf16[24,4096]{1,0:T(8,128)(2,1)S(1)}, bf16[24,4096]{1,0:T(8,128)(2,1)S(1)}, u32[]{:S(2)}, u32[]{:S(2)}) %collective-permute-start.10) | collective-permute-done | bytes 196640 | tf_op jit(solution)/shard_map/ppermute | solution.py:238
  35.4 2.6 %shard_map.87 = (bf16[192,640]{1,0:T(8,128)(2,1)S(1)}, bf16[192,640]{1,0:T(8,128)(2,1)S(1)}, bf16[192,2048]{1,0:T(8,128)(2,1)S(1)}) custom-call(bf16[192,4096]{1,0:T(8,128)(2,1)S(1)} %constant_dynamic-update-slice_fusion.5.refs_0_, bf16[640,2048]{1,0:T(8,128)(2,1)S(1)} %get-tuple-element.139.refs_1_, bf16[640,2048]{1,0:T(8,128)(2,1)S(1)} %get-tuple-element.140.refs_2_), custom_call_target="tpu_custom_call" | custom-call | flops 1509949440 | bytes 5242880 | tf_op jit(solution)/shard_map/pallas_call | solution.py:175
  38.1 1.4 %collective-permute-start.14 = (bf16[40,2048]{1,0:T(8,128)(2,1)S(1)}, bf16[40,2048]{1,0:T(8,128)(2,1)S(1)}, u32[]{:S(2)}, u32[]{:S(2)}) collective-permute-start(bf16[40,2048]{1,0:T(8,128)(2,1)S(1)} %pad_maximum_fusion.5), channel_id=1, source_target_pairs={{0,6},{1,7},{2,4},{3,5},{4,2},{5,3},{6,0},{7,1},{8,14},{9,15},{10,... | collective-permute-start | bytes 491528 | tf_op jit(solution)/shard_map/ppermute | solution.py:238
  40.1 1.7 %collective-permute-start.16 = (bf16[40,2048]{1,0:T(8,128)(2,1)S(1)}, bf16[40,2048]{1,0:T(8,128)(2,1)S(1)}, u32[]{:S(2)}, u32[]{:S(2)}) collective-permute-start(bf16[40,2048]{1,0:T(8,128)(2,1)S(1)} %pad_maximum_fusion.7), channel_id=1, source_target_pairs={{0,4},{1,5},{2,6},{3,7},{4,0},{5,1},{6,2},{7,3},{8,12},{9,13},{10,... | collective-permute-start | bytes 491528 | tf_op jit(solution)/shard_map/ppermute | solution.py:238
  41.8 1.3 %collective-permute-start.18 = (bf16[40,2048]{1,0:T(8,128)(2,1)S(1)}, bf16[40,2048]{1,0:T(8,128)(2,1)S(1)}, u32[]{:S(2)}, u32[]{:S(2)}) collective-permute-start(bf16[40,2048]{1,0:T(8,128)(2,1)S(1)} %pad_maximum_fusion.8), channel_id=1, source_target_pairs={{0,8},{1,9},{2,10},{3,11},{4,12},{5,13},{6,14},{7,15},{8,0},{9,1},... | collective-permute-start | bytes 491528 | tf_op jit(solution)/shard_map/ppermute | solution.py:238
  45.8 1.5 %collective-permute-start.15 = (bf16[40,2048]{1,0:T(8,128)(2,1)S(1)}, bf16[40,2048]{1,0:T(8,128)(2,1)S(1)}, u32[]{:S(2)}, u32[]{:S(2)}) collective-permute-start(bf16[40,2048]{1,0:T(8,128)(2,1)S(1)} %add_convert_fusion.3), channel_id=1, source_target_pairs={{0,8},{1,9},{2,10},{3,11},{4,12},{5,13},{6,14},{7,15},{8,0},{9,1},... | collective-permute-start | bytes 491528 | tf_op jit(solution)/shard_map/ppermute | solution.py:238
  47.3 2.5 %collective-permute-start.17 = (bf16[40,2048]{1,0:T(8,128)(2,1)S(1)}, bf16[40,2048]{1,0:T(8,128)(2,1)S(1)}, u32[]{:S(2)}, u32[]{:S(2)}) collective-permute-start(bf16[40,2048]{1,0:T(8,128)(2,1)S(1)} %add_convert_fusion.2), channel_id=1, source_target_pairs={{0,2},{1,3},{2,0},{3,1},{4,6},{5,7},{6,4},{7,5},{8,10},{9,11},{10,... | collective-permute-start | bytes 491528 | tf_op jit(solution)/shard_map/ppermute | solution.py:238
  53.4 2.0 %collective-permute-done.19 = bf16[40,2048]{1,0:T(8,128)(2,1)S(1)} collective-permute-done((bf16[40,2048]{1,0:T(8,128)(2,1)S(1)}, bf16[40,2048]{1,0:T(8,128)(2,1)S(1)}, u32[]{:S(2)}, u32[]{:S(2)}) %collective-permute-start.19) | collective-permute-done | bytes 163872 | tf_op jit(solution)/shard_map/ppermute | solution.py:238
  55.5 2.9 %collective-permute-start.22 = (bf16[40,1024]{1,0:T(8,128)(2,1)S(1)}, bf16[40,1024]{1,0:T(8,128)(2,1)S(1)}, u32[]{:S(2)}, u32[]{:S(2)}) collective-permute-start(bf16[40,1024]{1,0:T(8,128)(2,1)S(1)} %pad_maximum_fusion.9), channel_id=1, source_target_pairs={{0,16},{1,17},{2,18},{3,19},{4,20},{5,21},{6,22},{7,23},{8,24},{9,... | collective-permute-start | bytes 245768 | tf_op jit(solution)/shard_map/ppermute | solution.py:281
  58.9 2.5 %shard_map.88 = (f32[320,2048]{1,0:T(8,128)}, f32[320,2048]{1,0:T(8,128)}) custom-call(f32[320,2048]{1,0:T(8,128)S(1)} %fusion.3.refs_0_, f32[320,2048]{1,0:T(8,128)S(1)} %fusion.1.refs_1_, bf16[320,2048]{1,0:T(8,128)(2,1)S(1)} %collective-permute-done.20.refs_2_, bf16[320,2048]{1,0:T(8,128)(2,1)S(1)} %collective-permute-done.21.refs_3_), custom_call_target="tpu_custom_call" | custom-call | flops 2621440 | bytes 5242880 | tf_op jit(solution)/shard_map/pallas_call | solution.py:213
  (80 shorter events, 14.4 us)
Async XLA Ops:
  0.6 12.7 %copy-start = (f32[2048,320]{0,1:T(8,128)S(1)}, f32[2048,320]{0,1:T(8,128)}, u32[]{:S(2)}) copy-start(f32[2048,320]{0,1:T(8,128)} %param.11) | copy-start | bytes 7864324
  2.2 11.9 %collective-permute-start = (bf16[40,2048]{1,0:T(8,128)(2,1)S(1)}, bf16[40,2048]{1,0:T(8,128)(2,1)S(1)}, u32[]{:S(2)}, u32[]{:S(2)}) collective-permute-start(bf16[40,2048]{1,0:T(8,128)(2,1)S(1)} %get-tuple-element.56.refs_4_), channel_id=1, source_target_pairs={{0,16},{1,17},{2,18},{3,19},{4,20},{5,21},{6,22},{7,23},{8,24},{9,... | collective-permute-start | bytes 491528 | tf_op jit(solution)/shard_map/ppermute | solution.py:281
  6.3 7.9 %collective-permute-start.1 = (bf16[16,4096]{1,0:T(8,128)(2,1)S(1)}, bf16[16,4096]{1,0:T(8,128)(2,1)S(1)}, u32[]{:S(2)}, u32[]{:S(2)}) collective-permute-start(bf16[16,4096]{1,0:T(8,128)(2,1)S(1)} %get-tuple-element.61), channel_id=1, source_target_pairs={{0,6},{1,7},{2,4},{3,5},{4,2},{5,3},{6,0},{7,1},{8,14},{9,15},{10,... | collective-permute-start | bytes 393224 | tf_op jit(solution)/shard_map/ppermute | solution.py:238
  8.8 7.0 %collective-permute-start.2 = (bf16[16,4096]{1,0:T(8,128)(2,1)S(1)}, bf16[16,4096]{1,0:T(8,128)(2,1)S(1)}, u32[]{:S(2)}, u32[]{:S(2)}) collective-permute-start(bf16[16,4096]{1,0:T(8,128)(2,1)S(1)} %get-tuple-element.62), channel_id=1, source_target_pairs={{0,8},{1,9},{2,10},{3,11},{4,12},{5,13},{6,14},{7,15},{8,0},{9,1},... | collective-permute-start | bytes 393224 | tf_op jit(solution)/shard_map/ppermute | solution.py:238
  10.3 5.4 %collective-permute-start.3 = (bf16[16,4096]{1,0:T(8,128)(2,1)S(1)}, bf16[16,4096]{1,0:T(8,128)(2,1)S(1)}, u32[]{:S(2)}, u32[]{:S(2)}) collective-permute-start(bf16[16,4096]{1,0:T(8,128)(2,1)S(1)} %get-tuple-element.63), channel_id=1, source_target_pairs={{0,2},{1,3},{2,0},{3,1},{4,6},{5,7},{6,4},{7,5},{8,10},{9,11},{10,... | collective-permute-start | bytes 393224 | tf_op jit(solution)/shard_map/ppermute | solution.py:238
  10.9 5.0 %collective-permute-start.4 = (bf16[16,4096]{1,0:T(8,128)(2,1)S(1)}, bf16[16,4096]{1,0:T(8,128)(2,1)S(1)}, u32[]{:S(2)}, u32[]{:S(2)}) collective-permute-start(bf16[16,4096]{1,0:T(8,128)(2,1)S(1)} %get-tuple-element.64), channel_id=1, source_target_pairs={{0,4},{1,5},{2,6},{3,7},{4,0},{5,1},{6,2},{7,3},{8,12},{9,13},{10,... | collective-permute-start | bytes 393224 | tf_op jit(solution)/shard_map/ppermute | solution.py:238
  15.9 8.8 %collective-permute-start.6 = (bf16[40,4096]{1,0:T(8,128)(2,1)S(1)}, bf16[40,4096]{1,0:T(8,128)(2,1)S(1)}, u32[]{:S(2)}, u32[]{:S(2)}) collective-permute-start(bf16[40,4096]{1,0:T(8,128)(2,1)S(1)} %get-tuple-element.69), channel_id=1, source_target_pairs={{0,2},{1,3},{2,0},{3,1},{4,6},{5,7},{6,4},{7,5},{8,10},{9,11},{10,... | collective-permute-start | bytes 983048 | tf_op jit(solution)/shard_map/ppermute | solution.py:238
  17.5 9.4 %collective-permute-start.5 = (bf16[40,4096]{1,0:T(8,128)(2,1)S(1)}, bf16[40,4096]{1,0:T(8,128)(2,1)S(1)}, u32[]{:S(2)}, u32[]{:S(2)}) collective-permute-start(bf16[40,4096]{1,0:T(8,128)(2,1)S(1)} %get-tuple-element.69), channel_id=1, source_target_pairs={{0,4},{1,5},{2,6},{3,7},{4,0},{5,1},{6,2},{7,3},{8,12},{9,13},{10,... | collective-permute-start | bytes 983048 | tf_op jit(solution)/shard_map/ppermute | solution.py:238
  18.4 10.0 %collective-permute-start.7 = (bf16[40,4096]{1,0:T(8,128)(2,1)S(1)}, bf16[40,4096]{1,0:T(8,128)(2,1)S(1)}, u32[]{:S(2)}, u32[]{:S(2)}) collective-permute-start(bf16[40,4096]{1,0:T(8,128)(2,1)S(1)} %get-tuple-element.70), channel_id=1, source_target_pairs={{0,8},{1,9},{2,10},{3,11},{4,12},{5,13},{6,14},{7,15},{8,0},{9,1},... | collective-permute-start | bytes 983048 | tf_op jit(solution)/shard_map/ppermute | solution.py:238
  19.8 9.6 %collective-permute-start.8 = (bf16[640,2048]{1,0:T(8,128)(2,1)S(1)}, bf16[640,2048]{1,0:T(8,128)(2,1)S(1)}, u32[]{:S(2)}, u32[]{:S(2)}) collective-permute-start(bf16[640,2048]{1,0:T(8,128)(2,1)S(1)} %pad_maximum_fusion.1), channel_id=1, source_target_pairs={{0,1},{1,0},{2,3},{3,2},{4,5},{5,4},{6,7},{7,6},{8,9},{9,8},{10,11... | collective-permute-start | bytes 7864328 | tf_op jit(solution)/shard_map/ppermute | solution.py:238
  24.8 10.5 %collective-permute-start.9 = (bf16[24,4096]{1,0:T(8,128)(2,1)S(1)}, bf16[24,4096]{1,0:T(8,128)(2,1)S(1)}, u32[]{:S(2)}, u32[]{:S(2)}) collective-permute-start(bf16[24,4096]{1,0:T(8,128)(2,1)S(1)} %get-tuple-element.72), channel_id=1, source_target_pairs={{0,4},{1,5},{2,6},{3,7},{4,0},{5,1},{6,2},{7,3},{8,12},{9,13},{10,... | collective-permute-start | bytes 589832 | tf_op jit(solution)/shard_map/ppermute | solution.py:238
  25.2 10.1 %collective-permute-start.12 = (bf16[24,4096]{1,0:T(8,128)(2,1)S(1)}, bf16[24,4096]{1,0:T(8,128)(2,1)S(1)}, u32[]{:S(2)}, u32[]{:S(2)}) collective-permute-start(bf16[24,4096]{1,0:T(8,128)(2,1)S(1)} %get-tuple-element.72), channel_id=1, source_target_pairs={{0,12},{1,13},{2,14},{3,15},{4,8},{5,9},{6,10},{7,11},{8,4},{9,5},... | collective-permute-start | bytes 589832 | tf_op jit(solution)/shard_map/ppermute | solution.py:238
  27.0 8.3 %collective-permute-start.10 = (bf16[24,4096]{1,0:T(8,128)(2,1)S(1)}, bf16[24,4096]{1,0:T(8,128)(2,1)S(1)}, u32[]{:S(2)}, u32[]{:S(2)}) collective-permute-start(bf16[24,4096]{1,0:T(8,128)(2,1)S(1)} %get-tuple-element.73), channel_id=1, source_target_pairs={{0,8},{1,9},{2,10},{3,11},{4,12},{5,13},{6,14},{7,15},{8,0},{9,1},... | collective-permute-start | bytes 589832 | tf_op jit(solution)/shard_map/ppermute | solution.py:238
  28.4 5.7 %collective-permute-start.11 = (bf16[24,4096]{1,0:T(8,128)(2,1)S(1)}, bf16[24,4096]{1,0:T(8,128)(2,1)S(1)}, u32[]{:S(2)}, u32[]{:S(2)}) collective-permute-start(bf16[24,4096]{1,0:T(8,128)(2,1)S(1)} %get-tuple-element.74), channel_id=1, source_target_pairs={{0,2},{1,3},{2,0},{3,1},{4,6},{5,7},{6,4},{7,5},{8,10},{9,11},{10,... | collective-permute-start | bytes 589832 | tf_op jit(solution)/shard_map/ppermute | solution.py:238
  38.1 7.6 %collective-permute-start.14 = (bf16[40,2048]{1,0:T(8,128)(2,1)S(1)}, bf16[40,2048]{1,0:T(8,128)(2,1)S(1)}, u32[]{:S(2)}, u32[]{:S(2)}) collective-permute-start(bf16[40,2048]{1,0:T(8,128)(2,1)S(1)} %pad_maximum_fusion.5), channel_id=1, source_target_pairs={{0,6},{1,7},{2,4},{3,5},{4,2},{5,3},{6,0},{7,1},{8,14},{9,15},{10,... | collective-permute-start | bytes 491528 | tf_op jit(solution)/shard_map/ppermute | solution.py:238
  39.5 6.2 %collective-permute-start.13 = (bf16[40,2048]{1,0:T(8,128)(2,1)S(1)}, bf16[40,2048]{1,0:T(8,128)(2,1)S(1)}, u32[]{:S(2)}, u32[]{:S(2)}) collective-permute-start(bf16[40,2048]{1,0:T(8,128)(2,1)S(1)} %pad_maximum_fusion.6), channel_id=1, source_target_pairs={{0,2},{1,3},{2,0},{3,1},{4,6},{5,7},{6,4},{7,5},{8,10},{9,11},{10,... | collective-permute-start | bytes 491528 | tf_op jit(solution)/shard_map/ppermute | solution.py:238
  40.1 7.2 %collective-permute-start.16 = (bf16[40,2048]{1,0:T(8,128)(2,1)S(1)}, bf16[40,2048]{1,0:T(8,128)(2,1)S(1)}, u32[]{:S(2)}, u32[]{:S(2)}) collective-permute-start(bf16[40,2048]{1,0:T(8,128)(2,1)S(1)} %pad_maximum_fusion.7), channel_id=1, source_target_pairs={{0,4},{1,5},{2,6},{3,7},{4,0},{5,1},{6,2},{7,3},{8,12},{9,13},{10,... | collective-permute-start | bytes 491528 | tf_op jit(solution)/shard_map/ppermute | solution.py:238
  41.8 8.1 %collective-permute-start.18 = (bf16[40,2048]{1,0:T(8,128)(2,1)S(1)}, bf16[40,2048]{1,0:T(8,128)(2,1)S(1)}, u32[]{:S(2)}, u32[]{:S(2)}) collective-permute-start(bf16[40,2048]{1,0:T(8,128)(2,1)S(1)} %pad_maximum_fusion.8), channel_id=1, source_target_pairs={{0,8},{1,9},{2,10},{3,11},{4,12},{5,13},{6,14},{7,15},{8,0},{9,1},... | collective-permute-start | bytes 491528 | tf_op jit(solution)/shard_map/ppermute | solution.py:238
  45.8 9.6 %collective-permute-start.15 = (bf16[40,2048]{1,0:T(8,128)(2,1)S(1)}, bf16[40,2048]{1,0:T(8,128)(2,1)S(1)}, u32[]{:S(2)}, u32[]{:S(2)}) collective-permute-start(bf16[40,2048]{1,0:T(8,128)(2,1)S(1)} %add_convert_fusion.3), channel_id=1, source_target_pairs={{0,8},{1,9},{2,10},{3,11},{4,12},{5,13},{6,14},{7,15},{8,0},{9,1},... | collective-permute-start | bytes 491528 | tf_op jit(solution)/shard_map/ppermute | solution.py:238
  47.3 8.0 %collective-permute-start.17 = (bf16[40,2048]{1,0:T(8,128)(2,1)S(1)}, bf16[40,2048]{1,0:T(8,128)(2,1)S(1)}, u32[]{:S(2)}, u32[]{:S(2)}) collective-permute-start(bf16[40,2048]{1,0:T(8,128)(2,1)S(1)} %add_convert_fusion.2), channel_id=1, source_target_pairs={{0,2},{1,3},{2,0},{3,1},{4,6},{5,7},{6,4},{7,5},{8,10},{9,11},{10,... | collective-permute-start | bytes 491528 | tf_op jit(solution)/shard_map/ppermute | solution.py:238
  49.9 5.4 %collective-permute-start.19 = (bf16[40,2048]{1,0:T(8,128)(2,1)S(1)}, bf16[40,2048]{1,0:T(8,128)(2,1)S(1)}, u32[]{:S(2)}, u32[]{:S(2)}) collective-permute-start(bf16[40,2048]{1,0:T(8,128)(2,1)S(1)} %add_convert_fusion.1), channel_id=1, source_target_pairs={{0,4},{1,5},{2,6},{3,7},{4,0},{5,1},{6,2},{7,3},{8,12},{9,13},{10,... | collective-permute-start | bytes 491528 | tf_op jit(solution)/shard_map/ppermute | solution.py:238
  51.1 7.8 %collective-permute-start.20 = (bf16[320,2048]{1,0:T(8,128)(2,1)S(1)}, bf16[320,2048]{1,0:T(8,128)(2,1)S(1)}, u32[]{:S(2)}, u32[]{:S(2)}) collective-permute-start(bf16[320,2048]{1,0:T(8,128)(2,1)S(1)} %fusion.6), channel_id=1, source_target_pairs={{0,1},{1,0},{2,3},{3,2},{4,5},{5,4},{6,7},{7,6},{8,9},{9,8},{10,11... | collective-permute-start | bytes 3932168 | tf_op jit(solution)/shard_map/ppermute | solution.py:238
  51.2 7.8 %collective-permute-start.21 = (bf16[320,2048]{1,0:T(8,128)(2,1)S(1)}, bf16[320,2048]{1,0:T(8,128)(2,1)S(1)}, u32[]{:S(2)}, u32[]{:S(2)}) collective-permute-start(bf16[320,2048]{1,0:T(8,128)(2,1)S(1)} %fusion.7), channel_id=1, source_target_pairs={{0,1},{1,0},{2,3},{3,2},{4,5},{5,4},{6,7},{7,6},{8,9},{9,8},{10,11... | collective-permute-start | bytes 3932168 | tf_op jit(solution)/shard_map/ppermute | solution.py:238
  55.5 5.9 %collective-permute-start.22 = (bf16[40,1024]{1,0:T(8,128)(2,1)S(1)}, bf16[40,1024]{1,0:T(8,128)(2,1)S(1)}, u32[]{:S(2)}, u32[]{:S(2)}) collective-permute-start(bf16[40,1024]{1,0:T(8,128)(2,1)S(1)} %pad_maximum_fusion.9), channel_id=1, source_target_pairs={{0,16},{1,17},{2,18},{3,19},{4,20},{5,21},{6,22},{7,23},{8,24},{9,... | collective-permute-start | bytes 245768 | tf_op jit(solution)/shard_map/ppermute | solution.py:281
  (1 other events, 1.7 us)

commit v22 on v21

--- a/solution.py
+++ b/solution.py
@@ -343,9 +343,9 @@
         for pair in zip(split_rows(early_parts, first), split_rows(late_parts, rest))
     ]
     own, sum_x, sum_y, sum_z, sum_xy, sum_yz, sum_zx, sum_far = parts
-    back = chain([sum_far, sum_zx, sum_xy, sum_yz])
-    far, zx, xy, yz = [
-        swap(rows, mask) for rows, mask in zip(back, (x_bit | y_bit, x_bit, y_bit, z_bit))
+    back = chain([sum_far, sum_zx, sum_yz, sum_xy])
+    far, zx, yz, xy = [
+        swap(rows, mask) for rows, mask in zip(back, (y_bit | z_bit, x_bit, z_bit, y_bit))
     ]
 
     def gradients(part, awaited):
@@ -371,7 +371,7 @@
     else:
         new_weights = [weights.T for weights in stepped(mine, shares)]
     near = swaps(
-        [total(sum_z, zx, far), total(sum_x, xy), total(sum_y, yz)], (z_bit, x_bit, y_bit)
+        [total(sum_z, zx), total(sum_y, yz), total(sum_x, xy, far)], (z_bit, y_bit, x_bit)
     )
     sums = total(own, *near)
     early_sum, late_sum = sums[:first], sums[first:]

time: 62.6 us -> 62.2 us (level)
  starting transfers between devices: 30.2 us -> 29.5 us
    ppermute x21, starting transfers between devices: 23.2 us -> 21.9 us  [swap(): lax.ppermute(rows, 'expert', [(i, i ^ mask) for i in range(n_expert)])]
  transfers between devices with their start and end apart: 23 -> 23, of which waited for: 7 -> 9; matrix products, arithmetic and copies ran while one was open for 19% -> 19% of each run, Pallas kernels for 4% -> 4%
where the time goes in v22:
time: 62.2 us; the launch traced here: 62 us
  starting transfers between devices  29.5 us (47%)
  waiting for transfers between devices  11.4 us (18%)
  matrix products  8.73 us (14%)
  Pallas kernels  6.64 us (11%)
  other arithmetic  3.58 us (6%)
  local copies, waits for them, and re-layouts  1.17 us (2%)
  between operations  1.03 us (2%)
    ppermute x21, starting transfers between devices, swap(): lax.ppermute(rows, 'expert', [(i, i ^ mask) for i in range(n_expert)])  21.9 us
    ppermute x21, waiting for transfers between devices, swap(): lax.ppermute(rows, 'expert', [(i, i ^ mask) for i in range(n_expert)])  11 us
    ppermute x2, starting transfers between devices, shifted(): return lax.ppermute(rows, 'expert', pairs)  7.58 us
    dot_general x11, matrix products, contract_rows(): lax.dot_general(left, right, (((0,), (0,)), ((), ())), preferred_element_...  6.05 us
    pallas_call x1, Pallas kernels, worked(): pl.pallas_call(lambda *refs: expert_kernel(scale_in, scale_out, *refs), o...  2.6 us
    pallas_call x1, Pallas kernels, stepped(): pl.pallas_call(lambda *refs: step_kernel(rows, *refs), out_shape=[jax.Sha...  2.47 us
    dot_general x2, matrix products, contract_cols(): lax.dot_general(left, right, (((1,), (1,)), ((), ())), preferred_element_...  2.07 us
    transpose x1, other arithmetic, shards(): whole_weights(w_in)  1.93 us
  transfers between devices with their start and end apart: 23, of which 9 were waited for; matrix products, arithmetic and copies ran while one was open for 19% of the time, Pallas kernels for 4%

profile of v22, /device:TPU:0, one launch (start us, length us, event | category | flops | bytes accessed | tf_op | source)
XLA Modules:
  0.0 62.0 jit_solution(13636379705398567295)
XLA Ops:
  0.6 1.6 %shard_map.85 = (bf16[16,4096]{1,0:T(8,128)(2,1)S(1)}, bf16[24,4096]{1,0:T(8,128)(2,1)S(1)}, bf16[40,2048]{1,0:T(8,128)(2,1)S(1)}, bf16[16,64]{1,0:T(8,128)(2,1)...) custom-call(s32[1,64]{1,0:T(1,128)} %bitcast.17, ...), custom_call_target="tpu_custom_call" | custom-call | tf_op jit(solution)/shard_map/pallas_call | solution.py:124
  2.2 4.1 %collective-permute-start = (bf16[40,2048]{1,0:T(8,128)(2,1)S(1)}, bf16[40,2048]{1,0:T(8,128)(2,1)S(1)}, u32[]{:S(2)}, u32[]{:S(2)}) collective-permute-start(bf16[40,2048]{1,0:T(8,128)(2,1)S(1)} %get-tuple-element.56.refs_4_), channel_id=1, source_target_pairs={{0,16},{1,17},{2,18},{3,19},{4,20},{5,21},{6,22},{7,23},{8,24},{9,... | collective-permute-start | bytes 491528 | tf_op jit(solution)/shard_map/ppermute | solution.py:281
  6.3 2.5 %collective-permute-start.1 = (bf16[16,4096]{1,0:T(8,128)(2,1)S(1)}, bf16[16,4096]{1,0:T(8,128)(2,1)S(1)}, u32[]{:S(2)}, u32[]{:S(2)}) collective-permute-start(bf16[16,4096]{1,0:T(8,128)(2,1)S(1)} %get-tuple-element.61), channel_id=1, source_target_pairs={{0,6},{1,7},{2,4},{3,5},{4,2},{5,3},{6,0},{7,1},{8,14},{9,15},{10,... | collective-permute-start | bytes 393224 | tf_op jit(solution)/shard_map/ppermute | solution.py:238
  8.8 1.6 %collective-permute-start.2 = (bf16[16,4096]{1,0:T(8,128)(2,1)S(1)}, bf16[16,4096]{1,0:T(8,128)(2,1)S(1)}, u32[]{:S(2)}, u32[]{:S(2)}) collective-permute-start(bf16[16,4096]{1,0:T(8,128)(2,1)S(1)} %get-tuple-element.62), channel_id=1, source_target_pairs={{0,8},{1,9},{2,10},{3,11},{4,12},{5,13},{6,14},{7,15},{8,0},{9,1},... | collective-permute-start | bytes 393224 | tf_op jit(solution)/shard_map/ppermute | solution.py:238
  11.4 1.9 %convert_bitcast_fusion = bf16[320,2048]{1,0:T(8,128)(2,1)S(1)} fusion(f32[2048,320]{0,1:T(8,128)} %param.10), kind=kLoop, calls=%fused_computation.20 | loop fusion | flops 655360 | bytes 3932160 | tf_op jit(solution)/shard_map/transpose | solution.py:324
  14.2 1.6 %collective-permute-done.2 = bf16[16,4096]{1,0:T(8,128)(2,1)S(1)} collective-permute-done((bf16[16,4096]{1,0:T(8,128)(2,1)S(1)}, bf16[16,4096]{1,0:T(8,128)(2,1)S(1)}, u32[]{:S(2)}, u32[]{:S(2)}) %collective-permute-start.2) | collective-permute-done | bytes 131104 | tf_op jit(solution)/shard_map/ppermute | solution.py:238
  15.9 1.6 %collective-permute-start.6 = (bf16[40,4096]{1,0:T(8,128)(2,1)S(1)}, bf16[40,4096]{1,0:T(8,128)(2,1)S(1)}, u32[]{:S(2)}, u32[]{:S(2)}) collective-permute-start(bf16[40,4096]{1,0:T(8,128)(2,1)S(1)} %get-tuple-element.69), channel_id=1, source_target_pairs={{0,2},{1,3},{2,0},{3,1},{4,6},{5,7},{6,4},{7,5},{8,10},{9,11},{10,... | collective-permute-start | bytes 983048 | tf_op jit(solution)/shard_map/ppermute | solution.py:238
  18.4 1.4 %collective-permute-start.7 = (bf16[40,4096]{1,0:T(8,128)(2,1)S(1)}, bf16[40,4096]{1,0:T(8,128)(2,1)S(1)}, u32[]{:S(2)}, u32[]{:S(2)}) collective-permute-start(bf16[40,4096]{1,0:T(8,128)(2,1)S(1)} %get-tuple-element.70), channel_id=1, source_target_pairs={{0,8},{1,9},{2,10},{3,11},{4,12},{5,13},{6,14},{7,15},{8,0},{9,1},... | collective-permute-start | bytes 983048 | tf_op jit(solution)/shard_map/ppermute | solution.py:238
  19.8 4.9 %collective-permute-done.6 = bf16[40,4096]{1,0:T(8,128)(2,1)S(1)} collective-permute-done((bf16[40,4096]{1,0:T(8,128)(2,1)S(1)}, bf16[40,4096]{1,0:T(8,128)(2,1)S(1)}, u32[]{:S(2)}, u32[]{:S(2)}) %collective-permute-start.6) | collective-permute-done | bytes 327712 | tf_op jit(solution)/shard_map/ppermute | solution.py:238
  25.2 1.8 %collective-permute-start.12 = (bf16[24,4096]{1,0:T(8,128)(2,1)S(1)}, bf16[24,4096]{1,0:T(8,128)(2,1)S(1)}, u32[]{:S(2)}, u32[]{:S(2)}) collective-permute-start(bf16[24,4096]{1,0:T(8,128)(2,1)S(1)} %get-tuple-element.72), channel_id=1, source_target_pairs={{0,12},{1,13},{2,14},{3,15},{4,8},{5,9},{6,10},{7,11},{8,4},{9,5},... | collective-permute-start | bytes 589832 | tf_op jit(solution)/shard_map/ppermute | solution.py:238
  27.0 1.4 %collective-permute-start.10 = (bf16[24,4096]{1,0:T(8,128)(2,1)S(1)}, bf16[24,4096]{1,0:T(8,128)(2,1)S(1)}, u32[]{:S(2)}, u32[]{:S(2)}) collective-permute-start(bf16[24,4096]{1,0:T(8,128)(2,1)S(1)} %get-tuple-element.73), channel_id=1, source_target_pairs={{0,8},{1,9},{2,10},{3,11},{4,12},{5,13},{6,14},{7,15},{8,0},{9,1},... | collective-permute-start | bytes 589832 | tf_op jit(solution)/shard_map/ppermute | solution.py:238
  29.6 1.0 %multiply_convert_fusion = (bf16[128,640]{1,0:T(8,128)(2,1)S(1)}, f32[128,640]{1,0:T(8,128)S(1)}) fusion(bf16[320,2048]{1,0:T(8,128)(2,1)S(1)} %convert_bitcast_fusion, bf16[320,2048]{1,0:T(8,128)(2,1)S(1)} %get-tuple-element.106, bf16[128,4096]{1,0:T(8,128)(2,1)S(1)} %slice_dynamic-update-slice_fusion), kind=kOutput, calls=%fused_computation.52 | convolution fusion | flops 341606400 | bytes 3637248 | tf_op jit(solution)/shard_map/dot_general | solution.py:39
  30.6 1.1 %fusion.11 = bf16[128,640]{1,0:T(8,128)(2,1)S(1)} fusion(bf16[128,4096]{1,0:T(8,128)(2,1)S(1)} %slice_dynamic-update-slice_fusion, f32[128,640]{1,0:T(8,128)S(1)} %get-tuple-element.138, bf16[320,2048]{1,0:T(8,128)(2,1)S(1)} %get-tuple-element.105, bf16[320,2048]{1,0:T(8,128)(2,1)S(1)} %convert_bitcast_fusion.1), kind=kOutput, calls=%fused_computation.24 | convolution fusion | flops 342507520 | bytes 3637248 | tf_op jit(solution)/shard_map/dot_general | solution.py:39
  34.2 1.1 %collective-permute-done.10 = bf16[24,4096]{1,0:T(8,128)(2,1)S(1)} collective-permute-done((bf16[24,4096]{1,0:T(8,128)(2,1)S(1)}, bf16[24,4096]{1,0:T(8,128)(2,1)S(1)}, u32[]{:S(2)}, u32[]{:S(2)}) %collective-permute-start.10) | collective-permute-done | bytes 196640 | tf_op jit(solution)/shard_map/ppermute | solution.py:238
  35.4 2.6 %shard_map.87 = (bf16[192,640]{1,0:T(8,128)(2,1)S(1)}, bf16[192,640]{1,0:T(8,128)(2,1)S(1)}, bf16[192,2048]{1,0:T(8,128)(2,1)S(1)}) custom-call(bf16[192,4096]{1,0:T(8,128)(2,1)S(1)} %constant_dynamic-update-slice_fusion.5.refs_0_, bf16[640,2048]{1,0:T(8,128)(2,1)S(1)} %get-tuple-element.139.refs_1_, bf16[640,2048]{1,0:T(8,128)(2,1)S(1)} %get-tuple-element.140.refs_2_), custom_call_target="tpu_custom_call" | custom-call | flops 1509949440 | bytes 5242880 | tf_op jit(solution)/shard_map/pallas_call | solution.py:175
  38.1 1.9 %collective-permute-start.18 = (bf16[40,2048]{1,0:T(8,128)(2,1)S(1)}, bf16[40,2048]{1,0:T(8,128)(2,1)S(1)}, u32[]{:S(2)}, u32[]{:S(2)}) collective-permute-start(bf16[40,2048]{1,0:T(8,128)(2,1)S(1)} %pad_maximum_fusion.5), channel_id=1, source_target_pairs={{0,12},{1,13},{2,14},{3,15},{4,8},{5,9},{6,10},{7,11},{8,4},{9,5},... | collective-permute-start | bytes 491528 | tf_op jit(solution)/shard_map/ppermute | solution.py:238
  40.0 1.6 %collective-permute-start.13 = (bf16[40,2048]{1,0:T(8,128)(2,1)S(1)}, bf16[40,2048]{1,0:T(8,128)(2,1)S(1)}, u32[]{:S(2)}, u32[]{:S(2)}) collective-permute-start(bf16[40,2048]{1,0:T(8,128)(2,1)S(1)} %pad_maximum_fusion.6), channel_id=1, source_target_pairs={{0,2},{1,3},{2,0},{3,1},{4,6},{5,7},{6,4},{7,5},{8,10},{9,11},{10,... | collective-permute-start | bytes 491528 | tf_op jit(solution)/shard_map/ppermute | solution.py:238
  45.5 1.3 %collective-permute-start.14 = (bf16[40,2048]{1,0:T(8,128)(2,1)S(1)}, bf16[40,2048]{1,0:T(8,128)(2,1)S(1)}, u32[]{:S(2)}, u32[]{:S(2)}) collective-permute-start(bf16[40,2048]{1,0:T(8,128)(2,1)S(1)} %add_convert_fusion.3), channel_id=1, source_target_pairs={{0,8},{1,9},{2,10},{3,11},{4,12},{5,13},{6,14},{7,15},{8,0},{9,1},... | collective-permute-start | bytes 491528 | tf_op jit(solution)/shard_map/ppermute | solution.py:238
  46.8 1.1 %collective-permute-done.15 = bf16[40,2048]{1,0:T(8,128)(2,1)S(1)} collective-permute-done((bf16[40,2048]{1,0:T(8,128)(2,1)S(1)}, bf16[40,2048]{1,0:T(8,128)(2,1)S(1)}, u32[]{:S(2)}, u32[]{:S(2)}) %collective-permute-start.15) | collective-permute-done | bytes 163872 | tf_op jit(solution)/shard_map/ppermute | solution.py:238
  47.9 1.0 %collective-permute-start.16 = (bf16[40,2048]{1,0:T(8,128)(2,1)S(1)}, bf16[40,2048]{1,0:T(8,128)(2,1)S(1)}, u32[]{:S(2)}, u32[]{:S(2)}) collective-permute-start(bf16[40,2048]{1,0:T(8,128)(2,1)S(1)} %add_convert_fusion.2), channel_id=1, source_target_pairs={{0,4},{1,5},{2,6},{3,7},{4,0},{5,1},{6,2},{7,3},{8,12},{9,13},{10,... | collective-permute-start | bytes 491528 | tf_op jit(solution)/shard_map/ppermute | solution.py:238
  49.0 1.1 %collective-permute-start.19 = (bf16[40,2048]{1,0:T(8,128)(2,1)S(1)}, bf16[40,2048]{1,0:T(8,128)(2,1)S(1)}, u32[]{:S(2)}, u32[]{:S(2)}) collective-permute-start(bf16[40,2048]{1,0:T(8,128)(2,1)S(1)} %add_convert_fusion.1), channel_id=1, source_target_pairs={{0,2},{1,3},{2,0},{3,1},{4,6},{5,7},{6,4},{7,5},{8,10},{9,11},{10,... | collective-permute-start | bytes 491528 | tf_op jit(solution)/shard_map/ppermute | solution.py:238
  54.5 3.5 %collective-permute-start.22 = (bf16[40,1024]{1,0:T(8,128)(2,1)S(1)}, bf16[40,1024]{1,0:T(8,128)(2,1)S(1)}, u32[]{:S(2)}, u32[]{:S(2)}) collective-permute-start(bf16[40,1024]{1,0:T(8,128)(2,1)S(1)} %pad_maximum_fusion.9), channel_id=1, source_target_pairs={{0,16},{1,17},{2,18},{3,19},{4,20},{5,21},{6,22},{7,23},{8,24},{9,... | collective-permute-start | bytes 245768 | tf_op jit(solution)/shard_map/ppermute | solution.py:281
  58.5 2.5 %shard_map.88 = (f32[320,2048]{1,0:T(8,128)}, f32[320,2048]{1,0:T(8,128)}) custom-call(f32[320,2048]{1,0:T(8,128)S(1)} %fusion.3.refs_0_, f32[320,2048]{1,0:T(8,128)S(1)} %fusion.1.refs_1_, bf16[320,2048]{1,0:T(8,128)(2,1)S(1)} %collective-permute-done.20.refs_2_, bf16[320,2048]{1,0:T(8,128)(2,1)S(1)} %collective-permute-done.21.refs_3_), custom_call_target="tpu_custom_call" | custom-call | flops 2621440 | bytes 5242880 | tf_op jit(solution)/shard_map/pallas_call | solution.py:213
  61.1 1.0 %fusion.9 = bf16[64,2048]{1,0:T(8,128)(2,1)} fusion(f32[64,2048]{1,0:T(8,128)S(1)} %convolution_add_fusion.5, bf16[20,1024]{1,0:T(8,128)(2,1)S(1)} %get-tuple-element.136, bf16[20,1024]{1,0:T(8,128)(2,1)S(1)} %get-tuple-element.135, bf16[40,64]{1,0:T(8,128)(2,1)S(1)} %get-tuple-element.93), kind=kOutput, calls=%fused_computation.19 | convolution fusion | flops 5668864 | bytes 890880 | tf_op jit(solution)/shard_map/dot_general | solution.py:33
  (80 shorter events, 16.0 us)
Async XLA Ops:
  0.6 12.7 %copy-start = (f32[2048,320]{0,1:T(8,128)S(1)}, f32[2048,320]{0,1:T(8,128)}, u32[]{:S(2)}) copy-start(f32[2048,320]{0,1:T(8,128)} %param.11) | copy-start | bytes 7864324
  2.2 11.9 %collective-permute-start = (bf16[40,2048]{1,0:T(8,128)(2,1)S(1)}, bf16[40,2048]{1,0:T(8,128)(2,1)S(1)}, u32[]{:S(2)}, u32[]{:S(2)}) collective-permute-start(bf16[40,2048]{1,0:T(8,128)(2,1)S(1)} %get-tuple-element.56.refs_4_), channel_id=1, source_target_pairs={{0,16},{1,17},{2,18},{3,19},{4,20},{5,21},{6,22},{7,23},{8,24},{9,... | collective-permute-start | bytes 491528 | tf_op jit(solution)/shard_map/ppermute | solution.py:281
  6.3 7.9 %collective-permute-start.1 = (bf16[16,4096]{1,0:T(8,128)(2,1)S(1)}, bf16[16,4096]{1,0:T(8,128)(2,1)S(1)}, u32[]{:S(2)}, u32[]{:S(2)}) collective-permute-start(bf16[16,4096]{1,0:T(8,128)(2,1)S(1)} %get-tuple-element.61), channel_id=1, source_target_pairs={{0,6},{1,7},{2,4},{3,5},{4,2},{5,3},{6,0},{7,1},{8,14},{9,15},{10,... | collective-permute-start | bytes 393224 | tf_op jit(solution)/shard_map/ppermute | solution.py:238
  8.8 7.0 %collective-permute-start.2 = (bf16[16,4096]{1,0:T(8,128)(2,1)S(1)}, bf16[16,4096]{1,0:T(8,128)(2,1)S(1)}, u32[]{:S(2)}, u32[]{:S(2)}) collective-permute-start(bf16[16,4096]{1,0:T(8,128)(2,1)S(1)} %get-tuple-element.62), channel_id=1, source_target_pairs={{0,8},{1,9},{2,10},{3,11},{4,12},{5,13},{6,14},{7,15},{8,0},{9,1},... | collective-permute-start | bytes 393224 | tf_op jit(solution)/shard_map/ppermute | solution.py:238
  10.3 5.4 %collective-permute-start.3 = (bf16[16,4096]{1,0:T(8,128)(2,1)S(1)}, bf16[16,4096]{1,0:T(8,128)(2,1)S(1)}, u32[]{:S(2)}, u32[]{:S(2)}) collective-permute-start(bf16[16,4096]{1,0:T(8,128)(2,1)S(1)} %get-tuple-element.63), channel_id=1, source_target_pairs={{0,2},{1,3},{2,0},{3,1},{4,6},{5,7},{6,4},{7,5},{8,10},{9,11},{10,... | collective-permute-start | bytes 393224 | tf_op jit(solution)/shard_map/ppermute | solution.py:238
  10.9 5.0 %collective-permute-start.4 = (bf16[16,4096]{1,0:T(8,128)(2,1)S(1)}, bf16[16,4096]{1,0:T(8,128)(2,1)S(1)}, u32[]{:S(2)}, u32[]{:S(2)}) collective-permute-start(bf16[16,4096]{1,0:T(8,128)(2,1)S(1)} %get-tuple-element.64), channel_id=1, source_target_pairs={{0,4},{1,5},{2,6},{3,7},{4,0},{5,1},{6,2},{7,3},{8,12},{9,13},{10,... | collective-permute-start | bytes 393224 | tf_op jit(solution)/shard_map/ppermute | solution.py:238
  15.9 8.8 %collective-permute-start.6 = (bf16[40,4096]{1,0:T(8,128)(2,1)S(1)}, bf16[40,4096]{1,0:T(8,128)(2,1)S(1)}, u32[]{:S(2)}, u32[]{:S(2)}) collective-permute-start(bf16[40,4096]{1,0:T(8,128)(2,1)S(1)} %get-tuple-element.69), channel_id=1, source_target_pairs={{0,2},{1,3},{2,0},{3,1},{4,6},{5,7},{6,4},{7,5},{8,10},{9,11},{10,... | collective-permute-start | bytes 983048 | tf_op jit(solution)/shard_map/ppermute | solution.py:238
  17.5 9.4 %collective-permute-start.5 = (bf16[40,4096]{1,0:T(8,128)(2,1)S(1)}, bf16[40,4096]{1,0:T(8,128)(2,1)S(1)}, u32[]{:S(2)}, u32[]{:S(2)}) collective-permute-start(bf16[40,4096]{1,0:T(8,128)(2,1)S(1)} %get-tuple-element.69), channel_id=1, source_target_pairs={{0,4},{1,5},{2,6},{3,7},{4,0},{5,1},{6,2},{7,3},{8,12},{9,13},{10,... | collective-permute-start | bytes 983048 | tf_op jit(solution)/shard_map/ppermute | solution.py:238
  18.4 10.0 %collective-permute-start.7 = (bf16[40,4096]{1,0:T(8,128)(2,1)S(1)}, bf16[40,4096]{1,0:T(8,128)(2,1)S(1)}, u32[]{:S(2)}, u32[]{:S(2)}) collective-permute-start(bf16[40,4096]{1,0:T(8,128)(2,1)S(1)} %get-tuple-element.70), channel_id=1, source_target_pairs={{0,8},{1,9},{2,10},{3,11},{4,12},{5,13},{6,14},{7,15},{8,0},{9,1},... | collective-permute-start | bytes 983048 | tf_op jit(solution)/shard_map/ppermute | solution.py:238
  19.8 9.6 %collective-permute-start.8 = (bf16[640,2048]{1,0:T(8,128)(2,1)S(1)}, bf16[640,2048]{1,0:T(8,128)(2,1)S(1)}, u32[]{:S(2)}, u32[]{:S(2)}) collective-permute-start(bf16[640,2048]{1,0:T(8,128)(2,1)S(1)} %pad_maximum_fusion.1), channel_id=1, source_target_pairs={{0,1},{1,0},{2,3},{3,2},{4,5},{5,4},{6,7},{7,6},{8,9},{9,8},{10,11... | collective-permute-start | bytes 7864328 | tf_op jit(solution)/shard_map/ppermute | solution.py:238
  24.8 10.5 %collective-permute-start.9 = (bf16[24,4096]{1,0:T(8,128)(2,1)S(1)}, bf16[24,4096]{1,0:T(8,128)(2,1)S(1)}, u32[]{:S(2)}, u32[]{:S(2)}) collective-permute-start(bf16[24,4096]{1,0:T(8,128)(2,1)S(1)} %get-tuple-element.72), channel_id=1, source_target_pairs={{0,4},{1,5},{2,6},{3,7},{4,0},{5,1},{6,2},{7,3},{8,12},{9,13},{10,... | collective-permute-start | bytes 589832 | tf_op jit(solution)/shard_map/ppermute | solution.py:238
  25.2 10.1 %collective-permute-start.12 = (bf16[24,4096]{1,0:T(8,128)(2,1)S(1)}, bf16[24,4096]{1,0:T(8,128)(2,1)S(1)}, u32[]{:S(2)}, u32[]{:S(2)}) collective-permute-start(bf16[24,4096]{1,0:T(8,128)(2,1)S(1)} %get-tuple-element.72), channel_id=1, source_target_pairs={{0,12},{1,13},{2,14},{3,15},{4,8},{5,9},{6,10},{7,11},{8,4},{9,5},... | collective-permute-start | bytes 589832 | tf_op jit(solution)/shard_map/ppermute | solution.py:238
  27.0 8.3 %collective-permute-start.10 = (bf16[24,4096]{1,0:T(8,128)(2,1)S(1)}, bf16[24,4096]{1,0:T(8,128)(2,1)S(1)}, u32[]{:S(2)}, u32[]{:S(2)}) collective-permute-start(bf16[24,4096]{1,0:T(8,128)(2,1)S(1)} %get-tuple-element.73), channel_id=1, source_target_pairs={{0,8},{1,9},{2,10},{3,11},{4,12},{5,13},{6,14},{7,15},{8,0},{9,1},... | collective-permute-start | bytes 589832 | tf_op jit(solution)/shard_map/ppermute | solution.py:238
  28.4 5.7 %collective-permute-start.11 = (bf16[24,4096]{1,0:T(8,128)(2,1)S(1)}, bf16[24,4096]{1,0:T(8,128)(2,1)S(1)}, u32[]{:S(2)}, u32[]{:S(2)}) collective-permute-start(bf16[24,4096]{1,0:T(8,128)(2,1)S(1)} %get-tuple-element.74), channel_id=1, source_target_pairs={{0,2},{1,3},{2,0},{3,1},{4,6},{5,7},{6,4},{7,5},{8,10},{9,11},{10,... | collective-permute-start | bytes 589832 | tf_op jit(solution)/shard_map/ppermute | solution.py:238
  38.1 10.8 %collective-permute-start.18 = (bf16[40,2048]{1,0:T(8,128)(2,1)S(1)}, bf16[40,2048]{1,0:T(8,128)(2,1)S(1)}, u32[]{:S(2)}, u32[]{:S(2)}) collective-permute-start(bf16[40,2048]{1,0:T(8,128)(2,1)S(1)} %pad_maximum_fusion.5), channel_id=1, source_target_pairs={{0,12},{1,13},{2,14},{3,15},{4,8},{5,9},{6,10},{7,11},{8,4},{9,5},... | collective-permute-start | bytes 491528 | tf_op jit(solution)/shard_map/ppermute | solution.py:238
  40.0 5.4 %collective-permute-start.13 = (bf16[40,2048]{1,0:T(8,128)(2,1)S(1)}, bf16[40,2048]{1,0:T(8,128)(2,1)S(1)}, u32[]{:S(2)}, u32[]{:S(2)}) collective-permute-start(bf16[40,2048]{1,0:T(8,128)(2,1)S(1)} %pad_maximum_fusion.6), channel_id=1, source_target_pairs={{0,2},{1,3},{2,0},{3,1},{4,6},{5,7},{6,4},{7,5},{8,10},{9,11},{10,... | collective-permute-start | bytes 491528 | tf_op jit(solution)/shard_map/ppermute | solution.py:238
  41.6 6.3 %collective-permute-start.15 = (bf16[40,2048]{1,0:T(8,128)(2,1)S(1)}, bf16[40,2048]{1,0:T(8,128)(2,1)S(1)}, u32[]{:S(2)}, u32[]{:S(2)}) collective-permute-start(bf16[40,2048]{1,0:T(8,128)(2,1)S(1)} %pad_maximum_fusion.7), channel_id=1, source_target_pairs={{0,8},{1,9},{2,10},{3,11},{4,12},{5,13},{6,14},{7,15},{8,0},{9,1},... | collective-permute-start | bytes 491528 | tf_op jit(solution)/shard_map/ppermute | solution.py:238
  41.7 7.2 %collective-permute-start.17 = (bf16[40,2048]{1,0:T(8,128)(2,1)S(1)}, bf16[40,2048]{1,0:T(8,128)(2,1)S(1)}, u32[]{:S(2)}, u32[]{:S(2)}) collective-permute-start(bf16[40,2048]{1,0:T(8,128)(2,1)S(1)} %pad_maximum_fusion.8), channel_id=1, source_target_pairs={{0,4},{1,5},{2,6},{3,7},{4,0},{5,1},{6,2},{7,3},{8,12},{9,13},{10,... | collective-permute-start | bytes 491528 | tf_op jit(solution)/shard_map/ppermute | solution.py:238
  45.5 8.9 %collective-permute-start.14 = (bf16[40,2048]{1,0:T(8,128)(2,1)S(1)}, bf16[40,2048]{1,0:T(8,128)(2,1)S(1)}, u32[]{:S(2)}, u32[]{:S(2)}) collective-permute-start(bf16[40,2048]{1,0:T(8,128)(2,1)S(1)} %add_convert_fusion.3), channel_id=1, source_target_pairs={{0,8},{1,9},{2,10},{3,11},{4,12},{5,13},{6,14},{7,15},{8,0},{9,1},... | collective-permute-start | bytes 491528 | tf_op jit(solution)/shard_map/ppermute | solution.py:238
  47.9 6.5 %collective-permute-start.16 = (bf16[40,2048]{1,0:T(8,128)(2,1)S(1)}, bf16[40,2048]{1,0:T(8,128)(2,1)S(1)}, u32[]{:S(2)}, u32[]{:S(2)}) collective-permute-start(bf16[40,2048]{1,0:T(8,128)(2,1)S(1)} %add_convert_fusion.2), channel_id=1, source_target_pairs={{0,4},{1,5},{2,6},{3,7},{4,0},{5,1},{6,2},{7,3},{8,12},{9,13},{10,... | collective-permute-start | bytes 491528 | tf_op jit(solution)/shard_map/ppermute | solution.py:238
  49.0 5.4 %collective-permute-start.19 = (bf16[40,2048]{1,0:T(8,128)(2,1)S(1)}, bf16[40,2048]{1,0:T(8,128)(2,1)S(1)}, u32[]{:S(2)}, u32[]{:S(2)}) collective-permute-start(bf16[40,2048]{1,0:T(8,128)(2,1)S(1)} %add_convert_fusion.1), channel_id=1, source_target_pairs={{0,2},{1,3},{2,0},{3,1},{4,6},{5,7},{6,4},{7,5},{8,10},{9,11},{10,... | collective-permute-start | bytes 491528 | tf_op jit(solution)/shard_map/ppermute | solution.py:238
  51.2 7.3 %collective-permute-start.20 = (bf16[320,2048]{1,0:T(8,128)(2,1)S(1)}, bf16[320,2048]{1,0:T(8,128)(2,1)S(1)}, u32[]{:S(2)}, u32[]{:S(2)}) collective-permute-start(bf16[320,2048]{1,0:T(8,128)(2,1)S(1)} %fusion.6), channel_id=1, source_target_pairs={{0,1},{1,0},{2,3},{3,2},{4,5},{5,4},{6,7},{7,6},{8,9},{9,8},{10,11... | collective-permute-start | bytes 3932168 | tf_op jit(solution)/shard_map/ppermute | solution.py:238
  51.3 7.3 %collective-permute-start.21 = (bf16[320,2048]{1,0:T(8,128)(2,1)S(1)}, bf16[320,2048]{1,0:T(8,128)(2,1)S(1)}, u32[]{:S(2)}, u32[]{:S(2)}) collective-permute-start(bf16[320,2048]{1,0:T(8,128)(2,1)S(1)} %fusion.7), channel_id=1, source_target_pairs={{0,1},{1,0},{2,3},{3,2},{4,5},{5,4},{6,7},{7,6},{8,9},{9,8},{10,11... | collective-permute-start | bytes 3932168 | tf_op jit(solution)/shard_map/ppermute | solution.py:238
  54.5 6.5 %collective-permute-start.22 = (bf16[40,1024]{1,0:T(8,128)(2,1)S(1)}, bf16[40,1024]{1,0:T(8,128)(2,1)S(1)}, u32[]{:S(2)}, u32[]{:S(2)}) collective-permute-start(bf16[40,1024]{1,0:T(8,128)(2,1)S(1)} %pad_maximum_fusion.9), channel_id=1, source_target_pairs={{0,16},{1,17},{2,18},{3,19},{4,20},{5,21},{6,22},{7,23},{8,24},{9,... | collective-permute-start | bytes 245768 | tf_op jit(solution)/shard_map/ppermute | solution.py:281
  (1 other events, 1.7 us)

commit v23 on v22

--- a/solution.py
+++ b/solution.py
@@ -343,9 +343,9 @@
         for pair in zip(split_rows(early_parts, first), split_rows(late_parts, rest))
     ]
     own, sum_x, sum_y, sum_z, sum_xy, sum_yz, sum_zx, sum_far = parts
-    back = chain([sum_far, sum_zx, sum_yz, sum_xy])
-    far, zx, yz, xy = [
-        swap(rows, mask) for rows, mask in zip(back, (y_bit | z_bit, x_bit, z_bit, y_bit))
+    back = chain([sum_zx, sum_far, sum_yz, sum_xy])
+    zx, far, yz, xy = [
+        swap(rows, mask) for rows, mask in zip(back, (x_bit, y_bit | z_bit, z_bit, y_bit))
     ]
 
     def gradients(part, awaited):

time: 62.2 us -> 63.4 us (1.019)
  starting transfers between devices: 29.5 us -> 30.4 us
where the time goes in v23:
time: 63.4 us; the launch traced here: 63.2 us
  starting transfers between devices  30.4 us (48%)
  waiting for transfers between devices  11.7 us (18%)
  matrix products  8.72 us (14%)
  Pallas kernels  6.64 us (10%)
  other arithmetic  3.59 us (6%)
  local copies, waits for them, and re-layouts  1.17 us (2%)
  between operations  1.04 us (2%)
    ppermute x21, starting transfers between devices, swap(): lax.ppermute(rows, 'expert', [(i, i ^ mask) for i in range(n_expert)])  22.4 us
    ppermute x21, waiting for transfers between devices, swap(): lax.ppermute(rows, 'expert', [(i, i ^ mask) for i in range(n_expert)])  11 us
    ppermute x2, starting transfers between devices, shifted(): return lax.ppermute(rows, 'expert', pairs)  8.02 us
    dot_general x11, matrix products, contract_rows(): lax.dot_general(left, right, (((0,), (0,)), ((), ())), preferred_element_...  6.05 us
    pallas_call x1, Pallas kernels, worked(): pl.pallas_call(lambda *refs: expert_kernel(scale_in, scale_out, *refs), o...  2.6 us
    pallas_call x1, Pallas kernels, stepped(): pl.pallas_call(lambda *refs: step_kernel(rows, *refs), out_shape=[jax.Sha...  2.47 us
    dot_general x2, matrix products, contract_cols(): lax.dot_general(left, right, (((1,), (1,)), ((), ())), preferred_element_...  2.07 us
    transpose x1, other arithmetic, shards(): whole_weights(w_in)  1.93 us
  transfers between devices with their start and end apart: 23, of which 9 were waited for; matrix products, arithmetic and copies ran while one was open for 19% of the time, Pallas kernels for 4%

profile of v23, /device:TPU:0, one launch (start us, length us, event | category | flops | bytes accessed | tf_op | source)
XLA Modules:
  0.0 63.2 jit_solution(439745621231771927)
XLA Ops:
  0.6 1.6 %shard_map.85 = (bf16[16,4096]{1,0:T(8,128)(2,1)S(1)}, bf16[24,4096]{1,0:T(8,128)(2,1)S(1)}, bf16[40,2048]{1,0:T(8,128)(2,1)S(1)}, bf16[16,64]{1,0:T(8,128)(2,1)...) custom-call(s32[1,64]{1,0:T(1,128)} %bitcast.17, ...), custom_call_target="tpu_custom_call" | custom-call | tf_op jit(solution)/shard_map/pallas_call | solution.py:124
  2.2 4.1 %collective-permute-start = (bf16[40,2048]{1,0:T(8,128)(2,1)S(1)}, bf16[40,2048]{1,0:T(8,128)(2,1)S(1)}, u32[]{:S(2)}, u32[]{:S(2)}) collective-permute-start(bf16[40,2048]{1,0:T(8,128)(2,1)S(1)} %get-tuple-element.56.refs_4_), channel_id=1, source_target_pairs={{0,16},{1,17},{2,18},{3,19},{4,20},{5,21},{6,22},{7,23},{8,24},{9,... | collective-permute-start | bytes 491528 | tf_op jit(solution)/shard_map/ppermute | solution.py:281
  6.3 2.5 %collective-permute-start.1 = (bf16[16,4096]{1,0:T(8,128)(2,1)S(1)}, bf16[16,4096]{1,0:T(8,128)(2,1)S(1)}, u32[]{:S(2)}, u32[]{:S(2)}) collective-permute-start(bf16[16,4096]{1,0:T(8,128)(2,1)S(1)} %get-tuple-element.61), channel_id=1, source_target_pairs={{0,6},{1,7},{2,4},{3,5},{4,2},{5,3},{6,0},{7,1},{8,14},{9,15},{10,... | collective-permute-start | bytes 393224 | tf_op jit(solution)/shard_map/ppermute | solution.py:238
  8.8 1.6 %collective-permute-start.2 = (bf16[16,4096]{1,0:T(8,128)(2,1)S(1)}, bf16[16,4096]{1,0:T(8,128)(2,1)S(1)}, u32[]{:S(2)}, u32[]{:S(2)}) collective-permute-start(bf16[16,4096]{1,0:T(8,128)(2,1)S(1)} %get-tuple-element.62), channel_id=1, source_target_pairs={{0,8},{1,9},{2,10},{3,11},{4,12},{5,13},{6,14},{7,15},{8,0},{9,1},... | collective-permute-start | bytes 393224 | tf_op jit(solution)/shard_map/ppermute | solution.py:238
  11.4 1.9 %convert_bitcast_fusion = bf16[320,2048]{1,0:T(8,128)(2,1)S(1)} fusion(f32[2048,320]{0,1:T(8,128)} %param.10), kind=kLoop, calls=%fused_computation.20 | loop fusion | flops 655360 | bytes 3932160 | tf_op jit(solution)/shard_map/transpose | solution.py:324
  14.2 1.6 %collective-permute-done.2 = bf16[16,4096]{1,0:T(8,128)(2,1)S(1)} collective-permute-done((bf16[16,4096]{1,0:T(8,128)(2,1)S(1)}, bf16[16,4096]{1,0:T(8,128)(2,1)S(1)}, u32[]{:S(2)}, u32[]{:S(2)}) %collective-permute-start.2) | collective-permute-done | bytes 131104 | tf_op jit(solution)/shard_map/ppermute | solution.py:238
  15.9 1.6 %collective-permute-start.6 = (bf16[40,4096]{1,0:T(8,128)(2,1)S(1)}, bf16[40,4096]{1,0:T(8,128)(2,1)S(1)}, u32[]{:S(2)}, u32[]{:S(2)}) collective-permute-start(bf16[40,4096]{1,0:T(8,128)(2,1)S(1)} %get-tuple-element.69), channel_id=1, source_target_pairs={{0,2},{1,3},{2,0},{3,1},{4,6},{5,7},{6,4},{7,5},{8,10},{9,11},{10,... | collective-permute-start | bytes 983048 | tf_op jit(solution)/shard_map/ppermute | solution.py:238
  18.4 1.4 %collective-permute-start.7 = (bf16[40,4096]{1,0:T(8,128)(2,1)S(1)}, bf16[40,4096]{1,0:T(8,128)(2,1)S(1)}, u32[]{:S(2)}, u32[]{:S(2)}) collective-permute-start(bf16[40,4096]{1,0:T(8,128)(2,1)S(1)} %get-tuple-element.70), channel_id=1, source_target_pairs={{0,8},{1,9},{2,10},{3,11},{4,12},{5,13},{6,14},{7,15},{8,0},{9,1},... | collective-permute-start | bytes 983048 | tf_op jit(solution)/shard_map/ppermute | solution.py:238
  19.8 4.9 %collective-permute-done.6 = bf16[40,4096]{1,0:T(8,128)(2,1)S(1)} collective-permute-done((bf16[40,4096]{1,0:T(8,128)(2,1)S(1)}, bf16[40,4096]{1,0:T(8,128)(2,1)S(1)}, u32[]{:S(2)}, u32[]{:S(2)}) %collective-permute-start.6) | collective-permute-done | bytes 327712 | tf_op jit(solution)/shard_map/ppermute | solution.py:238
  25.2 1.8 %collective-permute-start.12 = (bf16[24,4096]{1,0:T(8,128)(2,1)S(1)}, bf16[24,4096]{1,0:T(8,128)(2,1)S(1)}, u32[]{:S(2)}, u32[]{:S(2)}) collective-permute-start(bf16[24,4096]{1,0:T(8,128)(2,1)S(1)} %get-tuple-element.72), channel_id=1, source_target_pairs={{0,12},{1,13},{2,14},{3,15},{4,8},{5,9},{6,10},{7,11},{8,4},{9,5},... | collective-permute-start | bytes 589832 | tf_op jit(solution)/shard_map/ppermute | solution.py:238
  27.0 1.4 %collective-permute-start.10 = (bf16[24,4096]{1,0:T(8,128)(2,1)S(1)}, bf16[24,4096]{1,0:T(8,128)(2,1)S(1)}, u32[]{:S(2)}, u32[]{:S(2)}) collective-permute-start(bf16[24,4096]{1,0:T(8,128)(2,1)S(1)} %get-tuple-element.73), channel_id=1, source_target_pairs={{0,8},{1,9},{2,10},{3,11},{4,12},{5,13},{6,14},{7,15},{8,0},{9,1},... | collective-permute-start | bytes 589832 | tf_op jit(solution)/shard_map/ppermute | solution.py:238
  29.6 1.0 %multiply_convert_fusion = (bf16[128,640]{1,0:T(8,128)(2,1)S(1)}, f32[128,640]{1,0:T(8,128)S(1)}) fusion(bf16[320,2048]{1,0:T(8,128)(2,1)S(1)} %convert_bitcast_fusion, bf16[320,2048]{1,0:T(8,128)(2,1)S(1)} %get-tuple-element.106, bf16[128,4096]{1,0:T(8,128)(2,1)S(1)} %slice_dynamic-update-slice_fusion), kind=kOutput, calls=%fused_computation.52 | convolution fusion | flops 341606400 | bytes 3637248 | tf_op jit(solution)/shard_map/dot_general | solution.py:39
  30.6 1.1 %fusion.11 = bf16[128,640]{1,0:T(8,128)(2,1)S(1)} fusion(bf16[128,4096]{1,0:T(8,128)(2,1)S(1)} %slice_dynamic-update-slice_fusion, f32[128,640]{1,0:T(8,128)S(1)} %get-tuple-element.138, bf16[320,2048]{1,0:T(8,128)(2,1)S(1)} %get-tuple-element.105, bf16[320,2048]{1,0:T(8,128)(2,1)S(1)} %convert_bitcast_fusion.1), kind=kOutput, calls=%fused_computation.24 | convolution fusion | flops 342507520 | bytes 3637248 | tf_op jit(solution)/shard_map/dot_general | solution.py:39
  33.2 1.0 %collective-permute-done.11 = bf16[24,4096]{1,0:T(8,128)(2,1)S(1)} collective-permute-done((bf16[24,4096]{1,0:T(8,128)(2,1)S(1)}, bf16[24,4096]{1,0:T(8,128)(2,1)S(1)}, u32[]{:S(2)}, u32[]{:S(2)}) %collective-permute-start.11) | collective-permute-done | bytes 196640 | tf_op jit(solution)/shard_map/ppermute | solution.py:238
  34.2 1.1 %collective-permute-done.10 = bf16[24,4096]{1,0:T(8,128)(2,1)S(1)} collective-permute-done((bf16[24,4096]{1,0:T(8,128)(2,1)S(1)}, bf16[24,4096]{1,0:T(8,128)(2,1)S(1)}, u32[]{:S(2)}, u32[]{:S(2)}) %collective-permute-start.10) | collective-permute-done | bytes 196640 | tf_op jit(solution)/shard_map/ppermute | solution.py:238
  35.4 2.6 %shard_map.87 = (bf16[192,640]{1,0:T(8,128)(2,1)S(1)}, bf16[192,640]{1,0:T(8,128)(2,1)S(1)}, bf16[192,2048]{1,0:T(8,128)(2,1)S(1)}) custom-call(bf16[192,4096]{1,0:T(8,128)(2,1)S(1)} %constant_dynamic-update-slice_fusion.5.refs_0_, bf16[640,2048]{1,0:T(8,128)(2,1)S(1)} %get-tuple-element.139.refs_1_, bf16[640,2048]{1,0:T(8,128)(2,1)S(1)} %get-tuple-element.140.refs_2_), custom_call_target="tpu_custom_call" | custom-call | flops 1509949440 | bytes 5242880 | tf_op jit(solution)/shard_map/pallas_call | solution.py:175
  38.9 2.7 %collective-permute-start.18 = (bf16[40,2048]{1,0:T(8,128)(2,1)S(1)}, bf16[40,2048]{1,0:T(8,128)(2,1)S(1)}, u32[]{:S(2)}, u32[]{:S(2)}) collective-permute-start(bf16[40,2048]{1,0:T(8,128)(2,1)S(1)} %pad_maximum_fusion.6), channel_id=1, source_target_pairs={{0,12},{1,13},{2,14},{3,15},{4,8},{5,9},{6,10},{7,11},{8,4},{9,5},... | collective-permute-start | bytes 491528 | tf_op jit(solution)/shard_map/ppermute | solution.py:238
  45.2 1.6 %collective-permute-start.14 = (bf16[40,2048]{1,0:T(8,128)(2,1)S(1)}, bf16[40,2048]{1,0:T(8,128)(2,1)S(1)}, u32[]{:S(2)}, u32[]{:S(2)}) collective-permute-start(bf16[40,2048]{1,0:T(8,128)(2,1)S(1)} %add_convert_fusion.3), channel_id=1, source_target_pairs={{0,8},{1,9},{2,10},{3,11},{4,12},{5,13},{6,14},{7,15},{8,0},{9,1},... | collective-permute-start | bytes 491528 | tf_op jit(solution)/shard_map/ppermute | solution.py:238
  46.8 1.6 %collective-permute-done.15 = bf16[40,2048]{1,0:T(8,128)(2,1)S(1)} collective-permute-done((bf16[40,2048]{1,0:T(8,128)(2,1)S(1)}, bf16[40,2048]{1,0:T(8,128)(2,1)S(1)}, u32[]{:S(2)}, u32[]{:S(2)}) %collective-permute-start.15) | collective-permute-done | bytes 163872 | tf_op jit(solution)/shard_map/ppermute | solution.py:238
  48.4 1.0 %collective-permute-start.16 = (bf16[40,2048]{1,0:T(8,128)(2,1)S(1)}, bf16[40,2048]{1,0:T(8,128)(2,1)S(1)}, u32[]{:S(2)}, u32[]{:S(2)}) collective-permute-start(bf16[40,2048]{1,0:T(8,128)(2,1)S(1)} %add_convert_fusion.2), channel_id=1, source_target_pairs={{0,4},{1,5},{2,6},{3,7},{4,0},{5,1},{6,2},{7,3},{8,12},{9,13},{10,... | collective-permute-start | bytes 491528 | tf_op jit(solution)/shard_map/ppermute | solution.py:238
  49.5 1.3 %collective-permute-start.19 = (bf16[40,2048]{1,0:T(8,128)(2,1)S(1)}, bf16[40,2048]{1,0:T(8,128)(2,1)S(1)}, u32[]{:S(2)}, u32[]{:S(2)}) collective-permute-start(bf16[40,2048]{1,0:T(8,128)(2,1)S(1)} %add_convert_fusion.1), channel_id=1, source_target_pairs={{0,2},{1,3},{2,0},{3,1},{4,6},{5,7},{6,4},{7,5},{8,10},{9,11},{10,... | collective-permute-start | bytes 491528 | tf_op jit(solution)/shard_map/ppermute | solution.py:238
  55.0 3.9 %collective-permute-start.22 = (bf16[40,1024]{1,0:T(8,128)(2,1)S(1)}, bf16[40,1024]{1,0:T(8,128)(2,1)S(1)}, u32[]{:S(2)}, u32[]{:S(2)}) collective-permute-start(bf16[40,1024]{1,0:T(8,128)(2,1)S(1)} %pad_maximum_fusion.9), channel_id=1, source_target_pairs={{0,16},{1,17},{2,18},{3,19},{4,20},{5,21},{6,22},{7,23},{8,24},{9,... | collective-permute-start | bytes 245768 | tf_op jit(solution)/shard_map/ppermute | solution.py:281
  59.5 2.5 %shard_map.88 = (f32[320,2048]{1,0:T(8,128)}, f32[320,2048]{1,0:T(8,128)}) custom-call(f32[320,2048]{1,0:T(8,128)S(1)} %fusion.3.refs_0_, f32[320,2048]{1,0:T(8,128)S(1)} %fusion.1.refs_1_, bf16[320,2048]{1,0:T(8,128)(2,1)S(1)} %collective-permute-done.20.refs_2_, bf16[320,2048]{1,0:T(8,128)(2,1)S(1)} %collective-permute-done.21.refs_3_), custom_call_target="tpu_custom_call" | custom-call | flops 2621440 | bytes 5242880 | tf_op jit(solution)/shard_map/pallas_call | solution.py:213
  62.3 1.0 %fusion.9 = bf16[64,2048]{1,0:T(8,128)(2,1)} fusion(f32[64,2048]{1,0:T(8,128)S(1)} %convolution_add_fusion.5, bf16[20,1024]{1,0:T(8,128)(2,1)S(1)} %get-tuple-element.136, bf16[20,1024]{1,0:T(8,128)(2,1)S(1)} %get-tuple-element.135, bf16[40,64]{1,0:T(8,128)(2,1)S(1)} %get-tuple-element.93), kind=kOutput, calls=%fused_computation.19 | convolution fusion | flops 5668864 | bytes 890880 | tf_op jit(solution)/shard_map/dot_general | solution.py:33
  (80 shorter events, 15.6 us)
Async XLA Ops:
  0.6 12.7 %copy-start = (f32[2048,320]{0,1:T(8,128)S(1)}, f32[2048,320]{0,1:T(8,128)}, u32[]{:S(2)}) copy-start(f32[2048,320]{0,1:T(8,128)} %param.11) | copy-start | bytes 7864324
  2.2 11.9 %collective-permute-start = (bf16[40,2048]{1,0:T(8,128)(2,1)S(1)}, bf16[40,2048]{1,0:T(8,128)(2,1)S(1)}, u32[]{:S(2)}, u32[]{:S(2)}) collective-permute-start(bf16[40,2048]{1,0:T(8,128)(2,1)S(1)} %get-tuple-element.56.refs_4_), channel_id=1, source_target_pairs={{0,16},{1,17},{2,18},{3,19},{4,20},{5,21},{6,22},{7,23},{8,24},{9,... | collective-permute-start | bytes 491528 | tf_op jit(solution)/shard_map/ppermute | solution.py:281
  6.3 7.9 %collective-permute-start.1 = (bf16[16,4096]{1,0:T(8,128)(2,1)S(1)}, bf16[16,4096]{1,0:T(8,128)(2,1)S(1)}, u32[]{:S(2)}, u32[]{:S(2)}) collective-permute-start(bf16[16,4096]{1,0:T(8,128)(2,1)S(1)} %get-tuple-element.61), channel_id=1, source_target_pairs={{0,6},{1,7},{2,4},{3,5},{4,2},{5,3},{6,0},{7,1},{8,14},{9,15},{10,... | collective-permute-start | bytes 393224 | tf_op jit(solution)/shard_map/ppermute | solution.py:238
  8.8 7.0 %collective-permute-start.2 = (bf16[16,4096]{1,0:T(8,128)(2,1)S(1)}, bf16[16,4096]{1,0:T(8,128)(2,1)S(1)}, u32[]{:S(2)}, u32[]{:S(2)}) collective-permute-start(bf16[16,4096]{1,0:T(8,128)(2,1)S(1)} %get-tuple-element.62), channel_id=1, source_target_pairs={{0,8},{1,9},{2,10},{3,11},{4,12},{5,13},{6,14},{7,15},{8,0},{9,1},... | collective-permute-start | bytes 393224 | tf_op jit(solution)/shard_map/ppermute | solution.py:238
  10.3 5.4 %collective-permute-start.3 = (bf16[16,4096]{1,0:T(8,128)(2,1)S(1)}, bf16[16,4096]{1,0:T(8,128)(2,1)S(1)}, u32[]{:S(2)}, u32[]{:S(2)}) collective-permute-start(bf16[16,4096]{1,0:T(8,128)(2,1)S(1)} %get-tuple-element.63), channel_id=1, source_target_pairs={{0,2},{1,3},{2,0},{3,1},{4,6},{5,7},{6,4},{7,5},{8,10},{9,11},{10,... | collective-permute-start | bytes 393224 | tf_op jit(solution)/shard_map/ppermute | solution.py:238
  10.9 5.0 %collective-permute-start.4 = (bf16[16,4096]{1,0:T(8,128)(2,1)S(1)}, bf16[16,4096]{1,0:T(8,128)(2,1)S(1)}, u32[]{:S(2)}, u32[]{:S(2)}) collective-permute-start(bf16[16,4096]{1,0:T(8,128)(2,1)S(1)} %get-tuple-element.64), channel_id=1, source_target_pairs={{0,4},{1,5},{2,6},{3,7},{4,0},{5,1},{6,2},{7,3},{8,12},{9,13},{10,... | collective-permute-start | bytes 393224 | tf_op jit(solution)/shard_map/ppermute | solution.py:238
  15.9 8.8 %collective-permute-start.6 = (bf16[40,4096]{1,0:T(8,128)(2,1)S(1)}, bf16[40,4096]{1,0:T(8,128)(2,1)S(1)}, u32[]{:S(2)}, u32[]{:S(2)}) collective-permute-start(bf16[40,4096]{1,0:T(8,128)(2,1)S(1)} %get-tuple-element.69), channel_id=1, source_target_pairs={{0,2},{1,3},{2,0},{3,1},{4,6},{5,7},{6,4},{7,5},{8,10},{9,11},{10,... | collective-permute-start | bytes 983048 | tf_op jit(solution)/shard_map/ppermute | solution.py:238
  17.5 9.4 %collective-permute-start.5 = (bf16[40,4096]{1,0:T(8,128)(2,1)S(1)}, bf16[40,4096]{1,0:T(8,128)(2,1)S(1)}, u32[]{:S(2)}, u32[]{:S(2)}) collective-permute-start(bf16[40,4096]{1,0:T(8,128)(2,1)S(1)} %get-tuple-element.69), channel_id=1, source_target_pairs={{0,4},{1,5},{2,6},{3,7},{4,0},{5,1},{6,2},{7,3},{8,12},{9,13},{10,... | collective-permute-start | bytes 983048 | tf_op jit(solution)/shard_map/ppermute | solution.py:238
  18.4 10.0 %collective-permute-start.7 = (bf16[40,4096]{1,0:T(8,128)(2,1)S(1)}, bf16[40,4096]{1,0:T(8,128)(2,1)S(1)}, u32[]{:S(2)}, u32[]{:S(2)}) collective-permute-start(bf16[40,4096]{1,0:T(8,128)(2,1)S(1)} %get-tuple-element.70), channel_id=1, source_target_pairs={{0,8},{1,9},{2,10},{3,11},{4,12},{5,13},{6,14},{7,15},{8,0},{9,1},... | collective-permute-start | bytes 983048 | tf_op jit(solution)/shard_map/ppermute | solution.py:238
  19.8 9.6 %collective-permute-start.8 = (bf16[640,2048]{1,0:T(8,128)(2,1)S(1)}, bf16[640,2048]{1,0:T(8,128)(2,1)S(1)}, u32[]{:S(2)}, u32[]{:S(2)}) collective-permute-start(bf16[640,2048]{1,0:T(8,128)(2,1)S(1)} %pad_maximum_fusion.1), channel_id=1, source_target_pairs={{0,1},{1,0},{2,3},{3,2},{4,5},{5,4},{6,7},{7,6},{8,9},{9,8},{10,11... | collective-permute-start | bytes 7864328 | tf_op jit(solution)/shard_map/ppermute | solution.py:238
  24.8 10.5 %collective-permute-start.9 = (bf16[24,4096]{1,0:T(8,128)(2,1)S(1)}, bf16[24,4096]{1,0:T(8,128)(2,1)S(1)}, u32[]{:S(2)}, u32[]{:S(2)}) collective-permute-start(bf16[24,4096]{1,0:T(8,128)(2,1)S(1)} %get-tuple-element.72), channel_id=1, source_target_pairs={{0,4},{1,5},{2,6},{3,7},{4,0},{5,1},{6,2},{7,3},{8,12},{9,13},{10,... | collective-permute-start | bytes 589832 | tf_op jit(solution)/shard_map/ppermute | solution.py:238
  25.2 10.1 %collective-permute-start.12 = (bf16[24,4096]{1,0:T(8,128)(2,1)S(1)}, bf16[24,4096]{1,0:T(8,128)(2,1)S(1)}, u32[]{:S(2)}, u32[]{:S(2)}) collective-permute-start(bf16[24,4096]{1,0:T(8,128)(2,1)S(1)} %get-tuple-element.72), channel_id=1, source_target_pairs={{0,12},{1,13},{2,14},{3,15},{4,8},{5,9},{6,10},{7,11},{8,4},{9,5},... | collective-permute-start | bytes 589832 | tf_op jit(solution)/shard_map/ppermute | solution.py:238
  27.0 8.3 %collective-permute-start.10 = (bf16[24,4096]{1,0:T(8,128)(2,1)S(1)}, bf16[24,4096]{1,0:T(8,128)(2,1)S(1)}, u32[]{:S(2)}, u32[]{:S(2)}) collective-permute-start(bf16[24,4096]{1,0:T(8,128)(2,1)S(1)} %get-tuple-element.73), channel_id=1, source_target_pairs={{0,8},{1,9},{2,10},{3,11},{4,12},{5,13},{6,14},{7,15},{8,0},{9,1},... | collective-permute-start | bytes 589832 | tf_op jit(solution)/shard_map/ppermute | solution.py:238
  28.4 5.7 %collective-permute-start.11 = (bf16[24,4096]{1,0:T(8,128)(2,1)S(1)}, bf16[24,4096]{1,0:T(8,128)(2,1)S(1)}, u32[]{:S(2)}, u32[]{:S(2)}) collective-permute-start(bf16[24,4096]{1,0:T(8,128)(2,1)S(1)} %get-tuple-element.74), channel_id=1, source_target_pairs={{0,2},{1,3},{2,0},{3,1},{4,6},{5,7},{6,4},{7,5},{8,10},{9,11},{10,... | collective-permute-start | bytes 589832 | tf_op jit(solution)/shard_map/ppermute | solution.py:238
  38.1 7.0 %collective-permute-start.13 = (bf16[40,2048]{1,0:T(8,128)(2,1)S(1)}, bf16[40,2048]{1,0:T(8,128)(2,1)S(1)}, u32[]{:S(2)}, u32[]{:S(2)}) collective-permute-start(bf16[40,2048]{1,0:T(8,128)(2,1)S(1)} %pad_maximum_fusion.5), channel_id=1, source_target_pairs={{0,2},{1,3},{2,0},{3,1},{4,6},{5,7},{6,4},{7,5},{8,10},{9,11},{10,... | collective-permute-start | bytes 491528 | tf_op jit(solution)/shard_map/ppermute | solution.py:238
  38.9 10.5 %collective-permute-start.18 = (bf16[40,2048]{1,0:T(8,128)(2,1)S(1)}, bf16[40,2048]{1,0:T(8,128)(2,1)S(1)}, u32[]{:S(2)}, u32[]{:S(2)}) collective-permute-start(bf16[40,2048]{1,0:T(8,128)(2,1)S(1)} %pad_maximum_fusion.6), channel_id=1, source_target_pairs={{0,12},{1,13},{2,14},{3,15},{4,8},{5,9},{6,10},{7,11},{8,4},{9,5},... | collective-permute-start | bytes 491528 | tf_op jit(solution)/shard_map/ppermute | solution.py:238
  41.6 6.8 %collective-permute-start.15 = (bf16[40,2048]{1,0:T(8,128)(2,1)S(1)}, bf16[40,2048]{1,0:T(8,128)(2,1)S(1)}, u32[]{:S(2)}, u32[]{:S(2)}) collective-permute-start(bf16[40,2048]{1,0:T(8,128)(2,1)S(1)} %pad_maximum_fusion.7), channel_id=1, source_target_pairs={{0,8},{1,9},{2,10},{3,11},{4,12},{5,13},{6,14},{7,15},{8,0},{9,1},... | collective-permute-start | bytes 491528 | tf_op jit(solution)/shard_map/ppermute | solution.py:238
  41.7 7.7 %collective-permute-start.17 = (bf16[40,2048]{1,0:T(8,128)(2,1)S(1)}, bf16[40,2048]{1,0:T(8,128)(2,1)S(1)}, u32[]{:S(2)}, u32[]{:S(2)}) collective-permute-start(bf16[40,2048]{1,0:T(8,128)(2,1)S(1)} %pad_maximum_fusion.8), channel_id=1, source_target_pairs={{0,4},{1,5},{2,6},{3,7},{4,0},{5,1},{6,2},{7,3},{8,12},{9,13},{10,... | collective-permute-start | bytes 491528 | tf_op jit(solution)/shard_map/ppermute | solution.py:238
  45.2 9.7 %collective-permute-start.14 = (bf16[40,2048]{1,0:T(8,128)(2,1)S(1)}, bf16[40,2048]{1,0:T(8,128)(2,1)S(1)}, u32[]{:S(2)}, u32[]{:S(2)}) collective-permute-start(bf16[40,2048]{1,0:T(8,128)(2,1)S(1)} %add_convert_fusion.3), channel_id=1, source_target_pairs={{0,8},{1,9},{2,10},{3,11},{4,12},{5,13},{6,14},{7,15},{8,0},{9,1},... | collective-permute-start | bytes 491528 | tf_op jit(solution)/shard_map/ppermute | solution.py:238
  48.4 6.4 %collective-permute-start.16 = (bf16[40,2048]{1,0:T(8,128)(2,1)S(1)}, bf16[40,2048]{1,0:T(8,128)(2,1)S(1)}, u32[]{:S(2)}, u32[]{:S(2)}) collective-permute-start(bf16[40,2048]{1,0:T(8,128)(2,1)S(1)} %add_convert_fusion.2), channel_id=1, source_target_pairs={{0,4},{1,5},{2,6},{3,7},{4,0},{5,1},{6,2},{7,3},{8,12},{9,13},{10,... | collective-permute-start | bytes 491528 | tf_op jit(solution)/shard_map/ppermute | solution.py:238
  49.5 5.4 %collective-permute-start.19 = (bf16[40,2048]{1,0:T(8,128)(2,1)S(1)}, bf16[40,2048]{1,0:T(8,128)(2,1)S(1)}, u32[]{:S(2)}, u32[]{:S(2)}) collective-permute-start(bf16[40,2048]{1,0:T(8,128)(2,1)S(1)} %add_convert_fusion.1), channel_id=1, source_target_pairs={{0,2},{1,3},{2,0},{3,1},{4,6},{5,7},{6,4},{7,5},{8,10},{9,11},{10,... | collective-permute-start | bytes 491528 | tf_op jit(solution)/shard_map/ppermute | solution.py:238
  51.9 7.6 %collective-permute-start.20 = (bf16[320,2048]{1,0:T(8,128)(2,1)S(1)}, bf16[320,2048]{1,0:T(8,128)(2,1)S(1)}, u32[]{:S(2)}, u32[]{:S(2)}) collective-permute-start(bf16[320,2048]{1,0:T(8,128)(2,1)S(1)} %fusion.6), channel_id=1, source_target_pairs={{0,1},{1,0},{2,3},{3,2},{4,5},{5,4},{6,7},{7,6},{8,9},{9,8},{10,11... | collective-permute-start | bytes 3932168 | tf_op jit(solution)/shard_map/ppermute | solution.py:238
  52.0 7.5 %collective-permute-start.21 = (bf16[320,2048]{1,0:T(8,128)(2,1)S(1)}, bf16[320,2048]{1,0:T(8,128)(2,1)S(1)}, u32[]{:S(2)}, u32[]{:S(2)}) collective-permute-start(bf16[320,2048]{1,0:T(8,128)(2,1)S(1)} %fusion.7), channel_id=1, source_target_pairs={{0,1},{1,0},{2,3},{3,2},{4,5},{5,4},{6,7},{7,6},{8,9},{9,8},{10,11... | collective-permute-start | bytes 3932168 | tf_op jit(solution)/shard_map/ppermute | solution.py:238
  55.0 7.2 %collective-permute-start.22 = (bf16[40,1024]{1,0:T(8,128)(2,1)S(1)}, bf16[40,1024]{1,0:T(8,128)(2,1)S(1)}, u32[]{:S(2)}, u32[]{:S(2)}) collective-permute-start(bf16[40,1024]{1,0:T(8,128)(2,1)S(1)} %pad_maximum_fusion.9), channel_id=1, source_target_pairs={{0,16},{1,17},{2,18},{3,19},{4,20},{5,21},{6,22},{7,23},{8,24},{9,... | collective-permute-start | bytes 245768 | tf_op jit(solution)/shard_map/ppermute | solution.py:281
  (1 other events, 1.7 us)

commit v24 on v21

--- a/solution.py
+++ b/solution.py
@@ -345,7 +345,7 @@
     own, sum_x, sum_y, sum_z, sum_xy, sum_yz, sum_zx, sum_far = parts
     back = chain([sum_far, sum_zx, sum_xy, sum_yz])
     far, zx, xy, yz = [
-        swap(rows, mask) for rows, mask in zip(back, (x_bit | y_bit, x_bit, y_bit, z_bit))
+        swap(rows, mask) for rows, mask in zip(back, (y_bit | z_bit, x_bit, y_bit, z_bit))
     ]
 
     def gradients(part, awaited):
@@ -371,7 +371,7 @@
     else:
         new_weights = [weights.T for weights in stepped(mine, shares)]
     near = swaps(
-        [total(sum_z, zx, far), total(sum_x, xy), total(sum_y, yz)], (z_bit, x_bit, y_bit)
+        [total(sum_z, zx), total(sum_x, xy, far), total(sum_y, yz)], (z_bit, x_bit, y_bit)
     )
     sums = total(own, *near)
     early_sum, late_sum = sums[:first], sums[first:]

time: 62.6 us -> 62 us (level)
  starting transfers between devices: 30.2 us -> 29.4 us
    ppermute x21, starting transfers between devices: 23.2 us -> 21.6 us  [swap(): lax.ppermute(rows, 'expert', [(i, i ^ mask) for i in range(n_expert)])]
    ppermute x2, starting transfers between devices: 7.03 us -> 7.81 us  [shifted(): return lax.ppermute(rows, 'expert', pairs)]
  transfers between devices with their start and end apart: 23 -> 23, of which waited for: 7 -> 10; matrix products, arithmetic and copies ran while one was open for 19% -> 19% of each run, Pallas kernels for 4% -> 4%
where the time goes in v24:
time: 62 us; the launch traced here: 61.8 us
  starting transfers between devices  29.4 us (47%)
  waiting for transfers between devices  11.2 us (18%)
  matrix products  8.72 us (14%)
  Pallas kernels  6.64 us (11%)
  other arithmetic  3.58 us (6%)
  local copies, waits for them, and re-layouts  1.17 us (2%)
  between operations  1.01 us (2%)
    ppermute x21, starting transfers between devices, swap(): lax.ppermute(rows, 'expert', [(i, i ^ mask) for i in range(n_expert)])  21.6 us
    ppermute x21, waiting for transfers between devices, swap(): lax.ppermute(rows, 'expert', [(i, i ^ mask) for i in range(n_expert)])  10.5 us
    ppermute x2, starting transfers between devices, shifted(): return lax.ppermute(rows, 'expert', pairs)  7.81 us
    dot_general x11, matrix products, contract_rows(): lax.dot_general(left, right, (((0,), (0,)), ((), ())), preferred_element_...  6.04 us
    pallas_call x1, Pallas kernels, worked(): pl.pallas_call(lambda *refs: expert_kernel(scale_in, scale_out, *refs), o...  2.6 us
    pallas_call x1, Pallas kernels, stepped(): pl.pallas_call(lambda *refs: step_kernel(rows, *refs), out_shape=[jax.Sha...  2.47 us
    dot_general x2, matrix products, contract_cols(): lax.dot_general(left, right, (((1,), (1,)), ((), ())), preferred_element_...  2.07 us
    transpose x1, other arithmetic, shards(): whole_weights(w_in)  1.93 us
  transfers between devices with their start and end apart: 23, of which 10 were waited for; matrix products, arithmetic and copies ran while one was open for 19% of the time, Pallas kernels for 4%

profile of v24, /device:TPU:0, one launch (start us, length us, event | category | flops | bytes accessed | tf_op | source)
XLA Modules:
  0.0 61.8 jit_solution(18041958420497937906)
XLA Ops:
  0.6 1.6 %shard_map.85 = (bf16[16,4096]{1,0:T(8,128)(2,1)S(1)}, bf16[24,4096]{1,0:T(8,128)(2,1)S(1)}, bf16[40,2048]{1,0:T(8,128)(2,1)S(1)}, bf16[16,64]{1,0:T(8,128)(2,1)...) custom-call(s32[1,64]{1,0:T(1,128)} %bitcast.17, ...), custom_call_target="tpu_custom_call" | custom-call | tf_op jit(solution)/shard_map/pallas_call | solution.py:124
  2.2 4.1 %collective-permute-start = (bf16[40,2048]{1,0:T(8,128)(2,1)S(1)}, bf16[40,2048]{1,0:T(8,128)(2,1)S(1)}, u32[]{:S(2)}, u32[]{:S(2)}) collective-permute-start(bf16[40,2048]{1,0:T(8,128)(2,1)S(1)} %get-tuple-element.56.refs_4_), channel_id=1, source_target_pairs={{0,16},{1,17},{2,18},{3,19},{4,20},{5,21},{6,22},{7,23},{8,24},{9,... | collective-permute-start | bytes 491528 | tf_op jit(solution)/shard_map/ppermute | solution.py:281
  6.3 2.5 %collective-permute-start.1 = (bf16[16,4096]{1,0:T(8,128)(2,1)S(1)}, bf16[16,4096]{1,0:T(8,128)(2,1)S(1)}, u32[]{:S(2)}, u32[]{:S(2)}) collective-permute-start(bf16[16,4096]{1,0:T(8,128)(2,1)S(1)} %get-tuple-element.61), channel_id=1, source_target_pairs={{0,6},{1,7},{2,4},{3,5},{4,2},{5,3},{6,0},{7,1},{8,14},{9,15},{10,... | collective-permute-start | bytes 393224 | tf_op jit(solution)/shard_map/ppermute | solution.py:238
  8.8 1.6 %collective-permute-start.2 = (bf16[16,4096]{1,0:T(8,128)(2,1)S(1)}, bf16[16,4096]{1,0:T(8,128)(2,1)S(1)}, u32[]{:S(2)}, u32[]{:S(2)}) collective-permute-start(bf16[16,4096]{1,0:T(8,128)(2,1)S(1)} %get-tuple-element.62), channel_id=1, source_target_pairs={{0,8},{1,9},{2,10},{3,11},{4,12},{5,13},{6,14},{7,15},{8,0},{9,1},... | collective-permute-start | bytes 393224 | tf_op jit(solution)/shard_map/ppermute | solution.py:238
  11.4 1.9 %convert_bitcast_fusion = bf16[320,2048]{1,0:T(8,128)(2,1)S(1)} fusion(f32[2048,320]{0,1:T(8,128)} %param.10), kind=kLoop, calls=%fused_computation.20 | loop fusion | flops 655360 | bytes 3932160 | tf_op jit(solution)/shard_map/transpose | solution.py:324
  14.2 1.6 %collective-permute-done.2 = bf16[16,4096]{1,0:T(8,128)(2,1)S(1)} collective-permute-done((bf16[16,4096]{1,0:T(8,128)(2,1)S(1)}, bf16[16,4096]{1,0:T(8,128)(2,1)S(1)}, u32[]{:S(2)}, u32[]{:S(2)}) %collective-permute-start.2) | collective-permute-done | bytes 131104 | tf_op jit(solution)/shard_map/ppermute | solution.py:238
  15.9 1.6 %collective-permute-start.6 = (bf16[40,4096]{1,0:T(8,128)(2,1)S(1)}, bf16[40,4096]{1,0:T(8,128)(2,1)S(1)}, u32[]{:S(2)}, u32[]{:S(2)}) collective-permute-start(bf16[40,4096]{1,0:T(8,128)(2,1)S(1)} %get-tuple-element.69), channel_id=1, source_target_pairs={{0,2},{1,3},{2,0},{3,1},{4,6},{5,7},{6,4},{7,5},{8,10},{9,11},{10,... | collective-permute-start | bytes 983048 | tf_op jit(solution)/shard_map/ppermute | solution.py:238
  18.4 1.4 %collective-permute-start.7 = (bf16[40,4096]{1,0:T(8,128)(2,1)S(1)}, bf16[40,4096]{1,0:T(8,128)(2,1)S(1)}, u32[]{:S(2)}, u32[]{:S(2)}) collective-permute-start(bf16[40,4096]{1,0:T(8,128)(2,1)S(1)} %get-tuple-element.70), channel_id=1, source_target_pairs={{0,8},{1,9},{2,10},{3,11},{4,12},{5,13},{6,14},{7,15},{8,0},{9,1},... | collective-permute-start | bytes 983048 | tf_op jit(solution)/shard_map/ppermute | solution.py:238
  19.8 4.9 %collective-permute-done.6 = bf16[40,4096]{1,0:T(8,128)(2,1)S(1)} collective-permute-done((bf16[40,4096]{1,0:T(8,128)(2,1)S(1)}, bf16[40,4096]{1,0:T(8,128)(2,1)S(1)}, u32[]{:S(2)}, u32[]{:S(2)}) %collective-permute-start.6) | collective-permute-done | bytes 327712 | tf_op jit(solution)/shard_map/ppermute | solution.py:238
  25.2 1.8 %collective-permute-start.12 = (bf16[24,4096]{1,0:T(8,128)(2,1)S(1)}, bf16[24,4096]{1,0:T(8,128)(2,1)S(1)}, u32[]{:S(2)}, u32[]{:S(2)}) collective-permute-start(bf16[24,4096]{1,0:T(8,128)(2,1)S(1)} %get-tuple-element.72), channel_id=1, source_target_pairs={{0,12},{1,13},{2,14},{3,15},{4,8},{5,9},{6,10},{7,11},{8,4},{9,5},... | collective-permute-start | bytes 589832 | tf_op jit(solution)/shard_map/ppermute | solution.py:238
  27.0 1.4 %collective-permute-start.10 = (bf16[24,4096]{1,0:T(8,128)(2,1)S(1)}, bf16[24,4096]{1,0:T(8,128)(2,1)S(1)}, u32[]{:S(2)}, u32[]{:S(2)}) collective-permute-start(bf16[24,4096]{1,0:T(8,128)(2,1)S(1)} %get-tuple-element.73), channel_id=1, source_target_pairs={{0,8},{1,9},{2,10},{3,11},{4,12},{5,13},{6,14},{7,15},{8,0},{9,1},... | collective-permute-start | bytes 589832 | tf_op jit(solution)/shard_map/ppermute | solution.py:238
  29.6 1.0 %multiply_convert_fusion = (bf16[128,640]{1,0:T(8,128)(2,1)S(1)}, f32[128,640]{1,0:T(8,128)S(1)}) fusion(bf16[320,2048]{1,0:T(8,128)(2,1)S(1)} %convert_bitcast_fusion, bf16[320,2048]{1,0:T(8,128)(2,1)S(1)} %get-tuple-element.106, bf16[128,4096]{1,0:T(8,128)(2,1)S(1)} %slice_dynamic-update-slice_fusion), kind=kOutput, calls=%fused_computation.52 | convolution fusion | flops 341606400 | bytes 3637248 | tf_op jit(solution)/shard_map/dot_general | solution.py:39
  30.6 1.1 %fusion.11 = bf16[128,640]{1,0:T(8,128)(2,1)S(1)} fusion(bf16[128,4096]{1,0:T(8,128)(2,1)S(1)} %slice_dynamic-update-slice_fusion, f32[128,640]{1,0:T(8,128)S(1)} %get-tuple-element.138, bf16[320,2048]{1,0:T(8,128)(2,1)S(1)} %get-tuple-element.105, bf16[320,2048]{1,0:T(8,128)(2,1)S(1)} %convert_bitcast_fusion.1), kind=kOutput, calls=%fused_computation.24 | convolution fusion | flops 342507520 | bytes 3637248 | tf_op jit(solution)/shard_map/dot_general | solution.py:39
  33.2 1.0 %collective-permute-done.11 = bf16[24,4096]{1,0:T(8,128)(2,1)S(1)} collective-permute-done((bf16[24,4096]{1,0:T(8,128)(2,1)S(1)}, bf16[24,4096]{1,0:T(8,128)(2,1)S(1)}, u32[]{:S(2)}, u32[]{:S(2)}) %collective-permute-start.11) | collective-permute-done | bytes 196640 | tf_op jit(solution)/shard_map/ppermute | solution.py:238
  34.2 1.1 %collective-permute-done.10 = bf16[24,4096]{1,0:T(8,128)(2,1)S(1)} collective-permute-done((bf16[24,4096]{1,0:T(8,128)(2,1)S(1)}, bf16[24,4096]{1,0:T(8,128)(2,1)S(1)}, u32[]{:S(2)}, u32[]{:S(2)}) %collective-permute-start.10) | collective-permute-done | bytes 196640 | tf_op jit(solution)/shard_map/ppermute | solution.py:238
  35.4 2.6 %shard_map.87 = (bf16[192,640]{1,0:T(8,128)(2,1)S(1)}, bf16[192,640]{1,0:T(8,128)(2,1)S(1)}, bf16[192,2048]{1,0:T(8,128)(2,1)S(1)}) custom-call(bf16[192,4096]{1,0:T(8,128)(2,1)S(1)} %constant_dynamic-update-slice_fusion.5.refs_0_, bf16[640,2048]{1,0:T(8,128)(2,1)S(1)} %get-tuple-element.139.refs_1_, bf16[640,2048]{1,0:T(8,128)(2,1)S(1)} %get-tuple-element.140.refs_2_), custom_call_target="tpu_custom_call" | custom-call | flops 1509949440 | bytes 5242880 | tf_op jit(solution)/shard_map/pallas_call | solution.py:175
  38.1 1.9 %collective-permute-start.16 = (bf16[40,2048]{1,0:T(8,128)(2,1)S(1)}, bf16[40,2048]{1,0:T(8,128)(2,1)S(1)}, u32[]{:S(2)}, u32[]{:S(2)}) collective-permute-start(bf16[40,2048]{1,0:T(8,128)(2,1)S(1)} %pad_maximum_fusion.5), channel_id=1, source_target_pairs={{0,12},{1,13},{2,14},{3,15},{4,8},{5,9},{6,10},{7,11},{8,4},{9,5},... | collective-permute-start | bytes 491528 | tf_op jit(solution)/shard_map/ppermute | solution.py:238
  40.0 1.6 %collective-permute-start.13 = (bf16[40,2048]{1,0:T(8,128)(2,1)S(1)}, bf16[40,2048]{1,0:T(8,128)(2,1)S(1)}, u32[]{:S(2)}, u32[]{:S(2)}) collective-permute-start(bf16[40,2048]{1,0:T(8,128)(2,1)S(1)} %pad_maximum_fusion.6), channel_id=1, source_target_pairs={{0,2},{1,3},{2,0},{3,1},{4,6},{5,7},{6,4},{7,5},{8,10},{9,11},{10,... | collective-permute-start | bytes 491528 | tf_op jit(solution)/shard_map/ppermute | solution.py:238
  45.5 1.2 %collective-permute-start.14 = (bf16[40,2048]{1,0:T(8,128)(2,1)S(1)}, bf16[40,2048]{1,0:T(8,128)(2,1)S(1)}, u32[]{:S(2)}, u32[]{:S(2)}) collective-permute-start(bf16[40,2048]{1,0:T(8,128)(2,1)S(1)} %add_convert_fusion.3), channel_id=1, source_target_pairs={{0,8},{1,9},{2,10},{3,11},{4,12},{5,13},{6,14},{7,15},{8,0},{9,1},... | collective-permute-start | bytes 491528 | tf_op jit(solution)/shard_map/ppermute | solution.py:238
  46.8 1.0 %collective-permute-done.15 = bf16[40,2048]{1,0:T(8,128)(2,1)S(1)} collective-permute-done((bf16[40,2048]{1,0:T(8,128)(2,1)S(1)}, bf16[40,2048]{1,0:T(8,128)(2,1)S(1)}, u32[]{:S(2)}, u32[]{:S(2)}) %collective-permute-start.15) | collective-permute-done | bytes 163872 | tf_op jit(solution)/shard_map/ppermute | solution.py:238
  48.3 1.6 %collective-permute-start.19 = (bf16[40,2048]{1,0:T(8,128)(2,1)S(1)}, bf16[40,2048]{1,0:T(8,128)(2,1)S(1)}, u32[]{:S(2)}, u32[]{:S(2)}) collective-permute-start(bf16[40,2048]{1,0:T(8,128)(2,1)S(1)} %add_convert_fusion.1), channel_id=1, source_target_pairs={{0,4},{1,5},{2,6},{3,7},{4,0},{5,1},{6,2},{7,3},{8,12},{9,13},{10,... | collective-permute-start | bytes 491528 | tf_op jit(solution)/shard_map/ppermute | solution.py:238
  53.8 3.7 %collective-permute-start.22 = (bf16[40,1024]{1,0:T(8,128)(2,1)S(1)}, bf16[40,1024]{1,0:T(8,128)(2,1)S(1)}, u32[]{:S(2)}, u32[]{:S(2)}) collective-permute-start(bf16[40,1024]{1,0:T(8,128)(2,1)S(1)} %pad_maximum_fusion.9), channel_id=1, source_target_pairs={{0,16},{1,17},{2,18},{3,19},{4,20},{5,21},{6,22},{7,23},{8,24},{9,... | collective-permute-start | bytes 245768 | tf_op jit(solution)/shard_map/ppermute | solution.py:281
  58.0 2.5 %shard_map.88 = (f32[320,2048]{1,0:T(8,128)}, f32[320,2048]{1,0:T(8,128)}) custom-call(f32[320,2048]{1,0:T(8,128)S(1)} %fusion.3.refs_0_, f32[320,2048]{1,0:T(8,128)S(1)} %fusion.1.refs_1_, bf16[320,2048]{1,0:T(8,128)(2,1)S(1)} %collective-permute-done.20.refs_2_, bf16[320,2048]{1,0:T(8,128)(2,1)S(1)} %collective-permute-done.21.refs_3_), custom_call_target="tpu_custom_call" | custom-call | flops 2621440 | bytes 5242880 | tf_op jit(solution)/shard_map/pallas_call | solution.py:213
  60.8 1.0 %fusion.9 = bf16[64,2048]{1,0:T(8,128)(2,1)} fusion(f32[64,2048]{1,0:T(8,128)S(1)} %convolution_add_fusion.5, bf16[20,1024]{1,0:T(8,128)(2,1)S(1)} %get-tuple-element.136, bf16[20,1024]{1,0:T(8,128)(2,1)S(1)} %get-tuple-element.135, bf16[40,64]{1,0:T(8,128)(2,1)S(1)} %get-tuple-element.93), kind=kOutput, calls=%fused_computation.19 | convolution fusion | flops 5668864 | bytes 890880 | tf_op jit(solution)/shard_map/dot_general | solution.py:33
  (80 shorter events, 15.3 us)
Async XLA Ops:
  0.6 12.7 %copy-start = (f32[2048,320]{0,1:T(8,128)S(1)}, f32[2048,320]{0,1:T(8,128)}, u32[]{:S(2)}) copy-start(f32[2048,320]{0,1:T(8,128)} %param.11) | copy-start | bytes 7864324
  2.2 11.9 %collective-permute-start = (bf16[40,2048]{1,0:T(8,128)(2,1)S(1)}, bf16[40,2048]{1,0:T(8,128)(2,1)S(1)}, u32[]{:S(2)}, u32[]{:S(2)}) collective-permute-start(bf16[40,2048]{1,0:T(8,128)(2,1)S(1)} %get-tuple-element.56.refs_4_), channel_id=1, source_target_pairs={{0,16},{1,17},{2,18},{3,19},{4,20},{5,21},{6,22},{7,23},{8,24},{9,... | collective-permute-start | bytes 491528 | tf_op jit(solution)/shard_map/ppermute | solution.py:281
  6.3 7.9 %collective-permute-start.1 = (bf16[16,4096]{1,0:T(8,128)(2,1)S(1)}, bf16[16,4096]{1,0:T(8,128)(2,1)S(1)}, u32[]{:S(2)}, u32[]{:S(2)}) collective-permute-start(bf16[16,4096]{1,0:T(8,128)(2,1)S(1)} %get-tuple-element.61), channel_id=1, source_target_pairs={{0,6},{1,7},{2,4},{3,5},{4,2},{5,3},{6,0},{7,1},{8,14},{9,15},{10,... | collective-permute-start | bytes 393224 | tf_op jit(solution)/shard_map/ppermute | solution.py:238
  8.8 7.0 %collective-permute-start.2 = (bf16[16,4096]{1,0:T(8,128)(2,1)S(1)}, bf16[16,4096]{1,0:T(8,128)(2,1)S(1)}, u32[]{:S(2)}, u32[]{:S(2)}) collective-permute-start(bf16[16,4096]{1,0:T(8,128)(2,1)S(1)} %get-tuple-element.62), channel_id=1, source_target_pairs={{0,8},{1,9},{2,10},{3,11},{4,12},{5,13},{6,14},{7,15},{8,0},{9,1},... | collective-permute-start | bytes 393224 | tf_op jit(solution)/shard_map/ppermute | solution.py:238
  10.3 5.4 %collective-permute-start.3 = (bf16[16,4096]{1,0:T(8,128)(2,1)S(1)}, bf16[16,4096]{1,0:T(8,128)(2,1)S(1)}, u32[]{:S(2)}, u32[]{:S(2)}) collective-permute-start(bf16[16,4096]{1,0:T(8,128)(2,1)S(1)} %get-tuple-element.63), channel_id=1, source_target_pairs={{0,2},{1,3},{2,0},{3,1},{4,6},{5,7},{6,4},{7,5},{8,10},{9,11},{10,... | collective-permute-start | bytes 393224 | tf_op jit(solution)/shard_map/ppermute | solution.py:238
  10.9 5.0 %collective-permute-start.4 = (bf16[16,4096]{1,0:T(8,128)(2,1)S(1)}, bf16[16,4096]{1,0:T(8,128)(2,1)S(1)}, u32[]{:S(2)}, u32[]{:S(2)}) collective-permute-start(bf16[16,4096]{1,0:T(8,128)(2,1)S(1)} %get-tuple-element.64), channel_id=1, source_target_pairs={{0,4},{1,5},{2,6},{3,7},{4,0},{5,1},{6,2},{7,3},{8,12},{9,13},{10,... | collective-permute-start | bytes 393224 | tf_op jit(solution)/shard_map/ppermute | solution.py:238
  15.9 8.8 %collective-permute-start.6 = (bf16[40,4096]{1,0:T(8,128)(2,1)S(1)}, bf16[40,4096]{1,0:T(8,128)(2,1)S(1)}, u32[]{:S(2)}, u32[]{:S(2)}) collective-permute-start(bf16[40,4096]{1,0:T(8,128)(2,1)S(1)} %get-tuple-element.69), channel_id=1, source_target_pairs={{0,2},{1,3},{2,0},{3,1},{4,6},{5,7},{6,4},{7,5},{8,10},{9,11},{10,... | collective-permute-start | bytes 983048 | tf_op jit(solution)/shard_map/ppermute | solution.py:238
  17.5 9.4 %collective-permute-start.5 = (bf16[40,4096]{1,0:T(8,128)(2,1)S(1)}, bf16[40,4096]{1,0:T(8,128)(2,1)S(1)}, u32[]{:S(2)}, u32[]{:S(2)}) collective-permute-start(bf16[40,4096]{1,0:T(8,128)(2,1)S(1)} %get-tuple-element.69), channel_id=1, source_target_pairs={{0,4},{1,5},{2,6},{3,7},{4,0},{5,1},{6,2},{7,3},{8,12},{9,13},{10,... | collective-permute-start | bytes 983048 | tf_op jit(solution)/shard_map/ppermute | solution.py:238
  18.4 10.0 %collective-permute-start.7 = (bf16[40,4096]{1,0:T(8,128)(2,1)S(1)}, bf16[40,4096]{1,0:T(8,128)(2,1)S(1)}, u32[]{:S(2)}, u32[]{:S(2)}) collective-permute-start(bf16[40,4096]{1,0:T(8,128)(2,1)S(1)} %get-tuple-element.70), channel_id=1, source_target_pairs={{0,8},{1,9},{2,10},{3,11},{4,12},{5,13},{6,14},{7,15},{8,0},{9,1},... | collective-permute-start | bytes 983048 | tf_op jit(solution)/shard_map/ppermute | solution.py:238
  19.8 9.6 %collective-permute-start.8 = (bf16[640,2048]{1,0:T(8,128)(2,1)S(1)}, bf16[640,2048]{1,0:T(8,128)(2,1)S(1)}, u32[]{:S(2)}, u32[]{:S(2)}) collective-permute-start(bf16[640,2048]{1,0:T(8,128)(2,1)S(1)} %pad_maximum_fusion.1), channel_id=1, source_target_pairs={{0,1},{1,0},{2,3},{3,2},{4,5},{5,4},{6,7},{7,6},{8,9},{9,8},{10,11... | collective-permute-start | bytes 7864328 | tf_op jit(solution)/shard_map/ppermute | solution.py:238
  24.8 10.5 %collective-permute-start.9 = (bf16[24,4096]{1,0:T(8,128)(2,1)S(1)}, bf16[24,4096]{1,0:T(8,128)(2,1)S(1)}, u32[]{:S(2)}, u32[]{:S(2)}) collective-permute-start(bf16[24,4096]{1,0:T(8,128)(2,1)S(1)} %get-tuple-element.72), channel_id=1, source_target_pairs={{0,4},{1,5},{2,6},{3,7},{4,0},{5,1},{6,2},{7,3},{8,12},{9,13},{10,... | collective-permute-start | bytes 589832 | tf_op jit(solution)/shard_map/ppermute | solution.py:238
  25.2 10.1 %collective-permute-start.12 = (bf16[24,4096]{1,0:T(8,128)(2,1)S(1)}, bf16[24,4096]{1,0:T(8,128)(2,1)S(1)}, u32[]{:S(2)}, u32[]{:S(2)}) collective-permute-start(bf16[24,4096]{1,0:T(8,128)(2,1)S(1)} %get-tuple-element.72), channel_id=1, source_target_pairs={{0,12},{1,13},{2,14},{3,15},{4,8},{5,9},{6,10},{7,11},{8,4},{9,5},... | collective-permute-start | bytes 589832 | tf_op jit(solution)/shard_map/ppermute | solution.py:238
  27.0 8.3 %collective-permute-start.10 = (bf16[24,4096]{1,0:T(8,128)(2,1)S(1)}, bf16[24,4096]{1,0:T(8,128)(2,1)S(1)}, u32[]{:S(2)}, u32[]{:S(2)}) collective-permute-start(bf16[24,4096]{1,0:T(8,128)(2,1)S(1)} %get-tuple-element.73), channel_id=1, source_target_pairs={{0,8},{1,9},{2,10},{3,11},{4,12},{5,13},{6,14},{7,15},{8,0},{9,1},... | collective-permute-start | bytes 589832 | tf_op jit(solution)/shard_map/ppermute | solution.py:238
  28.4 5.7 %collective-permute-start.11 = (bf16[24,4096]{1,0:T(8,128)(2,1)S(1)}, bf16[24,4096]{1,0:T(8,128)(2,1)S(1)}, u32[]{:S(2)}, u32[]{:S(2)}) collective-permute-start(bf16[24,4096]{1,0:T(8,128)(2,1)S(1)} %get-tuple-element.74), channel_id=1, source_target_pairs={{0,2},{1,3},{2,0},{3,1},{4,6},{5,7},{6,4},{7,5},{8,10},{9,11},{10,... | collective-permute-start | bytes 589832 | tf_op jit(solution)/shard_map/ppermute | solution.py:238
  38.1 9.7 %collective-permute-start.16 = (bf16[40,2048]{1,0:T(8,128)(2,1)S(1)}, bf16[40,2048]{1,0:T(8,128)(2,1)S(1)}, u32[]{:S(2)}, u32[]{:S(2)}) collective-permute-start(bf16[40,2048]{1,0:T(8,128)(2,1)S(1)} %pad_maximum_fusion.5), channel_id=1, source_target_pairs={{0,12},{1,13},{2,14},{3,15},{4,8},{5,9},{6,10},{7,11},{8,4},{9,5},... | collective-permute-start | bytes 491528 | tf_op jit(solution)/shard_map/ppermute | solution.py:238
  40.0 5.5 %collective-permute-start.13 = (bf16[40,2048]{1,0:T(8,128)(2,1)S(1)}, bf16[40,2048]{1,0:T(8,128)(2,1)S(1)}, u32[]{:S(2)}, u32[]{:S(2)}) collective-permute-start(bf16[40,2048]{1,0:T(8,128)(2,1)S(1)} %pad_maximum_fusion.6), channel_id=1, source_target_pairs={{0,2},{1,3},{2,0},{3,1},{4,6},{5,7},{6,4},{7,5},{8,10},{9,11},{10,... | collective-permute-start | bytes 491528 | tf_op jit(solution)/shard_map/ppermute | solution.py:238
  41.6 6.2 %collective-permute-start.15 = (bf16[40,2048]{1,0:T(8,128)(2,1)S(1)}, bf16[40,2048]{1,0:T(8,128)(2,1)S(1)}, u32[]{:S(2)}, u32[]{:S(2)}) collective-permute-start(bf16[40,2048]{1,0:T(8,128)(2,1)S(1)} %pad_maximum_fusion.7), channel_id=1, source_target_pairs={{0,4},{1,5},{2,6},{3,7},{4,0},{5,1},{6,2},{7,3},{8,12},{9,13},{10,... | collective-permute-start | bytes 491528 | tf_op jit(solution)/shard_map/ppermute | solution.py:238
  42.1 6.1 %collective-permute-start.18 = (bf16[40,2048]{1,0:T(8,128)(2,1)S(1)}, bf16[40,2048]{1,0:T(8,128)(2,1)S(1)}, u32[]{:S(2)}, u32[]{:S(2)}) collective-permute-start(bf16[40,2048]{1,0:T(8,128)(2,1)S(1)} %pad_maximum_fusion.8), channel_id=1, source_target_pairs={{0,8},{1,9},{2,10},{3,11},{4,12},{5,13},{6,14},{7,15},{8,0},{9,1},... | collective-permute-start | bytes 491528 | tf_op jit(solution)/shard_map/ppermute | solution.py:238
  45.5 8.1 %collective-permute-start.14 = (bf16[40,2048]{1,0:T(8,128)(2,1)S(1)}, bf16[40,2048]{1,0:T(8,128)(2,1)S(1)}, u32[]{:S(2)}, u32[]{:S(2)}) collective-permute-start(bf16[40,2048]{1,0:T(8,128)(2,1)S(1)} %add_convert_fusion.3), channel_id=1, source_target_pairs={{0,8},{1,9},{2,10},{3,11},{4,12},{5,13},{6,14},{7,15},{8,0},{9,1},... | collective-permute-start | bytes 491528 | tf_op jit(solution)/shard_map/ppermute | solution.py:238
  47.9 5.8 %collective-permute-start.17 = (bf16[40,2048]{1,0:T(8,128)(2,1)S(1)}, bf16[40,2048]{1,0:T(8,128)(2,1)S(1)}, u32[]{:S(2)}, u32[]{:S(2)}) collective-permute-start(bf16[40,2048]{1,0:T(8,128)(2,1)S(1)} %add_convert_fusion.2), channel_id=1, source_target_pairs={{0,2},{1,3},{2,0},{3,1},{4,6},{5,7},{6,4},{7,5},{8,10},{9,11},{10,... | collective-permute-start | bytes 491528 | tf_op jit(solution)/shard_map/ppermute | solution.py:238
  48.3 5.4 %collective-permute-start.19 = (bf16[40,2048]{1,0:T(8,128)(2,1)S(1)}, bf16[40,2048]{1,0:T(8,128)(2,1)S(1)}, u32[]{:S(2)}, u32[]{:S(2)}) collective-permute-start(bf16[40,2048]{1,0:T(8,128)(2,1)S(1)} %add_convert_fusion.1), channel_id=1, source_target_pairs={{0,4},{1,5},{2,6},{3,7},{4,0},{5,1},{6,2},{7,3},{8,12},{9,13},{10,... | collective-permute-start | bytes 491528 | tf_op jit(solution)/shard_map/ppermute | solution.py:238
  50.9 7.1 %collective-permute-start.20 = (bf16[320,2048]{1,0:T(8,128)(2,1)S(1)}, bf16[320,2048]{1,0:T(8,128)(2,1)S(1)}, u32[]{:S(2)}, u32[]{:S(2)}) collective-permute-start(bf16[320,2048]{1,0:T(8,128)(2,1)S(1)} %fusion.6), channel_id=1, source_target_pairs={{0,1},{1,0},{2,3},{3,2},{4,5},{5,4},{6,7},{7,6},{8,9},{9,8},{10,11... | collective-permute-start | bytes 3932168 | tf_op jit(solution)/shard_map/ppermute | solution.py:238
  51.0 7.1 %collective-permute-start.21 = (bf16[320,2048]{1,0:T(8,128)(2,1)S(1)}, bf16[320,2048]{1,0:T(8,128)(2,1)S(1)}, u32[]{:S(2)}, u32[]{:S(2)}) collective-permute-start(bf16[320,2048]{1,0:T(8,128)(2,1)S(1)} %fusion.7), channel_id=1, source_target_pairs={{0,1},{1,0},{2,3},{3,2},{4,5},{5,4},{6,7},{7,6},{8,9},{9,8},{10,11... | collective-permute-start | bytes 3932168 | tf_op jit(solution)/shard_map/ppermute | solution.py:238
  53.8 7.0 %collective-permute-start.22 = (bf16[40,1024]{1,0:T(8,128)(2,1)S(1)}, bf16[40,1024]{1,0:T(8,128)(2,1)S(1)}, u32[]{:S(2)}, u32[]{:S(2)}) collective-permute-start(bf16[40,1024]{1,0:T(8,128)(2,1)S(1)} %pad_maximum_fusion.9), channel_id=1, source_target_pairs={{0,16},{1,17},{2,18},{3,19},{4,20},{5,21},{6,22},{7,23},{8,24},{9,... | collective-permute-start | bytes 245768 | tf_op jit(solution)/shard_map/ppermute | solution.py:281
  (1 other events, 1.7 us)
